TPU v7x, 32 devices: a whole 2x2x4 slice. The times are simulated.
32 devices in a mesh: dp: 8 (over z, y), tensor: 4 (over x, core).
Axes of the slice: x: 2, y: 2, z: 4, core: 2. Of those that a mesh axis runs over, the one named last changes fastest.
Arguments:
- grad_up: bfloat16 [8, 512, 6144], P('dp', None, 'tensor'), may hold values from -400 to 400, as said below
- error_up: bfloat16 [8, 512, 6144], P('dp', None, 'tensor'), may hold values from -3 to 3
- grad_down: bfloat16 [8, 6144, 512], P('dp', 'tensor'), may hold values from -400 to 400, as said below
- error_down: bfloat16 [8, 6144, 512], P('dp', 'tensor'), may hold values from -3 to 3
- q_up: float32 [6144, 64], P('tensor'), may hold values from -6 to 6
- q_down: float32 [512, 64], replicated, may hold values from -6 to 6
Outputs:
- new_error_up: bfloat16 [8, 512, 6144], P('dp', None, 'tensor')
- update_up: bfloat16 [512, 6144], P(None, 'tensor')
- new_error_down: bfloat16 [8, 6144, 512], P('dp', 'tensor')
- update_down: bfloat16 [6144, 512], P('tensor')
Inputs may be any that keep to these rules, and one draw needn't show every extreme that they name: `grad_up`: no structure beyond the range is promised. `grad_down`: no structure beyond the range is promised.
All inputs are finite; a program needn't handle non-finite values.
Results may differ from a plain program's by a relative error of at most 0.001.
Values sent between devices are 32-bit elements; how exact they have to be, the bound alone decides.
No kernel may reach another device: no remote copies, remote signals or barrier semaphores. Data moves between devices by JAX's collectives and lax.ppermute only.
A program may use at most 64 MiB of HBM per device.

v0:
```python
import jax
import jax.numpy as jnp
from jax import lax
from jax.sharding import PartitionSpec as P

FF_DEV = 1536
ROWS = 512


HIGHEST = lax.Precision.HIGHEST
CLIP_RMS = 0.1


def solve_right(factor, left):
    return lax.linalg.triangular_solve(factor, left, left_side=False, lower=True, transpose_a=True)


def on_device(grad_up, error_up, grad_down, error_down, q_up, q_down):
    replicas = lax.axis_size("dp")
    merged_up = grad_up[0].astype(jnp.float32) + error_up[0].astype(jnp.float32)
    merged_down = grad_down[0].astype(jnp.float32) + error_down[0].astype(jnp.float32)
    left_up = lax.psum(jnp.dot(merged_up, q_up, precision=HIGHEST), ("dp", "tensor")) / replicas
    gram_up = jnp.dot(left_up.T, left_up, precision=HIGHEST)
    basis_up = solve_right(jnp.linalg.cholesky(gram_up), left_up)
    right_up = lax.psum(jnp.dot(merged_up.T, basis_up, precision=HIGHEST), "dp") / replicas
    rebuilt_up = jnp.dot(basis_up, right_up.T, precision=HIGHEST)
    term_left = jnp.dot(merged_down, q_down, precision=HIGHEST)
    left_down = lax.psum(term_left, "dp") / replicas
    gram_down = lax.psum(jnp.dot(left_down.T, left_down, precision=HIGHEST), "tensor")
    factor_down = jnp.linalg.cholesky(gram_down)
    basis_down = solve_right(factor_down, left_down)
    term_right = jnp.dot(merged_down.T, basis_down, precision=HIGHEST)
    right_down = lax.psum(term_right, ("dp", "tensor")) / replicas
    rebuilt_down = jnp.dot(basis_down, right_down.T, precision=HIGHEST)
    local_sq = jnp.sum(rebuilt_up * rebuilt_up) + jnp.sum(rebuilt_down * rebuilt_down)
    norm_sq = lax.psum(local_sq, "tensor")
    limit = CLIP_RMS * jnp.sqrt(jnp.float32(2 * ROWS * FF_DEV * lax.axis_size("tensor")))
    clip_factor = jnp.minimum(jnp.float32(1.0), limit / jnp.sqrt(norm_sq))
    new_error_up = (merged_up - rebuilt_up).astype(jnp.bfloat16)[None]
    new_error_down = (merged_down - rebuilt_down).astype(jnp.bfloat16)[None]
    update_up = (clip_factor * rebuilt_up).astype(jnp.bfloat16)
    update_down = (clip_factor * rebuilt_down).astype(jnp.bfloat16)
    return (new_error_up, update_up, new_error_down, update_down)


def solution(mesh):
    placed = (
        P("dp", None, "tensor"),
        P("dp", None, "tensor"),
        P("dp", "tensor", None),
        P("dp", "tensor", None),
        P("tensor", None),
        P(),
    )
    return jax.shard_map(
        on_device,
        mesh=mesh,
        in_specs=placed,
        out_specs=(
            P("dp", None, "tensor"),
            P(None, "tensor"),
            P("dp", "tensor", None),
            P("tensor", None),
        ),
        check_vma=False,
    )
```

profile of v0, /device:TPU:0, one launch (start us, length us, event | category | flops | bytes accessed | tf_op | source)
XLA Modules:
  0.0 377.9 jit_solution(17357084897101981012)
XLA Ops:
  7.2 0.0 copy-start
  7.2 0.0 all-reduce.7.cloned.1.call-start
  7.2 6.1 %fusion.2 = f32[1536,64]{0,1:T(8,128)} fusion(f32[512,64]{0,1:T(8,128)} %param.12, bf16[1,1536,512]{2,1,0:T(8,128)(2,1)} %param.10, bf16[1,1536,512]{2,1,0:T(8,128)(2,1)} %param.9), kind=kOutput, calls=%fused_computation.3 | convolution fusion | flops 606339072 | bytes 3670016 | tf_op jit(solution)/shard_map/dot_general | solution.py:27
  13.3 0.0 copy-start.1
  13.3 0.0 copy-start.2
  13.3 0.0 all-reduce.7.cloned.1.call-update
  13.3 0.0 all-reduce.9.cloned.1.call-start
  13.4 0.0 copy-done
  13.4 6.1 %fusion.7 = f32[512,64]{0,1:T(8,128)} fusion(f32[1536,64]{0,1:T(8,128)S(1)} %copy-done, bf16[1,512,1536]{2,1,0:T(8,128)(2,1)} %param.8, bf16[1,512,1536]{2,1,0:T(8,128)(2,1)} %param.7), kind=kOutput, calls=%fused_computation.9 | convolution fusion | flops 606339072 | bytes 3670016 | tf_op jit(solution)/shard_map/dot_general | solution.py:22
  19.5 68.0 %all-reduce.7.cloned.1.call-done = f32[1536,64]{0,1:T(8,128)} async-done(((f32[1536,64]{0,1:T(8,128)}), f32[1536,64]{0,1:T(8,128)}) %all-reduce.7.cloned.1.call-update) | async-done | bytes 393232 | tf_op jit(solution)/shard_map/psum | solution.py:28
  87.5 2.2 fusion.16
  89.7 11.4 %psum.45 = f32[64,64]{0,1:T(8,128)} all-reduce(f32[64,64]{0,1:T(8,128)} %fusion.16), channel_id=1, replica_groups=mesh['dp'=8,'tensor'=4] {'tensor'}, use_global_device_ids=true, to_apply=%region_6.0 | all-reduce | flops 4096 | bytes 32768 | tf_op jit(solution)/shard_map/psum | solution.py:29
  101.1 1.5 copy.12
  102.6 1.4 fusion.33
  104.0 7.2 %cholesky.55 = f32[64,64]{1,0:T(8,128)} custom-call(f32[64,64]{1,0:T(8,128)} %fusion.33), custom_call_target="Cholesky" | custom-call | tf_op jit(solution)/shard_map/jit(cholesky)/cholesky | solution.py:30
  111.2 0.8 select_reduce_fusion
  112.0 0.6 compare_reduce_fusion
  112.6 2.0 fusion.31
  114.6 6.3 %custom-call.9 = f32[1,64,64]{1,2,0:T(8,128)} custom-call(f32[1,64,64]{2,1,0:T(8,128)} %fusion.31), custom_call_target="InvertDiagBlocksLowerTriangular" | custom-call | tf_op jit(solution)/shard_map/triangular_solve | solution.py:15
  120.9 1.5 fusion.14
  122.4 0.0 copy-start.6
  122.4 0.7 copy-done.6
  123.2 0.0 copy-done.1
  123.2 0.0 copy-done.2
  123.2 3.1 fusion
  126.3 0.0 all-reduce.9.cloned.1.call-update
  126.3 0.2 all-reduce.5.cloned.1.call-start
  126.5 124.5 %all-reduce.9.cloned.1.call-done = (f32[512,64]{0,1:T(8,128)}, f32[512,64]{0,1:T(8,128)}) async-done(((f32[512,64]{0,1:T(8,128)}, f32[512,64]{0,1:T(8,128)}), (f32[512,64]{0,1:T(8,128)}, f32[512,64]{0,1:T(8,128)})) %all-reduce.9.cloned.1.call-update) | async-done | bytes 262160 | tf_op jit(solution)/shard_map/psum | solution.py:22
  251.0 1.9 fusion.25
  252.9 1.5 copy.10
  254.3 1.4 fusion.35
  255.7 7.2 %cholesky.44 = f32[64,64]{1,0:T(8,128)} custom-call(f32[64,64]{1,0:T(8,128)} %fusion.35), custom_call_target="Cholesky" | custom-call | tf_op jit(solution)/shard_map/jit(cholesky)/cholesky | solution.py:24
  262.9 0.8 select_reduce_fusion.1
  263.7 0.6 compare_reduce_fusion.1
  264.4 2.0 fusion.30
  266.4 6.3 %custom-call.8 = f32[1,64,64]{1,2,0:T(8,128)} custom-call(f32[1,64,64]{2,1,0:T(8,128)} %fusion.30), custom_call_target="InvertDiagBlocksLowerTriangular" | custom-call | tf_op jit(solution)/shard_map/triangular_solve | solution.py:15
  272.7 1.2 fusion.23
  273.9 0.0 copy-start.7
  273.9 0.6 copy-done.7
  274.6 5.0 %fusion.5 = f32[1536,64]{0,1:T(8,128)} fusion(f32[512,64]{0,1:T(8,128)S(1)} %fusion.23, bf16[1,512,1536]{2,1,0:T(8,128)(2,1)} %param.8, bf16[1,512,1536]{2,1,0:T(8,128)(2,1)} %param.7), kind=kOutput, calls=%fused_computation.7 | convolution fusion | flops 606339072 | bytes 3670016 | tf_op jit(solution)/shard_map/dot_general | solution.py:25
  279.6 0.0 all-reduce.5.cloned.1.call-update
  279.6 6.0 %multiply_reduce_fusion = (f32[]{:T(128)}, f32[1536,512]{1,0:T(8,128)}) fusion(f32[1536,64]{0,1:T(8,128)} %copy-done.6, f32[512,64]{0,1:T(8,128)} %get-tuple-element.6), kind=kOutput, calls=%fused_computation.14 | convolution fusion | flops 605585408 | bytes 3670020 | tf_op jit(solution)/shard_map/dot_general | solution.py:34
  285.6 64.5 %all-reduce.5.cloned.1.call-done = f32[1536,64]{0,1:T(8,128)} async-done(((f32[1536,64]{0,1:T(8,128)}), f32[1536,64]{0,1:T(8,128)}) %all-reduce.5.cloned.1.call-update) | async-done | bytes 393232 | tf_op jit(solution)/shard_map/psum | solution.py:25
  350.0 6.0 %multiply_reduce_fusion.1 = (f32[]{:T(128)}, f32[512,1536]{1,0:T(8,128)}) fusion(f32[512,64]{0,1:T(8,128)} %copy-done.7, f32[1536,64]{0,1:T(8,128)} %all-reduce.5.cloned.1.call-done), kind=kOutput, calls=%fused_computation.16 | convolution fusion | flops 605650944 | bytes 3670020 | tf_op jit(solution)/shard_map/dot_general | solution.py:26
  357.4 6.2 %psum.47 = f32[]{:T(128)} all-reduce(f32[]{:T(128)S(6)} %add.42), channel_id=1, replica_groups=mesh['dp'=8,'tensor'=4] {'tensor'}, use_global_device_ids=true, to_apply=%region_9.11 | all-reduce | flops 1 | bytes 8 | tf_op jit(solution)/shard_map/psum | solution.py:36
  364.2 0.0 copy-start.3
  364.2 0.0 copy-start.4
  364.2 0.0 copy-start.5
  364.2 4.5 %multiply_convert_fusion = (bf16[1536,512]{1,0:T(8,128)(2,1)}, bf16[1,1536,512]{2,1,0:T(8,128)(2,1)}) fusion(f32[1536,512]{1,0:T(8,128)} %get-tuple-element.14, f32[]{:T(128)S(6)} %min_shard_map.3, bf16[1,1536,512]{2,1,0:T(8,128)(2,1)S(1)} %copy-done.1, bf16[1,1536,512]{2,1,0:T(8,128)(2,1)S(1)} %copy-done.2), kind=kLoop, calls=%fused_computation.12 | loop fusion | flops 5505024 | bytes 9437188 | tf_op jit(solution)/shard_map/convert_element_type | solution.py:42
  368.8 0.0 copy-done.3
  368.8 0.0 copy-done.4
  368.8 0.0 copy-done.5
  368.8 2.6 multiply_convert_fusion.1
Async XLA Ops:
  7.2 6.2 %copy-start = (f32[1536,64]{0,1:T(8,128)S(1)}, f32[1536,64]{0,1:T(8,128)}, u32[]{:S(2)}) copy-start(f32[1536,64]{0,1:T(8,128)} %param.11) | copy-start | bytes 1179652
  7.2 80.3 %all-reduce.7.cloned.1.call-start = ((), (), s32[]{:S(2)}) async-start(), calls=%async_computation.1 | async-start | bytes 786432 | tf_op jit(solution)/shard_map/psum | solution.py:28
  13.3 109.9 %copy-start.1 = (bf16[1,1536,512]{2,1,0:T(8,128)(2,1)S(1)}, bf16[1,1536,512]{2,1,0:T(8,128)(2,1)}, u32[]{:S(2)}) copy-start(bf16[1,1536,512]{2,1,0:T(8,128)(2,1)} %param.10) | copy-start | bytes 4718596
  13.3 109.9 %copy-start.2 = (bf16[1,1536,512]{2,1,0:T(8,128)(2,1)S(1)}, bf16[1,1536,512]{2,1,0:T(8,128)(2,1)}, u32[]{:S(2)}) copy-start(bf16[1,1536,512]{2,1,0:T(8,128)(2,1)} %param.9) | copy-start | bytes 4718596
  13.3 237.7 %all-reduce.9.cloned.1.call-start = ((), (), s32[]{:S(2)}) async-start(), calls=%async_computation.2 | async-start | bytes 524288 | tf_op jit(solution)/shard_map/psum | solution.py:22
  122.4 0.7 copy-start.6
  126.3 223.8 %all-reduce.5.cloned.1.call-start = ((), (), s32[]{:S(2)}) async-start(), calls=%async_computation | async-start | bytes 786432 | tf_op jit(solution)/shard_map/psum | solution.py:25
  273.9 0.7 copy-start.7
  364.2 4.6 %copy-start.3 = (bf16[1,512,1536]{2,1,0:T(8,128)(2,1)S(1)}, bf16[1,512,1536]{2,1,0:T(8,128)(2,1)}, u32[]{:S(2)}) copy-start(bf16[1,512,1536]{2,1,0:T(8,128)(2,1)} %param.8) | copy-start | bytes 4718596
  364.2 4.6 %copy-start.4 = (bf16[1,512,1536]{2,1,0:T(8,128)(2,1)S(1)}, bf16[1,512,1536]{2,1,0:T(8,128)(2,1)}, u32[]{:S(2)}) copy-start(bf16[1,512,1536]{2,1,0:T(8,128)(2,1)} %param.7) | copy-start | bytes 4718596
  364.2 4.6 %copy-start.5 = (f32[512,1536]{1,0:T(8,128)S(1)}, f32[512,1536]{1,0:T(8,128)}, u32[]{:S(2)}) copy-start(f32[512,1536]{1,0:T(8,128)} %get-tuple-element.12) | copy-start | bytes 9437188
Sparse Core Ops, SparseCore 0:
  13.5 73.9 all-reduce.6
  126.4 124.5 all-reduce.8
  279.7 70.2 all-reduce.4
where the time goes:
time: 379 us; the launch traced here: 378 us
  waiting for transfers between devices  257 us (68%)
  other arithmetic  43.9 us (12%)
  matrix products  39 us (10%)
  blocking collectives  17.6 us (5%)
  between operations  15.8 us (4%)
  local copies, waits for them, and re-layouts  4.33 us (1%)
    psum x1, waiting for transfers between devices, on_device(): lax.psum(jnp.dot(merged_up, q_up, precision=HIGHEST), ('dp', 'tensor'))  124 us
    psum x1, waiting for transfers between devices, on_device(): left_down = lax.psum(term_left, 'dp') / replicas  68 us
    psum x1, waiting for transfers between devices, on_device(): lax.psum(jnp.dot(merged_up.T, basis_up, precision=HIGHEST), 'dp') / replicas  64.5 us
    another operation x4, other arithmetic, solve_right(): lax.linalg.triangular_solve(factor, left, left_side=False, lower=True, tr...  16.6 us
    psum x1, blocking collectives, on_device(): lax.psum(jnp.dot(left_down.T, left_down, precision=HIGHEST), 'tensor')  11.4 us
    another operation x3, other arithmetic, on_device(): factor_down = jnp.linalg.cholesky(gram_down)  8.65 us
    another operation x3, other arithmetic, on_device(): basis_up = solve_right(jnp.linalg.cholesky(gram_up), left_up)  8.65 us
  transfers between devices with their start and end apart: 3, of which 3 were waited for; matrix products, arithmetic and copies ran while one was open for 3% of the time, Pallas kernels for 0%

commit v1 on v0

v1 whole, which is shorter than its diff:
```python
import functools

import jax
import jax.numpy as jnp
from jax import lax
from jax.experimental import pallas as pl
from jax.experimental.pallas import tpu as pltpu
from jax.sharding import PartitionSpec as P

F32 = jnp.float32
BF16 = jnp.bfloat16
HIGHEST = lax.Precision.HIGHEST
CLIP_RMS = 0.1
STEPS = 4
VMEM_LIMIT = 48 * 1024 * 1024


def split3(x):
    first = x.astype(BF16)
    rest = x - first.astype(F32)
    second = rest.astype(BF16)
    return first, second, (rest - second.astype(F32)).astype(BF16)


def tree_sum(values):
    values = list(values)
    while len(values) > 1:
        values = [values[i] + values[i + 1] for i in range(0, len(values), 2)]
    return values[0]


def dot(a, b, dims=((1,), (0,)), precision=None):
    return lax.dot_general(a, b, (dims, ((), ())), precision=precision, preferred_element_type=F32)


def scatter_chunks(total, stage, keep, send):
    n_dp, per, _ = stage.shape
    me = lax.axis_index("dp")
    for c in range(n_dp):
        stage[c] = total[c * per : (c + 1) * per, :]
    for d in range(n_dp):
        (send if d % 2 else keep)[d // 2] = stage[lax.bitwise_xor(me, d)]


def gather_chunks(pieces, stage, total, start):
    n_dp, per, _ = stage.shape
    width = pieces[0].shape[1]
    me = lax.axis_index("dp")
    for d, piece in enumerate(pieces):
        stage[lax.bitwise_xor(me, d), :, :width] = piece[...]
    for c in range(n_dp):
        total[c * per : (c + 1) * per, start : start + width] = stage[c, :, :width]


def left_kernel(gu, eu, gd, ed, qu, qd, keep, send, qsu, qsd, total, stage):
    step = pl.program_id(0)
    rank = qu.shape[1]
    rows = total.shape[1] - qu.shape[0]

    @pl.when(step == 0)
    def _():
        for q, qs in ((qu, qsu), (qd, qsd)):
            first, second, third = split3(q[...])
            qs[:, :rank] = first
            qs[:, rank : 2 * rank] = second
            qs[:, 2 * rank : 3 * rank] = third
            qs[:, 3 * rank :] = jnp.zeros_like(third)

    def term(g, e, qs, start):
        block = g.shape[1]
        t = dot(g[0], qs[...]) + dot(e[0], qs[...])
        t = (t[:, : 2 * rank] + t[:, 2 * rank :]).T
        total[:, pl.ds(pl.multiple_of(start + step * block, 128), block)] = t[:rank] + t[rank:]

    term(gu, eu, qsu, 0)
    term(gd, ed, qsd, rows)

    @pl.when(step == STEPS - 1)
    def _():
        scatter_chunks(total, stage, keep, send)


def right_kernel(n_dp, gu, eu, gd, ed, *refs):
    step = pl.program_id(0)
    up, down = refs[:n_dp], refs[n_dp : 2 * n_dp]
    left, gram_up, gram_down, keep, send, pieces, total, stage = refs[2 * n_dp :]
    rank = left.shape[0]
    rows = gu.shape[1]
    ff = left.shape[1] - rows
    block = gu.shape[2]
    depth = gd.shape[1]

    @pl.when(step == 0)
    def _():
        gather_chunks(up, stage, left, 0)
        gather_chunks(down, stage, left, rows)
        for i, piece in enumerate(split3(left[...])):
            pieces[i * rank : (i + 1) * rank, :] = piece
        nt = ((1,), (1,))
        gram_up[...] = dot(left[:, :rows], left[:, :rows], nt, HIGHEST)
        gram_down[...] = dot(left[:, rows:], left[:, rows:], nt, HIGHEST)
        total[:, ff:] = jnp.zeros((rank, rows), F32)

    def fold(t):
        return t[:rank] + (t[rank : 2 * rank] + t[2 * rank :])

    lhs = pieces[:, :rows]
    total[:, pl.ds(pl.multiple_of(step * block, 128), block)] = fold(dot(lhs, gu[0]) + dot(lhs, eu[0]))
    lhs = pieces[:, pl.ds(pl.multiple_of(rows + step * depth, 128), depth)]
    total[:, ff:] += fold(dot(lhs, gd[0]) + dot(lhs, ed[0]))

    @pl.when(step == STEPS - 1)
    def _():
        scatter_chunks(total, stage, keep, send)


def half_kernel(keep, got, *outs):
    for i, out in enumerate(outs):
        out[...] = keep[i] + got[i]


def mean_kernel(n_dp, split, *refs):
    total = tree_sum(ref[...] for ref in refs[:-2]) / n_dp
    refs[-2][...] = total[:, :split]
    refs[-1][...] = total[:, split:]


def sum_kernel(*refs):
    refs[-1][...] = tree_sum(ref[...] for ref in refs[:-1])


def basis_kernel(left, gram_up, *refs):
    *grams, inv_up, inv_down, lhs_up, lhs_down = refs
    rank = left.shape[0]
    rows = lhs_up.shape[0]
    row_id = lax.broadcasted_iota(jnp.int32, (rank, 2 * rank), 0)
    lane_id = lax.broadcasted_iota(jnp.int32, (rank, 2 * rank), 1)
    eye = (lane_id == row_id + rank).astype(F32)

    def start(gram):
        return jnp.concatenate([gram, jnp.zeros_like(gram)], axis=1) + eye

    state = [start(gram_up[...]), start(tree_sum(g[...] for g in grams))]
    for k in range(rank):
        for s in range(2):
            a = state[s]
            pivot_row = a[k : k + 1, :]
            below = row_id[:, :1] > k
            factor = jnp.where(below, a[:, k : k + 1], 0.0) / a[k : k + 1, k : k + 1]
            state[s] = a - factor * pivot_row
    for a, inv, lhs, part in ((state[0], inv_up, lhs_up, slice(0, rows)), (state[1], inv_down, lhs_down, slice(rows, None))):
        diagonal = jnp.sum(jnp.where(lane_id == row_id, a, 0.0), axis=1, keepdims=True)
        inverse = (a / jnp.sqrt(diagonal))[:, rank:]
        inv[...] = inverse
        first, second, _ = split3(dot(inverse, left[:, part], precision=HIGHEST).T)
        lhs[:, :rank] = first
        lhs[:, rank : 2 * rank] = first
        lhs[:, 2 * rank : 3 * rank] = second
        lhs[:, 3 * rank :] = second


def factor_kernel(n_dp, inv_up, inv_down, *refs):
    up, down = refs[:n_dp], refs[n_dp : 2 * n_dp]
    rhs, sq_up, sq_down, total, stage = refs[2 * n_dp :]
    rank = total.shape[0]
    ff = up[0].shape[1]
    gather_chunks(up, stage, total, 0)
    gather_chunks(down, stage, total, ff)
    for inv, part, sq in ((inv_up, slice(0, ff), sq_up), (inv_down, slice(ff, None), sq_down)):
        right = dot(inv[...], total[:, part], precision=HIGHEST)
        sq[...] = jnp.full(sq.shape, jnp.sum(right * right), F32)
        first, second, _ = split3(right)
        rhs[:rank, part] = first
        rhs[rank : 2 * rank, part] = second
        rhs[2 * rank : 3 * rank, part] = first
        rhs[3 * rank :, part] = second


def error_kernel(gu, eu, gd, ed, lhs_up, lhs_down, rhs, out_up, out_down):
    ff = gu.shape[2]
    rebuilt = dot(lhs_up[...], rhs[:, :ff])
    out_up[0] = (gu[0].astype(F32) + eu[0].astype(F32) - rebuilt).astype(BF16)
    rebuilt = dot(lhs_down[...], rhs[:, ff:])
    out_down[0] = (gd[0].astype(F32) + ed[0].astype(F32) - rebuilt).astype(BF16)


def update_kernel(limit, lhs_up, lhs_down, rhs, *refs):
    *squares, sq_down, out_up, out_down = refs
    ff = out_up.shape[1]
    norm_sq = tree_sum(s[...] for s in squares) + sq_down[...]
    clip = jnp.minimum(jnp.float32(1.0), limit / jnp.sqrt(norm_sq))[:1, :1]
    out_up[...] = (clip * dot(lhs_up[...], rhs[:, :ff])).astype(BF16)
    out_down[...] = (clip * dot(lhs_down[...], rhs[:, ff:])).astype(BF16)


def shaped(*dims, dtype=F32):
    return jax.ShapeDtypeStruct(dims, dtype)


def whole(shape):
    return pl.BlockSpec(shape, lambda *_: (0,) * len(shape))


def params():
    return pltpu.CompilerParams(vmem_limit_bytes=VMEM_LIMIT)


def call(kernel, out_shape, *args, flops=0, name=None, **more):
    arrays = list(args) + jax.tree.leaves(out_shape)
    size = sum(a.size * a.dtype.itemsize for a in arrays)
    cost = pl.CostEstimate(flops=flops, bytes_accessed=size, transcendentals=0)
    return pl.pallas_call(kernel, out_shape=out_shape, compiler_params=params(), cost_estimate=cost, name=name, **more)(*args)


def swap(x, axis, distance):
    pairs = [(i, i ^ distance) for i in range(lax.axis_size(axis))]
    return lax.ppermute(x, axis, pairs)


def mean_over_replicas(keep, send, split):
    n_dp = lax.axis_size("dp")
    half, per, width = keep.shape
    got = swap(send, "dp", 1)
    parts = call(half_kernel, [shaped(per, width)] * half, keep, got, name="half_sum")
    got = [parts[0]] + [swap(parts[j], "dp", 2 * j) for j in range(1, half)]
    outs = [shaped(per, split), shaped(per, width - split)]
    return call(functools.partial(mean_kernel, n_dp, split), outs, *got, name="replica_mean")


def sum_over_shards(x):
    got = [x] + [swap(x, "tensor", j) for j in range(1, lax.axis_size("tensor"))]
    return call(sum_kernel, shaped(*x.shape), *got, name="shard_sum")


def gather(x):
    n_dp = lax.axis_size("dp")
    near = [x] + [swap(x, "dp", d) for d in range(2, n_dp, 2)]
    far = [swap(p, "dp", 1) for p in near]
    return [p for pair in zip(near, far) for p in pair]


def on_device(gu, eu, gd, ed, qu, qd):
    n_dp, n_shards = lax.axis_size("dp"), lax.axis_size("tensor")
    _, rows, ff = gu.shape
    rank = qu.shape[1]
    width = rows + ff
    half, per = n_dp // 2, rank // n_dp
    chunks = [shaped(half, per, width)] * 2
    chunk_specs = [whole((half, per, width))] * 2

    keep, send = call(
        left_kernel, chunks, gu, eu, gd, ed, qu, qd,
        name="left_terms", flops=8 * rows * ff * 4 * rank, grid=(STEPS,),
        in_specs=[pl.BlockSpec((1, rows // STEPS, ff), lambda i: (0, i, 0))] * 2
        + [pl.BlockSpec((1, ff // STEPS, rows), lambda i: (0, i, 0))] * 2
        + [whole(qu.shape), whole(qd.shape)],
        out_specs=chunk_specs,
        scratch_shapes=[pltpu.VMEM((ff, 4 * rank), BF16), pltpu.VMEM((rows, 4 * rank), BF16), pltpu.VMEM((rank, width), F32), pltpu.VMEM((n_dp, per, width), F32)],
    )
    chunk_up, chunk_down = mean_over_replicas(keep, send, rows)
    down = gather(chunk_down)
    up = gather(sum_over_shards(chunk_up))

    left, gram_up, gram_down, keep, send = call(
        functools.partial(right_kernel, n_dp),
        [shaped(rank, width), shaped(rank, rank), shaped(rank, rank)] + chunks, gu, eu, gd, ed, *up, *down,
        name="right_terms", flops=8 * rows * ff * 3 * rank, grid=(STEPS,),
        in_specs=[pl.BlockSpec((1, rows, ff // STEPS), lambda i: (0, 0, i))] * 2
        + [pl.BlockSpec((1, ff // STEPS, rows), lambda i: (0, i, 0))] * 2
        + [whole(p.shape) for p in up + down],
        out_specs=[whole((rank, width)), whole((rank, rank)), whole((rank, rank))] + chunk_specs,
        scratch_shapes=[pltpu.VMEM((3 * rank, width), BF16), pltpu.VMEM((rank, width), F32), pltpu.VMEM((n_dp, per, width), F32)],
    )
    grams = [gram_down] + [swap(gram_down, "tensor", j) for j in range(1, n_shards)]
    chunk_up, chunk_down = mean_over_replicas(keep, send, ff)
    inv_up, inv_down, lhs_up, lhs_down = call(
        basis_kernel,
        [shaped(rank, rank)] * 2 + [shaped(rows, 4 * rank, dtype=BF16), shaped(ff, 4 * rank, dtype=BF16)],
        left, gram_up, *grams, name="basis", flops=10**9,
    )
    up = gather(chunk_up)
    down = gather(sum_over_shards(chunk_down))

    rhs, sq_up, sq_down = call(
        functools.partial(factor_kernel, n_dp),
        [shaped(4 * rank, width, dtype=BF16), shaped(8, 128), shaped(8, 128)], inv_up, inv_down, *up, *down,
        name="right_factor", scratch_shapes=[pltpu.VMEM((rank, width), F32), pltpu.VMEM((n_dp, per, width), F32)],
    )
    squares = [sq_up] + [swap(sq_up, "tensor", j) for j in range(1, n_shards)]

    lhs_specs = [pl.BlockSpec((rows // STEPS, 4 * rank), lambda i: (i, 0)), pl.BlockSpec((ff // STEPS, 4 * rank), lambda i: (i, 0))]
    replica_specs = [pl.BlockSpec((1, rows // STEPS, ff), lambda i: (0, i, 0)), pl.BlockSpec((1, ff // STEPS, rows), lambda i: (0, i, 0))]
    new_error_up, new_error_down = call(
        error_kernel, [shaped(1, rows, ff, dtype=BF16), shaped(1, ff, rows, dtype=BF16)], gu, eu, gd, ed, lhs_up, lhs_down, rhs,
        name="new_error", flops=4 * rows * ff * 4 * rank, grid=(STEPS,),
        in_specs=[replica_specs[0]] * 2 + [replica_specs[1]] * 2 + lhs_specs + [whole(rhs.shape)],
        out_specs=replica_specs,
    )
    limit = CLIP_RMS * (2.0 * rows * ff * n_shards) ** 0.5
    update_up, update_down = call(
        functools.partial(update_kernel, limit), [shaped(rows, ff, dtype=BF16), shaped(ff, rows, dtype=BF16)],
        lhs_up, lhs_down, rhs, *squares, sq_down,
        name="update", flops=4 * rows * ff * 4 * rank, grid=(STEPS,),
        in_specs=lhs_specs + [whole(rhs.shape)] + [whole((8, 128))] * (n_shards + 1),
        out_specs=[pl.BlockSpec((rows // STEPS, ff), lambda i: (i, 0)), pl.BlockSpec((ff // STEPS, rows), lambda i: (i, 0))],
    )
    return new_error_up, update_up, new_error_down, update_down


def solution(mesh):
    placed = (
        P("dp", None, "tensor"),
        P("dp", None, "tensor"),
        P("dp", "tensor", None),
        P("dp", "tensor", None),
        P("tensor", None),
        P(),
    )
    return jax.shard_map(
        on_device,
        mesh=mesh,
        in_specs=placed,
        out_specs=(
            P("dp", None, "tensor"),
            P(None, "tensor"),
            P("dp", "tensor", None),
            P("tensor", None),
        ),
        check_vma=False,
    )
```

time: 379 us -> 119 us (0.31)
  waiting for transfers between devices: 257 us -> 34.9 us
  starting transfers between devices: 0.3 us -> 52.8 us
  other arithmetic: 43.9 us -> 0 us
  matrix products: 39 us -> 0 us
  Pallas kernels: 0 us -> 25.3 us
  blocking collectives: 17.6 us -> 0 us
  between operations: 15.8 us -> 0.86 us
    psum x3 -> x0, waiting for transfers between devices: 257 us -> none  [the longest x1 124 us: on_device(): lax.psum(jnp.dot(merged_up, q_up, precision=HIGHEST), ('dp', 'tensor'))]
    ppermute x0 -> x48, starting transfers between devices: none -> 52.8 us  [swap(): return lax.ppermute(x, axis, pairs)]
    dot_general x8 -> x0, matrix products: 36.3 us -> none  [the longest x1 6.09 us: on_device(): term_left = jnp.dot(merged_down, q_down, precision=HIGHEST)]
    ppermute x0 -> x48, waiting for transfers between devices: none -> 34.9 us  [swap(): return lax.ppermute(x, axis, pairs)]
    another operation x10 -> x0, other arithmetic: 33.9 us -> none  [the longest x4 16.6 us: solve_right(): lax.linalg.triangular_solve(factor, left, left_side=False, lower=True, tr...]
    pallas_call x0 -> x12, Pallas kernels: none -> 25.3 us  [call(): pl.pallas_call(kernel, out_shape=out_shape, compiler_params=params(), cos...]
    psum x2 -> x0, blocking collectives: 17.6 us -> none  [the longest x1 11.4 us: on_device(): lax.psum(jnp.dot(left_down.T, left_down, precision=HIGHEST), 'tensor')]
    convert_element_type x2 -> x0, other arithmetic: 7.16 us -> none  [the longest x1 4.55 us: on_device(): update_down = (clip_factor * rebuilt_down).astype(jnp.bfloat16)]
  transfers between devices with their start and end apart: 3 -> 48, of which waited for: 3 -> 15; matrix products, arithmetic and copies ran while one was open for 3% -> 0% of each run, Pallas kernels for 0% -> 10%
where the time goes in v1:
time: 119 us
  starting transfers between devices  52.8 us (44%)
  waiting for transfers between devices  34.9 us (29%)
  Pallas kernels  25.3 us (21%)
  local copies, waits for them, and re-layouts  5.11 us (4%)
    ppermute x48, starting transfers between devices, swap(): return lax.ppermute(x, axis, pairs)  52.8 us
    ppermute x48, waiting for transfers between devices, swap(): return lax.ppermute(x, axis, pairs)  34.9 us
    pallas_call x12, Pallas kernels, call(): pl.pallas_call(kernel, out_shape=out_shape, compiler_params=params(), cos...  25.3 us
    unnamed x10, local copies, waits for them, and re-layouts  5.11 us
  transfers between devices with their start and end apart: 48, of which 15 were waited for; matrix products, arithmetic and copies ran while one was open for 0% of the time, Pallas kernels for 10%

profile of v1, /device:TPU:0, one launch (start us, length us, event | category | flops | bytes accessed | tf_op | source)
XLA Modules:
  0.0 119.0 jit_solution(15758976006530954762)
XLA Ops:
  0.6 1.0 copy.11.qd
  1.7 1.3 %copy.10.qu = f32[1536,64]{1,0:T(8,128)S(1)} copy(f32[1536,64]{0,1:T(8,128)} %param.10) | data formatting | bytes 786432 | tf_op args[4]
  2.9 1.4 %copy-done = bf16[1,512,1536]{2,1,0:T(8,128)(2,1)S(1)} copy-done((bf16[1,512,1536]{2,1,0:T(8,128)(2,1)S(1)}, bf16[1,512,1536]{2,1,0:T(8,128)(2,1)}, u32[]{:S(2)}) %copy-start) | copy-done | bytes 1572888
  4.3 1.4 %copy-done.2 = bf16[1,512,1536]{2,1,0:T(8,128)(2,1)S(1)} copy-done((bf16[1,512,1536]{2,1,0:T(8,128)(2,1)S(1)}, bf16[1,512,1536]{2,1,0:T(8,128)(2,1)}, u32[]{:S(2)}) %copy-start.2) | copy-done | bytes 1572888
  5.8 4.9 %left_terms.1 = (f32[4,8,2048]{2,1,0:T(8,128)S(1)}, f32[4,8,2048]{2,1,0:T(8,128)S(1)}) custom-call(bf16[1,512,1536]{2,1,0:T(8,128)(2,1)S(1)} %copy-done, bf16[1,512,1536]{2,1,0:T(8,128)(2,1)S(1)} %copy-done.2, bf16[1,1536,512]{2,1,0:T(8,128)(2,1)} %gd.5, bf16[1,1536,512]{2,1,0:T(8,128)(2,1)} %ed.5, f32[1536,64]{1,0:T(8,128)S(1)} %copy.10.qu, ...), custom_call_target="tpu_custom_call" | custom-call | flops 1610612736 | bytes 7340032 | tf_op jit(solution)/shard_map/left_terms/pallas_call | solution.py:212
  10.7 3.0 %collective-permute-start = (f32[4,8,2048]{2,1,0:T(8,128)S(1)}, f32[4,8,2048]{2,1,0:T(8,128)S(1)}, u32[]{:S(2)}, u32[]{:S(2)}) collective-permute-start(f32[4,8,2048]{2,1,0:T(8,128)S(1)} %get-tuple-element.35), channel_id=1, source_target_pairs={{0,4},{4,0},{8,12},{12,8},{16,20},{20,16},{24,28},{28,24},{1,5},{5... | collective-permute-start | bytes 786440 | tf_op jit(solution)/shard_map/ppermute | solution.py:217
  13.7 6.3 %collective-permute-done.got = f32[4,8,2048]{2,1,0:T(8,128)S(1)} collective-permute-done((f32[4,8,2048]{2,1,0:T(8,128)S(1)}, f32[4,8,2048]{2,1,0:T(8,128)S(1)}, u32[]{:S(2)}, u32[]{:S(2)}) %collective-permute-start) | collective-permute-done | bytes 262176 | tf_op jit(solution)/shard_map/ppermute | solution.py:217
  20.1 1.9 %collective-permute-start.1 = (f32[8,2048]{1,0:T(8,128)S(1)}, f32[8,2048]{1,0:T(8,128)S(1)}, u32[]{:S(2)}, u32[]{:S(2)}) collective-permute-start(f32[8,2048]{1,0:T(8,128)S(1)} %get-tuple-element.37), channel_id=1, source_target_pairs={{0,8},{4,12},{8,0},{12,4},{16,24},{20,28},{24,16},{28,20},{1,9},{5... | collective-permute-start | bytes 196616 | tf_op jit(solution)/shard_map/ppermute | solution.py:217
  21.9 2.6 %collective-permute-start.2 = (f32[8,2048]{1,0:T(8,128)S(1)}, f32[8,2048]{1,0:T(8,128)S(1)}, u32[]{:S(2)}, u32[]{:S(2)}) collective-permute-start(f32[8,2048]{1,0:T(8,128)S(1)} %get-tuple-element.38), channel_id=1, source_target_pairs={{0,16},{4,20},{8,24},{12,28},{16,0},{20,4},{24,8},{28,12},{1,17},{... | collective-permute-start | bytes 196616 | tf_op jit(solution)/shard_map/ppermute | solution.py:217
  24.5 0.5 collective-permute-done.1.refs_1_
  25.0 3.5 %collective-permute-done.2.refs_2_ = f32[8,2048]{1,0:T(8,128)S(1)} collective-permute-done((f32[8,2048]{1,0:T(8,128)S(1)}, f32[8,2048]{1,0:T(8,128)S(1)}, u32[]{:S(2)}, u32[]{:S(2)}) %collective-permute-start.2) | collective-permute-done | bytes 65568 | tf_op jit(solution)/shard_map/ppermute | solution.py:217
  28.5 2.1 %collective-permute-done.3.refs_3_ = f32[8,2048]{1,0:T(8,128)S(1)} collective-permute-done((f32[8,2048]{1,0:T(8,128)S(1)}, f32[8,2048]{1,0:T(8,128)S(1)}, u32[]{:S(2)}, u32[]{:S(2)}) %collective-permute-start.3) | collective-permute-done | bytes 65568 | tf_op jit(solution)/shard_map/ppermute | solution.py:217
  30.7 1.6 %collective-permute-start.5 = (f32[8,512]{1,0:T(8,128)S(1)}, f32[8,512]{1,0:T(8,128)S(1)}, u32[]{:S(2)}, u32[]{:S(2)}) collective-permute-start(f32[8,512]{1,0:T(8,128)S(1)} %get-tuple-element.40.refs_0_), channel_id=1, source_target_pairs={{0,2},{1,3},{2,0},{3,1},{4,6},{5,7},{6,4},{7,5},{8,10},{9,11},{10,... | collective-permute-start | bytes 49160 | tf_op jit(solution)/shard_map/ppermute | solution.py:217
  32.2 0.3 collective-permute-start.4
  32.5 0.9 collective-permute-start.19
  33.5 0.5 collective-permute-done.6.refs_3_
  34.0 3.0 %collective-permute-start.15 = (f32[8,1536]{1,0:T(8,128)S(1)}, f32[8,1536]{1,0:T(8,128)S(1)}, u32[]{:S(2)}, u32[]{:S(2)}) collective-permute-start(f32[8,1536]{1,0:T(8,128)S(1)} %get-tuple-element.41.refs_8_), channel_id=1, source_target_pairs={{0,8},{4,12},{8,0},{12,4},{16,24},{20,28},{24,16},{28,20},{1,9},{5... | collective-permute-start | bytes 147464 | tf_op jit(solution)/shard_map/ppermute | solution.py:217
  36.9 1.0 collective-permute-start.12
  37.9 0.6 collective-permute-start.10
  38.5 4.1 %collective-permute-done.12.refs_6_ = f32[8,512]{1,0:T(8,128)S(1)} collective-permute-done((f32[8,512]{1,0:T(8,128)S(1)}, f32[8,512]{1,0:T(8,128)S(1)}, u32[]{:S(2)}, u32[]{:S(2)}) %collective-permute-start.12) | collective-permute-done | bytes 16416 | tf_op jit(solution)/shard_map/ppermute | solution.py:217
  42.6 0.3 collective-permute-done.10.refs_4_
  42.9 1.5 %collective-permute-start.14 = (f32[8,1536]{1,0:T(8,128)S(1)}, f32[8,1536]{1,0:T(8,128)S(1)}, u32[]{:S(2)}, u32[]{:S(2)}) collective-permute-start(f32[8,1536]{1,0:T(8,128)S(1)} %get-tuple-element.41.refs_8_), channel_id=1, source_target_pairs={{0,4},{4,0},{8,12},{12,8},{16,20},{20,16},{24,28},{28,24},{1,5},{5... | collective-permute-start | bytes 147464 | tf_op jit(solution)/shard_map/ppermute | solution.py:217
  44.4 1.9 %collective-permute-done.8.refs_2_ = f32[8,512]{1,0:T(8,128)S(1)} collective-permute-done((f32[8,512]{1,0:T(8,128)S(1)}, f32[8,512]{1,0:T(8,128)S(1)}, u32[]{:S(2)}, u32[]{:S(2)}) %collective-permute-start.8) | collective-permute-done | bytes 16416 | tf_op jit(solution)/shard_map/ppermute | solution.py:217
  46.3 1.5 %collective-permute-start.7 = (f32[8,512]{1,0:T(8,128)S(1)}, f32[8,512]{1,0:T(8,128)S(1)}, u32[]{:S(2)}, u32[]{:S(2)}) collective-permute-start(f32[8,512]{1,0:T(8,128)S(1)} %shard_sum.2.refs_0_), channel_id=1, source_target_pairs={{0,4},{4,0},{8,12},{12,8},{16,20},{20,16},{24,28},{28,24},{1,5},{5... | collective-permute-start | bytes 49160 | tf_op jit(solution)/shard_map/ppermute | solution.py:217
  47.8 0.5 collective-permute-start.20
  48.3 1.5 %collective-permute-start.18 = (f32[8,1536]{1,0:T(8,128)S(1)}, f32[8,1536]{1,0:T(8,128)S(1)}, u32[]{:S(2)}, u32[]{:S(2)}) collective-permute-start(f32[8,1536]{1,0:T(8,128)S(1)} %collective-permute-done.17.refs_12_), channel_id=1, source_target_pairs={{0,4},{4,0},{8,12},{12,8},{16,20},{20,16},{24,28},{28,24},{1,5},{5... | collective-permute-start | bytes 147464 | tf_op jit(solution)/shard_map/ppermute | solution.py:217
  49.8 0.5 collective-permute-start.16
  50.4 1.5 %collective-permute-start.13 = (f32[8,512]{1,0:T(8,128)S(1)}, f32[8,512]{1,0:T(8,128)S(1)}, u32[]{:S(2)}, u32[]{:S(2)}) collective-permute-start(f32[8,512]{1,0:T(8,128)S(1)} %collective-permute-done.12.refs_6_), channel_id=1, source_target_pairs={{0,4},{4,0},{8,12},{12,8},{16,20},{20,16},{24,28},{28,24},{1,5},{5... | collective-permute-start | bytes 49160 | tf_op jit(solution)/shard_map/ppermute | solution.py:217
  51.9 0.5 collective-permute-start.11
  52.4 1.7 %collective-permute-done.13.refs_7_ = f32[8,512]{1,0:T(8,128)S(1)} collective-permute-done((f32[8,512]{1,0:T(8,128)S(1)}, f32[8,512]{1,0:T(8,128)S(1)}, u32[]{:S(2)}, u32[]{:S(2)}) %collective-permute-start.13) | collective-permute-done | bytes 16416 | tf_op jit(solution)/shard_map/ppermute | solution.py:217
  54.1 1.5 %collective-permute-start.9 = (f32[8,512]{1,0:T(8,128)S(1)}, f32[8,512]{1,0:T(8,128)S(1)}, u32[]{:S(2)}, u32[]{:S(2)}) collective-permute-start(f32[8,512]{1,0:T(8,128)S(1)} %collective-permute-done.8.refs_2_), channel_id=1, source_target_pairs={{0,4},{4,0},{8,12},{12,8},{16,20},{20,16},{24,28},{28,24},{1,5},{5... | collective-permute-start | bytes 49160 | tf_op jit(solution)/shard_map/ppermute | solution.py:217
  55.6 2.2 %collective-permute-done.9.refs_3_ = f32[8,512]{1,0:T(8,128)S(1)} collective-permute-done((f32[8,512]{1,0:T(8,128)S(1)}, f32[8,512]{1,0:T(8,128)S(1)}, u32[]{:S(2)}, u32[]{:S(2)}) %collective-permute-start.9) | collective-permute-done | bytes 16416 | tf_op jit(solution)/shard_map/ppermute | solution.py:217
  57.9 5.0 %right_terms.1 = (f32[64,2048]{1,0:T(8,128)S(1)}, f32[64,64]{1,0:T(8,128)S(1)}, f32[64,64]{1,0:T(8,128)S(1)}, f32[4,8,2048]{2,1,0:T(8,128)S(1)}, f32[4,8,2048]{2,1,0:T(8,128)S(1)}) custom-call(bf16[1,512,1536]{2,1,0:T(8,128)(2,1)S(1)} %copy-done.1, bf16[1,512,1536]{2,1,0:T(8,128)(2,1)S(1)} %copy-done.2, bf16[1,1536,512]{2,1,0:T(8,128)(2,1)} %gd.5, ...), custom_call_target="tpu_custom_call" | custom-call | flops 1207959552 | bytes 7897088 | tf_op jit(solution)/shard_map/right_terms/pallas_call | solution.py:212
  62.9 1.6 %collective-permute-start.24 = (f32[4,8,2048]{2,1,0:T(8,128)S(1)}, f32[4,8,2048]{2,1,0:T(8,128)S(1)}, u32[]{:S(2)}, u32[]{:S(2)}) collective-permute-start(f32[4,8,2048]{2,1,0:T(8,128)S(1)} %get-tuple-element.50), channel_id=1, source_target_pairs={{0,4},{4,0},{8,12},{12,8},{16,20},{20,16},{24,28},{28,24},{1,5},{5... | collective-permute-start | bytes 786440 | tf_op jit(solution)/shard_map/ppermute | solution.py:217
  64.5 4.9 %collective-permute-done.24.got = f32[4,8,2048]{2,1,0:T(8,128)S(1)} collective-permute-done((f32[4,8,2048]{2,1,0:T(8,128)S(1)}, f32[4,8,2048]{2,1,0:T(8,128)S(1)}, u32[]{:S(2)}, u32[]{:S(2)}) %collective-permute-start.24) | collective-permute-done | bytes 262176 | tf_op jit(solution)/shard_map/ppermute | solution.py:217
  69.5 1.5 %collective-permute-start.26 = (f32[8,2048]{1,0:T(8,128)S(1)}, f32[8,2048]{1,0:T(8,128)S(1)}, u32[]{:S(2)}, u32[]{:S(2)}) collective-permute-start(f32[8,2048]{1,0:T(8,128)S(1)} %get-tuple-element.53), channel_id=1, source_target_pairs={{0,16},{4,20},{8,24},{12,28},{16,0},{20,4},{24,8},{28,12},{1,17},{... | collective-permute-start | bytes 196616 | tf_op jit(solution)/shard_map/ppermute | solution.py:217
  70.9 2.9 %collective-permute-start.27 = (f32[8,2048]{1,0:T(8,128)S(1)}, f32[8,2048]{1,0:T(8,128)S(1)}, u32[]{:S(2)}, u32[]{:S(2)}) collective-permute-start(f32[8,2048]{1,0:T(8,128)S(1)} %get-tuple-element.54), channel_id=1, source_target_pairs={{0,24},{4,28},{8,16},{12,20},{16,8},{20,12},{24,0},{28,4},{1,25},{... | collective-permute-start | bytes 196616 | tf_op jit(solution)/shard_map/ppermute | solution.py:217
  73.9 0.9 collective-permute-done.26.refs_2_
  74.7 2.3 %collective-permute-done.27.refs_3_ = f32[8,2048]{1,0:T(8,128)S(1)} collective-permute-done((f32[8,2048]{1,0:T(8,128)S(1)}, f32[8,2048]{1,0:T(8,128)S(1)}, u32[]{:S(2)}, u32[]{:S(2)}) %collective-permute-start.27) | collective-permute-done | bytes 65568 | tf_op jit(solution)/shard_map/ppermute | solution.py:217
  77.1 1.6 %collective-permute-start.36 = (f32[8,512]{1,0:T(8,128)S(1)}, f32[8,512]{1,0:T(8,128)S(1)}, u32[]{:S(2)}, u32[]{:S(2)}) collective-permute-start(f32[8,512]{1,0:T(8,128)S(1)} %get-tuple-element.56.refs_0_), channel_id=1, source_target_pairs={{0,2},{1,3},{2,0},{3,1},{4,6},{5,7},{6,4},{7,5},{8,10},{9,11},{10,... | collective-permute-start | bytes 49160 | tf_op jit(solution)/shard_map/ppermute | solution.py:217
  78.8 0.2 collective-permute-start.35
  79.0 1.2 collective-permute-start.23
  80.2 0.8 collective-permute-start.22
  80.9 3.0 %collective-permute-start.43 = (f32[8,512]{1,0:T(8,128)S(1)}, f32[8,512]{1,0:T(8,128)S(1)}, u32[]{:S(2)}, u32[]{:S(2)}) collective-permute-start(f32[8,512]{1,0:T(8,128)S(1)} %shard_sum.3.refs_8_), channel_id=1, source_target_pairs={{0,24},{4,28},{8,16},{12,20},{16,8},{20,12},{24,0},{28,4},{1,25},{... | collective-permute-start | bytes 49160 | tf_op jit(solution)/shard_map/ppermute | solution.py:217
  83.9 1.3 %collective-permute-start.33 = (f32[8,1536]{1,0:T(8,128)S(1)}, f32[8,1536]{1,0:T(8,128)S(1)}, u32[]{:S(2)}, u32[]{:S(2)}) collective-permute-start(f32[8,1536]{1,0:T(8,128)S(1)} %get-tuple-element.55.refs_0_), channel_id=1, source_target_pairs={{0,24},{4,28},{8,16},{12,20},{16,8},{20,12},{24,0},{28,4},{1,25},{... | collective-permute-start | bytes 147464 | tf_op jit(solution)/shard_map/ppermute | solution.py:217
  85.2 1.7 %collective-permute-start.31 = (f32[8,1536]{1,0:T(8,128)S(1)}, f32[8,1536]{1,0:T(8,128)S(1)}, u32[]{:S(2)}, u32[]{:S(2)}) collective-permute-start(f32[8,1536]{1,0:T(8,128)S(1)} %get-tuple-element.55.refs_0_), channel_id=1, source_target_pairs={{0,16},{4,20},{8,24},{12,28},{16,0},{20,4},{24,8},{28,12},{1,17},{... | collective-permute-start | bytes 147464 | tf_op jit(solution)/shard_map/ppermute | solution.py:217
  86.9 1.4 %collective-permute-start.29 = (f32[8,1536]{1,0:T(8,128)S(1)}, f32[8,1536]{1,0:T(8,128)S(1)}, u32[]{:S(2)}, u32[]{:S(2)}) collective-permute-start(f32[8,1536]{1,0:T(8,128)S(1)} %get-tuple-element.55.refs_0_), channel_id=1, source_target_pairs={{0,8},{4,12},{8,0},{12,4},{16,24},{20,28},{24,16},{28,20},{1,9},{5... | collective-permute-start | bytes 147464 | tf_op jit(solution)/shard_map/ppermute | solution.py:217
  88.3 0.6 collective-permute-start.39
  88.9 1.5 %collective-permute-start.38 = (f32[8,512]{1,0:T(8,128)S(1)}, f32[8,512]{1,0:T(8,128)S(1)}, u32[]{:S(2)}, u32[]{:S(2)}) collective-permute-start(f32[8,512]{1,0:T(8,128)S(1)} %shard_sum.3.refs_8_), channel_id=1, source_target_pairs={{0,4},{4,0},{8,12},{12,8},{16,20},{20,16},{24,28},{28,24},{1,5},{5... | collective-permute-start | bytes 49160 | tf_op jit(solution)/shard_map/ppermute | solution.py:217
  90.4 1.8 %collective-permute-done.39.refs_10_ = f32[8,512]{1,0:T(8,128)S(1)} collective-permute-done((f32[8,512]{1,0:T(8,128)S(1)}, f32[8,512]{1,0:T(8,128)S(1)}, u32[]{:S(2)}, u32[]{:S(2)}) %collective-permute-start.39) | collective-permute-done | bytes 16416 | tf_op jit(solution)/shard_map/ppermute | solution.py:217
  92.3 1.5 %collective-permute-start.44 = (f32[8,512]{1,0:T(8,128)S(1)}, f32[8,512]{1,0:T(8,128)S(1)}, u32[]{:S(2)}, u32[]{:S(2)}) collective-permute-start(f32[8,512]{1,0:T(8,128)S(1)} %collective-permute-done.43.refs_14_), channel_id=1, source_target_pairs={{0,4},{4,0},{8,12},{12,8},{16,20},{20,16},{24,28},{28,24},{1,5},{5... | collective-permute-start | bytes 49160 | tf_op jit(solution)/shard_map/ppermute | solution.py:217
  93.8 0.5 collective-permute-start.42
  94.3 1.9 %collective-permute-done.44.refs_15_ = f32[8,512]{1,0:T(8,128)S(1)} collective-permute-done((f32[8,512]{1,0:T(8,128)S(1)}, f32[8,512]{1,0:T(8,128)S(1)}, u32[]{:S(2)}, u32[]{:S(2)}) %collective-permute-start.44) | collective-permute-done | bytes 16416 | tf_op jit(solution)/shard_map/ppermute | solution.py:217
  96.2 1.5 %collective-permute-start.28 = (f32[8,1536]{1,0:T(8,128)S(1)}, f32[8,1536]{1,0:T(8,128)S(1)}, u32[]{:S(2)}, u32[]{:S(2)}) collective-permute-start(f32[8,1536]{1,0:T(8,128)S(1)} %get-tuple-element.55.refs_0_), channel_id=1, source_target_pairs={{0,4},{4,0},{8,12},{12,8},{16,20},{20,16},{24,28},{28,24},{1,5},{5... | collective-permute-start | bytes 147464 | tf_op jit(solution)/shard_map/ppermute | solution.py:217
  97.7 0.5 collective-permute-start.40
  98.2 1.5 %collective-permute-start.34 = (f32[8,1536]{1,0:T(8,128)S(1)}, f32[8,1536]{1,0:T(8,128)S(1)}, u32[]{:S(2)}, u32[]{:S(2)}) collective-permute-start(f32[8,1536]{1,0:T(8,128)S(1)} %collective-permute-done.33.refs_6_), channel_id=1, source_target_pairs={{0,4},{4,0},{8,12},{12,8},{16,20},{20,16},{24,28},{28,24},{1,5},{5... | collective-permute-start | bytes 147464 | tf_op jit(solution)/shard_map/ppermute | solution.py:217
  99.7 0.5 collective-permute-start.32
  100.3 1.5 %collective-permute-start.30 = (f32[8,1536]{1,0:T(8,128)S(1)}, f32[8,1536]{1,0:T(8,128)S(1)}, u32[]{:S(2)}, u32[]{:S(2)}) collective-permute-start(f32[8,1536]{1,0:T(8,128)S(1)} %collective-permute-done.29.refs_2_), channel_id=1, source_target_pairs={{0,4},{4,0},{8,12},{12,8},{16,20},{20,16},{24,28},{28,24},{1,5},{5... | collective-permute-start | bytes 147464 | tf_op jit(solution)/shard_map/ppermute | solution.py:217
  101.8 7.1 %basis.1 = (f32[64,64]{1,0:T(8,128)S(1)}, f32[64,64]{1,0:T(8,128)S(1)}, bf16[512,256]{1,0:T(8,128)(2,1)S(1)}, bf16[1536,256]{1,0:T(8,128)(2,1)S(1)}) custom-call(f32[64,2048]{1,0:T(8,128)S(1)} %get-tuple-element.42.left, f32[64,64]{1,0:T(8,128)S(1)} %get-tuple-element.43.gram_up, f32[64,64]{1,0:T(8,128)S(1)} %get-tuple-element.44.refs_0_, ...), custom_call_target="tpu_custom_call" | custom-call | flops 1000000000 | bytes 1687552 | tf_op jit(solution)/shard_map/basis/pallas_call | solution.py:212
  108.9 0.8 right_factor.1
  109.7 1.4 %collective-permute-start.46 = (f32[8,128]{1,0:T(8,128)S(1)}, f32[8,128]{1,0:T(8,128)S(1)}, u32[]{:S(2)}, u32[]{:S(2)}) collective-permute-start(f32[8,128]{1,0:T(8,128)S(1)} %get-tuple-element.59.refs_0_), channel_id=1, source_target_pairs={{0,2},{1,3},{2,0},{3,1},{4,6},{5,7},{6,4},{7,5},{8,10},{9,11},{10,... | collective-permute-start | bytes 12296 | tf_op jit(solution)/shard_map/ppermute | solution.py:217
  111.1 0.5 collective-permute-start.45
  111.6 4.6 %new_error.1 = (bf16[1,512,1536]{2,1,0:T(8,128)(2,1)}, bf16[1,1536,512]{2,1,0:T(8,128)(2,1)}) custom-call(bf16[1,512,1536]{2,1,0:T(8,128)(2,1)S(1)} %copy-done.1, bf16[1,512,1536]{2,1,0:T(8,128)(2,1)S(1)} %copy-done.3, bf16[1,1536,512]{2,1,0:T(8,128)(2,1)} %gd.5, bf16[1,1536,512]{2,1,0:T(8,128)(2,1)} %ed.5, bf16[512,256]{1,0:T(8,128)(2,1)S(1)} %get-tuple-element.45.lhs_up, ...), custom_call_target="tpu_custom_call" | custom-call | flops 805306368 | bytes 11534336 | tf_op jit(solution)/shard_map/new_error/pallas_call | solution.py:212
  116.2 2.7 %update.1 = (bf16[512,1536]{1,0:T(8,128)(2,1)}, bf16[1536,512]{1,0:T(8,128)(2,1)}) custom-call(bf16[512,256]{1,0:T(8,128)(2,1)S(1)} %get-tuple-element.45.lhs_up, bf16[1536,256]{1,0:T(8,128)(2,1)S(1)} %get-tuple-element.46.lhs_down, bf16[256,2048]{1,0:T(8,128)(2,1)S(1)} %get-tuple-element.57.rhs, f32[8,128]{1,0:T(8,128)S(1)} %get-tuple-element.59.refs_0_, ...), custom_call_target="tpu_custom_call" | custom-call | flops 805306368 | bytes 5263360 | tf_op jit(solution)/shard_map/update/pallas_call | solution.py:212
  (54 shorter events, 0.5 us)
Async XLA Ops:
  2.9 1.4 %copy-start = (bf16[1,512,1536]{2,1,0:T(8,128)(2,1)S(1)}, bf16[1,512,1536]{2,1,0:T(8,128)(2,1)}, u32[]{:S(2)}) copy-start(bf16[1,512,1536]{2,1,0:T(8,128)(2,1)} %gu.5) | copy-start | bytes 4718596
  4.3 1.4 %copy-start.2 = (bf16[1,512,1536]{2,1,0:T(8,128)(2,1)S(1)}, bf16[1,512,1536]{2,1,0:T(8,128)(2,1)}, u32[]{:S(2)}) copy-start(bf16[1,512,1536]{2,1,0:T(8,128)(2,1)} %eu.5) | copy-start | bytes 4718596
  5.8 52.1 %copy-start.1 = (bf16[1,512,1536]{2,1,0:T(8,128)(2,1)S(1)}, bf16[1,512,1536]{2,1,0:T(8,128)(2,1)}, u32[]{:S(2)}) copy-start(bf16[1,512,1536]{2,1,0:T(8,128)(2,1)} %gu.5) | copy-start | bytes 4718596
  10.7 9.3 %collective-permute-start = (f32[4,8,2048]{2,1,0:T(8,128)S(1)}, f32[4,8,2048]{2,1,0:T(8,128)S(1)}, u32[]{:S(2)}, u32[]{:S(2)}) collective-permute-start(f32[4,8,2048]{2,1,0:T(8,128)S(1)} %get-tuple-element.35), channel_id=1, source_target_pairs={{0,4},{4,0},{8,12},{12,8},{16,20},{20,16},{24,28},{28,24},{1,5},{5... | collective-permute-start | bytes 786440 | tf_op jit(solution)/shard_map/ppermute | solution.py:217
  20.1 5.0 %collective-permute-start.1 = (f32[8,2048]{1,0:T(8,128)S(1)}, f32[8,2048]{1,0:T(8,128)S(1)}, u32[]{:S(2)}, u32[]{:S(2)}) collective-permute-start(f32[8,2048]{1,0:T(8,128)S(1)} %get-tuple-element.37), channel_id=1, source_target_pairs={{0,8},{4,12},{8,0},{12,4},{16,24},{20,28},{24,16},{28,20},{1,9},{5... | collective-permute-start | bytes 196616 | tf_op jit(solution)/shard_map/ppermute | solution.py:217
  21.9 6.6 %collective-permute-start.2 = (f32[8,2048]{1,0:T(8,128)S(1)}, f32[8,2048]{1,0:T(8,128)S(1)}, u32[]{:S(2)}, u32[]{:S(2)}) collective-permute-start(f32[8,2048]{1,0:T(8,128)S(1)} %get-tuple-element.38), channel_id=1, source_target_pairs={{0,16},{4,20},{8,24},{12,28},{16,0},{20,4},{24,8},{28,12},{1,17},{... | collective-permute-start | bytes 196616 | tf_op jit(solution)/shard_map/ppermute | solution.py:217
  24.5 6.1 %collective-permute-start.3 = (f32[8,2048]{1,0:T(8,128)S(1)}, f32[8,2048]{1,0:T(8,128)S(1)}, u32[]{:S(2)}, u32[]{:S(2)}) collective-permute-start(f32[8,2048]{1,0:T(8,128)S(1)} %get-tuple-element.39), channel_id=1, source_target_pairs={{0,24},{4,28},{8,16},{12,20},{16,8},{20,12},{24,0},{28,4},{1,25},{... | collective-permute-start | bytes 196616 | tf_op jit(solution)/shard_map/ppermute | solution.py:217
  30.6 3.4 %collective-permute-start.6 = (f32[8,512]{1,0:T(8,128)S(1)}, f32[8,512]{1,0:T(8,128)S(1)}, u32[]{:S(2)}, u32[]{:S(2)}) collective-permute-start(f32[8,512]{1,0:T(8,128)S(1)} %get-tuple-element.40.refs_0_), channel_id=1, source_target_pairs={{0,3},{1,2},{2,1},{3,0},{4,7},{5,6},{6,5},{7,4},{8,11},{9,10},{10,... | collective-permute-start | bytes 49160 | tf_op jit(solution)/shard_map/ppermute | solution.py:217
  30.7 6.2 %collective-permute-start.5 = (f32[8,512]{1,0:T(8,128)S(1)}, f32[8,512]{1,0:T(8,128)S(1)}, u32[]{:S(2)}, u32[]{:S(2)}) collective-permute-start(f32[8,512]{1,0:T(8,128)S(1)} %get-tuple-element.40.refs_0_), channel_id=1, source_target_pairs={{0,2},{1,3},{2,0},{3,1},{4,6},{5,7},{6,4},{7,5},{8,10},{9,11},{10,... | collective-permute-start | bytes 49160 | tf_op jit(solution)/shard_map/ppermute | solution.py:217
  32.2 4.7 %collective-permute-start.4 = (f32[8,512]{1,0:T(8,128)S(1)}, f32[8,512]{1,0:T(8,128)S(1)}, u32[]{:S(2)}, u32[]{:S(2)}) collective-permute-start(f32[8,512]{1,0:T(8,128)S(1)} %get-tuple-element.40.refs_0_), channel_id=1, source_target_pairs={{0,1},{1,0},{2,3},{3,2},{4,5},{5,4},{6,7},{7,6},{8,9},{9,8},{10,11... | collective-permute-start | bytes 49160 | tf_op jit(solution)/shard_map/ppermute | solution.py:217
  32.5 15.3 %collective-permute-start.19 = (f32[8,1536]{1,0:T(8,128)S(1)}, f32[8,1536]{1,0:T(8,128)S(1)}, u32[]{:S(2)}, u32[]{:S(2)}) collective-permute-start(f32[8,1536]{1,0:T(8,128)S(1)} %get-tuple-element.41.refs_8_), channel_id=1, source_target_pairs={{0,24},{4,28},{8,16},{12,20},{16,8},{20,12},{24,0},{28,4},{1,25},{... | collective-permute-start | bytes 147464 | tf_op jit(solution)/shard_map/ppermute | solution.py:217
  33.5 14.9 %collective-permute-start.17 = (f32[8,1536]{1,0:T(8,128)S(1)}, f32[8,1536]{1,0:T(8,128)S(1)}, u32[]{:S(2)}, u32[]{:S(2)}) collective-permute-start(f32[8,1536]{1,0:T(8,128)S(1)} %get-tuple-element.41.refs_8_), channel_id=1, source_target_pairs={{0,16},{4,20},{8,24},{12,28},{16,0},{20,4},{24,8},{28,12},{1,17},{... | collective-permute-start | bytes 147464 | tf_op jit(solution)/shard_map/ppermute | solution.py:217
  34.0 15.9 %collective-permute-start.15 = (f32[8,1536]{1,0:T(8,128)S(1)}, f32[8,1536]{1,0:T(8,128)S(1)}, u32[]{:S(2)}, u32[]{:S(2)}) collective-permute-start(f32[8,1536]{1,0:T(8,128)S(1)} %get-tuple-element.41.refs_8_), channel_id=1, source_target_pairs={{0,8},{4,12},{8,0},{12,4},{16,24},{20,28},{24,16},{28,20},{1,9},{5... | collective-permute-start | bytes 147464 | tf_op jit(solution)/shard_map/ppermute | solution.py:217
  36.9 5.6 %collective-permute-start.12 = (f32[8,512]{1,0:T(8,128)S(1)}, f32[8,512]{1,0:T(8,128)S(1)}, u32[]{:S(2)}, u32[]{:S(2)}) collective-permute-start(f32[8,512]{1,0:T(8,128)S(1)} %shard_sum.2.refs_0_), channel_id=1, source_target_pairs={{0,24},{4,28},{8,16},{12,20},{16,8},{20,12},{24,0},{28,4},{1,25},{... | collective-permute-start | bytes 49160 | tf_op jit(solution)/shard_map/ppermute | solution.py:217
  37.9 5.0 %collective-permute-start.10 = (f32[8,512]{1,0:T(8,128)S(1)}, f32[8,512]{1,0:T(8,128)S(1)}, u32[]{:S(2)}, u32[]{:S(2)}) collective-permute-start(f32[8,512]{1,0:T(8,128)S(1)} %shard_sum.2.refs_0_), channel_id=1, source_target_pairs={{0,16},{4,20},{8,24},{12,28},{16,0},{20,4},{24,8},{28,12},{1,17},{... | collective-permute-start | bytes 49160 | tf_op jit(solution)/shard_map/ppermute | solution.py:217
  42.5 3.7 %collective-permute-start.8 = (f32[8,512]{1,0:T(8,128)S(1)}, f32[8,512]{1,0:T(8,128)S(1)}, u32[]{:S(2)}, u32[]{:S(2)}) collective-permute-start(f32[8,512]{1,0:T(8,128)S(1)} %shard_sum.2.refs_0_), channel_id=1, source_target_pairs={{0,8},{4,12},{8,0},{12,4},{16,24},{20,28},{24,16},{28,20},{1,9},{5... | collective-permute-start | bytes 49160 | tf_op jit(solution)/shard_map/ppermute | solution.py:217
  42.9 9.0 %collective-permute-start.14 = (f32[8,1536]{1,0:T(8,128)S(1)}, f32[8,1536]{1,0:T(8,128)S(1)}, u32[]{:S(2)}, u32[]{:S(2)}) collective-permute-start(f32[8,1536]{1,0:T(8,128)S(1)} %get-tuple-element.41.refs_8_), channel_id=1, source_target_pairs={{0,4},{4,0},{8,12},{12,8},{16,20},{20,16},{24,28},{28,24},{1,5},{5... | collective-permute-start | bytes 147464 | tf_op jit(solution)/shard_map/ppermute | solution.py:217
  46.3 4.1 %collective-permute-start.7 = (f32[8,512]{1,0:T(8,128)S(1)}, f32[8,512]{1,0:T(8,128)S(1)}, u32[]{:S(2)}, u32[]{:S(2)}) collective-permute-start(f32[8,512]{1,0:T(8,128)S(1)} %shard_sum.2.refs_0_), channel_id=1, source_target_pairs={{0,4},{4,0},{8,12},{12,8},{16,20},{20,16},{24,28},{28,24},{1,5},{5... | collective-permute-start | bytes 49160 | tf_op jit(solution)/shard_map/ppermute | solution.py:217
  47.8 10.0 %collective-permute-start.20 = (f32[8,1536]{1,0:T(8,128)S(1)}, f32[8,1536]{1,0:T(8,128)S(1)}, u32[]{:S(2)}, u32[]{:S(2)}) collective-permute-start(f32[8,1536]{1,0:T(8,128)S(1)} %collective-permute-done.19.refs_14_), channel_id=1, source_target_pairs={{0,4},{4,0},{8,12},{12,8},{16,20},{20,16},{24,28},{28,24},{1,5},{5... | collective-permute-start | bytes 147464 | tf_op jit(solution)/shard_map/ppermute | solution.py:217
  48.3 9.5 %collective-permute-start.18 = (f32[8,1536]{1,0:T(8,128)S(1)}, f32[8,1536]{1,0:T(8,128)S(1)}, u32[]{:S(2)}, u32[]{:S(2)}) collective-permute-start(f32[8,1536]{1,0:T(8,128)S(1)} %collective-permute-done.17.refs_12_), channel_id=1, source_target_pairs={{0,4},{4,0},{8,12},{12,8},{16,20},{20,16},{24,28},{28,24},{1,5},{5... | collective-permute-start | bytes 147464 | tf_op jit(solution)/shard_map/ppermute | solution.py:217
  49.8 8.0 %collective-permute-start.16 = (f32[8,1536]{1,0:T(8,128)S(1)}, f32[8,1536]{1,0:T(8,128)S(1)}, u32[]{:S(2)}, u32[]{:S(2)}) collective-permute-start(f32[8,1536]{1,0:T(8,128)S(1)} %collective-permute-done.15.refs_10_), channel_id=1, source_target_pairs={{0,4},{4,0},{8,12},{12,8},{16,20},{20,16},{24,28},{28,24},{1,5},{5... | collective-permute-start | bytes 147464 | tf_op jit(solution)/shard_map/ppermute | solution.py:217
  50.4 3.8 %collective-permute-start.13 = (f32[8,512]{1,0:T(8,128)S(1)}, f32[8,512]{1,0:T(8,128)S(1)}, u32[]{:S(2)}, u32[]{:S(2)}) collective-permute-start(f32[8,512]{1,0:T(8,128)S(1)} %collective-permute-done.12.refs_6_), channel_id=1, source_target_pairs={{0,4},{4,0},{8,12},{12,8},{16,20},{20,16},{24,28},{28,24},{1,5},{5... | collective-permute-start | bytes 49160 | tf_op jit(solution)/shard_map/ppermute | solution.py:217
  51.9 3.7 %collective-permute-start.11 = (f32[8,512]{1,0:T(8,128)S(1)}, f32[8,512]{1,0:T(8,128)S(1)}, u32[]{:S(2)}, u32[]{:S(2)}) collective-permute-start(f32[8,512]{1,0:T(8,128)S(1)} %collective-permute-done.10.refs_4_), channel_id=1, source_target_pairs={{0,4},{4,0},{8,12},{12,8},{16,20},{20,16},{24,28},{28,24},{1,5},{5... | collective-permute-start | bytes 49160 | tf_op jit(solution)/shard_map/ppermute | solution.py:217
  54.1 3.7 %collective-permute-start.9 = (f32[8,512]{1,0:T(8,128)S(1)}, f32[8,512]{1,0:T(8,128)S(1)}, u32[]{:S(2)}, u32[]{:S(2)}) collective-permute-start(f32[8,512]{1,0:T(8,128)S(1)} %collective-permute-done.8.refs_2_), channel_id=1, source_target_pairs={{0,4},{4,0},{8,12},{12,8},{16,20},{20,16},{24,28},{28,24},{1,5},{5... | collective-permute-start | bytes 49160 | tf_op jit(solution)/shard_map/ppermute | solution.py:217
  62.9 6.4 %collective-permute-start.24 = (f32[4,8,2048]{2,1,0:T(8,128)S(1)}, f32[4,8,2048]{2,1,0:T(8,128)S(1)}, u32[]{:S(2)}, u32[]{:S(2)}) collective-permute-start(f32[4,8,2048]{2,1,0:T(8,128)S(1)} %get-tuple-element.50), channel_id=1, source_target_pairs={{0,4},{4,0},{8,12},{12,8},{16,20},{20,16},{24,28},{28,24},{1,5},{5... | collective-permute-start | bytes 786440 | tf_op jit(solution)/shard_map/ppermute | solution.py:217
  69.4 4.5 %collective-permute-start.25 = (f32[8,2048]{1,0:T(8,128)S(1)}, f32[8,2048]{1,0:T(8,128)S(1)}, u32[]{:S(2)}, u32[]{:S(2)}) collective-permute-start(f32[8,2048]{1,0:T(8,128)S(1)} %get-tuple-element.52), channel_id=1, source_target_pairs={{0,8},{4,12},{8,0},{12,4},{16,24},{20,28},{24,16},{28,20},{1,9},{5... | collective-permute-start | bytes 196616 | tf_op jit(solution)/shard_map/ppermute | solution.py:217
  69.5 5.2 %collective-permute-start.26 = (f32[8,2048]{1,0:T(8,128)S(1)}, f32[8,2048]{1,0:T(8,128)S(1)}, u32[]{:S(2)}, u32[]{:S(2)}) collective-permute-start(f32[8,2048]{1,0:T(8,128)S(1)} %get-tuple-element.53), channel_id=1, source_target_pairs={{0,16},{4,20},{8,24},{12,28},{16,0},{20,4},{24,8},{28,12},{1,17},{... | collective-permute-start | bytes 196616 | tf_op jit(solution)/shard_map/ppermute | solution.py:217
  70.9 6.1 %collective-permute-start.27 = (f32[8,2048]{1,0:T(8,128)S(1)}, f32[8,2048]{1,0:T(8,128)S(1)}, u32[]{:S(2)}, u32[]{:S(2)}) collective-permute-start(f32[8,2048]{1,0:T(8,128)S(1)} %get-tuple-element.54), channel_id=1, source_target_pairs={{0,24},{4,28},{8,16},{12,20},{16,8},{20,12},{24,0},{28,4},{1,25},{... | collective-permute-start | bytes 196616 | tf_op jit(solution)/shard_map/ppermute | solution.py:217
  77.0 3.9 %collective-permute-start.37 = (f32[8,512]{1,0:T(8,128)S(1)}, f32[8,512]{1,0:T(8,128)S(1)}, u32[]{:S(2)}, u32[]{:S(2)}) collective-permute-start(f32[8,512]{1,0:T(8,128)S(1)} %get-tuple-element.56.refs_0_), channel_id=1, source_target_pairs={{0,3},{1,2},{2,1},{3,0},{4,7},{5,6},{6,5},{7,4},{8,11},{9,10},{10,... | collective-permute-start | bytes 49160 | tf_op jit(solution)/shard_map/ppermute | solution.py:217
  77.1 3.8 %collective-permute-start.36 = (f32[8,512]{1,0:T(8,128)S(1)}, f32[8,512]{1,0:T(8,128)S(1)}, u32[]{:S(2)}, u32[]{:S(2)}) collective-permute-start(f32[8,512]{1,0:T(8,128)S(1)} %get-tuple-element.56.refs_0_), channel_id=1, source_target_pairs={{0,2},{1,3},{2,0},{3,1},{4,6},{5,7},{6,4},{7,5},{8,10},{9,11},{10,... | collective-permute-start | bytes 49160 | tf_op jit(solution)/shard_map/ppermute | solution.py:217
  78.8 2.2 %collective-permute-start.35 = (f32[8,512]{1,0:T(8,128)S(1)}, f32[8,512]{1,0:T(8,128)S(1)}, u32[]{:S(2)}, u32[]{:S(2)}) collective-permute-start(f32[8,512]{1,0:T(8,128)S(1)} %get-tuple-element.56.refs_0_), channel_id=1, source_target_pairs={{0,1},{1,0},{2,3},{3,2},{4,5},{5,4},{6,7},{7,6},{8,9},{9,8},{10,11... | collective-permute-start | bytes 49160 | tf_op jit(solution)/shard_map/ppermute | solution.py:217
  79.0 4.9 %collective-permute-start.23 = (f32[64,64]{1,0:T(8,128)S(1)}, f32[64,64]{1,0:T(8,128)S(1)}, u32[]{:S(2)}, u32[]{:S(2)}) collective-permute-start(f32[64,64]{1,0:T(8,128)S(1)} %get-tuple-element.44.refs_0_), channel_id=1, source_target_pairs={{0,3},{1,2},{2,1},{3,0},{4,7},{5,6},{6,5},{7,4},{8,11},{9,10},{10,... | collective-permute-start | bytes 49160 | tf_op jit(solution)/shard_map/ppermute | solution.py:217
  80.2 5.1 %collective-permute-start.22 = (f32[64,64]{1,0:T(8,128)S(1)}, f32[64,64]{1,0:T(8,128)S(1)}, u32[]{:S(2)}, u32[]{:S(2)}) collective-permute-start(f32[64,64]{1,0:T(8,128)S(1)} %get-tuple-element.44.refs_0_), channel_id=1, source_target_pairs={{0,2},{1,3},{2,0},{3,1},{4,6},{5,7},{6,4},{7,5},{8,10},{9,11},{10,... | collective-permute-start | bytes 49160 | tf_op jit(solution)/shard_map/ppermute | solution.py:217
  80.9 6.0 %collective-permute-start.21 = (f32[64,64]{1,0:T(8,128)S(1)}, f32[64,64]{1,0:T(8,128)S(1)}, u32[]{:S(2)}, u32[]{:S(2)}) collective-permute-start(f32[64,64]{1,0:T(8,128)S(1)} %get-tuple-element.44.refs_0_), channel_id=1, source_target_pairs={{0,1},{1,0},{2,3},{3,2},{4,5},{5,4},{6,7},{7,6},{8,9},{9,8},{10,11... | collective-permute-start | bytes 49160 | tf_op jit(solution)/shard_map/ppermute | solution.py:217
  80.9 7.4 %collective-permute-start.43 = (f32[8,512]{1,0:T(8,128)S(1)}, f32[8,512]{1,0:T(8,128)S(1)}, u32[]{:S(2)}, u32[]{:S(2)}) collective-permute-start(f32[8,512]{1,0:T(8,128)S(1)} %shard_sum.3.refs_8_), channel_id=1, source_target_pairs={{0,24},{4,28},{8,16},{12,20},{16,8},{20,12},{24,0},{28,4},{1,25},{... | collective-permute-start | bytes 49160 | tf_op jit(solution)/shard_map/ppermute | solution.py:217
  83.9 5.0 %collective-permute-start.41 = (f32[8,512]{1,0:T(8,128)S(1)}, f32[8,512]{1,0:T(8,128)S(1)}, u32[]{:S(2)}, u32[]{:S(2)}) collective-permute-start(f32[8,512]{1,0:T(8,128)S(1)} %shard_sum.3.refs_8_), channel_id=1, source_target_pairs={{0,16},{4,20},{8,24},{12,28},{16,0},{20,4},{24,8},{28,12},{1,17},{... | collective-permute-start | bytes 49160 | tf_op jit(solution)/shard_map/ppermute | solution.py:217
  83.9 14.3 %collective-permute-start.33 = (f32[8,1536]{1,0:T(8,128)S(1)}, f32[8,1536]{1,0:T(8,128)S(1)}, u32[]{:S(2)}, u32[]{:S(2)}) collective-permute-start(f32[8,1536]{1,0:T(8,128)S(1)} %get-tuple-element.55.refs_0_), channel_id=1, source_target_pairs={{0,24},{4,28},{8,16},{12,20},{16,8},{20,12},{24,0},{28,4},{1,25},{... | collective-permute-start | bytes 147464 | tf_op jit(solution)/shard_map/ppermute | solution.py:217
  85.2 14.5 %collective-permute-start.31 = (f32[8,1536]{1,0:T(8,128)S(1)}, f32[8,1536]{1,0:T(8,128)S(1)}, u32[]{:S(2)}, u32[]{:S(2)}) collective-permute-start(f32[8,1536]{1,0:T(8,128)S(1)} %get-tuple-element.55.refs_0_), channel_id=1, source_target_pairs={{0,16},{4,20},{8,24},{12,28},{16,0},{20,4},{24,8},{28,12},{1,17},{... | collective-permute-start | bytes 147464 | tf_op jit(solution)/shard_map/ppermute | solution.py:217
  86.9 13.3 %collective-permute-start.29 = (f32[8,1536]{1,0:T(8,128)S(1)}, f32[8,1536]{1,0:T(8,128)S(1)}, u32[]{:S(2)}, u32[]{:S(2)}) collective-permute-start(f32[8,1536]{1,0:T(8,128)S(1)} %get-tuple-element.55.refs_0_), channel_id=1, source_target_pairs={{0,8},{4,12},{8,0},{12,4},{16,24},{20,28},{24,16},{28,20},{1,9},{5... | collective-permute-start | bytes 147464 | tf_op jit(solution)/shard_map/ppermute | solution.py:217
  88.3 4.0 %collective-permute-start.39 = (f32[8,512]{1,0:T(8,128)S(1)}, f32[8,512]{1,0:T(8,128)S(1)}, u32[]{:S(2)}, u32[]{:S(2)}) collective-permute-start(f32[8,512]{1,0:T(8,128)S(1)} %shard_sum.3.refs_8_), channel_id=1, source_target_pairs={{0,8},{4,12},{8,0},{12,4},{16,24},{20,28},{24,16},{28,20},{1,9},{5... | collective-permute-start | bytes 49160 | tf_op jit(solution)/shard_map/ppermute | solution.py:217
  88.9 4.8 %collective-permute-start.38 = (f32[8,512]{1,0:T(8,128)S(1)}, f32[8,512]{1,0:T(8,128)S(1)}, u32[]{:S(2)}, u32[]{:S(2)}) collective-permute-start(f32[8,512]{1,0:T(8,128)S(1)} %shard_sum.3.refs_8_), channel_id=1, source_target_pairs={{0,4},{4,0},{8,12},{12,8},{16,20},{20,16},{24,28},{28,24},{1,5},{5... | collective-permute-start | bytes 49160 | tf_op jit(solution)/shard_map/ppermute | solution.py:217
  92.3 3.9 %collective-permute-start.44 = (f32[8,512]{1,0:T(8,128)S(1)}, f32[8,512]{1,0:T(8,128)S(1)}, u32[]{:S(2)}, u32[]{:S(2)}) collective-permute-start(f32[8,512]{1,0:T(8,128)S(1)} %collective-permute-done.43.refs_14_), channel_id=1, source_target_pairs={{0,4},{4,0},{8,12},{12,8},{16,20},{20,16},{24,28},{28,24},{1,5},{5... | collective-permute-start | bytes 49160 | tf_op jit(solution)/shard_map/ppermute | solution.py:217
  93.8 3.9 %collective-permute-start.42 = (f32[8,512]{1,0:T(8,128)S(1)}, f32[8,512]{1,0:T(8,128)S(1)}, u32[]{:S(2)}, u32[]{:S(2)}) collective-permute-start(f32[8,512]{1,0:T(8,128)S(1)} %collective-permute-done.41.refs_12_), channel_id=1, source_target_pairs={{0,4},{4,0},{8,12},{12,8},{16,20},{20,16},{24,28},{28,24},{1,5},{5... | collective-permute-start | bytes 49160 | tf_op jit(solution)/shard_map/ppermute | solution.py:217
  96.2 12.7 %collective-permute-start.28 = (f32[8,1536]{1,0:T(8,128)S(1)}, f32[8,1536]{1,0:T(8,128)S(1)}, u32[]{:S(2)}, u32[]{:S(2)}) collective-permute-start(f32[8,1536]{1,0:T(8,128)S(1)} %get-tuple-element.55.refs_0_), channel_id=1, source_target_pairs={{0,4},{4,0},{8,12},{12,8},{16,20},{20,16},{24,28},{28,24},{1,5},{5... | collective-permute-start | bytes 147464 | tf_op jit(solution)/shard_map/ppermute | solution.py:217
  97.7 11.1 %collective-permute-start.40 = (f32[8,512]{1,0:T(8,128)S(1)}, f32[8,512]{1,0:T(8,128)S(1)}, u32[]{:S(2)}, u32[]{:S(2)}) collective-permute-start(f32[8,512]{1,0:T(8,128)S(1)} %collective-permute-done.39.refs_10_), channel_id=1, source_target_pairs={{0,4},{4,0},{8,12},{12,8},{16,20},{20,16},{24,28},{28,24},{1,5},{5... | collective-permute-start | bytes 49160 | tf_op jit(solution)/shard_map/ppermute | solution.py:217
  98.2 10.6 %collective-permute-start.34 = (f32[8,1536]{1,0:T(8,128)S(1)}, f32[8,1536]{1,0:T(8,128)S(1)}, u32[]{:S(2)}, u32[]{:S(2)}) collective-permute-start(f32[8,1536]{1,0:T(8,128)S(1)} %collective-permute-done.33.refs_6_), channel_id=1, source_target_pairs={{0,4},{4,0},{8,12},{12,8},{16,20},{20,16},{24,28},{28,24},{1,5},{5... | collective-permute-start | bytes 147464 | tf_op jit(solution)/shard_map/ppermute | solution.py:217
  99.7 9.1 %collective-permute-start.32 = (f32[8,1536]{1,0:T(8,128)S(1)}, f32[8,1536]{1,0:T(8,128)S(1)}, u32[]{:S(2)}, u32[]{:S(2)}) collective-permute-start(f32[8,1536]{1,0:T(8,128)S(1)} %collective-permute-done.31.refs_4_), channel_id=1, source_target_pairs={{0,4},{4,0},{8,12},{12,8},{16,20},{20,16},{24,28},{28,24},{1,5},{5... | collective-permute-start | bytes 147464 | tf_op jit(solution)/shard_map/ppermute | solution.py:217
  100.3 8.6 %collective-permute-start.30 = (f32[8,1536]{1,0:T(8,128)S(1)}, f32[8,1536]{1,0:T(8,128)S(1)}, u32[]{:S(2)}, u32[]{:S(2)}) collective-permute-start(f32[8,1536]{1,0:T(8,128)S(1)} %collective-permute-done.29.refs_2_), channel_id=1, source_target_pairs={{0,4},{4,0},{8,12},{12,8},{16,20},{20,16},{24,28},{28,24},{1,5},{5... | collective-permute-start | bytes 147464 | tf_op jit(solution)/shard_map/ppermute | solution.py:217
  101.8 9.8 %copy-start.3 = (bf16[1,512,1536]{2,1,0:T(8,128)(2,1)S(1)}, bf16[1,512,1536]{2,1,0:T(8,128)(2,1)}, u32[]{:S(2)}) copy-start(bf16[1,512,1536]{2,1,0:T(8,128)(2,1)} %eu.5) | copy-start | bytes 4718596
  109.7 6.6 %collective-permute-start.47 = (f32[8,128]{1,0:T(8,128)S(1)}, f32[8,128]{1,0:T(8,128)S(1)}, u32[]{:S(2)}, u32[]{:S(2)}) collective-permute-start(f32[8,128]{1,0:T(8,128)S(1)} %get-tuple-element.59.refs_0_), channel_id=1, source_target_pairs={{0,3},{1,2},{2,1},{3,0},{4,7},{5,6},{6,5},{7,4},{8,11},{9,10},{10,... | collective-permute-start | bytes 12296 | tf_op jit(solution)/shard_map/ppermute | solution.py:217
  109.7 6.5 %collective-permute-start.46 = (f32[8,128]{1,0:T(8,128)S(1)}, f32[8,128]{1,0:T(8,128)S(1)}, u32[]{:S(2)}, u32[]{:S(2)}) collective-permute-start(f32[8,128]{1,0:T(8,128)S(1)} %get-tuple-element.59.refs_0_), channel_id=1, source_target_pairs={{0,2},{1,3},{2,0},{3,1},{4,6},{5,7},{6,4},{7,5},{8,10},{9,11},{10,... | collective-permute-start | bytes 12296 | tf_op jit(solution)/shard_map/ppermute | solution.py:217
  111.1 5.1 %collective-permute-start.45 = (f32[8,128]{1,0:T(8,128)S(1)}, f32[8,128]{1,0:T(8,128)S(1)}, u32[]{:S(2)}, u32[]{:S(2)}) collective-permute-start(f32[8,128]{1,0:T(8,128)S(1)} %get-tuple-element.59.refs_0_), channel_id=1, source_target_pairs={{0,1},{1,0},{2,3},{3,2},{4,5},{5,4},{6,7},{7,6},{8,9},{9,8},{10,11... | collective-permute-start | bytes 12296 | tf_op jit(solution)/shard_map/ppermute | solution.py:217

commit v2 on v1

--- a/solution.py
+++ b/solution.py
@@ -33,42 +33,35 @@
     return lax.dot_general(a, b, (dims, ((), ())), precision=precision, preferred_element_type=F32)
 
 
-def scatter_chunks(total, stage, keep, send):
-    n_dp, per, _ = stage.shape
-    me = lax.axis_index("dp")
+def scatter_chunks(total, chunks):
+    n_dp, per, _ = chunks.shape
     for c in range(n_dp):
-        stage[c] = total[c * per : (c + 1) * per, :]
-    for d in range(n_dp):
-        (send if d % 2 else keep)[d // 2] = stage[lax.bitwise_xor(me, d)]
-
-
-def gather_chunks(pieces, stage, total, start):
-    n_dp, per, _ = stage.shape
-    width = pieces[0].shape[1]
-    me = lax.axis_index("dp")
-    for d, piece in enumerate(pieces):
-        stage[lax.bitwise_xor(me, d), :, :width] = piece[...]
+        chunks[c] = total[c * per : (c + 1) * per, :]
+
+
+def gather_chunks(chunks, total):
+    n_dp, per, _ = chunks.shape
     for c in range(n_dp):
-        total[c * per : (c + 1) * per, start : start + width] = stage[c, :, :width]
-
-
-def left_kernel(gu, eu, gd, ed, qu, qd, keep, send, qsu, qsd, total, stage):
+        total[c * per : (c + 1) * per, :] = chunks[c]
+
+
+def left_kernel(gu, eu, gd, ed, qu, qd, chunks, qsu, qsd, total):
     step = pl.program_id(0)
-    rank = qu.shape[1]
-    rows = total.shape[1] - qu.shape[0]
+    rank, ff = qu.shape
+    rows = total.shape[1] - ff
 
     @pl.when(step == 0)
     def _():
         for q, qs in ((qu, qsu), (qd, qsd)):
             first, second, third = split3(q[...])
-            qs[:, :rank] = first
-            qs[:, rank : 2 * rank] = second
-            qs[:, 2 * rank : 3 * rank] = third
-            qs[:, 3 * rank :] = jnp.zeros_like(third)
+            qs[:rank, :] = first
+            qs[rank : 2 * rank, :] = second
+            qs[2 * rank : 3 * rank, :] = third
+            qs[3 * rank :, :] = jnp.zeros_like(third)
 
     def term(g, e, qs, start):
         block = g.shape[1]
-        t = dot(g[0], qs[...]) + dot(e[0], qs[...])
+        t = dot(g[0], qs[...], ((1,), (1,))) + dot(e[0], qs[...], ((1,), (1,)))
         t = (t[:, : 2 * rank] + t[:, 2 * rank :]).T
         total[:, pl.ds(pl.multiple_of(start + step * block, 128), block)] = t[:rank] + t[rank:]
 
@@ -77,13 +70,11 @@
 
     @pl.when(step == STEPS - 1)
     def _():
-        scatter_chunks(total, stage, keep, send)
-
-
-def right_kernel(n_dp, gu, eu, gd, ed, *refs):
+        scatter_chunks(total, chunks)
+
+
+def right_kernel(gu, eu, gd, ed, gathered, left, gram_up, gram_down, chunks, pieces, total):
     step = pl.program_id(0)
-    up, down = refs[:n_dp], refs[n_dp : 2 * n_dp]
-    left, gram_up, gram_down, keep, send, pieces, total, stage = refs[2 * n_dp :]
     rank = left.shape[0]
     rows = gu.shape[1]
     ff = left.shape[1] - rows
@@ -92,8 +83,7 @@
 
     @pl.when(step == 0)
     def _():
-        gather_chunks(up, stage, left, 0)
-        gather_chunks(down, stage, left, rows)
+        gather_chunks(gathered, left)
         for i, piece in enumerate(split3(left[...])):
             pieces[i * rank : (i + 1) * rank, :] = piece
         nt = ((1,), (1,))
@@ -111,22 +101,22 @@
 
     @pl.when(step == STEPS - 1)
     def _():
-        scatter_chunks(total, stage, keep, send)
-
-
-def half_kernel(keep, got, *outs):
-    for i, out in enumerate(outs):
-        out[...] = keep[i] + got[i]
-
-
-def mean_kernel(n_dp, split, *refs):
-    total = tree_sum(ref[...] for ref in refs[:-2]) / n_dp
-    refs[-2][...] = total[:, :split]
-    refs[-1][...] = total[:, split:]
-
-
-def sum_kernel(*refs):
-    refs[-1][...] = tree_sum(ref[...] for ref in refs[:-1])
+        scatter_chunks(total, chunks)
+
+
+def mean_kernel(shared, got, own, parts):
+    n_dp = got.shape[0]
+    total = tree_sum(got[d] for d in range(n_dp)) / n_dp
+    own[...] = total
+    for t in range(parts.shape[0]):
+        parts[t] = total[:, shared]
+
+
+def copies_kernel(shared, own, parts, out):
+    total = tree_sum(parts[t] for t in range(parts.shape[0]))
+    for d in range(out.shape[0]):
+        out[d] = own[...]
+        out[d, :, shared] = total
 
 
 def basis_kernel(left, gram_up, *refs):
@@ -159,13 +149,9 @@
         lhs[:, 3 * rank :] = second
 
 
-def factor_kernel(n_dp, inv_up, inv_down, *refs):
-    up, down = refs[:n_dp], refs[n_dp : 2 * n_dp]
-    rhs, sq_up, sq_down, total, stage = refs[2 * n_dp :]
+def factor_kernel(ff, inv_up, inv_down, gathered, rhs, sq_up, sq_down, total):
     rank = total.shape[0]
-    ff = up[0].shape[1]
-    gather_chunks(up, stage, total, 0)
-    gather_chunks(down, stage, total, ff)
+    gather_chunks(gathered, total)
     for inv, part, sq in ((inv_up, slice(0, ff), sq_up), (inv_down, slice(ff, None), sq_down)):
         right = dot(inv[...], total[:, part], precision=HIGHEST)
         sq[...] = jnp.full(sq.shape, jnp.sum(right * right), F32)
@@ -217,74 +203,59 @@
     return lax.ppermute(x, axis, pairs)
 
 
-def mean_over_replicas(keep, send, split):
-    n_dp = lax.axis_size("dp")
-    half, per, width = keep.shape
-    got = swap(send, "dp", 1)
-    parts = call(half_kernel, [shaped(per, width)] * half, keep, got, name="half_sum")
-    got = [parts[0]] + [swap(parts[j], "dp", 2 * j) for j in range(1, half)]
-    outs = [shaped(per, split), shaped(per, width - split)]
-    return call(functools.partial(mean_kernel, n_dp, split), outs, *got, name="replica_mean")
-
-
-def sum_over_shards(x):
-    got = [x] + [swap(x, "tensor", j) for j in range(1, lax.axis_size("tensor"))]
-    return call(sum_kernel, shaped(*x.shape), *got, name="shard_sum")
-
-
-def gather(x):
-    n_dp = lax.axis_size("dp")
-    near = [x] + [swap(x, "dp", d) for d in range(2, n_dp, 2)]
-    far = [swap(p, "dp", 1) for p in near]
-    return [p for pair in zip(near, far) for p in pair]
+def exchange(x, axis):
+    return lax.all_to_all(x, axis, 0, 0)
+
+
+def mean_over_replicas(chunks, shared):
+    n_dp, n_shards = lax.axis_size("dp"), lax.axis_size("tensor")
+    _, per, width = chunks.shape
+    outs = [shaped(per, width), shaped(n_shards, per, shared.stop - shared.start)]
+    own, parts = call(functools.partial(mean_kernel, shared), outs, exchange(chunks, "dp"), name="replica_mean")
+    copies = call(functools.partial(copies_kernel, shared), shaped(n_dp, per, width), own, exchange(parts, "tensor"), name="shard_sum")
+    return exchange(copies, "dp")
 
 
 def on_device(gu, eu, gd, ed, qu, qd):
+    qu, qd = qu.T, qd.T
     n_dp, n_shards = lax.axis_size("dp"), lax.axis_size("tensor")
     _, rows, ff = gu.shape
-    rank = qu.shape[1]
+    rank = qu.shape[0]
     width = rows + ff
-    half, per = n_dp // 2, rank // n_dp
-    chunks = [shaped(half, per, width)] * 2
-    chunk_specs = [whole((half, per, width))] * 2
-
-    keep, send = call(
+    chunks = shaped(n_dp, rank // n_dp, width)
+
+    terms = call(
         left_kernel, chunks, gu, eu, gd, ed, qu, qd,
         name="left_terms", flops=8 * rows * ff * 4 * rank, grid=(STEPS,),
         in_specs=[pl.BlockSpec((1, rows // STEPS, ff), lambda i: (0, i, 0))] * 2
         + [pl.BlockSpec((1, ff // STEPS, rows), lambda i: (0, i, 0))] * 2
         + [whole(qu.shape), whole(qd.shape)],
-        out_specs=chunk_specs,
-        scratch_shapes=[pltpu.VMEM((ff, 4 * rank), BF16), pltpu.VMEM((rows, 4 * rank), BF16), pltpu.VMEM((rank, width), F32), pltpu.VMEM((n_dp, per, width), F32)],
-    )
-    chunk_up, chunk_down = mean_over_replicas(keep, send, rows)
-    down = gather(chunk_down)
-    up = gather(sum_over_shards(chunk_up))
-
-    left, gram_up, gram_down, keep, send = call(
-        functools.partial(right_kernel, n_dp),
-        [shaped(rank, width), shaped(rank, rank), shaped(rank, rank)] + chunks, gu, eu, gd, ed, *up, *down,
+        out_specs=whole(chunks.shape),
+        scratch_shapes=[pltpu.VMEM((4 * rank, ff), BF16), pltpu.VMEM((4 * rank, rows), BF16), pltpu.VMEM((rank, width), F32)],
+    )
+    gathered = mean_over_replicas(terms, slice(0, rows))
+
+    left, gram_up, gram_down, terms = call(
+        right_kernel, [shaped(rank, width), shaped(rank, rank), shaped(rank, rank), chunks], gu, eu, gd, ed, gathered,
         name="right_terms", flops=8 * rows * ff * 3 * rank, grid=(STEPS,),
         in_specs=[pl.BlockSpec((1, rows, ff // STEPS), lambda i: (0, 0, i))] * 2
         + [pl.BlockSpec((1, ff // STEPS, rows), lambda i: (0, i, 0))] * 2
-        + [whole(p.shape) for p in up + down],
-        out_specs=[whole((rank, width)), whole((rank, rank)), whole((rank, rank))] + chunk_specs,
-        scratch_shapes=[pltpu.VMEM((3 * rank, width), BF16), pltpu.VMEM((rank, width), F32), pltpu.VMEM((n_dp, per, width), F32)],
+        + [whole(gathered.shape)],
+        out_specs=[whole((rank, width)), whole((rank, rank)), whole((rank, rank)), whole(chunks.shape)],
+        scratch_shapes=[pltpu.VMEM((3 * rank, width), BF16), pltpu.VMEM((rank, width), F32)],
     )
     grams = [gram_down] + [swap(gram_down, "tensor", j) for j in range(1, n_shards)]
-    chunk_up, chunk_down = mean_over_replicas(keep, send, ff)
+    gathered = mean_over_replicas(terms, slice(ff, width))
     inv_up, inv_down, lhs_up, lhs_down = call(
         basis_kernel,
         [shaped(rank, rank)] * 2 + [shaped(rows, 4 * rank, dtype=BF16), shaped(ff, 4 * rank, dtype=BF16)],
         left, gram_up, *grams, name="basis", flops=10**9,
     )
-    up = gather(chunk_up)
-    down = gather(sum_over_shards(chunk_down))
 
     rhs, sq_up, sq_down = call(
-        functools.partial(factor_kernel, n_dp),
-        [shaped(4 * rank, width, dtype=BF16), shaped(8, 128), shaped(8, 128)], inv_up, inv_down, *up, *down,
-        name="right_factor", scratch_shapes=[pltpu.VMEM((rank, width), F32), pltpu.VMEM((n_dp, per, width), F32)],
+        functools.partial(factor_kernel, ff),
+        [shaped(4 * rank, width, dtype=BF16), shaped(8, 128), shaped(8, 128)], inv_up, inv_down, gathered,
+        name="right_factor", scratch_shapes=[pltpu.VMEM((rank, width), F32)],
     )
     squares = [sq_up] + [swap(sq_up, "tensor", j) for j in range(1, n_shards)]
 

time: 119 us -> 120 us (level)
  blocking collectives: 0 us -> 70.2 us
  starting transfers between devices: 52.8 us -> 7.98 us
  waiting for transfers between devices: 34.9 us -> 3.65 us
  local copies, waits for them, and re-layouts: 5.11 us -> 9.97 us
  Pallas kernels: 25.3 us -> 27.1 us
    all_to_all x0 -> x5, blocking collectives: none -> 70.2 us  [exchange(): return lax.all_to_all(x, axis, 0, 0)]
    ppermute x48 -> x6, starting transfers between devices: 52.8 us -> 3.84 us  [swap(): return lax.ppermute(x, axis, pairs)]
    ppermute x48 -> x6, waiting for transfers between devices: 34.9 us -> 2.36 us  [swap(): return lax.ppermute(x, axis, pairs)]
    unnamed x10 -> x22, local copies, waits for them, and re-layouts: 5.11 us -> 9.97 us
    all_to_all x0 -> x1, starting transfers between devices: none -> 4.14 us  [exchange(): return lax.all_to_all(x, axis, 0, 0)]
    pallas_call x12 -> x10, Pallas kernels: 25.3 us -> 27.1 us  [call(): pl.pallas_call(kernel, out_shape=out_shape, compiler_params=params(), cos...]
    all_to_all x0 -> x1, waiting for transfers between devices: none -> 1.28 us  [exchange(): return lax.all_to_all(x, axis, 0, 0)]
  transfers between devices with their start and end apart: 48 -> 7, of which waited for: 15 -> 3; matrix products, arithmetic and copies ran while one was open for 0% -> 0% of each run, Pallas kernels for 10% -> 10%
where the time goes in v2:
time: 120 us
  blocking collectives  70.2 us (58%)
  Pallas kernels  27.1 us (23%)
  local copies, waits for them, and re-layouts  9.97 us (8%)
  starting transfers between devices  7.98 us (7%)
  waiting for transfers between devices  3.65 us (3%)
    all_to_all x5, blocking collectives, exchange(): return lax.all_to_all(x, axis, 0, 0)  70.2 us
    pallas_call x10, Pallas kernels, call(): pl.pallas_call(kernel, out_shape=out_shape, compiler_params=params(), cos...  27.1 us
    unnamed x22, local copies, waits for them, and re-layouts  9.97 us
    all_to_all x1, starting transfers between devices, exchange(): return lax.all_to_all(x, axis, 0, 0)  4.14 us
    ppermute x6, starting transfers between devices, swap(): return lax.ppermute(x, axis, pairs)  3.84 us
  transfers between devices with their start and end apart: 7, of which 3 were waited for; matrix products, arithmetic and copies ran while one was open for 0% of the time, Pallas kernels for 10%

profile of v2, /device:TPU:0, one launch (start us, length us, event | category | flops | bytes accessed | tf_op | source)
XLA Modules:
  0.0 119.6 jit_solution(7869936171784800862)
XLA Ops:
  0.6 0.0 copy-start
  0.6 1.4 %copy-done = bf16[1,512,1536]{2,1,0:T(8,128)(2,1)S(1)} copy-done((bf16[1,512,1536]{2,1,0:T(8,128)(2,1)S(1)}, bf16[1,512,1536]{2,1,0:T(8,128)(2,1)}, u32[]{:S(2)}) %copy-start) | copy-done | bytes 1572888
  2.0 0.0 copy-start.2
  2.0 1.4 %copy-done.2 = bf16[1,512,1536]{2,1,0:T(8,128)(2,1)S(1)} copy-done((bf16[1,512,1536]{2,1,0:T(8,128)(2,1)S(1)}, bf16[1,512,1536]{2,1,0:T(8,128)(2,1)}, u32[]{:S(2)}) %copy-start.2) | copy-done | bytes 1572888
  3.5 0.0 copy-start.4
  3.5 1.4 %copy-done.4 = bf16[1,1536,512]{2,1,0:T(8,128)(2,1)S(1)} copy-done((bf16[1,1536,512]{2,1,0:T(8,128)(2,1)S(1)}, bf16[1,1536,512]{2,1,0:T(8,128)(2,1)}, u32[]{:S(2)}) %copy-start.4) | copy-done | bytes 1572888
  4.9 0.0 copy-start.7
  4.9 1.0 copy-done.7
  5.9 0.0 copy-start.8
  5.9 0.9 copy-done.8
  6.8 5.0 %left_terms.1 = f32[8,8,2048]{2,1,0:T(8,128)S(1)} custom-call(bf16[1,512,1536]{2,1,0:T(8,128)(2,1)S(1)} %copy-done, bf16[1,512,1536]{2,1,0:T(8,128)(2,1)S(1)} %copy-done.2, bf16[1,1536,512]{2,1,0:T(8,128)(2,1)S(1)} %copy-done.4, bf16[1,1536,512]{2,1,0:T(8,128)(2,1)} %ed.5, f32[64,1536]{1,0:T(8,128)S(1)} %bitcast.2, f32[64,512]{1,0:T(8,128)S(1)} %bitcast.3), custom_call_target="tpu_custom_call" | custom-call | flops 1610612736 | bytes 7340032 | tf_op jit(solution)/shard_map/left_terms/pallas_call | solution.py:198
  11.8 0.0 copy-start.1
  11.8 21.7 %all_to_all.30.got = f32[8,8,2048]{2,1,0:T(8,128)S(1)} all-to-all(f32[8,8,2048]{2,1,0:T(8,128)S(1)} %left_terms.1), channel_id=1, replica_groups=mesh['dp'=8,'tensor'=4] {'dp'}, dimensions={0} | all-to-all | bytes 1048576 | tf_op jit(solution)/shard_map/all_to_all | solution.py:207
  33.6 6.7 %all_to_all.31.parts = f32[4,8,512]{2,1,0:T(8,128)S(1)} all-to-all(f32[4,8,512]{2,1,0:T(8,128)S(1)} %get-tuple-element.24), channel_id=1, replica_groups=mesh['dp'=8,'tensor'=4] {'tensor'}, dimensions={0} | all-to-all | bytes 131072 | tf_op jit(solution)/shard_map/all_to_all | solution.py:207
  40.3 17.7 %all_to_all.32.gathered = f32[8,8,2048]{2,1,0:T(8,128)S(1)} all-to-all(f32[8,8,2048]{2,1,0:T(8,128)S(1)} %shard_sum.2), channel_id=1, replica_groups=mesh['dp'=8,'tensor'=4] {'dp'}, dimensions={0} | all-to-all | bytes 1048576 | tf_op jit(solution)/shard_map/all_to_all | solution.py:207
  58.0 0.0 copy-done.1
  58.0 4.9 %right_terms.1 = (f32[64,2048]{1,0:T(8,128)S(1)}, f32[64,64]{1,0:T(8,128)S(1)}, f32[64,64]{1,0:T(8,128)S(1)}, f32[8,8,2048]{2,1,0:T(8,128)S(1)}) custom-call(bf16[1,512,1536]{2,1,0:T(8,128)(2,1)S(1)} %copy-done.1, bf16[1,512,1536]{2,1,0:T(8,128)(2,1)S(1)} %copy-done.2, bf16[1,1536,512]{2,1,0:T(8,128)(2,1)} %gd.5, bf16[1,1536,512]{2,1,0:T(8,128)(2,1)} %ed.5, ...), custom_call_target="tpu_custom_call" | custom-call | flops 1207959552 | bytes 7897088 | tf_op jit(solution)/shard_map/right_terms/pallas_call | solution.py:198
  62.9 0.0 copy-start.9
  62.9 0.8 copy-done.9
  63.7 17.6 %all_to_all.33.got = f32[8,8,2048]{2,1,0:T(8,128)S(1)} all-to-all(f32[8,8,2048]{2,1,0:T(8,128)S(1)} %get-tuple-element.32), channel_id=1, replica_groups=mesh['dp'=8,'tensor'=4] {'dp'}, dimensions={0} | all-to-all | bytes 1048576 | tf_op jit(solution)/shard_map/all_to_all | solution.py:207
  81.3 6.5 %all_to_all.34.parts = f32[4,8,512]{2,1,0:T(8,128)S(1)} all-to-all(f32[4,8,512]{2,1,0:T(8,128)S(1)} %get-tuple-element.34), channel_id=1, replica_groups=mesh['dp'=8,'tensor'=4] {'tensor'}, dimensions={0} | all-to-all | bytes 131072 | tf_op jit(solution)/shard_map/all_to_all | solution.py:207
  87.8 0.8 shard_sum.3
  88.6 4.1 %all-to-all-start.5 = ((f32[8,8,2048]{2,1,0:T(8,128)}), f32[8,8,2048]{2,1,0:T(8,128)}, u32[]{:S(2)}, u32[]{:S(2)}) async-start(f32[8,8,2048]{2,1,0:T(8,128)} %shard_sum.3), calls=%async_computation.5 | async-start | bytes 1048576 | tf_op jit(solution)/shard_map/all_to_all | solution.py:207
  92.8 0.1 collective-permute-start.2
  92.9 1.3 %collective-permute-start.1 = (f32[64,64]{1,0:T(8,128)S(1)}, f32[64,64]{1,0:T(8,128)S(1)}, u32[]{:S(2)}, u32[]{:S(2)}) collective-permute-start(f32[64,64]{1,0:T(8,128)S(1)} %get-tuple-element.27.refs_0_), channel_id=1, source_target_pairs={{0,2},{1,3},{2,0},{3,1},{4,6},{5,7},{6,4},{7,5},{8,10},{9,11},{10,... | collective-permute-start | bytes 49160 | tf_op jit(solution)/shard_map/ppermute | solution.py:203
  94.1 0.6 collective-permute-start
  94.7 1.7 %collective-permute-done.2.refs_3_ = f32[64,64]{1,0:T(8,128)S(1)} collective-permute-done((f32[64,64]{1,0:T(8,128)S(1)}, f32[64,64]{1,0:T(8,128)S(1)}, u32[]{:S(2)}, u32[]{:S(2)}) %collective-permute-start.2) | collective-permute-done | bytes 16416 | tf_op jit(solution)/shard_map/ppermute | solution.py:203
  96.4 0.7 collective-permute-done.1.refs_2_
  97.1 0.0 collective-permute-done.refs_1_
  97.1 0.0 copy-start.10
  97.1 1.0 copy-done.10
  98.1 0.0 copy-start.3
  98.1 7.1 %basis.1 = (f32[64,64]{1,0:T(8,128)S(1)}, f32[64,64]{1,0:T(8,128)S(1)}, bf16[512,256]{1,0:T(8,128)(2,1)S(1)}, bf16[1536,256]{1,0:T(8,128)(2,1)S(1)}) custom-call(f32[64,2048]{1,0:T(8,128)S(1)} %copy-done.10, f32[64,64]{1,0:T(8,128)S(1)} %get-tuple-element.26.gram_up, f32[64,64]{1,0:T(8,128)S(1)} %get-tuple-element.27.refs_0_, ...), custom_call_target="tpu_custom_call" | custom-call | flops 1000000000 | bytes 1687552 | tf_op jit(solution)/shard_map/basis/pallas_call | solution.py:198
  105.2 0.0 copy-start.5
  105.2 0.9 copy-done.5
  106.1 1.3 %all-to-all-done.5.gathered = f32[8,8,2048]{2,1,0:T(8,128)} async-done(((f32[8,8,2048]{2,1,0:T(8,128)}), f32[8,8,2048]{2,1,0:T(8,128)}, u32[]{:S(2)}, u32[]{:S(2)}) %all-to-all-start.5) | async-done | bytes 524320 | tf_op jit(solution)/shard_map/all_to_all | solution.py:207
  107.3 1.8 %right_factor.1 = (bf16[256,2048]{1,0:T(8,128)(2,1)S(1)}, f32[8,128]{1,0:T(8,128)S(1)}, f32[8,128]{1,0:T(8,128)S(1)}) custom-call(f32[64,64]{1,0:T(8,128)S(1)} %get-tuple-element.30.inv_up, f32[64,64]{1,0:T(8,128)S(1)} %get-tuple-element.31.inv_down, f32[8,8,2048]{2,1,0:T(8,128)} %all-to-all-done.5.gathered), custom_call_target="tpu_custom_call" | custom-call | bytes 1613824 | tf_op jit(solution)/shard_map/right_factor/pallas_call | solution.py:198
  109.1 0.1 collective-permute-start.5
  109.2 0.5 collective-permute-start.4
  109.7 1.4 %collective-permute-start.3 = (f32[8,128]{1,0:T(8,128)S(1)}, f32[8,128]{1,0:T(8,128)S(1)}, u32[]{:S(2)}, u32[]{:S(2)}) collective-permute-start(f32[8,128]{1,0:T(8,128)S(1)} %get-tuple-element.37.refs_0_), channel_id=1, source_target_pairs={{0,1},{1,0},{2,3},{3,2},{4,5},{5,4},{6,7},{7,6},{8,9},{9,8},{10,11... | collective-permute-start | bytes 12296 | tf_op jit(solution)/shard_map/ppermute | solution.py:203
  111.0 0.0 copy-done.3
  111.0 0.0 copy-start.6
  111.0 1.1 copy-done.6
  112.2 4.6 %new_error.1 = (bf16[1,512,1536]{2,1,0:T(8,128)(2,1)}, bf16[1,1536,512]{2,1,0:T(8,128)(2,1)}) custom-call(bf16[1,512,1536]{2,1,0:T(8,128)(2,1)S(1)} %copy-done.1, bf16[1,512,1536]{2,1,0:T(8,128)(2,1)S(1)} %copy-done.3, bf16[1,1536,512]{2,1,0:T(8,128)(2,1)} %gd.5, bf16[1,1536,512]{2,1,0:T(8,128)(2,1)} %ed.5, bf16[512,256]{1,0:T(8,128)(2,1)S(1)} %get-tuple-element.28.lhs_up, ...), custom_call_target="tpu_custom_call" | custom-call | flops 805306368 | bytes 11534336 | tf_op jit(solution)/shard_map/new_error/pallas_call | solution.py:198
  116.8 0.0 collective-permute-done.5.refs_3_
  116.8 0.0 collective-permute-done.4.refs_2_
  116.8 0.0 collective-permute-done.3.refs_1_
  116.8 2.7 %update.1 = (bf16[512,1536]{1,0:T(8,128)(2,1)}, bf16[1536,512]{1,0:T(8,128)(2,1)}) custom-call(bf16[512,256]{1,0:T(8,128)(2,1)S(1)} %get-tuple-element.28.lhs_up, bf16[1536,256]{1,0:T(8,128)(2,1)S(1)} %copy-done.6, bf16[256,2048]{1,0:T(8,128)(2,1)S(1)} %get-tuple-element.35.rhs, f32[8,128]{1,0:T(8,128)S(1)} %get-tuple-element.37.refs_0_, ...), custom_call_target="tpu_custom_call" | custom-call | flops 805306368 | bytes 5263360 | tf_op jit(solution)/shard_map/update/pallas_call | solution.py:198
  (3 shorter events, 0.1 us)
Async XLA Ops:
  0.6 1.4 %copy-start = (bf16[1,512,1536]{2,1,0:T(8,128)(2,1)S(1)}, bf16[1,512,1536]{2,1,0:T(8,128)(2,1)}, u32[]{:S(2)}) copy-start(bf16[1,512,1536]{2,1,0:T(8,128)(2,1)} %gu.5) | copy-start | bytes 4718596
  2.0 1.4 %copy-start.2 = (bf16[1,512,1536]{2,1,0:T(8,128)(2,1)S(1)}, bf16[1,512,1536]{2,1,0:T(8,128)(2,1)}, u32[]{:S(2)}) copy-start(bf16[1,512,1536]{2,1,0:T(8,128)(2,1)} %eu.5) | copy-start | bytes 4718596
  3.5 1.4 %copy-start.4 = (bf16[1,1536,512]{2,1,0:T(8,128)(2,1)S(1)}, bf16[1,1536,512]{2,1,0:T(8,128)(2,1)}, u32[]{:S(2)}) copy-start(bf16[1,1536,512]{2,1,0:T(8,128)(2,1)} %gd.5) | copy-start | bytes 4718596
  4.9 1.0 copy-start.7
  5.9 0.9 copy-start.8
  11.8 46.2 %copy-start.1 = (bf16[1,512,1536]{2,1,0:T(8,128)(2,1)S(1)}, bf16[1,512,1536]{2,1,0:T(8,128)(2,1)}, u32[]{:S(2)}) copy-start(bf16[1,512,1536]{2,1,0:T(8,128)(2,1)} %gu.5) | copy-start | bytes 4718596
  62.9 0.8 copy-start.9
  88.6 18.7 %all-to-all-start.5 = ((f32[8,8,2048]{2,1,0:T(8,128)}), f32[8,8,2048]{2,1,0:T(8,128)}, u32[]{:S(2)}, u32[]{:S(2)}) async-start(f32[8,8,2048]{2,1,0:T(8,128)} %shard_sum.3), calls=%async_computation.5 | async-start | bytes 1048576 | tf_op jit(solution)/shard_map/all_to_all | solution.py:207
  92.8 3.6 %collective-permute-start.2 = (f32[64,64]{1,0:T(8,128)S(1)}, f32[64,64]{1,0:T(8,128)S(1)}, u32[]{:S(2)}, u32[]{:S(2)}) collective-permute-start(f32[64,64]{1,0:T(8,128)S(1)} %get-tuple-element.27.refs_0_), channel_id=1, source_target_pairs={{0,3},{1,2},{2,1},{3,0},{4,7},{5,6},{6,5},{7,4},{8,11},{9,10},{10,... | collective-permute-start | bytes 49160 | tf_op jit(solution)/shard_map/ppermute | solution.py:203
  92.9 4.2 %collective-permute-start.1 = (f32[64,64]{1,0:T(8,128)S(1)}, f32[64,64]{1,0:T(8,128)S(1)}, u32[]{:S(2)}, u32[]{:S(2)}) collective-permute-start(f32[64,64]{1,0:T(8,128)S(1)} %get-tuple-element.27.refs_0_), channel_id=1, source_target_pairs={{0,2},{1,3},{2,0},{3,1},{4,6},{5,7},{6,4},{7,5},{8,10},{9,11},{10,... | collective-permute-start | bytes 49160 | tf_op jit(solution)/shard_map/ppermute | solution.py:203
  94.1 2.9 %collective-permute-start = (f32[64,64]{1,0:T(8,128)S(1)}, f32[64,64]{1,0:T(8,128)S(1)}, u32[]{:S(2)}, u32[]{:S(2)}) collective-permute-start(f32[64,64]{1,0:T(8,128)S(1)} %get-tuple-element.27.refs_0_), channel_id=1, source_target_pairs={{0,1},{1,0},{2,3},{3,2},{4,5},{5,4},{6,7},{7,6},{8,9},{9,8},{10,11... | collective-permute-start | bytes 49160 | tf_op jit(solution)/shard_map/ppermute | solution.py:203
  97.1 1.0 copy-start.10
  98.1 12.9 %copy-start.3 = (bf16[1,512,1536]{2,1,0:T(8,128)(2,1)S(1)}, bf16[1,512,1536]{2,1,0:T(8,128)(2,1)}, u32[]{:S(2)}) copy-start(bf16[1,512,1536]{2,1,0:T(8,128)(2,1)} %eu.5) | copy-start | bytes 4718596
  105.2 0.9 copy-start.5
  109.1 7.7 %collective-permute-start.5 = (f32[8,128]{1,0:T(8,128)S(1)}, f32[8,128]{1,0:T(8,128)S(1)}, u32[]{:S(2)}, u32[]{:S(2)}) collective-permute-start(f32[8,128]{1,0:T(8,128)S(1)} %get-tuple-element.37.refs_0_), channel_id=1, source_target_pairs={{0,3},{1,2},{2,1},{3,0},{4,7},{5,6},{6,5},{7,4},{8,11},{9,10},{10,... | collective-permute-start | bytes 12296 | tf_op jit(solution)/shard_map/ppermute | solution.py:203
  109.2 7.6 %collective-permute-start.4 = (f32[8,128]{1,0:T(8,128)S(1)}, f32[8,128]{1,0:T(8,128)S(1)}, u32[]{:S(2)}, u32[]{:S(2)}) collective-permute-start(f32[8,128]{1,0:T(8,128)S(1)} %get-tuple-element.37.refs_0_), channel_id=1, source_target_pairs={{0,2},{1,3},{2,0},{3,1},{4,6},{5,7},{6,4},{7,5},{8,10},{9,11},{10,... | collective-permute-start | bytes 12296 | tf_op jit(solution)/shard_map/ppermute | solution.py:203
  109.7 7.2 %collective-permute-start.3 = (f32[8,128]{1,0:T(8,128)S(1)}, f32[8,128]{1,0:T(8,128)S(1)}, u32[]{:S(2)}, u32[]{:S(2)}) collective-permute-start(f32[8,128]{1,0:T(8,128)S(1)} %get-tuple-element.37.refs_0_), channel_id=1, source_target_pairs={{0,1},{1,0},{2,3},{3,2},{4,5},{5,4},{6,7},{7,6},{8,9},{9,8},{10,11... | collective-permute-start | bytes 12296 | tf_op jit(solution)/shard_map/ppermute | solution.py:203
  111.0 1.1 copy-start.6

commit v3 on v0

v3 whole, which is shorter than its diff:
```python
import functools

import jax
import jax.numpy as jnp
from jax import lax
from jax.experimental import pallas as pl
from jax.experimental.pallas import tpu as pltpu
from jax.sharding import PartitionSpec as P

F32 = jnp.float32
BF16 = jnp.bfloat16
HIGHEST = lax.Precision.HIGHEST
CLIP_RMS = 0.1
STEPS = 4
MIB = 1024 * 1024
NT = ((1,), (1,))


def split3(x):
    first = x.astype(BF16)
    rest = x - first.astype(F32)
    second = rest.astype(BF16)
    return first, second, (rest - second.astype(F32)).astype(BF16)


def tree_sum(values):
    values = list(values)
    while len(values) > 1:
        values = [values[i] + values[i + 1] for i in range(0, len(values), 2)]
    return values[0]


def dot(a, b, dims=((1,), (0,)), precision=None):
    return lax.dot_general(a, b, (dims, ((), ())), precision=precision, preferred_element_type=F32)


def fold(x, rows):
    return jnp.concatenate([x[i : i + rows] for i in range(0, x.shape[0], rows)], axis=1)


def unfold(x, rows):
    count = rows // x.shape[0]
    width = x.shape[1] // count
    return jnp.concatenate([x[:, i * width : (i + 1) * width] for i in range(count)], axis=0)


def place(axis):
    index = lax.axis_index(axis)
    return lax.bitwise_and(index, 1), lax.shift_right_logical(index, 1)


def split_cores(total, extra, keep, send):
    core, _ = place("tensor")
    rows, width = keep.shape[0], total.shape[1]
    keep[:, :width] = total[pl.ds(pl.multiple_of(core * rows, rows), rows), :]
    send[:, :width] = total[pl.ds(pl.multiple_of((1 - core) * rows, rows), rows), :]
    if extra is not None:
        keep[:, width:] = extra
        send[:, width:] = extra


def split_replicas(total, stage, keep, send):
    parity, _ = place("dp")
    half, per, _ = keep.shape
    for c in range(2 * half):
        stage[c] = total[c * per : (c + 1) * per, :]
    for c in range(half):
        keep[c] = stage[2 * c + parity]
        send[c] = stage[2 * c + 1 - parity]


def join_replicas(mine, other, stage, total):
    parity, _ = place("dp")
    half, per, _ = mine.shape
    width = total.shape[1]
    for c in range(half):
        stage[2 * c + parity] = mine[c, :, :width]
        stage[2 * c + 1 - parity] = other[c, :, :width]
    for c in range(2 * half):
        total[c * per : (c + 1) * per, :] = stage[c]


def join_cores(mine, other, total):
    core, _ = place("tensor")
    rows, width = mine.shape[0], total.shape[1]
    total[pl.ds(pl.multiple_of(core * rows, rows), rows), :] = mine[:, :width]
    total[pl.ds(pl.multiple_of((1 - core) * rows, rows), rows), :] = other[:, :width]


def left_product(g, e, q, pieces, total):
    step = pl.program_id(0)
    rank = q.shape[0]
    block = g.shape[1]

    @pl.when(step == 0)
    def _():
        for i, piece in enumerate(split3(q[...])):
            pieces[i * rank : (i + 1) * rank, :] = piece
        pieces[3 * rank :, :] = jnp.zeros((rank, q.shape[1]), BF16)

    t = dot(g[0], pieces[...], NT) + dot(e[0], pieces[...], NT)
    t = (t[:, : 2 * rank] + t[:, 2 * rank :]).T
    total[:, pl.ds(pl.multiple_of(step * block, 128), block)] = t[:rank] + t[rank:]


def left_up_kernel(g, e, q, keep, send, pieces, total):
    left_product(g, e, q, pieces, total)

    @pl.when(pl.program_id(0) == STEPS - 1)
    def _():
        split_cores(total, None, keep, send)


def left_down_kernel(g, e, q, keep, send, pieces, total, stage):
    left_product(g, e, q, pieces, total)

    @pl.when(pl.program_id(0) == STEPS - 1)
    def _():
        split_replicas(total, stage, keep, send)


def split_x_kernel(width, keep, got, *outs):
    _, x = place("tensor")
    total = outs[-1]
    outs = outs[:-1]
    rows = outs[0].shape[0]
    total[...] = keep[...] + got[...]
    for j, out in enumerate(outs):
        owner = lax.bitwise_xor(x, j)
        out[:, :width] = total[pl.ds(pl.multiple_of(owner * rows, rows), rows), :width]
        if total.shape[1] > width:
            out[:, width:] = fold(total[:, width:], rows)


def split_z_kernel(n_x, width, gram_shape, keep, got, *refs):
    shards, refs = refs[:n_x], refs[n_x:]
    gram = refs[0] if gram_shape else None
    outs, stage = refs[1 if gram_shape else 0 : -1], refs[-1]
    _, z = place("dp")
    half, per, ff = keep.shape
    summed = tree_sum(s[...] for s in shards)
    block = width // half
    for c in range(half):
        stage[c, :, :ff] = keep[c] + got[c]
        stage[c, :, ff:] = fold(summed[:, c * block : (c + 1) * block], per)
    for j, out in enumerate(outs):
        out[...] = stage[lax.bitwise_xor(z, j)]
    if gram_shape:
        whole_gram = unfold(summed[:, width:], gram_shape // 2)
        gram[...] = unfold(whole_gram, gram_shape)


def mean_kernel(n_dp, *refs):
    refs[-1][...] = tree_sum(ref[...] for ref in refs[:-1]) / n_dp


def stack_kernel(*refs):
    _, z = place("dp")
    for j, ref in enumerate(refs[:-1]):
        refs[-1][lax.bitwise_xor(z, j)] = ref[...]


def shard_rows(mine, other, ff, rows):
    half = mine.shape[0]
    return jnp.concatenate([unfold(mine[c, :, ff:] + other[c, :, ff:], rows) for c in range(half)], axis=1)


def shard_rows_kernel(ff, mine, other, out):
    out[...] = shard_rows(mine, other, ff, out.shape[0])


def stack_x_kernel(width, *refs):
    _, x = place("tensor")
    *pieces, out = refs
    rows = pieces[0].shape[0]
    for j, piece in enumerate(pieces):
        owner = lax.bitwise_xor(x, j)
        out[pl.ds(pl.multiple_of(owner * rows, rows), rows), :width] = piece[:, :width]
    if out.shape[1] > width:
        summed = tree_sum(piece[:, width:] for piece in pieces)
        for i in range(0, out.shape[0], rows):
            out[i : i + rows, width:] = summed


def split_rows(left, pieces):
    rank = left.shape[0]
    for i, piece in enumerate(split3(left[...])):
        pieces[i * rank : (i + 1) * rank, :] = piece


def add_pieces(t):
    rank = t.shape[0] // 3
    return t[:rank] + (t[rank : 2 * rank] + t[2 * rank :])


def right_down_kernel(mine, other, g, e, left, keep, send, pieces, total, stage):
    rank = left.shape[0]
    join_replicas(mine, other, stage, left)
    split_rows(left, pieces)
    total[...] = add_pieces(dot(pieces[...], g[0]) + dot(pieces[...], e[0]))
    gram = dot(left[...], left[...], NT, HIGHEST)
    split_cores(total, fold(gram, rank // 2), keep, send)


def right_up_kernel(mine, other, g, e, left, gram, keep, send, pieces, total, stage):
    join_cores(mine, other, left)
    split_rows(left, pieces)
    block = total.shape[1] // STEPS
    for i in range(STEPS):
        part = slice(i * block, (i + 1) * block)
        total[:, part] = add_pieces(dot(pieces[...], g[0, :, part]) + dot(pieces[...], e[0, :, part]))
    split_replicas(total, stage, keep, send)
    gram[...] = dot(left[...], left[...], NT, HIGHEST)


def inverse_factors(grams):
    rank = grams[0].shape[0]
    lane = lax.broadcasted_iota(jnp.int32, (8, 2 * rank), 1)
    row = lax.broadcasted_iota(jnp.int32, (8, 2 * rank), 0)
    states = []
    for gram in grams:
        wide = jnp.concatenate([gram, jnp.zeros_like(gram)], axis=1)
        states.append([wide[i : i + 8] + (lane == row + (rank + i)).astype(F32) for i in range(0, rank, 8)])
    for k in range(rank):
        at, inner = divmod(k, 8)
        for blocks in states:
            pivot_row = blocks[at][inner : inner + 1, :]
            scaled = pivot_row / pivot_row[:, k : k + 1]
            for i in range(at, rank // 8):
                column = blocks[i][:, k : k + 1]
                if i == at:
                    column = jnp.where(row[:, :1] > inner, column, 0.0)
                blocks[i] = blocks[i] - column * scaled
    results = []
    for blocks in states:
        rows = []
        for i, block in enumerate(blocks):
            diagonal = jnp.sum(jnp.where(lane == row + 8 * i, block, 0.0), axis=1, keepdims=True)
            rows.append((block / jnp.sqrt(diagonal))[:, rank:])
        results.append(jnp.concatenate(rows, axis=0))
    return results


def basis_kernel(left_up, left_down, gram_up, gram_down, inv_up, inv_down, lhs_up, lhs_down):
    inverses = inverse_factors([gram_up[...], gram_down[...]])
    rank = left_up.shape[0]
    for inverse, inv, left, lhs in zip(inverses, (inv_up, inv_down), (left_up, left_down), (lhs_up, lhs_down)):
        inv[...] = inverse
        first, second, _ = split3(dot(inverse, left[...], precision=HIGHEST).T)
        lhs[:, :rank] = first
        lhs[:, rank : 2 * rank] = first
        lhs[:, 2 * rank : 3 * rank] = second
        lhs[:, 3 * rank :] = second


def right_factor(inv, total, rhs):
    rank = inv.shape[0]
    right = dot(inv[...], total[...], precision=HIGHEST)
    first, second, _ = split3(right)
    rhs[:rank, :] = first
    rhs[rank : 2 * rank, :] = second
    rhs[2 * rank : 3 * rank, :] = first
    rhs[3 * rank :, :] = second
    return jnp.sum(right * right)


def factor_up_kernel(mine, other, inv, rhs, shard, total, stage):
    join_replicas(mine, other, stage, total)
    square = right_factor(inv, total, rhs)
    rows, ff = shard.shape[0], total.shape[1]
    width = shard.shape[1] - 128
    shard[:, :width] = shard_rows(mine, other, ff, rows)
    shard[:, width:] = jnp.full((rows, 128), square, F32)


def factor_down_kernel(limit, mine, other, inv, rhs, clip, total):
    join_cores(mine, other, total)
    square = right_factor(inv, total, rhs)
    width = total.shape[1]
    norm_sq = square + (mine[:8, width:] + other[:8, width:])
    clip[...] = jnp.minimum(jnp.float32(1.0), limit / jnp.sqrt(norm_sq))


def rows_of(block):
    return pl.ds(pl.multiple_of(pl.program_id(0) * block, block), block)


def error_up_kernel(g, e, lhs, rhs, error):
    part = rows_of(error.shape[1])
    rebuilt = dot(lhs[part, :], rhs[...])
    error[0] = (g[0, part, :].astype(F32) + e[0, part, :].astype(F32) - rebuilt).astype(BF16)


def last_kernel(g, e, lhs_up, rhs_up, lhs_down, rhs_down, clip, error, update_up, update_down):
    factor = clip[:1, :1]
    part = rows_of(update_down.shape[0])
    rebuilt = dot(lhs_down[part, :], rhs_down[...])
    update_down[...] = (factor * rebuilt).astype(BF16)
    error[0] = (g[0, part, :].astype(F32) + e[0, part, :].astype(F32) - rebuilt).astype(BF16)
    part = rows_of(update_up.shape[0])
    update_up[...] = (factor * dot(lhs_up[part, :], rhs_up[...])).astype(BF16)


def shaped(*dims, dtype=F32):
    return jax.ShapeDtypeStruct(dims, dtype)


def whole(shape):
    return pl.BlockSpec(shape, lambda *_: (0,) * len(shape))


def row_blocks(rows, columns):
    return pl.BlockSpec((rows // STEPS, columns), lambda i: (i, 0))


def replica_blocks(rows, columns):
    return pl.BlockSpec((1, rows // STEPS, columns), lambda i: (0, i, 0))


VMEM = pl.BlockSpec(memory_space=pltpu.VMEM)


def call(kernel, out_shape, *args, flops=0, limit=12, name=None, **more):
    arrays = list(args) + jax.tree.leaves(out_shape)
    size = sum(a.size * a.dtype.itemsize for a in arrays)
    cost = pl.CostEstimate(flops=flops, bytes_accessed=size, transcendentals=0)
    params = pltpu.CompilerParams(vmem_limit_bytes=limit * MIB)
    return pl.pallas_call(kernel, out_shape=out_shape, compiler_params=params, cost_estimate=cost, name=name, **more)(*args)


def swap(x, axis, distance):
    pairs = [(i, i ^ distance) for i in range(lax.axis_size(axis))]
    return lax.ppermute(x, axis, pairs)


def sum_shards(keep, send, width):
    n_x = lax.axis_size("tensor") // 2
    got = swap(send, "tensor", 1)
    rows, columns = keep.shape[0] // n_x, keep.shape[1]
    out = shaped(rows, width + (columns - width) * n_x)
    parts = call(
        functools.partial(split_x_kernel, width), [out] * n_x + [shaped(*keep.shape)], keep, got, name="split_x"
    )[:n_x]
    return [parts[0]] + [swap(parts[j], "tensor", 2 * j) for j in range(1, n_x)]


def mean_replicas(keep, got, shards, width, gram_rank=0):
    n_dp = lax.axis_size("dp")
    half, per, ff = keep.shape
    columns = ff + shards[0].shape[0] // per * (width // half)
    outs = [shaped(per, columns)] * half
    if gram_rank:
        outs = [shaped(gram_rank, gram_rank)] + outs
    parts = call(
        functools.partial(split_z_kernel, len(shards), width, gram_rank), outs, keep, got, *shards,
        name="split_z", scratch_shapes=[pltpu.VMEM((half, per, columns), F32)],
    )
    gram, parts = (parts[0], parts[1:]) if gram_rank else (None, parts)
    parts = [parts[0]] + [swap(parts[j], "dp", 2 * j) for j in range(1, half)]
    mean = call(functools.partial(mean_kernel, n_dp), shaped(per, columns), *parts, name="replica_mean")
    chunks = [mean] + [swap(mean, "dp", 2 * j) for j in range(1, half)]
    mine = call(stack_kernel, shaped(half, per, columns), *chunks, name="stack_z")
    return mine, swap(mine, "dp", 1), gram


def gather_shards(rows_here, width):
    n_x = lax.axis_size("tensor") // 2
    rows, columns = rows_here.shape
    pieces = [rows_here] + [swap(rows_here, "tensor", 2 * j) for j in range(1, n_x)]
    mine = call(functools.partial(stack_x_kernel, width), shaped(rows * n_x, columns), *pieces, name="stack_x")
    return mine, swap(mine, "tensor", 1)


def on_device(gu, eu, gd, ed, qu, qd):
    qu, qd = qu.T, qd.T
    n_dp, n_shards = lax.axis_size("dp"), lax.axis_size("tensor")
    _, rows, ff = gu.shape
    rank = qu.shape[0]
    half, per = n_dp // 2, rank // n_dp
    core_half = shaped(rank // 2, rows)
    replica_half = shaped(half, per, ff)
    stage = pltpu.VMEM((n_dp, per, ff), F32)
    wide = pltpu.VMEM((rank, ff), F32)
    narrow = pltpu.VMEM((rank, rows), F32)
    product = 4 * rows * ff * 4 * rank

    keep_up, send_up = call(
        left_up_kernel, [core_half] * 2, gu, eu, qu, name="left_up", flops=product, limit=60, grid=(STEPS,),
        in_specs=[replica_blocks(rows, ff)] * 2 + [whole(qu.shape)], out_specs=[whole(core_half.shape)] * 2,
        scratch_shapes=[pltpu.VMEM((4 * rank, ff), BF16), narrow],
    )
    shards = sum_shards(keep_up, send_up, rows)
    keep, send = call(
        left_down_kernel, [replica_half] * 2, gd, ed, qd, name="left_down", flops=product, limit=60, grid=(STEPS,),
        in_specs=[replica_blocks(ff, rows)] * 2 + [whole(qd.shape)], out_specs=[whole(replica_half.shape)] * 2,
        scratch_shapes=[pltpu.VMEM((4 * rank, rows), BF16), wide, stage],
    )
    mine, other, _ = mean_replicas(keep, swap(send, "dp", 1), shards, rows)

    shard = call(functools.partial(shard_rows_kernel, ff), shaped(rank // n_shards, rows), mine, other, name="shard_rows")
    left_half, left_other = gather_shards(shard, rows)
    core_half = shaped(rank // 2, rows + 2 * rank)
    left_down, keep_down, send_down = call(
        right_down_kernel, [shaped(rank, ff), core_half, core_half], mine, other, gd, ed, name="right_down", flops=product,
        in_specs=[VMEM] * 4, scratch_shapes=[pltpu.VMEM((3 * rank, ff), BF16), narrow, stage],
    )
    shards = sum_shards(keep_down, send_down, rows)
    left_up, gram_up, keep, send = call(
        right_up_kernel, [shaped(rank, rows), shaped(rank, rank), replica_half, replica_half], left_half, left_other, gu, eu,
        name="right_up", flops=product, in_specs=[VMEM] * 4, scratch_shapes=[pltpu.VMEM((3 * rank, rows), BF16), wide, stage],
    )
    mine, other, gram_down = mean_replicas(keep, swap(send, "dp", 1), shards, rows, rank)
    inv_up, inv_down, lhs_up, lhs_down = call(
        basis_kernel,
        [shaped(rank, rank)] * 2 + [shaped(rows, 4 * rank, dtype=BF16), shaped(ff, 4 * rank, dtype=BF16)],
        left_up, left_down, gram_up, gram_down, name="basis", flops=10**9,
    )
    rhs_up, shard = call(
        factor_up_kernel, [shaped(4 * rank, ff, dtype=BF16), shaped(rank // n_shards, rows + 128)], mine, other, inv_up,
        name="factor_up", scratch_shapes=[wide, stage],
    )
    right_half, right_other = gather_shards(shard, rows)
    new_error_up = call(
        error_up_kernel, shaped(1, rows, ff, dtype=BF16), gu, eu, lhs_up, rhs_up, name="error_up", flops=product // 2,
        grid=(STEPS,), in_specs=[VMEM] * 4, out_specs=replica_blocks(rows, ff),
    )
    limit = CLIP_RMS * (2.0 * rows * ff * n_shards) ** 0.5
    rhs_down, clip = call(
        functools.partial(factor_down_kernel, limit), [shaped(4 * rank, rows, dtype=BF16), shaped(8, 128)],
        right_half, right_other, inv_down, name="factor_down", scratch_shapes=[narrow],
    )
    new_error_down, update_up, update_down = call(
        last_kernel, [shaped(1, ff, rows, dtype=BF16), shaped(rows, ff, dtype=BF16), shaped(ff, rows, dtype=BF16)],
        gd, ed, lhs_up, rhs_up, lhs_down, rhs_down, clip, name="last", flops=product, grid=(STEPS,),
        in_specs=[VMEM] * 7, out_specs=[replica_blocks(ff, rows), row_blocks(rows, ff), row_blocks(ff, rows)],
    )
    return new_error_up, update_up, new_error_down, update_down


def solution(mesh):
    placed = (
        P("dp", None, "tensor"),
        P("dp", None, "tensor"),
        P("dp", "tensor", None),
        P("dp", "tensor", None),
        P("tensor", None),
        P(),
    )
    return jax.shard_map(
        on_device,
        mesh=mesh,
        in_specs=placed,
        out_specs=(
            P("dp", None, "tensor"),
            P(None, "tensor"),
            P("dp", "tensor", None),
            P("tensor", None),
        ),
        check_vma=False,
    )
```

time: 379 us -> 96.3 us (0.25)
  waiting for transfers between devices: 257 us -> 37 us
  other arithmetic: 43.9 us -> 0 us
  matrix products: 39 us -> 0 us
  starting transfers between devices: 0.3 us -> 29.8 us
  Pallas kernels: 0 us -> 27.5 us
  blocking collectives: 17.6 us -> 0 us
  between operations: 15.8 us -> 0.78 us
    psum x3 -> x0, waiting for transfers between devices: 257 us -> none  [the longest x1 124 us: on_device(): lax.psum(jnp.dot(merged_up, q_up, precision=HIGHEST), ('dp', 'tensor'))]
    ppermute x0 -> x24, waiting for transfers between devices: none -> 37 us  [swap(): return lax.ppermute(x, axis, pairs)]
    dot_general x8 -> x0, matrix products: 36.3 us -> none  [the longest x1 6.09 us: on_device(): term_left = jnp.dot(merged_down, q_down, precision=HIGHEST)]
    another operation x10 -> x0, other arithmetic: 33.9 us -> none  [the longest x4 16.6 us: solve_right(): lax.linalg.triangular_solve(factor, left, left_side=False, lower=True, tr...]
    ppermute x0 -> x24, starting transfers between devices: none -> 29.8 us  [swap(): return lax.ppermute(x, axis, pairs)]
    pallas_call x0 -> x20, Pallas kernels: none -> 27.5 us  [call(): pl.pallas_call(kernel, out_shape=out_shape, compiler_params=params, cost_...]
    psum x2 -> x0, blocking collectives: 17.6 us -> none  [the longest x1 11.4 us: on_device(): lax.psum(jnp.dot(left_down.T, left_down, precision=HIGHEST), 'tensor')]
    convert_element_type x2 -> x0, other arithmetic: 7.16 us -> none  [the longest x1 4.55 us: on_device(): update_down = (clip_factor * rebuilt_down).astype(jnp.bfloat16)]
  transfers between devices with their start and end apart: 3 -> 24, of which waited for: 3 -> 18; matrix products, arithmetic and copies ran while one was open for 3% -> 0% of each run, Pallas kernels for 0% -> 18%
where the time goes in v3:
time: 96.3 us; the launch traced here: 96 us
  waiting for transfers between devices  37 us (38%)
  starting transfers between devices  29.8 us (31%)
  Pallas kernels  27.5 us (29%)
    ppermute x24, waiting for transfers between devices, swap(): return lax.ppermute(x, axis, pairs)  37 us
    ppermute x24, starting transfers between devices, swap(): return lax.ppermute(x, axis, pairs)  29.8 us
    pallas_call x20, Pallas kernels, call(): pl.pallas_call(kernel, out_shape=out_shape, compiler_params=params, cost_...  27.5 us
  transfers between devices with their start and end apart: 24, of which 18 were waited for; matrix products, arithmetic and copies ran while one was open for 0% of the time, Pallas kernels for 18%

profile of v3, /device:TPU:0, one launch (start us, length us, event | category | flops | bytes accessed | tf_op | source)
XLA Modules:
  0.0 96.0 jit_solution(17596564725750525794)
XLA Ops:
  0.6 4.6 %left_down.1 = (f32[4,8,1536]{2,1,0:T(8,128)}, f32[4,8,1536]{2,1,0:T(8,128)}) custom-call(bf16[1,1536,512]{2,1,0:T(8,128)(2,1)} %g.11, bf16[1,1536,512]{2,1,0:T(8,128)(2,1)} %e.11, f32[64,512]{1,0:T(8,128)} %bitcast.3), custom_call_target="tpu_custom_call" | custom-call | flops 805306368 | bytes 3670016 | tf_op jit(solution)/shard_map/left_down/pallas_call | solution.py:328
  5.2 3.0 %collective-permute-start = (f32[4,8,1536]{2,1,0:T(8,128)}, f32[4,8,1536]{2,1,0:T(8,128)S(1)}, u32[]{:S(2)}, u32[]{:S(2)}) collective-permute-start(f32[4,8,1536]{2,1,0:T(8,128)} %get-tuple-element.40), channel_id=1, source_target_pairs={{0,4},{4,0},{8,12},{12,8},{16,20},{20,16},{24,28},{28,24},{1,5},{5... | collective-permute-start | bytes 589832 | tf_op jit(solution)/shard_map/ppermute | solution.py:333
  8.2 5.5 %left_up.1 = (f32[32,512]{1,0:T(8,128)}, f32[32,512]{1,0:T(8,128)}) custom-call(bf16[1,512,1536]{2,1,0:T(8,128)(2,1)} %g.10, bf16[1,512,1536]{2,1,0:T(8,128)(2,1)} %e.10, f32[64,1536]{1,0:T(8,128)} %bitcast.2), custom_call_target="tpu_custom_call" | custom-call | flops 805306368 | bytes 3670016 | tf_op jit(solution)/shard_map/left_up/pallas_call | solution.py:328
  13.7 0.0 collective-permute-start.1
  13.7 1.5 %collective-permute-done.1.got = f32[32,512]{1,0:T(8,128)S(1)} collective-permute-done((f32[32,512]{1,0:T(8,128)}, f32[32,512]{1,0:T(8,128)S(1)}, u32[]{:S(2)}, u32[]{:S(2)}) %collective-permute-start.1) | collective-permute-done | bytes 65568 | tf_op jit(solution)/shard_map/ppermute | solution.py:333
  15.1 0.8 copy-done.5
  16.0 0.6 split_x.2
  16.6 1.5 %collective-permute-start.2 = (f32[16,512]{1,0:T(8,128)S(1)}, f32[16,512]{1,0:T(8,128)S(1)}, u32[]{:S(2)}, u32[]{:S(2)}) collective-permute-start(f32[16,512]{1,0:T(8,128)S(1)} %get-tuple-element.44), channel_id=1, source_target_pairs={{0,2},{1,3},{2,0},{3,1},{4,6},{5,7},{6,4},{7,5},{8,10},{9,11},{10,... | collective-permute-start | bytes 98312 | tf_op jit(solution)/shard_map/ppermute | solution.py:333
  18.1 2.4 %collective-permute-done.2.refs_1_ = f32[16,512]{1,0:T(8,128)S(1)} collective-permute-done((f32[16,512]{1,0:T(8,128)S(1)}, f32[16,512]{1,0:T(8,128)S(1)}, u32[]{:S(2)}, u32[]{:S(2)}) %collective-permute-start.2) | collective-permute-done | bytes 32800 | tf_op jit(solution)/shard_map/ppermute | solution.py:333
  20.5 0.0 collective-permute-done.got
  20.6 1.6 %collective-permute-start.3 = (f32[8,1792]{1,0:T(8,128)S(1)}, f32[8,1792]{1,0:T(8,128)S(1)}, u32[]{:S(2)}, u32[]{:S(2)}) collective-permute-start(f32[8,1792]{1,0:T(8,128)S(1)} %get-tuple-element.46), channel_id=1, source_target_pairs={{0,8},{4,12},{8,0},{12,4},{16,24},{20,28},{24,16},{28,20},{1,9},{5... | collective-permute-start | bytes 172040 | tf_op jit(solution)/shard_map/ppermute | solution.py:333
  22.2 2.6 %collective-permute-start.4 = (f32[8,1792]{1,0:T(8,128)S(1)}, f32[8,1792]{1,0:T(8,128)S(1)}, u32[]{:S(2)}, u32[]{:S(2)}) collective-permute-start(f32[8,1792]{1,0:T(8,128)S(1)} %get-tuple-element.47), channel_id=1, source_target_pairs={{0,16},{4,20},{8,24},{12,28},{16,0},{20,4},{24,8},{28,12},{1,17},{... | collective-permute-start | bytes 172040 | tf_op jit(solution)/shard_map/ppermute | solution.py:333
  24.8 0.2 collective-permute-start.5
  25.0 0.4 collective-permute-done.3.refs_1_
  25.4 3.1 %collective-permute-done.4.refs_2_ = f32[8,1792]{1,0:T(8,128)S(1)} collective-permute-done((f32[8,1792]{1,0:T(8,128)S(1)}, f32[8,1792]{1,0:T(8,128)S(1)}, u32[]{:S(2)}, u32[]{:S(2)}) %collective-permute-start.4) | collective-permute-done | bytes 57376 | tf_op jit(solution)/shard_map/ppermute | solution.py:333
  28.5 2.9 %collective-permute-done.5.refs_3_ = f32[8,1792]{1,0:T(8,128)S(1)} collective-permute-done((f32[8,1792]{1,0:T(8,128)S(1)}, f32[8,1792]{1,0:T(8,128)S(1)}, u32[]{:S(2)}, u32[]{:S(2)}) %collective-permute-start.5) | collective-permute-done | bytes 57376 | tf_op jit(solution)/shard_map/ppermute | solution.py:333
  31.4 0.1 collective-permute-start.6
  31.5 0.7 collective-permute-start.7
  32.2 3.7 %collective-permute-start.8 = (f32[8,1792]{1,0:T(8,128)S(1)}, f32[8,1792]{1,0:T(8,128)S(1)}, u32[]{:S(2)}, u32[]{:S(2)}) collective-permute-start(f32[8,1792]{1,0:T(8,128)S(1)} %replica_mean.2.refs_0_), channel_id=1, source_target_pairs={{0,24},{4,28},{8,16},{12,20},{16,8},{20,12},{24,0},{28,4},{1,25},{... | collective-permute-start | bytes 172040 | tf_op jit(solution)/shard_map/ppermute | solution.py:333
  35.9 0.0 collective-permute-done.6.refs_1_
  35.9 0.8 collective-permute-done.7.refs_2_
  36.7 2.0 %collective-permute-done.8.refs_3_ = f32[8,1792]{1,0:T(8,128)S(1)} collective-permute-done((f32[8,1792]{1,0:T(8,128)S(1)}, f32[8,1792]{1,0:T(8,128)S(1)}, u32[]{:S(2)}, u32[]{:S(2)}) %collective-permute-start.8) | collective-permute-done | bytes 57376 | tf_op jit(solution)/shard_map/ppermute | solution.py:333
  38.7 0.5 collective-permute-start.9
  39.2 5.6 %collective-permute-done.9.other = f32[4,8,1792]{2,1,0:T(8,128)S(1)} collective-permute-done((f32[4,8,1792]{2,1,0:T(8,128)S(1)}, f32[4,8,1792]{2,1,0:T(8,128)S(1)}, u32[]{:S(2)}, u32[]{:S(2)}) %collective-permute-start.9) | collective-permute-done | bytes 229408 | tf_op jit(solution)/shard_map/ppermute | solution.py:333
  44.8 1.5 %collective-permute-start.10 = (f32[16,512]{1,0:T(8,128)S(1)}, f32[16,512]{1,0:T(8,128)S(1)}, u32[]{:S(2)}, u32[]{:S(2)}) collective-permute-start(f32[16,512]{1,0:T(8,128)S(1)} %shard_rows.1.refs_0_), channel_id=1, source_target_pairs={{0,2},{1,3},{2,0},{3,1},{4,6},{5,7},{6,4},{7,5},{8,10},{9,11},{10,... | collective-permute-start | bytes 98312 | tf_op jit(solution)/shard_map/ppermute | solution.py:333
  46.3 2.4 %collective-permute-done.10.refs_1_ = f32[16,512]{1,0:T(8,128)S(1)} collective-permute-done((f32[16,512]{1,0:T(8,128)S(1)}, f32[16,512]{1,0:T(8,128)S(1)}, u32[]{:S(2)}, u32[]{:S(2)}) %collective-permute-start.10) | collective-permute-done | bytes 32800 | tf_op jit(solution)/shard_map/ppermute | solution.py:333
  48.7 0.0 copy-start.2
  48.7 0.0 copy-start.3
  48.7 0.1 collective-permute-start.11
  48.8 1.2 %collective-permute-done.11.other = f32[32,512]{1,0:T(8,128)S(1)} collective-permute-done((f32[32,512]{1,0:T(8,128)S(1)}, f32[32,512]{1,0:T(8,128)S(1)}, u32[]{:S(2)}, u32[]{:S(2)}) %collective-permute-start.11) | collective-permute-done | bytes 65568 | tf_op jit(solution)/shard_map/ppermute | solution.py:333
  50.1 0.0 copy-done
  50.1 1.2 %right_up.1 = (f32[64,512]{1,0:T(8,128)S(1)}, f32[64,64]{1,0:T(8,128)S(1)}, f32[4,8,1536]{2,1,0:T(8,128)S(1)}, f32[4,8,1536]{2,1,0:T(8,128)S(1)}) custom-call(f32[32,512]{1,0:T(8,128)S(1)} %stack_x.2.mine, f32[32,512]{1,0:T(8,128)S(1)} %collective-permute-done.11.other, bf16[1,512,1536]{2,1,0:T(8,128)(2,1)S(1)} %copy-done, bf16[1,512,1536]{2,1,0:T(8,128)(2,1)S(1)} %copy-done.1), custom_call_target="tpu_custom_call" | custom-call | flops 805306368 | bytes 3817472 | tf_op jit(solution)/shard_map/right_up/pallas_call | solution.py:328
  51.2 0.5 collective-permute-start.12
  51.8 1.2 %right_down.1 = (f32[64,1536]{1,0:T(8,128)S(1)}, f32[32,640]{1,0:T(8,128)S(1)}, f32[32,640]{1,0:T(8,128)S(1)}) custom-call(f32[4,8,1792]{2,1,0:T(8,128)S(1)} %stack_z.2.mine, f32[4,8,1792]{2,1,0:T(8,128)S(1)} %collective-permute-done.9.other, bf16[1,1536,512]{2,1,0:T(8,128)(2,1)S(1)} %copy-done.2, bf16[1,1536,512]{2,1,0:T(8,128)(2,1)S(1)} %copy-done.3), custom_call_target="tpu_custom_call" | custom-call | flops 805306368 | bytes 4161536 | tf_op jit(solution)/shard_map/right_down/pallas_call | solution.py:328
  53.0 0.0 collective-permute-start.13
  53.0 1.3 %collective-permute-done.13.got = f32[32,640]{1,0:T(8,128)S(1)} collective-permute-done((f32[32,640]{1,0:T(8,128)S(1)}, f32[32,640]{1,0:T(8,128)S(1)}, u32[]{:S(2)}, u32[]{:S(2)}) %collective-permute-start.13) | collective-permute-done | bytes 81952 | tf_op jit(solution)/shard_map/ppermute | solution.py:333
  54.3 0.6 split_x.3
  54.9 1.5 %collective-permute-start.14 = (f32[16,768]{1,0:T(8,128)S(1)}, f32[16,768]{1,0:T(8,128)S(1)}, u32[]{:S(2)}, u32[]{:S(2)}) collective-permute-start(f32[16,768]{1,0:T(8,128)S(1)} %get-tuple-element.57), channel_id=1, source_target_pairs={{0,2},{1,3},{2,0},{3,1},{4,6},{5,7},{6,4},{7,5},{8,10},{9,11},{10,... | collective-permute-start | bytes 147464 | tf_op jit(solution)/shard_map/ppermute | solution.py:333
  56.5 2.6 %collective-permute-done.14.refs_1_ = f32[16,768]{1,0:T(8,128)S(1)} collective-permute-done((f32[16,768]{1,0:T(8,128)S(1)}, f32[16,768]{1,0:T(8,128)S(1)}, u32[]{:S(2)}, u32[]{:S(2)}) %collective-permute-start.14) | collective-permute-done | bytes 49184 | tf_op jit(solution)/shard_map/ppermute | solution.py:333
  59.0 0.0 collective-permute-done.12.got
  59.0 0.1 split_z.3
  59.1 0.0 collective-permute-start.15
  59.1 3.8 %collective-permute-start.16 = (f32[8,1792]{1,0:T(8,128)S(1)}, f32[8,1792]{1,0:T(8,128)S(1)}, u32[]{:S(2)}, u32[]{:S(2)}) collective-permute-start(f32[8,1792]{1,0:T(8,128)S(1)} %get-tuple-element.62), channel_id=1, source_target_pairs={{0,16},{4,20},{8,24},{12,28},{16,0},{20,4},{24,8},{28,12},{1,17},{... | collective-permute-start | bytes 172040 | tf_op jit(solution)/shard_map/ppermute | solution.py:333
  62.9 0.6 collective-permute-start.17
  63.5 0.2 collective-permute-done.15.refs_1_
  63.7 2.1 %collective-permute-done.16.refs_2_ = f32[8,1792]{1,0:T(8,128)S(1)} collective-permute-done((f32[8,1792]{1,0:T(8,128)S(1)}, f32[8,1792]{1,0:T(8,128)S(1)}, u32[]{:S(2)}, u32[]{:S(2)}) %collective-permute-start.16) | collective-permute-done | bytes 57376 | tf_op jit(solution)/shard_map/ppermute | solution.py:333
  65.9 3.3 %collective-permute-done.17.refs_3_ = f32[8,1792]{1,0:T(8,128)S(1)} collective-permute-done((f32[8,1792]{1,0:T(8,128)S(1)}, f32[8,1792]{1,0:T(8,128)S(1)}, u32[]{:S(2)}, u32[]{:S(2)}) %collective-permute-start.17) | collective-permute-done | bytes 57376 | tf_op jit(solution)/shard_map/ppermute | solution.py:333
  69.1 0.1 collective-permute-start.18
  69.2 1.0 %collective-permute-start.19 = (f32[8,1792]{1,0:T(8,128)S(1)}, f32[8,1792]{1,0:T(8,128)S(1)}, u32[]{:S(2)}, u32[]{:S(2)}) collective-permute-start(f32[8,1792]{1,0:T(8,128)S(1)} %replica_mean.3.refs_0_), channel_id=1, source_target_pairs={{0,16},{4,20},{8,24},{12,28},{16,0},{20,4},{24,8},{28,12},{1,17},{... | collective-permute-start | bytes 172040 | tf_op jit(solution)/shard_map/ppermute | solution.py:333
  70.2 3.4 %collective-permute-start.20 = (f32[8,1792]{1,0:T(8,128)S(1)}, f32[8,1792]{1,0:T(8,128)S(1)}, u32[]{:S(2)}, u32[]{:S(2)}) collective-permute-start(f32[8,1792]{1,0:T(8,128)S(1)} %replica_mean.3.refs_0_), channel_id=1, source_target_pairs={{0,24},{4,28},{8,16},{12,20},{16,8},{20,12},{24,0},{28,4},{1,25},{... | collective-permute-start | bytes 172040 | tf_op jit(solution)/shard_map/ppermute | solution.py:333
  73.6 0.0 collective-permute-done.18.refs_1_
  73.6 0.8 collective-permute-done.19.refs_2_
  74.4 2.0 %collective-permute-done.20.refs_3_ = f32[8,1792]{1,0:T(8,128)S(1)} collective-permute-done((f32[8,1792]{1,0:T(8,128)S(1)}, f32[8,1792]{1,0:T(8,128)S(1)}, u32[]{:S(2)}, u32[]{:S(2)}) %collective-permute-start.20) | collective-permute-done | bytes 57376 | tf_op jit(solution)/shard_map/ppermute | solution.py:333
  76.4 1.8 %collective-permute-start.21 = (f32[4,8,1792]{2,1,0:T(8,128)S(1)}, f32[4,8,1792]{2,1,0:T(8,128)S(1)}, u32[]{:S(2)}, u32[]{:S(2)}) collective-permute-start(f32[4,8,1792]{2,1,0:T(8,128)S(1)} %stack_z.3.mine), channel_id=1, source_target_pairs={{0,4},{4,0},{8,12},{12,8},{16,20},{20,16},{24,28},{28,24},{1,5},{5... | collective-permute-start | bytes 688136 | tf_op jit(solution)/shard_map/ppermute | solution.py:333
  78.2 7.1 %basis.1 = (f32[64,64]{1,0:T(8,128)S(1)}, f32[64,64]{1,0:T(8,128)S(1)}, bf16[512,256]{1,0:T(8,128)(2,1)S(1)}, bf16[1536,256]{1,0:T(8,128)(2,1)S(1)}) custom-call(f32[64,512]{1,0:T(8,128)S(1)} %get-tuple-element.49.left_up, f32[64,1536]{1,0:T(8,128)S(1)} %get-tuple-element.50.left_down, f32[64,64]{1,0:T(8,128)S(1)} %get-tuple-element.51.gram_up, ...), custom_call_target="tpu_custom_call" | custom-call | flops 1000000000 | bytes 1638400 | tf_op jit(solution)/shard_map/basis/pallas_call | solution.py:328
  85.3 0.0 collective-permute-done.21.other
  85.3 0.7 factor_up.1
  86.0 1.5 %collective-permute-start.22 = (f32[16,640]{1,0:T(8,128)S(1)}, f32[16,640]{1,0:T(8,128)S(1)}, u32[]{:S(2)}, u32[]{:S(2)}) collective-permute-start(f32[16,640]{1,0:T(8,128)S(1)} %get-tuple-element.67.refs_0_), channel_id=1, source_target_pairs={{0,2},{1,3},{2,0},{3,1},{4,6},{5,7},{6,4},{7,5},{8,10},{9,11},{10,... | collective-permute-start | bytes 122888 | tf_op jit(solution)/shard_map/ppermute | solution.py:333
  87.6 2.5 %collective-permute-done.22.refs_1_ = f32[16,640]{1,0:T(8,128)S(1)} collective-permute-done((f32[16,640]{1,0:T(8,128)S(1)}, f32[16,640]{1,0:T(8,128)S(1)}, u32[]{:S(2)}, u32[]{:S(2)}) %collective-permute-start.22) | collective-permute-done | bytes 40992 | tf_op jit(solution)/shard_map/ppermute | solution.py:333
  90.1 0.1 collective-permute-start.23
  90.2 2.3 %error_up.1 = bf16[1,512,1536]{2,1,0:T(8,128)(2,1)} custom-call(bf16[1,512,1536]{2,1,0:T(8,128)(2,1)S(1)} %copy-done, bf16[1,512,1536]{2,1,0:T(8,128)(2,1)S(1)} %copy-done.1, bf16[512,256]{1,0:T(8,128)(2,1)S(1)} %get-tuple-element.59.lhs.lhs_up, bf16[256,1536]{1,0:T(8,128)(2,1)S(1)} %get-tuple-element.65.rhs.rhs_up), custom_call_target="tpu_custom_call" | custom-call | flops 402653184 | bytes 5767168 | tf_op jit(solution)/shard_map/error_up/pallas_call | solution.py:328
  92.5 0.0 collective-permute-done.23.other
  92.5 0.4 factor_down.1
  93.0 3.0 %last.1 = (bf16[1,1536,512]{2,1,0:T(8,128)(2,1)}, bf16[512,1536]{1,0:T(8,128)(2,1)}, bf16[1536,512]{1,0:T(8,128)(2,1)}) custom-call(bf16[1,1536,512]{2,1,0:T(8,128)(2,1)S(1)} %copy-done.2, bf16[1,1536,512]{2,1,0:T(8,128)(2,1)S(1)} %copy-done.3, bf16[512,256]{1,0:T(8,128)(2,1)S(1)} %get-tuple-element.59.lhs.lhs_up, ...), custom_call_target="tpu_custom_call" | custom-call | flops 805306368 | bytes 9965568 | tf_op jit(solution)/shard_map/last/pallas_call | solution.py:328
  (16 shorter events, 0.2 us)
Async XLA Ops:
  5.2 15.3 %collective-permute-start = (f32[4,8,1536]{2,1,0:T(8,128)}, f32[4,8,1536]{2,1,0:T(8,128)S(1)}, u32[]{:S(2)}, u32[]{:S(2)}) collective-permute-start(f32[4,8,1536]{2,1,0:T(8,128)} %get-tuple-element.40), channel_id=1, source_target_pairs={{0,4},{4,0},{8,12},{12,8},{16,20},{20,16},{24,28},{28,24},{1,5},{5... | collective-permute-start | bytes 589832 | tf_op jit(solution)/shard_map/ppermute | solution.py:333
  8.2 12.3 %copy-start.4 = (f32[4,8,1536]{2,1,0:T(8,128)S(1)}, f32[4,8,1536]{2,1,0:T(8,128)}, u32[]{:S(2)}) copy-start(f32[4,8,1536]{2,1,0:T(8,128)} %get-tuple-element.39.keep) | copy-start | bytes 589828
  8.2 41.8 %copy-start.1 = (bf16[1,512,1536]{2,1,0:T(8,128)(2,1)S(1)}, bf16[1,512,1536]{2,1,0:T(8,128)(2,1)}, u32[]{:S(2)}) copy-start(bf16[1,512,1536]{2,1,0:T(8,128)(2,1)} %e.10) | copy-start | bytes 4718596
  13.7 36.4 %copy-start = (bf16[1,512,1536]{2,1,0:T(8,128)(2,1)S(1)}, bf16[1,512,1536]{2,1,0:T(8,128)(2,1)}, u32[]{:S(2)}) copy-start(bf16[1,512,1536]{2,1,0:T(8,128)(2,1)} %g.10) | copy-start | bytes 4718596
  13.7 1.5 %collective-permute-start.1 = (f32[32,512]{1,0:T(8,128)}, f32[32,512]{1,0:T(8,128)S(1)}, u32[]{:S(2)}, u32[]{:S(2)}) collective-permute-start(f32[32,512]{1,0:T(8,128)} %get-tuple-element.42), channel_id=1, source_target_pairs={{0,1},{1,0},{2,3},{3,2},{4,5},{5,4},{6,7},{7,6},{8,9},{9,8},{10,11... | collective-permute-start | bytes 196616 | tf_op jit(solution)/shard_map/ppermute | solution.py:333
  15.1 0.8 copy-start.5
  16.6 3.9 %collective-permute-start.2 = (f32[16,512]{1,0:T(8,128)S(1)}, f32[16,512]{1,0:T(8,128)S(1)}, u32[]{:S(2)}, u32[]{:S(2)}) collective-permute-start(f32[16,512]{1,0:T(8,128)S(1)} %get-tuple-element.44), channel_id=1, source_target_pairs={{0,2},{1,3},{2,0},{3,1},{4,6},{5,7},{6,4},{7,5},{8,10},{9,11},{10,... | collective-permute-start | bytes 98312 | tf_op jit(solution)/shard_map/ppermute | solution.py:333
  20.6 4.8 %collective-permute-start.3 = (f32[8,1792]{1,0:T(8,128)S(1)}, f32[8,1792]{1,0:T(8,128)S(1)}, u32[]{:S(2)}, u32[]{:S(2)}) collective-permute-start(f32[8,1792]{1,0:T(8,128)S(1)} %get-tuple-element.46), channel_id=1, source_target_pairs={{0,8},{4,12},{8,0},{12,4},{16,24},{20,28},{24,16},{28,20},{1,9},{5... | collective-permute-start | bytes 172040 | tf_op jit(solution)/shard_map/ppermute | solution.py:333
  22.2 6.3 %collective-permute-start.4 = (f32[8,1792]{1,0:T(8,128)S(1)}, f32[8,1792]{1,0:T(8,128)S(1)}, u32[]{:S(2)}, u32[]{:S(2)}) collective-permute-start(f32[8,1792]{1,0:T(8,128)S(1)} %get-tuple-element.47), channel_id=1, source_target_pairs={{0,16},{4,20},{8,24},{12,28},{16,0},{20,4},{24,8},{28,12},{1,17},{... | collective-permute-start | bytes 172040 | tf_op jit(solution)/shard_map/ppermute | solution.py:333
  24.8 6.6 %collective-permute-start.5 = (f32[8,1792]{1,0:T(8,128)S(1)}, f32[8,1792]{1,0:T(8,128)S(1)}, u32[]{:S(2)}, u32[]{:S(2)}) collective-permute-start(f32[8,1792]{1,0:T(8,128)S(1)} %get-tuple-element.48), channel_id=1, source_target_pairs={{0,24},{4,28},{8,16},{12,20},{16,8},{20,12},{24,0},{28,4},{1,25},{... | collective-permute-start | bytes 172040 | tf_op jit(solution)/shard_map/ppermute | solution.py:333
  31.4 4.5 %collective-permute-start.6 = (f32[8,1792]{1,0:T(8,128)S(1)}, f32[8,1792]{1,0:T(8,128)S(1)}, u32[]{:S(2)}, u32[]{:S(2)}) collective-permute-start(f32[8,1792]{1,0:T(8,128)S(1)} %replica_mean.2.refs_0_), channel_id=1, source_target_pairs={{0,8},{4,12},{8,0},{12,4},{16,24},{20,28},{24,16},{28,20},{1,9},{5... | collective-permute-start | bytes 172040 | tf_op jit(solution)/shard_map/ppermute | solution.py:333
  31.5 5.1 %collective-permute-start.7 = (f32[8,1792]{1,0:T(8,128)S(1)}, f32[8,1792]{1,0:T(8,128)S(1)}, u32[]{:S(2)}, u32[]{:S(2)}) collective-permute-start(f32[8,1792]{1,0:T(8,128)S(1)} %replica_mean.2.refs_0_), channel_id=1, source_target_pairs={{0,16},{4,20},{8,24},{12,28},{16,0},{20,4},{24,8},{28,12},{1,17},{... | collective-permute-start | bytes 172040 | tf_op jit(solution)/shard_map/ppermute | solution.py:333
  32.2 6.5 %collective-permute-start.8 = (f32[8,1792]{1,0:T(8,128)S(1)}, f32[8,1792]{1,0:T(8,128)S(1)}, u32[]{:S(2)}, u32[]{:S(2)}) collective-permute-start(f32[8,1792]{1,0:T(8,128)S(1)} %replica_mean.2.refs_0_), channel_id=1, source_target_pairs={{0,24},{4,28},{8,16},{12,20},{16,8},{20,12},{24,0},{28,4},{1,25},{... | collective-permute-start | bytes 172040 | tf_op jit(solution)/shard_map/ppermute | solution.py:333
  38.7 6.1 %collective-permute-start.9 = (f32[4,8,1792]{2,1,0:T(8,128)S(1)}, f32[4,8,1792]{2,1,0:T(8,128)S(1)}, u32[]{:S(2)}, u32[]{:S(2)}) collective-permute-start(f32[4,8,1792]{2,1,0:T(8,128)S(1)} %stack_z.2.mine), channel_id=1, source_target_pairs={{0,4},{4,0},{8,12},{12,8},{16,20},{20,16},{24,28},{28,24},{1,5},{5... | collective-permute-start | bytes 688136 | tf_op jit(solution)/shard_map/ppermute | solution.py:333
  44.8 3.9 %collective-permute-start.10 = (f32[16,512]{1,0:T(8,128)S(1)}, f32[16,512]{1,0:T(8,128)S(1)}, u32[]{:S(2)}, u32[]{:S(2)}) collective-permute-start(f32[16,512]{1,0:T(8,128)S(1)} %shard_rows.1.refs_0_), channel_id=1, source_target_pairs={{0,2},{1,3},{2,0},{3,1},{4,6},{5,7},{6,4},{7,5},{8,10},{9,11},{10,... | collective-permute-start | bytes 98312 | tf_op jit(solution)/shard_map/ppermute | solution.py:333
  48.7 3.1 %copy-start.2 = (bf16[1,1536,512]{2,1,0:T(8,128)(2,1)S(1)}, bf16[1,1536,512]{2,1,0:T(8,128)(2,1)}, u32[]{:S(2)}) copy-start(bf16[1,1536,512]{2,1,0:T(8,128)(2,1)} %g.11) | copy-start | bytes 4718596
  48.7 3.1 %copy-start.3 = (bf16[1,1536,512]{2,1,0:T(8,128)(2,1)S(1)}, bf16[1,1536,512]{2,1,0:T(8,128)(2,1)}, u32[]{:S(2)}) copy-start(bf16[1,1536,512]{2,1,0:T(8,128)(2,1)} %e.11) | copy-start | bytes 4718596
  48.7 1.3 %collective-permute-start.11 = (f32[32,512]{1,0:T(8,128)S(1)}, f32[32,512]{1,0:T(8,128)S(1)}, u32[]{:S(2)}, u32[]{:S(2)}) collective-permute-start(f32[32,512]{1,0:T(8,128)S(1)} %stack_x.2.mine), channel_id=1, source_target_pairs={{0,1},{1,0},{2,3},{3,2},{4,5},{5,4},{6,7},{7,6},{8,9},{9,8},{10,11... | collective-permute-start | bytes 196616 | tf_op jit(solution)/shard_map/ppermute | solution.py:333
  51.2 7.8 %collective-permute-start.12 = (f32[4,8,1536]{2,1,0:T(8,128)S(1)}, f32[4,8,1536]{2,1,0:T(8,128)S(1)}, u32[]{:S(2)}, u32[]{:S(2)}) collective-permute-start(f32[4,8,1536]{2,1,0:T(8,128)S(1)} %get-tuple-element.53), channel_id=1, source_target_pairs={{0,4},{4,0},{8,12},{12,8},{16,20},{20,16},{24,28},{28,24},{1,5},{5... | collective-permute-start | bytes 589832 | tf_op jit(solution)/shard_map/ppermute | solution.py:333
  53.0 1.3 %collective-permute-start.13 = (f32[32,640]{1,0:T(8,128)S(1)}, f32[32,640]{1,0:T(8,128)S(1)}, u32[]{:S(2)}, u32[]{:S(2)}) collective-permute-start(f32[32,640]{1,0:T(8,128)S(1)} %get-tuple-element.55), channel_id=1, source_target_pairs={{0,1},{1,0},{2,3},{3,2},{4,5},{5,4},{6,7},{7,6},{8,9},{9,8},{10,11... | collective-permute-start | bytes 245768 | tf_op jit(solution)/shard_map/ppermute | solution.py:333
  54.9 4.1 %collective-permute-start.14 = (f32[16,768]{1,0:T(8,128)S(1)}, f32[16,768]{1,0:T(8,128)S(1)}, u32[]{:S(2)}, u32[]{:S(2)}) collective-permute-start(f32[16,768]{1,0:T(8,128)S(1)} %get-tuple-element.57), channel_id=1, source_target_pairs={{0,2},{1,3},{2,0},{3,1},{4,6},{5,7},{6,4},{7,5},{8,10},{9,11},{10,... | collective-permute-start | bytes 147464 | tf_op jit(solution)/shard_map/ppermute | solution.py:333
  59.1 4.6 %collective-permute-start.15 = (f32[8,1792]{1,0:T(8,128)S(1)}, f32[8,1792]{1,0:T(8,128)S(1)}, u32[]{:S(2)}, u32[]{:S(2)}) collective-permute-start(f32[8,1792]{1,0:T(8,128)S(1)} %get-tuple-element.61), channel_id=1, source_target_pairs={{0,8},{4,12},{8,0},{12,4},{16,24},{20,28},{24,16},{28,20},{1,9},{5... | collective-permute-start | bytes 172040 | tf_op jit(solution)/shard_map/ppermute | solution.py:333
  59.1 6.7 %collective-permute-start.16 = (f32[8,1792]{1,0:T(8,128)S(1)}, f32[8,1792]{1,0:T(8,128)S(1)}, u32[]{:S(2)}, u32[]{:S(2)}) collective-permute-start(f32[8,1792]{1,0:T(8,128)S(1)} %get-tuple-element.62), channel_id=1, source_target_pairs={{0,16},{4,20},{8,24},{12,28},{16,0},{20,4},{24,8},{28,12},{1,17},{... | collective-permute-start | bytes 172040 | tf_op jit(solution)/shard_map/ppermute | solution.py:333
  62.9 6.2 %collective-permute-start.17 = (f32[8,1792]{1,0:T(8,128)S(1)}, f32[8,1792]{1,0:T(8,128)S(1)}, u32[]{:S(2)}, u32[]{:S(2)}) collective-permute-start(f32[8,1792]{1,0:T(8,128)S(1)} %get-tuple-element.63), channel_id=1, source_target_pairs={{0,24},{4,28},{8,16},{12,20},{16,8},{20,12},{24,0},{28,4},{1,25},{... | collective-permute-start | bytes 172040 | tf_op jit(solution)/shard_map/ppermute | solution.py:333
  69.1 4.5 %collective-permute-start.18 = (f32[8,1792]{1,0:T(8,128)S(1)}, f32[8,1792]{1,0:T(8,128)S(1)}, u32[]{:S(2)}, u32[]{:S(2)}) collective-permute-start(f32[8,1792]{1,0:T(8,128)S(1)} %replica_mean.3.refs_0_), channel_id=1, source_target_pairs={{0,8},{4,12},{8,0},{12,4},{16,24},{20,28},{24,16},{28,20},{1,9},{5... | collective-permute-start | bytes 172040 | tf_op jit(solution)/shard_map/ppermute | solution.py:333
  69.2 5.1 %collective-permute-start.19 = (f32[8,1792]{1,0:T(8,128)S(1)}, f32[8,1792]{1,0:T(8,128)S(1)}, u32[]{:S(2)}, u32[]{:S(2)}) collective-permute-start(f32[8,1792]{1,0:T(8,128)S(1)} %replica_mean.3.refs_0_), channel_id=1, source_target_pairs={{0,16},{4,20},{8,24},{12,28},{16,0},{20,4},{24,8},{28,12},{1,17},{... | collective-permute-start | bytes 172040 | tf_op jit(solution)/shard_map/ppermute | solution.py:333
  70.2 6.1 %collective-permute-start.20 = (f32[8,1792]{1,0:T(8,128)S(1)}, f32[8,1792]{1,0:T(8,128)S(1)}, u32[]{:S(2)}, u32[]{:S(2)}) collective-permute-start(f32[8,1792]{1,0:T(8,128)S(1)} %replica_mean.3.refs_0_), channel_id=1, source_target_pairs={{0,24},{4,28},{8,16},{12,20},{16,8},{20,12},{24,0},{28,4},{1,25},{... | collective-permute-start | bytes 172040 | tf_op jit(solution)/shard_map/ppermute | solution.py:333
  76.4 8.9 %collective-permute-start.21 = (f32[4,8,1792]{2,1,0:T(8,128)S(1)}, f32[4,8,1792]{2,1,0:T(8,128)S(1)}, u32[]{:S(2)}, u32[]{:S(2)}) collective-permute-start(f32[4,8,1792]{2,1,0:T(8,128)S(1)} %stack_z.3.mine), channel_id=1, source_target_pairs={{0,4},{4,0},{8,12},{12,8},{16,20},{20,16},{24,28},{28,24},{1,5},{5... | collective-permute-start | bytes 688136 | tf_op jit(solution)/shard_map/ppermute | solution.py:333
  86.0 4.1 %collective-permute-start.22 = (f32[16,640]{1,0:T(8,128)S(1)}, f32[16,640]{1,0:T(8,128)S(1)}, u32[]{:S(2)}, u32[]{:S(2)}) collective-permute-start(f32[16,640]{1,0:T(8,128)S(1)} %get-tuple-element.67.refs_0_), channel_id=1, source_target_pairs={{0,2},{1,3},{2,0},{3,1},{4,6},{5,7},{6,4},{7,5},{8,10},{9,11},{10,... | collective-permute-start | bytes 122888 | tf_op jit(solution)/shard_map/ppermute | solution.py:333
  90.1 2.4 %collective-permute-start.23 = (f32[32,640]{1,0:T(8,128)S(1)}, f32[32,640]{1,0:T(8,128)S(1)}, u32[]{:S(2)}, u32[]{:S(2)}) collective-permute-start(f32[32,640]{1,0:T(8,128)S(1)} %stack_x.3.mine), channel_id=1, source_target_pairs={{0,1},{1,0},{2,3},{3,2},{4,5},{5,4},{6,7},{7,6},{8,9},{9,8},{10,11... | collective-permute-start | bytes 245768 | tf_op jit(solution)/shard_map/ppermute | solution.py:333

commit v4 on v3

--- a/solution.py
+++ b/solution.py
@@ -87,36 +87,38 @@
     total[pl.ds(pl.multiple_of((1 - core) * rows, rows), rows), :] = other[:, :width]
 
 
-def left_product(g, e, q, pieces, total):
-    step = pl.program_id(0)
+def left_product(g, e, q, total, g_in, e_in, q_in, pieces, sems):
     rank = q.shape[0]
-    block = g.shape[1]
-
-    @pl.when(step == 0)
-    def _():
-        for i, piece in enumerate(split3(q[...])):
-            pieces[i * rank : (i + 1) * rank, :] = piece
-        pieces[3 * rank :, :] = jnp.zeros((rank, q.shape[1]), BF16)
-
-    t = dot(g[0], pieces[...], NT) + dot(e[0], pieces[...], NT)
-    t = (t[:, : 2 * rank] + t[:, 2 * rank :]).T
-    total[:, pl.ds(pl.multiple_of(step * block, 128), block)] = t[:rank] + t[rank:]
-
-
-def left_up_kernel(g, e, q, keep, send, pieces, total):
-    left_product(g, e, q, pieces, total)
-
-    @pl.when(pl.program_id(0) == STEPS - 1)
-    def _():
-        split_cores(total, None, keep, send)
-
-
-def left_down_kernel(g, e, q, keep, send, pieces, total, stage):
-    left_product(g, e, q, pieces, total)
-
-    @pl.when(pl.program_id(0) == STEPS - 1)
-    def _():
-        split_replicas(total, stage, keep, send)
+    block = g.shape[1] // STEPS
+    first = pltpu.make_async_copy(q, q_in, sems.at[2 * STEPS])
+    first.start()
+    copies = []
+    for i in range(STEPS):
+        rows = pl.ds(i * block, block)
+        pair = [pltpu.make_async_copy(src.at[0, rows, :], dst.at[rows, :], sems.at[2 * i + j]) for j, (src, dst) in enumerate(((g, g_in), (e, e_in)))]
+        for copy in pair:
+            copy.start()
+        copies.append(pair)
+    first.wait()
+    parts = split3(q_in[...])
+    pieces[...] = jnp.concatenate(parts + (jnp.zeros_like(parts[0]),), axis=0).T
+    for i, pair in enumerate(copies):
+        for copy in pair:
+            copy.wait()
+        rows = slice(i * block, (i + 1) * block)
+        t = dot(g_in[rows, :], pieces[...]) + dot(e_in[rows, :], pieces[...])
+        t = (t[:, : 2 * rank] + t[:, 2 * rank :]).T
+        total[:, rows] = t[:rank] + t[rank:]
+
+
+def left_up_kernel(g, e, q, keep, send, total, *scratch):
+    left_product(g, e, q, total, *scratch)
+    split_cores(total, None, keep, send)
+
+
+def left_down_kernel(g, e, q, keep, send, total, stage, *scratch):
+    left_product(g, e, q, total, *scratch)
+    split_replicas(total, stage, keep, send)
 
 
 def split_x_kernel(width, keep, got, *outs):
@@ -169,7 +171,7 @@
     out[...] = shard_rows(mine, other, ff, out.shape[0])
 
 
-def stack_x_kernel(width, *refs):
+def stack_x_kernel(width, _, *refs):
     _, x = place("tensor")
     *pieces, out = refs
     rows = pieces[0].shape[0]
@@ -215,29 +217,40 @@
 
 def inverse_factors(grams):
     rank = grams[0].shape[0]
+    count = rank // 8
+    panel = 4
     lane = lax.broadcasted_iota(jnp.int32, (8, 2 * rank), 1)
     row = lax.broadcasted_iota(jnp.int32, (8, 2 * rank), 0)
-    states = []
+    states, pivots = [], []
     for gram in grams:
         wide = jnp.concatenate([gram, jnp.zeros_like(gram)], axis=1)
         states.append([wide[i : i + 8] + (lane == row + (rank + i)).astype(F32) for i in range(0, rank, 8)])
-    for k in range(rank):
-        at, inner = divmod(k, 8)
-        for blocks in states:
-            pivot_row = blocks[at][inner : inner + 1, :]
-            scaled = pivot_row / pivot_row[:, k : k + 1]
-            for i in range(at, rank // 8):
-                column = blocks[i][:, k : k + 1]
-                if i == at:
-                    column = jnp.where(row[:, :1] > inner, column, 0.0)
-                blocks[i] = blocks[i] - column * scaled
+        pivots.append([])
+    for start in range(0, rank, panel):
+        at = start // 8
+        below = range(at, count)
+        spread = [
+            [{i: jnp.broadcast_to(blocks[i][:, start + j : start + j + 1], (8, 2 * rank)) for i in below} for j in range(panel)]
+            for blocks in states
+        ]
+        for j in range(panel):
+            inner = (start + j) % 8
+            for blocks, columns, found in zip(states, spread, pivots):
+                pivot = columns[j][at][inner : inner + 1, :]
+                found.append(pivot)
+                inverse = 1.0 / pivot
+                factor = {i: jnp.where(row > inner, columns[j][i], 0.0) if i == at else columns[j][i] for i in below}
+                for later in columns[j + 1 :]:
+                    head = later[at][inner : inner + 1, :] * inverse
+                    for i in below:
+                        later[i] = later[i] - factor[i] * head
+                scaled = blocks[at][inner : inner + 1, :] * inverse
+                for i in below:
+                    blocks[i] = blocks[i] - factor[i] * scaled
     results = []
-    for blocks in states:
-        rows = []
-        for i, block in enumerate(blocks):
-            diagonal = jnp.sum(jnp.where(lane == row + 8 * i, block, 0.0), axis=1, keepdims=True)
-            rows.append((block / jnp.sqrt(diagonal))[:, rank:])
-        results.append(jnp.concatenate(rows, axis=0))
+    for blocks, found in zip(states, pivots):
+        rows = [block / jnp.sqrt(jnp.concatenate(found[8 * i : 8 * i + 8], axis=0)) for i, block in enumerate(blocks)]
+        results.append(jnp.concatenate(rows, axis=0)[:, rank:])
     return results
 
 
@@ -339,8 +352,9 @@
     rows, columns = keep.shape[0] // n_x, keep.shape[1]
     out = shaped(rows, width + (columns - width) * n_x)
     parts = call(
-        functools.partial(split_x_kernel, width), [out] * n_x + [shaped(*keep.shape)], keep, got, name="split_x"
-    )[:n_x]
+        functools.partial(split_x_kernel, width), [out] * n_x, keep, got, name="split_x",
+        scratch_shapes=[pltpu.VMEM(keep.shape, F32)],
+    )
     return [parts[0]] + [swap(parts[j], "tensor", 2 * j) for j in range(1, n_x)]
 
 
@@ -363,11 +377,11 @@
     return mine, swap(mine, "dp", 1), gram
 
 
-def gather_shards(rows_here, width):
+def gather_shards(rows_here, width, meanwhile):
     n_x = lax.axis_size("tensor") // 2
     rows, columns = rows_here.shape
     pieces = [rows_here] + [swap(rows_here, "tensor", 2 * j) for j in range(1, n_x)]
-    mine = call(functools.partial(stack_x_kernel, width), shaped(rows * n_x, columns), *pieces, name="stack_x")
+    mine = call(functools.partial(stack_x_kernel, width), shaped(rows * n_x, columns), meanwhile, *pieces, name="stack_x", in_specs=[pl.BlockSpec(memory_space=pl.ANY)] + [VMEM] * n_x)
     return mine, swap(mine, "tensor", 1)
 
 
@@ -384,26 +398,25 @@
     narrow = pltpu.VMEM((rank, rows), F32)
     product = 4 * rows * ff * 4 * rank
 
-    keep_up, send_up = call(
-        left_up_kernel, [core_half] * 2, gu, eu, qu, name="left_up", flops=product, limit=60, grid=(STEPS,),
-        in_specs=[replica_blocks(rows, ff)] * 2 + [whole(qu.shape)], out_specs=[whole(core_half.shape)] * 2,
-        scratch_shapes=[pltpu.VMEM((4 * rank, ff), BF16), narrow],
-    )
+    def left(kernel, outs, g, e, q, scratch, name):
+        buffers = [pltpu.VMEM(g.shape[1:], BF16)] * 2 + [pltpu.VMEM(q.shape, F32), pltpu.VMEM((q.shape[1], 4 * rank), BF16)]
+        return call(
+            kernel, outs, g, e, q, name=name, flops=product, limit=61, in_specs=[pl.BlockSpec(memory_space=pltpu.HBM)] * 3,
+            scratch_shapes=scratch + buffers + [pltpu.SemaphoreType.DMA((2 * STEPS + 1,))],
+        )
+
+    keep_up, send_up = left(left_up_kernel, [core_half] * 2, gu, eu, qu, [narrow], "left_up")
     shards = sum_shards(keep_up, send_up, rows)
-    keep, send = call(
-        left_down_kernel, [replica_half] * 2, gd, ed, qd, name="left_down", flops=product, limit=60, grid=(STEPS,),
-        in_specs=[replica_blocks(ff, rows)] * 2 + [whole(qd.shape)], out_specs=[whole(replica_half.shape)] * 2,
-        scratch_shapes=[pltpu.VMEM((4 * rank, rows), BF16), wide, stage],
-    )
+    keep, send = left(left_down_kernel, [replica_half] * 2, gd, ed, qd, [wide, stage], "left_down")
     mine, other, _ = mean_replicas(keep, swap(send, "dp", 1), shards, rows)
 
     shard = call(functools.partial(shard_rows_kernel, ff), shaped(rank // n_shards, rows), mine, other, name="shard_rows")
-    left_half, left_other = gather_shards(shard, rows)
     core_half = shaped(rank // 2, rows + 2 * rank)
     left_down, keep_down, send_down = call(
         right_down_kernel, [shaped(rank, ff), core_half, core_half], mine, other, gd, ed, name="right_down", flops=product,
         in_specs=[VMEM] * 4, scratch_shapes=[pltpu.VMEM((3 * rank, ff), BF16), narrow, stage],
     )
+    left_half, left_other = gather_shards(shard, rows, left_down)
     shards = sum_shards(keep_down, send_down, rows)
     left_up, gram_up, keep, send = call(
         right_up_kernel, [shaped(rank, rows), shaped(rank, rank), replica_half, replica_half], left_half, left_other, gu, eu,
@@ -419,11 +432,11 @@
         factor_up_kernel, [shaped(4 * rank, ff, dtype=BF16), shaped(rank // n_shards, rows + 128)], mine, other, inv_up,
         name="factor_up", scratch_shapes=[wide, stage],
     )
-    right_half, right_other = gather_shards(shard, rows)
     new_error_up = call(
         error_up_kernel, shaped(1, rows, ff, dtype=BF16), gu, eu, lhs_up, rhs_up, name="error_up", flops=product // 2,
         grid=(STEPS,), in_specs=[VMEM] * 4, out_specs=replica_blocks(rows, ff),
     )
+    right_half, right_other = gather_shards(shard, rows, new_error_up)
     limit = CLIP_RMS * (2.0 * rows * ff * n_shards) ** 0.5
     rhs_down, clip = call(
         functools.partial(factor_down_kernel, limit), [shaped(4 * rank, rows, dtype=BF16), shaped(8, 128)],

time: 96.3 us -> 89.5 us (0.929)
  Pallas kernels: 27.5 us -> 21.4 us
  local copies, waits for them, and re-layouts: 0.86 us -> 2.27 us
  waiting for transfers between devices: 37 us -> 35.9 us
    pallas_call x20, Pallas kernels: 27.5 us -> 21.4 us  [call(): pl.pallas_call(kernel, out_shape=out_shape, compiler_params=params, cost_...]
    unnamed x12 -> x14, local copies, waits for them, and re-layouts: 0.86 us -> 2.27 us
    ppermute x24, waiting for transfers between devices: 37 us -> 35.9 us  [swap(): return lax.ppermute(x, axis, pairs)]
  transfers between devices with their start and end apart: 24 -> 24, of which waited for: 18 -> 20; matrix products, arithmetic and copies ran while one was open for 0% -> 0% of each run, Pallas kernels for 18% -> 13%
where the time goes in v4:
time: 89.5 us; the launch traced here: 89.4 us
  waiting for transfers between devices  35.9 us (40%)
  starting transfers between devices  29 us (32%)
  Pallas kernels  21.4 us (24%)
  local copies, waits for them, and re-layouts  2.27 us (3%)
    ppermute x24, waiting for transfers between devices, swap(): return lax.ppermute(x, axis, pairs)  35.9 us
    ppermute x24, starting transfers between devices, swap(): return lax.ppermute(x, axis, pairs)  29 us
    pallas_call x20, Pallas kernels, call(): pl.pallas_call(kernel, out_shape=out_shape, compiler_params=params, cost_...  21.4 us
    unnamed x14, local copies, waits for them, and re-layouts  2.27 us
  transfers between devices with their start and end apart: 24, of which 20 were waited for; matrix products, arithmetic and copies ran while one was open for 0% of the time, Pallas kernels for 13%

profile of v4, /device:TPU:0, one launch (start us, length us, event | category | flops | bytes accessed | tf_op | source)
XLA Modules:
  0.0 89.4 jit_solution(12929598379025055926)
XLA Ops:
  0.6 4.5 %left_down.1 = (f32[4,8,1536]{2,1,0:T(8,128)}, f32[4,8,1536]{2,1,0:T(8,128)}) custom-call(bf16[1,1536,512]{2,1,0:T(8,128)(2,1)} %g.11, bf16[1,1536,512]{2,1,0:T(8,128)(2,1)} %e.11, f32[64,512]{1,0:T(8,128)} %bitcast.3), custom_call_target="tpu_custom_call" | custom-call | flops 805306368 | bytes 3670016 | tf_op jit(solution)/shard_map/left_down/pallas_call | solution.py:341
  5.2 3.0 %collective-permute-start = (f32[4,8,1536]{2,1,0:T(8,128)}, f32[4,8,1536]{2,1,0:T(8,128)S(1)}, u32[]{:S(2)}, u32[]{:S(2)}) collective-permute-start(f32[4,8,1536]{2,1,0:T(8,128)} %get-tuple-element.40), channel_id=1, source_target_pairs={{0,4},{4,0},{8,12},{12,8},{16,20},{20,16},{24,28},{28,24},{1,5},{5... | collective-permute-start | bytes 589832 | tf_op jit(solution)/shard_map/ppermute | solution.py:346
  8.2 4.6 %left_up.1 = (f32[32,512]{1,0:T(8,128)}, f32[32,512]{1,0:T(8,128)}) custom-call(bf16[1,512,1536]{2,1,0:T(8,128)(2,1)} %g.10, bf16[1,512,1536]{2,1,0:T(8,128)(2,1)} %e.10, f32[64,1536]{1,0:T(8,128)} %bitcast.2), custom_call_target="tpu_custom_call" | custom-call | flops 805306368 | bytes 3670016 | tf_op jit(solution)/shard_map/left_up/pallas_call | solution.py:341
  12.8 0.0 copy-start.2
  12.9 0.1 collective-permute-start.1
  12.9 1.5 %collective-permute-done.1.got = f32[32,512]{1,0:T(8,128)S(1)} collective-permute-done((f32[32,512]{1,0:T(8,128)}, f32[32,512]{1,0:T(8,128)S(1)}, u32[]{:S(2)}, u32[]{:S(2)}) %collective-permute-start.1) | collective-permute-done | bytes 65568 | tf_op jit(solution)/shard_map/ppermute | solution.py:346
  14.4 0.8 copy-done.6
  15.2 1.6 %collective-permute-start.2 = (f32[16,512]{1,0:T(8,128)S(1)}, f32[16,512]{1,0:T(8,128)S(1)}, u32[]{:S(2)}, u32[]{:S(2)}) collective-permute-start(f32[16,512]{1,0:T(8,128)S(1)} %get-tuple-element.44), channel_id=1, source_target_pairs={{0,2},{1,3},{2,0},{3,1},{4,6},{5,7},{6,4},{7,5},{8,10},{9,11},{10,... | collective-permute-start | bytes 98312 | tf_op jit(solution)/shard_map/ppermute | solution.py:346
  16.8 2.4 %collective-permute-done.2.refs_1_ = f32[16,512]{1,0:T(8,128)S(1)} collective-permute-done((f32[16,512]{1,0:T(8,128)S(1)}, f32[16,512]{1,0:T(8,128)S(1)}, u32[]{:S(2)}, u32[]{:S(2)}) %collective-permute-start.2) | collective-permute-done | bytes 32800 | tf_op jit(solution)/shard_map/ppermute | solution.py:346
  19.2 0.0 collective-permute-done.got
  19.2 0.0 copy-done.5
  19.3 1.6 %collective-permute-start.3 = (f32[8,1792]{1,0:T(8,128)S(1)}, f32[8,1792]{1,0:T(8,128)S(1)}, u32[]{:S(2)}, u32[]{:S(2)}) collective-permute-start(f32[8,1792]{1,0:T(8,128)S(1)} %get-tuple-element.46), channel_id=1, source_target_pairs={{0,8},{4,12},{8,0},{12,4},{16,24},{20,28},{24,16},{28,20},{1,9},{5... | collective-permute-start | bytes 172040 | tf_op jit(solution)/shard_map/ppermute | solution.py:346
  20.9 2.6 %collective-permute-start.4 = (f32[8,1792]{1,0:T(8,128)S(1)}, f32[8,1792]{1,0:T(8,128)S(1)}, u32[]{:S(2)}, u32[]{:S(2)}) collective-permute-start(f32[8,1792]{1,0:T(8,128)S(1)} %get-tuple-element.47), channel_id=1, source_target_pairs={{0,16},{4,20},{8,24},{12,28},{16,0},{20,4},{24,8},{28,12},{1,17},{... | collective-permute-start | bytes 172040 | tf_op jit(solution)/shard_map/ppermute | solution.py:346
  23.5 0.2 collective-permute-start.5
  23.7 0.3 collective-permute-done.3.refs_1_
  24.1 3.2 %collective-permute-done.4.refs_2_ = f32[8,1792]{1,0:T(8,128)S(1)} collective-permute-done((f32[8,1792]{1,0:T(8,128)S(1)}, f32[8,1792]{1,0:T(8,128)S(1)}, u32[]{:S(2)}, u32[]{:S(2)}) %collective-permute-start.4) | collective-permute-done | bytes 57376 | tf_op jit(solution)/shard_map/ppermute | solution.py:346
  27.2 2.3 %collective-permute-done.5.refs_3_ = f32[8,1792]{1,0:T(8,128)S(1)} collective-permute-done((f32[8,1792]{1,0:T(8,128)S(1)}, f32[8,1792]{1,0:T(8,128)S(1)}, u32[]{:S(2)}, u32[]{:S(2)}) %collective-permute-start.5) | collective-permute-done | bytes 57376 | tf_op jit(solution)/shard_map/ppermute | solution.py:346
  29.5 0.8 collective-permute-start.8
  30.3 0.0 collective-permute-start.7
  30.3 3.7 %collective-permute-start.6 = (f32[8,1792]{1,0:T(8,128)S(1)}, f32[8,1792]{1,0:T(8,128)S(1)}, u32[]{:S(2)}, u32[]{:S(2)}) collective-permute-start(f32[8,1792]{1,0:T(8,128)S(1)} %replica_mean.2.refs_0_), channel_id=1, source_target_pairs={{0,8},{4,12},{8,0},{12,4},{16,24},{20,28},{24,16},{28,20},{1,9},{5... | collective-permute-start | bytes 172040 | tf_op jit(solution)/shard_map/ppermute | solution.py:346
  34.0 1.7 %collective-permute-done.8.refs_3_ = f32[8,1792]{1,0:T(8,128)S(1)} collective-permute-done((f32[8,1792]{1,0:T(8,128)S(1)}, f32[8,1792]{1,0:T(8,128)S(1)}, u32[]{:S(2)}, u32[]{:S(2)}) %collective-permute-start.8) | collective-permute-done | bytes 57376 | tf_op jit(solution)/shard_map/ppermute | solution.py:346
  35.7 0.9 %collective-permute-done.7.refs_2_ = f32[8,1792]{1,0:T(8,128)S(1)} collective-permute-done((f32[8,1792]{1,0:T(8,128)S(1)}, f32[8,1792]{1,0:T(8,128)S(1)}, u32[]{:S(2)}, u32[]{:S(2)}) %collective-permute-start.7) | collective-permute-done | bytes 57376 | tf_op jit(solution)/shard_map/ppermute | solution.py:346
  36.6 0.0 collective-permute-done.6.refs_1_
  36.6 0.6 collective-permute-start.9
  37.2 5.5 %collective-permute-done.9.other = f32[4,8,1792]{2,1,0:T(8,128)S(1)} collective-permute-done((f32[4,8,1792]{2,1,0:T(8,128)S(1)}, f32[4,8,1792]{2,1,0:T(8,128)S(1)}, u32[]{:S(2)}, u32[]{:S(2)}) %collective-permute-start.9) | collective-permute-done | bytes 229408 | tf_op jit(solution)/shard_map/ppermute | solution.py:346
  42.7 0.0 copy-start.1
  42.7 1.6 %collective-permute-start.10 = (f32[16,512]{1,0:T(8,128)S(1)}, f32[16,512]{1,0:T(8,128)S(1)}, u32[]{:S(2)}, u32[]{:S(2)}) collective-permute-start(f32[16,512]{1,0:T(8,128)S(1)} %shard_rows.1.refs_0_), channel_id=1, source_target_pairs={{0,2},{1,3},{2,0},{3,1},{4,6},{5,7},{6,4},{7,5},{8,10},{9,11},{10,... | collective-permute-start | bytes 98312 | tf_op jit(solution)/shard_map/ppermute | solution.py:346
  44.3 0.0 copy-done.3
  44.3 1.2 %right_down.1 = (f32[64,1536]{1,0:T(8,128)S(1)}, f32[32,640]{1,0:T(8,128)S(1)}, f32[32,640]{1,0:T(8,128)S(1)}) custom-call(f32[4,8,1792]{2,1,0:T(8,128)S(1)} %stack_z.2.mine, f32[4,8,1792]{2,1,0:T(8,128)S(1)} %collective-permute-done.9.other, bf16[1,1536,512]{2,1,0:T(8,128)(2,1)S(1)} %copy-done.2, bf16[1,1536,512]{2,1,0:T(8,128)(2,1)S(1)} %copy-done.3), custom_call_target="tpu_custom_call" | custom-call | flops 805306368 | bytes 4161536 | tf_op jit(solution)/shard_map/right_down/pallas_call | solution.py:341
  45.5 1.2 %collective-permute-done.10.refs_1_ = f32[16,512]{1,0:T(8,128)S(1)} collective-permute-done((f32[16,512]{1,0:T(8,128)S(1)}, f32[16,512]{1,0:T(8,128)S(1)}, u32[]{:S(2)}, u32[]{:S(2)}) %collective-permute-start.10) | collective-permute-done | bytes 32800 | tf_op jit(solution)/shard_map/ppermute | solution.py:346
  46.7 0.1 collective-permute-start.11
  46.8 1.2 %collective-permute-done.11.other = f32[32,512]{1,0:T(8,128)S(1)} collective-permute-done((f32[32,512]{1,0:T(8,128)S(1)}, f32[32,512]{1,0:T(8,128)S(1)}, u32[]{:S(2)}, u32[]{:S(2)}) %collective-permute-start.11) | collective-permute-done | bytes 65568 | tf_op jit(solution)/shard_map/ppermute | solution.py:346
  48.1 1.2 %right_up.1 = (f32[64,512]{1,0:T(8,128)S(1)}, f32[64,64]{1,0:T(8,128)S(1)}, f32[4,8,1536]{2,1,0:T(8,128)S(1)}, f32[4,8,1536]{2,1,0:T(8,128)S(1)}) custom-call(f32[32,512]{1,0:T(8,128)S(1)} %stack_x.2.mine, f32[32,512]{1,0:T(8,128)S(1)} %collective-permute-done.11.other, bf16[1,512,1536]{2,1,0:T(8,128)(2,1)S(1)} %copy-done, bf16[1,512,1536]{2,1,0:T(8,128)(2,1)S(1)} %copy-done.1), custom_call_target="tpu_custom_call" | custom-call | flops 805306368 | bytes 3817472 | tf_op jit(solution)/shard_map/right_up/pallas_call | solution.py:341
  49.3 0.6 collective-permute-start.12
  49.8 0.0 collective-permute-start.13
  49.8 1.3 %collective-permute-done.13.got = f32[32,640]{1,0:T(8,128)S(1)} collective-permute-done((f32[32,640]{1,0:T(8,128)S(1)}, f32[32,640]{1,0:T(8,128)S(1)}, u32[]{:S(2)}, u32[]{:S(2)}) %collective-permute-start.13) | collective-permute-done | bytes 81952 | tf_op jit(solution)/shard_map/ppermute | solution.py:346
  51.1 1.6 %collective-permute-start.14 = (f32[16,768]{1,0:T(8,128)S(1)}, f32[16,768]{1,0:T(8,128)S(1)}, u32[]{:S(2)}, u32[]{:S(2)}) collective-permute-start(f32[16,768]{1,0:T(8,128)S(1)} %get-tuple-element.57), channel_id=1, source_target_pairs={{0,2},{1,3},{2,0},{3,1},{4,6},{5,7},{6,4},{7,5},{8,10},{9,11},{10,... | collective-permute-start | bytes 147464 | tf_op jit(solution)/shard_map/ppermute | solution.py:346
  52.7 2.6 %collective-permute-done.14.refs_1_ = f32[16,768]{1,0:T(8,128)S(1)} collective-permute-done((f32[16,768]{1,0:T(8,128)S(1)}, f32[16,768]{1,0:T(8,128)S(1)}, u32[]{:S(2)}, u32[]{:S(2)}) %collective-permute-start.14) | collective-permute-done | bytes 49184 | tf_op jit(solution)/shard_map/ppermute | solution.py:346
  55.3 1.0 %collective-permute-done.12.got = f32[4,8,1536]{2,1,0:T(8,128)S(1)} collective-permute-done((f32[4,8,1536]{2,1,0:T(8,128)S(1)}, f32[4,8,1536]{2,1,0:T(8,128)S(1)}, u32[]{:S(2)}, u32[]{:S(2)}) %collective-permute-start.12) | collective-permute-done | bytes 196640 | tf_op jit(solution)/shard_map/ppermute | solution.py:346
  56.3 0.1 split_z.3
  56.4 1.6 %collective-permute-start.15 = (f32[8,1792]{1,0:T(8,128)S(1)}, f32[8,1792]{1,0:T(8,128)S(1)}, u32[]{:S(2)}, u32[]{:S(2)}) collective-permute-start(f32[8,1792]{1,0:T(8,128)S(1)} %get-tuple-element.61), channel_id=1, source_target_pairs={{0,8},{4,12},{8,0},{12,4},{16,24},{20,28},{24,16},{28,20},{1,9},{5... | collective-permute-start | bytes 172040 | tf_op jit(solution)/shard_map/ppermute | solution.py:346
  57.9 0.9 %collective-permute-start.16 = (f32[8,1792]{1,0:T(8,128)S(1)}, f32[8,1792]{1,0:T(8,128)S(1)}, u32[]{:S(2)}, u32[]{:S(2)}) collective-permute-start(f32[8,1792]{1,0:T(8,128)S(1)} %get-tuple-element.62), channel_id=1, source_target_pairs={{0,16},{4,20},{8,24},{12,28},{16,0},{20,4},{24,8},{28,12},{1,17},{... | collective-permute-start | bytes 172040 | tf_op jit(solution)/shard_map/ppermute | solution.py:346
  58.8 1.9 %collective-permute-start.17 = (f32[8,1792]{1,0:T(8,128)S(1)}, f32[8,1792]{1,0:T(8,128)S(1)}, u32[]{:S(2)}, u32[]{:S(2)}) collective-permute-start(f32[8,1792]{1,0:T(8,128)S(1)} %get-tuple-element.63), channel_id=1, source_target_pairs={{0,24},{4,28},{8,16},{12,20},{16,8},{20,12},{24,0},{28,4},{1,25},{... | collective-permute-start | bytes 172040 | tf_op jit(solution)/shard_map/ppermute | solution.py:346
  60.8 0.0 collective-permute-done.15.refs_1_
  60.8 3.3 %collective-permute-done.16.refs_2_ = f32[8,1792]{1,0:T(8,128)S(1)} collective-permute-done((f32[8,1792]{1,0:T(8,128)S(1)}, f32[8,1792]{1,0:T(8,128)S(1)}, u32[]{:S(2)}, u32[]{:S(2)}) %collective-permute-start.16) | collective-permute-done | bytes 57376 | tf_op jit(solution)/shard_map/ppermute | solution.py:346
  64.1 0.8 collective-permute-done.17.refs_3_
  64.9 1.9 %collective-permute-start.20 = (f32[8,1792]{1,0:T(8,128)S(1)}, f32[8,1792]{1,0:T(8,128)S(1)}, u32[]{:S(2)}, u32[]{:S(2)}) collective-permute-start(f32[8,1792]{1,0:T(8,128)S(1)} %replica_mean.3.refs_0_), channel_id=1, source_target_pairs={{0,24},{4,28},{8,16},{12,20},{16,8},{20,12},{24,0},{28,4},{1,25},{... | collective-permute-start | bytes 172040 | tf_op jit(solution)/shard_map/ppermute | solution.py:346
  66.9 0.6 collective-permute-start.19
  67.5 1.9 %collective-permute-start.18 = (f32[8,1792]{1,0:T(8,128)S(1)}, f32[8,1792]{1,0:T(8,128)S(1)}, u32[]{:S(2)}, u32[]{:S(2)}) collective-permute-start(f32[8,1792]{1,0:T(8,128)S(1)} %replica_mean.3.refs_0_), channel_id=1, source_target_pairs={{0,8},{4,12},{8,0},{12,4},{16,24},{20,28},{24,16},{28,20},{1,9},{5... | collective-permute-start | bytes 172040 | tf_op jit(solution)/shard_map/ppermute | solution.py:346
  69.4 1.6 %collective-permute-done.20.refs_3_ = f32[8,1792]{1,0:T(8,128)S(1)} collective-permute-done((f32[8,1792]{1,0:T(8,128)S(1)}, f32[8,1792]{1,0:T(8,128)S(1)}, u32[]{:S(2)}, u32[]{:S(2)}) %collective-permute-start.20) | collective-permute-done | bytes 57376 | tf_op jit(solution)/shard_map/ppermute | solution.py:346
  71.0 1.3 %collective-permute-done.19.refs_2_ = f32[8,1792]{1,0:T(8,128)S(1)} collective-permute-done((f32[8,1792]{1,0:T(8,128)S(1)}, f32[8,1792]{1,0:T(8,128)S(1)}, u32[]{:S(2)}, u32[]{:S(2)}) %collective-permute-start.19) | collective-permute-done | bytes 57376 | tf_op jit(solution)/shard_map/ppermute | solution.py:346
  72.3 0.0 collective-permute-done.18.refs_1_
  72.3 0.6 collective-permute-start.21
  72.9 3.2 %basis.1 = (f32[64,64]{1,0:T(8,128)S(1)}, f32[64,64]{1,0:T(8,128)S(1)}, bf16[512,256]{1,0:T(8,128)(2,1)S(1)}, bf16[1536,256]{1,0:T(8,128)(2,1)S(1)}) custom-call(f32[64,512]{1,0:T(8,128)S(1)} %get-tuple-element.50.left_up, f32[64,1536]{1,0:T(8,128)S(1)} %get-tuple-element.49._.left_down, f32[64,64]{1,0:T(8,128)S(1)} %get-tuple-element.51.gram_up, ...), custom_call_target="tpu_custom_call" | custom-call | flops 1000000000 | bytes 1638400 | tf_op jit(solution)/shard_map/basis/pallas_call | solution.py:341
  76.0 2.3 %collective-permute-done.21.other = f32[4,8,1792]{2,1,0:T(8,128)S(1)} collective-permute-done((f32[4,8,1792]{2,1,0:T(8,128)S(1)}, f32[4,8,1792]{2,1,0:T(8,128)S(1)}, u32[]{:S(2)}, u32[]{:S(2)}) %collective-permute-start.21) | collective-permute-done | bytes 229408 | tf_op jit(solution)/shard_map/ppermute | solution.py:346
  78.4 0.7 factor_up.1
  79.1 1.6 %collective-permute-start.22 = (f32[16,640]{1,0:T(8,128)S(1)}, f32[16,640]{1,0:T(8,128)S(1)}, u32[]{:S(2)}, u32[]{:S(2)}) collective-permute-start(f32[16,640]{1,0:T(8,128)S(1)} %get-tuple-element.67.refs_0_), channel_id=1, source_target_pairs={{0,2},{1,3},{2,0},{3,1},{4,6},{5,7},{6,4},{7,5},{8,10},{9,11},{10,... | collective-permute-start | bytes 122888 | tf_op jit(solution)/shard_map/ppermute | solution.py:346
  80.6 2.3 %error_up.1._ = bf16[1,512,1536]{2,1,0:T(8,128)(2,1)} custom-call(bf16[1,512,1536]{2,1,0:T(8,128)(2,1)S(1)} %copy-done, bf16[1,512,1536]{2,1,0:T(8,128)(2,1)S(1)} %copy-done.1, bf16[512,256]{1,0:T(8,128)(2,1)S(1)} %get-tuple-element.59.lhs.lhs_up, bf16[256,1536]{1,0:T(8,128)(2,1)S(1)} %get-tuple-element.65.rhs.rhs_up), custom_call_target="tpu_custom_call" | custom-call | flops 402653184 | bytes 5767168 | tf_op jit(solution)/shard_map/error_up/pallas_call | solution.py:341
  83.0 0.2 collective-permute-done.22.refs_1_
  83.1 1.4 %copy-done.4 = bf16[1,512,1536]{2,1,0:T(8,128)(2,1)S(1)} copy-done((bf16[1,512,1536]{2,1,0:T(8,128)(2,1)S(1)}, bf16[1,512,1536]{2,1,0:T(8,128)(2,1)}, u32[]{:S(2)}) %copy-start.4) | copy-done | bytes 1572888
  84.6 0.1 collective-permute-start.23
  84.6 1.3 %collective-permute-done.23.other = f32[32,640]{1,0:T(8,128)S(1)} collective-permute-done((f32[32,640]{1,0:T(8,128)S(1)}, f32[32,640]{1,0:T(8,128)S(1)}, u32[]{:S(2)}, u32[]{:S(2)}) %collective-permute-start.23) | collective-permute-done | bytes 81952 | tf_op jit(solution)/shard_map/ppermute | solution.py:346
  85.9 0.4 factor_down.1
  86.3 3.0 %last.1 = (bf16[1,1536,512]{2,1,0:T(8,128)(2,1)}, bf16[512,1536]{1,0:T(8,128)(2,1)}, bf16[1536,512]{1,0:T(8,128)(2,1)}) custom-call(bf16[1,1536,512]{2,1,0:T(8,128)(2,1)S(1)} %copy-done.2, bf16[1,1536,512]{2,1,0:T(8,128)(2,1)S(1)} %copy-done.3, bf16[512,256]{1,0:T(8,128)(2,1)S(1)} %get-tuple-element.59.lhs.lhs_up, ...), custom_call_target="tpu_custom_call" | custom-call | flops 805306368 | bytes 9965568 | tf_op jit(solution)/shard_map/last/pallas_call | solution.py:341
  (18 shorter events, 0.2 us)
Async XLA Ops:
  5.2 14.1 %collective-permute-start = (f32[4,8,1536]{2,1,0:T(8,128)}, f32[4,8,1536]{2,1,0:T(8,128)S(1)}, u32[]{:S(2)}, u32[]{:S(2)}) collective-permute-start(f32[4,8,1536]{2,1,0:T(8,128)} %get-tuple-element.40), channel_id=1, source_target_pairs={{0,4},{4,0},{8,12},{12,8},{16,20},{20,16},{24,28},{28,24},{1,5},{5... | collective-permute-start | bytes 589832 | tf_op jit(solution)/shard_map/ppermute | solution.py:346
  8.2 11.0 %copy-start.5 = (f32[4,8,1536]{2,1,0:T(8,128)S(1)}, f32[4,8,1536]{2,1,0:T(8,128)}, u32[]{:S(2)}) copy-start(f32[4,8,1536]{2,1,0:T(8,128)} %get-tuple-element.39.keep) | copy-start | bytes 589828
  8.2 36.1 %copy-start.3 = (bf16[1,1536,512]{2,1,0:T(8,128)(2,1)S(1)}, bf16[1,1536,512]{2,1,0:T(8,128)(2,1)}, u32[]{:S(2)}) copy-start(bf16[1,1536,512]{2,1,0:T(8,128)(2,1)} %e.11) | copy-start | bytes 4718596
  12.8 31.5 %copy-start.2 = (bf16[1,1536,512]{2,1,0:T(8,128)(2,1)S(1)}, bf16[1,1536,512]{2,1,0:T(8,128)(2,1)}, u32[]{:S(2)}) copy-start(bf16[1,1536,512]{2,1,0:T(8,128)(2,1)} %g.11) | copy-start | bytes 4718596
  12.9 1.5 %collective-permute-start.1 = (f32[32,512]{1,0:T(8,128)}, f32[32,512]{1,0:T(8,128)S(1)}, u32[]{:S(2)}, u32[]{:S(2)}) collective-permute-start(f32[32,512]{1,0:T(8,128)} %get-tuple-element.42), channel_id=1, source_target_pairs={{0,1},{1,0},{2,3},{3,2},{4,5},{5,4},{6,7},{7,6},{8,9},{9,8},{10,11... | collective-permute-start | bytes 196616 | tf_op jit(solution)/shard_map/ppermute | solution.py:346
  14.4 0.8 copy-start.6
  15.2 4.0 %collective-permute-start.2 = (f32[16,512]{1,0:T(8,128)S(1)}, f32[16,512]{1,0:T(8,128)S(1)}, u32[]{:S(2)}, u32[]{:S(2)}) collective-permute-start(f32[16,512]{1,0:T(8,128)S(1)} %get-tuple-element.44), channel_id=1, source_target_pairs={{0,2},{1,3},{2,0},{3,1},{4,6},{5,7},{6,4},{7,5},{8,10},{9,11},{10,... | collective-permute-start | bytes 98312 | tf_op jit(solution)/shard_map/ppermute | solution.py:346
  19.3 4.8 %collective-permute-start.3 = (f32[8,1792]{1,0:T(8,128)S(1)}, f32[8,1792]{1,0:T(8,128)S(1)}, u32[]{:S(2)}, u32[]{:S(2)}) collective-permute-start(f32[8,1792]{1,0:T(8,128)S(1)} %get-tuple-element.46), channel_id=1, source_target_pairs={{0,8},{4,12},{8,0},{12,4},{16,24},{20,28},{24,16},{28,20},{1,9},{5... | collective-permute-start | bytes 172040 | tf_op jit(solution)/shard_map/ppermute | solution.py:346
  20.9 6.3 %collective-permute-start.4 = (f32[8,1792]{1,0:T(8,128)S(1)}, f32[8,1792]{1,0:T(8,128)S(1)}, u32[]{:S(2)}, u32[]{:S(2)}) collective-permute-start(f32[8,1792]{1,0:T(8,128)S(1)} %get-tuple-element.47), channel_id=1, source_target_pairs={{0,16},{4,20},{8,24},{12,28},{16,0},{20,4},{24,8},{28,12},{1,17},{... | collective-permute-start | bytes 172040 | tf_op jit(solution)/shard_map/ppermute | solution.py:346
  23.5 6.0 %collective-permute-start.5 = (f32[8,1792]{1,0:T(8,128)S(1)}, f32[8,1792]{1,0:T(8,128)S(1)}, u32[]{:S(2)}, u32[]{:S(2)}) collective-permute-start(f32[8,1792]{1,0:T(8,128)S(1)} %get-tuple-element.48), channel_id=1, source_target_pairs={{0,24},{4,28},{8,16},{12,20},{16,8},{20,12},{24,0},{28,4},{1,25},{... | collective-permute-start | bytes 172040 | tf_op jit(solution)/shard_map/ppermute | solution.py:346
  29.5 6.2 %collective-permute-start.8 = (f32[8,1792]{1,0:T(8,128)S(1)}, f32[8,1792]{1,0:T(8,128)S(1)}, u32[]{:S(2)}, u32[]{:S(2)}) collective-permute-start(f32[8,1792]{1,0:T(8,128)S(1)} %replica_mean.2.refs_0_), channel_id=1, source_target_pairs={{0,24},{4,28},{8,16},{12,20},{16,8},{20,12},{24,0},{28,4},{1,25},{... | collective-permute-start | bytes 172040 | tf_op jit(solution)/shard_map/ppermute | solution.py:346
  30.3 6.3 %collective-permute-start.7 = (f32[8,1792]{1,0:T(8,128)S(1)}, f32[8,1792]{1,0:T(8,128)S(1)}, u32[]{:S(2)}, u32[]{:S(2)}) collective-permute-start(f32[8,1792]{1,0:T(8,128)S(1)} %replica_mean.2.refs_0_), channel_id=1, source_target_pairs={{0,16},{4,20},{8,24},{12,28},{16,0},{20,4},{24,8},{28,12},{1,17},{... | collective-permute-start | bytes 172040 | tf_op jit(solution)/shard_map/ppermute | solution.py:346
  30.3 6.3 %collective-permute-start.6 = (f32[8,1792]{1,0:T(8,128)S(1)}, f32[8,1792]{1,0:T(8,128)S(1)}, u32[]{:S(2)}, u32[]{:S(2)}) collective-permute-start(f32[8,1792]{1,0:T(8,128)S(1)} %replica_mean.2.refs_0_), channel_id=1, source_target_pairs={{0,8},{4,12},{8,0},{12,4},{16,24},{20,28},{24,16},{28,20},{1,9},{5... | collective-permute-start | bytes 172040 | tf_op jit(solution)/shard_map/ppermute | solution.py:346
  36.6 6.1 %collective-permute-start.9 = (f32[4,8,1792]{2,1,0:T(8,128)S(1)}, f32[4,8,1792]{2,1,0:T(8,128)S(1)}, u32[]{:S(2)}, u32[]{:S(2)}) collective-permute-start(f32[4,8,1792]{2,1,0:T(8,128)S(1)} %stack_z.2.mine), channel_id=1, source_target_pairs={{0,4},{4,0},{8,12},{12,8},{16,20},{20,16},{24,28},{28,24},{1,5},{5... | collective-permute-start | bytes 688136 | tf_op jit(solution)/shard_map/ppermute | solution.py:346
  42.7 5.3 %copy-start = (bf16[1,512,1536]{2,1,0:T(8,128)(2,1)S(1)}, bf16[1,512,1536]{2,1,0:T(8,128)(2,1)}, u32[]{:S(2)}) copy-start(bf16[1,512,1536]{2,1,0:T(8,128)(2,1)} %g.10) | copy-start | bytes 4718596
  42.7 5.3 %copy-start.1 = (bf16[1,512,1536]{2,1,0:T(8,128)(2,1)S(1)}, bf16[1,512,1536]{2,1,0:T(8,128)(2,1)}, u32[]{:S(2)}) copy-start(bf16[1,512,1536]{2,1,0:T(8,128)(2,1)} %e.10) | copy-start | bytes 4718596
  42.7 4.0 %collective-permute-start.10 = (f32[16,512]{1,0:T(8,128)S(1)}, f32[16,512]{1,0:T(8,128)S(1)}, u32[]{:S(2)}, u32[]{:S(2)}) collective-permute-start(f32[16,512]{1,0:T(8,128)S(1)} %shard_rows.1.refs_0_), channel_id=1, source_target_pairs={{0,2},{1,3},{2,0},{3,1},{4,6},{5,7},{6,4},{7,5},{8,10},{9,11},{10,... | collective-permute-start | bytes 98312 | tf_op jit(solution)/shard_map/ppermute | solution.py:346
  46.7 1.3 %collective-permute-start.11 = (f32[32,512]{1,0:T(8,128)S(1)}, f32[32,512]{1,0:T(8,128)S(1)}, u32[]{:S(2)}, u32[]{:S(2)}) collective-permute-start(f32[32,512]{1,0:T(8,128)S(1)} %stack_x.2.mine), channel_id=1, source_target_pairs={{0,1},{1,0},{2,3},{3,2},{4,5},{5,4},{6,7},{7,6},{8,9},{9,8},{10,11... | collective-permute-start | bytes 196616 | tf_op jit(solution)/shard_map/ppermute | solution.py:346
  49.3 7.0 %collective-permute-start.12 = (f32[4,8,1536]{2,1,0:T(8,128)S(1)}, f32[4,8,1536]{2,1,0:T(8,128)S(1)}, u32[]{:S(2)}, u32[]{:S(2)}) collective-permute-start(f32[4,8,1536]{2,1,0:T(8,128)S(1)} %get-tuple-element.53), channel_id=1, source_target_pairs={{0,4},{4,0},{8,12},{12,8},{16,20},{20,16},{24,28},{28,24},{1,5},{5... | collective-permute-start | bytes 589832 | tf_op jit(solution)/shard_map/ppermute | solution.py:346
  49.8 1.3 %collective-permute-start.13 = (f32[32,640]{1,0:T(8,128)S(1)}, f32[32,640]{1,0:T(8,128)S(1)}, u32[]{:S(2)}, u32[]{:S(2)}) collective-permute-start(f32[32,640]{1,0:T(8,128)S(1)} %get-tuple-element.55), channel_id=1, source_target_pairs={{0,1},{1,0},{2,3},{3,2},{4,5},{5,4},{6,7},{7,6},{8,9},{9,8},{10,11... | collective-permute-start | bytes 245768 | tf_op jit(solution)/shard_map/ppermute | solution.py:346
  51.1 4.2 %collective-permute-start.14 = (f32[16,768]{1,0:T(8,128)S(1)}, f32[16,768]{1,0:T(8,128)S(1)}, u32[]{:S(2)}, u32[]{:S(2)}) collective-permute-start(f32[16,768]{1,0:T(8,128)S(1)} %get-tuple-element.57), channel_id=1, source_target_pairs={{0,2},{1,3},{2,0},{3,1},{4,6},{5,7},{6,4},{7,5},{8,10},{9,11},{10,... | collective-permute-start | bytes 147464 | tf_op jit(solution)/shard_map/ppermute | solution.py:346
  56.4 4.4 %collective-permute-start.15 = (f32[8,1792]{1,0:T(8,128)S(1)}, f32[8,1792]{1,0:T(8,128)S(1)}, u32[]{:S(2)}, u32[]{:S(2)}) collective-permute-start(f32[8,1792]{1,0:T(8,128)S(1)} %get-tuple-element.61), channel_id=1, source_target_pairs={{0,8},{4,12},{8,0},{12,4},{16,24},{20,28},{24,16},{28,20},{1,9},{5... | collective-permute-start | bytes 172040 | tf_op jit(solution)/shard_map/ppermute | solution.py:346
  57.9 6.2 %collective-permute-start.16 = (f32[8,1792]{1,0:T(8,128)S(1)}, f32[8,1792]{1,0:T(8,128)S(1)}, u32[]{:S(2)}, u32[]{:S(2)}) collective-permute-start(f32[8,1792]{1,0:T(8,128)S(1)} %get-tuple-element.62), channel_id=1, source_target_pairs={{0,16},{4,20},{8,24},{12,28},{16,0},{20,4},{24,8},{28,12},{1,17},{... | collective-permute-start | bytes 172040 | tf_op jit(solution)/shard_map/ppermute | solution.py:346
  58.8 6.1 %collective-permute-start.17 = (f32[8,1792]{1,0:T(8,128)S(1)}, f32[8,1792]{1,0:T(8,128)S(1)}, u32[]{:S(2)}, u32[]{:S(2)}) collective-permute-start(f32[8,1792]{1,0:T(8,128)S(1)} %get-tuple-element.63), channel_id=1, source_target_pairs={{0,24},{4,28},{8,16},{12,20},{16,8},{20,12},{24,0},{28,4},{1,25},{... | collective-permute-start | bytes 172040 | tf_op jit(solution)/shard_map/ppermute | solution.py:346
  64.9 6.0 %collective-permute-start.20 = (f32[8,1792]{1,0:T(8,128)S(1)}, f32[8,1792]{1,0:T(8,128)S(1)}, u32[]{:S(2)}, u32[]{:S(2)}) collective-permute-start(f32[8,1792]{1,0:T(8,128)S(1)} %replica_mean.3.refs_0_), channel_id=1, source_target_pairs={{0,24},{4,28},{8,16},{12,20},{16,8},{20,12},{24,0},{28,4},{1,25},{... | collective-permute-start | bytes 172040 | tf_op jit(solution)/shard_map/ppermute | solution.py:346
  66.9 5.4 %collective-permute-start.19 = (f32[8,1792]{1,0:T(8,128)S(1)}, f32[8,1792]{1,0:T(8,128)S(1)}, u32[]{:S(2)}, u32[]{:S(2)}) collective-permute-start(f32[8,1792]{1,0:T(8,128)S(1)} %replica_mean.3.refs_0_), channel_id=1, source_target_pairs={{0,16},{4,20},{8,24},{12,28},{16,0},{20,4},{24,8},{28,12},{1,17},{... | collective-permute-start | bytes 172040 | tf_op jit(solution)/shard_map/ppermute | solution.py:346
  67.5 4.8 %collective-permute-start.18 = (f32[8,1792]{1,0:T(8,128)S(1)}, f32[8,1792]{1,0:T(8,128)S(1)}, u32[]{:S(2)}, u32[]{:S(2)}) collective-permute-start(f32[8,1792]{1,0:T(8,128)S(1)} %replica_mean.3.refs_0_), channel_id=1, source_target_pairs={{0,8},{4,12},{8,0},{12,4},{16,24},{20,28},{24,16},{28,20},{1,9},{5... | collective-permute-start | bytes 172040 | tf_op jit(solution)/shard_map/ppermute | solution.py:346
  72.3 6.1 %collective-permute-start.21 = (f32[4,8,1792]{2,1,0:T(8,128)S(1)}, f32[4,8,1792]{2,1,0:T(8,128)S(1)}, u32[]{:S(2)}, u32[]{:S(2)}) collective-permute-start(f32[4,8,1792]{2,1,0:T(8,128)S(1)} %stack_z.3.mine), channel_id=1, source_target_pairs={{0,4},{4,0},{8,12},{12,8},{16,20},{20,16},{24,28},{28,24},{1,5},{5... | collective-permute-start | bytes 688136 | tf_op jit(solution)/shard_map/ppermute | solution.py:346
  79.1 4.1 %collective-permute-start.22 = (f32[16,640]{1,0:T(8,128)S(1)}, f32[16,640]{1,0:T(8,128)S(1)}, u32[]{:S(2)}, u32[]{:S(2)}) collective-permute-start(f32[16,640]{1,0:T(8,128)S(1)} %get-tuple-element.67.refs_0_), channel_id=1, source_target_pairs={{0,2},{1,3},{2,0},{3,1},{4,6},{5,7},{6,4},{7,5},{8,10},{9,11},{10,... | collective-permute-start | bytes 122888 | tf_op jit(solution)/shard_map/ppermute | solution.py:346
  83.1 1.4 %copy-start.4 = (bf16[1,512,1536]{2,1,0:T(8,128)(2,1)S(1)}, bf16[1,512,1536]{2,1,0:T(8,128)(2,1)}, u32[]{:S(2)}) copy-start(bf16[1,512,1536]{2,1,0:T(8,128)(2,1)} %error_up.1._) | copy-start | bytes 4718596
  84.6 1.3 %collective-permute-start.23 = (f32[32,640]{1,0:T(8,128)S(1)}, f32[32,640]{1,0:T(8,128)S(1)}, u32[]{:S(2)}, u32[]{:S(2)}) collective-permute-start(f32[32,640]{1,0:T(8,128)S(1)} %stack_x.3.mine), channel_id=1, source_target_pairs={{0,1},{1,0},{2,3},{3,2},{4,5},{5,4},{6,7},{7,6},{8,9},{9,8},{10,11... | collective-permute-start | bytes 245768 | tf_op jit(solution)/shard_map/ppermute | solution.py:346

commit v5 on v4

v5 whole, which is shorter than its diff:
```python
import functools

import jax
import jax.numpy as jnp
from jax import lax
from jax.experimental import pallas as pl
from jax.experimental.pallas import tpu as pltpu
from jax.sharding import PartitionSpec as P

F32 = jnp.float32
BF16 = jnp.bfloat16
HIGHEST = lax.Precision.HIGHEST
CLIP_RMS = 0.1
STEPS = 4
AHEAD = 5
MIB = 1024 * 1024
NT = ((1,), (1,))


def split3(x):
    first = x.astype(BF16)
    rest = x - first.astype(F32)
    second = rest.astype(BF16)
    return first, second, (rest - second.astype(F32)).astype(BF16)


def tree_sum(values):
    values = list(values)
    while len(values) > 1:
        values = [values[i] + values[i + 1] for i in range(0, len(values), 2)]
    return values[0]


def dot(a, b, dims=((1,), (0,)), precision=None):
    return lax.dot_general(a, b, (dims, ((), ())), precision=precision, preferred_element_type=F32)


def fold(x, rows):
    return jnp.concatenate([x[i : i + rows] for i in range(0, x.shape[0], rows)], axis=1)


def unfold(x, rows):
    count = rows // x.shape[0]
    width = x.shape[1] // count
    return jnp.concatenate([x[:, i * width : (i + 1) * width] for i in range(count)], axis=0)


def place(axis):
    index = lax.axis_index(axis)
    return lax.bitwise_and(index, 1), lax.shift_right_logical(index, 1)


def split_cores(total, extra, keep, send):
    core, _ = place("tensor")
    rows, width = keep.shape[0], total.shape[1]
    keep[:, :width] = total[pl.ds(pl.multiple_of(core * rows, rows), rows), :]
    send[:, :width] = total[pl.ds(pl.multiple_of((1 - core) * rows, rows), rows), :]
    if extra is not None:
        keep[:, width:] = extra
        send[:, width:] = extra


def split_replicas(total, stage, keep, send):
    parity, _ = place("dp")
    half, per, _ = keep.shape
    for c in range(2 * half):
        stage[c] = total[c * per : (c + 1) * per, :]
    for c in range(half):
        keep[c] = stage[2 * c + parity]
        send[c] = stage[2 * c + 1 - parity]


def join_replicas(mine, other, stage, total):
    parity, _ = place("dp")
    half, per, _ = mine.shape
    width = total.shape[1]
    for c in range(half):
        stage[2 * c + parity] = mine[c, :, :width]
        stage[2 * c + 1 - parity] = other[c, :, :width]
    for c in range(2 * half):
        total[c * per : (c + 1) * per, :] = stage[c]


def join_cores(mine, other, total):
    core, _ = place("tensor")
    rows, width = mine.shape[0], total.shape[1]
    total[pl.ds(pl.multiple_of(core * rows, rows), rows), :] = mine[:, :width]
    total[pl.ds(pl.multiple_of((1 - core) * rows, rows), rows), :] = other[:, :width]


def left_kernel(gu, eu, qu, gd, ed, qd, keep_up, send_up, keep_down, send_down, *scratch):
    up, down, stage, q_sems, sems = scratch[:5], scratch[5:10], *scratch[10:]
    stages, waiting = [], []
    for i, (source, part) in enumerate(((qu, up), (qd, down))):
        waiting.append(pltpu.make_async_copy(source, part[2], q_sems.at[i]))
        waiting[i].start()
    for g, e, part in ((gu, eu, up), (gd, ed, down)):
        block = g.shape[1] // STEPS
        for i in range(STEPS):
            rows = pl.ds(i * block, block)
            n = 2 * len(stages)
            copies = [
                pltpu.make_async_copy(src.at[0, rows, :], dst.at[rows, :], sems.at[n + j])
                for j, (src, dst) in enumerate(((g, part[0]), (e, part[1])))
            ]
            stages.append((part, slice(i * block, (i + 1) * block), copies))

    def fetch(n):
        if n < len(stages):
            for copy in stages[n][2]:
                copy.start()

    for n in range(AHEAD):
        fetch(n)
    for copy, (_, _, q, pieces, _) in zip(waiting, (up, down)):
        copy.wait()
        parts = split3(q[...])
        pieces[...] = jnp.concatenate(parts + (jnp.zeros_like(parts[0]),), axis=0).T
    for n, ((g, e, q, pieces, total), rows, copies) in enumerate(stages):
        rank = q.shape[0]
        for copy in copies:
            copy.wait()
        fetch(n + AHEAD)
        t = dot(g[rows, :], pieces[...]) + dot(e[rows, :], pieces[...])
        t = (t[:, : 2 * rank] + t[:, 2 * rank :]).T
        total[:, rows] = t[:rank] + t[rank:]
    split_cores(up[4], None, keep_up, send_up)
    split_replicas(down[4], stage, keep_down, send_down)


def split_x_kernel(width, keep, got, *outs):
    _, x = place("tensor")
    total = outs[-1]
    outs = outs[:-1]
    rows = outs[0].shape[0]
    total[...] = keep[...] + got[...]
    for j, out in enumerate(outs):
        owner = lax.bitwise_xor(x, j)
        out[:, :width] = total[pl.ds(pl.multiple_of(owner * rows, rows), rows), :width]
        if total.shape[1] > width:
            out[:, width:] = fold(total[:, width:], rows)


def sum_kernel(scale, *refs):
    refs[-1][...] = tree_sum(ref[...] for ref in refs[:-1]) * scale


def sum_gram_kernel(*refs):
    *terms, out, gram = refs
    width = out.shape[1]
    total = tree_sum(term[...] for term in terms)
    out[...] = total[:, :width]
    gram[...] = unfold(unfold(total[:, width:], gram.shape[0] // 2), gram.shape[0])


def split_z_kernel(keep, got, *refs):
    *outs, stage = refs
    _, z = place("dp")
    stage[...] = keep[...] + got[...]
    for j, out in enumerate(outs):
        out[...] = stage[lax.bitwise_xor(z, j)]


def stack_z_kernel(*refs):
    _, z = place("dp")
    for j, ref in enumerate(refs[:-1]):
        refs[-1][lax.bitwise_xor(z, j)] = ref[...]


def stack_x_kernel(*refs):
    _, x = place("tensor")
    *pieces, out = refs
    rows = pieces[0].shape[0]
    for j, piece in enumerate(pieces):
        owner = lax.bitwise_xor(x, j)
        out[pl.ds(pl.multiple_of(owner * rows, rows), rows), :] = piece[...]


def split_rows(left, pieces):
    rank = left.shape[0]
    for i, piece in enumerate(split3(left[...])):
        pieces[i * rank : (i + 1) * rank, :] = piece


def add_pieces(t):
    rank = t.shape[0] // 3
    return t[:rank] + (t[rank : 2 * rank] + t[2 * rank :])


def right_down_kernel(mine, other, g, e, left, keep, send, pieces, total, stage):
    rank = left.shape[0]
    join_replicas(mine, other, stage, left)
    split_rows(left, pieces)
    total[...] = add_pieces(dot(pieces[...], g[0]) + dot(pieces[...], e[0]))
    gram = dot(left[...], left[...], NT, HIGHEST)
    split_cores(total, fold(gram, rank // 2), keep, send)


def right_up_kernel(mine, other, g, e, left, gram, keep, send, pieces, total, stage):
    join_cores(mine, other, left)
    split_rows(left, pieces)
    block = total.shape[1] // STEPS
    for i in range(STEPS):
        part = slice(i * block, (i + 1) * block)
        total[:, part] = add_pieces(dot(pieces[...], g[0, :, part]) + dot(pieces[...], e[0, :, part]))
    split_replicas(total, stage, keep, send)
    gram[...] = dot(left[...], left[...], NT, HIGHEST)


def inverse_factors(grams):
    rank = grams[0].shape[0]
    count = rank // 8
    panel = 4
    lane = lax.broadcasted_iota(jnp.int32, (8, 2 * rank), 1)
    row = lax.broadcasted_iota(jnp.int32, (8, 2 * rank), 0)
    states, pivots = [], []
    for gram in grams:
        wide = jnp.concatenate([gram, jnp.zeros_like(gram)], axis=1)
        states.append([wide[i : i + 8] + (lane == row + (rank + i)).astype(F32) for i in range(0, rank, 8)])
        pivots.append([])
    for start in range(0, rank, panel):
        at = start // 8
        below = range(at, count)
        spread = [
            [{i: jnp.broadcast_to(blocks[i][:, start + j : start + j + 1], (8, 2 * rank)) for i in below} for j in range(panel)]
            for blocks in states
        ]
        for j in range(panel):
            inner = (start + j) % 8
            for blocks, columns, found in zip(states, spread, pivots):
                pivot = columns[j][at][inner : inner + 1, :]
                found.append(pivot)
                inverse = 1.0 / pivot
                factor = {i: jnp.where(row > inner, columns[j][i], 0.0) if i == at else columns[j][i] for i in below}
                for later in columns[j + 1 :]:
                    head = later[at][inner : inner + 1, :] * inverse
                    for i in below:
                        later[i] = later[i] - factor[i] * head
                scaled = blocks[at][inner : inner + 1, :] * inverse
                for i in below:
                    blocks[i] = blocks[i] - factor[i] * scaled
    results = []
    for blocks, found in zip(states, pivots):
        rows = [block / jnp.sqrt(jnp.concatenate(found[8 * i : 8 * i + 8], axis=0)) for i, block in enumerate(blocks)]
        results.append(jnp.concatenate(rows, axis=0)[:, rank:])
    return results


def basis_kernel(left_up, left_down, gram_up, gram_down, inv_up, inv_down, lhs_up, lhs_down):
    inverses = inverse_factors([gram_up[...], gram_down[...]])
    rank = left_up.shape[0]
    for inverse, inv, left, lhs in zip(inverses, (inv_up, inv_down), (left_up, left_down), (lhs_up, lhs_down)):
        inv[...] = inverse
        first, second, _ = split3(dot(inverse, left[...], precision=HIGHEST).T)
        lhs[:, :rank] = first
        lhs[:, rank : 2 * rank] = first
        lhs[:, 2 * rank : 3 * rank] = second
        lhs[:, 3 * rank :] = second


def right_factor(inv, total, rhs):
    rank = inv.shape[0]
    right = dot(inv[...], total[...], precision=HIGHEST)
    first, second, _ = split3(right)
    rhs[:rank, :] = first
    rhs[rank : 2 * rank, :] = second
    rhs[2 * rank : 3 * rank, :] = first
    rhs[3 * rank :, :] = second
    return jnp.sum(right * right)


def factor_up_kernel(mine, other, inv, rhs, square, total, stage):
    join_replicas(mine, other, stage, total)
    square[...] = jnp.full(square.shape, right_factor(inv, total, rhs), F32)


def factor_down_kernel(mine, other, inv, rhs, square, total):
    join_cores(mine, other, total)
    square[...] = jnp.full(square.shape, right_factor(inv, total, rhs), F32)


def rows_of(block):
    return pl.ds(pl.multiple_of(pl.program_id(0) * block, block), block)


def error_kernel(g, e, lhs, rhs, error, made):
    made[...] = jnp.zeros_like(made)
    part = rows_of(error.shape[1])
    rebuilt = dot(lhs[part, :], rhs[...])
    error[0] = (g[0, part, :].astype(F32) + e[0, part, :].astype(F32) - rebuilt).astype(BF16)


def update_kernel(limit, lhs_up, rhs_up, lhs_down, rhs_down, square_down, *refs):
    *squares_up, update_up, update_down = refs
    norm_sq = tree_sum(square[...] for square in squares_up) + square_down[...]
    factor = jnp.minimum(jnp.float32(1.0), limit / jnp.sqrt(norm_sq))[:1, :1]
    for lhs, rhs, update in ((lhs_up, rhs_up, update_up), (lhs_down, rhs_down, update_down)):
        update[...] = (factor * dot(lhs[rows_of(update.shape[0]), :], rhs[...])).astype(BF16)


def shaped(*dims, dtype=F32):
    return jax.ShapeDtypeStruct(dims, dtype)


def whole(shape):
    return pl.BlockSpec(shape, lambda *_: (0,) * len(shape))


def row_blocks(rows, columns):
    return pl.BlockSpec((rows // STEPS, columns), lambda i: (i, 0))


def replica_blocks(rows, columns):
    return pl.BlockSpec((1, rows // STEPS, columns), lambda i: (0, i, 0))


VMEM = pl.BlockSpec(memory_space=pltpu.VMEM)


ANY = pl.BlockSpec(memory_space=pl.ANY)


def call(kernel, out_shape, *args, after=(), in_specs=None, limit=12, name=None, **more):
    skip = len(after)
    return pl.pallas_call(
        lambda *refs: kernel(*refs[skip:]), out_shape=out_shape, in_specs=[ANY] * skip + (in_specs or [VMEM] * len(args)),
        compiler_params=pltpu.CompilerParams(vmem_limit_bytes=limit * MIB),
        cost_estimate=pl.CostEstimate(flops=0, bytes_accessed=0, transcendentals=0), name=name, **more,
    )(*after, *args)


def swap(x, axis, distance):
    pairs = [(i, i ^ distance) for i in range(lax.axis_size(axis))]
    return lax.ppermute(x, axis, pairs)


def others(parts, axis):
    return [swap(part, axis, 2 * j) for j, part in enumerate(parts) if j]


def total_of(name, terms, scale=1.0, after=()):
    return call(functools.partial(sum_kernel, scale), shaped(*terms[0].shape), *terms, after=after, name=name)


def on_device(gu, eu, gd, ed, qu, qd):
    qu, qd = qu.T, qd.T
    n_dp, n_shards = lax.axis_size("dp"), lax.axis_size("tensor")
    _, rows, ff = gu.shape
    rank = qu.shape[0]
    half, per, n_x = n_dp // 2, rank // n_dp, n_shards // 2
    core_half = shaped(rank // 2, rows)
    shard = shaped(rank // n_shards, rows)
    replica_half = shaped(half, per, ff)
    chunk = shaped(per, ff)
    stage = pltpu.VMEM((n_dp, per, ff), F32)
    wide = pltpu.VMEM((rank, ff), F32)
    narrow = pltpu.VMEM((rank, rows), F32)

    def split_x(keep, got, out):
        return call(
            functools.partial(split_x_kernel, rows), [out] * n_x, keep, got, name="split_x",
            scratch_shapes=[pltpu.VMEM(keep.shape, F32)],
        )

    def split_z(keep, got, after):
        return call(
            split_z_kernel, [chunk] * half, keep, got, after=after, name="split_z",
            scratch_shapes=[pltpu.VMEM(replica_half.shape, F32)],
        )

    def stack_z(parts, after):
        return call(stack_z_kernel, replica_half, *parts, after=after, name="stack_z")

    def stack_x(parts, after):
        return call(stack_x_kernel, core_half, *parts, after=after, name="stack_x")

    buffers = [
        [pltpu.VMEM(g.shape[1:], BF16)] * 2 + [pltpu.VMEM(q.shape, F32), pltpu.VMEM((q.shape[1], 4 * rank), BF16), total]
        for g, q, total in ((gu, qu, narrow), (gd, qd, wide))
    ]
    keep_up, send_up, keep_down, send_down = call(
        left_kernel, [core_half] * 2 + [replica_half] * 2, gu, eu, qu, gd, ed, qd, name="left", limit=61,
        in_specs=[pl.BlockSpec(memory_space=pltpu.HBM)] * 6,
        scratch_shapes=buffers[0] + buffers[1] + [stage, pltpu.SemaphoreType.DMA((2,)), pltpu.SemaphoreType.DMA((4 * STEPS,))],
    )

    down_y = swap(send_down, "dp", 1)
    parts = split_x(keep_up, swap(send_up, "tensor", 1), shard)
    up = total_of("sum_x", [parts[0]] + others(parts, "tensor"))
    up = total_of("sum_y", [up, swap(up, "dp", 1)])
    up_z = others([up] * half, "dp")
    parts = split_z(keep_down, down_y, (up,))
    down_z = others(parts, "dp")
    up = total_of("sum_z", [up] + up_z, 1.0 / n_dp, after=(parts[0],))
    up_x = others([up] * n_x, "tensor")
    down = total_of("replica_mean", [parts[0]] + down_z, 1.0 / n_dp, after=(up,))
    down_z = others([down] * half, "dp")
    mine = stack_x([up] + up_x, (down,))
    left_up, gram_up, keep, send = call(
        right_up_kernel, [shaped(rank, rows), shaped(rank, rank), replica_half, replica_half],
        mine, swap(mine, "tensor", 1), gu, eu, name="right_up",
        scratch_shapes=[pltpu.VMEM((3 * rank, rows), BF16), wide, stage],
    )
    up_y = swap(send, "dp", 1)
    mine = stack_z([down] + down_z, (keep,))
    down_y = swap(mine, "dp", 1)

    up_parts = split_z(keep, up_y, (mine,))
    up_z = others(up_parts, "dp")
    core_wide = shaped(rank // 2, rows + 2 * rank)
    left_down, keep, send = call(
        right_down_kernel, [shaped(rank, ff), core_wide, core_wide], mine, down_y, gd, ed, after=(up_parts[0],),
        name="right_down", scratch_shapes=[pltpu.VMEM((3 * rank, ff), BF16), narrow, stage],
    )
    parts = split_x(keep, swap(send, "tensor", 1), shaped(rank // n_shards, rows + 2 * rank * n_x))
    down_x = others(parts, "tensor")
    up = total_of("replica_mean", [up_parts[0]] + up_z, 1.0 / n_dp, after=(parts[0],))
    up_z = others([up] * half, "dp")
    down, gram_down = call(sum_gram_kernel, [shard, shaped(rank, rank)], parts[0], *down_x, after=(up,), name="sum_x")
    down_y = swap(down, "dp", 1)
    inv_up, inv_down, lhs_up, lhs_down = call(
        basis_kernel,
        [shaped(rank, rank)] * 2 + [shaped(rows, 4 * rank, dtype=BF16), shaped(ff, 4 * rank, dtype=BF16)],
        left_up, left_down, gram_up, gram_down, name="basis",
    )
    down = total_of("sum_y", [down, down_y], after=(inv_up,))
    down_z = others([down] * half, "dp")
    mine = stack_z([up] + up_z, (down,))
    up_y = swap(mine, "dp", 1)
    down = total_of("sum_z", [down] + down_z, 1.0 / n_dp, after=(mine,))
    down_x = others([down] * n_x, "tensor")
    mine_down = stack_x([down] + down_x, ())
    rhs_down, square_down = call(
        factor_down_kernel, [shaped(4 * rank, rows, dtype=BF16), shaped(8, 128)],
        mine_down, swap(mine_down, "tensor", 1), inv_down, name="factor_down", scratch_shapes=[narrow],
    )

    def new_error(g, e, lhs, rhs, name):
        spec = replica_blocks(*g.shape[1:])
        outs = [shaped(*g.shape, dtype=BF16), shaped(8, 128)]
        return call(error_kernel, outs, g, e, lhs, rhs, name=name, grid=(STEPS,), out_specs=[spec, whole((8, 128))])

    new_error_down, made_down = new_error(gd, ed, lhs_down, rhs_down, "error_down")
    rhs_up, square_up = call(
        factor_up_kernel, [shaped(4 * rank, ff, dtype=BF16), shaped(8, 128)], mine, up_y, inv_up, after=(made_down,),
        name="factor_up", scratch_shapes=[wide, stage],
    )
    squares_up = [square_up] + [swap(square_up, "tensor", j) for j in range(1, n_shards)]
    new_error_up, made_up = new_error(gu, eu, lhs_up, rhs_up, "error_up")
    limit = CLIP_RMS * (2.0 * rows * ff * n_shards) ** 0.5
    update_up, update_down = call(
        functools.partial(update_kernel, limit), [shaped(rows, ff, dtype=BF16), shaped(ff, rows, dtype=BF16)],
        lhs_up, rhs_up, lhs_down, rhs_down, square_down, *squares_up, after=(made_up,),
        name="update", grid=(STEPS,), out_specs=[row_blocks(rows, ff), row_blocks(ff, rows)],
    )
    return new_error_up, update_up, new_error_down, update_down


def solution(mesh):
    placed = (
        P("dp", None, "tensor"),
        P("dp", None, "tensor"),
        P("dp", "tensor", None),
        P("dp", "tensor", None),
        P("tensor", None),
        P(),
    )
    return jax.shard_map(
        on_device,
        mesh=mesh,
        in_specs=placed,
        out_specs=(
            P("dp", None, "tensor"),
            P(None, "tensor"),
            P("dp", "tensor", None),
            P("tensor", None),
        ),
        check_vma=False,
    )
```

time: 89.5 us -> 98.6 us (1.10)
  starting transfers between devices: 29 us -> 41.7 us
  waiting for transfers between devices: 35.9 us -> 30 us
  Pallas kernels: 21.4 us -> 22.7 us
    ppermute x24 -> x35, starting transfers between devices: 29 us -> 41.7 us  [swap(): return lax.ppermute(x, axis, pairs)]
    ppermute x24 -> x35, waiting for transfers between devices: 35.9 us -> 30 us  [swap(): return lax.ppermute(x, axis, pairs)]
    pallas_call x20 -> x25, Pallas kernels: 21.4 us -> 22.7 us  [call(): pl.pallas_call(lambda *refs: kernel(*refs[skip:]), out_shape=out_shape, i...]
  transfers between devices with their start and end apart: 24 -> 35, of which waited for: 20 -> 16; matrix products, arithmetic and copies ran while one was open for 0% -> 0% of each run, Pallas kernels for 13% -> 10%
where the time goes in v5:
time: 98.6 us; the launch traced here: 98.4 us
  starting transfers between devices  41.7 us (42%)
  waiting for transfers between devices  30 us (30%)
  Pallas kernels  22.7 us (23%)
  local copies, waits for them, and re-layouts  3.2 us (3%)
    ppermute x35, starting transfers between devices, swap(): return lax.ppermute(x, axis, pairs)  41.7 us
    ppermute x35, waiting for transfers between devices, swap(): return lax.ppermute(x, axis, pairs)  30 us
    pallas_call x25, Pallas kernels, call(): pl.pallas_call(lambda *refs: kernel(*refs[skip:]), out_shape=out_shape, i...  22.7 us
    unnamed x14, local copies, waits for them, and re-layouts  3.2 us
  transfers between devices with their start and end apart: 35, of which 16 were waited for; matrix products, arithmetic and copies ran while one was open for 0% of the time, Pallas kernels for 10%

profile of v5, /device:TPU:0, one launch (start us, length us, event | category | flops | bytes accessed | tf_op | source)
XLA Modules:
  0.0 98.4 jit_solution(12348452917937860545)
XLA Ops:
  0.6 8.4 %left.1 = (f32[32,512]{1,0:T(8,128)}, f32[32,512]{1,0:T(8,128)}, f32[4,8,1536]{2,1,0:T(8,128)}, f32[4,8,1536]{2,1,0:T(8,128)}) custom-call(bf16[1,512,1536]{2,1,0:T(8,128)(2,1)} %refs_0_.5, bf16[1,512,1536]{2,1,0:T(8,128)(2,1)} %refs_1_.5, f32[64,1536]{1,0:T(8,128)} %bitcast.2, bf16[1,1536,512]{2,1,0:T(8,128)(2,1)} %refs_0_.4, ...), custom_call_target="tpu_custom_call" | custom-call | tf_op jit(solution)/shard_map/left/pallas_call | solution.py:325
  9.0 3.0 %collective-permute-start.3 = (f32[4,8,1536]{2,1,0:T(8,128)}, f32[4,8,1536]{2,1,0:T(8,128)S(1)}, u32[]{:S(2)}, u32[]{:S(2)}) collective-permute-start(f32[4,8,1536]{2,1,0:T(8,128)} %get-tuple-element.48), channel_id=1, source_target_pairs={{0,4},{4,0},{8,12},{12,8},{16,20},{20,16},{24,28},{28,24},{1,5},{5... | collective-permute-start | bytes 589832 | tf_op jit(solution)/shard_map/ppermute | solution.py:334
  12.1 0.0 collective-permute-start
  12.1 1.5 %collective-permute-done.refs_1_ = f32[32,512]{1,0:T(8,128)S(1)} collective-permute-done((f32[32,512]{1,0:T(8,128)}, f32[32,512]{1,0:T(8,128)S(1)}, u32[]{:S(2)}, u32[]{:S(2)}) %collective-permute-start) | collective-permute-done | bytes 65568 | tf_op jit(solution)/shard_map/ppermute | solution.py:334
  13.5 0.8 copy-done.6
  14.4 1.6 %collective-permute-start.1 = (f32[16,512]{1,0:T(8,128)S(1)}, f32[16,512]{1,0:T(8,128)S(1)}, u32[]{:S(2)}, u32[]{:S(2)}) collective-permute-start(f32[16,512]{1,0:T(8,128)S(1)} %get-tuple-element.46), channel_id=1, source_target_pairs={{0,2},{1,3},{2,0},{3,1},{4,6},{5,7},{6,4},{7,5},{8,10},{9,11},{10,... | collective-permute-start | bytes 98312 | tf_op jit(solution)/shard_map/ppermute | solution.py:334
  15.9 2.4 %collective-permute-done.1.refs_1_ = f32[16,512]{1,0:T(8,128)S(1)} collective-permute-done((f32[16,512]{1,0:T(8,128)S(1)}, f32[16,512]{1,0:T(8,128)S(1)}, u32[]{:S(2)}, u32[]{:S(2)}) %collective-permute-start.1) | collective-permute-done | bytes 32800 | tf_op jit(solution)/shard_map/ppermute | solution.py:334
  18.4 0.1 collective-permute-start.2
  18.4 3.8 %collective-permute-done.2.refs_1_ = f32[16,512]{1,0:T(8,128)S(1)} collective-permute-done((f32[16,512]{1,0:T(8,128)S(1)}, f32[16,512]{1,0:T(8,128)S(1)}, u32[]{:S(2)}, u32[]{:S(2)}) %collective-permute-start.2) | collective-permute-done | bytes 32800 | tf_op jit(solution)/shard_map/ppermute | solution.py:334
  22.3 3.6 %collective-permute-start.6 = (f32[16,512]{1,0:T(8,128)S(1)}, f32[16,512]{1,0:T(8,128)S(1)}, u32[]{:S(2)}, u32[]{:S(2)}) collective-permute-start(f32[16,512]{1,0:T(8,128)S(1)} %sum_y.2.refs_0_.refs_1_), channel_id=1, source_target_pairs={{0,24},{4,28},{8,16},{12,20},{16,8},{20,12},{24,0},{28,4},{1,25},{... | collective-permute-start | bytes 98312 | tf_op jit(solution)/shard_map/ppermute | solution.py:334
  25.9 0.0 collective-permute-start.5
  25.9 0.8 collective-permute-start.4
  26.7 0.9 copy-done.5
  27.7 1.3 %collective-permute-start.7 = (f32[8,1536]{1,0:T(8,128)S(1)}, f32[8,1536]{1,0:T(8,128)S(1)}, u32[]{:S(2)}, u32[]{:S(2)}) collective-permute-start(f32[8,1536]{1,0:T(8,128)S(1)} %get-tuple-element.50), channel_id=1, source_target_pairs={{0,8},{4,12},{8,0},{12,4},{16,24},{20,28},{24,16},{28,20},{1,9},{5... | collective-permute-start | bytes 147464 | tf_op jit(solution)/shard_map/ppermute | solution.py:334
  29.0 2.9 %collective-permute-start.8 = (f32[8,1536]{1,0:T(8,128)S(1)}, f32[8,1536]{1,0:T(8,128)S(1)}, u32[]{:S(2)}, u32[]{:S(2)}) collective-permute-start(f32[8,1536]{1,0:T(8,128)S(1)} %get-tuple-element.51), channel_id=1, source_target_pairs={{0,16},{4,20},{8,24},{12,28},{16,0},{20,4},{24,8},{28,12},{1,17},{... | collective-permute-start | bytes 147464 | tf_op jit(solution)/shard_map/ppermute | solution.py:334
  31.9 0.2 collective-permute-start.9
  32.1 1.6 %collective-permute-start.10 = (f32[16,512]{1,0:T(8,128)S(1)}, f32[16,512]{1,0:T(8,128)S(1)}, u32[]{:S(2)}, u32[]{:S(2)}) collective-permute-start(f32[16,512]{1,0:T(8,128)S(1)} %sum_z.2.refs_0_.refs_1_), channel_id=1, source_target_pairs={{0,2},{1,3},{2,0},{3,1},{4,6},{5,7},{6,4},{7,5},{8,10},{9,11},{10,... | collective-permute-start | bytes 98312 | tf_op jit(solution)/shard_map/ppermute | solution.py:334
  33.7 1.0 %collective-permute-done.8.refs_3_ = f32[8,1536]{1,0:T(8,128)S(1)} collective-permute-done((f32[8,1536]{1,0:T(8,128)S(1)}, f32[8,1536]{1,0:T(8,128)S(1)}, u32[]{:S(2)}, u32[]{:S(2)}) %collective-permute-start.8) | collective-permute-done | bytes 49184 | tf_op jit(solution)/shard_map/ppermute | solution.py:334
  34.7 3.1 %collective-permute-done.9.refs_4_ = f32[8,1536]{1,0:T(8,128)S(1)} collective-permute-done((f32[8,1536]{1,0:T(8,128)S(1)}, f32[8,1536]{1,0:T(8,128)S(1)}, u32[]{:S(2)}, u32[]{:S(2)}) %collective-permute-start.9) | collective-permute-done | bytes 49184 | tf_op jit(solution)/shard_map/ppermute | solution.py:334
  37.8 0.0 copy-start
  37.8 0.0 copy-start.1
  37.9 0.1 collective-permute-start.11
  37.9 2.0 %collective-permute-start.14 = (f32[8,1536]{1,0:T(8,128)S(1)}, f32[8,1536]{1,0:T(8,128)S(1)}, u32[]{:S(2)}, u32[]{:S(2)}) collective-permute-start(f32[8,1536]{1,0:T(8,128)S(1)} %replica_mean.2.refs_0_.refs_1_), channel_id=1, source_target_pairs={{0,24},{4,28},{8,16},{12,20},{16,8},{20,12},{24,0},{28,4},{1,25},{... | collective-permute-start | bytes 147464 | tf_op jit(solution)/shard_map/ppermute | solution.py:334
  39.9 2.5 %collective-permute-start.12 = (f32[8,1536]{1,0:T(8,128)S(1)}, f32[8,1536]{1,0:T(8,128)S(1)}, u32[]{:S(2)}, u32[]{:S(2)}) collective-permute-start(f32[8,1536]{1,0:T(8,128)S(1)} %replica_mean.2.refs_0_.refs_1_), channel_id=1, source_target_pairs={{0,8},{4,12},{8,0},{12,4},{16,24},{20,28},{24,16},{28,20},{1,9},{5... | collective-permute-start | bytes 147464 | tf_op jit(solution)/shard_map/ppermute | solution.py:334
  42.4 1.4 %copy-done.3 = bf16[1,512,1536]{2,1,0:T(8,128)(2,1)S(1)} copy-done((bf16[1,512,1536]{2,1,0:T(8,128)(2,1)S(1)}, bf16[1,512,1536]{2,1,0:T(8,128)(2,1)}, u32[]{:S(2)}) %copy-start.3) | copy-done | bytes 1572888
  43.8 1.2 %right_up.1 = (f32[64,512]{1,0:T(8,128)S(1)}, f32[64,64]{1,0:T(8,128)S(1)}, f32[4,8,1536]{2,1,0:T(8,128)S(1)}, f32[4,8,1536]{2,1,0:T(8,128)S(1)}) custom-call(f32[32,512]{1,0:T(8,128)S(1)} %stack_x.2.refs_0_, f32[32,512]{1,0:T(8,128)S(1)} %collective-permute-done.11.refs_1_, bf16[1,512,1536]{2,1,0:T(8,128)(2,1)S(1)} %copy-done.2, ...), custom_call_target="tpu_custom_call" | custom-call | tf_op jit(solution)/shard_map/right_up/pallas_call | solution.py:325
  45.0 0.6 collective-permute-start.15
  45.6 0.4 collective-permute-done.13.refs_3_
  46.0 1.2 %collective-permute-start.16 = (f32[4,8,1536]{2,1,0:T(8,128)S(1)}, f32[4,8,1536]{2,1,0:T(8,128)S(1)}, u32[]{:S(2)}, u32[]{:S(2)}) collective-permute-start(f32[4,8,1536]{2,1,0:T(8,128)S(1)} %stack_z.2.refs_0_.refs_1_), channel_id=1, source_target_pairs={{0,4},{4,0},{8,12},{12,8},{16,20},{20,16},{24,28},{28,24},{1,5},{5... | collective-permute-start | bytes 589832 | tf_op jit(solution)/shard_map/ppermute | solution.py:334
  47.2 5.7 %collective-permute-done.15.refs_2_ = f32[4,8,1536]{2,1,0:T(8,128)S(1)} collective-permute-done((f32[4,8,1536]{2,1,0:T(8,128)S(1)}, f32[4,8,1536]{2,1,0:T(8,128)S(1)}, u32[]{:S(2)}, u32[]{:S(2)}) %collective-permute-start.15) | collective-permute-done | bytes 196640 | tf_op jit(solution)/shard_map/ppermute | solution.py:334
  52.9 2.8 %collective-permute-done.16.refs_2_ = f32[4,8,1536]{2,1,0:T(8,128)S(1)} collective-permute-done((f32[4,8,1536]{2,1,0:T(8,128)S(1)}, f32[4,8,1536]{2,1,0:T(8,128)S(1)}, u32[]{:S(2)}, u32[]{:S(2)}) %collective-permute-start.16) | collective-permute-done | bytes 196640 | tf_op jit(solution)/shard_map/ppermute | solution.py:334
  55.7 1.2 %right_down.1 = (f32[64,1536]{1,0:T(8,128)S(1)}, f32[32,640]{1,0:T(8,128)S(1)}, f32[32,640]{1,0:T(8,128)S(1)}) custom-call(f32[8,1536]{1,0:T(8,128)S(1)} %get-tuple-element.56.refs_0_.refs_1_, f32[4,8,1536]{2,1,0:T(8,128)S(1)} %stack_z.2.refs_0_.refs_1_, f32[4,8,1536]{2,1,0:T(8,128)S(1)} %collective-permute-done.16.refs_2_, ...), custom_call_target="tpu_custom_call" | custom-call | tf_op jit(solution)/shard_map/right_down/pallas_call | solution.py:325
  56.9 0.0 collective-permute-start.17
  56.9 0.4 collective-permute-start.18
  57.3 2.2 %collective-permute-start.19 = (f32[8,1536]{1,0:T(8,128)S(1)}, f32[8,1536]{1,0:T(8,128)S(1)}, u32[]{:S(2)}, u32[]{:S(2)}) collective-permute-start(f32[8,1536]{1,0:T(8,128)S(1)} %get-tuple-element.63), channel_id=1, source_target_pairs={{0,16},{4,20},{8,24},{12,28},{16,0},{20,4},{24,8},{28,12},{1,17},{... | collective-permute-start | bytes 147464 | tf_op jit(solution)/shard_map/ppermute | solution.py:334
  59.5 1.9 %collective-permute-start.20 = (f32[8,1536]{1,0:T(8,128)S(1)}, f32[8,1536]{1,0:T(8,128)S(1)}, u32[]{:S(2)}, u32[]{:S(2)}) collective-permute-start(f32[8,1536]{1,0:T(8,128)S(1)} %get-tuple-element.64), channel_id=1, source_target_pairs={{0,24},{4,28},{8,16},{12,20},{16,8},{20,12},{24,0},{28,4},{1,25},{... | collective-permute-start | bytes 147464 | tf_op jit(solution)/shard_map/ppermute | solution.py:334
  61.4 1.6 %collective-permute-start.21 = (f32[16,768]{1,0:T(8,128)S(1)}, f32[16,768]{1,0:T(8,128)S(1)}, u32[]{:S(2)}, u32[]{:S(2)}) collective-permute-start(f32[16,768]{1,0:T(8,128)S(1)} %get-tuple-element.65), channel_id=1, source_target_pairs={{0,2},{1,3},{2,0},{3,1},{4,6},{5,7},{6,4},{7,5},{8,10},{9,11},{10,... | collective-permute-start | bytes 147464 | tf_op jit(solution)/shard_map/ppermute | solution.py:334
  63.0 1.3 %collective-permute-done.19.refs_3_ = f32[8,1536]{1,0:T(8,128)S(1)} collective-permute-done((f32[8,1536]{1,0:T(8,128)S(1)}, f32[8,1536]{1,0:T(8,128)S(1)}, u32[]{:S(2)}, u32[]{:S(2)}) %collective-permute-start.19) | collective-permute-done | bytes 49184 | tf_op jit(solution)/shard_map/ppermute | solution.py:334
  64.3 1.1 %collective-permute-done.20.refs_4_ = f32[8,1536]{1,0:T(8,128)S(1)} collective-permute-done((f32[8,1536]{1,0:T(8,128)S(1)}, f32[8,1536]{1,0:T(8,128)S(1)}, u32[]{:S(2)}, u32[]{:S(2)}) %collective-permute-start.20) | collective-permute-done | bytes 49184 | tf_op jit(solution)/shard_map/ppermute | solution.py:334
  65.4 2.0 %collective-permute-start.25 = (f32[8,1536]{1,0:T(8,128)S(1)}, f32[8,1536]{1,0:T(8,128)S(1)}, u32[]{:S(2)}, u32[]{:S(2)}) collective-permute-start(f32[8,1536]{1,0:T(8,128)S(1)} %replica_mean.3.refs_0_.refs_1_), channel_id=1, source_target_pairs={{0,24},{4,28},{8,16},{12,20},{16,8},{20,12},{24,0},{28,4},{1,25},{... | collective-permute-start | bytes 147464 | tf_op jit(solution)/shard_map/ppermute | solution.py:334
  67.4 2.5 %collective-permute-start.23 = (f32[8,1536]{1,0:T(8,128)S(1)}, f32[8,1536]{1,0:T(8,128)S(1)}, u32[]{:S(2)}, u32[]{:S(2)}) collective-permute-start(f32[8,1536]{1,0:T(8,128)S(1)} %replica_mean.3.refs_0_.refs_1_), channel_id=1, source_target_pairs={{0,8},{4,12},{8,0},{12,4},{16,24},{20,28},{24,16},{28,20},{1,9},{5... | collective-permute-start | bytes 147464 | tf_op jit(solution)/shard_map/ppermute | solution.py:334
  69.8 0.1 sum_x.3
  69.9 0.5 collective-permute-start.22
  70.4 3.2 %basis.1 = (f32[64,64]{1,0:T(8,128)S(1)}, f32[64,64]{1,0:T(8,128)S(1)}, bf16[512,256]{1,0:T(8,128)(2,1)S(1)}, bf16[1536,256]{1,0:T(8,128)(2,1)S(1)}) custom-call(f32[64,512]{1,0:T(8,128)S(1)} %get-tuple-element.53.refs_0_, f32[64,1536]{1,0:T(8,128)S(1)} %get-tuple-element.57.refs_1_, f32[64,64]{1,0:T(8,128)S(1)} %get-tuple-element.58.refs_2_, ...), custom_call_target="tpu_custom_call" | custom-call | tf_op jit(solution)/shard_map/basis/pallas_call | solution.py:325
  73.6 0.2 collective-permute-done.22.refs_2_
  73.9 1.4 %collective-permute-start.31 = (f32[4,8,1536]{2,1,0:T(8,128)S(1)}, f32[4,8,1536]{2,1,0:T(8,128)S(1)}, u32[]{:S(2)}, u32[]{:S(2)}) collective-permute-start(f32[4,8,1536]{2,1,0:T(8,128)S(1)} %stack_z.3.refs_0_.refs_1_), channel_id=1, source_target_pairs={{0,4},{4,0},{8,12},{12,8},{16,20},{20,16},{24,28},{28,24},{1,5},{5... | collective-permute-start | bytes 589832 | tf_op jit(solution)/shard_map/ppermute | solution.py:334
  75.3 1.9 %collective-permute-start.28 = (f32[16,512]{1,0:T(8,128)S(1)}, f32[16,512]{1,0:T(8,128)S(1)}, u32[]{:S(2)}, u32[]{:S(2)}) collective-permute-start(f32[16,512]{1,0:T(8,128)S(1)} %sum_y.3.refs_0_.refs_1_), channel_id=1, source_target_pairs={{0,24},{4,28},{8,16},{12,20},{16,8},{20,12},{24,0},{28,4},{1,25},{... | collective-permute-start | bytes 98312 | tf_op jit(solution)/shard_map/ppermute | solution.py:334
  77.2 2.5 %collective-permute-start.26 = (f32[16,512]{1,0:T(8,128)S(1)}, f32[16,512]{1,0:T(8,128)S(1)}, u32[]{:S(2)}, u32[]{:S(2)}) collective-permute-start(f32[16,512]{1,0:T(8,128)S(1)} %sum_y.3.refs_0_.refs_1_), channel_id=1, source_target_pairs={{0,8},{4,12},{8,0},{12,4},{16,24},{20,28},{24,16},{28,20},{1,9},{5... | collective-permute-start | bytes 98312 | tf_op jit(solution)/shard_map/ppermute | solution.py:334
  79.7 1.3 %collective-permute-done.28.refs_4_ = f32[16,512]{1,0:T(8,128)S(1)} collective-permute-done((f32[16,512]{1,0:T(8,128)S(1)}, f32[16,512]{1,0:T(8,128)S(1)}, u32[]{:S(2)}, u32[]{:S(2)}) %collective-permute-start.28) | collective-permute-done | bytes 32800 | tf_op jit(solution)/shard_map/ppermute | solution.py:334
  81.0 1.0 %collective-permute-done.27.refs_3_ = f32[16,512]{1,0:T(8,128)S(1)} collective-permute-done((f32[16,512]{1,0:T(8,128)S(1)}, f32[16,512]{1,0:T(8,128)S(1)}, u32[]{:S(2)}, u32[]{:S(2)}) %collective-permute-start.27) | collective-permute-done | bytes 32800 | tf_op jit(solution)/shard_map/ppermute | solution.py:334
  82.0 1.5 %collective-permute-start.29 = (f32[16,512]{1,0:T(8,128)S(1)}, f32[16,512]{1,0:T(8,128)S(1)}, u32[]{:S(2)}, u32[]{:S(2)}) collective-permute-start(f32[16,512]{1,0:T(8,128)S(1)} %sum_z.3.refs_0_), channel_id=1, source_target_pairs={{0,2},{1,3},{2,0},{3,1},{4,6},{5,7},{6,4},{7,5},{8,10},{9,11},{10,... | collective-permute-start | bytes 98312 | tf_op jit(solution)/shard_map/ppermute | solution.py:334
  83.6 2.4 %collective-permute-done.29.refs_1_ = f32[16,512]{1,0:T(8,128)S(1)} collective-permute-done((f32[16,512]{1,0:T(8,128)S(1)}, f32[16,512]{1,0:T(8,128)S(1)}, u32[]{:S(2)}, u32[]{:S(2)}) %collective-permute-start.29) | collective-permute-done | bytes 32800 | tf_op jit(solution)/shard_map/ppermute | solution.py:334
  86.0 0.1 collective-permute-start.30
  86.1 1.2 %collective-permute-done.30.refs_1_ = f32[32,512]{1,0:T(8,128)S(1)} collective-permute-done((f32[32,512]{1,0:T(8,128)S(1)}, f32[32,512]{1,0:T(8,128)S(1)}, u32[]{:S(2)}, u32[]{:S(2)}) %collective-permute-start.30) | collective-permute-done | bytes 65568 | tf_op jit(solution)/shard_map/ppermute | solution.py:334
  87.3 0.4 factor_down.1
  87.8 0.0 copy-start.4
  87.8 2.3 %error_down.1 = (bf16[1,1536,512]{2,1,0:T(8,128)(2,1)}, f32[8,128]{1,0:T(8,128)S(1)}) custom-call(bf16[1,1536,512]{2,1,0:T(8,128)(2,1)S(1)} %copy-done, bf16[1,1536,512]{2,1,0:T(8,128)(2,1)S(1)} %copy-done.1, bf16[1536,256]{1,0:T(8,128)(2,1)S(1)} %get-tuple-element.68.refs_2_.refs_3_, bf16[256,512]{1,0:T(8,128)(2,1)S(1)} %get-tuple-element.72.refs_3_.refs_4_), custom_call_target="tpu_custom_call" | custom-call | tf_op jit(solution)/shard_map/error_down/pallas_call | solution.py:325
  90.1 0.7 factor_up.1
  90.8 1.3 %collective-permute-start.34 = (f32[8,128]{1,0:T(8,128)S(1)}, f32[8,128]{1,0:T(8,128)S(1)}, u32[]{:S(2)}, u32[]{:S(2)}) collective-permute-start(f32[8,128]{1,0:T(8,128)S(1)} %get-tuple-element.78.refs_6_), channel_id=1, source_target_pairs={{0,3},{1,2},{2,1},{3,0},{4,7},{5,6},{6,5},{7,4},{8,11},{9,10},{10,... | collective-permute-start | bytes 12296 | tf_op jit(solution)/shard_map/ppermute | solution.py:334
  92.1 0.6 collective-permute-start.33
  92.6 0.1 collective-permute-start.32
  92.7 2.3 %error_up.1 = (bf16[1,512,1536]{2,1,0:T(8,128)(2,1)}, f32[8,128]{1,0:T(8,128)S(1)}) custom-call(bf16[1,512,1536]{2,1,0:T(8,128)(2,1)S(1)} %copy-done.2, bf16[1,512,1536]{2,1,0:T(8,128)(2,1)S(1)} %copy-done.4, bf16[512,256]{1,0:T(8,128)(2,1)S(1)} %get-tuple-element.67.refs_2_.refs_1_, bf16[256,1536]{1,0:T(8,128)(2,1)S(1)} %get-tuple-element.74.refs_3_.refs_2_), custom_call_target="tpu_custom_call" | custom-call | tf_op jit(solution)/shard_map/error_up/pallas_call | solution.py:325
  95.1 0.6 collective-permute-done.33.refs_8_
  95.7 2.7 %update.1 = (bf16[512,1536]{1,0:T(8,128)(2,1)}, bf16[1536,512]{1,0:T(8,128)(2,1)}) custom-call(f32[8,128]{1,0:T(8,128)S(1)} %get-tuple-element.76.refs_0_, bf16[512,256]{1,0:T(8,128)(2,1)S(1)} %get-tuple-element.67.refs_2_.refs_1_, bf16[256,1536]{1,0:T(8,128)(2,1)S(1)} %get-tuple-element.74.refs_3_.refs_2_, ...), custom_call_target="tpu_custom_call" | custom-call | tf_op jit(solution)/shard_map/update/pallas_call | solution.py:325
  (45 shorter events, 0.3 us)
Async XLA Ops:
  0.6 41.8 %copy-start.2 = (bf16[1,512,1536]{2,1,0:T(8,128)(2,1)S(1)}, bf16[1,512,1536]{2,1,0:T(8,128)(2,1)}, u32[]{:S(2)}) copy-start(bf16[1,512,1536]{2,1,0:T(8,128)(2,1)} %refs_0_.5) | copy-start | bytes 4718596
  9.0 17.7 %collective-permute-start.3 = (f32[4,8,1536]{2,1,0:T(8,128)}, f32[4,8,1536]{2,1,0:T(8,128)S(1)}, u32[]{:S(2)}, u32[]{:S(2)}) collective-permute-start(f32[4,8,1536]{2,1,0:T(8,128)} %get-tuple-element.48), channel_id=1, source_target_pairs={{0,4},{4,0},{8,12},{12,8},{16,20},{20,16},{24,28},{28,24},{1,5},{5... | collective-permute-start | bytes 589832 | tf_op jit(solution)/shard_map/ppermute | solution.py:334
  12.1 1.5 %collective-permute-start = (f32[32,512]{1,0:T(8,128)}, f32[32,512]{1,0:T(8,128)S(1)}, u32[]{:S(2)}, u32[]{:S(2)}) collective-permute-start(f32[32,512]{1,0:T(8,128)} %get-tuple-element.44), channel_id=1, source_target_pairs={{0,1},{1,0},{2,3},{3,2},{4,5},{5,4},{6,7},{7,6},{8,9},{9,8},{10,11... | collective-permute-start | bytes 196616 | tf_op jit(solution)/shard_map/ppermute | solution.py:334
  13.5 0.8 copy-start.6
  14.4 4.0 %collective-permute-start.1 = (f32[16,512]{1,0:T(8,128)S(1)}, f32[16,512]{1,0:T(8,128)S(1)}, u32[]{:S(2)}, u32[]{:S(2)}) collective-permute-start(f32[16,512]{1,0:T(8,128)S(1)} %get-tuple-element.46), channel_id=1, source_target_pairs={{0,2},{1,3},{2,0},{3,1},{4,6},{5,7},{6,4},{7,5},{8,10},{9,11},{10,... | collective-permute-start | bytes 98312 | tf_op jit(solution)/shard_map/ppermute | solution.py:334
  18.4 3.9 %collective-permute-start.2 = (f32[16,512]{1,0:T(8,128)S(1)}, f32[16,512]{1,0:T(8,128)S(1)}, u32[]{:S(2)}, u32[]{:S(2)}) collective-permute-start(f32[16,512]{1,0:T(8,128)S(1)} %sum_x.2.refs_0_), channel_id=1, source_target_pairs={{0,4},{4,0},{8,12},{12,8},{16,20},{20,16},{24,28},{28,24},{1,5},{5... | collective-permute-start | bytes 98312 | tf_op jit(solution)/shard_map/ppermute | solution.py:334
  22.3 9.6 %collective-permute-start.6 = (f32[16,512]{1,0:T(8,128)S(1)}, f32[16,512]{1,0:T(8,128)S(1)}, u32[]{:S(2)}, u32[]{:S(2)}) collective-permute-start(f32[16,512]{1,0:T(8,128)S(1)} %sum_y.2.refs_0_.refs_1_), channel_id=1, source_target_pairs={{0,24},{4,28},{8,16},{12,20},{16,8},{20,12},{24,0},{28,4},{1,25},{... | collective-permute-start | bytes 98312 | tf_op jit(solution)/shard_map/ppermute | solution.py:334
  25.9 6.2 %collective-permute-start.5 = (f32[16,512]{1,0:T(8,128)S(1)}, f32[16,512]{1,0:T(8,128)S(1)}, u32[]{:S(2)}, u32[]{:S(2)}) collective-permute-start(f32[16,512]{1,0:T(8,128)S(1)} %sum_y.2.refs_0_.refs_1_), channel_id=1, source_target_pairs={{0,16},{4,20},{8,24},{12,28},{16,0},{20,4},{24,8},{28,12},{1,17},{... | collective-permute-start | bytes 98312 | tf_op jit(solution)/shard_map/ppermute | solution.py:334
  25.9 6.2 %collective-permute-start.4 = (f32[16,512]{1,0:T(8,128)S(1)}, f32[16,512]{1,0:T(8,128)S(1)}, u32[]{:S(2)}, u32[]{:S(2)}) collective-permute-start(f32[16,512]{1,0:T(8,128)S(1)} %sum_y.2.refs_0_.refs_1_), channel_id=1, source_target_pairs={{0,8},{4,12},{8,0},{12,4},{16,24},{20,28},{24,16},{28,20},{1,9},{5... | collective-permute-start | bytes 98312 | tf_op jit(solution)/shard_map/ppermute | solution.py:334
  26.7 0.9 copy-start.5
  27.7 6.0 %collective-permute-start.7 = (f32[8,1536]{1,0:T(8,128)S(1)}, f32[8,1536]{1,0:T(8,128)S(1)}, u32[]{:S(2)}, u32[]{:S(2)}) collective-permute-start(f32[8,1536]{1,0:T(8,128)S(1)} %get-tuple-element.50), channel_id=1, source_target_pairs={{0,8},{4,12},{8,0},{12,4},{16,24},{20,28},{24,16},{28,20},{1,9},{5... | collective-permute-start | bytes 147464 | tf_op jit(solution)/shard_map/ppermute | solution.py:334
  29.0 5.8 %collective-permute-start.8 = (f32[8,1536]{1,0:T(8,128)S(1)}, f32[8,1536]{1,0:T(8,128)S(1)}, u32[]{:S(2)}, u32[]{:S(2)}) collective-permute-start(f32[8,1536]{1,0:T(8,128)S(1)} %get-tuple-element.51), channel_id=1, source_target_pairs={{0,16},{4,20},{8,24},{12,28},{16,0},{20,4},{24,8},{28,12},{1,17},{... | collective-permute-start | bytes 147464 | tf_op jit(solution)/shard_map/ppermute | solution.py:334
  31.9 5.9 %collective-permute-start.9 = (f32[8,1536]{1,0:T(8,128)S(1)}, f32[8,1536]{1,0:T(8,128)S(1)}, u32[]{:S(2)}, u32[]{:S(2)}) collective-permute-start(f32[8,1536]{1,0:T(8,128)S(1)} %get-tuple-element.52), channel_id=1, source_target_pairs={{0,24},{4,28},{8,16},{12,20},{16,8},{20,12},{24,0},{28,4},{1,25},{... | collective-permute-start | bytes 147464 | tf_op jit(solution)/shard_map/ppermute | solution.py:334
  32.1 5.7 %collective-permute-start.10 = (f32[16,512]{1,0:T(8,128)S(1)}, f32[16,512]{1,0:T(8,128)S(1)}, u32[]{:S(2)}, u32[]{:S(2)}) collective-permute-start(f32[16,512]{1,0:T(8,128)S(1)} %sum_z.2.refs_0_.refs_1_), channel_id=1, source_target_pairs={{0,2},{1,3},{2,0},{3,1},{4,6},{5,7},{6,4},{7,5},{8,10},{9,11},{10,... | collective-permute-start | bytes 98312 | tf_op jit(solution)/shard_map/ppermute | solution.py:334
  37.8 17.8 %copy-start = (bf16[1,1536,512]{2,1,0:T(8,128)(2,1)S(1)}, bf16[1,1536,512]{2,1,0:T(8,128)(2,1)}, u32[]{:S(2)}) copy-start(bf16[1,1536,512]{2,1,0:T(8,128)(2,1)} %refs_0_.4) | copy-start | bytes 4718596
  37.8 17.8 %copy-start.1 = (bf16[1,1536,512]{2,1,0:T(8,128)(2,1)S(1)}, bf16[1,1536,512]{2,1,0:T(8,128)(2,1)}, u32[]{:S(2)}) copy-start(bf16[1,1536,512]{2,1,0:T(8,128)(2,1)} %refs_1_.4) | copy-start | bytes 4718596
  37.9 4.5 %collective-permute-start.11 = (f32[32,512]{1,0:T(8,128)S(1)}, f32[32,512]{1,0:T(8,128)S(1)}, u32[]{:S(2)}, u32[]{:S(2)}) collective-permute-start(f32[32,512]{1,0:T(8,128)S(1)} %stack_x.2.refs_0_), channel_id=1, source_target_pairs={{0,1},{1,0},{2,3},{3,2},{4,5},{5,4},{6,7},{7,6},{8,9},{9,8},{10,11... | collective-permute-start | bytes 196616 | tf_op jit(solution)/shard_map/ppermute | solution.py:334
  37.9 7.6 %collective-permute-start.14 = (f32[8,1536]{1,0:T(8,128)S(1)}, f32[8,1536]{1,0:T(8,128)S(1)}, u32[]{:S(2)}, u32[]{:S(2)}) collective-permute-start(f32[8,1536]{1,0:T(8,128)S(1)} %replica_mean.2.refs_0_.refs_1_), channel_id=1, source_target_pairs={{0,24},{4,28},{8,16},{12,20},{16,8},{20,12},{24,0},{28,4},{1,25},{... | collective-permute-start | bytes 147464 | tf_op jit(solution)/shard_map/ppermute | solution.py:334
  39.9 6.1 %collective-permute-start.13 = (f32[8,1536]{1,0:T(8,128)S(1)}, f32[8,1536]{1,0:T(8,128)S(1)}, u32[]{:S(2)}, u32[]{:S(2)}) collective-permute-start(f32[8,1536]{1,0:T(8,128)S(1)} %replica_mean.2.refs_0_.refs_1_), channel_id=1, source_target_pairs={{0,16},{4,20},{8,24},{12,28},{16,0},{20,4},{24,8},{28,12},{1,17},{... | collective-permute-start | bytes 147464 | tf_op jit(solution)/shard_map/ppermute | solution.py:334
  39.9 6.1 %collective-permute-start.12 = (f32[8,1536]{1,0:T(8,128)S(1)}, f32[8,1536]{1,0:T(8,128)S(1)}, u32[]{:S(2)}, u32[]{:S(2)}) collective-permute-start(f32[8,1536]{1,0:T(8,128)S(1)} %replica_mean.2.refs_0_.refs_1_), channel_id=1, source_target_pairs={{0,8},{4,12},{8,0},{12,4},{16,24},{20,28},{24,16},{28,20},{1,9},{5... | collective-permute-start | bytes 147464 | tf_op jit(solution)/shard_map/ppermute | solution.py:334
  42.4 1.4 %copy-start.3 = (bf16[1,512,1536]{2,1,0:T(8,128)(2,1)S(1)}, bf16[1,512,1536]{2,1,0:T(8,128)(2,1)}, u32[]{:S(2)}) copy-start(bf16[1,512,1536]{2,1,0:T(8,128)(2,1)} %refs_1_.5) | copy-start | bytes 4718596
  45.0 7.9 %collective-permute-start.15 = (f32[4,8,1536]{2,1,0:T(8,128)S(1)}, f32[4,8,1536]{2,1,0:T(8,128)S(1)}, u32[]{:S(2)}, u32[]{:S(2)}) collective-permute-start(f32[4,8,1536]{2,1,0:T(8,128)S(1)} %get-tuple-element.55), channel_id=1, source_target_pairs={{0,4},{4,0},{8,12},{12,8},{16,20},{20,16},{24,28},{28,24},{1,5},{5... | collective-permute-start | bytes 589832 | tf_op jit(solution)/shard_map/ppermute | solution.py:334
  46.0 9.6 %collective-permute-start.16 = (f32[4,8,1536]{2,1,0:T(8,128)S(1)}, f32[4,8,1536]{2,1,0:T(8,128)S(1)}, u32[]{:S(2)}, u32[]{:S(2)}) collective-permute-start(f32[4,8,1536]{2,1,0:T(8,128)S(1)} %stack_z.2.refs_0_.refs_1_), channel_id=1, source_target_pairs={{0,4},{4,0},{8,12},{12,8},{16,20},{20,16},{24,28},{28,24},{1,5},{5... | collective-permute-start | bytes 589832 | tf_op jit(solution)/shard_map/ppermute | solution.py:334
  56.9 4.5 %collective-permute-start.17 = (f32[32,640]{1,0:T(8,128)S(1)}, f32[32,640]{1,0:T(8,128)S(1)}, u32[]{:S(2)}, u32[]{:S(2)}) collective-permute-start(f32[32,640]{1,0:T(8,128)S(1)} %get-tuple-element.60), channel_id=1, source_target_pairs={{0,1},{1,0},{2,3},{3,2},{4,5},{5,4},{6,7},{7,6},{8,9},{9,8},{10,11... | collective-permute-start | bytes 245768 | tf_op jit(solution)/shard_map/ppermute | solution.py:334
  56.9 6.0 %collective-permute-start.18 = (f32[8,1536]{1,0:T(8,128)S(1)}, f32[8,1536]{1,0:T(8,128)S(1)}, u32[]{:S(2)}, u32[]{:S(2)}) collective-permute-start(f32[8,1536]{1,0:T(8,128)S(1)} %get-tuple-element.62), channel_id=1, source_target_pairs={{0,8},{4,12},{8,0},{12,4},{16,24},{20,28},{24,16},{28,20},{1,9},{5... | collective-permute-start | bytes 147464 | tf_op jit(solution)/shard_map/ppermute | solution.py:334
  57.3 7.0 %collective-permute-start.19 = (f32[8,1536]{1,0:T(8,128)S(1)}, f32[8,1536]{1,0:T(8,128)S(1)}, u32[]{:S(2)}, u32[]{:S(2)}) collective-permute-start(f32[8,1536]{1,0:T(8,128)S(1)} %get-tuple-element.63), channel_id=1, source_target_pairs={{0,16},{4,20},{8,24},{12,28},{16,0},{20,4},{24,8},{28,12},{1,17},{... | collective-permute-start | bytes 147464 | tf_op jit(solution)/shard_map/ppermute | solution.py:334
  59.5 5.9 %collective-permute-start.20 = (f32[8,1536]{1,0:T(8,128)S(1)}, f32[8,1536]{1,0:T(8,128)S(1)}, u32[]{:S(2)}, u32[]{:S(2)}) collective-permute-start(f32[8,1536]{1,0:T(8,128)S(1)} %get-tuple-element.64), channel_id=1, source_target_pairs={{0,24},{4,28},{8,16},{12,20},{16,8},{20,12},{24,0},{28,4},{1,25},{... | collective-permute-start | bytes 147464 | tf_op jit(solution)/shard_map/ppermute | solution.py:334
  61.4 8.4 %collective-permute-start.21 = (f32[16,768]{1,0:T(8,128)S(1)}, f32[16,768]{1,0:T(8,128)S(1)}, u32[]{:S(2)}, u32[]{:S(2)}) collective-permute-start(f32[16,768]{1,0:T(8,128)S(1)} %get-tuple-element.65), channel_id=1, source_target_pairs={{0,2},{1,3},{2,0},{3,1},{4,6},{5,7},{6,4},{7,5},{8,10},{9,11},{10,... | collective-permute-start | bytes 147464 | tf_op jit(solution)/shard_map/ppermute | solution.py:334
  65.4 8.5 %collective-permute-start.25 = (f32[8,1536]{1,0:T(8,128)S(1)}, f32[8,1536]{1,0:T(8,128)S(1)}, u32[]{:S(2)}, u32[]{:S(2)}) collective-permute-start(f32[8,1536]{1,0:T(8,128)S(1)} %replica_mean.3.refs_0_.refs_1_), channel_id=1, source_target_pairs={{0,24},{4,28},{8,16},{12,20},{16,8},{20,12},{24,0},{28,4},{1,25},{... | collective-permute-start | bytes 147464 | tf_op jit(solution)/shard_map/ppermute | solution.py:334
  67.4 6.5 %collective-permute-start.24 = (f32[8,1536]{1,0:T(8,128)S(1)}, f32[8,1536]{1,0:T(8,128)S(1)}, u32[]{:S(2)}, u32[]{:S(2)}) collective-permute-start(f32[8,1536]{1,0:T(8,128)S(1)} %replica_mean.3.refs_0_.refs_1_), channel_id=1, source_target_pairs={{0,16},{4,20},{8,24},{12,28},{16,0},{20,4},{24,8},{28,12},{1,17},{... | collective-permute-start | bytes 147464 | tf_op jit(solution)/shard_map/ppermute | solution.py:334
  67.4 6.5 %collective-permute-start.23 = (f32[8,1536]{1,0:T(8,128)S(1)}, f32[8,1536]{1,0:T(8,128)S(1)}, u32[]{:S(2)}, u32[]{:S(2)}) collective-permute-start(f32[8,1536]{1,0:T(8,128)S(1)} %replica_mean.3.refs_0_.refs_1_), channel_id=1, source_target_pairs={{0,8},{4,12},{8,0},{12,4},{16,24},{20,28},{24,16},{28,20},{1,9},{5... | collective-permute-start | bytes 147464 | tf_op jit(solution)/shard_map/ppermute | solution.py:334
  69.9 3.9 %collective-permute-start.22 = (f32[16,512]{1,0:T(8,128)S(1)}, f32[16,512]{1,0:T(8,128)S(1)}, u32[]{:S(2)}, u32[]{:S(2)}) collective-permute-start(f32[16,512]{1,0:T(8,128)S(1)} %get-tuple-element.70.refs_1_), channel_id=1, source_target_pairs={{0,4},{4,0},{8,12},{12,8},{16,20},{20,16},{24,28},{28,24},{1,5},{5... | collective-permute-start | bytes 98312 | tf_op jit(solution)/shard_map/ppermute | solution.py:334
  73.9 16.2 %collective-permute-start.31 = (f32[4,8,1536]{2,1,0:T(8,128)S(1)}, f32[4,8,1536]{2,1,0:T(8,128)S(1)}, u32[]{:S(2)}, u32[]{:S(2)}) collective-permute-start(f32[4,8,1536]{2,1,0:T(8,128)S(1)} %stack_z.3.refs_0_.refs_1_), channel_id=1, source_target_pairs={{0,4},{4,0},{8,12},{12,8},{16,20},{20,16},{24,28},{28,24},{1,5},{5... | collective-permute-start | bytes 589832 | tf_op jit(solution)/shard_map/ppermute | solution.py:334
  75.3 5.7 %collective-permute-start.28 = (f32[16,512]{1,0:T(8,128)S(1)}, f32[16,512]{1,0:T(8,128)S(1)}, u32[]{:S(2)}, u32[]{:S(2)}) collective-permute-start(f32[16,512]{1,0:T(8,128)S(1)} %sum_y.3.refs_0_.refs_1_), channel_id=1, source_target_pairs={{0,24},{4,28},{8,16},{12,20},{16,8},{20,12},{24,0},{28,4},{1,25},{... | collective-permute-start | bytes 98312 | tf_op jit(solution)/shard_map/ppermute | solution.py:334
  77.2 4.8 %collective-permute-start.27 = (f32[16,512]{1,0:T(8,128)S(1)}, f32[16,512]{1,0:T(8,128)S(1)}, u32[]{:S(2)}, u32[]{:S(2)}) collective-permute-start(f32[16,512]{1,0:T(8,128)S(1)} %sum_y.3.refs_0_.refs_1_), channel_id=1, source_target_pairs={{0,16},{4,20},{8,24},{12,28},{16,0},{20,4},{24,8},{28,12},{1,17},{... | collective-permute-start | bytes 98312 | tf_op jit(solution)/shard_map/ppermute | solution.py:334
  77.2 4.8 %collective-permute-start.26 = (f32[16,512]{1,0:T(8,128)S(1)}, f32[16,512]{1,0:T(8,128)S(1)}, u32[]{:S(2)}, u32[]{:S(2)}) collective-permute-start(f32[16,512]{1,0:T(8,128)S(1)} %sum_y.3.refs_0_.refs_1_), channel_id=1, source_target_pairs={{0,8},{4,12},{8,0},{12,4},{16,24},{20,28},{24,16},{28,20},{1,9},{5... | collective-permute-start | bytes 98312 | tf_op jit(solution)/shard_map/ppermute | solution.py:334
  82.0 4.0 %collective-permute-start.29 = (f32[16,512]{1,0:T(8,128)S(1)}, f32[16,512]{1,0:T(8,128)S(1)}, u32[]{:S(2)}, u32[]{:S(2)}) collective-permute-start(f32[16,512]{1,0:T(8,128)S(1)} %sum_z.3.refs_0_), channel_id=1, source_target_pairs={{0,2},{1,3},{2,0},{3,1},{4,6},{5,7},{6,4},{7,5},{8,10},{9,11},{10,... | collective-permute-start | bytes 98312 | tf_op jit(solution)/shard_map/ppermute | solution.py:334
  86.0 1.3 %collective-permute-start.30 = (f32[32,512]{1,0:T(8,128)S(1)}, f32[32,512]{1,0:T(8,128)S(1)}, u32[]{:S(2)}, u32[]{:S(2)}) collective-permute-start(f32[32,512]{1,0:T(8,128)S(1)} %stack_x.3.refs_0_), channel_id=1, source_target_pairs={{0,1},{1,0},{2,3},{3,2},{4,5},{5,4},{6,7},{7,6},{8,9},{9,8},{10,11... | collective-permute-start | bytes 196616 | tf_op jit(solution)/shard_map/ppermute | solution.py:334
  87.8 5.0 %copy-start.4 = (bf16[1,512,1536]{2,1,0:T(8,128)(2,1)S(1)}, bf16[1,512,1536]{2,1,0:T(8,128)(2,1)}, u32[]{:S(2)}) copy-start(bf16[1,512,1536]{2,1,0:T(8,128)(2,1)} %refs_1_.5) | copy-start | bytes 4718596
  90.8 4.3 %collective-permute-start.34 = (f32[8,128]{1,0:T(8,128)S(1)}, f32[8,128]{1,0:T(8,128)S(1)}, u32[]{:S(2)}, u32[]{:S(2)}) collective-permute-start(f32[8,128]{1,0:T(8,128)S(1)} %get-tuple-element.78.refs_6_), channel_id=1, source_target_pairs={{0,3},{1,2},{2,1},{3,0},{4,7},{5,6},{6,5},{7,4},{8,11},{9,10},{10,... | collective-permute-start | bytes 12296 | tf_op jit(solution)/shard_map/ppermute | solution.py:334
  92.1 3.6 %collective-permute-start.33 = (f32[8,128]{1,0:T(8,128)S(1)}, f32[8,128]{1,0:T(8,128)S(1)}, u32[]{:S(2)}, u32[]{:S(2)}) collective-permute-start(f32[8,128]{1,0:T(8,128)S(1)} %get-tuple-element.78.refs_6_), channel_id=1, source_target_pairs={{0,2},{1,3},{2,0},{3,1},{4,6},{5,7},{6,4},{7,5},{8,10},{9,11},{10,... | collective-permute-start | bytes 12296 | tf_op jit(solution)/shard_map/ppermute | solution.py:334
  92.6 3.1 %collective-permute-start.32 = (f32[8,128]{1,0:T(8,128)S(1)}, f32[8,128]{1,0:T(8,128)S(1)}, u32[]{:S(2)}, u32[]{:S(2)}) collective-permute-start(f32[8,128]{1,0:T(8,128)S(1)} %get-tuple-element.78.refs_6_), channel_id=1, source_target_pairs={{0,1},{1,0},{2,3},{3,2},{4,5},{5,4},{6,7},{7,6},{8,9},{9,8},{10,11... | collective-permute-start | bytes 12296 | tf_op jit(solution)/shard_map/ppermute | solution.py:334

commit v6 on v4

--- a/solution.py
+++ b/solution.py
@@ -87,38 +87,34 @@
     total[pl.ds(pl.multiple_of((1 - core) * rows, rows), rows), :] = other[:, :width]
 
 
-def left_product(g, e, q, total, g_in, e_in, q_in, pieces, sems):
-    rank = q.shape[0]
-    block = g.shape[1] // STEPS
-    first = pltpu.make_async_copy(q, q_in, sems.at[2 * STEPS])
-    first.start()
-    copies = []
-    for i in range(STEPS):
-        rows = pl.ds(i * block, block)
-        pair = [pltpu.make_async_copy(src.at[0, rows, :], dst.at[rows, :], sems.at[2 * i + j]) for j, (src, dst) in enumerate(((g, g_in), (e, e_in)))]
-        for copy in pair:
+def left_kernel(gu, eu, qu, gd, ed, qd, keep_up, send_up, keep_down, send_down, *scratch):
+    up, down, stage, q_sems, sems = scratch[:5], scratch[5:10], *scratch[10:]
+    stages, waiting = [], []
+    for i, (source, part) in enumerate(((qu, up), (qd, down))):
+        waiting.append(pltpu.make_async_copy(source, part[2], q_sems.at[i]))
+        waiting[i].start()
+    for g, e, part in ((gu, eu, up), (gd, ed, down)):
+        block = g.shape[1] // STEPS
+        for i in range(STEPS):
+            rows = pl.ds(i * block, block)
+            n = 2 * len(stages)
+            copies = [
+                pltpu.make_async_copy(src.at[0, rows, :], dst.at[rows, :], sems.at[n + j])
+                for j, (src, dst) in enumerate(((g, part[0]), (e, part[1])))
+            ]
+            stages.append((part, slice(i * block, (i + 1) * block), copies))
+    for _, _, copies in stages:
+        for copy in copies:
             copy.start()
-        copies.append(pair)
-    first.wait()
-    parts = split3(q_in[...])
-    pieces[...] = jnp.concatenate(parts + (jnp.zeros_like(parts[0]),), axis=0).T
-    for i, pair in enumerate(copies):
-        for copy in pair:
+    for copy, (_, _, q, pieces, _) in zip(waiting, (up, down)):
+        copy.wait()
+        split_rows(q, pieces)
+    for (g, e, q, pieces, total), rows, copies in stages:
+        for copy in copies:
             copy.wait()
-        rows = slice(i * block, (i + 1) * block)
-        t = dot(g_in[rows, :], pieces[...]) + dot(e_in[rows, :], pieces[...])
-        t = (t[:, : 2 * rank] + t[:, 2 * rank :]).T
-        total[:, rows] = t[:rank] + t[rank:]
-
-
-def left_up_kernel(g, e, q, keep, send, total, *scratch):
-    left_product(g, e, q, total, *scratch)
-    split_cores(total, None, keep, send)
-
-
-def left_down_kernel(g, e, q, keep, send, total, stage, *scratch):
-    left_product(g, e, q, total, *scratch)
-    split_replicas(total, stage, keep, send)
+        total[:, rows] = add_pieces(dot(pieces[...], g[rows, :], NT) + dot(pieces[...], e[rows, :], NT))
+    split_cores(up[4], None, keep_up, send_up)
+    split_replicas(down[4], stage, keep_down, send_down)
 
 
 def split_x_kernel(width, keep, got, *outs):
@@ -254,7 +250,8 @@
     return results
 
 
-def basis_kernel(left_up, left_down, gram_up, gram_down, inv_up, inv_down, lhs_up, lhs_down):
+def basis_kernel(left_up, left_down, gram_up, gram_down, *refs):
+    inv_up, inv_down, lhs_up, lhs_down = refs[-4:]
     inverses = inverse_factors([gram_up[...], gram_down[...]])
     rank = left_up.shape[0]
     for inverse, inv, left, lhs in zip(inverses, (inv_up, inv_down), (left_up, left_down), (lhs_up, lhs_down)):
@@ -298,7 +295,8 @@
     return pl.ds(pl.multiple_of(pl.program_id(0) * block, block), block)
 
 
-def error_up_kernel(g, e, lhs, rhs, error):
+def error_up_kernel(g, e, lhs, rhs, error, made):
+    made[...] = jnp.zeros_like(made)
     part = rows_of(error.shape[1])
     rebuilt = dot(lhs[part, :], rhs[...])
     error[0] = (g[0, part, :].astype(F32) + e[0, part, :].astype(F32) - rebuilt).astype(BF16)
@@ -398,16 +396,16 @@
     narrow = pltpu.VMEM((rank, rows), F32)
     product = 4 * rows * ff * 4 * rank
 
-    def left(kernel, outs, g, e, q, scratch, name):
-        buffers = [pltpu.VMEM(g.shape[1:], BF16)] * 2 + [pltpu.VMEM(q.shape, F32), pltpu.VMEM((q.shape[1], 4 * rank), BF16)]
-        return call(
-            kernel, outs, g, e, q, name=name, flops=product, limit=61, in_specs=[pl.BlockSpec(memory_space=pltpu.HBM)] * 3,
-            scratch_shapes=scratch + buffers + [pltpu.SemaphoreType.DMA((2 * STEPS + 1,))],
-        )
-
-    keep_up, send_up = left(left_up_kernel, [core_half] * 2, gu, eu, qu, [narrow], "left_up")
+    buffers = [
+        [pltpu.VMEM(g.shape[1:], BF16)] * 2 + [pltpu.VMEM(q.shape, F32), pltpu.VMEM((3 * rank, q.shape[1]), BF16), total]
+        for g, q, total in ((gu, qu, narrow), (gd, qd, wide))
+    ]
+    keep_up, send_up, keep, send = call(
+        left_kernel, [core_half] * 2 + [replica_half] * 2, gu, eu, qu, gd, ed, qd, name="left", flops=2 * product, limit=61,
+        in_specs=[pl.BlockSpec(memory_space=pltpu.HBM)] * 6,
+        scratch_shapes=buffers[0] + buffers[1] + [stage, pltpu.SemaphoreType.DMA((2,)), pltpu.SemaphoreType.DMA((4 * STEPS,))],
+    )
     shards = sum_shards(keep_up, send_up, rows)
-    keep, send = left(left_down_kernel, [replica_half] * 2, gd, ed, qd, [wide, stage], "left_down")
     mine, other, _ = mean_replicas(keep, swap(send, "dp", 1), shards, rows)
 
     shard = call(functools.partial(shard_rows_kernel, ff), shaped(rank // n_shards, rows), mine, other, name="shard_rows")
@@ -426,17 +424,17 @@
     inv_up, inv_down, lhs_up, lhs_down = call(
         basis_kernel,
         [shaped(rank, rank)] * 2 + [shaped(rows, 4 * rank, dtype=BF16), shaped(ff, 4 * rank, dtype=BF16)],
-        left_up, left_down, gram_up, gram_down, name="basis", flops=10**9,
+        left_up, left_down, gram_up, gram_down, gu, eu, gd, ed, name="basis", in_specs=[VMEM] * 8,
     )
     rhs_up, shard = call(
         factor_up_kernel, [shaped(4 * rank, ff, dtype=BF16), shaped(rank // n_shards, rows + 128)], mine, other, inv_up,
         name="factor_up", scratch_shapes=[wide, stage],
     )
-    new_error_up = call(
-        error_up_kernel, shaped(1, rows, ff, dtype=BF16), gu, eu, lhs_up, rhs_up, name="error_up", flops=product // 2,
-        grid=(STEPS,), in_specs=[VMEM] * 4, out_specs=replica_blocks(rows, ff),
-    )
-    right_half, right_other = gather_shards(shard, rows, new_error_up)
+    new_error_up, made = call(
+        error_up_kernel, [shaped(1, rows, ff, dtype=BF16), shaped(8, 128)], gu, eu, lhs_up, rhs_up, name="error_up", flops=product // 2,
+        grid=(STEPS,), in_specs=[VMEM] * 4, out_specs=[replica_blocks(rows, ff), whole((8, 128))],
+    )
+    right_half, right_other = gather_shards(shard, rows, made)
     limit = CLIP_RMS * (2.0 * rows * ff * n_shards) ** 0.5
     rhs_down, clip = call(
         functools.partial(factor_down_kernel, limit), [shaped(4 * rank, rows, dtype=BF16), shaped(8, 128)],

time: 89.5 us -> 88.5 us (0.989)
    unnamed x14 -> x12, local copies, waits for them, and re-layouts: 2.27 us -> 1.79 us
    pallas_call x20 -> x19, Pallas kernels: 21.4 us -> 20.9 us  [call(): pl.pallas_call(kernel, out_shape=out_shape, compiler_params=params, cost_...]
  transfers between devices with their start and end apart: 24 -> 24, of which waited for: 20 -> 20; matrix products, arithmetic and copies ran while one was open for 0% -> 0% of each run, Pallas kernels for 13% -> 8%
where the time goes in v6:
time: 88.5 us; the launch traced here: 88.3 us
  waiting for transfers between devices  35.8 us (40%)
  starting transfers between devices  29 us (33%)
  Pallas kernels  20.9 us (24%)
  local copies, waits for them, and re-layouts  1.79 us (2%)
    ppermute x24, waiting for transfers between devices, swap(): return lax.ppermute(x, axis, pairs)  35.8 us
    ppermute x24, starting transfers between devices, swap(): return lax.ppermute(x, axis, pairs)  29 us
    pallas_call x19, Pallas kernels, call(): pl.pallas_call(kernel, out_shape=out_shape, compiler_params=params, cost_...  20.9 us
    unnamed x12, local copies, waits for them, and re-layouts  1.79 us
  transfers between devices with their start and end apart: 24, of which 20 were waited for; matrix products, arithmetic and copies ran while one was open for 0% of the time, Pallas kernels for 8%

profile of v6, /device:TPU:0, one launch (start us, length us, event | category | flops | bytes accessed | tf_op | source)
XLA Modules:
  0.0 88.3 jit_solution(1611512878808071123)
XLA Ops:
  0.6 0.0 copy-start.3
  0.6 8.7 %left.1 = (f32[32,512]{1,0:T(8,128)}, f32[32,512]{1,0:T(8,128)}, f32[4,8,1536]{2,1,0:T(8,128)}, f32[4,8,1536]{2,1,0:T(8,128)}) custom-call(bf16[1,512,1536]{2,1,0:T(8,128)(2,1)} %g.6, bf16[1,512,1536]{2,1,0:T(8,128)(2,1)} %e.6, f32[64,1536]{1,0:T(8,128)} %bitcast.2, bf16[1,1536,512]{2,1,0:T(8,128)(2,1)} %g.7, bf16[1,1536,512]{2,1,0:T(8,128)(2,1)} %e.7, ...), custom_call_target="tpu_custom_call" | custom-call | flops 1610612736 | bytes 7340032 | tf_op jit(solution)/shard_map/left/pallas_call | solution.py:339
  9.3 0.0 copy-start.2
  9.3 3.0 %collective-permute-start = (f32[4,8,1536]{2,1,0:T(8,128)}, f32[4,8,1536]{2,1,0:T(8,128)S(1)}, u32[]{:S(2)}, u32[]{:S(2)}) collective-permute-start(f32[4,8,1536]{2,1,0:T(8,128)} %get-tuple-element.42), channel_id=1, source_target_pairs={{0,4},{4,0},{8,12},{12,8},{16,20},{20,16},{24,28},{28,24},{1,5},{5... | collective-permute-start | bytes 589832 | tf_op jit(solution)/shard_map/ppermute | solution.py:344
  12.4 0.0 collective-permute-start.1
  12.4 1.5 %collective-permute-done.1.got = f32[32,512]{1,0:T(8,128)S(1)} collective-permute-done((f32[32,512]{1,0:T(8,128)}, f32[32,512]{1,0:T(8,128)S(1)}, u32[]{:S(2)}, u32[]{:S(2)}) %collective-permute-start.1) | collective-permute-done | bytes 65568 | tf_op jit(solution)/shard_map/ppermute | solution.py:344
  13.9 0.8 copy-done.5
  14.7 1.6 %collective-permute-start.2 = (f32[16,512]{1,0:T(8,128)S(1)}, f32[16,512]{1,0:T(8,128)S(1)}, u32[]{:S(2)}, u32[]{:S(2)}) collective-permute-start(f32[16,512]{1,0:T(8,128)S(1)} %get-tuple-element.46), channel_id=1, source_target_pairs={{0,2},{1,3},{2,0},{3,1},{4,6},{5,7},{6,4},{7,5},{8,10},{9,11},{10,... | collective-permute-start | bytes 98312 | tf_op jit(solution)/shard_map/ppermute | solution.py:344
  16.3 2.4 %collective-permute-done.2.refs_1_ = f32[16,512]{1,0:T(8,128)S(1)} collective-permute-done((f32[16,512]{1,0:T(8,128)S(1)}, f32[16,512]{1,0:T(8,128)S(1)}, u32[]{:S(2)}, u32[]{:S(2)}) %collective-permute-start.2) | collective-permute-done | bytes 32800 | tf_op jit(solution)/shard_map/ppermute | solution.py:344
  18.7 0.0 collective-permute-done.got
  18.7 0.9 %copy-done.4 = f32[4,8,1536]{2,1,0:T(8,128)S(1)} copy-done((f32[4,8,1536]{2,1,0:T(8,128)S(1)}, f32[4,8,1536]{2,1,0:T(8,128)}, u32[]{:S(2)}) %copy-start.4) | copy-done | bytes 196632
  19.7 1.6 %collective-permute-start.3 = (f32[8,1792]{1,0:T(8,128)S(1)}, f32[8,1792]{1,0:T(8,128)S(1)}, u32[]{:S(2)}, u32[]{:S(2)}) collective-permute-start(f32[8,1792]{1,0:T(8,128)S(1)} %get-tuple-element.48), channel_id=1, source_target_pairs={{0,8},{4,12},{8,0},{12,4},{16,24},{20,28},{24,16},{28,20},{1,9},{5... | collective-permute-start | bytes 172040 | tf_op jit(solution)/shard_map/ppermute | solution.py:344
  21.3 2.6 %collective-permute-start.4 = (f32[8,1792]{1,0:T(8,128)S(1)}, f32[8,1792]{1,0:T(8,128)S(1)}, u32[]{:S(2)}, u32[]{:S(2)}) collective-permute-start(f32[8,1792]{1,0:T(8,128)S(1)} %get-tuple-element.49), channel_id=1, source_target_pairs={{0,16},{4,20},{8,24},{12,28},{16,0},{20,4},{24,8},{28,12},{1,17},{... | collective-permute-start | bytes 172040 | tf_op jit(solution)/shard_map/ppermute | solution.py:344
  23.9 0.2 collective-permute-start.5
  24.1 0.3 collective-permute-done.3.refs_1_
  24.5 3.2 %collective-permute-done.4.refs_2_ = f32[8,1792]{1,0:T(8,128)S(1)} collective-permute-done((f32[8,1792]{1,0:T(8,128)S(1)}, f32[8,1792]{1,0:T(8,128)S(1)}, u32[]{:S(2)}, u32[]{:S(2)}) %collective-permute-start.4) | collective-permute-done | bytes 57376 | tf_op jit(solution)/shard_map/ppermute | solution.py:344
  27.6 2.3 %collective-permute-done.5.refs_3_ = f32[8,1792]{1,0:T(8,128)S(1)} collective-permute-done((f32[8,1792]{1,0:T(8,128)S(1)}, f32[8,1792]{1,0:T(8,128)S(1)}, u32[]{:S(2)}, u32[]{:S(2)}) %collective-permute-start.5) | collective-permute-done | bytes 57376 | tf_op jit(solution)/shard_map/ppermute | solution.py:344
  29.9 0.8 collective-permute-start.8
  30.7 0.0 collective-permute-start.7
  30.7 3.7 %collective-permute-start.6 = (f32[8,1792]{1,0:T(8,128)S(1)}, f32[8,1792]{1,0:T(8,128)S(1)}, u32[]{:S(2)}, u32[]{:S(2)}) collective-permute-start(f32[8,1792]{1,0:T(8,128)S(1)} %replica_mean.2.refs_0_), channel_id=1, source_target_pairs={{0,8},{4,12},{8,0},{12,4},{16,24},{20,28},{24,16},{28,20},{1,9},{5... | collective-permute-start | bytes 172040 | tf_op jit(solution)/shard_map/ppermute | solution.py:344
  34.3 1.7 %collective-permute-done.8.refs_3_ = f32[8,1792]{1,0:T(8,128)S(1)} collective-permute-done((f32[8,1792]{1,0:T(8,128)S(1)}, f32[8,1792]{1,0:T(8,128)S(1)}, u32[]{:S(2)}, u32[]{:S(2)}) %collective-permute-start.8) | collective-permute-done | bytes 57376 | tf_op jit(solution)/shard_map/ppermute | solution.py:344
  36.0 0.9 %collective-permute-done.7.refs_2_ = f32[8,1792]{1,0:T(8,128)S(1)} collective-permute-done((f32[8,1792]{1,0:T(8,128)S(1)}, f32[8,1792]{1,0:T(8,128)S(1)}, u32[]{:S(2)}, u32[]{:S(2)}) %collective-permute-start.7) | collective-permute-done | bytes 57376 | tf_op jit(solution)/shard_map/ppermute | solution.py:344
  37.0 0.0 collective-permute-done.6.refs_1_
  37.0 0.6 collective-permute-start.9
  37.6 5.5 %collective-permute-done.9.other = f32[4,8,1792]{2,1,0:T(8,128)S(1)} collective-permute-done((f32[4,8,1792]{2,1,0:T(8,128)S(1)}, f32[4,8,1792]{2,1,0:T(8,128)S(1)}, u32[]{:S(2)}, u32[]{:S(2)}) %collective-permute-start.9) | collective-permute-done | bytes 229408 | tf_op jit(solution)/shard_map/ppermute | solution.py:344
  43.1 0.0 copy-start.1
  43.1 1.6 %collective-permute-start.10 = (f32[16,512]{1,0:T(8,128)S(1)}, f32[16,512]{1,0:T(8,128)S(1)}, u32[]{:S(2)}, u32[]{:S(2)}) collective-permute-start(f32[16,512]{1,0:T(8,128)S(1)} %shard_rows.1.refs_0_), channel_id=1, source_target_pairs={{0,2},{1,3},{2,0},{3,1},{4,6},{5,7},{6,4},{7,5},{8,10},{9,11},{10,... | collective-permute-start | bytes 98312 | tf_op jit(solution)/shard_map/ppermute | solution.py:344
  44.7 0.0 copy-done.3
  44.7 1.2 %right_down.1 = (f32[64,1536]{1,0:T(8,128)S(1)}, f32[32,640]{1,0:T(8,128)S(1)}, f32[32,640]{1,0:T(8,128)S(1)}) custom-call(f32[4,8,1792]{2,1,0:T(8,128)S(1)} %stack_z.2.mine, f32[4,8,1792]{2,1,0:T(8,128)S(1)} %collective-permute-done.9.other, bf16[1,1536,512]{2,1,0:T(8,128)(2,1)S(1)} %copy-done.2, bf16[1,1536,512]{2,1,0:T(8,128)(2,1)S(1)} %copy-done.3), custom_call_target="tpu_custom_call" | custom-call | flops 805306368 | bytes 4161536 | tf_op jit(solution)/shard_map/right_down/pallas_call | solution.py:339
  45.9 1.2 %collective-permute-done.10.refs_1_ = f32[16,512]{1,0:T(8,128)S(1)} collective-permute-done((f32[16,512]{1,0:T(8,128)S(1)}, f32[16,512]{1,0:T(8,128)S(1)}, u32[]{:S(2)}, u32[]{:S(2)}) %collective-permute-start.10) | collective-permute-done | bytes 32800 | tf_op jit(solution)/shard_map/ppermute | solution.py:344
  47.1 0.1 collective-permute-start.11
  47.2 1.2 %collective-permute-done.11.other = f32[32,512]{1,0:T(8,128)S(1)} collective-permute-done((f32[32,512]{1,0:T(8,128)S(1)}, f32[32,512]{1,0:T(8,128)S(1)}, u32[]{:S(2)}, u32[]{:S(2)}) %collective-permute-start.11) | collective-permute-done | bytes 65568 | tf_op jit(solution)/shard_map/ppermute | solution.py:344
  48.4 0.0 copy-done.1
  48.4 1.2 %right_up.1 = (f32[64,512]{1,0:T(8,128)S(1)}, f32[64,64]{1,0:T(8,128)S(1)}, f32[4,8,1536]{2,1,0:T(8,128)S(1)}, f32[4,8,1536]{2,1,0:T(8,128)S(1)}) custom-call(f32[32,512]{1,0:T(8,128)S(1)} %stack_x.2.mine, f32[32,512]{1,0:T(8,128)S(1)} %collective-permute-done.11.other, bf16[1,512,1536]{2,1,0:T(8,128)(2,1)S(1)} %copy-done, bf16[1,512,1536]{2,1,0:T(8,128)(2,1)S(1)} %copy-done.1), custom_call_target="tpu_custom_call" | custom-call | flops 805306368 | bytes 3817472 | tf_op jit(solution)/shard_map/right_up/pallas_call | solution.py:339
  49.6 0.6 collective-permute-start.12
  50.2 0.0 collective-permute-start.13
  50.2 1.3 %collective-permute-done.13.got = f32[32,640]{1,0:T(8,128)S(1)} collective-permute-done((f32[32,640]{1,0:T(8,128)S(1)}, f32[32,640]{1,0:T(8,128)S(1)}, u32[]{:S(2)}, u32[]{:S(2)}) %collective-permute-start.13) | collective-permute-done | bytes 81952 | tf_op jit(solution)/shard_map/ppermute | solution.py:344
  51.5 1.6 %collective-permute-start.14 = (f32[16,768]{1,0:T(8,128)S(1)}, f32[16,768]{1,0:T(8,128)S(1)}, u32[]{:S(2)}, u32[]{:S(2)}) collective-permute-start(f32[16,768]{1,0:T(8,128)S(1)} %get-tuple-element.59), channel_id=1, source_target_pairs={{0,2},{1,3},{2,0},{3,1},{4,6},{5,7},{6,4},{7,5},{8,10},{9,11},{10,... | collective-permute-start | bytes 147464 | tf_op jit(solution)/shard_map/ppermute | solution.py:344
  53.1 2.6 %collective-permute-done.14.refs_1_ = f32[16,768]{1,0:T(8,128)S(1)} collective-permute-done((f32[16,768]{1,0:T(8,128)S(1)}, f32[16,768]{1,0:T(8,128)S(1)}, u32[]{:S(2)}, u32[]{:S(2)}) %collective-permute-start.14) | collective-permute-done | bytes 49184 | tf_op jit(solution)/shard_map/ppermute | solution.py:344
  55.7 1.0 %collective-permute-done.12.got = f32[4,8,1536]{2,1,0:T(8,128)S(1)} collective-permute-done((f32[4,8,1536]{2,1,0:T(8,128)S(1)}, f32[4,8,1536]{2,1,0:T(8,128)S(1)}, u32[]{:S(2)}, u32[]{:S(2)}) %collective-permute-start.12) | collective-permute-done | bytes 196640 | tf_op jit(solution)/shard_map/ppermute | solution.py:344
  56.7 0.1 split_z.3
  56.8 1.6 %collective-permute-start.15 = (f32[8,1792]{1,0:T(8,128)S(1)}, f32[8,1792]{1,0:T(8,128)S(1)}, u32[]{:S(2)}, u32[]{:S(2)}) collective-permute-start(f32[8,1792]{1,0:T(8,128)S(1)} %get-tuple-element.63), channel_id=1, source_target_pairs={{0,8},{4,12},{8,0},{12,4},{16,24},{20,28},{24,16},{28,20},{1,9},{5... | collective-permute-start | bytes 172040 | tf_op jit(solution)/shard_map/ppermute | solution.py:344
  58.3 0.9 %collective-permute-start.16 = (f32[8,1792]{1,0:T(8,128)S(1)}, f32[8,1792]{1,0:T(8,128)S(1)}, u32[]{:S(2)}, u32[]{:S(2)}) collective-permute-start(f32[8,1792]{1,0:T(8,128)S(1)} %get-tuple-element.64), channel_id=1, source_target_pairs={{0,16},{4,20},{8,24},{12,28},{16,0},{20,4},{24,8},{28,12},{1,17},{... | collective-permute-start | bytes 172040 | tf_op jit(solution)/shard_map/ppermute | solution.py:344
  59.2 1.9 %collective-permute-start.17 = (f32[8,1792]{1,0:T(8,128)S(1)}, f32[8,1792]{1,0:T(8,128)S(1)}, u32[]{:S(2)}, u32[]{:S(2)}) collective-permute-start(f32[8,1792]{1,0:T(8,128)S(1)} %get-tuple-element.65), channel_id=1, source_target_pairs={{0,24},{4,28},{8,16},{12,20},{16,8},{20,12},{24,0},{28,4},{1,25},{... | collective-permute-start | bytes 172040 | tf_op jit(solution)/shard_map/ppermute | solution.py:344
  61.2 0.0 collective-permute-done.15.refs_1_
  61.2 3.3 %collective-permute-done.16.refs_2_ = f32[8,1792]{1,0:T(8,128)S(1)} collective-permute-done((f32[8,1792]{1,0:T(8,128)S(1)}, f32[8,1792]{1,0:T(8,128)S(1)}, u32[]{:S(2)}, u32[]{:S(2)}) %collective-permute-start.16) | collective-permute-done | bytes 57376 | tf_op jit(solution)/shard_map/ppermute | solution.py:344
  64.5 0.8 collective-permute-done.17.refs_3_
  65.3 1.9 %collective-permute-start.20 = (f32[8,1792]{1,0:T(8,128)S(1)}, f32[8,1792]{1,0:T(8,128)S(1)}, u32[]{:S(2)}, u32[]{:S(2)}) collective-permute-start(f32[8,1792]{1,0:T(8,128)S(1)} %replica_mean.3.refs_0_), channel_id=1, source_target_pairs={{0,24},{4,28},{8,16},{12,20},{16,8},{20,12},{24,0},{28,4},{1,25},{... | collective-permute-start | bytes 172040 | tf_op jit(solution)/shard_map/ppermute | solution.py:344
  67.3 0.6 collective-permute-start.19
  67.8 1.9 %collective-permute-start.18 = (f32[8,1792]{1,0:T(8,128)S(1)}, f32[8,1792]{1,0:T(8,128)S(1)}, u32[]{:S(2)}, u32[]{:S(2)}) collective-permute-start(f32[8,1792]{1,0:T(8,128)S(1)} %replica_mean.3.refs_0_), channel_id=1, source_target_pairs={{0,8},{4,12},{8,0},{12,4},{16,24},{20,28},{24,16},{28,20},{1,9},{5... | collective-permute-start | bytes 172040 | tf_op jit(solution)/shard_map/ppermute | solution.py:344
  69.8 1.6 %collective-permute-done.20.refs_3_ = f32[8,1792]{1,0:T(8,128)S(1)} collective-permute-done((f32[8,1792]{1,0:T(8,128)S(1)}, f32[8,1792]{1,0:T(8,128)S(1)}, u32[]{:S(2)}, u32[]{:S(2)}) %collective-permute-start.20) | collective-permute-done | bytes 57376 | tf_op jit(solution)/shard_map/ppermute | solution.py:344
  71.4 1.3 %collective-permute-done.19.refs_2_ = f32[8,1792]{1,0:T(8,128)S(1)} collective-permute-done((f32[8,1792]{1,0:T(8,128)S(1)}, f32[8,1792]{1,0:T(8,128)S(1)}, u32[]{:S(2)}, u32[]{:S(2)}) %collective-permute-start.19) | collective-permute-done | bytes 57376 | tf_op jit(solution)/shard_map/ppermute | solution.py:344
  72.6 0.0 collective-permute-done.18.refs_1_
  72.7 0.6 collective-permute-start.21
  73.3 3.2 %basis.1 = (f32[64,64]{1,0:T(8,128)S(1)}, f32[64,64]{1,0:T(8,128)S(1)}, bf16[512,256]{1,0:T(8,128)(2,1)S(1)}, bf16[1536,256]{1,0:T(8,128)(2,1)S(1)}) custom-call(f32[64,512]{1,0:T(8,128)S(1)} %get-tuple-element.52.left_up, f32[64,1536]{1,0:T(8,128)S(1)} %get-tuple-element.51._.left_down, f32[64,64]{1,0:T(8,128)S(1)} %get-tuple-element.53.gram_up, ...), custom_call_target="tpu_custom_call" | custom-call | bytes 7929856 | tf_op jit(solution)/shard_map/basis/pallas_call | solution.py:339
  76.5 2.3 %collective-permute-done.21.other = f32[4,8,1792]{2,1,0:T(8,128)S(1)} collective-permute-done((f32[4,8,1792]{2,1,0:T(8,128)S(1)}, f32[4,8,1792]{2,1,0:T(8,128)S(1)}, u32[]{:S(2)}, u32[]{:S(2)}) %collective-permute-start.21) | collective-permute-done | bytes 229408 | tf_op jit(solution)/shard_map/ppermute | solution.py:344
  78.8 0.7 factor_up.1
  79.4 1.6 %collective-permute-start.22 = (f32[16,640]{1,0:T(8,128)S(1)}, f32[16,640]{1,0:T(8,128)S(1)}, u32[]{:S(2)}, u32[]{:S(2)}) collective-permute-start(f32[16,640]{1,0:T(8,128)S(1)} %get-tuple-element.71.refs_0_), channel_id=1, source_target_pairs={{0,2},{1,3},{2,0},{3,1},{4,6},{5,7},{6,4},{7,5},{8,10},{9,11},{10,... | collective-permute-start | bytes 122888 | tf_op jit(solution)/shard_map/ppermute | solution.py:344
  81.0 2.3 %error_up.1 = (bf16[1,512,1536]{2,1,0:T(8,128)(2,1)}, f32[8,128]{1,0:T(8,128)S(1)}) custom-call(bf16[1,512,1536]{2,1,0:T(8,128)(2,1)S(1)} %copy-done, bf16[1,512,1536]{2,1,0:T(8,128)(2,1)S(1)} %copy-done.1, bf16[512,256]{1,0:T(8,128)(2,1)S(1)} %get-tuple-element.61.lhs.lhs_up, bf16[256,1536]{1,0:T(8,128)(2,1)S(1)} %get-tuple-element.67.rhs.rhs_up), custom_call_target="tpu_custom_call" | custom-call | flops 402653184 | bytes 5771264 | tf_op jit(solution)/shard_map/error_up/pallas_call | solution.py:339
  83.3 0.2 collective-permute-done.22.refs_1_
  83.5 0.1 collective-permute-start.23
  83.6 1.3 %collective-permute-done.23.other = f32[32,640]{1,0:T(8,128)S(1)} collective-permute-done((f32[32,640]{1,0:T(8,128)S(1)}, f32[32,640]{1,0:T(8,128)S(1)}, u32[]{:S(2)}, u32[]{:S(2)}) %collective-permute-start.23) | collective-permute-done | bytes 81952 | tf_op jit(solution)/shard_map/ppermute | solution.py:344
  84.9 0.4 factor_down.1
  85.3 3.0 %last.1 = (bf16[1,1536,512]{2,1,0:T(8,128)(2,1)}, bf16[512,1536]{1,0:T(8,128)(2,1)}, bf16[1536,512]{1,0:T(8,128)(2,1)}) custom-call(bf16[1,1536,512]{2,1,0:T(8,128)(2,1)S(1)} %copy-done.2, bf16[1,1536,512]{2,1,0:T(8,128)(2,1)S(1)} %copy-done.3, bf16[512,256]{1,0:T(8,128)(2,1)S(1)} %get-tuple-element.61.lhs.lhs_up, ...), custom_call_target="tpu_custom_call" | custom-call | flops 805306368 | bytes 9965568 | tf_op jit(solution)/shard_map/last/pallas_call | solution.py:339
  (15 shorter events, 0.2 us)
Async XLA Ops:
  0.6 44.1 %copy-start.3 = (bf16[1,1536,512]{2,1,0:T(8,128)(2,1)S(1)}, bf16[1,1536,512]{2,1,0:T(8,128)(2,1)}, u32[]{:S(2)}) copy-start(bf16[1,1536,512]{2,1,0:T(8,128)(2,1)} %e.7) | copy-start | bytes 4718596
  9.3 35.4 %copy-start.2 = (bf16[1,1536,512]{2,1,0:T(8,128)(2,1)S(1)}, bf16[1,1536,512]{2,1,0:T(8,128)(2,1)}, u32[]{:S(2)}) copy-start(bf16[1,1536,512]{2,1,0:T(8,128)(2,1)} %g.7) | copy-start | bytes 4718596
  9.3 9.3 %collective-permute-start = (f32[4,8,1536]{2,1,0:T(8,128)}, f32[4,8,1536]{2,1,0:T(8,128)S(1)}, u32[]{:S(2)}, u32[]{:S(2)}) collective-permute-start(f32[4,8,1536]{2,1,0:T(8,128)} %get-tuple-element.42), channel_id=1, source_target_pairs={{0,4},{4,0},{8,12},{12,8},{16,20},{20,16},{24,28},{28,24},{1,5},{5... | collective-permute-start | bytes 589832 | tf_op jit(solution)/shard_map/ppermute | solution.py:344
  12.4 1.5 %collective-permute-start.1 = (f32[32,512]{1,0:T(8,128)}, f32[32,512]{1,0:T(8,128)S(1)}, u32[]{:S(2)}, u32[]{:S(2)}) collective-permute-start(f32[32,512]{1,0:T(8,128)} %get-tuple-element.44), channel_id=1, source_target_pairs={{0,1},{1,0},{2,3},{3,2},{4,5},{5,4},{6,7},{7,6},{8,9},{9,8},{10,11... | collective-permute-start | bytes 196616 | tf_op jit(solution)/shard_map/ppermute | solution.py:344
  13.8 0.8 copy-start.5
  14.7 4.0 %collective-permute-start.2 = (f32[16,512]{1,0:T(8,128)S(1)}, f32[16,512]{1,0:T(8,128)S(1)}, u32[]{:S(2)}, u32[]{:S(2)}) collective-permute-start(f32[16,512]{1,0:T(8,128)S(1)} %get-tuple-element.46), channel_id=1, source_target_pairs={{0,2},{1,3},{2,0},{3,1},{4,6},{5,7},{6,4},{7,5},{8,10},{9,11},{10,... | collective-permute-start | bytes 98312 | tf_op jit(solution)/shard_map/ppermute | solution.py:344
  18.7 0.9 %copy-start.4 = (f32[4,8,1536]{2,1,0:T(8,128)S(1)}, f32[4,8,1536]{2,1,0:T(8,128)}, u32[]{:S(2)}) copy-start(f32[4,8,1536]{2,1,0:T(8,128)} %get-tuple-element.41.keep) | copy-start | bytes 589828
  19.7 4.8 %collective-permute-start.3 = (f32[8,1792]{1,0:T(8,128)S(1)}, f32[8,1792]{1,0:T(8,128)S(1)}, u32[]{:S(2)}, u32[]{:S(2)}) collective-permute-start(f32[8,1792]{1,0:T(8,128)S(1)} %get-tuple-element.48), channel_id=1, source_target_pairs={{0,8},{4,12},{8,0},{12,4},{16,24},{20,28},{24,16},{28,20},{1,9},{5... | collective-permute-start | bytes 172040 | tf_op jit(solution)/shard_map/ppermute | solution.py:344
  21.3 6.3 %collective-permute-start.4 = (f32[8,1792]{1,0:T(8,128)S(1)}, f32[8,1792]{1,0:T(8,128)S(1)}, u32[]{:S(2)}, u32[]{:S(2)}) collective-permute-start(f32[8,1792]{1,0:T(8,128)S(1)} %get-tuple-element.49), channel_id=1, source_target_pairs={{0,16},{4,20},{8,24},{12,28},{16,0},{20,4},{24,8},{28,12},{1,17},{... | collective-permute-start | bytes 172040 | tf_op jit(solution)/shard_map/ppermute | solution.py:344
  23.9 6.0 %collective-permute-start.5 = (f32[8,1792]{1,0:T(8,128)S(1)}, f32[8,1792]{1,0:T(8,128)S(1)}, u32[]{:S(2)}, u32[]{:S(2)}) collective-permute-start(f32[8,1792]{1,0:T(8,128)S(1)} %get-tuple-element.50), channel_id=1, source_target_pairs={{0,24},{4,28},{8,16},{12,20},{16,8},{20,12},{24,0},{28,4},{1,25},{... | collective-permute-start | bytes 172040 | tf_op jit(solution)/shard_map/ppermute | solution.py:344
  29.9 6.2 %collective-permute-start.8 = (f32[8,1792]{1,0:T(8,128)S(1)}, f32[8,1792]{1,0:T(8,128)S(1)}, u32[]{:S(2)}, u32[]{:S(2)}) collective-permute-start(f32[8,1792]{1,0:T(8,128)S(1)} %replica_mean.2.refs_0_), channel_id=1, source_target_pairs={{0,24},{4,28},{8,16},{12,20},{16,8},{20,12},{24,0},{28,4},{1,25},{... | collective-permute-start | bytes 172040 | tf_op jit(solution)/shard_map/ppermute | solution.py:344
  30.7 6.3 %collective-permute-start.7 = (f32[8,1792]{1,0:T(8,128)S(1)}, f32[8,1792]{1,0:T(8,128)S(1)}, u32[]{:S(2)}, u32[]{:S(2)}) collective-permute-start(f32[8,1792]{1,0:T(8,128)S(1)} %replica_mean.2.refs_0_), channel_id=1, source_target_pairs={{0,16},{4,20},{8,24},{12,28},{16,0},{20,4},{24,8},{28,12},{1,17},{... | collective-permute-start | bytes 172040 | tf_op jit(solution)/shard_map/ppermute | solution.py:344
  30.7 6.3 %collective-permute-start.6 = (f32[8,1792]{1,0:T(8,128)S(1)}, f32[8,1792]{1,0:T(8,128)S(1)}, u32[]{:S(2)}, u32[]{:S(2)}) collective-permute-start(f32[8,1792]{1,0:T(8,128)S(1)} %replica_mean.2.refs_0_), channel_id=1, source_target_pairs={{0,8},{4,12},{8,0},{12,4},{16,24},{20,28},{24,16},{28,20},{1,9},{5... | collective-permute-start | bytes 172040 | tf_op jit(solution)/shard_map/ppermute | solution.py:344
  37.0 6.1 %collective-permute-start.9 = (f32[4,8,1792]{2,1,0:T(8,128)S(1)}, f32[4,8,1792]{2,1,0:T(8,128)S(1)}, u32[]{:S(2)}, u32[]{:S(2)}) collective-permute-start(f32[4,8,1792]{2,1,0:T(8,128)S(1)} %stack_z.2.mine), channel_id=1, source_target_pairs={{0,4},{4,0},{8,12},{12,8},{16,20},{20,16},{24,28},{28,24},{1,5},{5... | collective-permute-start | bytes 688136 | tf_op jit(solution)/shard_map/ppermute | solution.py:344
  43.1 5.3 %copy-start = (bf16[1,512,1536]{2,1,0:T(8,128)(2,1)S(1)}, bf16[1,512,1536]{2,1,0:T(8,128)(2,1)}, u32[]{:S(2)}) copy-start(bf16[1,512,1536]{2,1,0:T(8,128)(2,1)} %g.6) | copy-start | bytes 4718596
  43.1 5.3 %copy-start.1 = (bf16[1,512,1536]{2,1,0:T(8,128)(2,1)S(1)}, bf16[1,512,1536]{2,1,0:T(8,128)(2,1)}, u32[]{:S(2)}) copy-start(bf16[1,512,1536]{2,1,0:T(8,128)(2,1)} %e.6) | copy-start | bytes 4718596
  43.1 4.0 %collective-permute-start.10 = (f32[16,512]{1,0:T(8,128)S(1)}, f32[16,512]{1,0:T(8,128)S(1)}, u32[]{:S(2)}, u32[]{:S(2)}) collective-permute-start(f32[16,512]{1,0:T(8,128)S(1)} %shard_rows.1.refs_0_), channel_id=1, source_target_pairs={{0,2},{1,3},{2,0},{3,1},{4,6},{5,7},{6,4},{7,5},{8,10},{9,11},{10,... | collective-permute-start | bytes 98312 | tf_op jit(solution)/shard_map/ppermute | solution.py:344
  47.1 1.3 %collective-permute-start.11 = (f32[32,512]{1,0:T(8,128)S(1)}, f32[32,512]{1,0:T(8,128)S(1)}, u32[]{:S(2)}, u32[]{:S(2)}) collective-permute-start(f32[32,512]{1,0:T(8,128)S(1)} %stack_x.2.mine), channel_id=1, source_target_pairs={{0,1},{1,0},{2,3},{3,2},{4,5},{5,4},{6,7},{7,6},{8,9},{9,8},{10,11... | collective-permute-start | bytes 196616 | tf_op jit(solution)/shard_map/ppermute | solution.py:344
  49.6 7.0 %collective-permute-start.12 = (f32[4,8,1536]{2,1,0:T(8,128)S(1)}, f32[4,8,1536]{2,1,0:T(8,128)S(1)}, u32[]{:S(2)}, u32[]{:S(2)}) collective-permute-start(f32[4,8,1536]{2,1,0:T(8,128)S(1)} %get-tuple-element.55), channel_id=1, source_target_pairs={{0,4},{4,0},{8,12},{12,8},{16,20},{20,16},{24,28},{28,24},{1,5},{5... | collective-permute-start | bytes 589832 | tf_op jit(solution)/shard_map/ppermute | solution.py:344
  50.2 1.3 %collective-permute-start.13 = (f32[32,640]{1,0:T(8,128)S(1)}, f32[32,640]{1,0:T(8,128)S(1)}, u32[]{:S(2)}, u32[]{:S(2)}) collective-permute-start(f32[32,640]{1,0:T(8,128)S(1)} %get-tuple-element.57), channel_id=1, source_target_pairs={{0,1},{1,0},{2,3},{3,2},{4,5},{5,4},{6,7},{7,6},{8,9},{9,8},{10,11... | collective-permute-start | bytes 245768 | tf_op jit(solution)/shard_map/ppermute | solution.py:344
  51.5 4.2 %collective-permute-start.14 = (f32[16,768]{1,0:T(8,128)S(1)}, f32[16,768]{1,0:T(8,128)S(1)}, u32[]{:S(2)}, u32[]{:S(2)}) collective-permute-start(f32[16,768]{1,0:T(8,128)S(1)} %get-tuple-element.59), channel_id=1, source_target_pairs={{0,2},{1,3},{2,0},{3,1},{4,6},{5,7},{6,4},{7,5},{8,10},{9,11},{10,... | collective-permute-start | bytes 147464 | tf_op jit(solution)/shard_map/ppermute | solution.py:344
  56.8 4.4 %collective-permute-start.15 = (f32[8,1792]{1,0:T(8,128)S(1)}, f32[8,1792]{1,0:T(8,128)S(1)}, u32[]{:S(2)}, u32[]{:S(2)}) collective-permute-start(f32[8,1792]{1,0:T(8,128)S(1)} %get-tuple-element.63), channel_id=1, source_target_pairs={{0,8},{4,12},{8,0},{12,4},{16,24},{20,28},{24,16},{28,20},{1,9},{5... | collective-permute-start | bytes 172040 | tf_op jit(solution)/shard_map/ppermute | solution.py:344
  58.3 6.2 %collective-permute-start.16 = (f32[8,1792]{1,0:T(8,128)S(1)}, f32[8,1792]{1,0:T(8,128)S(1)}, u32[]{:S(2)}, u32[]{:S(2)}) collective-permute-start(f32[8,1792]{1,0:T(8,128)S(1)} %get-tuple-element.64), channel_id=1, source_target_pairs={{0,16},{4,20},{8,24},{12,28},{16,0},{20,4},{24,8},{28,12},{1,17},{... | collective-permute-start | bytes 172040 | tf_op jit(solution)/shard_map/ppermute | solution.py:344
  59.2 6.1 %collective-permute-start.17 = (f32[8,1792]{1,0:T(8,128)S(1)}, f32[8,1792]{1,0:T(8,128)S(1)}, u32[]{:S(2)}, u32[]{:S(2)}) collective-permute-start(f32[8,1792]{1,0:T(8,128)S(1)} %get-tuple-element.65), channel_id=1, source_target_pairs={{0,24},{4,28},{8,16},{12,20},{16,8},{20,12},{24,0},{28,4},{1,25},{... | collective-permute-start | bytes 172040 | tf_op jit(solution)/shard_map/ppermute | solution.py:344
  65.3 6.0 %collective-permute-start.20 = (f32[8,1792]{1,0:T(8,128)S(1)}, f32[8,1792]{1,0:T(8,128)S(1)}, u32[]{:S(2)}, u32[]{:S(2)}) collective-permute-start(f32[8,1792]{1,0:T(8,128)S(1)} %replica_mean.3.refs_0_), channel_id=1, source_target_pairs={{0,24},{4,28},{8,16},{12,20},{16,8},{20,12},{24,0},{28,4},{1,25},{... | collective-permute-start | bytes 172040 | tf_op jit(solution)/shard_map/ppermute | solution.py:344
  67.3 5.4 %collective-permute-start.19 = (f32[8,1792]{1,0:T(8,128)S(1)}, f32[8,1792]{1,0:T(8,128)S(1)}, u32[]{:S(2)}, u32[]{:S(2)}) collective-permute-start(f32[8,1792]{1,0:T(8,128)S(1)} %replica_mean.3.refs_0_), channel_id=1, source_target_pairs={{0,16},{4,20},{8,24},{12,28},{16,0},{20,4},{24,8},{28,12},{1,17},{... | collective-permute-start | bytes 172040 | tf_op jit(solution)/shard_map/ppermute | solution.py:344
  67.8 4.8 %collective-permute-start.18 = (f32[8,1792]{1,0:T(8,128)S(1)}, f32[8,1792]{1,0:T(8,128)S(1)}, u32[]{:S(2)}, u32[]{:S(2)}) collective-permute-start(f32[8,1792]{1,0:T(8,128)S(1)} %replica_mean.3.refs_0_), channel_id=1, source_target_pairs={{0,8},{4,12},{8,0},{12,4},{16,24},{20,28},{24,16},{28,20},{1,9},{5... | collective-permute-start | bytes 172040 | tf_op jit(solution)/shard_map/ppermute | solution.py:344
  72.7 6.1 %collective-permute-start.21 = (f32[4,8,1792]{2,1,0:T(8,128)S(1)}, f32[4,8,1792]{2,1,0:T(8,128)S(1)}, u32[]{:S(2)}, u32[]{:S(2)}) collective-permute-start(f32[4,8,1792]{2,1,0:T(8,128)S(1)} %stack_z.3.mine), channel_id=1, source_target_pairs={{0,4},{4,0},{8,12},{12,8},{16,20},{20,16},{24,28},{28,24},{1,5},{5... | collective-permute-start | bytes 688136 | tf_op jit(solution)/shard_map/ppermute | solution.py:344
  79.4 4.1 %collective-permute-start.22 = (f32[16,640]{1,0:T(8,128)S(1)}, f32[16,640]{1,0:T(8,128)S(1)}, u32[]{:S(2)}, u32[]{:S(2)}) collective-permute-start(f32[16,640]{1,0:T(8,128)S(1)} %get-tuple-element.71.refs_0_), channel_id=1, source_target_pairs={{0,2},{1,3},{2,0},{3,1},{4,6},{5,7},{6,4},{7,5},{8,10},{9,11},{10,... | collective-permute-start | bytes 122888 | tf_op jit(solution)/shard_map/ppermute | solution.py:344
  83.5 1.3 %collective-permute-start.23 = (f32[32,640]{1,0:T(8,128)S(1)}, f32[32,640]{1,0:T(8,128)S(1)}, u32[]{:S(2)}, u32[]{:S(2)}) collective-permute-start(f32[32,640]{1,0:T(8,128)S(1)} %stack_x.3.mine), channel_id=1, source_target_pairs={{0,1},{1,0},{2,3},{3,2},{4,5},{5,4},{6,7},{7,6},{8,9},{9,8},{10,11... | collective-permute-start | bytes 245768 | tf_op jit(solution)/shard_map/ppermute | solution.py:344

commit v7 on v6

v7 whole, which is shorter than its diff:
```python
import functools

import jax
import jax.numpy as jnp
from jax import lax
from jax.experimental import pallas as pl
from jax.experimental.pallas import tpu as pltpu
from jax.sharding import PartitionSpec as P

F32 = jnp.float32
BF16 = jnp.bfloat16
HIGHEST = lax.Precision.HIGHEST
CLIP_RMS = 0.1
STEPS = 4
MIB = 1024 * 1024
NT = ((1,), (1,))


def split3(x):
    first = x.astype(BF16)
    rest = x - first.astype(F32)
    second = rest.astype(BF16)
    return first, second, (rest - second.astype(F32)).astype(BF16)


def tree_sum(values):
    values = list(values)
    while len(values) > 1:
        values = [values[i] + values[i + 1] for i in range(0, len(values), 2)]
    return values[0]


def dot(a, b, dims=((1,), (0,)), precision=None):
    return lax.dot_general(a, b, (dims, ((), ())), precision=precision, preferred_element_type=F32)


def fold(x, rows):
    return jnp.concatenate([x[i : i + rows] for i in range(0, x.shape[0], rows)], axis=1)


def unfold(x, rows):
    count = rows // x.shape[0]
    width = x.shape[1] // count
    return jnp.concatenate([x[:, i * width : (i + 1) * width] for i in range(count)], axis=0)


def mine_and_other(j, bit, position):
    mine = lax.bitwise_and(lax.shift_right_logical(lax.axis_index("dp"), bit), 1)
    base = ((j >> position) << (position + 1)) | (j & ((1 << position) - 1))
    return base + mine * (1 << position), base + (1 - mine) * (1 << position)


def split_bit(chunks, bit, position, keep, send):
    for j in range(keep.shape[0]):
        mine, other = mine_and_other(j, bit, position)
        keep[j] = chunks[mine]
        send[j] = chunks[other]


def split_replicas(total, stage, halves):
    n_dp, per, _ = stage.shape
    for c in range(n_dp):
        stage[c] = total[c * per : (c + 1) * per, :]
    start = 0
    for (bit, position), keep, send in halves:
        width = keep.shape[2]
        split_bit(stage.at[:, :, start : start + width], bit, position, keep, send)
        start += width


def join_replicas(halves, stage, total):
    n_dp, per, ff = stage.shape
    start = 0
    for (bit, position), mine, other in halves:
        width = ff // 2
        for j in range(n_dp // 2):
            here, there = mine_and_other(j, bit, position)
            stage[here, :, start : start + width] = mine[j, :, :width]
            stage[there, :, start : start + width] = other[j, :, :width]
        start += width
    for c in range(n_dp):
        total[c * per : (c + 1) * per, :] = stage[c]


def split_shards(total, extra, outs):
    me = lax.axis_index("tensor")
    rows, width = outs[0].shape[0], total.shape[1]
    for j, out in enumerate(outs):
        owner = lax.bitwise_xor(me, j)
        out[:, :width] = total[pl.ds(pl.multiple_of(owner * rows, rows), rows), :]
        if extra is not None:
            out[:, width:] = fold(extra, rows)


def join_shards(pieces, total):
    me = lax.axis_index("tensor")
    rows, width = pieces[0].shape[0], total.shape[1]
    for j, piece in enumerate(pieces):
        owner = lax.bitwise_xor(me, j)
        total[pl.ds(pl.multiple_of(owner * rows, rows), rows), :] = piece[:, :width]


def left_kernel(firsts, gu, eu, qu, gd, ed, qd, *refs):
    *outs, gu_in, eu_in, qu_in, pieces_up, total_up, gd_in, ed_in, qd_in, pieces_down, total_down, stage, q_sems, sems = refs
    step = pl.program_id(0)
    arrays = ((gu, gu_in), (eu, eu_in), (gd, gd_in), (ed, ed_in))

    def copy(i, n):
        src, dst = arrays[n]
        block = dst.shape[0] // STEPS
        rows = pl.ds(pl.multiple_of(i * block, block), block)
        return pltpu.make_async_copy(src.at[0, rows, :], dst.at[rows, :], sems.at[i, n])

    @pl.when(step == 0)
    def _():
        firsts_in = [pltpu.make_async_copy(src, dst, q_sems.at[i]) for i, (src, dst) in enumerate(((qu, qu_in), (qd, qd_in)))]
        for first in firsts_in:
            first.start()
        for i in range(STEPS):
            for n in range(4):
                copy(i, n).start()
        for first in firsts_in:
            first.wait()
        split_rows(qu_in, pieces_up)
        split_rows(qd_in, pieces_down)

    for n in range(4):
        copy(step, n).wait()
    for g, e, pieces, total in ((gu_in, eu_in, pieces_up, total_up), (gd_in, ed_in, pieces_down, total_down)):
        block = g.shape[0] // STEPS
        rows = pl.ds(pl.multiple_of(step * block, 128), block)
        total[:, rows] = add_pieces(dot(pieces[...], g[rows, :], NT) + dot(pieces[...], e[rows, :], NT))

    @pl.when(step == STEPS - 1)
    def _():
        split_shards(total_up, None, outs[:-4])
        split_replicas(total_down, stage, [(firsts[0], *outs[-4:-2]), (firsts[1], *outs[-2:])])


def halve_kernel(bit, position, keep, got, keep_out, send_out, chunks):
    chunks[...] = keep[...] + got[...]
    split_bit(chunks, bit, position, keep_out, send_out)


def halve_with_shards_kernel(bit, position, width, keep, got, *refs):
    *terms, gram, keep_out, send_out, chunks = refs
    half, per, columns = keep.shape
    summed = tree_sum(term[...] for term in terms)
    block = width // half
    for c in range(half):
        chunks[c, :, :columns] = keep[c] + got[c]
        chunks[c, :, columns:] = fold(summed[:, c * block : (c + 1) * block], per)
    split_bit(chunks, bit, position, keep_out, send_out)
    if summed.shape[1] > width:
        gram[...] = unfold(summed[:, width:], gram.shape[0])
    else:
        gram[...] = jnp.zeros_like(gram)


def mean_kernel(n_dp, keep, got, out):
    out[...] = (keep[...] + got[...]) / n_dp


def double_kernel(bit, position, mine, other, out):
    for j in range(mine.shape[0]):
        here, there = mine_and_other(j, bit, position)
        out[here] = mine[j]
        out[there] = other[j]


def shard_rows(mine, other, ff, rows):
    half = mine.shape[0]
    return jnp.concatenate([unfold(mine[c, :, ff:] + other[c, :, ff:], rows) for c in range(half)], axis=1)


def shard_rows_kernel(ff, mine, other, out):
    out[...] = shard_rows(mine, other, ff, out.shape[0])


def split_rows(left, pieces):
    rank = left.shape[0]
    for i, piece in enumerate(split3(left[...])):
        pieces[i * rank : (i + 1) * rank, :] = piece


def add_pieces(t):
    rank = t.shape[0] // 3
    return t[:rank] + (t[rank : 2 * rank] + t[2 * rank :])


def right_down_kernel(lasts, mine_a, other_a, mine_b, other_b, g, e, left, *refs):
    *outs, pieces, total, stage = refs
    join_replicas([(lasts[0], mine_a, other_a), (lasts[1], mine_b, other_b)], stage, left)
    split_rows(left, pieces)
    total[...] = add_pieces(dot(pieces[...], g[0]) + dot(pieces[...], e[0]))
    split_shards(total, dot(left[...], left[...], NT, HIGHEST), outs)


def right_up_kernel(firsts, n_shards, *refs):
    shards, refs = refs[:n_shards], refs[n_shards:]
    g, e, _, left, gram, keep_a, send_a, keep_b, send_b, pieces, total, stage = refs
    join_shards(shards, left)
    split_rows(left, pieces)
    block = total.shape[1] // STEPS
    for i in range(STEPS):
        part = slice(i * block, (i + 1) * block)
        total[:, part] = add_pieces(dot(pieces[...], g[0, :, part]) + dot(pieces[...], e[0, :, part]))
    split_replicas(total, stage, [(firsts[0], keep_a, send_a), (firsts[1], keep_b, send_b)])
    gram[...] = dot(left[...], left[...], NT, HIGHEST)


def inverse_factors(grams):
    rank = grams[0].shape[0]
    count = rank // 8
    panel = 4
    lane = lax.broadcasted_iota(jnp.int32, (8, 2 * rank), 1)
    row = lax.broadcasted_iota(jnp.int32, (8, 2 * rank), 0)
    states, pivots = [], []
    for gram in grams:
        wide = jnp.concatenate([gram, jnp.zeros_like(gram)], axis=1)
        states.append([wide[i : i + 8] + (lane == row + (rank + i)).astype(F32) for i in range(0, rank, 8)])
        pivots.append([])
    for start in range(0, rank, panel):
        at = start // 8
        below = range(at, count)
        spread = [
            [{i: jnp.broadcast_to(blocks[i][:, start + j : start + j + 1], (8, 2 * rank)) for i in below} for j in range(panel)]
            for blocks in states
        ]
        for j in range(panel):
            inner = (start + j) % 8
            for blocks, columns, found in zip(states, spread, pivots):
                pivot = columns[j][at][inner : inner + 1, :]
                found.append(pivot)
                inverse = 1.0 / pivot
                factor = {i: jnp.where(row > inner, columns[j][i], 0.0) if i == at else columns[j][i] for i in below}
                for later in columns[j + 1 :]:
                    head = later[at][inner : inner + 1, :] * inverse
                    for i in below:
                        later[i] = later[i] - factor[i] * head
                scaled = blocks[at][inner : inner + 1, :] * inverse
                for i in below:
                    blocks[i] = blocks[i] - factor[i] * scaled
    results = []
    for blocks, found in zip(states, pivots):
        rows = [block / jnp.sqrt(jnp.concatenate(found[8 * i : 8 * i + 8], axis=0)) for i, block in enumerate(blocks)]
        results.append(jnp.concatenate(rows, axis=0)[:, rank:])
    return results


def basis_kernel(left_up, left_down, gram_up, gram_down, *refs):
    inv_up, inv_down, lhs_up, lhs_down = refs[-4:]
    inverses = inverse_factors([gram_up[...], gram_down[...]])
    rank = left_up.shape[0]
    for inverse, inv, left, lhs in zip(inverses, (inv_up, inv_down), (left_up, left_down), (lhs_up, lhs_down)):
        inv[...] = inverse
        first, second, _ = split3(dot(inverse, left[...], precision=HIGHEST).T)
        lhs[:, :rank] = first
        lhs[:, rank : 2 * rank] = first
        lhs[:, 2 * rank : 3 * rank] = second
        lhs[:, 3 * rank :] = second


def right_factor(inv, total, rhs):
    rank = inv.shape[0]
    right = dot(inv[...], total[...], precision=HIGHEST)
    first, second, _ = split3(right)
    rhs[:rank, :] = first
    rhs[rank : 2 * rank, :] = second
    rhs[2 * rank : 3 * rank, :] = first
    rhs[3 * rank :, :] = second
    return jnp.sum(right * right)


def factor_up_kernel(lasts, mine_a, other_a, mine_b, other_b, inv, rhs, shard, total, stage):
    join_replicas([(lasts[0], mine_a, other_a), (lasts[1], mine_b, other_b)], stage, total)
    square = right_factor(inv, total, rhs)
    rows, ff = shard.shape[0], total.shape[1]
    width = shard.shape[1] - 128
    shard[:, :width] = shard_rows(mine_a, other_a, ff // 2, rows)
    shard[:, width:] = jnp.full((rows, 128), square, F32)


def factor_down_kernel(limit, n_shards, *refs):
    shards, refs = refs[:n_shards], refs[n_shards:]
    inv, _, rhs, clip, total = refs
    join_shards(shards, total)
    square = right_factor(inv, total, rhs)
    width = total.shape[1]
    norm_sq = square + tree_sum(shard[:8, width:] for shard in shards)
    clip[...] = jnp.minimum(jnp.float32(1.0), limit / jnp.sqrt(norm_sq))


def rows_of(block):
    return pl.ds(pl.multiple_of(pl.program_id(0) * block, block), block)


def error_up_kernel(g, e, lhs, rhs, error, made):
    made[...] = jnp.zeros_like(made)
    part = rows_of(error.shape[1])
    rebuilt = dot(lhs[part, :], rhs[...])
    error[0] = (g[0, part, :].astype(F32) + e[0, part, :].astype(F32) - rebuilt).astype(BF16)


def last_kernel(g, e, lhs_up, rhs_up, lhs_down, rhs_down, clip, error, update_up, update_down):
    factor = clip[:1, :1]
    part = rows_of(update_down.shape[0])
    rebuilt = dot(lhs_down[part, :], rhs_down[...])
    update_down[...] = (factor * rebuilt).astype(BF16)
    error[0] = (g[0, part, :].astype(F32) + e[0, part, :].astype(F32) - rebuilt).astype(BF16)
    part = rows_of(update_up.shape[0])
    update_up[...] = (factor * dot(lhs_up[part, :], rhs_up[...])).astype(BF16)


def shaped(*dims, dtype=F32):
    return jax.ShapeDtypeStruct(dims, dtype)


def whole(shape):
    return pl.BlockSpec(shape, lambda *_: (0,) * len(shape))


def row_blocks(rows, columns):
    return pl.BlockSpec((rows // STEPS, columns), lambda i: (i, 0))


def replica_blocks(rows, columns):
    return pl.BlockSpec((1, rows // STEPS, columns), lambda i: (0, i, 0))


VMEM = pl.BlockSpec(memory_space=pltpu.VMEM)
ANY = pl.BlockSpec(memory_space=pl.ANY)


def call(kernel, out_shape, *args, flops=0, limit=12, name=None, **more):
    arrays = list(args) + jax.tree.leaves(out_shape)
    size = sum(a.size * a.dtype.itemsize for a in arrays)
    cost = pl.CostEstimate(flops=flops, bytes_accessed=size, transcendentals=0)
    params = pltpu.CompilerParams(vmem_limit_bytes=limit * MIB)
    return pl.pallas_call(kernel, out_shape=out_shape, compiler_params=params, cost_estimate=cost, name=name, **more)(*args)


def swap(x, axis, distance):
    pairs = [(i, i ^ distance) for i in range(lax.axis_size(axis))]
    return lax.ppermute(x, axis, pairs)


def exchange_orders(n_dp):
    bits = n_dp.bit_length() - 1
    return [(b, 0) for b in range(bits)], [(b, 1) for b in range(1, bits)] + [(0, 0)]


def scatter_mean(order, keep, send, shards=(), width=0, rank=0):
    n_dp = lax.axis_size("dp")
    gram = None
    for i, (bit, _) in enumerate(order):
        got = swap(send, "dp", 1 << bit)
        if i == len(order) - 1:
            return call(functools.partial(mean_kernel, n_dp), shaped(*keep.shape), keep, got, name="replica_mean"), gram
        count, per, columns = keep.shape
        if shards and i == 0:
            columns += shards[0].shape[0] // per * (width // count)
            out = shaped(count // 2, per, columns)
            gram, keep, send = call(
                functools.partial(halve_with_shards_kernel, *order[i + 1], width), [shaped(rank, rank), out, out], keep, got, *shards,
                name="halve_with_shards", scratch_shapes=[pltpu.VMEM((count, per, columns), F32)],
            )
        else:
            out = shaped(count // 2, per, columns)
            keep, send = call(
                functools.partial(halve_kernel, *order[i + 1]), [out, out], keep, got, name="halve",
                scratch_shapes=[pltpu.VMEM(keep.shape, F32)],
            )


def gather_chunks(order, mine):
    for bit, position in order[:0:-1]:
        other = swap(mine, "dp", 1 << bit)
        out = shaped(2 * mine.shape[0], *mine.shape[1:])
        mine = call(functools.partial(double_kernel, bit, position), out, mine, other, name="double")
    return mine, swap(mine, "dp", 1 << order[0][0])


def from_shards(parts):
    n_shards = lax.axis_size("tensor")
    parts = parts if isinstance(parts, (list, tuple)) else [parts] * n_shards
    return [parts[0]] + [swap(parts[j], "tensor", j) for j in range(1, n_shards)]


def on_device(gu, eu, gd, ed, qu, qd):
    qu, qd = qu.T, qd.T
    n_dp, n_shards = lax.axis_size("dp"), lax.axis_size("tensor")
    _, rows, ff = gu.shape
    rank = qu.shape[0]
    half, per, rows_here = n_dp // 2, rank // n_dp, rank // n_shards
    order_a, order_b = exchange_orders(n_dp)
    firsts = order_a[0], order_b[0]
    halves = [shaped(half, per, ff // 2)] * 4
    stage = pltpu.VMEM((n_dp, per, ff), F32)
    wide = pltpu.VMEM((rank, ff), F32)
    narrow = pltpu.VMEM((rank, rows), F32)
    product = 4 * rows * ff * 4 * rank

    buffers = [
        [pltpu.VMEM(g.shape[1:], BF16)] * 2 + [pltpu.VMEM(q.shape, F32), pltpu.VMEM((3 * rank, q.shape[1]), BF16), total]
        for g, q, total in ((gu, qu, narrow), (gd, qd, wide))
    ]
    outs = [shaped(rows_here, rows)] * n_shards + halves
    *parts, keep_a, send_a, keep_b, send_b = call(
        functools.partial(left_kernel, firsts), outs, gu, eu, qu, gd, ed, qd, name="left", flops=2 * product, limit=61,
        grid=(STEPS,), in_specs=[pl.BlockSpec(memory_space=pltpu.HBM)] * 6, out_specs=[whole(out.shape) for out in outs],
        scratch_shapes=buffers[0] + buffers[1] + [stage, pltpu.SemaphoreType.DMA((2,)), pltpu.SemaphoreType.DMA((STEPS, 4))],
    )
    mean_a, _ = scatter_mean(order_a, keep_a, send_a, from_shards(parts), rows, rank)
    mean_b, _ = scatter_mean(order_b, keep_b, send_b)
    mine_a, other_a = gather_chunks(order_a, mean_a)
    mine_b, other_b = gather_chunks(order_b, mean_b)

    shard = call(functools.partial(shard_rows_kernel, ff // 2), shaped(rows_here, rows), mine_a, other_a, name="shard_rows")
    left_rows = from_shards(shard)
    out = shaped(rows_here, rows + rank * n_shards)
    left_down, *parts = call(
        functools.partial(right_down_kernel, firsts), [shaped(rank, ff)] + [out] * n_shards, mine_a, other_a, mine_b, other_b, gd, ed,
        name="right_down", flops=product, scratch_shapes=[pltpu.VMEM((3 * rank, ff), BF16), narrow, stage],
    )
    left_up, gram_up, keep_a, send_a, keep_b, send_b = call(
        functools.partial(right_up_kernel, firsts, n_shards), [shaped(rank, rows), shaped(rank, rank)] + halves,
        *left_rows, gu, eu, left_down, name="right_up", flops=product, in_specs=[VMEM] * (n_shards + 2) + [ANY],
        scratch_shapes=[pltpu.VMEM((3 * rank, rows), BF16), wide, stage],
    )
    mean_a, gram_down = scatter_mean(order_a, keep_a, send_a, from_shards(parts), rows, rank)
    mean_b, _ = scatter_mean(order_b, keep_b, send_b)
    mine_a, other_a = gather_chunks(order_a, mean_a)
    mine_b, other_b = gather_chunks(order_b, mean_b)
    inv_up, inv_down, lhs_up, lhs_down = call(
        basis_kernel,
        [shaped(rank, rank)] * 2 + [shaped(rows, 4 * rank, dtype=BF16), shaped(ff, 4 * rank, dtype=BF16)],
        left_up, left_down, gram_up, gram_down, gu, eu, gd, ed, mine_a, name="basis", in_specs=[VMEM] * 8 + [ANY],
    )
    rhs_up, shard = call(
        functools.partial(factor_up_kernel, firsts), [shaped(4 * rank, ff, dtype=BF16), shaped(rows_here, rows + 128)],
        mine_a, other_a, mine_b, other_b, inv_up, name="factor_up", scratch_shapes=[wide, stage],
    )
    right_rows = from_shards(shard)
    new_error_up, made = call(
        error_up_kernel, [shaped(1, rows, ff, dtype=BF16), shaped(8, 128)], gu, eu, lhs_up, rhs_up, name="error_up", flops=product // 2,
        grid=(STEPS,), in_specs=[VMEM] * 4, out_specs=[replica_blocks(rows, ff), whole((8, 128))],
    )
    limit = CLIP_RMS * (2.0 * rows * ff * n_shards) ** 0.5
    rhs_down, clip = call(
        functools.partial(factor_down_kernel, limit, n_shards), [shaped(4 * rank, rows, dtype=BF16), shaped(8, 128)],
        *right_rows, inv_down, made, name="factor_down", in_specs=[VMEM] * (n_shards + 1) + [ANY], scratch_shapes=[narrow],
    )
    new_error_down, update_up, update_down = call(
        last_kernel, [shaped(1, ff, rows, dtype=BF16), shaped(rows, ff, dtype=BF16), shaped(ff, rows, dtype=BF16)],
        gd, ed, lhs_up, rhs_up, lhs_down, rhs_down, clip, name="last", flops=product, grid=(STEPS,),
        in_specs=[VMEM] * 7, out_specs=[replica_blocks(ff, rows), row_blocks(rows, ff), row_blocks(ff, rows)],
    )
    return new_error_up, update_up, new_error_down, update_down


def solution(mesh):
    placed = (
        P("dp", None, "tensor"),
        P("dp", None, "tensor"),
        P("dp", "tensor", None),
        P("dp", "tensor", None),
        P("tensor", None),
        P(),
    )
    return jax.shard_map(
        on_device,
        mesh=mesh,
        in_specs=placed,
        out_specs=(
            P("dp", None, "tensor"),
            P(None, "tensor"),
            P("dp", "tensor", None),
            P("tensor", None),
        ),
        check_vma=False,
    )
```

time: 88.5 us -> 95.9 us (1.084)
  starting transfers between devices: 29 us -> 41.2 us
  waiting for transfers between devices: 35.8 us -> 31.2 us
  Pallas kernels: 20.9 us -> 19.9 us
    ppermute x24 -> x36, starting transfers between devices: 29 us -> 41.2 us  [swap(): return lax.ppermute(x, axis, pairs)]
    ppermute x24 -> x36, waiting for transfers between devices: 35.8 us -> 31.2 us  [swap(): return lax.ppermute(x, axis, pairs)]
    pallas_call x19 -> x29, Pallas kernels: 20.9 us -> 19.9 us  [call(): pl.pallas_call(kernel, out_shape=out_shape, compiler_params=params, cost_...]
    unnamed x12 -> x14, local copies, waits for them, and re-layouts: 1.79 us -> 2.56 us
  transfers between devices with their start and end apart: 24 -> 36, of which waited for: 20 -> 23; matrix products, arithmetic and copies ran while one was open for 0% -> 0% of each run, Pallas kernels for 8% -> 8%
where the time goes in v7:
time: 95.9 us; the launch traced here: 95.7 us
  starting transfers between devices  41.2 us (43%)
  waiting for transfers between devices  31.2 us (33%)
  Pallas kernels  19.9 us (21%)
  local copies, waits for them, and re-layouts  2.56 us (3%)
    ppermute x36, starting transfers between devices, swap(): return lax.ppermute(x, axis, pairs)  41.2 us
    ppermute x36, waiting for transfers between devices, swap(): return lax.ppermute(x, axis, pairs)  31.2 us
    pallas_call x29, Pallas kernels, call(): pl.pallas_call(kernel, out_shape=out_shape, compiler_params=params, cost_...  19.9 us
    unnamed x14, local copies, waits for them, and re-layouts  2.56 us
  transfers between devices with their start and end apart: 36, of which 23 were waited for; matrix products, arithmetic and copies ran while one was open for 0% of the time, Pallas kernels for 8%

profile of v7, /device:TPU:0, one launch (start us, length us, event | category | flops | bytes accessed | tf_op | source)
XLA Modules:
  0.0 95.7 jit_solution(495187517208886401)
XLA Ops:
  0.6 7.0 %left.1 = (f32[16,512]{1,0:T(8,128)}, f32[16,512]{1,0:T(8,128)}, f32[16,512]{1,0:T(8,128)}, f32[16,512]{1,0:T(8,128)}, f32[4,8,768]{2,1,0:T(8,128)}, /*index=5*/...) custom-call(bf16[1,512,1536]{2,1,0:T(8,128)(2,1)} %g.4, bf16[1,512,1536]{2,1,0:T(8,128)(2,1)} %e.4, ...), custom_call_target="tpu_custom_call" | custom-call | flops 1610612736 | bytes 7340032 | tf_op jit(solution)/shard_map/left/pallas_call | solution.py:340
  7.7 3.0 %collective-permute-start = (f32[4,8,768]{2,1,0:T(8,128)}, f32[4,8,768]{2,1,0:T(8,128)S(1)}, u32[]{:S(2)}, u32[]{:S(2)}) collective-permute-start(f32[4,8,768]{2,1,0:T(8,128)} %get-tuple-element.54), channel_id=1, source_target_pairs={{0,4},{4,0},{8,12},{12,8},{16,20},{20,16},{24,28},{28,24},{1,5},{5... | collective-permute-start | bytes 294920 | tf_op jit(solution)/shard_map/ppermute | solution.py:345
  10.7 1.5 %collective-permute-start.2 = (f32[16,512]{1,0:T(8,128)}, f32[16,512]{1,0:T(8,128)S(1)}, u32[]{:S(2)}, u32[]{:S(2)}) collective-permute-start(f32[16,512]{1,0:T(8,128)} %get-tuple-element.57), channel_id=1, source_target_pairs={{0,2},{1,3},{2,0},{3,1},{4,6},{5,7},{6,4},{7,5},{8,10},{9,11},{10,... | collective-permute-start | bytes 98312 | tf_op jit(solution)/shard_map/ppermute | solution.py:345
  12.2 0.4 collective-permute-start.3
  12.6 1.6 %collective-permute-start.12 = (f32[4,8,768]{2,1,0:T(8,128)}, f32[4,8,768]{2,1,0:T(8,128)S(1)}, u32[]{:S(2)}, u32[]{:S(2)}) collective-permute-start(f32[4,8,768]{2,1,0:T(8,128)} %get-tuple-element.64), channel_id=1, source_target_pairs={{0,8},{4,12},{8,0},{12,4},{16,24},{20,28},{24,16},{28,20},{1,9},{5... | collective-permute-start | bytes 294920 | tf_op jit(solution)/shard_map/ppermute | solution.py:345
  14.2 0.7 collective-permute-done.2.refs_2_
  14.9 0.9 collective-permute-done.3.refs_3_
  15.8 0.9 copy-done.5
  16.7 0.8 copy-done.6
  17.4 0.6 halve_with_shards.2
  18.1 1.6 %collective-permute-start.4 = (f32[2,8,1024]{2,1,0:T(8,128)S(1)}, f32[2,8,1024]{2,1,0:T(8,128)S(1)}, u32[]{:S(2)}, u32[]{:S(2)}) collective-permute-start(f32[2,8,1024]{2,1,0:T(8,128)S(1)} %get-tuple-element.60), channel_id=1, source_target_pairs={{0,8},{4,12},{8,0},{12,4},{16,24},{20,28},{24,16},{28,20},{1,9},{5... | collective-permute-start | bytes 196616 | tf_op jit(solution)/shard_map/ppermute | solution.py:345
  19.6 2.7 %collective-permute-done.4.got = f32[2,8,1024]{2,1,0:T(8,128)S(1)} collective-permute-done((f32[2,8,1024]{2,1,0:T(8,128)S(1)}, f32[2,8,1024]{2,1,0:T(8,128)S(1)}, u32[]{:S(2)}, u32[]{:S(2)}) %collective-permute-start.4) | collective-permute-done | bytes 65568 | tf_op jit(solution)/shard_map/ppermute | solution.py:345
  22.3 2.7 %collective-permute-start.5 = (f32[1,8,1024]{2,1,0:T(8,128)S(1)}, f32[1,8,1024]{2,1,0:T(8,128)S(1)}, u32[]{:S(2)}, u32[]{:S(2)}) collective-permute-start(f32[1,8,1024]{2,1,0:T(8,128)S(1)} %get-tuple-element.62), channel_id=1, source_target_pairs={{0,16},{4,20},{8,24},{12,28},{16,0},{20,4},{24,8},{28,12},{1,17},{... | collective-permute-start | bytes 98312 | tf_op jit(solution)/shard_map/ppermute | solution.py:345
  25.0 0.9 copy-done.4
  25.9 0.4 collective-permute-start.13
  26.3 0.9 collective-permute-done.5.got
  27.2 2.6 %collective-permute-start.6 = (f32[1,8,1024]{2,1,0:T(8,128)S(1)}, f32[1,8,1024]{2,1,0:T(8,128)S(1)}, u32[]{:S(2)}, u32[]{:S(2)}) collective-permute-start(f32[1,8,1024]{2,1,0:T(8,128)S(1)} %replica_mean.4.mine), channel_id=1, source_target_pairs={{0,16},{4,20},{8,24},{12,28},{16,0},{20,4},{24,8},{28,12},{1,17},{... | collective-permute-start | bytes 98312 | tf_op jit(solution)/shard_map/ppermute | solution.py:345
  29.8 1.1 %collective-permute-done.13.got = f32[2,8,768]{2,1,0:T(8,128)S(1)} collective-permute-done((f32[2,8,768]{2,1,0:T(8,128)S(1)}, f32[2,8,768]{2,1,0:T(8,128)S(1)}, u32[]{:S(2)}, u32[]{:S(2)}) %collective-permute-start.13) | collective-permute-done | bytes 49184 | tf_op jit(solution)/shard_map/ppermute | solution.py:345
  31.0 0.7 collective-permute-start.14
  31.7 0.8 collective-permute-done.6.other
  32.5 1.3 %collective-permute-start.7 = (f32[2,8,1024]{2,1,0:T(8,128)S(1)}, f32[2,8,1024]{2,1,0:T(8,128)S(1)}, u32[]{:S(2)}, u32[]{:S(2)}) collective-permute-start(f32[2,8,1024]{2,1,0:T(8,128)S(1)} %double.8.mine), channel_id=1, source_target_pairs={{0,8},{4,12},{8,0},{12,4},{16,24},{20,28},{24,16},{28,20},{1,9},{5... | collective-permute-start | bytes 196616 | tf_op jit(solution)/shard_map/ppermute | solution.py:345
  33.8 1.1 %collective-permute-done.14.got = f32[1,8,768]{2,1,0:T(8,128)S(1)} collective-permute-done((f32[1,8,768]{2,1,0:T(8,128)S(1)}, f32[1,8,768]{2,1,0:T(8,128)S(1)}, u32[]{:S(2)}, u32[]{:S(2)}) %collective-permute-start.14) | collective-permute-done | bytes 24608 | tf_op jit(solution)/shard_map/ppermute | solution.py:345
  34.9 0.6 collective-permute-start.15
  35.5 3.2 %collective-permute-done.15.other = f32[1,8,768]{2,1,0:T(8,128)S(1)} collective-permute-done((f32[1,8,768]{2,1,0:T(8,128)S(1)}, f32[1,8,768]{2,1,0:T(8,128)S(1)}, u32[]{:S(2)}, u32[]{:S(2)}) %collective-permute-start.15) | collective-permute-done | bytes 24608 | tf_op jit(solution)/shard_map/ppermute | solution.py:345
  38.7 2.3 %collective-permute-start.16 = (f32[2,8,768]{2,1,0:T(8,128)S(1)}, f32[2,8,768]{2,1,0:T(8,128)S(1)}, u32[]{:S(2)}, u32[]{:S(2)}) collective-permute-start(f32[2,8,768]{2,1,0:T(8,128)S(1)} %double.10.mine), channel_id=1, source_target_pairs={{0,16},{4,20},{8,24},{12,28},{16,0},{20,4},{24,8},{28,12},{1,17},{... | collective-permute-start | bytes 147464 | tf_op jit(solution)/shard_map/ppermute | solution.py:345
  41.0 0.7 collective-permute-start.8
  41.7 2.0 %collective-permute-done.16.other = f32[2,8,768]{2,1,0:T(8,128)S(1)} collective-permute-done((f32[2,8,768]{2,1,0:T(8,128)S(1)}, f32[2,8,768]{2,1,0:T(8,128)S(1)}, u32[]{:S(2)}, u32[]{:S(2)}) %collective-permute-start.16) | collective-permute-done | bytes 49184 | tf_op jit(solution)/shard_map/ppermute | solution.py:345
  43.7 1.9 %collective-permute-start.17 = (f32[4,8,768]{2,1,0:T(8,128)S(1)}, f32[4,8,768]{2,1,0:T(8,128)S(1)}, u32[]{:S(2)}, u32[]{:S(2)}) collective-permute-start(f32[4,8,768]{2,1,0:T(8,128)S(1)} %double.11.mine_b), channel_id=1, source_target_pairs={{0,8},{4,12},{8,0},{12,4},{16,24},{20,28},{24,16},{28,20},{1,9},{5... | collective-permute-start | bytes 294920 | tf_op jit(solution)/shard_map/ppermute | solution.py:345
  45.6 0.5 collective-permute-done.8.other.other_a
  46.1 0.9 collective-permute-start.10
  47.1 0.9 collective-permute-start.9
  48.0 0.4 collective-permute-done.17.other_b
  48.4 1.2 %right_down.1 = (f32[64,1536]{1,0:T(8,128)S(1)}, f32[16,768]{1,0:T(8,128)S(1)}, f32[16,768]{1,0:T(8,128)S(1)}, f32[16,768]{1,0:T(8,128)S(1)}, f32[16,768]{1,0:T(8,128)S(1)}) custom-call(f32[4,8,1024]{2,1,0:T(8,128)S(1)} %double.9.mine.mine_a, f32[4,8,1024]{2,1,0:T(8,128)S(1)} %collective-permute-done.8.other.other_a, f32[4,8,768]{2,1,0:T(8,128)S(1)} %double.11.mine_b, ...), custom_call_target="tpu_custom_call" | custom-call | flops 805306368 | bytes 4194304 | tf_op jit(solution)/shard_map/right_down/pallas_call | solution.py:340
  49.6 0.8 collective-permute-done.10.refs_2_
  50.4 1.2 %right_up.1 = (f32[64,512]{1,0:T(8,128)S(1)}, f32[64,64]{1,0:T(8,128)S(1)}, f32[4,8,768]{2,1,0:T(8,128)S(1)}, f32[4,8,768]{2,1,0:T(8,128)S(1)}, f32[4,8,768]{2,1,0:T(8,128)S(1)}, /*index=5*/f32[4,8,768]{2,1,0:T(8,128)S(1)}) custom-call(f32[16,512]{1,0:T(8,128)S(1)} %shard_rows.1.refs_0_, f32[16,512]{1,0:T(8,128)S(1)} %collective-permute-done.9.refs_1_, ...), custom_call_target="tpu_custom_call" | custom-call | flops 805306368 | bytes 4210688 | tf_op jit(solution)/shard_map/right_up/pallas_call | solution.py:340
  51.6 0.5 collective-permute-start.18
  52.1 0.6 collective-permute-start.20
  52.7 1.3 %collective-permute-start.21 = (f32[16,768]{1,0:T(8,128)S(1)}, f32[16,768]{1,0:T(8,128)S(1)}, u32[]{:S(2)}, u32[]{:S(2)}) collective-permute-start(f32[16,768]{1,0:T(8,128)S(1)} %get-tuple-element.77), channel_id=1, source_target_pairs={{0,3},{1,2},{2,1},{3,0},{4,7},{5,6},{6,5},{7,4},{8,11},{9,10},{10,... | collective-permute-start | bytes 147464 | tf_op jit(solution)/shard_map/ppermute | solution.py:345
  53.9 1.1 %collective-permute-start.27 = (f32[4,8,768]{2,1,0:T(8,128)S(1)}, f32[4,8,768]{2,1,0:T(8,128)S(1)}, u32[]{:S(2)}, u32[]{:S(2)}) collective-permute-start(f32[4,8,768]{2,1,0:T(8,128)S(1)} %get-tuple-element.85), channel_id=1, source_target_pairs={{0,8},{4,12},{8,0},{12,4},{16,24},{20,28},{24,16},{28,20},{1,9},{5... | collective-permute-start | bytes 294920 | tf_op jit(solution)/shard_map/ppermute | solution.py:345
  55.0 1.6 %collective-permute-done.20.refs_2_ = f32[16,768]{1,0:T(8,128)S(1)} collective-permute-done((f32[16,768]{1,0:T(8,128)S(1)}, f32[16,768]{1,0:T(8,128)S(1)}, u32[]{:S(2)}, u32[]{:S(2)}) %collective-permute-start.20) | collective-permute-done | bytes 49184 | tf_op jit(solution)/shard_map/ppermute | solution.py:345
  57.0 1.3 %collective-permute-start.22 = (f32[2,8,1024]{2,1,0:T(8,128)S(1)}, f32[2,8,1024]{2,1,0:T(8,128)S(1)}, u32[]{:S(2)}, u32[]{:S(2)}) collective-permute-start(f32[2,8,1024]{2,1,0:T(8,128)S(1)} %get-tuple-element.80), channel_id=1, source_target_pairs={{0,8},{4,12},{8,0},{12,4},{16,24},{20,28},{24,16},{28,20},{1,9},{5... | collective-permute-start | bytes 196616 | tf_op jit(solution)/shard_map/ppermute | solution.py:345
  58.3 3.0 %collective-permute-done.22.got = f32[2,8,1024]{2,1,0:T(8,128)S(1)} collective-permute-done((f32[2,8,1024]{2,1,0:T(8,128)S(1)}, f32[2,8,1024]{2,1,0:T(8,128)S(1)}, u32[]{:S(2)}, u32[]{:S(2)}) %collective-permute-start.22) | collective-permute-done | bytes 65568 | tf_op jit(solution)/shard_map/ppermute | solution.py:345
  61.3 1.8 %collective-permute-start.23 = (f32[1,8,1024]{2,1,0:T(8,128)S(1)}, f32[1,8,1024]{2,1,0:T(8,128)S(1)}, u32[]{:S(2)}, u32[]{:S(2)}) collective-permute-start(f32[1,8,1024]{2,1,0:T(8,128)S(1)} %get-tuple-element.82), channel_id=1, source_target_pairs={{0,16},{4,20},{8,24},{12,28},{16,0},{20,4},{24,8},{28,12},{1,17},{... | collective-permute-start | bytes 98312 | tf_op jit(solution)/shard_map/ppermute | solution.py:345
  63.1 1.3 %collective-permute-start.28 = (f32[2,8,768]{2,1,0:T(8,128)S(1)}, f32[2,8,768]{2,1,0:T(8,128)S(1)}, u32[]{:S(2)}, u32[]{:S(2)}) collective-permute-start(f32[2,8,768]{2,1,0:T(8,128)S(1)} %get-tuple-element.87), channel_id=1, source_target_pairs={{0,16},{4,20},{8,24},{12,28},{16,0},{20,4},{24,8},{28,12},{1,17},{... | collective-permute-start | bytes 147464 | tf_op jit(solution)/shard_map/ppermute | solution.py:345
  64.4 2.8 %collective-permute-done.23.got = f32[1,8,1024]{2,1,0:T(8,128)S(1)} collective-permute-done((f32[1,8,1024]{2,1,0:T(8,128)S(1)}, f32[1,8,1024]{2,1,0:T(8,128)S(1)}, u32[]{:S(2)}, u32[]{:S(2)}) %collective-permute-start.23) | collective-permute-done | bytes 32800 | tf_op jit(solution)/shard_map/ppermute | solution.py:345
  67.2 0.7 collective-permute-start.24
  67.9 1.4 %collective-permute-done.28.got = f32[2,8,768]{2,1,0:T(8,128)S(1)} collective-permute-done((f32[2,8,768]{2,1,0:T(8,128)S(1)}, f32[2,8,768]{2,1,0:T(8,128)S(1)}, u32[]{:S(2)}, u32[]{:S(2)}) %collective-permute-start.28) | collective-permute-done | bytes 49184 | tf_op jit(solution)/shard_map/ppermute | solution.py:345
  69.4 1.6 %collective-permute-start.29 = (f32[1,8,768]{2,1,0:T(8,128)S(1)}, f32[1,8,768]{2,1,0:T(8,128)S(1)}, u32[]{:S(2)}, u32[]{:S(2)}) collective-permute-start(f32[1,8,768]{2,1,0:T(8,128)S(1)} %get-tuple-element.89), channel_id=1, source_target_pairs={{0,4},{4,0},{8,12},{12,8},{16,20},{20,16},{24,28},{28,24},{1,5},{5... | collective-permute-start | bytes 73736 | tf_op jit(solution)/shard_map/ppermute | solution.py:345
  71.0 1.1 %collective-permute-done.24.other = f32[1,8,1024]{2,1,0:T(8,128)S(1)} collective-permute-done((f32[1,8,1024]{2,1,0:T(8,128)S(1)}, f32[1,8,1024]{2,1,0:T(8,128)S(1)}, u32[]{:S(2)}, u32[]{:S(2)}) %collective-permute-start.24) | collective-permute-done | bytes 32800 | tf_op jit(solution)/shard_map/ppermute | solution.py:345
  72.4 0.9 collective-permute-done.29.got
  73.3 1.6 %collective-permute-start.30 = (f32[1,8,768]{2,1,0:T(8,128)S(1)}, f32[1,8,768]{2,1,0:T(8,128)S(1)}, u32[]{:S(2)}, u32[]{:S(2)}) collective-permute-start(f32[1,8,768]{2,1,0:T(8,128)S(1)} %replica_mean.7.mine), channel_id=1, source_target_pairs={{0,4},{4,0},{8,12},{12,8},{16,20},{20,16},{24,28},{28,24},{1,5},{5... | collective-permute-start | bytes 73736 | tf_op jit(solution)/shard_map/ppermute | solution.py:345
  74.8 2.4 %collective-permute-done.30.other = f32[1,8,768]{2,1,0:T(8,128)S(1)} collective-permute-done((f32[1,8,768]{2,1,0:T(8,128)S(1)}, f32[1,8,768]{2,1,0:T(8,128)S(1)}, u32[]{:S(2)}, u32[]{:S(2)}) %collective-permute-start.30) | collective-permute-done | bytes 24608 | tf_op jit(solution)/shard_map/ppermute | solution.py:345
  77.2 1.5 %collective-permute-start.31 = (f32[2,8,768]{2,1,0:T(8,128)S(1)}, f32[2,8,768]{2,1,0:T(8,128)S(1)}, u32[]{:S(2)}, u32[]{:S(2)}) collective-permute-start(f32[2,8,768]{2,1,0:T(8,128)S(1)} %double.14.mine), channel_id=1, source_target_pairs={{0,16},{4,20},{8,24},{12,28},{16,0},{20,4},{24,8},{28,12},{1,17},{... | collective-permute-start | bytes 147464 | tf_op jit(solution)/shard_map/ppermute | solution.py:345
  78.8 1.5 %collective-permute-start.26 = (f32[4,8,1024]{2,1,0:T(8,128)S(1)}, f32[4,8,1024]{2,1,0:T(8,128)S(1)}, u32[]{:S(2)}, u32[]{:S(2)}) collective-permute-start(f32[4,8,1024]{2,1,0:T(8,128)S(1)} %double.13.refs_4_.mine_a), channel_id=1, source_target_pairs={{0,4},{4,0},{8,12},{12,8},{16,20},{20,16},{24,28},{28,24},{1,5},{5... | collective-permute-start | bytes 393224 | tf_op jit(solution)/shard_map/ppermute | solution.py:345
  80.3 1.9 %collective-permute-done.31.other = f32[2,8,768]{2,1,0:T(8,128)S(1)} collective-permute-done((f32[2,8,768]{2,1,0:T(8,128)S(1)}, f32[2,8,768]{2,1,0:T(8,128)S(1)}, u32[]{:S(2)}, u32[]{:S(2)}) %collective-permute-start.31) | collective-permute-done | bytes 49184 | tf_op jit(solution)/shard_map/ppermute | solution.py:345
  82.3 1.1 %collective-permute-start.32 = (f32[4,8,768]{2,1,0:T(8,128)S(1)}, f32[4,8,768]{2,1,0:T(8,128)S(1)}, u32[]{:S(2)}, u32[]{:S(2)}) collective-permute-start(f32[4,8,768]{2,1,0:T(8,128)S(1)} %double.15.mine_b), channel_id=1, source_target_pairs={{0,8},{4,12},{8,0},{12,4},{16,24},{20,28},{24,16},{28,20},{1,9},{5... | collective-permute-start | bytes 294920 | tf_op jit(solution)/shard_map/ppermute | solution.py:345
  83.4 3.2 %basis.1 = (f32[64,64]{1,0:T(8,128)S(1)}, f32[64,64]{1,0:T(8,128)S(1)}, bf16[512,256]{1,0:T(8,128)(2,1)S(1)}, bf16[1536,256]{1,0:T(8,128)(2,1)S(1)}) custom-call(f32[64,512]{1,0:T(8,128)S(1)} %get-tuple-element.70.left_up, f32[64,1536]{1,0:T(8,128)S(1)} %get-tuple-element.69.refs_6_.left_down, f32[64,64]{1,0:T(8,128)S(1)} %get-tuple-element.71.gram_up, ...), custom_call_target="tpu_custom_call" | custom-call | bytes 8060928 | tf_op jit(solution)/shard_map/basis/pallas_call | solution.py:340
  86.6 0.4 collective-permute-done.32.other_b
  87.0 0.7 factor_up.1
  87.7 1.0 %collective-permute-start.34 = (f32[16,640]{1,0:T(8,128)S(1)}, f32[16,640]{1,0:T(8,128)S(1)}, u32[]{:S(2)}, u32[]{:S(2)}) collective-permute-start(f32[16,640]{1,0:T(8,128)S(1)} %get-tuple-element.94.refs_0_), channel_id=1, source_target_pairs={{0,2},{1,3},{2,0},{3,1},{4,6},{5,7},{6,4},{7,5},{8,10},{9,11},{10,... | collective-permute-start | bytes 122888 | tf_op jit(solution)/shard_map/ppermute | solution.py:345
  88.7 0.9 collective-permute-start.33
  89.6 2.3 %error_up.1 = (bf16[1,512,1536]{2,1,0:T(8,128)(2,1)}, f32[8,128]{1,0:T(8,128)S(1)}) custom-call(bf16[1,512,1536]{2,1,0:T(8,128)(2,1)S(1)} %copy-done, bf16[1,512,1536]{2,1,0:T(8,128)(2,1)S(1)} %copy-done.1, bf16[512,256]{1,0:T(8,128)(2,1)S(1)} %get-tuple-element.83.lhs.lhs_up, bf16[256,1536]{1,0:T(8,128)(2,1)S(1)} %get-tuple-element.91.rhs.rhs_up), custom_call_target="tpu_custom_call" | custom-call | flops 402653184 | bytes 5771264 | tf_op jit(solution)/shard_map/error_up/pallas_call | solution.py:340
  92.2 0.4 factor_down.1
  92.6 3.0 %last.1 = (bf16[1,1536,512]{2,1,0:T(8,128)(2,1)}, bf16[512,1536]{1,0:T(8,128)(2,1)}, bf16[1536,512]{1,0:T(8,128)(2,1)}) custom-call(bf16[1,1536,512]{2,1,0:T(8,128)(2,1)S(1)} %copy-done.2, bf16[1,1536,512]{2,1,0:T(8,128)(2,1)S(1)} %copy-done.3, bf16[512,256]{1,0:T(8,128)(2,1)S(1)} %get-tuple-element.83.lhs.lhs_up, ...), custom_call_target="tpu_custom_call" | custom-call | flops 805306368 | bytes 9965568 | tf_op jit(solution)/shard_map/last/pallas_call | solution.py:340
  (51 shorter events, 1.4 us)
Async XLA Ops:
  0.6 47.8 %copy-start.3 = (bf16[1,1536,512]{2,1,0:T(8,128)(2,1)S(1)}, bf16[1,1536,512]{2,1,0:T(8,128)(2,1)}, u32[]{:S(2)}) copy-start(bf16[1,1536,512]{2,1,0:T(8,128)(2,1)} %e.5) | copy-start | bytes 4718596
  7.7 40.7 %copy-start.2 = (bf16[1,1536,512]{2,1,0:T(8,128)(2,1)S(1)}, bf16[1,1536,512]{2,1,0:T(8,128)(2,1)}, u32[]{:S(2)}) copy-start(bf16[1,1536,512]{2,1,0:T(8,128)(2,1)} %g.5) | copy-start | bytes 4718596
  7.7 8.1 %collective-permute-start = (f32[4,8,768]{2,1,0:T(8,128)}, f32[4,8,768]{2,1,0:T(8,128)S(1)}, u32[]{:S(2)}, u32[]{:S(2)}) collective-permute-start(f32[4,8,768]{2,1,0:T(8,128)} %get-tuple-element.54), channel_id=1, source_target_pairs={{0,4},{4,0},{8,12},{12,8},{16,20},{20,16},{24,28},{28,24},{1,5},{5... | collective-permute-start | bytes 294920 | tf_op jit(solution)/shard_map/ppermute | solution.py:345
  10.7 3.4 %collective-permute-start.1 = (f32[16,512]{1,0:T(8,128)}, f32[16,512]{1,0:T(8,128)S(1)}, u32[]{:S(2)}, u32[]{:S(2)}) collective-permute-start(f32[16,512]{1,0:T(8,128)} %get-tuple-element.56), channel_id=1, source_target_pairs={{0,1},{1,0},{2,3},{3,2},{4,5},{5,4},{6,7},{7,6},{8,9},{9,8},{10,11... | collective-permute-start | bytes 98312 | tf_op jit(solution)/shard_map/ppermute | solution.py:345
  10.7 4.1 %collective-permute-start.2 = (f32[16,512]{1,0:T(8,128)}, f32[16,512]{1,0:T(8,128)S(1)}, u32[]{:S(2)}, u32[]{:S(2)}) collective-permute-start(f32[16,512]{1,0:T(8,128)} %get-tuple-element.57), channel_id=1, source_target_pairs={{0,2},{1,3},{2,0},{3,1},{4,6},{5,7},{6,4},{7,5},{8,10},{9,11},{10,... | collective-permute-start | bytes 98312 | tf_op jit(solution)/shard_map/ppermute | solution.py:345
  12.2 3.6 %collective-permute-start.3 = (f32[16,512]{1,0:T(8,128)}, f32[16,512]{1,0:T(8,128)S(1)}, u32[]{:S(2)}, u32[]{:S(2)}) collective-permute-start(f32[16,512]{1,0:T(8,128)} %get-tuple-element.58), channel_id=1, source_target_pairs={{0,3},{1,2},{2,1},{3,0},{4,7},{5,6},{6,5},{7,4},{8,11},{9,10},{10,... | collective-permute-start | bytes 98312 | tf_op jit(solution)/shard_map/ppermute | solution.py:345
  12.6 12.4 %collective-permute-start.12 = (f32[4,8,768]{2,1,0:T(8,128)}, f32[4,8,768]{2,1,0:T(8,128)S(1)}, u32[]{:S(2)}, u32[]{:S(2)}) collective-permute-start(f32[4,8,768]{2,1,0:T(8,128)} %get-tuple-element.64), channel_id=1, source_target_pairs={{0,8},{4,12},{8,0},{12,4},{16,24},{20,28},{24,16},{28,20},{1,9},{5... | collective-permute-start | bytes 294920 | tf_op jit(solution)/shard_map/ppermute | solution.py:345
  15.8 0.9 copy-start.5
  16.7 0.8 copy-start.6
  18.1 4.3 %collective-permute-start.4 = (f32[2,8,1024]{2,1,0:T(8,128)S(1)}, f32[2,8,1024]{2,1,0:T(8,128)S(1)}, u32[]{:S(2)}, u32[]{:S(2)}) collective-permute-start(f32[2,8,1024]{2,1,0:T(8,128)S(1)} %get-tuple-element.60), channel_id=1, source_target_pairs={{0,8},{4,12},{8,0},{12,4},{16,24},{20,28},{24,16},{28,20},{1,9},{5... | collective-permute-start | bytes 196616 | tf_op jit(solution)/shard_map/ppermute | solution.py:345
  22.3 4.9 %collective-permute-start.5 = (f32[1,8,1024]{2,1,0:T(8,128)S(1)}, f32[1,8,1024]{2,1,0:T(8,128)S(1)}, u32[]{:S(2)}, u32[]{:S(2)}) collective-permute-start(f32[1,8,1024]{2,1,0:T(8,128)S(1)} %get-tuple-element.62), channel_id=1, source_target_pairs={{0,16},{4,20},{8,24},{12,28},{16,0},{20,4},{24,8},{28,12},{1,17},{... | collective-permute-start | bytes 98312 | tf_op jit(solution)/shard_map/ppermute | solution.py:345
  25.0 0.9 copy-start.4
  25.9 5.1 %collective-permute-start.13 = (f32[2,8,768]{2,1,0:T(8,128)S(1)}, f32[2,8,768]{2,1,0:T(8,128)S(1)}, u32[]{:S(2)}, u32[]{:S(2)}) collective-permute-start(f32[2,8,768]{2,1,0:T(8,128)S(1)} %get-tuple-element.66), channel_id=1, source_target_pairs={{0,16},{4,20},{8,24},{12,28},{16,0},{20,4},{24,8},{28,12},{1,17},{... | collective-permute-start | bytes 147464 | tf_op jit(solution)/shard_map/ppermute | solution.py:345
  27.2 5.2 %collective-permute-start.6 = (f32[1,8,1024]{2,1,0:T(8,128)S(1)}, f32[1,8,1024]{2,1,0:T(8,128)S(1)}, u32[]{:S(2)}, u32[]{:S(2)}) collective-permute-start(f32[1,8,1024]{2,1,0:T(8,128)S(1)} %replica_mean.4.mine), channel_id=1, source_target_pairs={{0,16},{4,20},{8,24},{12,28},{16,0},{20,4},{24,8},{28,12},{1,17},{... | collective-permute-start | bytes 98312 | tf_op jit(solution)/shard_map/ppermute | solution.py:345
  31.0 3.9 %collective-permute-start.14 = (f32[1,8,768]{2,1,0:T(8,128)S(1)}, f32[1,8,768]{2,1,0:T(8,128)S(1)}, u32[]{:S(2)}, u32[]{:S(2)}) collective-permute-start(f32[1,8,768]{2,1,0:T(8,128)S(1)} %get-tuple-element.68), channel_id=1, source_target_pairs={{0,4},{4,0},{8,12},{12,8},{16,20},{20,16},{24,28},{28,24},{1,5},{5... | collective-permute-start | bytes 73736 | tf_op jit(solution)/shard_map/ppermute | solution.py:345
  32.5 8.5 %collective-permute-start.7 = (f32[2,8,1024]{2,1,0:T(8,128)S(1)}, f32[2,8,1024]{2,1,0:T(8,128)S(1)}, u32[]{:S(2)}, u32[]{:S(2)}) collective-permute-start(f32[2,8,1024]{2,1,0:T(8,128)S(1)} %double.8.mine), channel_id=1, source_target_pairs={{0,8},{4,12},{8,0},{12,4},{16,24},{20,28},{24,16},{28,20},{1,9},{5... | collective-permute-start | bytes 196616 | tf_op jit(solution)/shard_map/ppermute | solution.py:345
  34.9 3.8 %collective-permute-start.15 = (f32[1,8,768]{2,1,0:T(8,128)S(1)}, f32[1,8,768]{2,1,0:T(8,128)S(1)}, u32[]{:S(2)}, u32[]{:S(2)}) collective-permute-start(f32[1,8,768]{2,1,0:T(8,128)S(1)} %replica_mean.5.mine), channel_id=1, source_target_pairs={{0,4},{4,0},{8,12},{12,8},{16,20},{20,16},{24,28},{28,24},{1,5},{5... | collective-permute-start | bytes 73736 | tf_op jit(solution)/shard_map/ppermute | solution.py:345
  38.7 5.0 %collective-permute-start.16 = (f32[2,8,768]{2,1,0:T(8,128)S(1)}, f32[2,8,768]{2,1,0:T(8,128)S(1)}, u32[]{:S(2)}, u32[]{:S(2)}) collective-permute-start(f32[2,8,768]{2,1,0:T(8,128)S(1)} %double.10.mine), channel_id=1, source_target_pairs={{0,16},{4,20},{8,24},{12,28},{16,0},{20,4},{24,8},{28,12},{1,17},{... | collective-permute-start | bytes 147464 | tf_op jit(solution)/shard_map/ppermute | solution.py:345
  41.0 5.0 %collective-permute-start.8 = (f32[4,8,1024]{2,1,0:T(8,128)S(1)}, f32[4,8,1024]{2,1,0:T(8,128)S(1)}, u32[]{:S(2)}, u32[]{:S(2)}) collective-permute-start(f32[4,8,1024]{2,1,0:T(8,128)S(1)} %double.9.mine.mine_a), channel_id=1, source_target_pairs={{0,4},{4,0},{8,12},{12,8},{16,20},{20,16},{24,28},{28,24},{1,5},{5... | collective-permute-start | bytes 393224 | tf_op jit(solution)/shard_map/ppermute | solution.py:345
  43.7 4.7 %collective-permute-start.17 = (f32[4,8,768]{2,1,0:T(8,128)S(1)}, f32[4,8,768]{2,1,0:T(8,128)S(1)}, u32[]{:S(2)}, u32[]{:S(2)}) collective-permute-start(f32[4,8,768]{2,1,0:T(8,128)S(1)} %double.11.mine_b), channel_id=1, source_target_pairs={{0,8},{4,12},{8,0},{12,4},{16,24},{20,28},{24,16},{28,20},{1,9},{5... | collective-permute-start | bytes 294920 | tf_op jit(solution)/shard_map/ppermute | solution.py:345
  46.0 4.4 %copy-start = (bf16[1,512,1536]{2,1,0:T(8,128)(2,1)S(1)}, bf16[1,512,1536]{2,1,0:T(8,128)(2,1)}, u32[]{:S(2)}) copy-start(bf16[1,512,1536]{2,1,0:T(8,128)(2,1)} %g.4) | copy-start | bytes 4718596
  46.1 4.4 %copy-start.1 = (bf16[1,512,1536]{2,1,0:T(8,128)(2,1)S(1)}, bf16[1,512,1536]{2,1,0:T(8,128)(2,1)}, u32[]{:S(2)}) copy-start(bf16[1,512,1536]{2,1,0:T(8,128)(2,1)} %e.4) | copy-start | bytes 4718596
  46.1 3.5 %collective-permute-start.11 = (f32[16,512]{1,0:T(8,128)S(1)}, f32[16,512]{1,0:T(8,128)S(1)}, u32[]{:S(2)}, u32[]{:S(2)}) collective-permute-start(f32[16,512]{1,0:T(8,128)S(1)} %shard_rows.1.refs_0_), channel_id=1, source_target_pairs={{0,3},{1,2},{2,1},{3,0},{4,7},{5,6},{6,5},{7,4},{8,11},{9,10},{10,... | collective-permute-start | bytes 98312 | tf_op jit(solution)/shard_map/ppermute | solution.py:345
  46.1 4.3 %collective-permute-start.10 = (f32[16,512]{1,0:T(8,128)S(1)}, f32[16,512]{1,0:T(8,128)S(1)}, u32[]{:S(2)}, u32[]{:S(2)}) collective-permute-start(f32[16,512]{1,0:T(8,128)S(1)} %shard_rows.1.refs_0_), channel_id=1, source_target_pairs={{0,2},{1,3},{2,0},{3,1},{4,6},{5,7},{6,4},{7,5},{8,10},{9,11},{10,... | collective-permute-start | bytes 98312 | tf_op jit(solution)/shard_map/ppermute | solution.py:345
  47.1 3.3 %collective-permute-start.9 = (f32[16,512]{1,0:T(8,128)S(1)}, f32[16,512]{1,0:T(8,128)S(1)}, u32[]{:S(2)}, u32[]{:S(2)}) collective-permute-start(f32[16,512]{1,0:T(8,128)S(1)} %shard_rows.1.refs_0_), channel_id=1, source_target_pairs={{0,1},{1,0},{2,3},{3,2},{4,5},{5,4},{6,7},{7,6},{8,9},{9,8},{10,11... | collective-permute-start | bytes 98312 | tf_op jit(solution)/shard_map/ppermute | solution.py:345
  51.6 5.3 %collective-permute-start.18 = (f32[4,8,768]{2,1,0:T(8,128)S(1)}, f32[4,8,768]{2,1,0:T(8,128)S(1)}, u32[]{:S(2)}, u32[]{:S(2)}) collective-permute-start(f32[4,8,768]{2,1,0:T(8,128)S(1)} %get-tuple-element.73), channel_id=1, source_target_pairs={{0,4},{4,0},{8,12},{12,8},{16,20},{20,16},{24,28},{28,24},{1,5},{5... | collective-permute-start | bytes 294920 | tf_op jit(solution)/shard_map/ppermute | solution.py:345
  52.1 3.0 %collective-permute-start.19 = (f32[16,768]{1,0:T(8,128)S(1)}, f32[16,768]{1,0:T(8,128)S(1)}, u32[]{:S(2)}, u32[]{:S(2)}) collective-permute-start(f32[16,768]{1,0:T(8,128)S(1)} %get-tuple-element.75), channel_id=1, source_target_pairs={{0,1},{1,0},{2,3},{3,2},{4,5},{5,4},{6,7},{7,6},{8,9},{9,8},{10,11... | collective-permute-start | bytes 147464 | tf_op jit(solution)/shard_map/ppermute | solution.py:345
  52.1 4.5 %collective-permute-start.20 = (f32[16,768]{1,0:T(8,128)S(1)}, f32[16,768]{1,0:T(8,128)S(1)}, u32[]{:S(2)}, u32[]{:S(2)}) collective-permute-start(f32[16,768]{1,0:T(8,128)S(1)} %get-tuple-element.76), channel_id=1, source_target_pairs={{0,2},{1,3},{2,0},{3,1},{4,6},{5,7},{6,4},{7,5},{8,10},{9,11},{10,... | collective-permute-start | bytes 147464 | tf_op jit(solution)/shard_map/ppermute | solution.py:345
  52.7 4.2 %collective-permute-start.21 = (f32[16,768]{1,0:T(8,128)S(1)}, f32[16,768]{1,0:T(8,128)S(1)}, u32[]{:S(2)}, u32[]{:S(2)}) collective-permute-start(f32[16,768]{1,0:T(8,128)S(1)} %get-tuple-element.77), channel_id=1, source_target_pairs={{0,3},{1,2},{2,1},{3,0},{4,7},{5,6},{6,5},{7,4},{8,11},{9,10},{10,... | collective-permute-start | bytes 147464 | tf_op jit(solution)/shard_map/ppermute | solution.py:345
  53.9 9.1 %collective-permute-start.27 = (f32[4,8,768]{2,1,0:T(8,128)S(1)}, f32[4,8,768]{2,1,0:T(8,128)S(1)}, u32[]{:S(2)}, u32[]{:S(2)}) collective-permute-start(f32[4,8,768]{2,1,0:T(8,128)S(1)} %get-tuple-element.85), channel_id=1, source_target_pairs={{0,8},{4,12},{8,0},{12,4},{16,24},{20,28},{24,16},{28,20},{1,9},{5... | collective-permute-start | bytes 294920 | tf_op jit(solution)/shard_map/ppermute | solution.py:345
  57.0 4.3 %collective-permute-start.22 = (f32[2,8,1024]{2,1,0:T(8,128)S(1)}, f32[2,8,1024]{2,1,0:T(8,128)S(1)}, u32[]{:S(2)}, u32[]{:S(2)}) collective-permute-start(f32[2,8,1024]{2,1,0:T(8,128)S(1)} %get-tuple-element.80), channel_id=1, source_target_pairs={{0,8},{4,12},{8,0},{12,4},{16,24},{20,28},{24,16},{28,20},{1,9},{5... | collective-permute-start | bytes 196616 | tf_op jit(solution)/shard_map/ppermute | solution.py:345
  61.3 5.9 %collective-permute-start.23 = (f32[1,8,1024]{2,1,0:T(8,128)S(1)}, f32[1,8,1024]{2,1,0:T(8,128)S(1)}, u32[]{:S(2)}, u32[]{:S(2)}) collective-permute-start(f32[1,8,1024]{2,1,0:T(8,128)S(1)} %get-tuple-element.82), channel_id=1, source_target_pairs={{0,16},{4,20},{8,24},{12,28},{16,0},{20,4},{24,8},{28,12},{1,17},{... | collective-permute-start | bytes 98312 | tf_op jit(solution)/shard_map/ppermute | solution.py:345
  63.1 6.2 %collective-permute-start.28 = (f32[2,8,768]{2,1,0:T(8,128)S(1)}, f32[2,8,768]{2,1,0:T(8,128)S(1)}, u32[]{:S(2)}, u32[]{:S(2)}) collective-permute-start(f32[2,8,768]{2,1,0:T(8,128)S(1)} %get-tuple-element.87), channel_id=1, source_target_pairs={{0,16},{4,20},{8,24},{12,28},{16,0},{20,4},{24,8},{28,12},{1,17},{... | collective-permute-start | bytes 147464 | tf_op jit(solution)/shard_map/ppermute | solution.py:345
  67.2 4.9 %collective-permute-start.24 = (f32[1,8,1024]{2,1,0:T(8,128)S(1)}, f32[1,8,1024]{2,1,0:T(8,128)S(1)}, u32[]{:S(2)}, u32[]{:S(2)}) collective-permute-start(f32[1,8,1024]{2,1,0:T(8,128)S(1)} %replica_mean.6.mine), channel_id=1, source_target_pairs={{0,16},{4,20},{8,24},{12,28},{16,0},{20,4},{24,8},{28,12},{1,17},{... | collective-permute-start | bytes 98312 | tf_op jit(solution)/shard_map/ppermute | solution.py:345
  69.4 3.9 %collective-permute-start.29 = (f32[1,8,768]{2,1,0:T(8,128)S(1)}, f32[1,8,768]{2,1,0:T(8,128)S(1)}, u32[]{:S(2)}, u32[]{:S(2)}) collective-permute-start(f32[1,8,768]{2,1,0:T(8,128)S(1)} %get-tuple-element.89), channel_id=1, source_target_pairs={{0,4},{4,0},{8,12},{12,8},{16,20},{20,16},{24,28},{28,24},{1,5},{5... | collective-permute-start | bytes 73736 | tf_op jit(solution)/shard_map/ppermute | solution.py:345
  72.1 6.7 %collective-permute-start.25 = (f32[2,8,1024]{2,1,0:T(8,128)S(1)}, f32[2,8,1024]{2,1,0:T(8,128)S(1)}, u32[]{:S(2)}, u32[]{:S(2)}) collective-permute-start(f32[2,8,1024]{2,1,0:T(8,128)S(1)} %double.12.mine), channel_id=1, source_target_pairs={{0,8},{4,12},{8,0},{12,4},{16,24},{20,28},{24,16},{28,20},{1,9},{5... | collective-permute-start | bytes 196616 | tf_op jit(solution)/shard_map/ppermute | solution.py:345
  73.3 4.0 %collective-permute-start.30 = (f32[1,8,768]{2,1,0:T(8,128)S(1)}, f32[1,8,768]{2,1,0:T(8,128)S(1)}, u32[]{:S(2)}, u32[]{:S(2)}) collective-permute-start(f32[1,8,768]{2,1,0:T(8,128)S(1)} %replica_mean.7.mine), channel_id=1, source_target_pairs={{0,4},{4,0},{8,12},{12,8},{16,20},{20,16},{24,28},{28,24},{1,5},{5... | collective-permute-start | bytes 73736 | tf_op jit(solution)/shard_map/ppermute | solution.py:345
  77.2 5.0 %collective-permute-start.31 = (f32[2,8,768]{2,1,0:T(8,128)S(1)}, f32[2,8,768]{2,1,0:T(8,128)S(1)}, u32[]{:S(2)}, u32[]{:S(2)}) collective-permute-start(f32[2,8,768]{2,1,0:T(8,128)S(1)} %double.14.mine), channel_id=1, source_target_pairs={{0,16},{4,20},{8,24},{12,28},{16,0},{20,4},{24,8},{28,12},{1,17},{... | collective-permute-start | bytes 147464 | tf_op jit(solution)/shard_map/ppermute | solution.py:345
  78.8 8.1 %collective-permute-start.26 = (f32[4,8,1024]{2,1,0:T(8,128)S(1)}, f32[4,8,1024]{2,1,0:T(8,128)S(1)}, u32[]{:S(2)}, u32[]{:S(2)}) collective-permute-start(f32[4,8,1024]{2,1,0:T(8,128)S(1)} %double.13.refs_4_.mine_a), channel_id=1, source_target_pairs={{0,4},{4,0},{8,12},{12,8},{16,20},{20,16},{24,28},{28,24},{1,5},{5... | collective-permute-start | bytes 393224 | tf_op jit(solution)/shard_map/ppermute | solution.py:345
  82.3 4.7 %collective-permute-start.32 = (f32[4,8,768]{2,1,0:T(8,128)S(1)}, f32[4,8,768]{2,1,0:T(8,128)S(1)}, u32[]{:S(2)}, u32[]{:S(2)}) collective-permute-start(f32[4,8,768]{2,1,0:T(8,128)S(1)} %double.15.mine_b), channel_id=1, source_target_pairs={{0,8},{4,12},{8,0},{12,4},{16,24},{20,28},{24,16},{28,20},{1,9},{5... | collective-permute-start | bytes 294920 | tf_op jit(solution)/shard_map/ppermute | solution.py:345
  87.6 4.3 %collective-permute-start.35 = (f32[16,640]{1,0:T(8,128)S(1)}, f32[16,640]{1,0:T(8,128)S(1)}, u32[]{:S(2)}, u32[]{:S(2)}) collective-permute-start(f32[16,640]{1,0:T(8,128)S(1)} %get-tuple-element.94.refs_0_), channel_id=1, source_target_pairs={{0,3},{1,2},{2,1},{3,0},{4,7},{5,6},{6,5},{7,4},{8,11},{9,10},{10,... | collective-permute-start | bytes 122888 | tf_op jit(solution)/shard_map/ppermute | solution.py:345
  87.7 4.5 %collective-permute-start.34 = (f32[16,640]{1,0:T(8,128)S(1)}, f32[16,640]{1,0:T(8,128)S(1)}, u32[]{:S(2)}, u32[]{:S(2)}) collective-permute-start(f32[16,640]{1,0:T(8,128)S(1)} %get-tuple-element.94.refs_0_), channel_id=1, source_target_pairs={{0,2},{1,3},{2,0},{3,1},{4,6},{5,7},{6,4},{7,5},{8,10},{9,11},{10,... | collective-permute-start | bytes 122888 | tf_op jit(solution)/shard_map/ppermute | solution.py:345
  88.7 3.5 %collective-permute-start.33 = (f32[16,640]{1,0:T(8,128)S(1)}, f32[16,640]{1,0:T(8,128)S(1)}, u32[]{:S(2)}, u32[]{:S(2)}) collective-permute-start(f32[16,640]{1,0:T(8,128)S(1)} %get-tuple-element.94.refs_0_), channel_id=1, source_target_pairs={{0,1},{1,0},{2,3},{3,2},{4,5},{5,4},{6,7},{7,6},{8,9},{9,8},{10,11... | collective-permute-start | bytes 122888 | tf_op jit(solution)/shard_map/ppermute | solution.py:345

commit v8 on v5

v8 whole, which is shorter than its diff:
```python
import functools

import jax
import jax.numpy as jnp
from jax import lax
from jax.experimental import pallas as pl
from jax.experimental.pallas import tpu as pltpu
from jax.sharding import PartitionSpec as P

F32 = jnp.float32
BF16 = jnp.bfloat16
HIGHEST = lax.Precision.HIGHEST
CLIP_RMS = 0.1
STEPS = 4
LEFT_STEPS = 2
MIB = 1024 * 1024
NT = ((1,), (1,))


def split3(x):
    first = x.astype(BF16)
    rest = x - first.astype(F32)
    second = rest.astype(BF16)
    return first, second, (rest - second.astype(F32)).astype(BF16)


def tree_sum(values):
    values = list(values)
    while len(values) > 1:
        values = [values[i] + values[i + 1] for i in range(0, len(values), 2)]
    return values[0]


def dot(a, b, dims=((1,), (0,)), precision=None):
    return lax.dot_general(a, b, (dims, ((), ())), precision=precision, preferred_element_type=F32)


def fold(x, rows):
    return jnp.concatenate([x[i : i + rows] for i in range(0, x.shape[0], rows)], axis=1)


def unfold(x, rows):
    count = rows // x.shape[0]
    width = x.shape[1] // count
    return jnp.concatenate([x[:, i * width : (i + 1) * width] for i in range(count)], axis=0)


def split_z(total, stage, outs):
    half, rows, _ = stage.shape
    z = lax.shift_right_logical(lax.axis_index("dp"), 1)
    for c in range(half):
        stage[c] = total[c * rows : (c + 1) * rows, :]
    for j, out in enumerate(outs):
        out[...] = stage[lax.bitwise_xor(z, j)]


def join_z(pieces, stage, total):
    half, rows, _ = stage.shape
    z = lax.shift_right_logical(lax.axis_index("dp"), 1)
    for j, piece in enumerate(pieces):
        stage[lax.bitwise_xor(z, j)] = piece[...]
    for c in range(half):
        total[c * rows : (c + 1) * rows, :] = stage[c]


def split_shards(total, extra, outs):
    me = lax.axis_index("tensor")
    rows, width = outs[0].shape[0], total.shape[1]
    for j, out in enumerate(outs):
        owner = lax.bitwise_xor(me, j)
        out[:, :width] = total[pl.ds(pl.multiple_of(owner * rows, rows), rows), :]
        if extra is not None:
            out[:, width:] = fold(extra, rows)


def join_shards(pieces, total):
    me = lax.axis_index("tensor")
    rows = pieces[0].shape[0]
    for j, piece in enumerate(pieces):
        owner = lax.bitwise_xor(me, j)
        total[pl.ds(pl.multiple_of(owner * rows, rows), rows), :] = piece[...]


def left_kernel(n_shards, gu, eu, qu, gd, ed, qd, *refs):
    *outs, gu_in, eu_in, qu_in, pieces_up, total_up, gd_in, ed_in, qd_in, pieces_down, total_down, stage, q_sems, sems = refs
    up, down = (qu_in, pieces_up, total_up), (qd_in, pieces_down, total_down)
    firsts = [pltpu.make_async_copy(src, dst, q_sems.at[i]) for i, (src, dst) in enumerate(((qu, qu_in), (qd, qd_in)))]
    for first in firsts:
        first.start()
    stages = []
    for g, e, g_in, e_in, part in ((gu, eu, gu_in, eu_in, up), (gd, ed, gd_in, ed_in, down)):
        block = g_in.shape[0] // LEFT_STEPS
        for i in range(LEFT_STEPS):
            rows = pl.ds(i * block, block)
            n = len(stages)
            copies = [pltpu.make_async_copy(src.at[0, rows, :], dst.at[rows, :], sems.at[n, k]) for k, (src, dst) in enumerate(((g, g_in), (e, e_in)))]
            for copy in copies:
                copy.start()
            stages.append((copies, g_in, e_in, slice(i * block, (i + 1) * block), part))
    for first, (q, pieces, _) in zip(firsts, (up, down)):
        first.wait()
        split_rows(q, pieces)
    for copies, g, e, rows, (_, pieces, total) in stages:
        for copy in copies:
            copy.wait()
        total[:, rows] = add_pieces(dot(pieces[...], g[rows, :], NT) + dot(pieces[...], e[rows, :], NT))
    split_shards(total_up, None, outs[:n_shards])
    split_z(total_down, stage, outs[n_shards:])


def sum_shards_kernel(*refs):
    *terms, out, gram = refs
    width = out.shape[1]
    total = tree_sum(term[...] for term in terms)
    out[...] = total[:, :width]
    if total.shape[1] > width:
        gram[...] = unfold(total[:, width:], gram.shape[0])
    else:
        gram[...] = jnp.zeros_like(gram)


def sum_z_kernel(half, *refs):
    chunks, shards, out = refs[:half], refs[half:-1], refs[-1]
    rows, width = chunks[0].shape
    out[:, :width] = tree_sum(chunk[...] for chunk in chunks)
    out[:, width:] = fold(tree_sum(shard[...] for shard in shards), rows)


def mean_kernel(n_dp, mine, other, chunk, shard):
    width = chunk.shape[1]
    total = (mine[...] + other[...]) / n_dp
    chunk[...] = total[:, :width]
    shard[...] = unfold(total[:, width:], shard.shape[0])


def split_rows(left, pieces):
    rank = left.shape[0]
    for i, piece in enumerate(split3(left[...])):
        pieces[i * rank : (i + 1) * rank, :] = piece


def add_pieces(t):
    rank = t.shape[0] // 3
    return t[:rank] + (t[rank : 2 * rank] + t[2 * rank :])


def right_down_kernel(half, *refs):
    chunks, refs = refs[:half], refs[half:]
    g, e, left, *outs, pieces, total, stage = refs
    join_z(chunks, stage, left)
    split_rows(left, pieces)
    total[...] = add_pieces(dot(pieces[...], g[0]) + dot(pieces[...], e[0]))
    split_shards(total, dot(left[...], left[...], NT, HIGHEST), outs)


def right_up_kernel(n_shards, *refs):
    shards, refs = refs[:n_shards], refs[n_shards:]
    g, e, left, gram, *outs, pieces, total, stage = refs
    join_shards(shards, left)
    split_rows(left, pieces)
    block = total.shape[1] // STEPS
    for i in range(STEPS):
        part = slice(i * block, (i + 1) * block)
        total[:, part] = add_pieces(dot(pieces[...], g[0, :, part]) + dot(pieces[...], e[0, :, part]))
    split_z(total, stage, outs)
    gram[...] = dot(left[...], left[...], NT, HIGHEST)


def inverse_factors(grams):
    rank = grams[0].shape[0]
    count = rank // 8
    panel = 4
    lane = lax.broadcasted_iota(jnp.int32, (8, 2 * rank), 1)
    row = lax.broadcasted_iota(jnp.int32, (8, 2 * rank), 0)
    states, pivots = [], []
    for gram in grams:
        wide = jnp.concatenate([gram, jnp.zeros_like(gram)], axis=1)
        states.append([wide[i : i + 8] + (lane == row + (rank + i)).astype(F32) for i in range(0, rank, 8)])
        pivots.append([])
    for start in range(0, rank, panel):
        at = start // 8
        below = range(at, count)
        spread = [
            [{i: jnp.broadcast_to(blocks[i][:, start + j : start + j + 1], (8, 2 * rank)) for i in below} for j in range(panel)]
            for blocks in states
        ]
        for j in range(panel):
            inner = (start + j) % 8
            for blocks, columns, found in zip(states, spread, pivots):
                pivot = columns[j][at][inner : inner + 1, :]
                found.append(pivot)
                inverse = 1.0 / pivot
                factor = {i: jnp.where(row > inner, columns[j][i], 0.0) if i == at else columns[j][i] for i in below}
                for later in columns[j + 1 :]:
                    head = later[at][inner : inner + 1, :] * inverse
                    for i in below:
                        later[i] = later[i] - factor[i] * head
                scaled = blocks[at][inner : inner + 1, :] * inverse
                for i in below:
                    blocks[i] = blocks[i] - factor[i] * scaled
    results = []
    for blocks, found in zip(states, pivots):
        rows = [block / jnp.sqrt(jnp.concatenate(found[8 * i : 8 * i + 8], axis=0)) for i, block in enumerate(blocks)]
        results.append(jnp.concatenate(rows, axis=0)[:, rank:])
    return results


def basis_kernel(left_up, left_down, gram_up, gram_down, *refs):
    inv_up, inv_down, lhs_up, lhs_down = refs[-4:]
    inverses = inverse_factors([gram_up[...], gram_down[...]])
    rank = left_up.shape[0]
    for inverse, inv, left, lhs in zip(inverses, (inv_up, inv_down), (left_up, left_down), (lhs_up, lhs_down)):
        inv[...] = inverse
        first, second, _ = split3(dot(inverse, left[...], precision=HIGHEST).T)
        lhs[:, :rank] = first
        lhs[:, rank : 2 * rank] = first
        lhs[:, 2 * rank : 3 * rank] = second
        lhs[:, 3 * rank :] = second


def right_factor(inv, total, rhs):
    rank = inv.shape[0]
    right = dot(inv[...], total[...], precision=HIGHEST)
    first, second, _ = split3(right)
    rhs[:rank, :] = first
    rhs[rank : 2 * rank, :] = second
    rhs[2 * rank : 3 * rank, :] = first
    rhs[3 * rank :, :] = second
    return jnp.sum(right * right)


def factor_up_kernel(half, *refs):
    chunks, (inv, rhs, square, total, stage) = refs[:half], refs[half:]
    join_z(chunks, stage, total)
    square[...] = jnp.full(square.shape, right_factor(inv, total, rhs), F32)


def factor_down_kernel(n_shards, *refs):
    shards, (inv, rhs, square, total) = refs[:n_shards], refs[n_shards:]
    join_shards(shards, total)
    square[...] = jnp.full(square.shape, right_factor(inv, total, rhs), F32)


def rows_of(block):
    return pl.ds(pl.multiple_of(pl.program_id(0) * block, block), block)


def error_kernel(g, e, lhs, rhs, error, made):
    made[...] = jnp.zeros_like(made)
    part = rows_of(error.shape[1])
    rebuilt = dot(lhs[part, :], rhs[...])
    error[0] = (g[0, part, :].astype(F32) + e[0, part, :].astype(F32) - rebuilt).astype(BF16)


def update_kernel(limit, lhs_up, rhs_up, lhs_down, rhs_down, square_down, *refs):
    *squares_up, update_up, update_down = refs
    norm_sq = tree_sum(square[...] for square in squares_up) + square_down[...]
    factor = jnp.minimum(jnp.float32(1.0), limit / jnp.sqrt(norm_sq))[:1, :1]
    for lhs, rhs, update in ((lhs_up, rhs_up, update_up), (lhs_down, rhs_down, update_down)):
        update[...] = (factor * dot(lhs[rows_of(update.shape[0]), :], rhs[...])).astype(BF16)


def shaped(*dims, dtype=F32):
    return jax.ShapeDtypeStruct(dims, dtype)


def whole(shape):
    return pl.BlockSpec(shape, lambda *_: (0,) * len(shape))


def row_blocks(rows, columns):
    return pl.BlockSpec((rows // STEPS, columns), lambda i: (i, 0))


def replica_blocks(rows, columns):
    return pl.BlockSpec((1, rows // STEPS, columns), lambda i: (0, i, 0))


VMEM = pl.BlockSpec(memory_space=pltpu.VMEM)
ANY = pl.BlockSpec(memory_space=pl.ANY)


def call(kernel, out_shape, *args, after=(), in_specs=None, flops=0, limit=12, name=None, **more):
    arrays = list(args) + jax.tree.leaves(out_shape)
    size = sum(a.size * a.dtype.itemsize for a in arrays)
    skip = len(after)
    return pl.pallas_call(
        lambda *refs: kernel(*refs[skip:]), out_shape=out_shape, in_specs=[ANY] * skip + (in_specs or [VMEM] * len(args)),
        compiler_params=pltpu.CompilerParams(vmem_limit_bytes=limit * MIB),
        cost_estimate=pl.CostEstimate(flops=flops, bytes_accessed=size, transcendentals=0), name=name, **more,
    )(*after, *args)


def swap(x, axis, distance):
    pairs = [(i, i ^ distance) for i in range(lax.axis_size(axis))]
    return lax.ppermute(x, axis, pairs)


def from_z(parts):
    return [parts[0]] + [swap(part, "dp", 2 * j) for j, part in enumerate(parts) if j]


def from_shards(parts):
    return [parts[0]] + [swap(part, "tensor", j) for j, part in enumerate(parts) if j]


def reduce_both(chunks, shards, rows, rank, after):
    n_dp, half = lax.axis_size("dp"), len(chunks)
    chunks = from_z(chunks)
    rows_here = shards[0].shape[0]
    shard, gram = call(sum_shards_kernel, [shaped(rows_here, rows), shaped(rank, rank)], *from_shards(shards), after=after, name="shard_sum")
    per, width = chunks[0].shape
    buffer = shaped(per, width + rows_here * rows // per)
    mine = call(functools.partial(sum_z_kernel, half), buffer, *chunks, *from_z([shard] * half), name="z_sum")
    chunk, shard = call(
        functools.partial(mean_kernel, n_dp), [shaped(per, width), shaped(rows_here, rows)], mine, swap(mine, "dp", 1), name="mean"
    )
    return chunk, shard, gram


def on_device(gu, eu, gd, ed, qu, qd):
    qu, qd = qu.T, qd.T
    n_dp, n_shards = lax.axis_size("dp"), lax.axis_size("tensor")
    _, rows, ff = gu.shape
    rank = qu.shape[0]
    half, rows_here = n_dp // 2, rank // n_shards
    chunks = [shaped(rank // half, ff)] * half
    stage = pltpu.VMEM((half, rank // half, ff), F32)
    wide = pltpu.VMEM((rank, ff), F32)
    narrow = pltpu.VMEM((rank, rows), F32)
    product = 4 * rows * ff * 4 * rank

    buffers = [
        [pltpu.VMEM(g.shape[1:], BF16)] * 2 + [pltpu.VMEM(q.shape, F32), pltpu.VMEM((3 * rank, q.shape[1]), BF16), total]
        for g, q, total in ((gu, qu, narrow), (gd, qd, wide))
    ]
    outs = call(
        functools.partial(left_kernel, n_shards), [shaped(rows_here, rows)] * n_shards + chunks, gu, eu, qu, gd, ed, qd, name="left",
        flops=2 * product, limit=61, in_specs=[pl.BlockSpec(memory_space=pltpu.HBM)] * 6,
        scratch_shapes=buffers[0] + buffers[1] + [stage, pltpu.SemaphoreType.DMA((2,)), pltpu.SemaphoreType.DMA((2 * LEFT_STEPS, 2))],
    )
    chunk, shard, _ = reduce_both(outs[n_shards:], outs[:n_shards], rows, rank, ())
    left_chunks, left_rows = from_z([chunk] * half), from_shards([shard] * n_shards)
    left_up, gram_up, *terms = call(
        functools.partial(right_up_kernel, n_shards), [shaped(rank, rows), shaped(rank, rank)] + chunks, *left_rows, gu, eu,
        name="right_up", flops=product, scratch_shapes=[pltpu.VMEM((3 * rank, rows), BF16), wide, stage],
    )
    left_down, *shards = call(
        functools.partial(right_down_kernel, half), [shaped(rank, ff)] + [shaped(rows_here, rows + rank * n_shards)] * n_shards,
        *left_chunks, gd, ed, after=(left_up,), name="right_down", flops=product,
        scratch_shapes=[pltpu.VMEM((3 * rank, ff), BF16), narrow, stage],
    )
    chunk, shard, gram_down = reduce_both(terms, shards, rows, rank, ())
    right_chunks, right_rows = from_z([chunk] * half), from_shards([shard] * n_shards)
    inv_up, inv_down, lhs_up, lhs_down = call(
        basis_kernel,
        [shaped(rank, rank)] * 2 + [shaped(rows, 4 * rank, dtype=BF16), shaped(ff, 4 * rank, dtype=BF16)],
        left_up, left_down, gram_up, gram_down, gu, eu, gd, ed, after=(chunk,), name="basis",
    )
    rhs_down, square_down = call(
        functools.partial(factor_down_kernel, n_shards), [shaped(4 * rank, rows, dtype=BF16), shaped(8, 128)],
        *right_rows, inv_down, name="factor_down", scratch_shapes=[narrow],
    )

    def new_error(g, e, lhs, rhs, name):
        outs = [shaped(*g.shape, dtype=BF16), shaped(8, 128)]
        specs = [replica_blocks(*g.shape[1:]), whole((8, 128))]
        return call(error_kernel, outs, g, e, lhs, rhs, name=name, flops=product // 2, grid=(STEPS,), out_specs=specs)

    new_error_down, made_down = new_error(gd, ed, lhs_down, rhs_down, "error_down")
    rhs_up, square_up = call(
        functools.partial(factor_up_kernel, half), [shaped(4 * rank, ff, dtype=BF16), shaped(8, 128)], *right_chunks, inv_up,
        after=(made_down,), name="factor_up", scratch_shapes=[wide, stage],
    )
    squares_up = from_shards([square_up] * n_shards)
    new_error_up, made_up = new_error(gu, eu, lhs_up, rhs_up, "error_up")
    limit = CLIP_RMS * (2.0 * rows * ff * n_shards) ** 0.5
    update_up, update_down = call(
        functools.partial(update_kernel, limit), [shaped(rows, ff, dtype=BF16), shaped(ff, rows, dtype=BF16)],
        lhs_up, rhs_up, lhs_down, rhs_down, square_down, *squares_up, after=(made_up,),
        name="update", flops=product, grid=(STEPS,), out_specs=[row_blocks(rows, ff), row_blocks(ff, rows)],
    )
    return new_error_up, update_up, new_error_down, update_down


def solution(mesh):
    placed = (
        P("dp", None, "tensor"),
        P("dp", None, "tensor"),
        P("dp", "tensor", None),
        P("dp", "tensor", None),
        P("tensor", None),
        P(),
    )
    return jax.shard_map(
        on_device,
        mesh=mesh,
        in_specs=placed,
        out_specs=(
            P("dp", None, "tensor"),
            P(None, "tensor"),
            P("dp", "tensor", None),
            P("tensor", None),
        ),
        check_vma=False,
    )
```

time: 98.6 us -> 94.4 us (0.957)
  waiting for transfers between devices: 30 us -> 25.8 us
    ppermute x35, waiting for transfers between devices: 30 us -> 25.8 us  [swap(): return lax.ppermute(x, axis, pairs)]
    pallas_call x25 -> x15, Pallas kernels: 22.7 us -> 22 us  [call(): pl.pallas_call(lambda *refs: kernel(*refs[skip:]), out_shape=out_shape, i...]
  transfers between devices with their start and end apart: 35 -> 35, of which waited for: 16 -> 11; matrix products, arithmetic and copies ran while one was open for 0% -> 0% of each run, Pallas kernels for 10% -> 11%
where the time goes in v8:
time: 94.4 us; the launch traced here: 94.2 us
  starting transfers between devices  42.6 us (45%)
  waiting for transfers between devices  25.8 us (27%)
  Pallas kernels  22 us (23%)
  local copies, waits for them, and re-layouts  3.06 us (3%)
    ppermute x35, starting transfers between devices, swap(): return lax.ppermute(x, axis, pairs)  42.6 us
    ppermute x35, waiting for transfers between devices, swap(): return lax.ppermute(x, axis, pairs)  25.8 us
    pallas_call x15, Pallas kernels, call(): pl.pallas_call(lambda *refs: kernel(*refs[skip:]), out_shape=out_shape, i...  22 us
    unnamed x14, local copies, waits for them, and re-layouts  3.06 us
  transfers between devices with their start and end apart: 35, of which 11 were waited for; matrix products, arithmetic and copies ran while one was open for 0% of the time, Pallas kernels for 11%

profile of v8, /device:TPU:0, one launch (start us, length us, event | category | flops | bytes accessed | tf_op | source)
XLA Modules:
  0.0 94.2 jit_solution(11170937817854731445)
XLA Ops:
  0.6 7.2 %left.1 = (f32[16,512]{1,0:T(8,128)}, f32[16,512]{1,0:T(8,128)}, f32[16,512]{1,0:T(8,128)}, f32[16,512]{1,0:T(8,128)}, f32[16,1536]{1,0:T(8,128)}, /*index=5*/f3...) custom-call(bf16[1,512,1536]{2,1,0:T(8,128)(2,1)} %refs_0_.5, bf16[1,512,1536]{2,1,0:T(8,128)(2,1)} %refs_1_.5, ...), custom_call_target="tpu_custom_call" | custom-call | flops 1610612736 | bytes 7340032 | tf_op jit(solution)/shard_map/left/pallas_call | solution.py:287
  7.9 0.5 collective-permute-start.3
  8.4 2.6 %collective-permute-start.4 = (f32[16,512]{1,0:T(8,128)}, f32[16,512]{1,0:T(8,128)S(1)}, u32[]{:S(2)}, u32[]{:S(2)}) collective-permute-start(f32[16,512]{1,0:T(8,128)} %get-tuple-element.50), channel_id=1, source_target_pairs={{0,2},{1,3},{2,0},{3,1},{4,6},{5,7},{6,4},{7,5},{8,10},{9,11},{10,... | collective-permute-start | bytes 98312 | tf_op jit(solution)/shard_map/ppermute | solution.py:296
  10.9 0.1 collective-permute-start.5
  11.0 1.8 %collective-permute-start = (f32[16,1536]{1,0:T(8,128)}, f32[16,1536]{1,0:T(8,128)S(1)}, u32[]{:S(2)}, u32[]{:S(2)}) collective-permute-start(f32[16,1536]{1,0:T(8,128)} %get-tuple-element.45), channel_id=1, source_target_pairs={{0,8},{4,12},{8,0},{12,4},{16,24},{20,28},{24,16},{28,20},{1,9},{5... | collective-permute-start | bytes 294920 | tf_op jit(solution)/shard_map/ppermute | solution.py:296
  12.8 2.6 %collective-permute-start.1 = (f32[16,1536]{1,0:T(8,128)}, f32[16,1536]{1,0:T(8,128)S(1)}, u32[]{:S(2)}, u32[]{:S(2)}) collective-permute-start(f32[16,1536]{1,0:T(8,128)} %get-tuple-element.46), channel_id=1, source_target_pairs={{0,16},{4,20},{8,24},{12,28},{16,0},{20,4},{24,8},{28,12},{1,17},{... | collective-permute-start | bytes 294920 | tf_op jit(solution)/shard_map/ppermute | solution.py:296
  15.4 0.0 collective-permute-done.3.refs_1_
  15.4 0.0 collective-permute-done.5.refs_3_
  15.4 0.7 copy-done.6
  16.2 0.6 shard_sum.2
  16.8 3.8 %collective-permute-start.8 = (f32[16,512]{1,0:T(8,128)S(1)}, f32[16,512]{1,0:T(8,128)S(1)}, u32[]{:S(2)}, u32[]{:S(2)}) collective-permute-start(f32[16,512]{1,0:T(8,128)S(1)} %get-tuple-element.52.refs_4_), channel_id=1, source_target_pairs={{0,24},{4,28},{8,16},{12,20},{16,8},{20,12},{24,0},{28,4},{1,25},{... | collective-permute-start | bytes 98312 | tf_op jit(solution)/shard_map/ppermute | solution.py:296
  20.6 0.0 collective-permute-start.7
  20.6 3.3 %collective-permute-done.8.refs_7_ = f32[16,512]{1,0:T(8,128)S(1)} collective-permute-done((f32[16,512]{1,0:T(8,128)S(1)}, f32[16,512]{1,0:T(8,128)S(1)}, u32[]{:S(2)}, u32[]{:S(2)}) %collective-permute-start.8) | collective-permute-done | bytes 32800 | tf_op jit(solution)/shard_map/ppermute | solution.py:296
  23.9 4.2 %collective-permute-start.6 = (f32[16,512]{1,0:T(8,128)S(1)}, f32[16,512]{1,0:T(8,128)S(1)}, u32[]{:S(2)}, u32[]{:S(2)}) collective-permute-start(f32[16,512]{1,0:T(8,128)S(1)} %get-tuple-element.52.refs_4_), channel_id=1, source_target_pairs={{0,8},{4,12},{8,0},{12,4},{16,24},{20,28},{24,16},{28,20},{1,9},{5... | collective-permute-start | bytes 98312 | tf_op jit(solution)/shard_map/ppermute | solution.py:296
  28.1 0.0 collective-permute-done.7.refs_6_
  28.1 1.9 %collective-permute-done.6.refs_5_ = f32[16,512]{1,0:T(8,128)S(1)} collective-permute-done((f32[16,512]{1,0:T(8,128)S(1)}, f32[16,512]{1,0:T(8,128)S(1)}, u32[]{:S(2)}, u32[]{:S(2)}) %collective-permute-start.6) | collective-permute-done | bytes 32800 | tf_op jit(solution)/shard_map/ppermute | solution.py:296
  29.9 0.0 collective-permute-done.refs_1_
  30.0 0.0 copy-start.5
  30.0 0.9 copy-done.5
  30.9 1.6 %collective-permute-start.9 = (f32[16,2048]{1,0:T(8,128)S(1)}, f32[16,2048]{1,0:T(8,128)S(1)}, u32[]{:S(2)}, u32[]{:S(2)}) collective-permute-start(f32[16,2048]{1,0:T(8,128)S(1)} %z_sum.2.refs_0_), channel_id=1, source_target_pairs={{0,4},{4,0},{8,12},{12,8},{16,20},{20,16},{24,28},{28,24},{1,5},{5... | collective-permute-start | bytes 393224 | tf_op jit(solution)/shard_map/ppermute | solution.py:296
  32.5 3.5 %collective-permute-done.9.refs_1_ = f32[16,2048]{1,0:T(8,128)S(1)} collective-permute-done((f32[16,2048]{1,0:T(8,128)S(1)}, f32[16,2048]{1,0:T(8,128)S(1)}, u32[]{:S(2)}, u32[]{:S(2)}) %collective-permute-start.9) | collective-permute-done | bytes 131104 | tf_op jit(solution)/shard_map/ppermute | solution.py:296
  35.9 0.1 collective-permute-start.12
  36.0 1.5 %collective-permute-start.11 = (f32[16,512]{1,0:T(8,128)S(1)}, f32[16,512]{1,0:T(8,128)S(1)}, u32[]{:S(2)}, u32[]{:S(2)}) collective-permute-start(f32[16,512]{1,0:T(8,128)S(1)} %get-tuple-element.53.refs_0_), channel_id=1, source_target_pairs={{0,2},{1,3},{2,0},{3,1},{4,6},{5,7},{6,4},{7,5},{8,10},{9,11},{10,... | collective-permute-start | bytes 98312 | tf_op jit(solution)/shard_map/ppermute | solution.py:296
  37.6 0.3 collective-permute-start.10
  37.9 2.5 %collective-permute-start.18 = (f32[16,1536]{1,0:T(8,128)S(1)}, f32[16,1536]{1,0:T(8,128)S(1)}, u32[]{:S(2)}, u32[]{:S(2)}) collective-permute-start(f32[16,1536]{1,0:T(8,128)S(1)} %get-tuple-element.59.refs_1_), channel_id=1, source_target_pairs={{0,24},{4,28},{8,16},{12,20},{16,8},{20,12},{24,0},{28,4},{1,25},{... | collective-permute-start | bytes 294920 | tf_op jit(solution)/shard_map/ppermute | solution.py:296
  40.4 1.0 %collective-permute-start.17 = (f32[16,1536]{1,0:T(8,128)S(1)}, f32[16,1536]{1,0:T(8,128)S(1)}, u32[]{:S(2)}, u32[]{:S(2)}) collective-permute-start(f32[16,1536]{1,0:T(8,128)S(1)} %get-tuple-element.59.refs_1_), channel_id=1, source_target_pairs={{0,16},{4,20},{8,24},{12,28},{16,0},{20,4},{24,8},{28,12},{1,17},{... | collective-permute-start | bytes 294920 | tf_op jit(solution)/shard_map/ppermute | solution.py:296
  41.4 0.9 collective-permute-start.16
  42.3 0.0 copy-start.3
  42.3 1.4 %copy-done.3 = bf16[1,512,1536]{2,1,0:T(8,128)(2,1)S(1)} copy-done((bf16[1,512,1536]{2,1,0:T(8,128)(2,1)S(1)}, bf16[1,512,1536]{2,1,0:T(8,128)(2,1)}, u32[]{:S(2)}) %copy-start.3) | copy-done | bytes 1572888
  43.7 1.1 %right_up.1 = (f32[64,512]{1,0:T(8,128)S(1)}, f32[64,64]{1,0:T(8,128)S(1)}, f32[16,1536]{1,0:T(8,128)S(1)}, f32[16,1536]{1,0:T(8,128)S(1)}, f32[16,1536]{1,0:T(8,128)S(1)}, /*index=5*/f32[16,1536]{1,0:T(8,128)S(1)}) custom-call(f32[16,512]{1,0:T(8,128)S(1)} %get-tuple-element.53.refs_0_, f32[16,512]{1,0:T(8,128)S(1)} %collective-permute-done.10.refs_1_, ...), custom_call_target="tpu_custom_call" | custom-call | flops 805306368 | bytes 3817472 | tf_op jit(solution)/shard_map/right_up/pallas_call | solution.py:287
  44.8 0.1 collective-permute-done.18.refs_4_
  44.9 5.7 %collective-permute-done.17.refs_3_ = f32[16,1536]{1,0:T(8,128)S(1)} collective-permute-done((f32[16,1536]{1,0:T(8,128)S(1)}, f32[16,1536]{1,0:T(8,128)S(1)}, u32[]{:S(2)}, u32[]{:S(2)}) %collective-permute-start.17) | collective-permute-done | bytes 98336 | tf_op jit(solution)/shard_map/ppermute | solution.py:296
  50.6 0.0 copy-start.4
  50.6 1.2 %right_down.1 = (f32[64,1536]{1,0:T(8,128)S(1)}, f32[16,768]{1,0:T(8,128)S(1)}, f32[16,768]{1,0:T(8,128)S(1)}, f32[16,768]{1,0:T(8,128)S(1)}, f32[16,768]{1,0:T(8,128)S(1)}) custom-call(f32[64,512]{1,0:T(8,128)S(1)} %get-tuple-element.58.refs_0_.refs_1_, f32[16,1536]{1,0:T(8,128)S(1)} %get-tuple-element.59.refs_1_, ...), custom_call_target="tpu_custom_call" | custom-call | flops 805306368 | bytes 4128768 | tf_op jit(solution)/shard_map/right_down/pallas_call | solution.py:287
  51.8 0.0 collective-permute-start.19
  51.8 0.1 collective-permute-start.13
  51.9 3.1 %collective-permute-start.14 = (f32[16,1536]{1,0:T(8,128)S(1)}, f32[16,1536]{1,0:T(8,128)S(1)}, u32[]{:S(2)}, u32[]{:S(2)}) collective-permute-start(f32[16,1536]{1,0:T(8,128)S(1)} %get-tuple-element.56), channel_id=1, source_target_pairs={{0,16},{4,20},{8,24},{12,28},{16,0},{20,4},{24,8},{28,12},{1,17},{... | collective-permute-start | bytes 294920 | tf_op jit(solution)/shard_map/ppermute | solution.py:296
  55.0 1.3 %collective-permute-start.15 = (f32[16,1536]{1,0:T(8,128)S(1)}, f32[16,1536]{1,0:T(8,128)S(1)}, u32[]{:S(2)}, u32[]{:S(2)}) collective-permute-start(f32[16,1536]{1,0:T(8,128)S(1)} %get-tuple-element.57), channel_id=1, source_target_pairs={{0,24},{4,28},{8,16},{12,20},{16,8},{20,12},{24,0},{28,4},{1,25},{... | collective-permute-start | bytes 294920 | tf_op jit(solution)/shard_map/ppermute | solution.py:296
  56.3 1.3 %collective-permute-start.20 = (f32[16,768]{1,0:T(8,128)S(1)}, f32[16,768]{1,0:T(8,128)S(1)}, u32[]{:S(2)}, u32[]{:S(2)}) collective-permute-start(f32[16,768]{1,0:T(8,128)S(1)} %get-tuple-element.62), channel_id=1, source_target_pairs={{0,2},{1,3},{2,0},{3,1},{4,6},{5,7},{6,4},{7,5},{8,10},{9,11},{10,... | collective-permute-start | bytes 147464 | tf_op jit(solution)/shard_map/ppermute | solution.py:296
  57.5 2.8 %collective-permute-done.20.refs_2_ = f32[16,768]{1,0:T(8,128)S(1)} collective-permute-done((f32[16,768]{1,0:T(8,128)S(1)}, f32[16,768]{1,0:T(8,128)S(1)}, u32[]{:S(2)}, u32[]{:S(2)}) %collective-permute-start.20) | collective-permute-done | bytes 49184 | tf_op jit(solution)/shard_map/ppermute | solution.py:296
  60.3 1.1 %collective-permute-done.21.refs_3_ = f32[16,768]{1,0:T(8,128)S(1)} collective-permute-done((f32[16,768]{1,0:T(8,128)S(1)}, f32[16,768]{1,0:T(8,128)S(1)}, u32[]{:S(2)}, u32[]{:S(2)}) %collective-permute-start.21) | collective-permute-done | bytes 49184 | tf_op jit(solution)/shard_map/ppermute | solution.py:296
  61.4 0.1 shard_sum.3
  61.5 2.5 %collective-permute-start.24 = (f32[16,512]{1,0:T(8,128)S(1)}, f32[16,512]{1,0:T(8,128)S(1)}, u32[]{:S(2)}, u32[]{:S(2)}) collective-permute-start(f32[16,512]{1,0:T(8,128)S(1)} %get-tuple-element.64.refs_4_), channel_id=1, source_target_pairs={{0,24},{4,28},{8,16},{12,20},{16,8},{20,12},{24,0},{28,4},{1,25},{... | collective-permute-start | bytes 98312 | tf_op jit(solution)/shard_map/ppermute | solution.py:296
  64.0 1.9 %collective-permute-start.22 = (f32[16,512]{1,0:T(8,128)S(1)}, f32[16,512]{1,0:T(8,128)S(1)}, u32[]{:S(2)}, u32[]{:S(2)}) collective-permute-start(f32[16,512]{1,0:T(8,128)S(1)} %get-tuple-element.64.refs_4_), channel_id=1, source_target_pairs={{0,8},{4,12},{8,0},{12,4},{16,24},{20,28},{24,16},{28,20},{1,9},{5... | collective-permute-start | bytes 98312 | tf_op jit(solution)/shard_map/ppermute | solution.py:296
  65.9 1.3 %collective-permute-done.24.refs_7_ = f32[16,512]{1,0:T(8,128)S(1)} collective-permute-done((f32[16,512]{1,0:T(8,128)S(1)}, f32[16,512]{1,0:T(8,128)S(1)}, u32[]{:S(2)}, u32[]{:S(2)}) %collective-permute-start.24) | collective-permute-done | bytes 32800 | tf_op jit(solution)/shard_map/ppermute | solution.py:296
  67.2 1.6 %collective-permute-done.23.refs_6_ = f32[16,512]{1,0:T(8,128)S(1)} collective-permute-done((f32[16,512]{1,0:T(8,128)S(1)}, f32[16,512]{1,0:T(8,128)S(1)}, u32[]{:S(2)}, u32[]{:S(2)}) %collective-permute-start.23) | collective-permute-done | bytes 32800 | tf_op jit(solution)/shard_map/ppermute | solution.py:296
  68.9 1.6 %collective-permute-start.25 = (f32[16,2048]{1,0:T(8,128)S(1)}, f32[16,2048]{1,0:T(8,128)S(1)}, u32[]{:S(2)}, u32[]{:S(2)}) collective-permute-start(f32[16,2048]{1,0:T(8,128)S(1)} %z_sum.3.refs_0_), channel_id=1, source_target_pairs={{0,4},{4,0},{8,12},{12,8},{16,20},{20,16},{24,28},{28,24},{1,5},{5... | collective-permute-start | bytes 393224 | tf_op jit(solution)/shard_map/ppermute | solution.py:296
  70.4 3.4 %collective-permute-done.25.refs_1_ = f32[16,2048]{1,0:T(8,128)S(1)} collective-permute-done((f32[16,2048]{1,0:T(8,128)S(1)}, f32[16,2048]{1,0:T(8,128)S(1)}, u32[]{:S(2)}, u32[]{:S(2)}) %collective-permute-start.25) | collective-permute-done | bytes 131104 | tf_op jit(solution)/shard_map/ppermute | solution.py:296
  73.9 0.1 collective-permute-start.28
  74.0 2.3 %collective-permute-start.31 = (f32[16,1536]{1,0:T(8,128)S(1)}, f32[16,1536]{1,0:T(8,128)S(1)}, u32[]{:S(2)}, u32[]{:S(2)}) collective-permute-start(f32[16,1536]{1,0:T(8,128)S(1)} %get-tuple-element.65.refs_0_.refs_1_), channel_id=1, source_target_pairs={{0,24},{4,28},{8,16},{12,20},{16,8},{20,12},{24,0},{28,4},{1,25},{... | collective-permute-start | bytes 294920 | tf_op jit(solution)/shard_map/ppermute | solution.py:296
  76.3 0.2 collective-permute-start.30
  76.5 2.0 %collective-permute-start.29 = (f32[16,1536]{1,0:T(8,128)S(1)}, f32[16,1536]{1,0:T(8,128)S(1)}, u32[]{:S(2)}, u32[]{:S(2)}) collective-permute-start(f32[16,1536]{1,0:T(8,128)S(1)} %get-tuple-element.65.refs_0_.refs_1_), channel_id=1, source_target_pairs={{0,8},{4,12},{8,0},{12,4},{16,24},{20,28},{24,16},{28,20},{1,9},{5... | collective-permute-start | bytes 294920 | tf_op jit(solution)/shard_map/ppermute | solution.py:296
  78.5 0.9 collective-permute-start.27
  79.4 0.0 collective-permute-start.26
  79.4 3.2 %basis.1 = (f32[64,64]{1,0:T(8,128)S(1)}, f32[64,64]{1,0:T(8,128)S(1)}, bf16[512,256]{1,0:T(8,128)(2,1)S(1)}, bf16[1536,256]{1,0:T(8,128)(2,1)S(1)}) custom-call(f32[16,1536]{1,0:T(8,128)S(1)} %get-tuple-element.65.refs_0_.refs_1_, f32[64,512]{1,0:T(8,128)S(1)} %get-tuple-element.58.refs_0_.refs_1_, f32[64,1536]{1,0:T(8,128)S(1)} %get-tuple-element.66.refs_2_, ...), custom_call_target="tpu_custom_call" | custom-call | bytes 7929856 | tf_op jit(solution)/shard_map/basis/pallas_call | solution.py:287
  82.6 0.4 factor_down.1
  83.0 2.3 %error_down.1 = (bf16[1,1536,512]{2,1,0:T(8,128)(2,1)}, f32[8,128]{1,0:T(8,128)S(1)}) custom-call(bf16[1,1536,512]{2,1,0:T(8,128)(2,1)S(1)} %copy-done, bf16[1,1536,512]{2,1,0:T(8,128)(2,1)S(1)} %copy-done.1, bf16[1536,256]{1,0:T(8,128)(2,1)S(1)} %get-tuple-element.70.refs_2_.refs_3_, bf16[256,512]{1,0:T(8,128)(2,1)S(1)} %get-tuple-element.73.refs_3_.refs_4_), custom_call_target="tpu_custom_call" | custom-call | flops 402653184 | bytes 5771264 | tf_op jit(solution)/shard_map/error_down/pallas_call | solution.py:287
  85.3 1.1 %collective-permute-done.30.refs_3_ = f32[16,1536]{1,0:T(8,128)S(1)} collective-permute-done((f32[16,1536]{1,0:T(8,128)S(1)}, f32[16,1536]{1,0:T(8,128)S(1)}, u32[]{:S(2)}, u32[]{:S(2)}) %collective-permute-start.30) | collective-permute-done | bytes 98336 | tf_op jit(solution)/shard_map/ppermute | solution.py:296
  86.4 0.7 factor_up.1
  87.2 0.5 collective-permute-start.34
  87.7 1.3 %collective-permute-start.33 = (f32[8,128]{1,0:T(8,128)S(1)}, f32[8,128]{1,0:T(8,128)S(1)}, u32[]{:S(2)}, u32[]{:S(2)}) collective-permute-start(f32[8,128]{1,0:T(8,128)S(1)} %get-tuple-element.80.refs_6_), channel_id=1, source_target_pairs={{0,2},{1,3},{2,0},{3,1},{4,6},{5,7},{6,4},{7,5},{8,10},{9,11},{10,... | collective-permute-start | bytes 12296 | tf_op jit(solution)/shard_map/ppermute | solution.py:296
  89.0 0.1 collective-permute-start.32
  89.1 2.3 %error_up.1 = (bf16[1,512,1536]{2,1,0:T(8,128)(2,1)}, f32[8,128]{1,0:T(8,128)S(1)}) custom-call(bf16[1,512,1536]{2,1,0:T(8,128)(2,1)S(1)} %copy-done.2, bf16[1,512,1536]{2,1,0:T(8,128)(2,1)S(1)} %copy-done.4, bf16[512,256]{1,0:T(8,128)(2,1)S(1)} %get-tuple-element.69.refs_2_.refs_1_, bf16[256,1536]{1,0:T(8,128)(2,1)S(1)} %get-tuple-element.76.refs_3_.refs_2_), custom_call_target="tpu_custom_call" | custom-call | flops 402653184 | bytes 5771264 | tf_op jit(solution)/shard_map/error_up/pallas_call | solution.py:287
  91.5 2.7 %update.1 = (bf16[512,1536]{1,0:T(8,128)(2,1)}, bf16[1536,512]{1,0:T(8,128)(2,1)}) custom-call(f32[8,128]{1,0:T(8,128)S(1)} %get-tuple-element.78.refs_0_, bf16[512,256]{1,0:T(8,128)(2,1)S(1)} %get-tuple-element.69.refs_2_.refs_1_, bf16[256,1536]{1,0:T(8,128)(2,1)S(1)} %get-tuple-element.76.refs_3_.refs_2_, ...), custom_call_target="tpu_custom_call" | custom-call | flops 805306368 | bytes 5263360 | tf_op jit(solution)/shard_map/update/pallas_call | solution.py:287
  (35 shorter events, 0.2 us)
Async XLA Ops:
  0.6 41.6 %copy-start.2 = (bf16[1,512,1536]{2,1,0:T(8,128)(2,1)S(1)}, bf16[1,512,1536]{2,1,0:T(8,128)(2,1)}, u32[]{:S(2)}) copy-start(bf16[1,512,1536]{2,1,0:T(8,128)(2,1)} %refs_0_.5) | copy-start | bytes 4718596
  7.9 7.6 %collective-permute-start.3 = (f32[16,512]{1,0:T(8,128)}, f32[16,512]{1,0:T(8,128)S(1)}, u32[]{:S(2)}, u32[]{:S(2)}) collective-permute-start(f32[16,512]{1,0:T(8,128)} %get-tuple-element.49), channel_id=1, source_target_pairs={{0,1},{1,0},{2,3},{3,2},{4,5},{5,4},{6,7},{7,6},{8,9},{9,8},{10,11... | collective-permute-start | bytes 98312 | tf_op jit(solution)/shard_map/ppermute | solution.py:296
  8.4 7.0 %collective-permute-start.4 = (f32[16,512]{1,0:T(8,128)}, f32[16,512]{1,0:T(8,128)S(1)}, u32[]{:S(2)}, u32[]{:S(2)}) collective-permute-start(f32[16,512]{1,0:T(8,128)} %get-tuple-element.50), channel_id=1, source_target_pairs={{0,2},{1,3},{2,0},{3,1},{4,6},{5,7},{6,4},{7,5},{8,10},{9,11},{10,... | collective-permute-start | bytes 98312 | tf_op jit(solution)/shard_map/ppermute | solution.py:296
  10.9 4.5 %collective-permute-start.5 = (f32[16,512]{1,0:T(8,128)}, f32[16,512]{1,0:T(8,128)S(1)}, u32[]{:S(2)}, u32[]{:S(2)}) collective-permute-start(f32[16,512]{1,0:T(8,128)} %get-tuple-element.51), channel_id=1, source_target_pairs={{0,3},{1,2},{2,1},{3,0},{4,7},{5,6},{6,5},{7,4},{8,11},{9,10},{10,... | collective-permute-start | bytes 98312 | tf_op jit(solution)/shard_map/ppermute | solution.py:296
  11.0 18.9 %collective-permute-start = (f32[16,1536]{1,0:T(8,128)}, f32[16,1536]{1,0:T(8,128)S(1)}, u32[]{:S(2)}, u32[]{:S(2)}) collective-permute-start(f32[16,1536]{1,0:T(8,128)} %get-tuple-element.45), channel_id=1, source_target_pairs={{0,8},{4,12},{8,0},{12,4},{16,24},{20,28},{24,16},{28,20},{1,9},{5... | collective-permute-start | bytes 294920 | tf_op jit(solution)/shard_map/ppermute | solution.py:296
  12.8 17.1 %collective-permute-start.1 = (f32[16,1536]{1,0:T(8,128)}, f32[16,1536]{1,0:T(8,128)S(1)}, u32[]{:S(2)}, u32[]{:S(2)}) collective-permute-start(f32[16,1536]{1,0:T(8,128)} %get-tuple-element.46), channel_id=1, source_target_pairs={{0,16},{4,20},{8,24},{12,28},{16,0},{20,4},{24,8},{28,12},{1,17},{... | collective-permute-start | bytes 294920 | tf_op jit(solution)/shard_map/ppermute | solution.py:296
  15.4 14.5 %collective-permute-start.2 = (f32[16,1536]{1,0:T(8,128)}, f32[16,1536]{1,0:T(8,128)S(1)}, u32[]{:S(2)}, u32[]{:S(2)}) collective-permute-start(f32[16,1536]{1,0:T(8,128)} %get-tuple-element.47), channel_id=1, source_target_pairs={{0,24},{4,28},{8,16},{12,20},{16,8},{20,12},{24,0},{28,4},{1,25},{... | collective-permute-start | bytes 294920 | tf_op jit(solution)/shard_map/ppermute | solution.py:296
  15.4 0.8 copy-start.6
  16.8 7.1 %collective-permute-start.8 = (f32[16,512]{1,0:T(8,128)S(1)}, f32[16,512]{1,0:T(8,128)S(1)}, u32[]{:S(2)}, u32[]{:S(2)}) collective-permute-start(f32[16,512]{1,0:T(8,128)S(1)} %get-tuple-element.52.refs_4_), channel_id=1, source_target_pairs={{0,24},{4,28},{8,16},{12,20},{16,8},{20,12},{24,0},{28,4},{1,25},{... | collective-permute-start | bytes 98312 | tf_op jit(solution)/shard_map/ppermute | solution.py:296
  20.6 7.4 %collective-permute-start.7 = (f32[16,512]{1,0:T(8,128)S(1)}, f32[16,512]{1,0:T(8,128)S(1)}, u32[]{:S(2)}, u32[]{:S(2)}) collective-permute-start(f32[16,512]{1,0:T(8,128)S(1)} %get-tuple-element.52.refs_4_), channel_id=1, source_target_pairs={{0,16},{4,20},{8,24},{12,28},{16,0},{20,4},{24,8},{28,12},{1,17},{... | collective-permute-start | bytes 98312 | tf_op jit(solution)/shard_map/ppermute | solution.py:296
  23.9 6.0 %collective-permute-start.6 = (f32[16,512]{1,0:T(8,128)S(1)}, f32[16,512]{1,0:T(8,128)S(1)}, u32[]{:S(2)}, u32[]{:S(2)}) collective-permute-start(f32[16,512]{1,0:T(8,128)S(1)} %get-tuple-element.52.refs_4_), channel_id=1, source_target_pairs={{0,8},{4,12},{8,0},{12,4},{16,24},{20,28},{24,16},{28,20},{1,9},{5... | collective-permute-start | bytes 98312 | tf_op jit(solution)/shard_map/ppermute | solution.py:296
  30.0 0.9 copy-start.5
  30.9 5.0 %collective-permute-start.9 = (f32[16,2048]{1,0:T(8,128)S(1)}, f32[16,2048]{1,0:T(8,128)S(1)}, u32[]{:S(2)}, u32[]{:S(2)}) collective-permute-start(f32[16,2048]{1,0:T(8,128)S(1)} %z_sum.2.refs_0_), channel_id=1, source_target_pairs={{0,4},{4,0},{8,12},{12,8},{16,20},{20,16},{24,28},{28,24},{1,5},{5... | collective-permute-start | bytes 393224 | tf_op jit(solution)/shard_map/ppermute | solution.py:296
  35.9 5.4 %collective-permute-start.12 = (f32[16,512]{1,0:T(8,128)S(1)}, f32[16,512]{1,0:T(8,128)S(1)}, u32[]{:S(2)}, u32[]{:S(2)}) collective-permute-start(f32[16,512]{1,0:T(8,128)S(1)} %get-tuple-element.53.refs_0_), channel_id=1, source_target_pairs={{0,3},{1,2},{2,1},{3,0},{4,7},{5,6},{6,5},{7,4},{8,11},{9,10},{10,... | collective-permute-start | bytes 98312 | tf_op jit(solution)/shard_map/ppermute | solution.py:296
  36.0 6.2 %collective-permute-start.11 = (f32[16,512]{1,0:T(8,128)S(1)}, f32[16,512]{1,0:T(8,128)S(1)}, u32[]{:S(2)}, u32[]{:S(2)}) collective-permute-start(f32[16,512]{1,0:T(8,128)S(1)} %get-tuple-element.53.refs_0_), channel_id=1, source_target_pairs={{0,2},{1,3},{2,0},{3,1},{4,6},{5,7},{6,4},{7,5},{8,10},{9,11},{10,... | collective-permute-start | bytes 98312 | tf_op jit(solution)/shard_map/ppermute | solution.py:296
  37.6 4.7 %collective-permute-start.10 = (f32[16,512]{1,0:T(8,128)S(1)}, f32[16,512]{1,0:T(8,128)S(1)}, u32[]{:S(2)}, u32[]{:S(2)}) collective-permute-start(f32[16,512]{1,0:T(8,128)S(1)} %get-tuple-element.53.refs_0_), channel_id=1, source_target_pairs={{0,1},{1,0},{2,3},{3,2},{4,5},{5,4},{6,7},{7,6},{8,9},{9,8},{10,11... | collective-permute-start | bytes 98312 | tf_op jit(solution)/shard_map/ppermute | solution.py:296
  37.9 12.7 %copy-start = (bf16[1,1536,512]{2,1,0:T(8,128)(2,1)S(1)}, bf16[1,1536,512]{2,1,0:T(8,128)(2,1)}, u32[]{:S(2)}) copy-start(bf16[1,1536,512]{2,1,0:T(8,128)(2,1)} %refs_0_.4) | copy-start | bytes 4718596
  37.9 12.7 %copy-start.1 = (bf16[1,1536,512]{2,1,0:T(8,128)(2,1)S(1)}, bf16[1,1536,512]{2,1,0:T(8,128)(2,1)}, u32[]{:S(2)}) copy-start(bf16[1,1536,512]{2,1,0:T(8,128)(2,1)} %refs_1_.4) | copy-start | bytes 4718596
  37.9 7.0 %collective-permute-start.18 = (f32[16,1536]{1,0:T(8,128)S(1)}, f32[16,1536]{1,0:T(8,128)S(1)}, u32[]{:S(2)}, u32[]{:S(2)}) collective-permute-start(f32[16,1536]{1,0:T(8,128)S(1)} %get-tuple-element.59.refs_1_), channel_id=1, source_target_pairs={{0,24},{4,28},{8,16},{12,20},{16,8},{20,12},{24,0},{28,4},{1,25},{... | collective-permute-start | bytes 294920 | tf_op jit(solution)/shard_map/ppermute | solution.py:296
  40.4 10.2 %collective-permute-start.17 = (f32[16,1536]{1,0:T(8,128)S(1)}, f32[16,1536]{1,0:T(8,128)S(1)}, u32[]{:S(2)}, u32[]{:S(2)}) collective-permute-start(f32[16,1536]{1,0:T(8,128)S(1)} %get-tuple-element.59.refs_1_), channel_id=1, source_target_pairs={{0,16},{4,20},{8,24},{12,28},{16,0},{20,4},{24,8},{28,12},{1,17},{... | collective-permute-start | bytes 294920 | tf_op jit(solution)/shard_map/ppermute | solution.py:296
  41.4 9.2 %collective-permute-start.16 = (f32[16,1536]{1,0:T(8,128)S(1)}, f32[16,1536]{1,0:T(8,128)S(1)}, u32[]{:S(2)}, u32[]{:S(2)}) collective-permute-start(f32[16,1536]{1,0:T(8,128)S(1)} %get-tuple-element.59.refs_1_), channel_id=1, source_target_pairs={{0,8},{4,12},{8,0},{12,4},{16,24},{20,28},{24,16},{28,20},{1,9},{5... | collective-permute-start | bytes 294920 | tf_op jit(solution)/shard_map/ppermute | solution.py:296
  42.3 1.4 %copy-start.3 = (bf16[1,512,1536]{2,1,0:T(8,128)(2,1)S(1)}, bf16[1,512,1536]{2,1,0:T(8,128)(2,1)}, u32[]{:S(2)}) copy-start(bf16[1,512,1536]{2,1,0:T(8,128)(2,1)} %refs_1_.5) | copy-start | bytes 4718596
  50.6 28.8 %copy-start.4 = (bf16[1,512,1536]{2,1,0:T(8,128)(2,1)S(1)}, bf16[1,512,1536]{2,1,0:T(8,128)(2,1)}, u32[]{:S(2)}) copy-start(bf16[1,512,1536]{2,1,0:T(8,128)(2,1)} %refs_1_.5) | copy-start | bytes 4718596
  51.8 5.8 %collective-permute-start.19 = (f32[16,768]{1,0:T(8,128)S(1)}, f32[16,768]{1,0:T(8,128)S(1)}, u32[]{:S(2)}, u32[]{:S(2)}) collective-permute-start(f32[16,768]{1,0:T(8,128)S(1)} %get-tuple-element.61), channel_id=1, source_target_pairs={{0,1},{1,0},{2,3},{3,2},{4,5},{5,4},{6,7},{7,6},{8,9},{9,8},{10,11... | collective-permute-start | bytes 147464 | tf_op jit(solution)/shard_map/ppermute | solution.py:296
  51.8 12.2 %collective-permute-start.13 = (f32[16,1536]{1,0:T(8,128)S(1)}, f32[16,1536]{1,0:T(8,128)S(1)}, u32[]{:S(2)}, u32[]{:S(2)}) collective-permute-start(f32[16,1536]{1,0:T(8,128)S(1)} %get-tuple-element.55), channel_id=1, source_target_pairs={{0,8},{4,12},{8,0},{12,4},{16,24},{20,28},{24,16},{28,20},{1,9},{5... | collective-permute-start | bytes 294920 | tf_op jit(solution)/shard_map/ppermute | solution.py:296
  51.9 14.0 %collective-permute-start.14 = (f32[16,1536]{1,0:T(8,128)S(1)}, f32[16,1536]{1,0:T(8,128)S(1)}, u32[]{:S(2)}, u32[]{:S(2)}) collective-permute-start(f32[16,1536]{1,0:T(8,128)S(1)} %get-tuple-element.56), channel_id=1, source_target_pairs={{0,16},{4,20},{8,24},{12,28},{16,0},{20,4},{24,8},{28,12},{1,17},{... | collective-permute-start | bytes 294920 | tf_op jit(solution)/shard_map/ppermute | solution.py:296
  55.0 10.9 %collective-permute-start.15 = (f32[16,1536]{1,0:T(8,128)S(1)}, f32[16,1536]{1,0:T(8,128)S(1)}, u32[]{:S(2)}, u32[]{:S(2)}) collective-permute-start(f32[16,1536]{1,0:T(8,128)S(1)} %get-tuple-element.57), channel_id=1, source_target_pairs={{0,24},{4,28},{8,16},{12,20},{16,8},{20,12},{24,0},{28,4},{1,25},{... | collective-permute-start | bytes 294920 | tf_op jit(solution)/shard_map/ppermute | solution.py:296
  56.3 4.1 %collective-permute-start.20 = (f32[16,768]{1,0:T(8,128)S(1)}, f32[16,768]{1,0:T(8,128)S(1)}, u32[]{:S(2)}, u32[]{:S(2)}) collective-permute-start(f32[16,768]{1,0:T(8,128)S(1)} %get-tuple-element.62), channel_id=1, source_target_pairs={{0,2},{1,3},{2,0},{3,1},{4,6},{5,7},{6,4},{7,5},{8,10},{9,11},{10,... | collective-permute-start | bytes 147464 | tf_op jit(solution)/shard_map/ppermute | solution.py:296
  57.5 3.9 %collective-permute-start.21 = (f32[16,768]{1,0:T(8,128)S(1)}, f32[16,768]{1,0:T(8,128)S(1)}, u32[]{:S(2)}, u32[]{:S(2)}) collective-permute-start(f32[16,768]{1,0:T(8,128)S(1)} %get-tuple-element.63), channel_id=1, source_target_pairs={{0,3},{1,2},{2,1},{3,0},{4,7},{5,6},{6,5},{7,4},{8,11},{9,10},{10,... | collective-permute-start | bytes 147464 | tf_op jit(solution)/shard_map/ppermute | solution.py:296
  61.5 5.7 %collective-permute-start.24 = (f32[16,512]{1,0:T(8,128)S(1)}, f32[16,512]{1,0:T(8,128)S(1)}, u32[]{:S(2)}, u32[]{:S(2)}) collective-permute-start(f32[16,512]{1,0:T(8,128)S(1)} %get-tuple-element.64.refs_4_), channel_id=1, source_target_pairs={{0,24},{4,28},{8,16},{12,20},{16,8},{20,12},{24,0},{28,4},{1,25},{... | collective-permute-start | bytes 98312 | tf_op jit(solution)/shard_map/ppermute | solution.py:296
  64.0 4.8 %collective-permute-start.23 = (f32[16,512]{1,0:T(8,128)S(1)}, f32[16,512]{1,0:T(8,128)S(1)}, u32[]{:S(2)}, u32[]{:S(2)}) collective-permute-start(f32[16,512]{1,0:T(8,128)S(1)} %get-tuple-element.64.refs_4_), channel_id=1, source_target_pairs={{0,16},{4,20},{8,24},{12,28},{16,0},{20,4},{24,8},{28,12},{1,17},{... | collective-permute-start | bytes 98312 | tf_op jit(solution)/shard_map/ppermute | solution.py:296
  64.0 4.8 %collective-permute-start.22 = (f32[16,512]{1,0:T(8,128)S(1)}, f32[16,512]{1,0:T(8,128)S(1)}, u32[]{:S(2)}, u32[]{:S(2)}) collective-permute-start(f32[16,512]{1,0:T(8,128)S(1)} %get-tuple-element.64.refs_4_), channel_id=1, source_target_pairs={{0,8},{4,12},{8,0},{12,4},{16,24},{20,28},{24,16},{28,20},{1,9},{5... | collective-permute-start | bytes 98312 | tf_op jit(solution)/shard_map/ppermute | solution.py:296
  68.9 5.0 %collective-permute-start.25 = (f32[16,2048]{1,0:T(8,128)S(1)}, f32[16,2048]{1,0:T(8,128)S(1)}, u32[]{:S(2)}, u32[]{:S(2)}) collective-permute-start(f32[16,2048]{1,0:T(8,128)S(1)} %z_sum.3.refs_0_), channel_id=1, source_target_pairs={{0,4},{4,0},{8,12},{12,8},{16,20},{20,16},{24,28},{28,24},{1,5},{5... | collective-permute-start | bytes 393224 | tf_op jit(solution)/shard_map/ppermute | solution.py:296
  73.9 5.5 %collective-permute-start.28 = (f32[16,512]{1,0:T(8,128)S(1)}, f32[16,512]{1,0:T(8,128)S(1)}, u32[]{:S(2)}, u32[]{:S(2)}) collective-permute-start(f32[16,512]{1,0:T(8,128)S(1)} %get-tuple-element.71.refs_0_), channel_id=1, source_target_pairs={{0,3},{1,2},{2,1},{3,0},{4,7},{5,6},{6,5},{7,4},{8,11},{9,10},{10,... | collective-permute-start | bytes 98312 | tf_op jit(solution)/shard_map/ppermute | solution.py:296
  74.0 11.4 %collective-permute-start.31 = (f32[16,1536]{1,0:T(8,128)S(1)}, f32[16,1536]{1,0:T(8,128)S(1)}, u32[]{:S(2)}, u32[]{:S(2)}) collective-permute-start(f32[16,1536]{1,0:T(8,128)S(1)} %get-tuple-element.65.refs_0_.refs_1_), channel_id=1, source_target_pairs={{0,24},{4,28},{8,16},{12,20},{16,8},{20,12},{24,0},{28,4},{1,25},{... | collective-permute-start | bytes 294920 | tf_op jit(solution)/shard_map/ppermute | solution.py:296
  76.3 10.1 %collective-permute-start.30 = (f32[16,1536]{1,0:T(8,128)S(1)}, f32[16,1536]{1,0:T(8,128)S(1)}, u32[]{:S(2)}, u32[]{:S(2)}) collective-permute-start(f32[16,1536]{1,0:T(8,128)S(1)} %get-tuple-element.65.refs_0_.refs_1_), channel_id=1, source_target_pairs={{0,16},{4,20},{8,24},{12,28},{16,0},{20,4},{24,8},{28,12},{1,17},{... | collective-permute-start | bytes 294920 | tf_op jit(solution)/shard_map/ppermute | solution.py:296
  76.5 10.0 %collective-permute-start.29 = (f32[16,1536]{1,0:T(8,128)S(1)}, f32[16,1536]{1,0:T(8,128)S(1)}, u32[]{:S(2)}, u32[]{:S(2)}) collective-permute-start(f32[16,1536]{1,0:T(8,128)S(1)} %get-tuple-element.65.refs_0_.refs_1_), channel_id=1, source_target_pairs={{0,8},{4,12},{8,0},{12,4},{16,24},{20,28},{24,16},{28,20},{1,9},{5... | collective-permute-start | bytes 294920 | tf_op jit(solution)/shard_map/ppermute | solution.py:296
  78.5 4.1 %collective-permute-start.27 = (f32[16,512]{1,0:T(8,128)S(1)}, f32[16,512]{1,0:T(8,128)S(1)}, u32[]{:S(2)}, u32[]{:S(2)}) collective-permute-start(f32[16,512]{1,0:T(8,128)S(1)} %get-tuple-element.71.refs_0_), channel_id=1, source_target_pairs={{0,2},{1,3},{2,0},{3,1},{4,6},{5,7},{6,4},{7,5},{8,10},{9,11},{10,... | collective-permute-start | bytes 98312 | tf_op jit(solution)/shard_map/ppermute | solution.py:296
  79.4 3.2 %collective-permute-start.26 = (f32[16,512]{1,0:T(8,128)S(1)}, f32[16,512]{1,0:T(8,128)S(1)}, u32[]{:S(2)}, u32[]{:S(2)}) collective-permute-start(f32[16,512]{1,0:T(8,128)S(1)} %get-tuple-element.71.refs_0_), channel_id=1, source_target_pairs={{0,1},{1,0},{2,3},{3,2},{4,5},{5,4},{6,7},{7,6},{8,9},{9,8},{10,11... | collective-permute-start | bytes 98312 | tf_op jit(solution)/shard_map/ppermute | solution.py:296
  87.2 4.3 %collective-permute-start.34 = (f32[8,128]{1,0:T(8,128)S(1)}, f32[8,128]{1,0:T(8,128)S(1)}, u32[]{:S(2)}, u32[]{:S(2)}) collective-permute-start(f32[8,128]{1,0:T(8,128)S(1)} %get-tuple-element.80.refs_6_), channel_id=1, source_target_pairs={{0,3},{1,2},{2,1},{3,0},{4,7},{5,6},{6,5},{7,4},{8,11},{9,10},{10,... | collective-permute-start | bytes 12296 | tf_op jit(solution)/shard_map/ppermute | solution.py:296
  87.7 3.7 %collective-permute-start.33 = (f32[8,128]{1,0:T(8,128)S(1)}, f32[8,128]{1,0:T(8,128)S(1)}, u32[]{:S(2)}, u32[]{:S(2)}) collective-permute-start(f32[8,128]{1,0:T(8,128)S(1)} %get-tuple-element.80.refs_6_), channel_id=1, source_target_pairs={{0,2},{1,3},{2,0},{3,1},{4,6},{5,7},{6,4},{7,5},{8,10},{9,11},{10,... | collective-permute-start | bytes 12296 | tf_op jit(solution)/shard_map/ppermute | solution.py:296
  89.0 2.5 %collective-permute-start.32 = (f32[8,128]{1,0:T(8,128)S(1)}, f32[8,128]{1,0:T(8,128)S(1)}, u32[]{:S(2)}, u32[]{:S(2)}) collective-permute-start(f32[8,128]{1,0:T(8,128)S(1)} %get-tuple-element.80.refs_6_), channel_id=1, source_target_pairs={{0,1},{1,0},{2,3},{3,2},{4,5},{5,4},{6,7},{7,6},{8,9},{9,8},{10,11... | collective-permute-start | bytes 12296 | tf_op jit(solution)/shard_map/ppermute | solution.py:296

commit v9 on v6

v9 whole, which is shorter than its diff:
```python
import functools

import jax
import jax.numpy as jnp
from jax import lax
from jax.experimental import pallas as pl
from jax.experimental.pallas import tpu as pltpu
from jax.sharding import PartitionSpec as P

F32 = jnp.float32
BF16 = jnp.bfloat16
HIGHEST = lax.Precision.HIGHEST
CLIP_RMS = 0.1
STEPS = 4
LEFT_STEPS = 2
MIB = 1024 * 1024
NT = ((1,), (1,))


def split3(x):
    first = x.astype(BF16)
    rest = x - first.astype(F32)
    second = rest.astype(BF16)
    return first, second, (rest - second.astype(F32)).astype(BF16)


def tree_sum(values):
    values = list(values)
    while len(values) > 1:
        values = [values[i] + values[i + 1] for i in range(0, len(values), 2)]
    return values[0]


def dot(a, b, dims=((1,), (0,)), precision=None):
    return lax.dot_general(a, b, (dims, ((), ())), precision=precision, preferred_element_type=F32)


def fold(x, rows):
    return jnp.concatenate([x[i : i + rows] for i in range(0, x.shape[0], rows)], axis=1)


def unfold(x, rows):
    count = rows // x.shape[0]
    width = x.shape[1] // count
    return jnp.concatenate([x[:, i * width : (i + 1) * width] for i in range(count)], axis=0)


def place(axis):
    index = lax.axis_index(axis)
    return lax.bitwise_and(index, 1), lax.shift_right_logical(index, 1)


def split_replicas(total, stage, keep, send):
    parity, _ = place("dp")
    half, per, _ = keep.shape
    for c in range(2 * half):
        stage[c] = total[c * per : (c + 1) * per, :]
    for c in range(half):
        keep[c] = stage[2 * c + parity]
        send[c] = stage[2 * c + 1 - parity]


def join_replicas(mine, other, stage, total):
    parity, _ = place("dp")
    half, per, _ = mine.shape
    width = total.shape[1]
    for c in range(half):
        stage[2 * c + parity] = mine[c, :, :width]
        stage[2 * c + 1 - parity] = other[c, :, :width]
    for c in range(2 * half):
        total[c * per : (c + 1) * per, :] = stage[c]


def split_shards(total, extra, outs):
    me = lax.axis_index("tensor")
    rows, width = outs[0].shape[0], total.shape[1]
    for j, out in enumerate(outs):
        owner = lax.bitwise_xor(me, j)
        out[:, :width] = total[pl.ds(pl.multiple_of(owner * rows, rows), rows), :]
        if extra is not None:
            out[:, width:] = fold(extra, rows)


def join_shards(pieces, total):
    me = lax.axis_index("tensor")
    rows, width = pieces[0].shape[0], total.shape[1]
    for j, piece in enumerate(pieces):
        owner = lax.bitwise_xor(me, j)
        total[pl.ds(pl.multiple_of(owner * rows, rows), rows), :] = piece[:, :width]


def left_kernel(n_shards, gu, eu, qu, gd, ed, qd, *refs):
    *outs, gu_in, eu_in, qu_in, pieces_up, total_up, gd_in, ed_in, qd_in, pieces_down, total_down, stage, q_sems, sems = refs
    up, down = (qu_in, pieces_up, total_up), (qd_in, pieces_down, total_down)
    firsts = [pltpu.make_async_copy(src, dst, q_sems.at[i]) for i, (src, dst) in enumerate(((qu, qu_in), (qd, qd_in)))]
    for first in firsts:
        first.start()
    stages = []
    for g, e, g_in, e_in, part in ((gu, eu, gu_in, eu_in, up), (gd, ed, gd_in, ed_in, down)):
        block = g_in.shape[0] // LEFT_STEPS
        for i in range(LEFT_STEPS):
            rows = pl.ds(i * block, block)
            n = len(stages)
            copies = [pltpu.make_async_copy(src.at[0, rows, :], dst.at[rows, :], sems.at[n, k]) for k, (src, dst) in enumerate(((g, g_in), (e, e_in)))]
            for copy in copies:
                copy.start()
            stages.append((copies, g_in, e_in, slice(i * block, (i + 1) * block), part))
    for first, (q, pieces, _) in zip(firsts, (up, down)):
        first.wait()
        rank = q.shape[0]
        for i, piece in enumerate(split3(q[...].T)):
            pieces[:, i * rank : (i + 1) * rank] = piece
        pieces[:, 3 * rank :] = jnp.zeros((q.shape[1], rank), BF16)
    for copies, g, e, rows, (q, pieces, total) in stages:
        rank = q.shape[0]
        for copy in copies:
            copy.wait()
        t = dot(g[rows, :], pieces[...]) + dot(e[rows, :], pieces[...])
        t = (t[:, : 2 * rank] + t[:, 2 * rank :]).T
        total[:, rows] = t[:rank] + t[rank:]
    split_shards(total_up, None, outs[:n_shards])
    split_replicas(total_down, stage, *outs[n_shards:])


def sum_shards_kernel(n_shards, *refs):
    terms, (out, gram) = refs[:n_shards], refs[n_shards:]
    total = tree_sum(term[...] for term in terms)
    out[...] = total[:, : out.shape[1]]
    gram[...] = unfold(total[:, out.shape[1] :], gram.shape[0])


def first_shards_kernel(n_shards, own, kept, *refs):
    *others, out, copy, own_in, sems = refs
    copies = [pltpu.make_async_copy(own, own_in, sems.at[0]), pltpu.make_async_copy(kept, copy, sems.at[1])]
    for each in copies:
        each.start()
    for each in copies:
        each.wait()
    out[...] = tree_sum([own_in[...]] + [term[...] for term in others])


def split_z_kernel(keep, got, shard, *refs):
    *outs, stage = refs
    _, z = place("dp")
    half, per, ff = keep.shape
    block = shard.shape[1] // half
    for c in range(half):
        stage[c, :, :ff] = keep[c] + got[c]
        stage[c, :, ff:] = fold(shard[:, c * block : (c + 1) * block], per)
    for j, out in zip([0, *range(half - 1, 0, -1)], outs):
        out[...] = stage[lax.bitwise_xor(z, j)]


def mean_kernel(n_dp, *refs):
    refs[-1][...] = tree_sum(ref[...] for ref in refs[:-1]) / n_dp


def stack_kernel(*refs):
    _, z = place("dp")
    for j, ref in enumerate(refs[:-1]):
        refs[-1][lax.bitwise_xor(z, j)] = ref[...]


def shard_rows(mine, other, ff, rows):
    half = mine.shape[0]
    return jnp.concatenate([unfold(mine[c, :, ff:] + other[c, :, ff:], rows) for c in range(half)], axis=1)


def shard_rows_kernel(ff, mine, other, out):
    out[...] = shard_rows(mine, other, ff, out.shape[0])


def split_rows(left, pieces):
    rank = left.shape[0]
    for i, piece in enumerate(split3(left[...])):
        pieces[i * rank : (i + 1) * rank, :] = piece


def add_pieces(t):
    rank = t.shape[0] // 3
    return t[:rank] + (t[rank : 2 * rank] + t[2 * rank :])


def right_down_kernel(mine, other, g, e, left, *refs):
    *outs, pieces, total, stage = refs
    join_replicas(mine, other, stage, left)
    split_rows(left, pieces)
    total[...] = add_pieces(dot(pieces[...], g[0]) + dot(pieces[...], e[0]))
    split_shards(total, dot(left[...], left[...], NT, HIGHEST), outs)


def right_up_kernel(n_shards, *refs):
    shards, refs = refs[:n_shards], refs[n_shards:]
    g, e, _, left, gram, keep, send, pieces, total, stage = refs
    join_shards(shards, left)
    split_rows(left, pieces)
    block = total.shape[1] // STEPS
    for i in range(STEPS):
        part = slice(i * block, (i + 1) * block)
        total[:, part] = add_pieces(dot(pieces[...], g[0, :, part]) + dot(pieces[...], e[0, :, part]))
    split_replicas(total, stage, keep, send)
    gram[...] = dot(left[...], left[...], NT, HIGHEST)


def inverse_factors(grams):
    rank = grams[0].shape[0]
    count = rank // 8
    panel = 4
    lane = lax.broadcasted_iota(jnp.int32, (8, 2 * rank), 1)
    row = lax.broadcasted_iota(jnp.int32, (8, 2 * rank), 0)
    states, pivots = [], []
    for gram in grams:
        wide = jnp.concatenate([gram, jnp.zeros_like(gram)], axis=1)
        states.append([wide[i : i + 8] + (lane == row + (rank + i)).astype(F32) for i in range(0, rank, 8)])
        pivots.append([])
    for start in range(0, rank, panel):
        at = start // 8
        below = range(at, count)
        spread = [
            [{i: jnp.broadcast_to(blocks[i][:, start + j : start + j + 1], (8, 2 * rank)) for i in below} for j in range(panel)]
            for blocks in states
        ]
        for j in range(panel):
            inner = (start + j) % 8
            for blocks, columns, found in zip(states, spread, pivots):
                pivot = columns[j][at][inner : inner + 1, :]
                found.append(pivot)
                inverse = 1.0 / pivot
                factor = {i: jnp.where(row > inner, columns[j][i], 0.0) if i == at else columns[j][i] for i in below}
                for later in columns[j + 1 :]:
                    head = later[at][inner : inner + 1, :] * inverse
                    for i in below:
                        later[i] = later[i] - factor[i] * head
                scaled = blocks[at][inner : inner + 1, :] * inverse
                for i in below:
                    blocks[i] = blocks[i] - factor[i] * scaled
    results = []
    for blocks, found in zip(states, pivots):
        rows = [block / jnp.sqrt(jnp.concatenate(found[8 * i : 8 * i + 8], axis=0)) for i, block in enumerate(blocks)]
        results.append(jnp.concatenate(rows, axis=0)[:, rank:])
    return results


def basis_kernel(left_up, left_down, gram_up, gram_down, *refs):
    inv_up, inv_down, lhs_up, lhs_down = refs[-4:]
    inverses = inverse_factors([gram_up[...], gram_down[...]])
    rank = left_up.shape[0]
    for inverse, inv, left, lhs in zip(inverses, (inv_up, inv_down), (left_up, left_down), (lhs_up, lhs_down)):
        inv[...] = inverse
        first, second, _ = split3(dot(inverse, left[...], precision=HIGHEST).T)
        lhs[:, :rank] = first
        lhs[:, rank : 2 * rank] = first
        lhs[:, 2 * rank : 3 * rank] = second
        lhs[:, 3 * rank :] = second


def right_factor(inv, total, rhs):
    rank = inv.shape[0]
    right = dot(inv[...], total[...], precision=HIGHEST)
    first, second, _ = split3(right)
    rhs[:rank, :] = first
    rhs[rank : 2 * rank, :] = second
    rhs[2 * rank : 3 * rank, :] = first
    rhs[3 * rank :, :] = second
    return jnp.sum(right * right)


def factor_up_kernel(mine, other, inv, rhs, shard, total, stage):
    join_replicas(mine, other, stage, total)
    square = right_factor(inv, total, rhs)
    rows, ff = shard.shape[0], total.shape[1]
    width = shard.shape[1] - 128
    shard[:, :width] = shard_rows(mine, other, ff, rows)
    shard[:, width:] = jnp.full((rows, 128), square, F32)


def factor_down_kernel(limit, n_shards, *refs):
    shards, refs = refs[:n_shards], refs[n_shards:]
    inv, _, rhs, clip, total = refs
    join_shards(shards, total)
    square = right_factor(inv, total, rhs)
    width = total.shape[1]
    norm_sq = square + tree_sum(shard[:8, width:] for shard in shards)
    clip[...] = jnp.minimum(jnp.float32(1.0), limit / jnp.sqrt(norm_sq))


def rows_of(block):
    return pl.ds(pl.multiple_of(pl.program_id(0) * block, block), block)


def error_up_kernel(g, e, lhs, rhs, error, made):
    made[...] = jnp.zeros_like(made)
    part = rows_of(error.shape[1])
    rebuilt = dot(lhs[part, :], rhs[...])
    error[0] = (g[0, part, :].astype(F32) + e[0, part, :].astype(F32) - rebuilt).astype(BF16)


def last_kernel(g, e, lhs_up, rhs_up, lhs_down, rhs_down, clip, error, update_up, update_down):
    factor = clip[:1, :1]
    part = rows_of(update_down.shape[0])
    rebuilt = dot(lhs_down[part, :], rhs_down[...])
    update_down[...] = (factor * rebuilt).astype(BF16)
    error[0] = (g[0, part, :].astype(F32) + e[0, part, :].astype(F32) - rebuilt).astype(BF16)
    part = rows_of(update_up.shape[0])
    update_up[...] = (factor * dot(lhs_up[part, :], rhs_up[...])).astype(BF16)


def shaped(*dims, dtype=F32):
    return jax.ShapeDtypeStruct(dims, dtype)


def whole(shape):
    return pl.BlockSpec(shape, lambda *_: (0,) * len(shape))


def row_blocks(rows, columns):
    return pl.BlockSpec((rows // STEPS, columns), lambda i: (i, 0))


def replica_blocks(rows, columns):
    return pl.BlockSpec((1, rows // STEPS, columns), lambda i: (0, i, 0))


VMEM = pl.BlockSpec(memory_space=pltpu.VMEM)
ANY = pl.BlockSpec(memory_space=pl.ANY)


def call(kernel, out_shape, *args, flops=0, limit=12, name=None, **more):
    arrays = list(args) + jax.tree.leaves(out_shape)
    size = sum(a.size * a.dtype.itemsize for a in arrays)
    cost = pl.CostEstimate(flops=flops, bytes_accessed=size, transcendentals=0)
    params = pltpu.CompilerParams(vmem_limit_bytes=limit * MIB)
    return pl.pallas_call(kernel, out_shape=out_shape, compiler_params=params, cost_estimate=cost, name=name, **more)(*args)


def swap(x, axis, distance):
    pairs = [(i, i ^ distance) for i in range(lax.axis_size(axis))]
    return lax.ppermute(x, axis, pairs)


def from_shards(parts):
    return [parts[0]] + [swap(parts[j], "tensor", j) for j in range(1, len(parts))]


def from_z(parts):
    got = {j: swap(parts[j], "dp", 2 * j) for j in range(len(parts) - 1, 0, -1)}
    return [parts[0]] + [got[j] for j in range(1, len(parts))]


def mean_replicas(keep, got, shard):
    n_dp = lax.axis_size("dp")
    half, per, ff = keep.shape
    piece = shaped(per, ff + shard.shape[0] * shard.shape[1] // (half * per))
    stack = shaped(half, *piece.shape)
    parts = call(split_z_kernel, [piece] * half, keep, got, shard, name="split_z", scratch_shapes=[pltpu.VMEM(stack.shape, F32)])
    parts = [parts[0], *parts[:0:-1]]
    mean = call(functools.partial(mean_kernel, n_dp), piece, *from_z(parts), name="replica_mean")
    mine = call(stack_kernel, stack, *from_z([mean] * half), name="stack_z")
    return mine, swap(mine, "dp", 1)


def on_device(gu, eu, gd, ed, qu, qd):
    qu, qd = qu.T, qd.T
    n_dp, n_shards = lax.axis_size("dp"), lax.axis_size("tensor")
    _, rows, ff = gu.shape
    rank = qu.shape[0]
    half, per, rows_here = n_dp // 2, rank // n_dp, rank // n_shards
    shard_rows_here = shaped(rows_here, rows)
    replica_half = shaped(half, per, ff)
    stage = pltpu.VMEM((n_dp, per, ff), F32)
    wide = pltpu.VMEM((rank, ff), F32)
    narrow = pltpu.VMEM((rank, rows), F32)
    product = 4 * rows * ff * 4 * rank

    buffers = [
        [pltpu.VMEM(g.shape[1:], BF16)] * 2 + [pltpu.VMEM(q.shape, F32), pltpu.VMEM((q.shape[1], 4 * rank), BF16), total]
        for g, q, total in ((gu, qu, narrow), (gd, qd, wide))
    ]
    *parts, keep, send = call(
        functools.partial(left_kernel, n_shards), [shard_rows_here] * n_shards + [replica_half] * 2, gu, eu, qu, gd, ed, qd,
        name="left", flops=2 * product, limit=61, in_specs=[pl.BlockSpec(memory_space=pltpu.HBM)] * 6,
        scratch_shapes=buffers[0] + buffers[1] + [stage, pltpu.SemaphoreType.DMA((2,)), pltpu.SemaphoreType.DMA((2 * LEFT_STEPS, 2))],
    )
    got = swap(send, "dp", 1)
    shard, keep = call(
        functools.partial(first_shards_kernel, n_shards), [shard_rows_here, replica_half], parts[0], keep, *from_shards(parts)[1:],
        name="shard_sum", in_specs=[pl.BlockSpec(memory_space=pltpu.HBM)] * 2 + [VMEM] * (n_shards - 1),
        scratch_shapes=[pltpu.VMEM((rows_here, rows), F32), pltpu.SemaphoreType.DMA((2,))],
    )
    mine, other = mean_replicas(keep, got, shard)

    shard = call(functools.partial(shard_rows_kernel, ff), shard_rows_here, mine, other, name="shard_rows")
    left_rows = from_shards([shard] * n_shards)
    left_down, *parts = call(
        right_down_kernel, [shaped(rank, ff)] + [shaped(rows_here, rows + rank * n_shards)] * n_shards, mine, other, gd, ed,
        name="right_down", flops=product, in_specs=[VMEM] * 4, scratch_shapes=[pltpu.VMEM((3 * rank, ff), BF16), narrow, stage],
    )
    left_up, gram_up, keep, send = call(
        functools.partial(right_up_kernel, n_shards), [shaped(rank, rows), shaped(rank, rank), replica_half, replica_half],
        *left_rows, gu, eu, left_down, name="right_up", flops=product, in_specs=[VMEM] * (n_shards + 2) + [ANY],
        scratch_shapes=[pltpu.VMEM((3 * rank, rows), BF16), wide, stage],
    )
    got = swap(send, "dp", 1)
    shard, gram_down = call(
        functools.partial(sum_shards_kernel, n_shards), [shard_rows_here, shaped(rank, rank)], *from_shards(parts), name="shard_sum"
    )
    mine, other = mean_replicas(keep, got, shard)
    inv_up, inv_down, lhs_up, lhs_down = call(
        basis_kernel,
        [shaped(rank, rank)] * 2 + [shaped(rows, 4 * rank, dtype=BF16), shaped(ff, 4 * rank, dtype=BF16)],
        left_up, left_down, gram_up, gram_down, gu, eu, gd, ed, mine, name="basis", in_specs=[VMEM] * 8 + [ANY],
    )
    rhs_up, shard = call(
        factor_up_kernel, [shaped(4 * rank, ff, dtype=BF16), shaped(rows_here, rows + 128)], mine, other, inv_up,
        name="factor_up", scratch_shapes=[wide, stage],
    )
    right_rows = from_shards([shard] * n_shards)
    new_error_up, made = call(
        error_up_kernel, [shaped(1, rows, ff, dtype=BF16), shaped(8, 128)], gu, eu, lhs_up, rhs_up, name="error_up", flops=product // 2,
        grid=(STEPS,), in_specs=[VMEM] * 4, out_specs=[replica_blocks(rows, ff), whole((8, 128))],
    )
    limit = CLIP_RMS * (2.0 * rows * ff * n_shards) ** 0.5
    rhs_down, clip = call(
        functools.partial(factor_down_kernel, limit, n_shards), [shaped(4 * rank, rows, dtype=BF16), shaped(8, 128)],
        *right_rows, inv_down, made, name="factor_down", in_specs=[VMEM] * (n_shards + 1) + [ANY], scratch_shapes=[narrow],
    )
    new_error_down, update_up, update_down = call(
        last_kernel, [shaped(1, ff, rows, dtype=BF16), shaped(rows, ff, dtype=BF16), shaped(ff, rows, dtype=BF16)],
        gd, ed, lhs_up, rhs_up, lhs_down, rhs_down, clip, name="last", flops=product, grid=(STEPS,),
        in_specs=[VMEM] * 7, out_specs=[replica_blocks(ff, rows), row_blocks(rows, ff), row_blocks(ff, rows)],
    )
    return new_error_up, update_up, new_error_down, update_down


def solution(mesh):
    placed = (
        P("dp", None, "tensor"),
        P("dp", None, "tensor"),
        P("dp", "tensor", None),
        P("dp", "tensor", None),
        P("tensor", None),
        P(),
    )
    return jax.shard_map(
        on_device,
        mesh=mesh,
        in_specs=placed,
        out_specs=(
            P("dp", None, "tensor"),
            P(None, "tensor"),
            P("dp", "tensor", None),
            P("tensor", None),
        ),
        check_vma=False,
    )
```

time: 88.5 us -> 86.8 us (0.981)
  waiting for transfers between devices: 35.8 us -> 32.9 us
  starting transfers between devices: 29 us -> 30.4 us
    ppermute x24 -> x28, waiting for transfers between devices: 35.8 us -> 32.9 us  [swap(): return lax.ppermute(x, axis, pairs)]
    ppermute x24 -> x28, starting transfers between devices: 29 us -> 30.4 us  [swap(): return lax.ppermute(x, axis, pairs)]
    pallas_call x19 -> x17, Pallas kernels: 20.9 us -> 20.8 us  [call(): pl.pallas_call(kernel, out_shape=out_shape, compiler_params=params, cost_...]
  transfers between devices with their start and end apart: 24 -> 28, of which waited for: 20 -> 18; matrix products, arithmetic and copies ran while one was open for 0% -> 0% of each run, Pallas kernels for 8% -> 8%
where the time goes in v9:
time: 86.8 us; the launch traced here: 86.6 us
  waiting for transfers between devices  32.9 us (38%)
  starting transfers between devices  30.4 us (35%)
  Pallas kernels  20.8 us (24%)
  local copies, waits for them, and re-layouts  1.7 us (2%)
    ppermute x28, waiting for transfers between devices, swap(): return lax.ppermute(x, axis, pairs)  32.9 us
    ppermute x28, starting transfers between devices, swap(): return lax.ppermute(x, axis, pairs)  30.4 us
    pallas_call x17, Pallas kernels, call(): pl.pallas_call(kernel, out_shape=out_shape, compiler_params=params, cost_...  20.8 us
  transfers between devices with their start and end apart: 28, of which 18 were waited for; matrix products, arithmetic and copies ran while one was open for 0% of the time, Pallas kernels for 8%

profile of v9, /device:TPU:0, one launch (start us, length us, event | category | flops | bytes accessed | tf_op | source)
XLA Modules:
  0.0 86.6 jit_solution(2522628469589243907)
XLA Ops:
  0.6 8.3 %left.1 = (f32[16,512]{1,0:T(8,128)}, f32[16,512]{1,0:T(8,128)}, f32[16,512]{1,0:T(8,128)}, f32[16,512]{1,0:T(8,128)}, f32[4,8,1536]{2,1,0:T(8,128)}, /*index=5*/f32[4,8,1536]{2,1,0:T(8,128)}) custom-call(bf16[1,512,1536]{2,1,0:T(8,128)(2,1)} %g.4, bf16[1,512,1536]{2,1,0:T(8,128)(2,1)} %e.4, f32[64,1536]{1,0:T(8,128)} %bitcast.2, bf16[1,1536,512]{2,1,0:T(8,128)(2,1)} %g.5, ...), custom_call_target="tpu_custom_call" | custom-call | flops 1610612736 | bytes 7340032 | tf_op jit(solution)/shard_map/left/pallas_call | solution.py:333
  8.9 0.0 copy-start.2
  8.9 3.0 %collective-permute-start.3 = (f32[4,8,1536]{2,1,0:T(8,128)}, f32[4,8,1536]{2,1,0:T(8,128)S(1)}, u32[]{:S(2)}, u32[]{:S(2)}) collective-permute-start(f32[4,8,1536]{2,1,0:T(8,128)} %get-tuple-element.50), channel_id=1, source_target_pairs={{0,4},{4,0},{8,12},{12,8},{16,20},{20,16},{24,28},{28,24},{1,5},{5... | collective-permute-start | bytes 589832 | tf_op jit(solution)/shard_map/ppermute | solution.py:338
  12.0 1.5 %collective-permute-start.1 = (f32[16,512]{1,0:T(8,128)}, f32[16,512]{1,0:T(8,128)S(1)}, u32[]{:S(2)}, u32[]{:S(2)}) collective-permute-start(f32[16,512]{1,0:T(8,128)} %get-tuple-element.47), channel_id=1, source_target_pairs={{0,2},{1,3},{2,0},{3,1},{4,6},{5,7},{6,4},{7,5},{8,10},{9,11},{10,... | collective-permute-start | bytes 98312 | tf_op jit(solution)/shard_map/ppermute | solution.py:338
  13.5 0.4 collective-permute-start.2
  13.8 0.0 collective-permute-done.refs_0_
  13.8 2.3 %collective-permute-done.1.refs_1_ = f32[16,512]{1,0:T(8,128)S(1)} collective-permute-done((f32[16,512]{1,0:T(8,128)}, f32[16,512]{1,0:T(8,128)S(1)}, u32[]{:S(2)}, u32[]{:S(2)}) %collective-permute-start.1) | collective-permute-done | bytes 32800 | tf_op jit(solution)/shard_map/ppermute | solution.py:338
  16.1 0.9 %collective-permute-done.2.refs_2_ = f32[16,512]{1,0:T(8,128)S(1)} collective-permute-done((f32[16,512]{1,0:T(8,128)}, f32[16,512]{1,0:T(8,128)S(1)}, u32[]{:S(2)}, u32[]{:S(2)}) %collective-permute-start.2) | collective-permute-done | bytes 32800 | tf_op jit(solution)/shard_map/ppermute | solution.py:338
  17.0 0.9 %copy-done.4 = f32[4,8,1536]{2,1,0:T(8,128)S(1)} copy-done((f32[4,8,1536]{2,1,0:T(8,128)S(1)}, f32[4,8,1536]{2,1,0:T(8,128)}, u32[]{:S(2)}) %copy-start.4) | copy-done | bytes 196632
  17.9 0.8 copy-done.5
  18.7 0.3 shard_sum.2
  19.0 0.0 collective-permute-done.3.got
  19.0 1.7 %collective-permute-start.4 = (f32[8,1792]{1,0:T(8,128)S(1)}, f32[8,1792]{1,0:T(8,128)S(1)}, u32[]{:S(2)}, u32[]{:S(2)}) collective-permute-start(f32[8,1792]{1,0:T(8,128)S(1)} %get-tuple-element.53), channel_id=1, source_target_pairs={{0,8},{4,12},{8,0},{12,4},{16,24},{20,28},{24,16},{28,20},{1,9},{5... | collective-permute-start | bytes 172040 | tf_op jit(solution)/shard_map/ppermute | solution.py:338
  20.7 2.6 %collective-permute-start.5 = (f32[8,1792]{1,0:T(8,128)S(1)}, f32[8,1792]{1,0:T(8,128)S(1)}, u32[]{:S(2)}, u32[]{:S(2)}) collective-permute-start(f32[8,1792]{1,0:T(8,128)S(1)} %get-tuple-element.54), channel_id=1, source_target_pairs={{0,16},{4,20},{8,24},{12,28},{16,0},{20,4},{24,8},{28,12},{1,17},{... | collective-permute-start | bytes 172040 | tf_op jit(solution)/shard_map/ppermute | solution.py:338
  23.3 0.2 collective-permute-start.6
  23.5 0.0 collective-permute-done.4.refs_1_
  23.5 3.7 %collective-permute-done.5.refs_2_ = f32[8,1792]{1,0:T(8,128)S(1)} collective-permute-done((f32[8,1792]{1,0:T(8,128)S(1)}, f32[8,1792]{1,0:T(8,128)S(1)}, u32[]{:S(2)}, u32[]{:S(2)}) %collective-permute-start.5) | collective-permute-done | bytes 57376 | tf_op jit(solution)/shard_map/ppermute | solution.py:338
  27.2 2.1 %collective-permute-done.6.refs_3_ = f32[8,1792]{1,0:T(8,128)S(1)} collective-permute-done((f32[8,1792]{1,0:T(8,128)S(1)}, f32[8,1792]{1,0:T(8,128)S(1)}, u32[]{:S(2)}, u32[]{:S(2)}) %collective-permute-start.6) | collective-permute-done | bytes 57376 | tf_op jit(solution)/shard_map/ppermute | solution.py:338
  29.3 1.8 %collective-permute-start.9 = (f32[8,1792]{1,0:T(8,128)S(1)}, f32[8,1792]{1,0:T(8,128)S(1)}, u32[]{:S(2)}, u32[]{:S(2)}) collective-permute-start(f32[8,1792]{1,0:T(8,128)S(1)} %replica_mean.2.refs_0_), channel_id=1, source_target_pairs={{0,24},{4,28},{8,16},{12,20},{16,8},{20,12},{24,0},{28,4},{1,25},{... | collective-permute-start | bytes 172040 | tf_op jit(solution)/shard_map/ppermute | solution.py:338
  31.2 0.0 collective-permute-start.8
  31.2 2.6 %collective-permute-start.7 = (f32[8,1792]{1,0:T(8,128)S(1)}, f32[8,1792]{1,0:T(8,128)S(1)}, u32[]{:S(2)}, u32[]{:S(2)}) collective-permute-start(f32[8,1792]{1,0:T(8,128)S(1)} %replica_mean.2.refs_0_), channel_id=1, source_target_pairs={{0,8},{4,12},{8,0},{12,4},{16,24},{20,28},{24,16},{28,20},{1,9},{5... | collective-permute-start | bytes 172040 | tf_op jit(solution)/shard_map/ppermute | solution.py:338
  33.8 1.7 %collective-permute-done.9.refs_3_ = f32[8,1792]{1,0:T(8,128)S(1)} collective-permute-done((f32[8,1792]{1,0:T(8,128)S(1)}, f32[8,1792]{1,0:T(8,128)S(1)}, u32[]{:S(2)}, u32[]{:S(2)}) %collective-permute-start.9) | collective-permute-done | bytes 57376 | tf_op jit(solution)/shard_map/ppermute | solution.py:338
  35.5 1.4 %collective-permute-done.8.refs_2_ = f32[8,1792]{1,0:T(8,128)S(1)} collective-permute-done((f32[8,1792]{1,0:T(8,128)S(1)}, f32[8,1792]{1,0:T(8,128)S(1)}, u32[]{:S(2)}, u32[]{:S(2)}) %collective-permute-start.8) | collective-permute-done | bytes 57376 | tf_op jit(solution)/shard_map/ppermute | solution.py:338
  36.9 0.0 collective-permute-done.7.refs_1_
  36.9 0.7 collective-permute-start.10
  37.5 6.1 %collective-permute-done.10.other = f32[4,8,1792]{2,1,0:T(8,128)S(1)} collective-permute-done((f32[4,8,1792]{2,1,0:T(8,128)S(1)}, f32[4,8,1792]{2,1,0:T(8,128)S(1)}, u32[]{:S(2)}, u32[]{:S(2)}) %collective-permute-start.10) | collective-permute-done | bytes 229408 | tf_op jit(solution)/shard_map/ppermute | solution.py:338
  43.7 0.0 copy-start.1
  43.7 0.1 collective-permute-start.13
  43.8 1.0 %collective-permute-start.12 = (f32[16,512]{1,0:T(8,128)S(1)}, f32[16,512]{1,0:T(8,128)S(1)}, u32[]{:S(2)}, u32[]{:S(2)}) collective-permute-start(f32[16,512]{1,0:T(8,128)S(1)} %shard_rows.1.refs_0_), channel_id=1, source_target_pairs={{0,2},{1,3},{2,0},{3,1},{4,6},{5,7},{6,4},{7,5},{8,10},{9,11},{10,... | collective-permute-start | bytes 98312 | tf_op jit(solution)/shard_map/ppermute | solution.py:338
  44.7 0.9 %collective-permute-start.11 = (f32[16,512]{1,0:T(8,128)S(1)}, f32[16,512]{1,0:T(8,128)S(1)}, u32[]{:S(2)}, u32[]{:S(2)}) collective-permute-start(f32[16,512]{1,0:T(8,128)S(1)} %shard_rows.1.refs_0_), channel_id=1, source_target_pairs={{0,1},{1,0},{2,3},{3,2},{4,5},{5,4},{6,7},{7,6},{8,9},{9,8},{10,11... | collective-permute-start | bytes 98312 | tf_op jit(solution)/shard_map/ppermute | solution.py:338
  45.6 1.2 %right_down.1 = (f32[64,1536]{1,0:T(8,128)S(1)}, f32[16,768]{1,0:T(8,128)S(1)}, f32[16,768]{1,0:T(8,128)S(1)}, f32[16,768]{1,0:T(8,128)S(1)}, f32[16,768]{1,0:T(8,128)S(1)}) custom-call(f32[4,8,1792]{2,1,0:T(8,128)S(1)} %stack_z.2.mine, f32[4,8,1792]{2,1,0:T(8,128)S(1)} %collective-permute-done.10.other, bf16[1,1536,512]{2,1,0:T(8,128)(2,1)S(1)} %copy-done.2, ...), custom_call_target="tpu_custom_call" | custom-call | flops 805306368 | bytes 4194304 | tf_op jit(solution)/shard_map/right_down/pallas_call | solution.py:333
  46.8 0.3 collective-permute-done.13.refs_3_
  47.1 1.0 %collective-permute-done.12.refs_2_ = f32[16,512]{1,0:T(8,128)S(1)} collective-permute-done((f32[16,512]{1,0:T(8,128)S(1)}, f32[16,512]{1,0:T(8,128)S(1)}, u32[]{:S(2)}, u32[]{:S(2)}) %collective-permute-start.12) | collective-permute-done | bytes 32800 | tf_op jit(solution)/shard_map/ppermute | solution.py:338
  48.1 1.2 %right_up.1 = (f32[64,512]{1,0:T(8,128)S(1)}, f32[64,64]{1,0:T(8,128)S(1)}, f32[4,8,1536]{2,1,0:T(8,128)S(1)}, f32[4,8,1536]{2,1,0:T(8,128)S(1)}) custom-call(f32[16,512]{1,0:T(8,128)S(1)} %shard_rows.1.refs_0_, f32[16,512]{1,0:T(8,128)S(1)} %collective-permute-done.11.refs_1_, f32[16,512]{1,0:T(8,128)S(1)} %collective-permute-done.12.refs_2_, ...), custom_call_target="tpu_custom_call" | custom-call | flops 805306368 | bytes 4210688 | tf_op jit(solution)/shard_map/right_up/pallas_call | solution.py:333
  49.3 0.6 collective-permute-start.17
  49.9 0.0 collective-permute-start.14
  49.9 0.7 collective-permute-start.15
  50.5 1.2 %collective-permute-start.16 = (f32[16,768]{1,0:T(8,128)S(1)}, f32[16,768]{1,0:T(8,128)S(1)}, u32[]{:S(2)}, u32[]{:S(2)}) collective-permute-start(f32[16,768]{1,0:T(8,128)S(1)} %get-tuple-element.62), channel_id=1, source_target_pairs={{0,3},{1,2},{2,1},{3,0},{4,7},{5,6},{6,5},{7,4},{8,11},{9,10},{10,... | collective-permute-start | bytes 147464 | tf_op jit(solution)/shard_map/ppermute | solution.py:338
  51.7 2.7 %collective-permute-done.15.refs_2_ = f32[16,768]{1,0:T(8,128)S(1)} collective-permute-done((f32[16,768]{1,0:T(8,128)S(1)}, f32[16,768]{1,0:T(8,128)S(1)}, u32[]{:S(2)}, u32[]{:S(2)}) %collective-permute-start.15) | collective-permute-done | bytes 49184 | tf_op jit(solution)/shard_map/ppermute | solution.py:338
  54.4 0.3 collective-permute-done.16.refs_3_
  54.7 0.1 shard_sum.3
  54.8 1.5 %collective-permute-done.17.got = f32[4,8,1536]{2,1,0:T(8,128)S(1)} collective-permute-done((f32[4,8,1536]{2,1,0:T(8,128)S(1)}, f32[4,8,1536]{2,1,0:T(8,128)S(1)}, u32[]{:S(2)}, u32[]{:S(2)}) %collective-permute-start.17) | collective-permute-done | bytes 196640 | tf_op jit(solution)/shard_map/ppermute | solution.py:338
  56.3 0.5 collective-permute-start.18
  56.8 1.5 %collective-permute-start.19 = (f32[8,1792]{1,0:T(8,128)S(1)}, f32[8,1792]{1,0:T(8,128)S(1)}, u32[]{:S(2)}, u32[]{:S(2)}) collective-permute-start(f32[8,1792]{1,0:T(8,128)S(1)} %get-tuple-element.69), channel_id=1, source_target_pairs={{0,16},{4,20},{8,24},{12,28},{16,0},{20,4},{24,8},{28,12},{1,17},{... | collective-permute-start | bytes 172040 | tf_op jit(solution)/shard_map/ppermute | solution.py:338
  58.3 2.5 %collective-permute-start.20 = (f32[8,1792]{1,0:T(8,128)S(1)}, f32[8,1792]{1,0:T(8,128)S(1)}, u32[]{:S(2)}, u32[]{:S(2)}) collective-permute-start(f32[8,1792]{1,0:T(8,128)S(1)} %get-tuple-element.70), channel_id=1, source_target_pairs={{0,24},{4,28},{8,16},{12,20},{16,8},{20,12},{24,0},{28,4},{1,25},{... | collective-permute-start | bytes 172040 | tf_op jit(solution)/shard_map/ppermute | solution.py:338
  60.8 0.0 collective-permute-done.18.refs_1_
  60.8 2.4 %collective-permute-done.19.refs_2_ = f32[8,1792]{1,0:T(8,128)S(1)} collective-permute-done((f32[8,1792]{1,0:T(8,128)S(1)}, f32[8,1792]{1,0:T(8,128)S(1)}, u32[]{:S(2)}, u32[]{:S(2)}) %collective-permute-start.19) | collective-permute-done | bytes 57376 | tf_op jit(solution)/shard_map/ppermute | solution.py:338
  63.2 1.2 %collective-permute-done.20.refs_3_ = f32[8,1792]{1,0:T(8,128)S(1)} collective-permute-done((f32[8,1792]{1,0:T(8,128)S(1)}, f32[8,1792]{1,0:T(8,128)S(1)}, u32[]{:S(2)}, u32[]{:S(2)}) %collective-permute-start.20) | collective-permute-done | bytes 57376 | tf_op jit(solution)/shard_map/ppermute | solution.py:338
  64.4 2.4 %collective-permute-start.23 = (f32[8,1792]{1,0:T(8,128)S(1)}, f32[8,1792]{1,0:T(8,128)S(1)}, u32[]{:S(2)}, u32[]{:S(2)}) collective-permute-start(f32[8,1792]{1,0:T(8,128)S(1)} %replica_mean.3.refs_0_), channel_id=1, source_target_pairs={{0,24},{4,28},{8,16},{12,20},{16,8},{20,12},{24,0},{28,4},{1,25},{... | collective-permute-start | bytes 172040 | tf_op jit(solution)/shard_map/ppermute | solution.py:338
  66.8 0.0 collective-permute-start.22
  66.8 2.0 %collective-permute-start.21 = (f32[8,1792]{1,0:T(8,128)S(1)}, f32[8,1792]{1,0:T(8,128)S(1)}, u32[]{:S(2)}, u32[]{:S(2)}) collective-permute-start(f32[8,1792]{1,0:T(8,128)S(1)} %replica_mean.3.refs_0_), channel_id=1, source_target_pairs={{0,8},{4,12},{8,0},{12,4},{16,24},{20,28},{24,16},{28,20},{1,9},{5... | collective-permute-start | bytes 172040 | tf_op jit(solution)/shard_map/ppermute | solution.py:338
  68.8 1.7 %collective-permute-done.23.refs_3_ = f32[8,1792]{1,0:T(8,128)S(1)} collective-permute-done((f32[8,1792]{1,0:T(8,128)S(1)}, f32[8,1792]{1,0:T(8,128)S(1)}, u32[]{:S(2)}, u32[]{:S(2)}) %collective-permute-start.23) | collective-permute-done | bytes 57376 | tf_op jit(solution)/shard_map/ppermute | solution.py:338
  70.5 1.4 %collective-permute-done.22.refs_2_ = f32[8,1792]{1,0:T(8,128)S(1)} collective-permute-done((f32[8,1792]{1,0:T(8,128)S(1)}, f32[8,1792]{1,0:T(8,128)S(1)}, u32[]{:S(2)}, u32[]{:S(2)}) %collective-permute-start.22) | collective-permute-done | bytes 57376 | tf_op jit(solution)/shard_map/ppermute | solution.py:338
  71.9 0.8 collective-permute-start.24
  72.7 3.2 %basis.1 = (f32[64,64]{1,0:T(8,128)S(1)}, f32[64,64]{1,0:T(8,128)S(1)}, bf16[512,256]{1,0:T(8,128)(2,1)S(1)}, bf16[1536,256]{1,0:T(8,128)(2,1)S(1)}) custom-call(f32[64,512]{1,0:T(8,128)S(1)} %get-tuple-element.57.left_up, f32[64,1536]{1,0:T(8,128)S(1)} %get-tuple-element.56.refs_6_.left_down, f32[64,64]{1,0:T(8,128)S(1)} %get-tuple-element.58.gram_up, ...), custom_call_target="tpu_custom_call" | custom-call | bytes 8159232 | tf_op jit(solution)/shard_map/basis/pallas_call | solution.py:333
  75.9 2.1 %collective-permute-done.24.other = f32[4,8,1792]{2,1,0:T(8,128)S(1)} collective-permute-done((f32[4,8,1792]{2,1,0:T(8,128)S(1)}, f32[4,8,1792]{2,1,0:T(8,128)S(1)}, u32[]{:S(2)}, u32[]{:S(2)}) %collective-permute-start.24) | collective-permute-done | bytes 229408 | tf_op jit(solution)/shard_map/ppermute | solution.py:338
  78.0 0.7 factor_up.1
  78.7 0.1 collective-permute-start.27
  78.8 0.9 %collective-permute-start.26 = (f32[16,640]{1,0:T(8,128)S(1)}, f32[16,640]{1,0:T(8,128)S(1)}, u32[]{:S(2)}, u32[]{:S(2)}) collective-permute-start(f32[16,640]{1,0:T(8,128)S(1)} %get-tuple-element.76.refs_0_), channel_id=1, source_target_pairs={{0,2},{1,3},{2,0},{3,1},{4,6},{5,7},{6,4},{7,5},{8,10},{9,11},{10,... | collective-permute-start | bytes 122888 | tf_op jit(solution)/shard_map/ppermute | solution.py:338
  79.7 0.9 %collective-permute-start.25 = (f32[16,640]{1,0:T(8,128)S(1)}, f32[16,640]{1,0:T(8,128)S(1)}, u32[]{:S(2)}, u32[]{:S(2)}) collective-permute-start(f32[16,640]{1,0:T(8,128)S(1)} %get-tuple-element.76.refs_0_), channel_id=1, source_target_pairs={{0,1},{1,0},{2,3},{3,2},{4,5},{5,4},{6,7},{7,6},{8,9},{9,8},{10,11... | collective-permute-start | bytes 122888 | tf_op jit(solution)/shard_map/ppermute | solution.py:338
  80.6 2.3 %error_up.1 = (bf16[1,512,1536]{2,1,0:T(8,128)(2,1)}, f32[8,128]{1,0:T(8,128)S(1)}) custom-call(bf16[1,512,1536]{2,1,0:T(8,128)(2,1)S(1)} %copy-done, bf16[1,512,1536]{2,1,0:T(8,128)(2,1)S(1)} %copy-done.1, bf16[512,256]{1,0:T(8,128)(2,1)S(1)} %get-tuple-element.71.lhs.lhs_up, bf16[256,1536]{1,0:T(8,128)(2,1)S(1)} %get-tuple-element.73.rhs.rhs_up), custom_call_target="tpu_custom_call" | custom-call | flops 402653184 | bytes 5771264 | tf_op jit(solution)/shard_map/error_up/pallas_call | solution.py:333
  82.9 0.2 collective-permute-done.26.refs_2_
  83.2 0.4 factor_down.1
  83.6 3.0 %last.1 = (bf16[1,1536,512]{2,1,0:T(8,128)(2,1)}, bf16[512,1536]{1,0:T(8,128)(2,1)}, bf16[1536,512]{1,0:T(8,128)(2,1)}) custom-call(bf16[1,1536,512]{2,1,0:T(8,128)(2,1)S(1)} %copy-done.2, bf16[1,1536,512]{2,1,0:T(8,128)(2,1)S(1)} %copy-done.3, bf16[512,256]{1,0:T(8,128)(2,1)S(1)} %get-tuple-element.71.lhs.lhs_up, ...), custom_call_target="tpu_custom_call" | custom-call | flops 805306368 | bytes 9965568 | tf_op jit(solution)/shard_map/last/pallas_call | solution.py:333
  (21 shorter events, 0.2 us)
Async XLA Ops:
  0.6 45.0 %copy-start.3 = (bf16[1,1536,512]{2,1,0:T(8,128)(2,1)S(1)}, bf16[1,1536,512]{2,1,0:T(8,128)(2,1)}, u32[]{:S(2)}) copy-start(bf16[1,1536,512]{2,1,0:T(8,128)(2,1)} %e.5) | copy-start | bytes 4718596
  8.9 36.7 %copy-start.2 = (bf16[1,1536,512]{2,1,0:T(8,128)(2,1)S(1)}, bf16[1,1536,512]{2,1,0:T(8,128)(2,1)}, u32[]{:S(2)}) copy-start(bf16[1,1536,512]{2,1,0:T(8,128)(2,1)} %g.5) | copy-start | bytes 4718596
  8.9 10.1 %collective-permute-start.3 = (f32[4,8,1536]{2,1,0:T(8,128)}, f32[4,8,1536]{2,1,0:T(8,128)S(1)}, u32[]{:S(2)}, u32[]{:S(2)}) collective-permute-start(f32[4,8,1536]{2,1,0:T(8,128)} %get-tuple-element.50), channel_id=1, source_target_pairs={{0,4},{4,0},{8,12},{12,8},{16,20},{20,16},{24,28},{28,24},{1,5},{5... | collective-permute-start | bytes 589832 | tf_op jit(solution)/shard_map/ppermute | solution.py:338
  12.0 1.9 %collective-permute-start = (f32[16,512]{1,0:T(8,128)}, f32[16,512]{1,0:T(8,128)S(1)}, u32[]{:S(2)}, u32[]{:S(2)}) collective-permute-start(f32[16,512]{1,0:T(8,128)} %get-tuple-element.46), channel_id=1, source_target_pairs={{0,1},{1,0},{2,3},{3,2},{4,5},{5,4},{6,7},{7,6},{8,9},{9,8},{10,11... | collective-permute-start | bytes 98312 | tf_op jit(solution)/shard_map/ppermute | solution.py:338
  12.0 4.1 %collective-permute-start.1 = (f32[16,512]{1,0:T(8,128)}, f32[16,512]{1,0:T(8,128)S(1)}, u32[]{:S(2)}, u32[]{:S(2)}) collective-permute-start(f32[16,512]{1,0:T(8,128)} %get-tuple-element.47), channel_id=1, source_target_pairs={{0,2},{1,3},{2,0},{3,1},{4,6},{5,7},{6,4},{7,5},{8,10},{9,11},{10,... | collective-permute-start | bytes 98312 | tf_op jit(solution)/shard_map/ppermute | solution.py:338
  13.5 3.6 %collective-permute-start.2 = (f32[16,512]{1,0:T(8,128)}, f32[16,512]{1,0:T(8,128)S(1)}, u32[]{:S(2)}, u32[]{:S(2)}) collective-permute-start(f32[16,512]{1,0:T(8,128)} %get-tuple-element.48), channel_id=1, source_target_pairs={{0,3},{1,2},{2,1},{3,0},{4,7},{5,6},{6,5},{7,4},{8,11},{9,10},{10,... | collective-permute-start | bytes 98312 | tf_op jit(solution)/shard_map/ppermute | solution.py:338
  17.0 0.9 %copy-start.4 = (f32[4,8,1536]{2,1,0:T(8,128)S(1)}, f32[4,8,1536]{2,1,0:T(8,128)}, u32[]{:S(2)}) copy-start(f32[4,8,1536]{2,1,0:T(8,128)} %get-tuple-element.45.kept) | copy-start | bytes 589828
  17.9 0.8 copy-start.5
  19.0 4.5 %collective-permute-start.4 = (f32[8,1792]{1,0:T(8,128)S(1)}, f32[8,1792]{1,0:T(8,128)S(1)}, u32[]{:S(2)}, u32[]{:S(2)}) collective-permute-start(f32[8,1792]{1,0:T(8,128)S(1)} %get-tuple-element.53), channel_id=1, source_target_pairs={{0,8},{4,12},{8,0},{12,4},{16,24},{20,28},{24,16},{28,20},{1,9},{5... | collective-permute-start | bytes 172040 | tf_op jit(solution)/shard_map/ppermute | solution.py:338
  20.7 6.5 %collective-permute-start.5 = (f32[8,1792]{1,0:T(8,128)S(1)}, f32[8,1792]{1,0:T(8,128)S(1)}, u32[]{:S(2)}, u32[]{:S(2)}) collective-permute-start(f32[8,1792]{1,0:T(8,128)S(1)} %get-tuple-element.54), channel_id=1, source_target_pairs={{0,16},{4,20},{8,24},{12,28},{16,0},{20,4},{24,8},{28,12},{1,17},{... | collective-permute-start | bytes 172040 | tf_op jit(solution)/shard_map/ppermute | solution.py:338
  23.3 6.0 %collective-permute-start.6 = (f32[8,1792]{1,0:T(8,128)S(1)}, f32[8,1792]{1,0:T(8,128)S(1)}, u32[]{:S(2)}, u32[]{:S(2)}) collective-permute-start(f32[8,1792]{1,0:T(8,128)S(1)} %get-tuple-element.55), channel_id=1, source_target_pairs={{0,24},{4,28},{8,16},{12,20},{16,8},{20,12},{24,0},{28,4},{1,25},{... | collective-permute-start | bytes 172040 | tf_op jit(solution)/shard_map/ppermute | solution.py:338
  29.3 6.2 %collective-permute-start.9 = (f32[8,1792]{1,0:T(8,128)S(1)}, f32[8,1792]{1,0:T(8,128)S(1)}, u32[]{:S(2)}, u32[]{:S(2)}) collective-permute-start(f32[8,1792]{1,0:T(8,128)S(1)} %replica_mean.2.refs_0_), channel_id=1, source_target_pairs={{0,24},{4,28},{8,16},{12,20},{16,8},{20,12},{24,0},{28,4},{1,25},{... | collective-permute-start | bytes 172040 | tf_op jit(solution)/shard_map/ppermute | solution.py:338
  31.2 5.7 %collective-permute-start.8 = (f32[8,1792]{1,0:T(8,128)S(1)}, f32[8,1792]{1,0:T(8,128)S(1)}, u32[]{:S(2)}, u32[]{:S(2)}) collective-permute-start(f32[8,1792]{1,0:T(8,128)S(1)} %replica_mean.2.refs_0_), channel_id=1, source_target_pairs={{0,16},{4,20},{8,24},{12,28},{16,0},{20,4},{24,8},{28,12},{1,17},{... | collective-permute-start | bytes 172040 | tf_op jit(solution)/shard_map/ppermute | solution.py:338
  31.2 5.7 %collective-permute-start.7 = (f32[8,1792]{1,0:T(8,128)S(1)}, f32[8,1792]{1,0:T(8,128)S(1)}, u32[]{:S(2)}, u32[]{:S(2)}) collective-permute-start(f32[8,1792]{1,0:T(8,128)S(1)} %replica_mean.2.refs_0_), channel_id=1, source_target_pairs={{0,8},{4,12},{8,0},{12,4},{16,24},{20,28},{24,16},{28,20},{1,9},{5... | collective-permute-start | bytes 172040 | tf_op jit(solution)/shard_map/ppermute | solution.py:338
  36.9 6.8 %collective-permute-start.10 = (f32[4,8,1792]{2,1,0:T(8,128)S(1)}, f32[4,8,1792]{2,1,0:T(8,128)S(1)}, u32[]{:S(2)}, u32[]{:S(2)}) collective-permute-start(f32[4,8,1792]{2,1,0:T(8,128)S(1)} %stack_z.2.mine), channel_id=1, source_target_pairs={{0,4},{4,0},{8,12},{12,8},{16,20},{20,16},{24,28},{28,24},{1,5},{5... | collective-permute-start | bytes 688136 | tf_op jit(solution)/shard_map/ppermute | solution.py:338
  43.7 4.4 %copy-start = (bf16[1,512,1536]{2,1,0:T(8,128)(2,1)S(1)}, bf16[1,512,1536]{2,1,0:T(8,128)(2,1)}, u32[]{:S(2)}) copy-start(bf16[1,512,1536]{2,1,0:T(8,128)(2,1)} %g.4) | copy-start | bytes 4718596
  43.7 4.4 %copy-start.1 = (bf16[1,512,1536]{2,1,0:T(8,128)(2,1)S(1)}, bf16[1,512,1536]{2,1,0:T(8,128)(2,1)}, u32[]{:S(2)}) copy-start(bf16[1,512,1536]{2,1,0:T(8,128)(2,1)} %e.4) | copy-start | bytes 4718596
  43.7 3.4 %collective-permute-start.13 = (f32[16,512]{1,0:T(8,128)S(1)}, f32[16,512]{1,0:T(8,128)S(1)}, u32[]{:S(2)}, u32[]{:S(2)}) collective-permute-start(f32[16,512]{1,0:T(8,128)S(1)} %shard_rows.1.refs_0_), channel_id=1, source_target_pairs={{0,3},{1,2},{2,1},{3,0},{4,7},{5,6},{6,5},{7,4},{8,11},{9,10},{10,... | collective-permute-start | bytes 98312 | tf_op jit(solution)/shard_map/ppermute | solution.py:338
  43.8 4.3 %collective-permute-start.12 = (f32[16,512]{1,0:T(8,128)S(1)}, f32[16,512]{1,0:T(8,128)S(1)}, u32[]{:S(2)}, u32[]{:S(2)}) collective-permute-start(f32[16,512]{1,0:T(8,128)S(1)} %shard_rows.1.refs_0_), channel_id=1, source_target_pairs={{0,2},{1,3},{2,0},{3,1},{4,6},{5,7},{6,4},{7,5},{8,10},{9,11},{10,... | collective-permute-start | bytes 98312 | tf_op jit(solution)/shard_map/ppermute | solution.py:338
  44.7 3.3 %collective-permute-start.11 = (f32[16,512]{1,0:T(8,128)S(1)}, f32[16,512]{1,0:T(8,128)S(1)}, u32[]{:S(2)}, u32[]{:S(2)}) collective-permute-start(f32[16,512]{1,0:T(8,128)S(1)} %shard_rows.1.refs_0_), channel_id=1, source_target_pairs={{0,1},{1,0},{2,3},{3,2},{4,5},{5,4},{6,7},{7,6},{8,9},{9,8},{10,11... | collective-permute-start | bytes 98312 | tf_op jit(solution)/shard_map/ppermute | solution.py:338
  49.3 6.9 %collective-permute-start.17 = (f32[4,8,1536]{2,1,0:T(8,128)S(1)}, f32[4,8,1536]{2,1,0:T(8,128)S(1)}, u32[]{:S(2)}, u32[]{:S(2)}) collective-permute-start(f32[4,8,1536]{2,1,0:T(8,128)S(1)} %get-tuple-element.65), channel_id=1, source_target_pairs={{0,4},{4,0},{8,12},{12,8},{16,20},{20,16},{24,28},{28,24},{1,5},{5... | collective-permute-start | bytes 589832 | tf_op jit(solution)/shard_map/ppermute | solution.py:338
  49.9 1.9 %collective-permute-start.14 = (f32[16,768]{1,0:T(8,128)S(1)}, f32[16,768]{1,0:T(8,128)S(1)}, u32[]{:S(2)}, u32[]{:S(2)}) collective-permute-start(f32[16,768]{1,0:T(8,128)S(1)} %get-tuple-element.60), channel_id=1, source_target_pairs={{0,1},{1,0},{2,3},{3,2},{4,5},{5,4},{6,7},{7,6},{8,9},{9,8},{10,11... | collective-permute-start | bytes 147464 | tf_op jit(solution)/shard_map/ppermute | solution.py:338
  49.9 4.5 %collective-permute-start.15 = (f32[16,768]{1,0:T(8,128)S(1)}, f32[16,768]{1,0:T(8,128)S(1)}, u32[]{:S(2)}, u32[]{:S(2)}) collective-permute-start(f32[16,768]{1,0:T(8,128)S(1)} %get-tuple-element.61), channel_id=1, source_target_pairs={{0,2},{1,3},{2,0},{3,1},{4,6},{5,7},{6,4},{7,5},{8,10},{9,11},{10,... | collective-permute-start | bytes 147464 | tf_op jit(solution)/shard_map/ppermute | solution.py:338
  50.5 4.2 %collective-permute-start.16 = (f32[16,768]{1,0:T(8,128)S(1)}, f32[16,768]{1,0:T(8,128)S(1)}, u32[]{:S(2)}, u32[]{:S(2)}) collective-permute-start(f32[16,768]{1,0:T(8,128)S(1)} %get-tuple-element.62), channel_id=1, source_target_pairs={{0,3},{1,2},{2,1},{3,0},{4,7},{5,6},{6,5},{7,4},{8,11},{9,10},{10,... | collective-permute-start | bytes 147464 | tf_op jit(solution)/shard_map/ppermute | solution.py:338
  56.3 4.5 %collective-permute-start.18 = (f32[8,1792]{1,0:T(8,128)S(1)}, f32[8,1792]{1,0:T(8,128)S(1)}, u32[]{:S(2)}, u32[]{:S(2)}) collective-permute-start(f32[8,1792]{1,0:T(8,128)S(1)} %get-tuple-element.68), channel_id=1, source_target_pairs={{0,8},{4,12},{8,0},{12,4},{16,24},{20,28},{24,16},{28,20},{1,9},{5... | collective-permute-start | bytes 172040 | tf_op jit(solution)/shard_map/ppermute | solution.py:338
  56.8 6.4 %collective-permute-start.19 = (f32[8,1792]{1,0:T(8,128)S(1)}, f32[8,1792]{1,0:T(8,128)S(1)}, u32[]{:S(2)}, u32[]{:S(2)}) collective-permute-start(f32[8,1792]{1,0:T(8,128)S(1)} %get-tuple-element.69), channel_id=1, source_target_pairs={{0,16},{4,20},{8,24},{12,28},{16,0},{20,4},{24,8},{28,12},{1,17},{... | collective-permute-start | bytes 172040 | tf_op jit(solution)/shard_map/ppermute | solution.py:338
  58.3 6.1 %collective-permute-start.20 = (f32[8,1792]{1,0:T(8,128)S(1)}, f32[8,1792]{1,0:T(8,128)S(1)}, u32[]{:S(2)}, u32[]{:S(2)}) collective-permute-start(f32[8,1792]{1,0:T(8,128)S(1)} %get-tuple-element.70), channel_id=1, source_target_pairs={{0,24},{4,28},{8,16},{12,20},{16,8},{20,12},{24,0},{28,4},{1,25},{... | collective-permute-start | bytes 172040 | tf_op jit(solution)/shard_map/ppermute | solution.py:338
  64.4 6.1 %collective-permute-start.23 = (f32[8,1792]{1,0:T(8,128)S(1)}, f32[8,1792]{1,0:T(8,128)S(1)}, u32[]{:S(2)}, u32[]{:S(2)}) collective-permute-start(f32[8,1792]{1,0:T(8,128)S(1)} %replica_mean.3.refs_0_), channel_id=1, source_target_pairs={{0,24},{4,28},{8,16},{12,20},{16,8},{20,12},{24,0},{28,4},{1,25},{... | collective-permute-start | bytes 172040 | tf_op jit(solution)/shard_map/ppermute | solution.py:338
  66.8 5.1 %collective-permute-start.22 = (f32[8,1792]{1,0:T(8,128)S(1)}, f32[8,1792]{1,0:T(8,128)S(1)}, u32[]{:S(2)}, u32[]{:S(2)}) collective-permute-start(f32[8,1792]{1,0:T(8,128)S(1)} %replica_mean.3.refs_0_), channel_id=1, source_target_pairs={{0,16},{4,20},{8,24},{12,28},{16,0},{20,4},{24,8},{28,12},{1,17},{... | collective-permute-start | bytes 172040 | tf_op jit(solution)/shard_map/ppermute | solution.py:338
  66.8 5.1 %collective-permute-start.21 = (f32[8,1792]{1,0:T(8,128)S(1)}, f32[8,1792]{1,0:T(8,128)S(1)}, u32[]{:S(2)}, u32[]{:S(2)}) collective-permute-start(f32[8,1792]{1,0:T(8,128)S(1)} %replica_mean.3.refs_0_), channel_id=1, source_target_pairs={{0,8},{4,12},{8,0},{12,4},{16,24},{20,28},{24,16},{28,20},{1,9},{5... | collective-permute-start | bytes 172040 | tf_op jit(solution)/shard_map/ppermute | solution.py:338
  71.9 6.1 %collective-permute-start.24 = (f32[4,8,1792]{2,1,0:T(8,128)S(1)}, f32[4,8,1792]{2,1,0:T(8,128)S(1)}, u32[]{:S(2)}, u32[]{:S(2)}) collective-permute-start(f32[4,8,1792]{2,1,0:T(8,128)S(1)} %stack_z.3.refs_4_.mine), channel_id=1, source_target_pairs={{0,4},{4,0},{8,12},{12,8},{16,20},{20,16},{24,28},{28,24},{1,5},{5... | collective-permute-start | bytes 688136 | tf_op jit(solution)/shard_map/ppermute | solution.py:338
  78.7 4.3 %collective-permute-start.27 = (f32[16,640]{1,0:T(8,128)S(1)}, f32[16,640]{1,0:T(8,128)S(1)}, u32[]{:S(2)}, u32[]{:S(2)}) collective-permute-start(f32[16,640]{1,0:T(8,128)S(1)} %get-tuple-element.76.refs_0_), channel_id=1, source_target_pairs={{0,3},{1,2},{2,1},{3,0},{4,7},{5,6},{6,5},{7,4},{8,11},{9,10},{10,... | collective-permute-start | bytes 122888 | tf_op jit(solution)/shard_map/ppermute | solution.py:338
  78.8 4.4 %collective-permute-start.26 = (f32[16,640]{1,0:T(8,128)S(1)}, f32[16,640]{1,0:T(8,128)S(1)}, u32[]{:S(2)}, u32[]{:S(2)}) collective-permute-start(f32[16,640]{1,0:T(8,128)S(1)} %get-tuple-element.76.refs_0_), channel_id=1, source_target_pairs={{0,2},{1,3},{2,0},{3,1},{4,6},{5,7},{6,4},{7,5},{8,10},{9,11},{10,... | collective-permute-start | bytes 122888 | tf_op jit(solution)/shard_map/ppermute | solution.py:338
  79.7 3.5 %collective-permute-start.25 = (f32[16,640]{1,0:T(8,128)S(1)}, f32[16,640]{1,0:T(8,128)S(1)}, u32[]{:S(2)}, u32[]{:S(2)}) collective-permute-start(f32[16,640]{1,0:T(8,128)S(1)} %get-tuple-element.76.refs_0_), channel_id=1, source_target_pairs={{0,1},{1,0},{2,3},{3,2},{4,5},{5,4},{6,7},{7,6},{8,9},{9,8},{10,11... | collective-permute-start | bytes 122888 | tf_op jit(solution)/shard_map/ppermute | solution.py:338

commit v10 on v9

--- a/solution.py
+++ b/solution.py
@@ -12,7 +12,6 @@
 HIGHEST = lax.Precision.HIGHEST
 CLIP_RMS = 0.1
 STEPS = 4
-LEFT_STEPS = 2
 MIB = 1024 * 1024
 NT = ((1,), (1,))
 
@@ -92,34 +91,41 @@
 def left_kernel(n_shards, gu, eu, qu, gd, ed, qd, *refs):
     *outs, gu_in, eu_in, qu_in, pieces_up, total_up, gd_in, ed_in, qd_in, pieces_down, total_down, stage, q_sems, sems = refs
     up, down = (qu_in, pieces_up, total_up), (qd_in, pieces_down, total_down)
-    firsts = [pltpu.make_async_copy(src, dst, q_sems.at[i]) for i, (src, dst) in enumerate(((qu, qu_in), (qd, qd_in)))]
-    for first in firsts:
-        first.start()
+    firsts = [pltpu.make_async_copy(src, dst, q_sems.at[i]) for i, (src, dst) in enumerate(((qd, qd_in), (qu, qu_in)))]
     stages = []
-    for g, e, g_in, e_in, part in ((gu, eu, gu_in, eu_in, up), (gd, ed, gd_in, ed_in, down)):
-        block = g_in.shape[0] // LEFT_STEPS
-        for i in range(LEFT_STEPS):
+    for g, e, g_in, e_in, part, count in ((gd, ed, gd_in, ed_in, down, 3), (gu, eu, gu_in, eu_in, up, 2)):
+        block = g_in.shape[0] // count
+        for i in range(count):
             rows = pl.ds(i * block, block)
             n = len(stages)
             copies = [pltpu.make_async_copy(src.at[0, rows, :], dst.at[rows, :], sems.at[n, k]) for k, (src, dst) in enumerate(((g, g_in), (e, e_in)))]
-            for copy in copies:
+            stages.append((copies, g_in, e_in, slice(i * block, (i + 1) * block), part))
+
+    def fetch(n):
+        if n < len(stages):
+            for copy in stages[n][0]:
                 copy.start()
-            stages.append((copies, g_in, e_in, slice(i * block, (i + 1) * block), part))
-    for first, (q, pieces, _) in zip(firsts, (up, down)):
+
+    firsts[0].start()
+    fetch(0)
+    firsts[1].start()
+    for n, (first, (q, pieces, _)) in enumerate(zip(firsts, (down, up))):
         first.wait()
-        rank = q.shape[0]
-        for i, piece in enumerate(split3(q[...].T)):
-            pieces[:, i * rank : (i + 1) * rank] = piece
-        pieces[:, 3 * rank :] = jnp.zeros((q.shape[1], rank), BF16)
-    for copies, g, e, rows, (q, pieces, total) in stages:
-        rank = q.shape[0]
+        fetch(n + 1)
+        split_rows(q, pieces)
+    for n, (copies, g, e, rows, (_, pieces, total)) in enumerate(stages):
         for copy in copies:
             copy.wait()
-        t = dot(g[rows, :], pieces[...]) + dot(e[rows, :], pieces[...])
-        t = (t[:, : 2 * rank] + t[:, 2 * rank :]).T
-        total[:, rows] = t[:rank] + t[rank:]
+        fetch(n + 3)
+        total[:, rows] = add_pieces(dot(pieces[...], g[rows, :], NT) + dot(pieces[...], e[rows, :], NT))
     split_shards(total_up, None, outs[:n_shards])
     split_replicas(total_down, stage, *outs[n_shards:])
+
+
+def fetch_kernel(*refs):
+    half = len(refs) // 2
+    for source, out in zip(refs[:half], refs[half:]):
+        out[...] = source[...]
 
 
 def sum_shards_kernel(n_shards, *refs):
@@ -129,14 +135,8 @@
     gram[...] = unfold(total[:, out.shape[1] :], gram.shape[0])
 
 
-def first_shards_kernel(n_shards, own, kept, *refs):
-    *others, out, copy, own_in, sems = refs
-    copies = [pltpu.make_async_copy(own, own_in, sems.at[0]), pltpu.make_async_copy(kept, copy, sems.at[1])]
-    for each in copies:
-        each.start()
-    for each in copies:
-        each.wait()
-    out[...] = tree_sum([own_in[...]] + [term[...] for term in others])
+def first_shards_kernel(*refs):
+    refs[-1][...] = tree_sum(term[...] for term in refs[:-1])
 
 
 def split_z_kernel(keep, got, shard, *refs):
@@ -373,20 +373,18 @@
     product = 4 * rows * ff * 4 * rank
 
     buffers = [
-        [pltpu.VMEM(g.shape[1:], BF16)] * 2 + [pltpu.VMEM(q.shape, F32), pltpu.VMEM((q.shape[1], 4 * rank), BF16), total]
+        [pltpu.VMEM(g.shape[1:], BF16)] * 2 + [pltpu.VMEM(q.shape, F32), pltpu.VMEM((3 * rank, q.shape[1]), BF16), total]
         for g, q, total in ((gu, qu, narrow), (gd, qd, wide))
     ]
     *parts, keep, send = call(
         functools.partial(left_kernel, n_shards), [shard_rows_here] * n_shards + [replica_half] * 2, gu, eu, qu, gd, ed, qd,
         name="left", flops=2 * product, limit=61, in_specs=[pl.BlockSpec(memory_space=pltpu.HBM)] * 6,
-        scratch_shapes=buffers[0] + buffers[1] + [stage, pltpu.SemaphoreType.DMA((2,)), pltpu.SemaphoreType.DMA((2 * LEFT_STEPS, 2))],
+        scratch_shapes=buffers[0] + buffers[1] + [stage, pltpu.SemaphoreType.DMA((2,)), pltpu.SemaphoreType.DMA((5, 2))],
     )
     got = swap(send, "dp", 1)
-    shard, keep = call(
-        functools.partial(first_shards_kernel, n_shards), [shard_rows_here, replica_half], parts[0], keep, *from_shards(parts)[1:],
-        name="shard_sum", in_specs=[pl.BlockSpec(memory_space=pltpu.HBM)] * 2 + [VMEM] * (n_shards - 1),
-        scratch_shapes=[pltpu.VMEM((rows_here, rows), F32), pltpu.SemaphoreType.DMA((2,))],
-    )
+    parts = from_shards(parts)
+    parts[0], keep = call(fetch_kernel, [shard_rows_here, replica_half], parts[0], keep, name="fetch", flops=product // 4)
+    shard = call(first_shards_kernel, shard_rows_here, *parts, name="shard_sum")
     mine, other = mean_replicas(keep, got, shard)
 
     shard = call(functools.partial(shard_rows_kernel, ff), shard_rows_here, mine, other, name="shard_rows")

time: 86.8 us -> 83 us (0.956)
  waiting for transfers between devices: 32.9 us -> 29.4 us
  Pallas kernels: 20.8 us -> 18.5 us
  starting transfers between devices: 30.4 us -> 32.4 us
    ppermute x28, waiting for transfers between devices: 32.9 us -> 29.4 us  [swap(): return lax.ppermute(x, axis, pairs)]
    pallas_call x17 -> x18, Pallas kernels: 20.8 us -> 18.5 us  [call(): pl.pallas_call(kernel, out_shape=out_shape, compiler_params=params, cost_...]
    ppermute x28, starting transfers between devices: 30.4 us -> 32.4 us  [swap(): return lax.ppermute(x, axis, pairs)]
  transfers between devices with their start and end apart: 28 -> 28, of which waited for: 18 -> 17; matrix products, arithmetic and copies ran while one was open for 0% -> 0% of each run, Pallas kernels for 8% -> 8%
where the time goes in v10:
time: 83 us; the launch traced here: 82.8 us
  starting transfers between devices  32.4 us (39%)
  waiting for transfers between devices  29.4 us (35%)
  Pallas kernels  18.5 us (22%)
  local copies, waits for them, and re-layouts  1.7 us (2%)
    ppermute x28, starting transfers between devices, swap(): return lax.ppermute(x, axis, pairs)  32.4 us
    ppermute x28, waiting for transfers between devices, swap(): return lax.ppermute(x, axis, pairs)  29.4 us
    pallas_call x18, Pallas kernels, call(): pl.pallas_call(kernel, out_shape=out_shape, compiler_params=params, cost_...  18.5 us
    unnamed x12, local copies, waits for them, and re-layouts  1.7 us
  transfers between devices with their start and end apart: 28, of which 17 were waited for; matrix products, arithmetic and copies ran while one was open for 0% of the time, Pallas kernels for 8%

profile of v10, /device:TPU:0, one launch (start us, length us, event | category | flops | bytes accessed | tf_op | source)
XLA Modules:
  0.0 82.8 jit_solution(1318245783743097842)
XLA Ops:
  0.6 6.2 %left.1 = (f32[16,512]{1,0:T(8,128)}, f32[16,512]{1,0:T(8,128)}, f32[16,512]{1,0:T(8,128)}, f32[16,512]{1,0:T(8,128)}, f32[4,8,1536]{2,1,0:T(8,128)}, /*index=5*/f32[4,8,1536]{2,1,0:T(8,128)}) custom-call(bf16[1,512,1536]{2,1,0:T(8,128)(2,1)} %g.4, bf16[1,512,1536]{2,1,0:T(8,128)(2,1)} %e.4, f32[64,1536]{1,0:T(8,128)} %bitcast.2, bf16[1,1536,512]{2,1,0:T(8,128)(2,1)} %g.5, ...), custom_call_target="tpu_custom_call" | custom-call | flops 1610612736 | bytes 7340032 | tf_op jit(solution)/shard_map/left/pallas_call | solution.py:333
  6.8 0.0 copy-start.2
  6.8 3.0 %collective-permute-start = (f32[4,8,1536]{2,1,0:T(8,128)}, f32[4,8,1536]{2,1,0:T(8,128)S(1)}, u32[]{:S(2)}, u32[]{:S(2)}) collective-permute-start(f32[4,8,1536]{2,1,0:T(8,128)} %get-tuple-element.47), channel_id=1, source_target_pairs={{0,4},{4,0},{8,12},{12,8},{16,20},{20,16},{24,28},{28,24},{1,5},{5... | collective-permute-start | bytes 589832 | tf_op jit(solution)/shard_map/ppermute | solution.py:338
  9.9 0.0 collective-permute-start.1
  9.9 1.5 %collective-permute-start.2 = (f32[16,512]{1,0:T(8,128)}, f32[16,512]{1,0:T(8,128)S(1)}, u32[]{:S(2)}, u32[]{:S(2)}) collective-permute-start(f32[16,512]{1,0:T(8,128)} %get-tuple-element.50), channel_id=1, source_target_pairs={{0,2},{1,3},{2,0},{3,1},{4,6},{5,7},{6,4},{7,5},{8,10},{9,11},{10,... | collective-permute-start | bytes 98312 | tf_op jit(solution)/shard_map/ppermute | solution.py:338
  11.4 0.4 collective-permute-start.3
  11.7 0.9 %copy-done.4 = f32[4,8,1536]{2,1,0:T(8,128)S(1)} copy-done((f32[4,8,1536]{2,1,0:T(8,128)S(1)}, f32[4,8,1536]{2,1,0:T(8,128)}, u32[]{:S(2)}) %copy-start.4) | copy-done | bytes 196632
  12.7 0.8 copy-done.5
  13.4 0.0 collective-permute-done.1.refs_1_
  13.5 0.6 collective-permute-done.2.refs_2_
  14.0 0.9 %collective-permute-done.3.refs_3_ = f32[16,512]{1,0:T(8,128)S(1)} collective-permute-done((f32[16,512]{1,0:T(8,128)}, f32[16,512]{1,0:T(8,128)S(1)}, u32[]{:S(2)}, u32[]{:S(2)}) %collective-permute-start.3) | collective-permute-done | bytes 32800 | tf_op jit(solution)/shard_map/ppermute | solution.py:338
  14.9 0.1 collective-permute-done.got
  15.0 1.9 %collective-permute-start.4 = (f32[8,1792]{1,0:T(8,128)S(1)}, f32[8,1792]{1,0:T(8,128)S(1)}, u32[]{:S(2)}, u32[]{:S(2)}) collective-permute-start(f32[8,1792]{1,0:T(8,128)S(1)} %get-tuple-element.53), channel_id=1, source_target_pairs={{0,8},{4,12},{8,0},{12,4},{16,24},{20,28},{24,16},{28,20},{1,9},{5... | collective-permute-start | bytes 172040 | tf_op jit(solution)/shard_map/ppermute | solution.py:338
  16.9 2.6 %collective-permute-start.5 = (f32[8,1792]{1,0:T(8,128)S(1)}, f32[8,1792]{1,0:T(8,128)S(1)}, u32[]{:S(2)}, u32[]{:S(2)}) collective-permute-start(f32[8,1792]{1,0:T(8,128)S(1)} %get-tuple-element.54), channel_id=1, source_target_pairs={{0,16},{4,20},{8,24},{12,28},{16,0},{20,4},{24,8},{28,12},{1,17},{... | collective-permute-start | bytes 172040 | tf_op jit(solution)/shard_map/ppermute | solution.py:338
  19.5 0.0 collective-permute-start.6
  19.5 0.0 collective-permute-done.4.refs_1_
  19.5 3.8 %collective-permute-done.5.refs_2_ = f32[8,1792]{1,0:T(8,128)S(1)} collective-permute-done((f32[8,1792]{1,0:T(8,128)S(1)}, f32[8,1792]{1,0:T(8,128)S(1)}, u32[]{:S(2)}, u32[]{:S(2)}) %collective-permute-start.5) | collective-permute-done | bytes 57376 | tf_op jit(solution)/shard_map/ppermute | solution.py:338
  23.3 2.2 %collective-permute-done.6.refs_3_ = f32[8,1792]{1,0:T(8,128)S(1)} collective-permute-done((f32[8,1792]{1,0:T(8,128)S(1)}, f32[8,1792]{1,0:T(8,128)S(1)}, u32[]{:S(2)}, u32[]{:S(2)}) %collective-permute-start.6) | collective-permute-done | bytes 57376 | tf_op jit(solution)/shard_map/ppermute | solution.py:338
  25.5 1.6 %collective-permute-start.9 = (f32[8,1792]{1,0:T(8,128)S(1)}, f32[8,1792]{1,0:T(8,128)S(1)}, u32[]{:S(2)}, u32[]{:S(2)}) collective-permute-start(f32[8,1792]{1,0:T(8,128)S(1)} %replica_mean.2.refs_0_), channel_id=1, source_target_pairs={{0,24},{4,28},{8,16},{12,20},{16,8},{20,12},{24,0},{28,4},{1,25},{... | collective-permute-start | bytes 172040 | tf_op jit(solution)/shard_map/ppermute | solution.py:338
  27.1 0.0 collective-permute-start.8
  27.1 2.8 %collective-permute-start.7 = (f32[8,1792]{1,0:T(8,128)S(1)}, f32[8,1792]{1,0:T(8,128)S(1)}, u32[]{:S(2)}, u32[]{:S(2)}) collective-permute-start(f32[8,1792]{1,0:T(8,128)S(1)} %replica_mean.2.refs_0_), channel_id=1, source_target_pairs={{0,8},{4,12},{8,0},{12,4},{16,24},{20,28},{24,16},{28,20},{1,9},{5... | collective-permute-start | bytes 172040 | tf_op jit(solution)/shard_map/ppermute | solution.py:338
  29.9 1.6 %collective-permute-done.9.refs_3_ = f32[8,1792]{1,0:T(8,128)S(1)} collective-permute-done((f32[8,1792]{1,0:T(8,128)S(1)}, f32[8,1792]{1,0:T(8,128)S(1)}, u32[]{:S(2)}, u32[]{:S(2)}) %collective-permute-start.9) | collective-permute-done | bytes 57376 | tf_op jit(solution)/shard_map/ppermute | solution.py:338
  31.5 1.2 %collective-permute-done.8.refs_2_ = f32[8,1792]{1,0:T(8,128)S(1)} collective-permute-done((f32[8,1792]{1,0:T(8,128)S(1)}, f32[8,1792]{1,0:T(8,128)S(1)}, u32[]{:S(2)}, u32[]{:S(2)}) %collective-permute-start.8) | collective-permute-done | bytes 57376 | tf_op jit(solution)/shard_map/ppermute | solution.py:338
  32.8 1.4 %collective-permute-start.10 = (f32[4,8,1792]{2,1,0:T(8,128)S(1)}, f32[4,8,1792]{2,1,0:T(8,128)S(1)}, u32[]{:S(2)}, u32[]{:S(2)}) collective-permute-start(f32[4,8,1792]{2,1,0:T(8,128)S(1)} %stack_z.2.mine), channel_id=1, source_target_pairs={{0,4},{4,0},{8,12},{12,8},{16,20},{20,16},{24,28},{28,24},{1,5},{5... | collective-permute-start | bytes 688136 | tf_op jit(solution)/shard_map/ppermute | solution.py:338
  34.2 4.7 %collective-permute-done.10.other = f32[4,8,1792]{2,1,0:T(8,128)S(1)} collective-permute-done((f32[4,8,1792]{2,1,0:T(8,128)S(1)}, f32[4,8,1792]{2,1,0:T(8,128)S(1)}, u32[]{:S(2)}, u32[]{:S(2)}) %collective-permute-start.10) | collective-permute-done | bytes 229408 | tf_op jit(solution)/shard_map/ppermute | solution.py:338
  38.9 0.0 copy-start.1
  38.9 0.1 collective-permute-start.13
  39.0 1.6 %collective-permute-start.12 = (f32[16,512]{1,0:T(8,128)S(1)}, f32[16,512]{1,0:T(8,128)S(1)}, u32[]{:S(2)}, u32[]{:S(2)}) collective-permute-start(f32[16,512]{1,0:T(8,128)S(1)} %shard_rows.1.refs_0_), channel_id=1, source_target_pairs={{0,2},{1,3},{2,0},{3,1},{4,6},{5,7},{6,4},{7,5},{8,10},{9,11},{10,... | collective-permute-start | bytes 98312 | tf_op jit(solution)/shard_map/ppermute | solution.py:338
  40.6 0.2 collective-permute-start.11
  40.8 1.2 %right_down.1 = (f32[64,1536]{1,0:T(8,128)S(1)}, f32[16,768]{1,0:T(8,128)S(1)}, f32[16,768]{1,0:T(8,128)S(1)}, f32[16,768]{1,0:T(8,128)S(1)}, f32[16,768]{1,0:T(8,128)S(1)}) custom-call(f32[4,8,1792]{2,1,0:T(8,128)S(1)} %stack_z.2.mine, f32[4,8,1792]{2,1,0:T(8,128)S(1)} %collective-permute-done.10.other, bf16[1,1536,512]{2,1,0:T(8,128)(2,1)S(1)} %copy-done.2, ...), custom_call_target="tpu_custom_call" | custom-call | flops 805306368 | bytes 4194304 | tf_op jit(solution)/shard_map/right_down/pallas_call | solution.py:333
  42.0 0.6 collective-permute-done.13.refs_3_
  42.6 0.4 collective-permute-done.12.refs_2_
  43.0 1.2 %right_up.1 = (f32[64,512]{1,0:T(8,128)S(1)}, f32[64,64]{1,0:T(8,128)S(1)}, f32[4,8,1536]{2,1,0:T(8,128)S(1)}, f32[4,8,1536]{2,1,0:T(8,128)S(1)}) custom-call(f32[16,512]{1,0:T(8,128)S(1)} %shard_rows.1.refs_0_, f32[16,512]{1,0:T(8,128)S(1)} %collective-permute-done.11.refs_1_, f32[16,512]{1,0:T(8,128)S(1)} %collective-permute-done.12.refs_2_, ...), custom_call_target="tpu_custom_call" | custom-call | flops 805306368 | bytes 4210688 | tf_op jit(solution)/shard_map/right_up/pallas_call | solution.py:333
  44.2 1.4 %collective-permute-start.17 = (f32[4,8,1536]{2,1,0:T(8,128)S(1)}, f32[4,8,1536]{2,1,0:T(8,128)S(1)}, u32[]{:S(2)}, u32[]{:S(2)}) collective-permute-start(f32[4,8,1536]{2,1,0:T(8,128)S(1)} %get-tuple-element.65), channel_id=1, source_target_pairs={{0,4},{4,0},{8,12},{12,8},{16,20},{20,16},{24,28},{28,24},{1,5},{5... | collective-permute-start | bytes 589832 | tf_op jit(solution)/shard_map/ppermute | solution.py:338
  45.6 0.1 collective-permute-start.14
  45.7 1.4 %collective-permute-start.15 = (f32[16,768]{1,0:T(8,128)S(1)}, f32[16,768]{1,0:T(8,128)S(1)}, u32[]{:S(2)}, u32[]{:S(2)}) collective-permute-start(f32[16,768]{1,0:T(8,128)S(1)} %get-tuple-element.61), channel_id=1, source_target_pairs={{0,2},{1,3},{2,0},{3,1},{4,6},{5,7},{6,4},{7,5},{8,10},{9,11},{10,... | collective-permute-start | bytes 147464 | tf_op jit(solution)/shard_map/ppermute | solution.py:338
  47.1 0.4 collective-permute-start.16
  47.5 0.0 collective-permute-done.14.refs_1_
  47.5 2.3 %collective-permute-done.15.refs_2_ = f32[16,768]{1,0:T(8,128)S(1)} collective-permute-done((f32[16,768]{1,0:T(8,128)S(1)}, f32[16,768]{1,0:T(8,128)S(1)}, u32[]{:S(2)}, u32[]{:S(2)}) %collective-permute-start.15) | collective-permute-done | bytes 49184 | tf_op jit(solution)/shard_map/ppermute | solution.py:338
  49.8 1.1 %collective-permute-done.16.refs_3_ = f32[16,768]{1,0:T(8,128)S(1)} collective-permute-done((f32[16,768]{1,0:T(8,128)S(1)}, f32[16,768]{1,0:T(8,128)S(1)}, u32[]{:S(2)}, u32[]{:S(2)}) %collective-permute-start.16) | collective-permute-done | bytes 49184 | tf_op jit(solution)/shard_map/ppermute | solution.py:338
  50.9 0.1 shard_sum.3
  50.9 0.5 collective-permute-done.17.got
  51.5 1.4 %collective-permute-start.18 = (f32[8,1792]{1,0:T(8,128)S(1)}, f32[8,1792]{1,0:T(8,128)S(1)}, u32[]{:S(2)}, u32[]{:S(2)}) collective-permute-start(f32[8,1792]{1,0:T(8,128)S(1)} %get-tuple-element.68), channel_id=1, source_target_pairs={{0,8},{4,12},{8,0},{12,4},{16,24},{20,28},{24,16},{28,20},{1,9},{5... | collective-permute-start | bytes 172040 | tf_op jit(solution)/shard_map/ppermute | solution.py:338
  52.9 1.0 %collective-permute-start.19 = (f32[8,1792]{1,0:T(8,128)S(1)}, f32[8,1792]{1,0:T(8,128)S(1)}, u32[]{:S(2)}, u32[]{:S(2)}) collective-permute-start(f32[8,1792]{1,0:T(8,128)S(1)} %get-tuple-element.69), channel_id=1, source_target_pairs={{0,16},{4,20},{8,24},{12,28},{16,0},{20,4},{24,8},{28,12},{1,17},{... | collective-permute-start | bytes 172040 | tf_op jit(solution)/shard_map/ppermute | solution.py:338
  53.9 2.1 %collective-permute-start.20 = (f32[8,1792]{1,0:T(8,128)S(1)}, f32[8,1792]{1,0:T(8,128)S(1)}, u32[]{:S(2)}, u32[]{:S(2)}) collective-permute-start(f32[8,1792]{1,0:T(8,128)S(1)} %get-tuple-element.70), channel_id=1, source_target_pairs={{0,24},{4,28},{8,16},{12,20},{16,8},{20,12},{24,0},{28,4},{1,25},{... | collective-permute-start | bytes 172040 | tf_op jit(solution)/shard_map/ppermute | solution.py:338
  56.0 0.0 collective-permute-done.18.refs_1_
  56.0 4.5 %collective-permute-done.19.refs_2_ = f32[8,1792]{1,0:T(8,128)S(1)} collective-permute-done((f32[8,1792]{1,0:T(8,128)S(1)}, f32[8,1792]{1,0:T(8,128)S(1)}, u32[]{:S(2)}, u32[]{:S(2)}) %collective-permute-start.19) | collective-permute-done | bytes 57376 | tf_op jit(solution)/shard_map/ppermute | solution.py:338
  60.5 1.6 %collective-permute-start.23 = (f32[8,1792]{1,0:T(8,128)S(1)}, f32[8,1792]{1,0:T(8,128)S(1)}, u32[]{:S(2)}, u32[]{:S(2)}) collective-permute-start(f32[8,1792]{1,0:T(8,128)S(1)} %replica_mean.3.refs_0_), channel_id=1, source_target_pairs={{0,24},{4,28},{8,16},{12,20},{16,8},{20,12},{24,0},{28,4},{1,25},{... | collective-permute-start | bytes 172040 | tf_op jit(solution)/shard_map/ppermute | solution.py:338
  62.1 1.1 %collective-permute-start.22 = (f32[8,1792]{1,0:T(8,128)S(1)}, f32[8,1792]{1,0:T(8,128)S(1)}, u32[]{:S(2)}, u32[]{:S(2)}) collective-permute-start(f32[8,1792]{1,0:T(8,128)S(1)} %replica_mean.3.refs_0_), channel_id=1, source_target_pairs={{0,16},{4,20},{8,24},{12,28},{16,0},{20,4},{24,8},{28,12},{1,17},{... | collective-permute-start | bytes 172040 | tf_op jit(solution)/shard_map/ppermute | solution.py:338
  63.2 1.7 %collective-permute-start.21 = (f32[8,1792]{1,0:T(8,128)S(1)}, f32[8,1792]{1,0:T(8,128)S(1)}, u32[]{:S(2)}, u32[]{:S(2)}) collective-permute-start(f32[8,1792]{1,0:T(8,128)S(1)} %replica_mean.3.refs_0_), channel_id=1, source_target_pairs={{0,8},{4,12},{8,0},{12,4},{16,24},{20,28},{24,16},{28,20},{1,9},{5... | collective-permute-start | bytes 172040 | tf_op jit(solution)/shard_map/ppermute | solution.py:338
  65.0 1.7 %collective-permute-done.23.refs_3_ = f32[8,1792]{1,0:T(8,128)S(1)} collective-permute-done((f32[8,1792]{1,0:T(8,128)S(1)}, f32[8,1792]{1,0:T(8,128)S(1)}, u32[]{:S(2)}, u32[]{:S(2)}) %collective-permute-start.23) | collective-permute-done | bytes 57376 | tf_op jit(solution)/shard_map/ppermute | solution.py:338
  66.7 1.4 %collective-permute-done.22.refs_2_ = f32[8,1792]{1,0:T(8,128)S(1)} collective-permute-done((f32[8,1792]{1,0:T(8,128)S(1)}, f32[8,1792]{1,0:T(8,128)S(1)}, u32[]{:S(2)}, u32[]{:S(2)}) %collective-permute-start.22) | collective-permute-done | bytes 57376 | tf_op jit(solution)/shard_map/ppermute | solution.py:338
  68.0 0.0 collective-permute-done.21.refs_1_
  68.1 1.0 %collective-permute-start.24 = (f32[4,8,1792]{2,1,0:T(8,128)S(1)}, f32[4,8,1792]{2,1,0:T(8,128)S(1)}, u32[]{:S(2)}, u32[]{:S(2)}) collective-permute-start(f32[4,8,1792]{2,1,0:T(8,128)S(1)} %stack_z.3.refs_4_.mine), channel_id=1, source_target_pairs={{0,4},{4,0},{8,12},{12,8},{16,20},{20,16},{24,28},{28,24},{1,5},{5... | collective-permute-start | bytes 688136 | tf_op jit(solution)/shard_map/ppermute | solution.py:338
  69.0 3.2 %basis.1 = (f32[64,64]{1,0:T(8,128)S(1)}, f32[64,64]{1,0:T(8,128)S(1)}, bf16[512,256]{1,0:T(8,128)(2,1)S(1)}, bf16[1536,256]{1,0:T(8,128)(2,1)S(1)}) custom-call(f32[64,512]{1,0:T(8,128)S(1)} %get-tuple-element.57.left_up, f32[64,1536]{1,0:T(8,128)S(1)} %get-tuple-element.56.refs_6_.left_down, f32[64,64]{1,0:T(8,128)S(1)} %get-tuple-element.58.gram_up, ...), custom_call_target="tpu_custom_call" | custom-call | bytes 8159232 | tf_op jit(solution)/shard_map/basis/pallas_call | solution.py:333
  72.2 1.9 %collective-permute-done.24.other = f32[4,8,1792]{2,1,0:T(8,128)S(1)} collective-permute-done((f32[4,8,1792]{2,1,0:T(8,128)S(1)}, f32[4,8,1792]{2,1,0:T(8,128)S(1)}, u32[]{:S(2)}, u32[]{:S(2)}) %collective-permute-start.24) | collective-permute-done | bytes 229408 | tf_op jit(solution)/shard_map/ppermute | solution.py:338
  74.2 0.7 factor_up.1
  74.8 0.1 collective-permute-start.27
  74.9 2.0 %collective-permute-start.26 = (f32[16,640]{1,0:T(8,128)S(1)}, f32[16,640]{1,0:T(8,128)S(1)}, u32[]{:S(2)}, u32[]{:S(2)}) collective-permute-start(f32[16,640]{1,0:T(8,128)S(1)} %get-tuple-element.76.refs_0_), channel_id=1, source_target_pairs={{0,2},{1,3},{2,0},{3,1},{4,6},{5,7},{6,4},{7,5},{8,10},{9,11},{10,... | collective-permute-start | bytes 122888 | tf_op jit(solution)/shard_map/ppermute | solution.py:338
  76.9 0.0 collective-permute-start.25
  77.0 2.3 %error_up.1 = (bf16[1,512,1536]{2,1,0:T(8,128)(2,1)}, f32[8,128]{1,0:T(8,128)S(1)}) custom-call(bf16[1,512,1536]{2,1,0:T(8,128)(2,1)S(1)} %copy-done, bf16[1,512,1536]{2,1,0:T(8,128)(2,1)S(1)} %copy-done.1, bf16[512,256]{1,0:T(8,128)(2,1)S(1)} %get-tuple-element.71.lhs.lhs_up, bf16[256,1536]{1,0:T(8,128)(2,1)S(1)} %get-tuple-element.73.rhs.rhs_up), custom_call_target="tpu_custom_call" | custom-call | flops 402653184 | bytes 5771264 | tf_op jit(solution)/shard_map/error_up/pallas_call | solution.py:333
  79.3 0.0 collective-permute-done.27.refs_3_
  79.3 0.4 factor_down.1
  79.7 3.0 %last.1 = (bf16[1,1536,512]{2,1,0:T(8,128)(2,1)}, bf16[512,1536]{1,0:T(8,128)(2,1)}, bf16[1536,512]{1,0:T(8,128)(2,1)}) custom-call(bf16[1,1536,512]{2,1,0:T(8,128)(2,1)S(1)} %copy-done.2, bf16[1,1536,512]{2,1,0:T(8,128)(2,1)S(1)} %copy-done.3, bf16[512,256]{1,0:T(8,128)(2,1)S(1)} %get-tuple-element.71.lhs.lhs_up, ...), custom_call_target="tpu_custom_call" | custom-call | flops 805306368 | bytes 9965568 | tf_op jit(solution)/shard_map/last/pallas_call | solution.py:333
  (22 shorter events, 0.2 us)
Async XLA Ops:
  0.6 40.2 %copy-start.3 = (bf16[1,1536,512]{2,1,0:T(8,128)(2,1)S(1)}, bf16[1,1536,512]{2,1,0:T(8,128)(2,1)}, u32[]{:S(2)}) copy-start(bf16[1,1536,512]{2,1,0:T(8,128)(2,1)} %e.5) | copy-start | bytes 4718596
  6.8 34.0 %copy-start.2 = (bf16[1,1536,512]{2,1,0:T(8,128)(2,1)S(1)}, bf16[1,1536,512]{2,1,0:T(8,128)(2,1)}, u32[]{:S(2)}) copy-start(bf16[1,1536,512]{2,1,0:T(8,128)(2,1)} %g.5) | copy-start | bytes 4718596
  6.8 8.1 %collective-permute-start = (f32[4,8,1536]{2,1,0:T(8,128)}, f32[4,8,1536]{2,1,0:T(8,128)S(1)}, u32[]{:S(2)}, u32[]{:S(2)}) collective-permute-start(f32[4,8,1536]{2,1,0:T(8,128)} %get-tuple-element.47), channel_id=1, source_target_pairs={{0,4},{4,0},{8,12},{12,8},{16,20},{20,16},{24,28},{28,24},{1,5},{5... | collective-permute-start | bytes 589832 | tf_op jit(solution)/shard_map/ppermute | solution.py:338
  9.9 3.6 %collective-permute-start.1 = (f32[16,512]{1,0:T(8,128)}, f32[16,512]{1,0:T(8,128)S(1)}, u32[]{:S(2)}, u32[]{:S(2)}) collective-permute-start(f32[16,512]{1,0:T(8,128)} %get-tuple-element.49), channel_id=1, source_target_pairs={{0,1},{1,0},{2,3},{3,2},{4,5},{5,4},{6,7},{7,6},{8,9},{9,8},{10,11... | collective-permute-start | bytes 98312 | tf_op jit(solution)/shard_map/ppermute | solution.py:338
  9.9 4.1 %collective-permute-start.2 = (f32[16,512]{1,0:T(8,128)}, f32[16,512]{1,0:T(8,128)S(1)}, u32[]{:S(2)}, u32[]{:S(2)}) collective-permute-start(f32[16,512]{1,0:T(8,128)} %get-tuple-element.50), channel_id=1, source_target_pairs={{0,2},{1,3},{2,0},{3,1},{4,6},{5,7},{6,4},{7,5},{8,10},{9,11},{10,... | collective-permute-start | bytes 98312 | tf_op jit(solution)/shard_map/ppermute | solution.py:338
  11.4 3.6 %collective-permute-start.3 = (f32[16,512]{1,0:T(8,128)}, f32[16,512]{1,0:T(8,128)S(1)}, u32[]{:S(2)}, u32[]{:S(2)}) collective-permute-start(f32[16,512]{1,0:T(8,128)} %get-tuple-element.51), channel_id=1, source_target_pairs={{0,3},{1,2},{2,1},{3,0},{4,7},{5,6},{6,5},{7,4},{8,11},{9,10},{10,... | collective-permute-start | bytes 98312 | tf_op jit(solution)/shard_map/ppermute | solution.py:338
  11.7 0.9 %copy-start.4 = (f32[4,8,1536]{2,1,0:T(8,128)S(1)}, f32[4,8,1536]{2,1,0:T(8,128)}, u32[]{:S(2)}) copy-start(f32[4,8,1536]{2,1,0:T(8,128)} %get-tuple-element.45.refs_1_) | copy-start | bytes 589828
  12.7 0.8 copy-start.5
  15.0 4.5 %collective-permute-start.4 = (f32[8,1792]{1,0:T(8,128)S(1)}, f32[8,1792]{1,0:T(8,128)S(1)}, u32[]{:S(2)}, u32[]{:S(2)}) collective-permute-start(f32[8,1792]{1,0:T(8,128)S(1)} %get-tuple-element.53), channel_id=1, source_target_pairs={{0,8},{4,12},{8,0},{12,4},{16,24},{20,28},{24,16},{28,20},{1,9},{5... | collective-permute-start | bytes 172040 | tf_op jit(solution)/shard_map/ppermute | solution.py:338
  16.9 6.4 %collective-permute-start.5 = (f32[8,1792]{1,0:T(8,128)S(1)}, f32[8,1792]{1,0:T(8,128)S(1)}, u32[]{:S(2)}, u32[]{:S(2)}) collective-permute-start(f32[8,1792]{1,0:T(8,128)S(1)} %get-tuple-element.54), channel_id=1, source_target_pairs={{0,16},{4,20},{8,24},{12,28},{16,0},{20,4},{24,8},{28,12},{1,17},{... | collective-permute-start | bytes 172040 | tf_op jit(solution)/shard_map/ppermute | solution.py:338
  19.5 6.0 %collective-permute-start.6 = (f32[8,1792]{1,0:T(8,128)S(1)}, f32[8,1792]{1,0:T(8,128)S(1)}, u32[]{:S(2)}, u32[]{:S(2)}) collective-permute-start(f32[8,1792]{1,0:T(8,128)S(1)} %get-tuple-element.55), channel_id=1, source_target_pairs={{0,24},{4,28},{8,16},{12,20},{16,8},{20,12},{24,0},{28,4},{1,25},{... | collective-permute-start | bytes 172040 | tf_op jit(solution)/shard_map/ppermute | solution.py:338
  25.5 6.0 %collective-permute-start.9 = (f32[8,1792]{1,0:T(8,128)S(1)}, f32[8,1792]{1,0:T(8,128)S(1)}, u32[]{:S(2)}, u32[]{:S(2)}) collective-permute-start(f32[8,1792]{1,0:T(8,128)S(1)} %replica_mean.2.refs_0_), channel_id=1, source_target_pairs={{0,24},{4,28},{8,16},{12,20},{16,8},{20,12},{24,0},{28,4},{1,25},{... | collective-permute-start | bytes 172040 | tf_op jit(solution)/shard_map/ppermute | solution.py:338
  27.1 5.6 %collective-permute-start.8 = (f32[8,1792]{1,0:T(8,128)S(1)}, f32[8,1792]{1,0:T(8,128)S(1)}, u32[]{:S(2)}, u32[]{:S(2)}) collective-permute-start(f32[8,1792]{1,0:T(8,128)S(1)} %replica_mean.2.refs_0_), channel_id=1, source_target_pairs={{0,16},{4,20},{8,24},{12,28},{16,0},{20,4},{24,8},{28,12},{1,17},{... | collective-permute-start | bytes 172040 | tf_op jit(solution)/shard_map/ppermute | solution.py:338
  27.1 5.6 %collective-permute-start.7 = (f32[8,1792]{1,0:T(8,128)S(1)}, f32[8,1792]{1,0:T(8,128)S(1)}, u32[]{:S(2)}, u32[]{:S(2)}) collective-permute-start(f32[8,1792]{1,0:T(8,128)S(1)} %replica_mean.2.refs_0_), channel_id=1, source_target_pairs={{0,8},{4,12},{8,0},{12,4},{16,24},{20,28},{24,16},{28,20},{1,9},{5... | collective-permute-start | bytes 172040 | tf_op jit(solution)/shard_map/ppermute | solution.py:338
  32.8 6.1 %collective-permute-start.10 = (f32[4,8,1792]{2,1,0:T(8,128)S(1)}, f32[4,8,1792]{2,1,0:T(8,128)S(1)}, u32[]{:S(2)}, u32[]{:S(2)}) collective-permute-start(f32[4,8,1792]{2,1,0:T(8,128)S(1)} %stack_z.2.mine), channel_id=1, source_target_pairs={{0,4},{4,0},{8,12},{12,8},{16,20},{20,16},{24,28},{28,24},{1,5},{5... | collective-permute-start | bytes 688136 | tf_op jit(solution)/shard_map/ppermute | solution.py:338
  38.9 4.1 %copy-start = (bf16[1,512,1536]{2,1,0:T(8,128)(2,1)S(1)}, bf16[1,512,1536]{2,1,0:T(8,128)(2,1)}, u32[]{:S(2)}) copy-start(bf16[1,512,1536]{2,1,0:T(8,128)(2,1)} %g.4) | copy-start | bytes 4718596
  38.9 4.1 %copy-start.1 = (bf16[1,512,1536]{2,1,0:T(8,128)(2,1)S(1)}, bf16[1,512,1536]{2,1,0:T(8,128)(2,1)}, u32[]{:S(2)}) copy-start(bf16[1,512,1536]{2,1,0:T(8,128)(2,1)} %e.4) | copy-start | bytes 4718596
  38.9 3.7 %collective-permute-start.13 = (f32[16,512]{1,0:T(8,128)S(1)}, f32[16,512]{1,0:T(8,128)S(1)}, u32[]{:S(2)}, u32[]{:S(2)}) collective-permute-start(f32[16,512]{1,0:T(8,128)S(1)} %shard_rows.1.refs_0_), channel_id=1, source_target_pairs={{0,3},{1,2},{2,1},{3,0},{4,7},{5,6},{6,5},{7,4},{8,11},{9,10},{10,... | collective-permute-start | bytes 98312 | tf_op jit(solution)/shard_map/ppermute | solution.py:338
  39.0 4.0 %collective-permute-start.12 = (f32[16,512]{1,0:T(8,128)S(1)}, f32[16,512]{1,0:T(8,128)S(1)}, u32[]{:S(2)}, u32[]{:S(2)}) collective-permute-start(f32[16,512]{1,0:T(8,128)S(1)} %shard_rows.1.refs_0_), channel_id=1, source_target_pairs={{0,2},{1,3},{2,0},{3,1},{4,6},{5,7},{6,4},{7,5},{8,10},{9,11},{10,... | collective-permute-start | bytes 98312 | tf_op jit(solution)/shard_map/ppermute | solution.py:338
  40.6 2.4 %collective-permute-start.11 = (f32[16,512]{1,0:T(8,128)S(1)}, f32[16,512]{1,0:T(8,128)S(1)}, u32[]{:S(2)}, u32[]{:S(2)}) collective-permute-start(f32[16,512]{1,0:T(8,128)S(1)} %shard_rows.1.refs_0_), channel_id=1, source_target_pairs={{0,1},{1,0},{2,3},{3,2},{4,5},{5,4},{6,7},{7,6},{8,9},{9,8},{10,11... | collective-permute-start | bytes 98312 | tf_op jit(solution)/shard_map/ppermute | solution.py:338
  44.2 7.2 %collective-permute-start.17 = (f32[4,8,1536]{2,1,0:T(8,128)S(1)}, f32[4,8,1536]{2,1,0:T(8,128)S(1)}, u32[]{:S(2)}, u32[]{:S(2)}) collective-permute-start(f32[4,8,1536]{2,1,0:T(8,128)S(1)} %get-tuple-element.65), channel_id=1, source_target_pairs={{0,4},{4,0},{8,12},{12,8},{16,20},{20,16},{24,28},{28,24},{1,5},{5... | collective-permute-start | bytes 589832 | tf_op jit(solution)/shard_map/ppermute | solution.py:338
  45.6 1.9 %collective-permute-start.14 = (f32[16,768]{1,0:T(8,128)S(1)}, f32[16,768]{1,0:T(8,128)S(1)}, u32[]{:S(2)}, u32[]{:S(2)}) collective-permute-start(f32[16,768]{1,0:T(8,128)S(1)} %get-tuple-element.60), channel_id=1, source_target_pairs={{0,1},{1,0},{2,3},{3,2},{4,5},{5,4},{6,7},{7,6},{8,9},{9,8},{10,11... | collective-permute-start | bytes 147464 | tf_op jit(solution)/shard_map/ppermute | solution.py:338
  45.7 4.1 %collective-permute-start.15 = (f32[16,768]{1,0:T(8,128)S(1)}, f32[16,768]{1,0:T(8,128)S(1)}, u32[]{:S(2)}, u32[]{:S(2)}) collective-permute-start(f32[16,768]{1,0:T(8,128)S(1)} %get-tuple-element.61), channel_id=1, source_target_pairs={{0,2},{1,3},{2,0},{3,1},{4,6},{5,7},{6,4},{7,5},{8,10},{9,11},{10,... | collective-permute-start | bytes 147464 | tf_op jit(solution)/shard_map/ppermute | solution.py:338
  47.1 3.7 %collective-permute-start.16 = (f32[16,768]{1,0:T(8,128)S(1)}, f32[16,768]{1,0:T(8,128)S(1)}, u32[]{:S(2)}, u32[]{:S(2)}) collective-permute-start(f32[16,768]{1,0:T(8,128)S(1)} %get-tuple-element.62), channel_id=1, source_target_pairs={{0,3},{1,2},{2,1},{3,0},{4,7},{5,6},{6,5},{7,4},{8,11},{9,10},{10,... | collective-permute-start | bytes 147464 | tf_op jit(solution)/shard_map/ppermute | solution.py:338
  51.5 4.5 %collective-permute-start.18 = (f32[8,1792]{1,0:T(8,128)S(1)}, f32[8,1792]{1,0:T(8,128)S(1)}, u32[]{:S(2)}, u32[]{:S(2)}) collective-permute-start(f32[8,1792]{1,0:T(8,128)S(1)} %get-tuple-element.68), channel_id=1, source_target_pairs={{0,8},{4,12},{8,0},{12,4},{16,24},{20,28},{24,16},{28,20},{1,9},{5... | collective-permute-start | bytes 172040 | tf_op jit(solution)/shard_map/ppermute | solution.py:338
  52.9 7.6 %collective-permute-start.19 = (f32[8,1792]{1,0:T(8,128)S(1)}, f32[8,1792]{1,0:T(8,128)S(1)}, u32[]{:S(2)}, u32[]{:S(2)}) collective-permute-start(f32[8,1792]{1,0:T(8,128)S(1)} %get-tuple-element.69), channel_id=1, source_target_pairs={{0,16},{4,20},{8,24},{12,28},{16,0},{20,4},{24,8},{28,12},{1,17},{... | collective-permute-start | bytes 172040 | tf_op jit(solution)/shard_map/ppermute | solution.py:338
  53.9 6.6 %collective-permute-start.20 = (f32[8,1792]{1,0:T(8,128)S(1)}, f32[8,1792]{1,0:T(8,128)S(1)}, u32[]{:S(2)}, u32[]{:S(2)}) collective-permute-start(f32[8,1792]{1,0:T(8,128)S(1)} %get-tuple-element.70), channel_id=1, source_target_pairs={{0,24},{4,28},{8,16},{12,20},{16,8},{20,12},{24,0},{28,4},{1,25},{... | collective-permute-start | bytes 172040 | tf_op jit(solution)/shard_map/ppermute | solution.py:338
  60.5 6.1 %collective-permute-start.23 = (f32[8,1792]{1,0:T(8,128)S(1)}, f32[8,1792]{1,0:T(8,128)S(1)}, u32[]{:S(2)}, u32[]{:S(2)}) collective-permute-start(f32[8,1792]{1,0:T(8,128)S(1)} %replica_mean.3.refs_0_), channel_id=1, source_target_pairs={{0,24},{4,28},{8,16},{12,20},{16,8},{20,12},{24,0},{28,4},{1,25},{... | collective-permute-start | bytes 172040 | tf_op jit(solution)/shard_map/ppermute | solution.py:338
  62.1 5.9 %collective-permute-start.22 = (f32[8,1792]{1,0:T(8,128)S(1)}, f32[8,1792]{1,0:T(8,128)S(1)}, u32[]{:S(2)}, u32[]{:S(2)}) collective-permute-start(f32[8,1792]{1,0:T(8,128)S(1)} %replica_mean.3.refs_0_), channel_id=1, source_target_pairs={{0,16},{4,20},{8,24},{12,28},{16,0},{20,4},{24,8},{28,12},{1,17},{... | collective-permute-start | bytes 172040 | tf_op jit(solution)/shard_map/ppermute | solution.py:338
  63.2 4.8 %collective-permute-start.21 = (f32[8,1792]{1,0:T(8,128)S(1)}, f32[8,1792]{1,0:T(8,128)S(1)}, u32[]{:S(2)}, u32[]{:S(2)}) collective-permute-start(f32[8,1792]{1,0:T(8,128)S(1)} %replica_mean.3.refs_0_), channel_id=1, source_target_pairs={{0,8},{4,12},{8,0},{12,4},{16,24},{20,28},{24,16},{28,20},{1,9},{5... | collective-permute-start | bytes 172040 | tf_op jit(solution)/shard_map/ppermute | solution.py:338
  68.1 6.1 %collective-permute-start.24 = (f32[4,8,1792]{2,1,0:T(8,128)S(1)}, f32[4,8,1792]{2,1,0:T(8,128)S(1)}, u32[]{:S(2)}, u32[]{:S(2)}) collective-permute-start(f32[4,8,1792]{2,1,0:T(8,128)S(1)} %stack_z.3.refs_4_.mine), channel_id=1, source_target_pairs={{0,4},{4,0},{8,12},{12,8},{16,20},{20,16},{24,28},{28,24},{1,5},{5... | collective-permute-start | bytes 688136 | tf_op jit(solution)/shard_map/ppermute | solution.py:338
  74.8 4.5 %collective-permute-start.27 = (f32[16,640]{1,0:T(8,128)S(1)}, f32[16,640]{1,0:T(8,128)S(1)}, u32[]{:S(2)}, u32[]{:S(2)}) collective-permute-start(f32[16,640]{1,0:T(8,128)S(1)} %get-tuple-element.76.refs_0_), channel_id=1, source_target_pairs={{0,3},{1,2},{2,1},{3,0},{4,7},{5,6},{6,5},{7,4},{8,11},{9,10},{10,... | collective-permute-start | bytes 122888 | tf_op jit(solution)/shard_map/ppermute | solution.py:338
  74.9 4.4 %collective-permute-start.26 = (f32[16,640]{1,0:T(8,128)S(1)}, f32[16,640]{1,0:T(8,128)S(1)}, u32[]{:S(2)}, u32[]{:S(2)}) collective-permute-start(f32[16,640]{1,0:T(8,128)S(1)} %get-tuple-element.76.refs_0_), channel_id=1, source_target_pairs={{0,2},{1,3},{2,0},{3,1},{4,6},{5,7},{6,4},{7,5},{8,10},{9,11},{10,... | collective-permute-start | bytes 122888 | tf_op jit(solution)/shard_map/ppermute | solution.py:338
  76.9 2.4 %collective-permute-start.25 = (f32[16,640]{1,0:T(8,128)S(1)}, f32[16,640]{1,0:T(8,128)S(1)}, u32[]{:S(2)}, u32[]{:S(2)}) collective-permute-start(f32[16,640]{1,0:T(8,128)S(1)} %get-tuple-element.76.refs_0_), channel_id=1, source_target_pairs={{0,1},{1,0},{2,3},{3,2},{4,5},{5,4},{6,7},{7,6},{8,9},{9,8},{10,11... | collective-permute-start | bytes 122888 | tf_op jit(solution)/shard_map/ppermute | solution.py:338

commit v11 on v10

--- a/solution.py
+++ b/solution.py
@@ -161,13 +161,17 @@
         refs[-1][lax.bitwise_xor(z, j)] = ref[...]
 
 
+def stack_apart_kernel(*refs):
+    *pieces, out, shard, stack = refs
+    stack_kernel(*pieces, stack)
+    half, _, ff = out.shape
+    out[...] = stack[:, :, :ff]
+    shard[...] = jnp.concatenate([unfold(stack[c, :, ff:], shard.shape[0]) for c in range(half)], axis=1)
+
+
 def shard_rows(mine, other, ff, rows):
     half = mine.shape[0]
     return jnp.concatenate([unfold(mine[c, :, ff:] + other[c, :, ff:], rows) for c in range(half)], axis=1)
-
-
-def shard_rows_kernel(ff, mine, other, out):
-    out[...] = shard_rows(mine, other, ff, out.shape[0])
 
 
 def split_rows(left, pieces):
@@ -181,7 +185,7 @@
     return t[:rank] + (t[rank : 2 * rank] + t[2 * rank :])
 
 
-def right_down_kernel(mine, other, g, e, left, *refs):
+def right_down_kernel(_, mine, other, g, e, left, *refs):
     *outs, pieces, total, stage = refs
     join_replicas(mine, other, stage, left)
     split_rows(left, pieces)
@@ -191,7 +195,7 @@
 
 def right_up_kernel(n_shards, *refs):
     shards, refs = refs[:n_shards], refs[n_shards:]
-    g, e, _, left, gram, keep, send, pieces, total, stage = refs
+    g, e, left, gram, keep, send, pieces, total, stage = refs
     join_shards(shards, left)
     split_rows(left, pieces)
     block = total.shape[1] // STEPS
@@ -351,12 +355,11 @@
     n_dp = lax.axis_size("dp")
     half, per, ff = keep.shape
     piece = shaped(per, ff + shard.shape[0] * shard.shape[1] // (half * per))
-    stack = shaped(half, *piece.shape)
-    parts = call(split_z_kernel, [piece] * half, keep, got, shard, name="split_z", scratch_shapes=[pltpu.VMEM(stack.shape, F32)])
+    stage = pltpu.VMEM((half, *piece.shape), F32)
+    parts = call(split_z_kernel, [piece] * half, keep, got, shard, name="split_z", scratch_shapes=[stage])
     parts = [parts[0], *parts[:0:-1]]
     mean = call(functools.partial(mean_kernel, n_dp), piece, *from_z(parts), name="replica_mean")
-    mine = call(stack_kernel, stack, *from_z([mean] * half), name="stack_z")
-    return mine, swap(mine, "dp", 1)
+    return from_z([mean] * half)
 
 
 def on_device(gu, eu, gd, ed, qu, qd):
@@ -385,24 +388,30 @@
     parts = from_shards(parts)
     parts[0], keep = call(fetch_kernel, [shard_rows_here, replica_half], parts[0], keep, name="fetch", flops=product // 4)
     shard = call(first_shards_kernel, shard_rows_here, *parts, name="shard_sum")
-    mine, other = mean_replicas(keep, got, shard)
-
-    shard = call(functools.partial(shard_rows_kernel, ff), shard_rows_here, mine, other, name="shard_rows")
+    pieces = mean_replicas(keep, got, shard)
+    mine, shard = call(
+        stack_apart_kernel, [replica_half, shard_rows_here], *pieces, name="stack_z",
+        scratch_shapes=[pltpu.VMEM((half, *pieces[0].shape), F32)],
+    )
+    shard = call(first_shards_kernel, shard_rows_here, shard, swap(shard, "dp", 1), name="replica_sum")
+    other = swap(mine, "dp", 1)
     left_rows = from_shards([shard] * n_shards)
-    left_down, *parts = call(
-        right_down_kernel, [shaped(rank, ff)] + [shaped(rows_here, rows + rank * n_shards)] * n_shards, mine, other, gd, ed,
-        name="right_down", flops=product, in_specs=[VMEM] * 4, scratch_shapes=[pltpu.VMEM((3 * rank, ff), BF16), narrow, stage],
-    )
     left_up, gram_up, keep, send = call(
         functools.partial(right_up_kernel, n_shards), [shaped(rank, rows), shaped(rank, rank), replica_half, replica_half],
-        *left_rows, gu, eu, left_down, name="right_up", flops=product, in_specs=[VMEM] * (n_shards + 2) + [ANY],
+        *left_rows, gu, eu, name="right_up", flops=product,
         scratch_shapes=[pltpu.VMEM((3 * rank, rows), BF16), wide, stage],
+    )
+    left_down, *parts = call(
+        right_down_kernel, [shaped(rank, ff)] + [shaped(rows_here, rows + rank * n_shards)] * n_shards, left_up, mine, other, gd, ed,
+        name="right_down", flops=product, in_specs=[ANY] + [VMEM] * 4, scratch_shapes=[pltpu.VMEM((3 * rank, ff), BF16), narrow, stage],
     )
     got = swap(send, "dp", 1)
     shard, gram_down = call(
         functools.partial(sum_shards_kernel, n_shards), [shard_rows_here, shaped(rank, rank)], *from_shards(parts), name="shard_sum"
     )
-    mine, other = mean_replicas(keep, got, shard)
+    pieces = mean_replicas(keep, got, shard)
+    mine = call(stack_kernel, shaped(half, *pieces[0].shape), *pieces, name="stack_z")
+    other = swap(mine, "dp", 1)
     inv_up, inv_down, lhs_up, lhs_down = call(
         basis_kernel,
         [shaped(rank, rank)] * 2 + [shaped(rows, 4 * rank, dtype=BF16), shaped(ff, 4 * rank, dtype=BF16)],

time: 83 us -> 82.6 us (level)
    ppermute x28 -> x29, waiting for transfers between devices: 29.4 us -> 28.7 us  [swap(): return lax.ppermute(x, axis, pairs)]
    ppermute x28 -> x29, starting transfers between devices: 32.4 us -> 32.7 us  [swap(): return lax.ppermute(x, axis, pairs)]
  transfers between devices with their start and end apart: 28 -> 29, of which waited for: 17 -> 17; matrix products, arithmetic and copies ran while one was open for 0% -> 0% of each run, Pallas kernels for 8% -> 10%
where the time goes in v11:
time: 82.6 us; the launch traced here: 82.4 us
  starting transfers between devices  32.7 us (40%)
  waiting for transfers between devices  28.7 us (35%)
  Pallas kernels  18.5 us (22%)
  local copies, waits for them, and re-layouts  1.7 us (2%)
    ppermute x29, starting transfers between devices, swap(): return lax.ppermute(x, axis, pairs)  32.7 us
    ppermute x29, waiting for transfers between devices, swap(): return lax.ppermute(x, axis, pairs)  28.7 us
    pallas_call x18, Pallas kernels, call(): pl.pallas_call(kernel, out_shape=out_shape, compiler_params=params, cost_...  18.5 us
    unnamed x12, local copies, waits for them, and re-layouts  1.7 us
  transfers between devices with their start and end apart: 29, of which 17 were waited for; matrix products, arithmetic and copies ran while one was open for 0% of the time, Pallas kernels for 10%

profile of v11, /device:TPU:0, one launch (start us, length us, event | category | flops | bytes accessed | tf_op | source)
XLA Modules:
  0.0 82.4 jit_solution(849941683403931377)
XLA Ops:
  0.6 6.2 %left.1 = (f32[16,512]{1,0:T(8,128)}, f32[16,512]{1,0:T(8,128)}, f32[16,512]{1,0:T(8,128)}, f32[16,512]{1,0:T(8,128)}, f32[4,8,1536]{2,1,0:T(8,128)}, /*index=5*/f32[4,8,1536]{2,1,0:T(8,128)}) custom-call(bf16[1,512,1536]{2,1,0:T(8,128)(2,1)} %g.4, bf16[1,512,1536]{2,1,0:T(8,128)(2,1)} %e.4, f32[64,1536]{1,0:T(8,128)} %bitcast.2, bf16[1,1536,512]{2,1,0:T(8,128)(2,1)} %g.5, ...), custom_call_target="tpu_custom_call" | custom-call | flops 1610612736 | bytes 7340032 | tf_op jit(solution)/shard_map/left/pallas_call | solution.py:337
  6.8 0.0 copy-start.2
  6.8 3.0 %collective-permute-start = (f32[4,8,1536]{2,1,0:T(8,128)}, f32[4,8,1536]{2,1,0:T(8,128)S(1)}, u32[]{:S(2)}, u32[]{:S(2)}) collective-permute-start(f32[4,8,1536]{2,1,0:T(8,128)} %get-tuple-element.49), channel_id=1, source_target_pairs={{0,4},{4,0},{8,12},{12,8},{16,20},{20,16},{24,28},{28,24},{1,5},{5... | collective-permute-start | bytes 589832 | tf_op jit(solution)/shard_map/ppermute | solution.py:342
  9.9 0.0 collective-permute-start.1
  9.9 1.5 %collective-permute-start.2 = (f32[16,512]{1,0:T(8,128)}, f32[16,512]{1,0:T(8,128)S(1)}, u32[]{:S(2)}, u32[]{:S(2)}) collective-permute-start(f32[16,512]{1,0:T(8,128)} %get-tuple-element.52), channel_id=1, source_target_pairs={{0,2},{1,3},{2,0},{3,1},{4,6},{5,7},{6,4},{7,5},{8,10},{9,11},{10,... | collective-permute-start | bytes 98312 | tf_op jit(solution)/shard_map/ppermute | solution.py:342
  11.4 0.4 collective-permute-start.3
  11.7 0.9 %copy-done.4 = f32[4,8,1536]{2,1,0:T(8,128)S(1)} copy-done((f32[4,8,1536]{2,1,0:T(8,128)S(1)}, f32[4,8,1536]{2,1,0:T(8,128)}, u32[]{:S(2)}) %copy-start.4) | copy-done | bytes 196632
  12.7 0.8 copy-done.5
  13.5 0.6 collective-permute-done.2.refs_2_
  14.0 0.9 %collective-permute-done.3.refs_3_ = f32[16,512]{1,0:T(8,128)S(1)} collective-permute-done((f32[16,512]{1,0:T(8,128)}, f32[16,512]{1,0:T(8,128)S(1)}, u32[]{:S(2)}, u32[]{:S(2)}) %collective-permute-start.3) | collective-permute-done | bytes 32800 | tf_op jit(solution)/shard_map/ppermute | solution.py:342
  14.9 0.1 collective-permute-done.got
  15.0 1.9 %collective-permute-start.4 = (f32[8,1792]{1,0:T(8,128)S(1)}, f32[8,1792]{1,0:T(8,128)S(1)}, u32[]{:S(2)}, u32[]{:S(2)}) collective-permute-start(f32[8,1792]{1,0:T(8,128)S(1)} %get-tuple-element.55), channel_id=1, source_target_pairs={{0,8},{4,12},{8,0},{12,4},{16,24},{20,28},{24,16},{28,20},{1,9},{5... | collective-permute-start | bytes 172040 | tf_op jit(solution)/shard_map/ppermute | solution.py:342
  16.9 2.6 %collective-permute-start.5 = (f32[8,1792]{1,0:T(8,128)S(1)}, f32[8,1792]{1,0:T(8,128)S(1)}, u32[]{:S(2)}, u32[]{:S(2)}) collective-permute-start(f32[8,1792]{1,0:T(8,128)S(1)} %get-tuple-element.56), channel_id=1, source_target_pairs={{0,16},{4,20},{8,24},{12,28},{16,0},{20,4},{24,8},{28,12},{1,17},{... | collective-permute-start | bytes 172040 | tf_op jit(solution)/shard_map/ppermute | solution.py:342
  19.5 0.0 collective-permute-start.6
  19.5 0.0 collective-permute-done.4.refs_1_
  19.5 3.8 %collective-permute-done.5.refs_2_ = f32[8,1792]{1,0:T(8,128)S(1)} collective-permute-done((f32[8,1792]{1,0:T(8,128)S(1)}, f32[8,1792]{1,0:T(8,128)S(1)}, u32[]{:S(2)}, u32[]{:S(2)}) %collective-permute-start.5) | collective-permute-done | bytes 57376 | tf_op jit(solution)/shard_map/ppermute | solution.py:342
  23.3 2.2 %collective-permute-done.6.refs_3_ = f32[8,1792]{1,0:T(8,128)S(1)} collective-permute-done((f32[8,1792]{1,0:T(8,128)S(1)}, f32[8,1792]{1,0:T(8,128)S(1)}, u32[]{:S(2)}, u32[]{:S(2)}) %collective-permute-start.6) | collective-permute-done | bytes 57376 | tf_op jit(solution)/shard_map/ppermute | solution.py:342
  25.5 1.6 %collective-permute-start.9 = (f32[8,1792]{1,0:T(8,128)S(1)}, f32[8,1792]{1,0:T(8,128)S(1)}, u32[]{:S(2)}, u32[]{:S(2)}) collective-permute-start(f32[8,1792]{1,0:T(8,128)S(1)} %replica_mean.2.refs_0_), channel_id=1, source_target_pairs={{0,24},{4,28},{8,16},{12,20},{16,8},{20,12},{24,0},{28,4},{1,25},{... | collective-permute-start | bytes 172040 | tf_op jit(solution)/shard_map/ppermute | solution.py:342
  27.1 0.0 collective-permute-start.8
  27.1 2.8 %collective-permute-start.7 = (f32[8,1792]{1,0:T(8,128)S(1)}, f32[8,1792]{1,0:T(8,128)S(1)}, u32[]{:S(2)}, u32[]{:S(2)}) collective-permute-start(f32[8,1792]{1,0:T(8,128)S(1)} %replica_mean.2.refs_0_), channel_id=1, source_target_pairs={{0,8},{4,12},{8,0},{12,4},{16,24},{20,28},{24,16},{28,20},{1,9},{5... | collective-permute-start | bytes 172040 | tf_op jit(solution)/shard_map/ppermute | solution.py:342
  29.9 1.6 %collective-permute-done.9.refs_3_ = f32[8,1792]{1,0:T(8,128)S(1)} collective-permute-done((f32[8,1792]{1,0:T(8,128)S(1)}, f32[8,1792]{1,0:T(8,128)S(1)}, u32[]{:S(2)}, u32[]{:S(2)}) %collective-permute-start.9) | collective-permute-done | bytes 57376 | tf_op jit(solution)/shard_map/ppermute | solution.py:342
  31.5 1.2 %collective-permute-done.8.refs_2_ = f32[8,1792]{1,0:T(8,128)S(1)} collective-permute-done((f32[8,1792]{1,0:T(8,128)S(1)}, f32[8,1792]{1,0:T(8,128)S(1)}, u32[]{:S(2)}, u32[]{:S(2)}) %collective-permute-start.8) | collective-permute-done | bytes 57376 | tf_op jit(solution)/shard_map/ppermute | solution.py:342
  32.8 0.0 collective-permute-done.7.refs_1_
  32.8 1.4 %collective-permute-start.10 = (f32[16,512]{1,0:T(8,128)S(1)}, f32[16,512]{1,0:T(8,128)S(1)}, u32[]{:S(2)}, u32[]{:S(2)}) collective-permute-start(f32[16,512]{1,0:T(8,128)S(1)} %get-tuple-element.58.refs_0_), channel_id=1, source_target_pairs={{0,4},{4,0},{8,12},{12,8},{16,20},{20,16},{24,28},{28,24},{1,5},{5... | collective-permute-start | bytes 98312 | tf_op jit(solution)/shard_map/ppermute | solution.py:342
  34.2 0.7 collective-permute-start.14
  34.9 1.9 %collective-permute-done.10.refs_1_ = f32[16,512]{1,0:T(8,128)S(1)} collective-permute-done((f32[16,512]{1,0:T(8,128)S(1)}, f32[16,512]{1,0:T(8,128)S(1)}, u32[]{:S(2)}, u32[]{:S(2)}) %collective-permute-start.10) | collective-permute-done | bytes 32800 | tf_op jit(solution)/shard_map/ppermute | solution.py:342
  36.8 0.0 copy-start.1
  36.8 0.1 collective-permute-start.13
  36.9 1.6 %collective-permute-start.12 = (f32[16,512]{1,0:T(8,128)S(1)}, f32[16,512]{1,0:T(8,128)S(1)}, u32[]{:S(2)}, u32[]{:S(2)}) collective-permute-start(f32[16,512]{1,0:T(8,128)S(1)} %replica_sum.1.refs_0_), channel_id=1, source_target_pairs={{0,2},{1,3},{2,0},{3,1},{4,6},{5,7},{6,4},{7,5},{8,10},{9,11},{10,... | collective-permute-start | bytes 98312 | tf_op jit(solution)/shard_map/ppermute | solution.py:342
  38.5 0.2 collective-permute-start.11
  38.7 1.7 %collective-permute-done.13.refs_3_ = f32[16,512]{1,0:T(8,128)S(1)} collective-permute-done((f32[16,512]{1,0:T(8,128)S(1)}, f32[16,512]{1,0:T(8,128)S(1)}, u32[]{:S(2)}, u32[]{:S(2)}) %collective-permute-start.13) | collective-permute-done | bytes 32800 | tf_op jit(solution)/shard_map/ppermute | solution.py:342
  40.5 0.4 collective-permute-done.12.refs_2_
  40.9 1.2 %right_up.1 = (f32[64,512]{1,0:T(8,128)S(1)}, f32[64,64]{1,0:T(8,128)S(1)}, f32[4,8,1536]{2,1,0:T(8,128)S(1)}, f32[4,8,1536]{2,1,0:T(8,128)S(1)}) custom-call(f32[16,512]{1,0:T(8,128)S(1)} %replica_sum.1.refs_0_, f32[16,512]{1,0:T(8,128)S(1)} %collective-permute-done.11.refs_1_, f32[16,512]{1,0:T(8,128)S(1)} %collective-permute-done.12.refs_2_, ...), custom_call_target="tpu_custom_call" | custom-call | flops 805306368 | bytes 3817472 | tf_op jit(solution)/shard_map/right_up/pallas_call | solution.py:337
  42.1 1.4 %collective-permute-start.18 = (f32[4,8,1536]{2,1,0:T(8,128)S(1)}, f32[4,8,1536]{2,1,0:T(8,128)S(1)}, u32[]{:S(2)}, u32[]{:S(2)}) collective-permute-start(f32[4,8,1536]{2,1,0:T(8,128)S(1)} %get-tuple-element.69), channel_id=1, source_target_pairs={{0,4},{4,0},{8,12},{12,8},{16,20},{20,16},{24,28},{28,24},{1,5},{5... | collective-permute-start | bytes 589832 | tf_op jit(solution)/shard_map/ppermute | solution.py:342
  43.6 0.0 collective-permute-done.14.other
  43.6 1.2 %right_down.1 = (f32[64,1536]{1,0:T(8,128)S(1)}, f32[16,768]{1,0:T(8,128)S(1)}, f32[16,768]{1,0:T(8,128)S(1)}, f32[16,768]{1,0:T(8,128)S(1)}, f32[16,768]{1,0:T(8,128)S(1)}) custom-call(f32[64,512]{1,0:T(8,128)S(1)} %get-tuple-element.59._.left_up, f32[4,8,1536]{2,1,0:T(8,128)S(1)} %get-tuple-element.60.mine, ...), custom_call_target="tpu_custom_call" | custom-call | flops 805306368 | bytes 4259840 | tf_op jit(solution)/shard_map/right_down/pallas_call | solution.py:337
  44.7 0.1 collective-permute-start.15
  44.8 1.5 %collective-permute-start.16 = (f32[16,768]{1,0:T(8,128)S(1)}, f32[16,768]{1,0:T(8,128)S(1)}, u32[]{:S(2)}, u32[]{:S(2)}) collective-permute-start(f32[16,768]{1,0:T(8,128)S(1)} %get-tuple-element.65), channel_id=1, source_target_pairs={{0,2},{1,3},{2,0},{3,1},{4,6},{5,7},{6,4},{7,5},{8,10},{9,11},{10,... | collective-permute-start | bytes 147464 | tf_op jit(solution)/shard_map/ppermute | solution.py:342
  46.4 0.3 collective-permute-start.17
  46.7 2.3 %collective-permute-done.16.refs_2_ = f32[16,768]{1,0:T(8,128)S(1)} collective-permute-done((f32[16,768]{1,0:T(8,128)S(1)}, f32[16,768]{1,0:T(8,128)S(1)}, u32[]{:S(2)}, u32[]{:S(2)}) %collective-permute-start.16) | collective-permute-done | bytes 49184 | tf_op jit(solution)/shard_map/ppermute | solution.py:342
  49.0 1.1 %collective-permute-done.17.refs_3_ = f32[16,768]{1,0:T(8,128)S(1)} collective-permute-done((f32[16,768]{1,0:T(8,128)S(1)}, f32[16,768]{1,0:T(8,128)S(1)}, u32[]{:S(2)}, u32[]{:S(2)}) %collective-permute-start.17) | collective-permute-done | bytes 49184 | tf_op jit(solution)/shard_map/ppermute | solution.py:342
  50.1 0.1 shard_sum.3
  50.2 1.6 %collective-permute-start.19 = (f32[8,1792]{1,0:T(8,128)S(1)}, f32[8,1792]{1,0:T(8,128)S(1)}, u32[]{:S(2)}, u32[]{:S(2)}) collective-permute-start(f32[8,1792]{1,0:T(8,128)S(1)} %get-tuple-element.72), channel_id=1, source_target_pairs={{0,8},{4,12},{8,0},{12,4},{16,24},{20,28},{24,16},{28,20},{1,9},{5... | collective-permute-start | bytes 172040 | tf_op jit(solution)/shard_map/ppermute | solution.py:342
  51.8 0.9 %collective-permute-start.20 = (f32[8,1792]{1,0:T(8,128)S(1)}, f32[8,1792]{1,0:T(8,128)S(1)}, u32[]{:S(2)}, u32[]{:S(2)}) collective-permute-start(f32[8,1792]{1,0:T(8,128)S(1)} %get-tuple-element.73), channel_id=1, source_target_pairs={{0,16},{4,20},{8,24},{12,28},{16,0},{20,4},{24,8},{28,12},{1,17},{... | collective-permute-start | bytes 172040 | tf_op jit(solution)/shard_map/ppermute | solution.py:342
  52.7 1.9 %collective-permute-start.21 = (f32[8,1792]{1,0:T(8,128)S(1)}, f32[8,1792]{1,0:T(8,128)S(1)}, u32[]{:S(2)}, u32[]{:S(2)}) collective-permute-start(f32[8,1792]{1,0:T(8,128)S(1)} %get-tuple-element.74), channel_id=1, source_target_pairs={{0,24},{4,28},{8,16},{12,20},{16,8},{20,12},{24,0},{28,4},{1,25},{... | collective-permute-start | bytes 172040 | tf_op jit(solution)/shard_map/ppermute | solution.py:342
  54.6 4.6 %collective-permute-done.20.refs_2_ = f32[8,1792]{1,0:T(8,128)S(1)} collective-permute-done((f32[8,1792]{1,0:T(8,128)S(1)}, f32[8,1792]{1,0:T(8,128)S(1)}, u32[]{:S(2)}, u32[]{:S(2)}) %collective-permute-start.20) | collective-permute-done | bytes 57376 | tf_op jit(solution)/shard_map/ppermute | solution.py:342
  59.3 0.0 collective-permute-done.21.refs_3_
  59.3 1.5 %collective-permute-start.24 = (f32[8,1792]{1,0:T(8,128)S(1)}, f32[8,1792]{1,0:T(8,128)S(1)}, u32[]{:S(2)}, u32[]{:S(2)}) collective-permute-start(f32[8,1792]{1,0:T(8,128)S(1)} %replica_mean.3.refs_0_), channel_id=1, source_target_pairs={{0,24},{4,28},{8,16},{12,20},{16,8},{20,12},{24,0},{28,4},{1,25},{... | collective-permute-start | bytes 172040 | tf_op jit(solution)/shard_map/ppermute | solution.py:342
  60.8 1.3 %collective-permute-start.23 = (f32[8,1792]{1,0:T(8,128)S(1)}, f32[8,1792]{1,0:T(8,128)S(1)}, u32[]{:S(2)}, u32[]{:S(2)}) collective-permute-start(f32[8,1792]{1,0:T(8,128)S(1)} %replica_mean.3.refs_0_), channel_id=1, source_target_pairs={{0,16},{4,20},{8,24},{12,28},{16,0},{20,4},{24,8},{28,12},{1,17},{... | collective-permute-start | bytes 172040 | tf_op jit(solution)/shard_map/ppermute | solution.py:342
  62.1 1.6 %collective-permute-start.22 = (f32[8,1792]{1,0:T(8,128)S(1)}, f32[8,1792]{1,0:T(8,128)S(1)}, u32[]{:S(2)}, u32[]{:S(2)}) collective-permute-start(f32[8,1792]{1,0:T(8,128)S(1)} %replica_mean.3.refs_0_), channel_id=1, source_target_pairs={{0,8},{4,12},{8,0},{12,4},{16,24},{20,28},{24,16},{28,20},{1,9},{5... | collective-permute-start | bytes 172040 | tf_op jit(solution)/shard_map/ppermute | solution.py:342
  63.7 1.7 %collective-permute-done.24.refs_3_ = f32[8,1792]{1,0:T(8,128)S(1)} collective-permute-done((f32[8,1792]{1,0:T(8,128)S(1)}, f32[8,1792]{1,0:T(8,128)S(1)}, u32[]{:S(2)}, u32[]{:S(2)}) %collective-permute-start.24) | collective-permute-done | bytes 57376 | tf_op jit(solution)/shard_map/ppermute | solution.py:342
  65.5 1.7 %collective-permute-done.23.refs_2_ = f32[8,1792]{1,0:T(8,128)S(1)} collective-permute-done((f32[8,1792]{1,0:T(8,128)S(1)}, f32[8,1792]{1,0:T(8,128)S(1)}, u32[]{:S(2)}, u32[]{:S(2)}) %collective-permute-start.23) | collective-permute-done | bytes 57376 | tf_op jit(solution)/shard_map/ppermute | solution.py:342
  67.2 0.0 collective-permute-done.22.refs_1_
  67.2 0.8 collective-permute-start.25
  68.0 3.2 %basis.1 = (f32[64,64]{1,0:T(8,128)S(1)}, f32[64,64]{1,0:T(8,128)S(1)}, bf16[512,256]{1,0:T(8,128)(2,1)S(1)}, bf16[1536,256]{1,0:T(8,128)(2,1)S(1)}) custom-call(f32[64,512]{1,0:T(8,128)S(1)} %get-tuple-element.59._.left_up, f32[64,1536]{1,0:T(8,128)S(1)} %get-tuple-element.61.left_down, f32[64,64]{1,0:T(8,128)S(1)} %get-tuple-element.62.gram_up, ...), custom_call_target="tpu_custom_call" | custom-call | bytes 8159232 | tf_op jit(solution)/shard_map/basis/pallas_call | solution.py:337
  71.2 2.7 %collective-permute-done.25.other = f32[4,8,1792]{2,1,0:T(8,128)S(1)} collective-permute-done((f32[4,8,1792]{2,1,0:T(8,128)S(1)}, f32[4,8,1792]{2,1,0:T(8,128)S(1)}, u32[]{:S(2)}, u32[]{:S(2)}) %collective-permute-start.25) | collective-permute-done | bytes 229408 | tf_op jit(solution)/shard_map/ppermute | solution.py:342
  73.9 0.7 factor_up.1
  74.6 0.1 collective-permute-start.28
  74.6 1.4 %collective-permute-start.27 = (f32[16,640]{1,0:T(8,128)S(1)}, f32[16,640]{1,0:T(8,128)S(1)}, u32[]{:S(2)}, u32[]{:S(2)}) collective-permute-start(f32[16,640]{1,0:T(8,128)S(1)} %get-tuple-element.80.refs_0_), channel_id=1, source_target_pairs={{0,2},{1,3},{2,0},{3,1},{4,6},{5,7},{6,4},{7,5},{8,10},{9,11},{10,... | collective-permute-start | bytes 122888 | tf_op jit(solution)/shard_map/ppermute | solution.py:342
  76.0 0.5 collective-permute-start.26
  76.5 2.3 %error_up.1 = (bf16[1,512,1536]{2,1,0:T(8,128)(2,1)}, f32[8,128]{1,0:T(8,128)S(1)}) custom-call(bf16[1,512,1536]{2,1,0:T(8,128)(2,1)S(1)} %copy-done.2, bf16[1,512,1536]{2,1,0:T(8,128)(2,1)S(1)} %copy-done.3, bf16[512,256]{1,0:T(8,128)(2,1)S(1)} %get-tuple-element.75.lhs.lhs_up, bf16[256,1536]{1,0:T(8,128)(2,1)S(1)} %get-tuple-element.77.rhs.rhs_up), custom_call_target="tpu_custom_call" | custom-call | flops 402653184 | bytes 5771264 | tf_op jit(solution)/shard_map/error_up/pallas_call | solution.py:337
  78.8 0.1 collective-permute-done.27.refs_2_
  79.0 0.4 factor_down.1
  79.4 3.0 %last.1 = (bf16[1,1536,512]{2,1,0:T(8,128)(2,1)}, bf16[512,1536]{1,0:T(8,128)(2,1)}, bf16[1536,512]{1,0:T(8,128)(2,1)}) custom-call(bf16[1,1536,512]{2,1,0:T(8,128)(2,1)S(1)} %copy-done, bf16[1,1536,512]{2,1,0:T(8,128)(2,1)S(1)} %copy-done.1, bf16[512,256]{1,0:T(8,128)(2,1)S(1)} %get-tuple-element.75.lhs.lhs_up, ...), custom_call_target="tpu_custom_call" | custom-call | flops 805306368 | bytes 9965568 | tf_op jit(solution)/shard_map/last/pallas_call | solution.py:337
  (24 shorter events, 0.2 us)
Async XLA Ops:
  0.6 40.3 %copy-start.3 = (bf16[1,512,1536]{2,1,0:T(8,128)(2,1)S(1)}, bf16[1,512,1536]{2,1,0:T(8,128)(2,1)}, u32[]{:S(2)}) copy-start(bf16[1,512,1536]{2,1,0:T(8,128)(2,1)} %e.4) | copy-start | bytes 4718596
  6.8 34.1 %copy-start.2 = (bf16[1,512,1536]{2,1,0:T(8,128)(2,1)S(1)}, bf16[1,512,1536]{2,1,0:T(8,128)(2,1)}, u32[]{:S(2)}) copy-start(bf16[1,512,1536]{2,1,0:T(8,128)(2,1)} %g.4) | copy-start | bytes 4718596
  6.8 8.1 %collective-permute-start = (f32[4,8,1536]{2,1,0:T(8,128)}, f32[4,8,1536]{2,1,0:T(8,128)S(1)}, u32[]{:S(2)}, u32[]{:S(2)}) collective-permute-start(f32[4,8,1536]{2,1,0:T(8,128)} %get-tuple-element.49), channel_id=1, source_target_pairs={{0,4},{4,0},{8,12},{12,8},{16,20},{20,16},{24,28},{28,24},{1,5},{5... | collective-permute-start | bytes 589832 | tf_op jit(solution)/shard_map/ppermute | solution.py:342
  9.9 3.6 %collective-permute-start.1 = (f32[16,512]{1,0:T(8,128)}, f32[16,512]{1,0:T(8,128)S(1)}, u32[]{:S(2)}, u32[]{:S(2)}) collective-permute-start(f32[16,512]{1,0:T(8,128)} %get-tuple-element.51), channel_id=1, source_target_pairs={{0,1},{1,0},{2,3},{3,2},{4,5},{5,4},{6,7},{7,6},{8,9},{9,8},{10,11... | collective-permute-start | bytes 98312 | tf_op jit(solution)/shard_map/ppermute | solution.py:342
  9.9 4.1 %collective-permute-start.2 = (f32[16,512]{1,0:T(8,128)}, f32[16,512]{1,0:T(8,128)S(1)}, u32[]{:S(2)}, u32[]{:S(2)}) collective-permute-start(f32[16,512]{1,0:T(8,128)} %get-tuple-element.52), channel_id=1, source_target_pairs={{0,2},{1,3},{2,0},{3,1},{4,6},{5,7},{6,4},{7,5},{8,10},{9,11},{10,... | collective-permute-start | bytes 98312 | tf_op jit(solution)/shard_map/ppermute | solution.py:342
  11.4 3.6 %collective-permute-start.3 = (f32[16,512]{1,0:T(8,128)}, f32[16,512]{1,0:T(8,128)S(1)}, u32[]{:S(2)}, u32[]{:S(2)}) collective-permute-start(f32[16,512]{1,0:T(8,128)} %get-tuple-element.53), channel_id=1, source_target_pairs={{0,3},{1,2},{2,1},{3,0},{4,7},{5,6},{6,5},{7,4},{8,11},{9,10},{10,... | collective-permute-start | bytes 98312 | tf_op jit(solution)/shard_map/ppermute | solution.py:342
  11.7 0.9 %copy-start.4 = (f32[4,8,1536]{2,1,0:T(8,128)S(1)}, f32[4,8,1536]{2,1,0:T(8,128)}, u32[]{:S(2)}) copy-start(f32[4,8,1536]{2,1,0:T(8,128)} %get-tuple-element.47.refs_1_) | copy-start | bytes 589828
  12.7 0.8 copy-start.5
  15.0 4.5 %collective-permute-start.4 = (f32[8,1792]{1,0:T(8,128)S(1)}, f32[8,1792]{1,0:T(8,128)S(1)}, u32[]{:S(2)}, u32[]{:S(2)}) collective-permute-start(f32[8,1792]{1,0:T(8,128)S(1)} %get-tuple-element.55), channel_id=1, source_target_pairs={{0,8},{4,12},{8,0},{12,4},{16,24},{20,28},{24,16},{28,20},{1,9},{5... | collective-permute-start | bytes 172040 | tf_op jit(solution)/shard_map/ppermute | solution.py:342
  16.9 6.4 %collective-permute-start.5 = (f32[8,1792]{1,0:T(8,128)S(1)}, f32[8,1792]{1,0:T(8,128)S(1)}, u32[]{:S(2)}, u32[]{:S(2)}) collective-permute-start(f32[8,1792]{1,0:T(8,128)S(1)} %get-tuple-element.56), channel_id=1, source_target_pairs={{0,16},{4,20},{8,24},{12,28},{16,0},{20,4},{24,8},{28,12},{1,17},{... | collective-permute-start | bytes 172040 | tf_op jit(solution)/shard_map/ppermute | solution.py:342
  19.5 6.0 %collective-permute-start.6 = (f32[8,1792]{1,0:T(8,128)S(1)}, f32[8,1792]{1,0:T(8,128)S(1)}, u32[]{:S(2)}, u32[]{:S(2)}) collective-permute-start(f32[8,1792]{1,0:T(8,128)S(1)} %get-tuple-element.57), channel_id=1, source_target_pairs={{0,24},{4,28},{8,16},{12,20},{16,8},{20,12},{24,0},{28,4},{1,25},{... | collective-permute-start | bytes 172040 | tf_op jit(solution)/shard_map/ppermute | solution.py:342
  25.5 6.0 %collective-permute-start.9 = (f32[8,1792]{1,0:T(8,128)S(1)}, f32[8,1792]{1,0:T(8,128)S(1)}, u32[]{:S(2)}, u32[]{:S(2)}) collective-permute-start(f32[8,1792]{1,0:T(8,128)S(1)} %replica_mean.2.refs_0_), channel_id=1, source_target_pairs={{0,24},{4,28},{8,16},{12,20},{16,8},{20,12},{24,0},{28,4},{1,25},{... | collective-permute-start | bytes 172040 | tf_op jit(solution)/shard_map/ppermute | solution.py:342
  27.1 5.6 %collective-permute-start.8 = (f32[8,1792]{1,0:T(8,128)S(1)}, f32[8,1792]{1,0:T(8,128)S(1)}, u32[]{:S(2)}, u32[]{:S(2)}) collective-permute-start(f32[8,1792]{1,0:T(8,128)S(1)} %replica_mean.2.refs_0_), channel_id=1, source_target_pairs={{0,16},{4,20},{8,24},{12,28},{16,0},{20,4},{24,8},{28,12},{1,17},{... | collective-permute-start | bytes 172040 | tf_op jit(solution)/shard_map/ppermute | solution.py:342
  27.1 5.6 %collective-permute-start.7 = (f32[8,1792]{1,0:T(8,128)S(1)}, f32[8,1792]{1,0:T(8,128)S(1)}, u32[]{:S(2)}, u32[]{:S(2)}) collective-permute-start(f32[8,1792]{1,0:T(8,128)S(1)} %replica_mean.2.refs_0_), channel_id=1, source_target_pairs={{0,8},{4,12},{8,0},{12,4},{16,24},{20,28},{24,16},{28,20},{1,9},{5... | collective-permute-start | bytes 172040 | tf_op jit(solution)/shard_map/ppermute | solution.py:342
  32.8 4.0 %collective-permute-start.10 = (f32[16,512]{1,0:T(8,128)S(1)}, f32[16,512]{1,0:T(8,128)S(1)}, u32[]{:S(2)}, u32[]{:S(2)}) collective-permute-start(f32[16,512]{1,0:T(8,128)S(1)} %get-tuple-element.58.refs_0_), channel_id=1, source_target_pairs={{0,4},{4,0},{8,12},{12,8},{16,20},{20,16},{24,28},{28,24},{1,5},{5... | collective-permute-start | bytes 98312 | tf_op jit(solution)/shard_map/ppermute | solution.py:342
  34.2 9.3 %collective-permute-start.14 = (f32[4,8,1536]{2,1,0:T(8,128)S(1)}, f32[4,8,1536]{2,1,0:T(8,128)S(1)}, u32[]{:S(2)}, u32[]{:S(2)}) collective-permute-start(f32[4,8,1536]{2,1,0:T(8,128)S(1)} %get-tuple-element.60.mine), channel_id=1, source_target_pairs={{0,4},{4,0},{8,12},{12,8},{16,20},{20,16},{24,28},{28,24},{1,5},{5... | collective-permute-start | bytes 589832 | tf_op jit(solution)/shard_map/ppermute | solution.py:342
  36.8 6.8 %copy-start = (bf16[1,1536,512]{2,1,0:T(8,128)(2,1)S(1)}, bf16[1,1536,512]{2,1,0:T(8,128)(2,1)}, u32[]{:S(2)}) copy-start(bf16[1,1536,512]{2,1,0:T(8,128)(2,1)} %g.5) | copy-start | bytes 4718596
  36.8 6.8 %copy-start.1 = (bf16[1,1536,512]{2,1,0:T(8,128)(2,1)S(1)}, bf16[1,1536,512]{2,1,0:T(8,128)(2,1)}, u32[]{:S(2)}) copy-start(bf16[1,1536,512]{2,1,0:T(8,128)(2,1)} %e.5) | copy-start | bytes 4718596
  36.8 3.7 %collective-permute-start.13 = (f32[16,512]{1,0:T(8,128)S(1)}, f32[16,512]{1,0:T(8,128)S(1)}, u32[]{:S(2)}, u32[]{:S(2)}) collective-permute-start(f32[16,512]{1,0:T(8,128)S(1)} %replica_sum.1.refs_0_), channel_id=1, source_target_pairs={{0,3},{1,2},{2,1},{3,0},{4,7},{5,6},{6,5},{7,4},{8,11},{9,10},{10,... | collective-permute-start | bytes 98312 | tf_op jit(solution)/shard_map/ppermute | solution.py:342
  36.9 4.0 %collective-permute-start.12 = (f32[16,512]{1,0:T(8,128)S(1)}, f32[16,512]{1,0:T(8,128)S(1)}, u32[]{:S(2)}, u32[]{:S(2)}) collective-permute-start(f32[16,512]{1,0:T(8,128)S(1)} %replica_sum.1.refs_0_), channel_id=1, source_target_pairs={{0,2},{1,3},{2,0},{3,1},{4,6},{5,7},{6,4},{7,5},{8,10},{9,11},{10,... | collective-permute-start | bytes 98312 | tf_op jit(solution)/shard_map/ppermute | solution.py:342
  38.5 2.4 %collective-permute-start.11 = (f32[16,512]{1,0:T(8,128)S(1)}, f32[16,512]{1,0:T(8,128)S(1)}, u32[]{:S(2)}, u32[]{:S(2)}) collective-permute-start(f32[16,512]{1,0:T(8,128)S(1)} %replica_sum.1.refs_0_), channel_id=1, source_target_pairs={{0,1},{1,0},{2,3},{3,2},{4,5},{5,4},{6,7},{7,6},{8,9},{9,8},{10,11... | collective-permute-start | bytes 98312 | tf_op jit(solution)/shard_map/ppermute | solution.py:342
  42.1 8.0 %collective-permute-start.18 = (f32[4,8,1536]{2,1,0:T(8,128)S(1)}, f32[4,8,1536]{2,1,0:T(8,128)S(1)}, u32[]{:S(2)}, u32[]{:S(2)}) collective-permute-start(f32[4,8,1536]{2,1,0:T(8,128)S(1)} %get-tuple-element.69), channel_id=1, source_target_pairs={{0,4},{4,0},{8,12},{12,8},{16,20},{20,16},{24,28},{28,24},{1,5},{5... | collective-permute-start | bytes 589832 | tf_op jit(solution)/shard_map/ppermute | solution.py:342
  44.7 1.9 %collective-permute-start.15 = (f32[16,768]{1,0:T(8,128)S(1)}, f32[16,768]{1,0:T(8,128)S(1)}, u32[]{:S(2)}, u32[]{:S(2)}) collective-permute-start(f32[16,768]{1,0:T(8,128)S(1)} %get-tuple-element.64), channel_id=1, source_target_pairs={{0,1},{1,0},{2,3},{3,2},{4,5},{5,4},{6,7},{7,6},{8,9},{9,8},{10,11... | collective-permute-start | bytes 147464 | tf_op jit(solution)/shard_map/ppermute | solution.py:342
  44.8 4.1 %collective-permute-start.16 = (f32[16,768]{1,0:T(8,128)S(1)}, f32[16,768]{1,0:T(8,128)S(1)}, u32[]{:S(2)}, u32[]{:S(2)}) collective-permute-start(f32[16,768]{1,0:T(8,128)S(1)} %get-tuple-element.65), channel_id=1, source_target_pairs={{0,2},{1,3},{2,0},{3,1},{4,6},{5,7},{6,4},{7,5},{8,10},{9,11},{10,... | collective-permute-start | bytes 147464 | tf_op jit(solution)/shard_map/ppermute | solution.py:342
  46.4 3.7 %collective-permute-start.17 = (f32[16,768]{1,0:T(8,128)S(1)}, f32[16,768]{1,0:T(8,128)S(1)}, u32[]{:S(2)}, u32[]{:S(2)}) collective-permute-start(f32[16,768]{1,0:T(8,128)S(1)} %get-tuple-element.66), channel_id=1, source_target_pairs={{0,3},{1,2},{2,1},{3,0},{4,7},{5,6},{6,5},{7,4},{8,11},{9,10},{10,... | collective-permute-start | bytes 147464 | tf_op jit(solution)/shard_map/ppermute | solution.py:342
  50.2 4.5 %collective-permute-start.19 = (f32[8,1792]{1,0:T(8,128)S(1)}, f32[8,1792]{1,0:T(8,128)S(1)}, u32[]{:S(2)}, u32[]{:S(2)}) collective-permute-start(f32[8,1792]{1,0:T(8,128)S(1)} %get-tuple-element.72), channel_id=1, source_target_pairs={{0,8},{4,12},{8,0},{12,4},{16,24},{20,28},{24,16},{28,20},{1,9},{5... | collective-permute-start | bytes 172040 | tf_op jit(solution)/shard_map/ppermute | solution.py:342
  51.8 7.5 %collective-permute-start.20 = (f32[8,1792]{1,0:T(8,128)S(1)}, f32[8,1792]{1,0:T(8,128)S(1)}, u32[]{:S(2)}, u32[]{:S(2)}) collective-permute-start(f32[8,1792]{1,0:T(8,128)S(1)} %get-tuple-element.73), channel_id=1, source_target_pairs={{0,16},{4,20},{8,24},{12,28},{16,0},{20,4},{24,8},{28,12},{1,17},{... | collective-permute-start | bytes 172040 | tf_op jit(solution)/shard_map/ppermute | solution.py:342
  52.7 6.6 %collective-permute-start.21 = (f32[8,1792]{1,0:T(8,128)S(1)}, f32[8,1792]{1,0:T(8,128)S(1)}, u32[]{:S(2)}, u32[]{:S(2)}) collective-permute-start(f32[8,1792]{1,0:T(8,128)S(1)} %get-tuple-element.74), channel_id=1, source_target_pairs={{0,24},{4,28},{8,16},{12,20},{16,8},{20,12},{24,0},{28,4},{1,25},{... | collective-permute-start | bytes 172040 | tf_op jit(solution)/shard_map/ppermute | solution.py:342
  59.3 6.2 %collective-permute-start.24 = (f32[8,1792]{1,0:T(8,128)S(1)}, f32[8,1792]{1,0:T(8,128)S(1)}, u32[]{:S(2)}, u32[]{:S(2)}) collective-permute-start(f32[8,1792]{1,0:T(8,128)S(1)} %replica_mean.3.refs_0_), channel_id=1, source_target_pairs={{0,24},{4,28},{8,16},{12,20},{16,8},{20,12},{24,0},{28,4},{1,25},{... | collective-permute-start | bytes 172040 | tf_op jit(solution)/shard_map/ppermute | solution.py:342
  60.8 6.4 %collective-permute-start.23 = (f32[8,1792]{1,0:T(8,128)S(1)}, f32[8,1792]{1,0:T(8,128)S(1)}, u32[]{:S(2)}, u32[]{:S(2)}) collective-permute-start(f32[8,1792]{1,0:T(8,128)S(1)} %replica_mean.3.refs_0_), channel_id=1, source_target_pairs={{0,16},{4,20},{8,24},{12,28},{16,0},{20,4},{24,8},{28,12},{1,17},{... | collective-permute-start | bytes 172040 | tf_op jit(solution)/shard_map/ppermute | solution.py:342
  62.1 5.1 %collective-permute-start.22 = (f32[8,1792]{1,0:T(8,128)S(1)}, f32[8,1792]{1,0:T(8,128)S(1)}, u32[]{:S(2)}, u32[]{:S(2)}) collective-permute-start(f32[8,1792]{1,0:T(8,128)S(1)} %replica_mean.3.refs_0_), channel_id=1, source_target_pairs={{0,8},{4,12},{8,0},{12,4},{16,24},{20,28},{24,16},{28,20},{1,9},{5... | collective-permute-start | bytes 172040 | tf_op jit(solution)/shard_map/ppermute | solution.py:342
  67.2 6.6 %collective-permute-start.25 = (f32[4,8,1792]{2,1,0:T(8,128)S(1)}, f32[4,8,1792]{2,1,0:T(8,128)S(1)}, u32[]{:S(2)}, u32[]{:S(2)}) collective-permute-start(f32[4,8,1792]{2,1,0:T(8,128)S(1)} %stack_z.3.refs_4_.mine), channel_id=1, source_target_pairs={{0,4},{4,0},{8,12},{12,8},{16,20},{20,16},{24,28},{28,24},{1,5},{5... | collective-permute-start | bytes 688136 | tf_op jit(solution)/shard_map/ppermute | solution.py:342
  74.6 4.3 %collective-permute-start.28 = (f32[16,640]{1,0:T(8,128)S(1)}, f32[16,640]{1,0:T(8,128)S(1)}, u32[]{:S(2)}, u32[]{:S(2)}) collective-permute-start(f32[16,640]{1,0:T(8,128)S(1)} %get-tuple-element.80.refs_0_), channel_id=1, source_target_pairs={{0,3},{1,2},{2,1},{3,0},{4,7},{5,6},{6,5},{7,4},{8,11},{9,10},{10,... | collective-permute-start | bytes 122888 | tf_op jit(solution)/shard_map/ppermute | solution.py:342
  74.6 4.3 %collective-permute-start.27 = (f32[16,640]{1,0:T(8,128)S(1)}, f32[16,640]{1,0:T(8,128)S(1)}, u32[]{:S(2)}, u32[]{:S(2)}) collective-permute-start(f32[16,640]{1,0:T(8,128)S(1)} %get-tuple-element.80.refs_0_), channel_id=1, source_target_pairs={{0,2},{1,3},{2,0},{3,1},{4,6},{5,7},{6,4},{7,5},{8,10},{9,11},{10,... | collective-permute-start | bytes 122888 | tf_op jit(solution)/shard_map/ppermute | solution.py:342
  76.0 2.9 %collective-permute-start.26 = (f32[16,640]{1,0:T(8,128)S(1)}, f32[16,640]{1,0:T(8,128)S(1)}, u32[]{:S(2)}, u32[]{:S(2)}) collective-permute-start(f32[16,640]{1,0:T(8,128)S(1)} %get-tuple-element.80.refs_0_), channel_id=1, source_target_pairs={{0,1},{1,0},{2,3},{3,2},{4,5},{5,4},{6,7},{7,6},{8,9},{9,8},{10,11... | collective-permute-start | bytes 122888 | tf_op jit(solution)/shard_map/ppermute | solution.py:342

commit v12 on v11

--- a/solution.py
+++ b/solution.py
@@ -139,31 +139,44 @@
     refs[-1][...] = tree_sum(term[...] for term in refs[:-1])
 
 
-def split_z_kernel(keep, got, shard, *refs):
-    *outs, stage = refs
-    _, z = place("dp")
+def own_and_other(j, bit):
+    mine = lax.bitwise_and(lax.shift_right_logical(lax.axis_index("dp"), bit), 1)
+    return 2 * j + mine, 2 * j + 1 - mine
+
+
+def split_chunks(bit, chunks, keep, send):
+    for j in range(keep.shape[0]):
+        mine, other = own_and_other(j, bit)
+        keep[j] = chunks[mine]
+        send[j] = chunks[other]
+
+
+def halve_with_shard_kernel(bit, keep, got, shard, keep_out, send_out, chunks):
     half, per, ff = keep.shape
     block = shard.shape[1] // half
     for c in range(half):
-        stage[c, :, :ff] = keep[c] + got[c]
-        stage[c, :, ff:] = fold(shard[:, c * block : (c + 1) * block], per)
-    for j, out in zip([0, *range(half - 1, 0, -1)], outs):
-        out[...] = stage[lax.bitwise_xor(z, j)]
-
-
-def mean_kernel(n_dp, *refs):
-    refs[-1][...] = tree_sum(ref[...] for ref in refs[:-1]) / n_dp
-
-
-def stack_kernel(*refs):
-    _, z = place("dp")
-    for j, ref in enumerate(refs[:-1]):
-        refs[-1][lax.bitwise_xor(z, j)] = ref[...]
-
-
-def stack_apart_kernel(*refs):
-    *pieces, out, shard, stack = refs
-    stack_kernel(*pieces, stack)
+        chunks[c, :, :ff] = keep[c] + got[c]
+        chunks[c, :, ff:] = fold(shard[:, c * block : (c + 1) * block], per)
+    split_chunks(bit, chunks, keep_out, send_out)
+
+
+def halve_kernel(bit, keep, got, keep_out, send_out, chunks):
+    chunks[...] = keep[...] + got[...]
+    split_chunks(bit, chunks, keep_out, send_out)
+
+
+def sum_kernel(scale, mine, other, out):
+    out[...] = (mine[...] + other[...]) * scale
+
+
+def double_kernel(bit, mine, other, out):
+    for j in range(mine.shape[0]):
+        here, there = own_and_other(j, bit)
+        out[here] = mine[j]
+        out[there] = other[j]
+
+
+def apart_kernel(stack, out, shard):
     half, _, ff = out.shape
     out[...] = stack[:, :, :ff]
     shard[...] = jnp.concatenate([unfold(stack[c, :, ff:], shard.shape[0]) for c in range(half)], axis=1)
@@ -346,20 +359,27 @@
     return [parts[0]] + [swap(parts[j], "tensor", j) for j in range(1, len(parts))]
 
 
-def from_z(parts):
-    got = {j: swap(parts[j], "dp", 2 * j) for j in range(len(parts) - 1, 0, -1)}
-    return [parts[0]] + [got[j] for j in range(1, len(parts))]
-
-
 def mean_replicas(keep, got, shard):
     n_dp = lax.axis_size("dp")
-    half, per, ff = keep.shape
-    piece = shaped(per, ff + shard.shape[0] * shard.shape[1] // (half * per))
-    stage = pltpu.VMEM((half, *piece.shape), F32)
-    parts = call(split_z_kernel, [piece] * half, keep, got, shard, name="split_z", scratch_shapes=[stage])
-    parts = [parts[0], *parts[:0:-1]]
-    mean = call(functools.partial(mean_kernel, n_dp), piece, *from_z(parts), name="replica_mean")
-    return from_z([mean] * half)
+    last = n_dp.bit_length() - 2
+    count, per, ff = keep.shape
+    columns = ff + shard.shape[0] * shard.shape[1] // (count * per)
+    for bit in range(1, last):
+        out = shaped(count // 2, per, columns)
+        kernel, more = (halve_with_shard_kernel, (shard,)) if bit == 1 else (halve_kernel, ())
+        keep, send = call(
+            functools.partial(kernel, bit), [out, out], keep, got, *more, name="halve",
+            scratch_shapes=[pltpu.VMEM((count, per, columns), F32)],
+        )
+        got = swap(send, "dp", 1 << bit)
+        count //= 2
+    total = call(functools.partial(sum_kernel, 1.0), out, keep, got, name="half_sum")
+    mine = call(functools.partial(sum_kernel, 1.0 / n_dp), out, total, swap(total, "dp", 1 << last), name="mean")
+    for bit in range(last - 1, 0, -1):
+        count *= 2
+        out = shaped(count, per, columns)
+        mine = call(functools.partial(double_kernel, bit), out, mine, swap(mine, "dp", 1 << bit), name="double")
+    return mine
 
 
 def on_device(gu, eu, gd, ed, qu, qd):
@@ -388,11 +408,7 @@
     parts = from_shards(parts)
     parts[0], keep = call(fetch_kernel, [shard_rows_here, replica_half], parts[0], keep, name="fetch", flops=product // 4)
     shard = call(first_shards_kernel, shard_rows_here, *parts, name="shard_sum")
-    pieces = mean_replicas(keep, got, shard)
-    mine, shard = call(
-        stack_apart_kernel, [replica_half, shard_rows_here], *pieces, name="stack_z",
-        scratch_shapes=[pltpu.VMEM((half, *pieces[0].shape), F32)],
-    )
+    mine, shard = call(apart_kernel, [replica_half, shard_rows_here], mean_replicas(keep, got, shard), name="apart")
     shard = call(first_shards_kernel, shard_rows_here, shard, swap(shard, "dp", 1), name="replica_sum")
     other = swap(mine, "dp", 1)
     left_rows = from_shards([shard] * n_shards)
@@ -409,8 +425,7 @@
     shard, gram_down = call(
         functools.partial(sum_shards_kernel, n_shards), [shard_rows_here, shaped(rank, rank)], *from_shards(parts), name="shard_sum"
     )
-    pieces = mean_replicas(keep, got, shard)
-    mine = call(stack_kernel, shaped(half, *pieces[0].shape), *pieces, name="stack_z")
+    mine = mean_replicas(keep, got, shard)
     other = swap(mine, "dp", 1)
     inv_up, inv_down, lhs_up, lhs_down = call(
         basis_kernel,

time: 82.6 us -> 82.6 us (level)
  starting transfers between devices: 32.7 us -> 24.2 us
  waiting for transfers between devices: 28.7 us -> 37.2 us
    ppermute x29 -> x23, starting transfers between devices: 32.7 us -> 24.2 us  [swap(): return lax.ppermute(x, axis, pairs)]
    ppermute x29 -> x23, waiting for transfers between devices: 28.7 us -> 37.2 us  [swap(): return lax.ppermute(x, axis, pairs)]
    pallas_call x18 -> x21, Pallas kernels: 18.5 us -> 18.5 us  [call(): pl.pallas_call(kernel, out_shape=out_shape, compiler_params=params, cost_...]
  transfers between devices with their start and end apart: 29 -> 23, of which waited for: 17 -> 16; matrix products, arithmetic and copies ran while one was open for 0% -> 0% of each run, Pallas kernels for 10% -> 10%
where the time goes in v12:
time: 82.6 us; the launch traced here: 82.4 us
  waiting for transfers between devices  37.2 us (45%)
  starting transfers between devices  24.2 us (29%)
  Pallas kernels  18.5 us (22%)
  local copies, waits for them, and re-layouts  1.7 us (2%)
    ppermute x23, waiting for transfers between devices, swap(): return lax.ppermute(x, axis, pairs)  37.2 us
    ppermute x23, starting transfers between devices, swap(): return lax.ppermute(x, axis, pairs)  24.2 us
    pallas_call x21, Pallas kernels, call(): pl.pallas_call(kernel, out_shape=out_shape, compiler_params=params, cost_...  18.5 us
    unnamed x12, local copies, waits for them, and re-layouts  1.7 us
  transfers between devices with their start and end apart: 23, of which 16 were waited for; matrix products, arithmetic and copies ran while one was open for 0% of the time, Pallas kernels for 10%

profile of v12, /device:TPU:0, one launch (start us, length us, event | category | flops | bytes accessed | tf_op | source)
XLA Modules:
  0.0 82.4 jit_solution(3792716498656349929)
XLA Ops:
  0.6 0.0 copy-start.3
  0.6 6.2 %left.1 = (f32[16,512]{1,0:T(8,128)}, f32[16,512]{1,0:T(8,128)}, f32[16,512]{1,0:T(8,128)}, f32[16,512]{1,0:T(8,128)}, f32[4,8,1536]{2,1,0:T(8,128)}, /*index=5*/f32[4,8,1536]{2,1,0:T(8,128)}) custom-call(bf16[1,512,1536]{2,1,0:T(8,128)(2,1)} %g.4, bf16[1,512,1536]{2,1,0:T(8,128)(2,1)} %e.4, f32[64,1536]{1,0:T(8,128)} %bitcast.2, bf16[1,1536,512]{2,1,0:T(8,128)(2,1)} %g.5, ...), custom_call_target="tpu_custom_call" | custom-call | flops 1610612736 | bytes 7340032 | tf_op jit(solution)/shard_map/left/pallas_call | solution.py:350
  6.8 0.0 copy-start.2
  6.8 3.0 %collective-permute-start = (f32[4,8,1536]{2,1,0:T(8,128)}, f32[4,8,1536]{2,1,0:T(8,128)S(1)}, u32[]{:S(2)}, u32[]{:S(2)}) collective-permute-start(f32[4,8,1536]{2,1,0:T(8,128)} %get-tuple-element.45), channel_id=1, source_target_pairs={{0,4},{4,0},{8,12},{12,8},{16,20},{20,16},{24,28},{28,24},{1,5},{5... | collective-permute-start | bytes 589832 | tf_op jit(solution)/shard_map/ppermute | solution.py:355
  9.9 0.0 collective-permute-start.1
  9.9 1.5 %collective-permute-start.2 = (f32[16,512]{1,0:T(8,128)}, f32[16,512]{1,0:T(8,128)S(1)}, u32[]{:S(2)}, u32[]{:S(2)}) collective-permute-start(f32[16,512]{1,0:T(8,128)} %get-tuple-element.48), channel_id=1, source_target_pairs={{0,2},{1,3},{2,0},{3,1},{4,6},{5,7},{6,4},{7,5},{8,10},{9,11},{10,... | collective-permute-start | bytes 98312 | tf_op jit(solution)/shard_map/ppermute | solution.py:355
  11.4 0.4 collective-permute-start.3
  11.7 0.9 %copy-done.4 = f32[4,8,1536]{2,1,0:T(8,128)S(1)} copy-done((f32[4,8,1536]{2,1,0:T(8,128)S(1)}, f32[4,8,1536]{2,1,0:T(8,128)}, u32[]{:S(2)}) %copy-start.4) | copy-done | bytes 196632
  12.7 0.8 copy-done.5
  13.4 0.0 collective-permute-done.1.refs_1_
  13.5 0.6 collective-permute-done.2.refs_2_
  14.0 0.9 %collective-permute-done.3.refs_3_ = f32[16,512]{1,0:T(8,128)S(1)} collective-permute-done((f32[16,512]{1,0:T(8,128)}, f32[16,512]{1,0:T(8,128)S(1)}, u32[]{:S(2)}, u32[]{:S(2)}) %collective-permute-start.3) | collective-permute-done | bytes 32800 | tf_op jit(solution)/shard_map/ppermute | solution.py:355
  14.9 0.1 collective-permute-done.got
  15.0 1.9 %collective-permute-start.4 = (f32[2,8,1792]{2,1,0:T(8,128)S(1)}, f32[2,8,1792]{2,1,0:T(8,128)S(1)}, u32[]{:S(2)}, u32[]{:S(2)}) collective-permute-start(f32[2,8,1792]{2,1,0:T(8,128)S(1)} %get-tuple-element.51), channel_id=1, source_target_pairs={{0,8},{4,12},{8,0},{12,4},{16,24},{20,28},{24,16},{28,20},{1,9},{5... | collective-permute-start | bytes 344072 | tf_op jit(solution)/shard_map/ppermute | solution.py:355
  16.9 3.5 %collective-permute-done.4.other = f32[2,8,1792]{2,1,0:T(8,128)S(1)} collective-permute-done((f32[2,8,1792]{2,1,0:T(8,128)S(1)}, f32[2,8,1792]{2,1,0:T(8,128)S(1)}, u32[]{:S(2)}, u32[]{:S(2)}) %collective-permute-start.4) | collective-permute-done | bytes 114720 | tf_op jit(solution)/shard_map/ppermute | solution.py:355
  20.4 2.8 %collective-permute-start.5 = (f32[2,8,1792]{2,1,0:T(8,128)S(1)}, f32[2,8,1792]{2,1,0:T(8,128)S(1)}, u32[]{:S(2)}, u32[]{:S(2)}) collective-permute-start(f32[2,8,1792]{2,1,0:T(8,128)S(1)} %half_sum.2.mine), channel_id=1, source_target_pairs={{0,16},{4,20},{8,24},{12,28},{16,0},{20,4},{24,8},{28,12},{1,17},{... | collective-permute-start | bytes 344072 | tf_op jit(solution)/shard_map/ppermute | solution.py:355
  23.2 5.1 %collective-permute-done.5.other = f32[2,8,1792]{2,1,0:T(8,128)S(1)} collective-permute-done((f32[2,8,1792]{2,1,0:T(8,128)S(1)}, f32[2,8,1792]{2,1,0:T(8,128)S(1)}, u32[]{:S(2)}, u32[]{:S(2)}) %collective-permute-start.5) | collective-permute-done | bytes 114720 | tf_op jit(solution)/shard_map/ppermute | solution.py:355
  28.3 0.8 collective-permute-start.6
  29.1 4.1 %collective-permute-done.6.other = f32[2,8,1792]{2,1,0:T(8,128)S(1)} collective-permute-done((f32[2,8,1792]{2,1,0:T(8,128)S(1)}, f32[2,8,1792]{2,1,0:T(8,128)S(1)}, u32[]{:S(2)}, u32[]{:S(2)}) %collective-permute-start.6) | collective-permute-done | bytes 114720 | tf_op jit(solution)/shard_map/ppermute | solution.py:355
  33.2 0.5 collective-permute-start.7
  33.7 1.6 %collective-permute-start.11 = (f32[4,8,1536]{2,1,0:T(8,128)S(1)}, f32[4,8,1536]{2,1,0:T(8,128)S(1)}, u32[]{:S(2)}, u32[]{:S(2)}) collective-permute-start(f32[4,8,1536]{2,1,0:T(8,128)S(1)} %get-tuple-element.54.mine), channel_id=1, source_target_pairs={{0,4},{4,0},{8,12},{12,8},{16,20},{20,16},{24,28},{28,24},{1,5},{5... | collective-permute-start | bytes 589832 | tf_op jit(solution)/shard_map/ppermute | solution.py:355
  35.3 1.9 %collective-permute-done.7.refs_1_ = f32[16,512]{1,0:T(8,128)S(1)} collective-permute-done((f32[16,512]{1,0:T(8,128)S(1)}, f32[16,512]{1,0:T(8,128)S(1)}, u32[]{:S(2)}, u32[]{:S(2)}) %collective-permute-start.7) | collective-permute-done | bytes 32800 | tf_op jit(solution)/shard_map/ppermute | solution.py:355
  37.2 0.0 copy-start.1
  37.2 0.1 collective-permute-start.10
  37.3 0.4 collective-permute-start.9
  37.7 1.4 %collective-permute-start.8 = (f32[16,512]{1,0:T(8,128)S(1)}, f32[16,512]{1,0:T(8,128)S(1)}, u32[]{:S(2)}, u32[]{:S(2)}) collective-permute-start(f32[16,512]{1,0:T(8,128)S(1)} %replica_sum.1.refs_0_), channel_id=1, source_target_pairs={{0,1},{1,0},{2,3},{3,2},{4,5},{5,4},{6,7},{7,6},{8,9},{9,8},{10,11... | collective-permute-start | bytes 98312 | tf_op jit(solution)/shard_map/ppermute | solution.py:355
  39.1 1.5 %collective-permute-done.10.refs_3_ = f32[16,512]{1,0:T(8,128)S(1)} collective-permute-done((f32[16,512]{1,0:T(8,128)S(1)}, f32[16,512]{1,0:T(8,128)S(1)}, u32[]{:S(2)}, u32[]{:S(2)}) %collective-permute-start.10) | collective-permute-done | bytes 32800 | tf_op jit(solution)/shard_map/ppermute | solution.py:355
  40.6 0.7 collective-permute-done.9.refs_2_
  41.3 0.0 collective-permute-done.8.refs_1_
  41.3 0.0 copy-done.3
  41.3 0.0 copy-done.2
  41.3 1.2 %right_up.1 = (f32[64,512]{1,0:T(8,128)S(1)}, f32[64,64]{1,0:T(8,128)S(1)}, f32[4,8,1536]{2,1,0:T(8,128)S(1)}, f32[4,8,1536]{2,1,0:T(8,128)S(1)}) custom-call(f32[16,512]{1,0:T(8,128)S(1)} %replica_sum.1.refs_0_, f32[16,512]{1,0:T(8,128)S(1)} %collective-permute-done.8.refs_1_, f32[16,512]{1,0:T(8,128)S(1)} %collective-permute-done.9.refs_2_, ...), custom_call_target="tpu_custom_call" | custom-call | flops 805306368 | bytes 3817472 | tf_op jit(solution)/shard_map/right_up/pallas_call | solution.py:350
  42.5 0.5 collective-permute-start.15
  43.1 0.0 collective-permute-done.11.other
  43.1 0.0 copy-done
  43.1 0.0 copy-done.1
  43.1 1.2 %right_down.1 = (f32[64,1536]{1,0:T(8,128)S(1)}, f32[16,768]{1,0:T(8,128)S(1)}, f32[16,768]{1,0:T(8,128)S(1)}, f32[16,768]{1,0:T(8,128)S(1)}, f32[16,768]{1,0:T(8,128)S(1)}) custom-call(f32[64,512]{1,0:T(8,128)S(1)} %get-tuple-element.53._.left_up, f32[4,8,1536]{2,1,0:T(8,128)S(1)} %get-tuple-element.54.mine, ...), custom_call_target="tpu_custom_call" | custom-call | flops 805306368 | bytes 4259840 | tf_op jit(solution)/shard_map/right_down/pallas_call | solution.py:350
  44.3 0.1 collective-permute-start.12
  44.4 1.5 %collective-permute-start.13 = (f32[16,768]{1,0:T(8,128)S(1)}, f32[16,768]{1,0:T(8,128)S(1)}, u32[]{:S(2)}, u32[]{:S(2)}) collective-permute-start(f32[16,768]{1,0:T(8,128)S(1)} %get-tuple-element.59), channel_id=1, source_target_pairs={{0,2},{1,3},{2,0},{3,1},{4,6},{5,7},{6,4},{7,5},{8,10},{9,11},{10,... | collective-permute-start | bytes 147464 | tf_op jit(solution)/shard_map/ppermute | solution.py:355
  45.9 0.3 collective-permute-start.14
  46.2 0.0 collective-permute-done.12.refs_1_
  46.2 2.3 %collective-permute-done.13.refs_2_ = f32[16,768]{1,0:T(8,128)S(1)} collective-permute-done((f32[16,768]{1,0:T(8,128)S(1)}, f32[16,768]{1,0:T(8,128)S(1)}, u32[]{:S(2)}, u32[]{:S(2)}) %collective-permute-start.13) | collective-permute-done | bytes 49184 | tf_op jit(solution)/shard_map/ppermute | solution.py:355
  48.5 1.1 %collective-permute-done.14.refs_3_ = f32[16,768]{1,0:T(8,128)S(1)} collective-permute-done((f32[16,768]{1,0:T(8,128)S(1)}, f32[16,768]{1,0:T(8,128)S(1)}, u32[]{:S(2)}, u32[]{:S(2)}) %collective-permute-start.14) | collective-permute-done | bytes 49184 | tf_op jit(solution)/shard_map/ppermute | solution.py:355
  49.6 0.1 shard_sum.3
  49.7 0.0 collective-permute-done.15.got
  49.7 0.9 %collective-permute-start.16 = (f32[2,8,1792]{2,1,0:T(8,128)S(1)}, f32[2,8,1792]{2,1,0:T(8,128)S(1)}, u32[]{:S(2)}, u32[]{:S(2)}) collective-permute-start(f32[2,8,1792]{2,1,0:T(8,128)S(1)} %get-tuple-element.66), channel_id=1, source_target_pairs={{0,8},{4,12},{8,0},{12,4},{16,24},{20,28},{24,16},{28,20},{1,9},{5... | collective-permute-start | bytes 344072 | tf_op jit(solution)/shard_map/ppermute | solution.py:355
  50.6 4.4 %collective-permute-done.16.other = f32[2,8,1792]{2,1,0:T(8,128)S(1)} collective-permute-done((f32[2,8,1792]{2,1,0:T(8,128)S(1)}, f32[2,8,1792]{2,1,0:T(8,128)S(1)}, u32[]{:S(2)}, u32[]{:S(2)}) %collective-permute-start.16) | collective-permute-done | bytes 114720 | tf_op jit(solution)/shard_map/ppermute | solution.py:355
  55.0 2.6 %collective-permute-start.17 = (f32[2,8,1792]{2,1,0:T(8,128)S(1)}, f32[2,8,1792]{2,1,0:T(8,128)S(1)}, u32[]{:S(2)}, u32[]{:S(2)}) collective-permute-start(f32[2,8,1792]{2,1,0:T(8,128)S(1)} %half_sum.3.mine), channel_id=1, source_target_pairs={{0,16},{4,20},{8,24},{12,28},{16,0},{20,4},{24,8},{28,12},{1,17},{... | collective-permute-start | bytes 344072 | tf_op jit(solution)/shard_map/ppermute | solution.py:355
  57.6 5.4 %collective-permute-done.17.other = f32[2,8,1792]{2,1,0:T(8,128)S(1)} collective-permute-done((f32[2,8,1792]{2,1,0:T(8,128)S(1)}, f32[2,8,1792]{2,1,0:T(8,128)S(1)}, u32[]{:S(2)}, u32[]{:S(2)}) %collective-permute-start.17) | collective-permute-done | bytes 114720 | tf_op jit(solution)/shard_map/ppermute | solution.py:355
  63.0 0.8 collective-permute-start.18
  63.8 4.1 %collective-permute-done.18.other = f32[2,8,1792]{2,1,0:T(8,128)S(1)} collective-permute-done((f32[2,8,1792]{2,1,0:T(8,128)S(1)}, f32[2,8,1792]{2,1,0:T(8,128)S(1)}, u32[]{:S(2)}, u32[]{:S(2)}) %collective-permute-start.18) | collective-permute-done | bytes 114720 | tf_op jit(solution)/shard_map/ppermute | solution.py:355
  67.9 1.2 %collective-permute-start.19 = (f32[4,8,1792]{2,1,0:T(8,128)S(1)}, f32[4,8,1792]{2,1,0:T(8,128)S(1)}, u32[]{:S(2)}, u32[]{:S(2)}) collective-permute-start(f32[4,8,1792]{2,1,0:T(8,128)S(1)} %double.3.refs_4_.mine), channel_id=1, source_target_pairs={{0,4},{4,0},{8,12},{12,8},{16,20},{20,16},{24,28},{28,24},{1,5},{5... | collective-permute-start | bytes 688136 | tf_op jit(solution)/shard_map/ppermute | solution.py:355
  69.1 3.2 %basis.1 = (f32[64,64]{1,0:T(8,128)S(1)}, f32[64,64]{1,0:T(8,128)S(1)}, bf16[512,256]{1,0:T(8,128)(2,1)S(1)}, bf16[1536,256]{1,0:T(8,128)(2,1)S(1)}) custom-call(f32[64,512]{1,0:T(8,128)S(1)} %get-tuple-element.53._.left_up, f32[64,1536]{1,0:T(8,128)S(1)} %get-tuple-element.55.left_down, f32[64,64]{1,0:T(8,128)S(1)} %get-tuple-element.56.gram_up, ...), custom_call_target="tpu_custom_call" | custom-call | bytes 8159232 | tf_op jit(solution)/shard_map/basis/pallas_call | solution.py:350
  72.3 1.7 %collective-permute-done.19.other = f32[4,8,1792]{2,1,0:T(8,128)S(1)} collective-permute-done((f32[4,8,1792]{2,1,0:T(8,128)S(1)}, f32[4,8,1792]{2,1,0:T(8,128)S(1)}, u32[]{:S(2)}, u32[]{:S(2)}) %collective-permute-start.19) | collective-permute-done | bytes 229408 | tf_op jit(solution)/shard_map/ppermute | solution.py:355
  74.0 0.7 factor_up.1
  74.7 0.1 collective-permute-start.22
  74.7 1.3 %collective-permute-start.21 = (f32[16,640]{1,0:T(8,128)S(1)}, f32[16,640]{1,0:T(8,128)S(1)}, u32[]{:S(2)}, u32[]{:S(2)}) collective-permute-start(f32[16,640]{1,0:T(8,128)S(1)} %get-tuple-element.72.refs_0_), channel_id=1, source_target_pairs={{0,2},{1,3},{2,0},{3,1},{4,6},{5,7},{6,4},{7,5},{8,10},{9,11},{10,... | collective-permute-start | bytes 122888 | tf_op jit(solution)/shard_map/ppermute | solution.py:355
  76.0 0.6 collective-permute-start.20
  76.6 2.3 %error_up.1 = (bf16[1,512,1536]{2,1,0:T(8,128)(2,1)}, f32[8,128]{1,0:T(8,128)S(1)}) custom-call(bf16[1,512,1536]{2,1,0:T(8,128)(2,1)S(1)} %copy-done.2, bf16[1,512,1536]{2,1,0:T(8,128)(2,1)S(1)} %copy-done.3, bf16[512,256]{1,0:T(8,128)(2,1)S(1)} %get-tuple-element.67.lhs.lhs_up, bf16[256,1536]{1,0:T(8,128)(2,1)S(1)} %get-tuple-element.69.rhs.rhs_up), custom_call_target="tpu_custom_call" | custom-call | flops 402653184 | bytes 5771264 | tf_op jit(solution)/shard_map/error_up/pallas_call | solution.py:350
  78.9 0.0 collective-permute-done.22.refs_3_
  78.9 0.1 collective-permute-done.21.refs_2_
  79.0 0.0 collective-permute-done.20.refs_1_
  79.0 0.4 factor_down.1
  79.4 3.0 %last.1 = (bf16[1,1536,512]{2,1,0:T(8,128)(2,1)}, bf16[512,1536]{1,0:T(8,128)(2,1)}, bf16[1536,512]{1,0:T(8,128)(2,1)}) custom-call(bf16[1,1536,512]{2,1,0:T(8,128)(2,1)S(1)} %copy-done, bf16[1,1536,512]{2,1,0:T(8,128)(2,1)S(1)} %copy-done.1, bf16[512,256]{1,0:T(8,128)(2,1)S(1)} %get-tuple-element.67.lhs.lhs_up, ...), custom_call_target="tpu_custom_call" | custom-call | flops 805306368 | bytes 9965568 | tf_op jit(solution)/shard_map/last/pallas_call | solution.py:350
  (15 shorter events, 0.2 us)
Async XLA Ops:
  0.6 40.7 %copy-start.3 = (bf16[1,512,1536]{2,1,0:T(8,128)(2,1)S(1)}, bf16[1,512,1536]{2,1,0:T(8,128)(2,1)}, u32[]{:S(2)}) copy-start(bf16[1,512,1536]{2,1,0:T(8,128)(2,1)} %e.4) | copy-start | bytes 4718596
  6.8 34.5 %copy-start.2 = (bf16[1,512,1536]{2,1,0:T(8,128)(2,1)S(1)}, bf16[1,512,1536]{2,1,0:T(8,128)(2,1)}, u32[]{:S(2)}) copy-start(bf16[1,512,1536]{2,1,0:T(8,128)(2,1)} %g.4) | copy-start | bytes 4718596
  6.8 8.1 %collective-permute-start = (f32[4,8,1536]{2,1,0:T(8,128)}, f32[4,8,1536]{2,1,0:T(8,128)S(1)}, u32[]{:S(2)}, u32[]{:S(2)}) collective-permute-start(f32[4,8,1536]{2,1,0:T(8,128)} %get-tuple-element.45), channel_id=1, source_target_pairs={{0,4},{4,0},{8,12},{12,8},{16,20},{20,16},{24,28},{28,24},{1,5},{5... | collective-permute-start | bytes 589832 | tf_op jit(solution)/shard_map/ppermute | solution.py:355
  9.9 3.6 %collective-permute-start.1 = (f32[16,512]{1,0:T(8,128)}, f32[16,512]{1,0:T(8,128)S(1)}, u32[]{:S(2)}, u32[]{:S(2)}) collective-permute-start(f32[16,512]{1,0:T(8,128)} %get-tuple-element.47), channel_id=1, source_target_pairs={{0,1},{1,0},{2,3},{3,2},{4,5},{5,4},{6,7},{7,6},{8,9},{9,8},{10,11... | collective-permute-start | bytes 98312 | tf_op jit(solution)/shard_map/ppermute | solution.py:355
  9.9 4.1 %collective-permute-start.2 = (f32[16,512]{1,0:T(8,128)}, f32[16,512]{1,0:T(8,128)S(1)}, u32[]{:S(2)}, u32[]{:S(2)}) collective-permute-start(f32[16,512]{1,0:T(8,128)} %get-tuple-element.48), channel_id=1, source_target_pairs={{0,2},{1,3},{2,0},{3,1},{4,6},{5,7},{6,4},{7,5},{8,10},{9,11},{10,... | collective-permute-start | bytes 98312 | tf_op jit(solution)/shard_map/ppermute | solution.py:355
  11.4 3.6 %collective-permute-start.3 = (f32[16,512]{1,0:T(8,128)}, f32[16,512]{1,0:T(8,128)S(1)}, u32[]{:S(2)}, u32[]{:S(2)}) collective-permute-start(f32[16,512]{1,0:T(8,128)} %get-tuple-element.49), channel_id=1, source_target_pairs={{0,3},{1,2},{2,1},{3,0},{4,7},{5,6},{6,5},{7,4},{8,11},{9,10},{10,... | collective-permute-start | bytes 98312 | tf_op jit(solution)/shard_map/ppermute | solution.py:355
  11.7 0.9 %copy-start.4 = (f32[4,8,1536]{2,1,0:T(8,128)S(1)}, f32[4,8,1536]{2,1,0:T(8,128)}, u32[]{:S(2)}) copy-start(f32[4,8,1536]{2,1,0:T(8,128)} %get-tuple-element.43.refs_1_) | copy-start | bytes 589828
  12.7 0.8 copy-start.5
  15.0 5.3 %collective-permute-start.4 = (f32[2,8,1792]{2,1,0:T(8,128)S(1)}, f32[2,8,1792]{2,1,0:T(8,128)S(1)}, u32[]{:S(2)}, u32[]{:S(2)}) collective-permute-start(f32[2,8,1792]{2,1,0:T(8,128)S(1)} %get-tuple-element.51), channel_id=1, source_target_pairs={{0,8},{4,12},{8,0},{12,4},{16,24},{20,28},{24,16},{28,20},{1,9},{5... | collective-permute-start | bytes 344072 | tf_op jit(solution)/shard_map/ppermute | solution.py:355
  20.4 7.9 %collective-permute-start.5 = (f32[2,8,1792]{2,1,0:T(8,128)S(1)}, f32[2,8,1792]{2,1,0:T(8,128)S(1)}, u32[]{:S(2)}, u32[]{:S(2)}) collective-permute-start(f32[2,8,1792]{2,1,0:T(8,128)S(1)} %half_sum.2.mine), channel_id=1, source_target_pairs={{0,16},{4,20},{8,24},{12,28},{16,0},{20,4},{24,8},{28,12},{1,17},{... | collective-permute-start | bytes 344072 | tf_op jit(solution)/shard_map/ppermute | solution.py:355
  28.3 4.9 %collective-permute-start.6 = (f32[2,8,1792]{2,1,0:T(8,128)S(1)}, f32[2,8,1792]{2,1,0:T(8,128)S(1)}, u32[]{:S(2)}, u32[]{:S(2)}) collective-permute-start(f32[2,8,1792]{2,1,0:T(8,128)S(1)} %mean.2.mine), channel_id=1, source_target_pairs={{0,8},{4,12},{8,0},{12,4},{16,24},{20,28},{24,16},{28,20},{1,9},{5... | collective-permute-start | bytes 344072 | tf_op jit(solution)/shard_map/ppermute | solution.py:355
  33.2 4.0 %collective-permute-start.7 = (f32[16,512]{1,0:T(8,128)S(1)}, f32[16,512]{1,0:T(8,128)S(1)}, u32[]{:S(2)}, u32[]{:S(2)}) collective-permute-start(f32[16,512]{1,0:T(8,128)S(1)} %get-tuple-element.52.refs_0_), channel_id=1, source_target_pairs={{0,4},{4,0},{8,12},{12,8},{16,20},{20,16},{24,28},{28,24},{1,5},{5... | collective-permute-start | bytes 98312 | tf_op jit(solution)/shard_map/ppermute | solution.py:355
  33.7 9.3 %collective-permute-start.11 = (f32[4,8,1536]{2,1,0:T(8,128)S(1)}, f32[4,8,1536]{2,1,0:T(8,128)S(1)}, u32[]{:S(2)}, u32[]{:S(2)}) collective-permute-start(f32[4,8,1536]{2,1,0:T(8,128)S(1)} %get-tuple-element.54.mine), channel_id=1, source_target_pairs={{0,4},{4,0},{8,12},{12,8},{16,20},{20,16},{24,28},{28,24},{1,5},{5... | collective-permute-start | bytes 589832 | tf_op jit(solution)/shard_map/ppermute | solution.py:355
  37.2 5.9 %copy-start = (bf16[1,1536,512]{2,1,0:T(8,128)(2,1)S(1)}, bf16[1,1536,512]{2,1,0:T(8,128)(2,1)}, u32[]{:S(2)}) copy-start(bf16[1,1536,512]{2,1,0:T(8,128)(2,1)} %g.5) | copy-start | bytes 4718596
  37.2 5.9 %copy-start.1 = (bf16[1,1536,512]{2,1,0:T(8,128)(2,1)S(1)}, bf16[1,1536,512]{2,1,0:T(8,128)(2,1)}, u32[]{:S(2)}) copy-start(bf16[1,1536,512]{2,1,0:T(8,128)(2,1)} %e.5) | copy-start | bytes 4718596
  37.2 3.4 %collective-permute-start.10 = (f32[16,512]{1,0:T(8,128)S(1)}, f32[16,512]{1,0:T(8,128)S(1)}, u32[]{:S(2)}, u32[]{:S(2)}) collective-permute-start(f32[16,512]{1,0:T(8,128)S(1)} %replica_sum.1.refs_0_), channel_id=1, source_target_pairs={{0,3},{1,2},{2,1},{3,0},{4,7},{5,6},{6,5},{7,4},{8,11},{9,10},{10,... | collective-permute-start | bytes 98312 | tf_op jit(solution)/shard_map/ppermute | solution.py:355
  37.3 4.0 %collective-permute-start.9 = (f32[16,512]{1,0:T(8,128)S(1)}, f32[16,512]{1,0:T(8,128)S(1)}, u32[]{:S(2)}, u32[]{:S(2)}) collective-permute-start(f32[16,512]{1,0:T(8,128)S(1)} %replica_sum.1.refs_0_), channel_id=1, source_target_pairs={{0,2},{1,3},{2,0},{3,1},{4,6},{5,7},{6,4},{7,5},{8,10},{9,11},{10,... | collective-permute-start | bytes 98312 | tf_op jit(solution)/shard_map/ppermute | solution.py:355
  37.7 3.6 %collective-permute-start.8 = (f32[16,512]{1,0:T(8,128)S(1)}, f32[16,512]{1,0:T(8,128)S(1)}, u32[]{:S(2)}, u32[]{:S(2)}) collective-permute-start(f32[16,512]{1,0:T(8,128)S(1)} %replica_sum.1.refs_0_), channel_id=1, source_target_pairs={{0,1},{1,0},{2,3},{3,2},{4,5},{5,4},{6,7},{7,6},{8,9},{9,8},{10,11... | collective-permute-start | bytes 98312 | tf_op jit(solution)/shard_map/ppermute | solution.py:355
  42.5 7.1 %collective-permute-start.15 = (f32[4,8,1536]{2,1,0:T(8,128)S(1)}, f32[4,8,1536]{2,1,0:T(8,128)S(1)}, u32[]{:S(2)}, u32[]{:S(2)}) collective-permute-start(f32[4,8,1536]{2,1,0:T(8,128)S(1)} %get-tuple-element.63), channel_id=1, source_target_pairs={{0,4},{4,0},{8,12},{12,8},{16,20},{20,16},{24,28},{28,24},{1,5},{5... | collective-permute-start | bytes 589832 | tf_op jit(solution)/shard_map/ppermute | solution.py:355
  44.3 1.9 %collective-permute-start.12 = (f32[16,768]{1,0:T(8,128)S(1)}, f32[16,768]{1,0:T(8,128)S(1)}, u32[]{:S(2)}, u32[]{:S(2)}) collective-permute-start(f32[16,768]{1,0:T(8,128)S(1)} %get-tuple-element.58), channel_id=1, source_target_pairs={{0,1},{1,0},{2,3},{3,2},{4,5},{5,4},{6,7},{7,6},{8,9},{9,8},{10,11... | collective-permute-start | bytes 147464 | tf_op jit(solution)/shard_map/ppermute | solution.py:355
  44.4 4.1 %collective-permute-start.13 = (f32[16,768]{1,0:T(8,128)S(1)}, f32[16,768]{1,0:T(8,128)S(1)}, u32[]{:S(2)}, u32[]{:S(2)}) collective-permute-start(f32[16,768]{1,0:T(8,128)S(1)} %get-tuple-element.59), channel_id=1, source_target_pairs={{0,2},{1,3},{2,0},{3,1},{4,6},{5,7},{6,4},{7,5},{8,10},{9,11},{10,... | collective-permute-start | bytes 147464 | tf_op jit(solution)/shard_map/ppermute | solution.py:355
  45.9 3.7 %collective-permute-start.14 = (f32[16,768]{1,0:T(8,128)S(1)}, f32[16,768]{1,0:T(8,128)S(1)}, u32[]{:S(2)}, u32[]{:S(2)}) collective-permute-start(f32[16,768]{1,0:T(8,128)S(1)} %get-tuple-element.60), channel_id=1, source_target_pairs={{0,3},{1,2},{2,1},{3,0},{4,7},{5,6},{6,5},{7,4},{8,11},{9,10},{10,... | collective-permute-start | bytes 147464 | tf_op jit(solution)/shard_map/ppermute | solution.py:355
  49.7 5.3 %collective-permute-start.16 = (f32[2,8,1792]{2,1,0:T(8,128)S(1)}, f32[2,8,1792]{2,1,0:T(8,128)S(1)}, u32[]{:S(2)}, u32[]{:S(2)}) collective-permute-start(f32[2,8,1792]{2,1,0:T(8,128)S(1)} %get-tuple-element.66), channel_id=1, source_target_pairs={{0,8},{4,12},{8,0},{12,4},{16,24},{20,28},{24,16},{28,20},{1,9},{5... | collective-permute-start | bytes 344072 | tf_op jit(solution)/shard_map/ppermute | solution.py:355
  55.0 8.0 %collective-permute-start.17 = (f32[2,8,1792]{2,1,0:T(8,128)S(1)}, f32[2,8,1792]{2,1,0:T(8,128)S(1)}, u32[]{:S(2)}, u32[]{:S(2)}) collective-permute-start(f32[2,8,1792]{2,1,0:T(8,128)S(1)} %half_sum.3.mine), channel_id=1, source_target_pairs={{0,16},{4,20},{8,24},{12,28},{16,0},{20,4},{24,8},{28,12},{1,17},{... | collective-permute-start | bytes 344072 | tf_op jit(solution)/shard_map/ppermute | solution.py:355
  63.0 4.9 %collective-permute-start.18 = (f32[2,8,1792]{2,1,0:T(8,128)S(1)}, f32[2,8,1792]{2,1,0:T(8,128)S(1)}, u32[]{:S(2)}, u32[]{:S(2)}) collective-permute-start(f32[2,8,1792]{2,1,0:T(8,128)S(1)} %mean.3.mine), channel_id=1, source_target_pairs={{0,8},{4,12},{8,0},{12,4},{16,24},{20,28},{24,16},{28,20},{1,9},{5... | collective-permute-start | bytes 344072 | tf_op jit(solution)/shard_map/ppermute | solution.py:355
  67.9 6.1 %collective-permute-start.19 = (f32[4,8,1792]{2,1,0:T(8,128)S(1)}, f32[4,8,1792]{2,1,0:T(8,128)S(1)}, u32[]{:S(2)}, u32[]{:S(2)}) collective-permute-start(f32[4,8,1792]{2,1,0:T(8,128)S(1)} %double.3.refs_4_.mine), channel_id=1, source_target_pairs={{0,4},{4,0},{8,12},{12,8},{16,20},{20,16},{24,28},{28,24},{1,5},{5... | collective-permute-start | bytes 688136 | tf_op jit(solution)/shard_map/ppermute | solution.py:355
  74.7 4.3 %collective-permute-start.22 = (f32[16,640]{1,0:T(8,128)S(1)}, f32[16,640]{1,0:T(8,128)S(1)}, u32[]{:S(2)}, u32[]{:S(2)}) collective-permute-start(f32[16,640]{1,0:T(8,128)S(1)} %get-tuple-element.72.refs_0_), channel_id=1, source_target_pairs={{0,3},{1,2},{2,1},{3,0},{4,7},{5,6},{6,5},{7,4},{8,11},{9,10},{10,... | collective-permute-start | bytes 122888 | tf_op jit(solution)/shard_map/ppermute | solution.py:355
  74.7 4.2 %collective-permute-start.21 = (f32[16,640]{1,0:T(8,128)S(1)}, f32[16,640]{1,0:T(8,128)S(1)}, u32[]{:S(2)}, u32[]{:S(2)}) collective-permute-start(f32[16,640]{1,0:T(8,128)S(1)} %get-tuple-element.72.refs_0_), channel_id=1, source_target_pairs={{0,2},{1,3},{2,0},{3,1},{4,6},{5,7},{6,4},{7,5},{8,10},{9,11},{10,... | collective-permute-start | bytes 122888 | tf_op jit(solution)/shard_map/ppermute | solution.py:355
  76.0 3.0 %collective-permute-start.20 = (f32[16,640]{1,0:T(8,128)S(1)}, f32[16,640]{1,0:T(8,128)S(1)}, u32[]{:S(2)}, u32[]{:S(2)}) collective-permute-start(f32[16,640]{1,0:T(8,128)S(1)} %get-tuple-element.72.refs_0_), channel_id=1, source_target_pairs={{0,1},{1,0},{2,3},{3,2},{4,5},{5,4},{6,7},{7,6},{8,9},{9,8},{10,11... | collective-permute-start | bytes 122888 | tf_op jit(solution)/shard_map/ppermute | solution.py:355

commit v13 on v12

--- a/solution.py
+++ b/solution.py
@@ -88,44 +88,46 @@
         total[pl.ds(pl.multiple_of(owner * rows, rows), rows), :] = piece[:, :width]
 
 
-def left_kernel(n_shards, gu, eu, qu, gd, ed, qd, *refs):
-    *outs, gu_in, eu_in, qu_in, pieces_up, total_up, gd_in, ed_in, qd_in, pieces_down, total_down, stage, q_sems, sems = refs
-    up, down = (qu_in, pieces_up, total_up), (qd_in, pieces_down, total_down)
-    firsts = [pltpu.make_async_copy(src, dst, q_sems.at[i]) for i, (src, dst) in enumerate(((qd, qd_in), (qu, qu_in)))]
+def left_product(g, e, q, g_in, e_in, q_in, pieces, total, sems):
+    count = sems.shape[0] - 1
+    block = g_in.shape[0] // count
+    first = pltpu.make_async_copy(q, q_in, sems.at[count, 0])
     stages = []
-    for g, e, g_in, e_in, part, count in ((gd, ed, gd_in, ed_in, down, 3), (gu, eu, gu_in, eu_in, up, 2)):
-        block = g_in.shape[0] // count
-        for i in range(count):
-            rows = pl.ds(i * block, block)
-            n = len(stages)
-            copies = [pltpu.make_async_copy(src.at[0, rows, :], dst.at[rows, :], sems.at[n, k]) for k, (src, dst) in enumerate(((g, g_in), (e, e_in)))]
-            stages.append((copies, g_in, e_in, slice(i * block, (i + 1) * block), part))
+    for i in range(count):
+        rows = pl.ds(i * block, block)
+        stages.append([pltpu.make_async_copy(src.at[0, rows, :], dst.at[rows, :], sems.at[i, k]) for k, (src, dst) in enumerate(((g, g_in), (e, e_in)))])
 
     def fetch(n):
-        if n < len(stages):
-            for copy in stages[n][0]:
+        if n < count:
+            for copy in stages[n]:
                 copy.start()
 
-    firsts[0].start()
+    first.start()
     fetch(0)
-    firsts[1].start()
-    for n, (first, (q, pieces, _)) in enumerate(zip(firsts, (down, up))):
-        first.wait()
-        fetch(n + 1)
-        split_rows(q, pieces)
-    for n, (copies, g, e, rows, (_, pieces, total)) in enumerate(stages):
+    first.wait()
+    fetch(1)
+    split_rows(q_in, pieces)
+    for i, copies in enumerate(stages):
         for copy in copies:
             copy.wait()
-        fetch(n + 3)
-        total[:, rows] = add_pieces(dot(pieces[...], g[rows, :], NT) + dot(pieces[...], e[rows, :], NT))
-    split_shards(total_up, None, outs[:n_shards])
-    split_replicas(total_down, stage, *outs[n_shards:])
-
-
-def fetch_kernel(*refs):
-    half = len(refs) // 2
-    for source, out in zip(refs[:half], refs[half:]):
-        out[...] = source[...]
+        fetch(i + 2)
+        rows = slice(i * block, (i + 1) * block)
+        total[:, rows] = add_pieces(dot(pieces[...], g_in[rows, :], NT) + dot(pieces[...], e_in[rows, :], NT))
+
+
+def left_up_kernel(g, e, q, *refs):
+    *outs, g_in, e_in, q_in, pieces, total, sems = refs
+    left_product(g, e, q, g_in, e_in, q_in, pieces, total, sems)
+    split_shards(total, None, outs)
+
+
+def left_down_kernel(g, e, q, keep, send, g_in, e_in, q_in, pieces, total, sems, stage):
+    left_product(g, e, q, g_in, e_in, q_in, pieces, total, sems)
+    split_replicas(total, stage, keep, send)
+
+
+def fetch_kernel(source, out):
+    out[...] = source[...]
 
 
 def sum_shards_kernel(n_shards, *refs):
@@ -151,15 +153,6 @@
         send[j] = chunks[other]
 
 
-def halve_with_shard_kernel(bit, keep, got, shard, keep_out, send_out, chunks):
-    half, per, ff = keep.shape
-    block = shard.shape[1] // half
-    for c in range(half):
-        chunks[c, :, :ff] = keep[c] + got[c]
-        chunks[c, :, ff:] = fold(shard[:, c * block : (c + 1) * block], per)
-    split_chunks(bit, chunks, keep_out, send_out)
-
-
 def halve_kernel(bit, keep, got, keep_out, send_out, chunks):
     chunks[...] = keep[...] + got[...]
     split_chunks(bit, chunks, keep_out, send_out)
@@ -176,10 +169,33 @@
         out[there] = other[j]
 
 
-def apart_kernel(stack, out, shard):
-    half, _, ff = out.shape
-    out[...] = stack[:, :, :ff]
-    shard[...] = jnp.concatenate([unfold(stack[c, :, ff:], shard.shape[0]) for c in range(half)], axis=1)
+def half_sum_kernel(keep, got, shard, out):
+    count, per, ff = keep.shape
+    block = shard.shape[1] // count
+    for c in range(count):
+        out[c, :, :ff] = keep[c] + got[c]
+        out[c, :, ff:] = fold(shard[:, c * block : (c + 1) * block], per)
+
+
+def join_shard(chunks, ff, rows):
+    return jnp.concatenate([unfold(chunks[c, :, ff:], rows) for c in range(chunks.shape[0])], axis=1)
+
+
+def double_apart_kernel(bit, mine, other, out, shard):
+    ff = out.shape[2]
+    for j in range(mine.shape[0]):
+        here, there = own_and_other(j, bit)
+        out[here] = mine[j, :, :ff]
+        out[there] = other[j, :, :ff]
+    shard[...] = join_shard(mine, ff, shard.shape[0]) + join_shard(other, ff, shard.shape[0])
+
+
+def add_columns_kernel(chunks, shard, out):
+    count, per, ff = chunks.shape
+    block = shard.shape[1] // count
+    for c in range(count):
+        out[c, :, :ff] = chunks[c]
+        out[c, :, ff:] = fold(shard[:, c * block : (c + 1) * block], per)
 
 
 def shard_rows(mine, other, ff, rows):
@@ -198,7 +214,7 @@
     return t[:rank] + (t[rank : 2 * rank] + t[2 * rank :])
 
 
-def right_down_kernel(_, mine, other, g, e, left, *refs):
+def right_down_kernel(mine, other, g, e, left, *refs):
     *outs, pieces, total, stage = refs
     join_replicas(mine, other, stage, left)
     split_rows(left, pieces)
@@ -342,12 +358,15 @@
 ANY = pl.BlockSpec(memory_space=pl.ANY)
 
 
-def call(kernel, out_shape, *args, flops=0, limit=12, name=None, **more):
+def call(kernel, out_shape, *args, after=(), in_specs=None, flops=0, limit=12, name=None, **more):
     arrays = list(args) + jax.tree.leaves(out_shape)
     size = sum(a.size * a.dtype.itemsize for a in arrays)
-    cost = pl.CostEstimate(flops=flops, bytes_accessed=size, transcendentals=0)
-    params = pltpu.CompilerParams(vmem_limit_bytes=limit * MIB)
-    return pl.pallas_call(kernel, out_shape=out_shape, compiler_params=params, cost_estimate=cost, name=name, **more)(*args)
+    skip = len(after)
+    return pl.pallas_call(
+        lambda *refs: kernel(*refs[skip:]), out_shape=out_shape, in_specs=[ANY] * skip + (in_specs or [VMEM] * len(args)),
+        compiler_params=pltpu.CompilerParams(vmem_limit_bytes=limit * MIB),
+        cost_estimate=pl.CostEstimate(flops=flops, bytes_accessed=size, transcendentals=0), name=name, **more,
+    )(*after, *args)
 
 
 def swap(x, axis, distance):
@@ -359,27 +378,41 @@
     return [parts[0]] + [swap(parts[j], "tensor", j) for j in range(1, len(parts))]
 
 
-def mean_replicas(keep, got, shard):
+def scatter_replicas(keep, send, got, after):
+    n_dp = lax.axis_size("dp")
+    for bit in range(n_dp.bit_length() - 2):
+        got = swap(send, "dp", 1 << bit) if bit else got
+        if bit == n_dp.bit_length() - 3:
+            return keep, got
+        count, per, ff = keep.shape
+        out = shaped(count // 2, per, ff)
+        keep, send = call(
+            functools.partial(halve_kernel, bit + 1), [out, out], keep, got, after=after if bit == 0 else (), name="halve",
+            scratch_shapes=[pltpu.VMEM(keep.shape, F32)],
+        )
+
+
+def gather_replicas(keep, got, shard):
     n_dp = lax.axis_size("dp")
     last = n_dp.bit_length() - 2
     count, per, ff = keep.shape
     columns = ff + shard.shape[0] * shard.shape[1] // (count * per)
-    for bit in range(1, last):
-        out = shaped(count // 2, per, columns)
-        kernel, more = (halve_with_shard_kernel, (shard,)) if bit == 1 else (halve_kernel, ())
-        keep, send = call(
-            functools.partial(kernel, bit), [out, out], keep, got, *more, name="halve",
-            scratch_shapes=[pltpu.VMEM((count, per, columns), F32)],
-        )
-        got = swap(send, "dp", 1 << bit)
-        count //= 2
-    total = call(functools.partial(sum_kernel, 1.0), out, keep, got, name="half_sum")
-    mine = call(functools.partial(sum_kernel, 1.0 / n_dp), out, total, swap(total, "dp", 1 << last), name="mean")
+    both = shaped(count, per, columns)
+    total = call(half_sum_kernel, both, keep, got, shard, name="half_sum")
+    mine = call(functools.partial(sum_kernel, 1.0 / n_dp), both, total, swap(total, "dp", 1 << last), name="mean")
     for bit in range(last - 1, 0, -1):
+        other = swap(mine, "dp", 1 << bit)
         count *= 2
-        out = shaped(count, per, columns)
-        mine = call(functools.partial(double_kernel, bit), out, mine, swap(mine, "dp", 1 << bit), name="double")
-    return mine
+        mine, shard = call(functools.partial(double_apart_kernel, bit), [shaped(count, per, ff), shaped(*shard.shape)], mine, other, name="double")
+        if bit > 1:
+            mine = add_columns(mine, shard)
+    return mine, shard
+
+
+def add_columns(mine, shard):
+    count, per, ff = mine.shape
+    columns = ff + shard.shape[0] * shard.shape[1] // (count * per)
+    return call(add_columns_kernel, shaped(count, per, columns), mine, shard, name="add_columns")
 
 
 def on_device(gu, eu, gd, ed, qu, qd):
@@ -395,37 +428,37 @@
     narrow = pltpu.VMEM((rank, rows), F32)
     product = 4 * rows * ff * 4 * rank
 
-    buffers = [
-        [pltpu.VMEM(g.shape[1:], BF16)] * 2 + [pltpu.VMEM(q.shape, F32), pltpu.VMEM((3 * rank, q.shape[1]), BF16), total]
-        for g, q, total in ((gu, qu, narrow), (gd, qd, wide))
-    ]
-    *parts, keep, send = call(
-        functools.partial(left_kernel, n_shards), [shard_rows_here] * n_shards + [replica_half] * 2, gu, eu, qu, gd, ed, qd,
-        name="left", flops=2 * product, limit=61, in_specs=[pl.BlockSpec(memory_space=pltpu.HBM)] * 6,
-        scratch_shapes=buffers[0] + buffers[1] + [stage, pltpu.SemaphoreType.DMA((2,)), pltpu.SemaphoreType.DMA((5, 2))],
-    )
+    def left(kernel, outs, g, e, q, total, count, scratch, name):
+        buffers = [pltpu.VMEM(g.shape[1:], BF16)] * 2 + [pltpu.VMEM(q.shape, F32), pltpu.VMEM((3 * rank, q.shape[1]), BF16), total]
+        return call(
+            kernel, outs, g, e, q, name=name, flops=product, limit=61, in_specs=[pl.BlockSpec(memory_space=pltpu.HBM)] * 3,
+            scratch_shapes=buffers + [pltpu.SemaphoreType.DMA((count + 1, 2))] + scratch,
+        )
+
+    keep, send = left(left_down_kernel, [replica_half] * 2, gd, ed, qd, wide, 3, [stage], "left_down")
+    parts = left(left_up_kernel, [shard_rows_here] * n_shards, gu, eu, qu, narrow, 2, [], "left_up")
+    keep = call(fetch_kernel, replica_half, keep, after=(parts[0],), name="fetch", flops=product // 4)
     got = swap(send, "dp", 1)
-    parts = from_shards(parts)
-    parts[0], keep = call(fetch_kernel, [shard_rows_here, replica_half], parts[0], keep, name="fetch", flops=product // 4)
-    shard = call(first_shards_kernel, shard_rows_here, *parts, name="shard_sum")
-    mine, shard = call(apart_kernel, [replica_half, shard_rows_here], mean_replicas(keep, got, shard), name="apart")
+    shard = call(first_shards_kernel, shard_rows_here, *from_shards(parts), name="shard_sum")
+    keep, got = scatter_replicas(keep, send, got, (shard,))
     shard = call(first_shards_kernel, shard_rows_here, shard, swap(shard, "dp", 1), name="replica_sum")
+    mine, shard = gather_replicas(keep, got, shard)
     other = swap(mine, "dp", 1)
     left_rows = from_shards([shard] * n_shards)
     left_up, gram_up, keep, send = call(
         functools.partial(right_up_kernel, n_shards), [shaped(rank, rows), shaped(rank, rank), replica_half, replica_half],
-        *left_rows, gu, eu, name="right_up", flops=product,
+        *left_rows, gu, eu, after=(other,), name="right_up", flops=product,
         scratch_shapes=[pltpu.VMEM((3 * rank, rows), BF16), wide, stage],
     )
     left_down, *parts = call(
-        right_down_kernel, [shaped(rank, ff)] + [shaped(rows_here, rows + rank * n_shards)] * n_shards, left_up, mine, other, gd, ed,
-        name="right_down", flops=product, in_specs=[ANY] + [VMEM] * 4, scratch_shapes=[pltpu.VMEM((3 * rank, ff), BF16), narrow, stage],
-    )
-    got = swap(send, "dp", 1)
+        right_down_kernel, [shaped(rank, ff)] + [shaped(rows_here, rows + rank * n_shards)] * n_shards, mine, other, gd, ed, after=(left_up,),
+        name="right_down", flops=product, scratch_shapes=[pltpu.VMEM((3 * rank, ff), BF16), narrow, stage],
+    )
+    keep, got = scatter_replicas(keep, send, swap(send, "dp", 1), (left_down,))
     shard, gram_down = call(
         functools.partial(sum_shards_kernel, n_shards), [shard_rows_here, shaped(rank, rank)], *from_shards(parts), name="shard_sum"
     )
-    mine = mean_replicas(keep, got, shard)
+    mine = add_columns(*gather_replicas(keep, got, shard))
     other = swap(mine, "dp", 1)
     inv_up, inv_down, lhs_up, lhs_down = call(
         basis_kernel,

time: 82.6 us -> 86.2 us (1.044)
  waiting for transfers between devices: 37.2 us -> 40.7 us
  Pallas kernels: 18.5 us -> 20.7 us
  starting transfers between devices: 24.2 us -> 23 us
  local copies, waits for them, and re-layouts: 1.7 us -> 0.78 us
    ppermute x23, waiting for transfers between devices: 37.2 us -> 40.7 us  [swap(): return lax.ppermute(x, axis, pairs)]
    pallas_call x21 -> x22, Pallas kernels: 18.5 us -> 20.7 us  [call(): pl.pallas_call(lambda *refs: kernel(*refs[skip:]), out_shape=out_shape, i...]
    ppermute x23, starting transfers between devices: 24.2 us -> 23 us  [swap(): return lax.ppermute(x, axis, pairs)]
    unnamed x12, local copies, waits for them, and re-layouts: 1.7 us -> 0.78 us
  transfers between devices with their start and end apart: 23 -> 23, of which waited for: 16 -> 15; matrix products, arithmetic and copies ran while one was open for 0% -> 0% of each run, Pallas kernels for 10% -> 13%
where the time goes in v13:
time: 86.2 us; the launch traced here: 86 us
  waiting for transfers between devices  40.7 us (47%)
  starting transfers between devices  23 us (27%)
  Pallas kernels  20.7 us (24%)
    ppermute x23, waiting for transfers between devices, swap(): return lax.ppermute(x, axis, pairs)  40.7 us
    ppermute x23, starting transfers between devices, swap(): return lax.ppermute(x, axis, pairs)  23 us
    pallas_call x22, Pallas kernels, call(): pl.pallas_call(lambda *refs: kernel(*refs[skip:]), out_shape=out_shape, i...  20.7 us
  transfers between devices with their start and end apart: 23, of which 15 were waited for; matrix products, arithmetic and copies ran while one was open for 0% of the time, Pallas kernels for 13%

profile of v13, /device:TPU:0, one launch (start us, length us, event | category | flops | bytes accessed | tf_op | source)
XLA Modules:
  0.0 86.0 jit_solution(3016051762634642407)
XLA Ops:
  0.6 4.0 %left_down.1 = (f32[4,8,1536]{2,1,0:T(8,128)}, f32[4,8,1536]{2,1,0:T(8,128)}) custom-call(bf16[1,1536,512]{2,1,0:T(8,128)(2,1)} %refs_0_.7, bf16[1,1536,512]{2,1,0:T(8,128)(2,1)} %refs_1_.7, f32[64,512]{1,0:T(8,128)} %bitcast.3), custom_call_target="tpu_custom_call" | custom-call | flops 805306368 | bytes 3670016 | tf_op jit(solution)/shard_map/left_down/pallas_call | solution.py:365
  4.7 3.0 %collective-permute-start.3 = (f32[4,8,1536]{2,1,0:T(8,128)}, f32[4,8,1536]{2,1,0:T(8,128)S(1)}, u32[]{:S(2)}, u32[]{:S(2)}) collective-permute-start(f32[4,8,1536]{2,1,0:T(8,128)} %get-tuple-element.47), channel_id=1, source_target_pairs={{0,4},{4,0},{8,12},{12,8},{16,20},{20,16},{24,28},{28,24},{1,5},{5... | collective-permute-start | bytes 589832 | tf_op jit(solution)/shard_map/ppermute | solution.py:374
  7.7 0.0 copy-start.5
  7.7 4.3 %left_up.1 = (f32[16,512]{1,0:T(8,128)}, f32[16,512]{1,0:T(8,128)}, f32[16,512]{1,0:T(8,128)}, f32[16,512]{1,0:T(8,128)}) custom-call(bf16[1,512,1536]{2,1,0:T(8,128)(2,1)} %refs_0_.6, bf16[1,512,1536]{2,1,0:T(8,128)(2,1)} %refs_1_.6, f32[64,1536]{1,0:T(8,128)} %bitcast.2), custom_call_target="tpu_custom_call" | custom-call | flops 805306368 | bytes 3670016 | tf_op jit(solution)/shard_map/left_up/pallas_call | solution.py:365
  12.1 0.0 copy-start
  12.1 0.1 collective-permute-start
  12.1 1.6 %collective-permute-start.1 = (f32[16,512]{1,0:T(8,128)}, f32[16,512]{1,0:T(8,128)S(1)}, u32[]{:S(2)}, u32[]{:S(2)}) collective-permute-start(f32[16,512]{1,0:T(8,128)} %get-tuple-element.44), channel_id=1, source_target_pairs={{0,2},{1,3},{2,0},{3,1},{4,6},{5,7},{6,4},{7,5},{8,10},{9,11},{10,... | collective-permute-start | bytes 98312 | tf_op jit(solution)/shard_map/ppermute | solution.py:374
  13.7 0.3 collective-permute-start.2
  14.0 0.0 copy-done.5
  14.0 0.8 copy-done.4
  14.8 0.0 collective-permute-done.refs_1_
  14.8 1.5 %collective-permute-done.1.refs_2_ = f32[16,512]{1,0:T(8,128)S(1)} collective-permute-done((f32[16,512]{1,0:T(8,128)}, f32[16,512]{1,0:T(8,128)S(1)}, u32[]{:S(2)}, u32[]{:S(2)}) %collective-permute-start.1) | collective-permute-done | bytes 32800 | tf_op jit(solution)/shard_map/ppermute | solution.py:374
  16.3 0.9 %collective-permute-done.2.refs_3_ = f32[16,512]{1,0:T(8,128)S(1)} collective-permute-done((f32[16,512]{1,0:T(8,128)}, f32[16,512]{1,0:T(8,128)S(1)}, u32[]{:S(2)}, u32[]{:S(2)}) %collective-permute-start.2) | collective-permute-done | bytes 32800 | tf_op jit(solution)/shard_map/ppermute | solution.py:374
  17.3 0.0 collective-permute-done.3.refs_2_
  17.3 1.6 %collective-permute-start.4 = (f32[2,8,1536]{2,1,0:T(8,128)S(1)}, f32[2,8,1536]{2,1,0:T(8,128)S(1)}, u32[]{:S(2)}, u32[]{:S(2)}) collective-permute-start(f32[2,8,1536]{2,1,0:T(8,128)S(1)} %get-tuple-element.49), channel_id=1, source_target_pairs={{0,8},{4,12},{8,0},{12,4},{16,24},{20,28},{24,16},{28,20},{1,9},{5... | collective-permute-start | bytes 294920 | tf_op jit(solution)/shard_map/ppermute | solution.py:374
  19.0 0.5 collective-permute-start.5
  19.5 3.4 %collective-permute-done.5.refs_1_ = f32[16,512]{1,0:T(8,128)S(1)} collective-permute-done((f32[16,512]{1,0:T(8,128)S(1)}, f32[16,512]{1,0:T(8,128)S(1)}, u32[]{:S(2)}, u32[]{:S(2)}) %collective-permute-start.5) | collective-permute-done | bytes 32800 | tf_op jit(solution)/shard_map/ppermute | solution.py:374
  22.9 0.0 collective-permute-done.4.refs_1_
  22.9 2.7 %collective-permute-start.6 = (f32[2,8,2048]{2,1,0:T(8,128)S(1)}, f32[2,8,2048]{2,1,0:T(8,128)S(1)}, u32[]{:S(2)}, u32[]{:S(2)}) collective-permute-start(f32[2,8,2048]{2,1,0:T(8,128)S(1)} %half_sum.2.refs_0_), channel_id=1, source_target_pairs={{0,16},{4,20},{8,24},{12,28},{16,0},{20,4},{24,8},{28,12},{1,17},{... | collective-permute-start | bytes 393224 | tf_op jit(solution)/shard_map/ppermute | solution.py:374
  25.6 5.6 %collective-permute-done.6.refs_1_ = f32[2,8,2048]{2,1,0:T(8,128)S(1)} collective-permute-done((f32[2,8,2048]{2,1,0:T(8,128)S(1)}, f32[2,8,2048]{2,1,0:T(8,128)S(1)}, u32[]{:S(2)}, u32[]{:S(2)}) %collective-permute-start.6) | collective-permute-done | bytes 131104 | tf_op jit(solution)/shard_map/ppermute | solution.py:374
  31.2 0.5 collective-permute-start.7
  31.7 4.5 %collective-permute-done.7.refs_1_ = f32[2,8,2048]{2,1,0:T(8,128)S(1)} collective-permute-done((f32[2,8,2048]{2,1,0:T(8,128)S(1)}, f32[2,8,2048]{2,1,0:T(8,128)S(1)}, u32[]{:S(2)}, u32[]{:S(2)}) %collective-permute-start.7) | collective-permute-done | bytes 131104 | tf_op jit(solution)/shard_map/ppermute | solution.py:374
  36.2 0.6 collective-permute-start.8
  36.8 0.0 collective-permute-start.11
  36.8 0.9 %collective-permute-start.10 = (f32[16,512]{1,0:T(8,128)S(1)}, f32[16,512]{1,0:T(8,128)S(1)}, u32[]{:S(2)}, u32[]{:S(2)}) collective-permute-start(f32[16,512]{1,0:T(8,128)S(1)} %get-tuple-element.51.refs_1_), channel_id=1, source_target_pairs={{0,2},{1,3},{2,0},{3,1},{4,6},{5,7},{6,4},{7,5},{8,10},{9,11},{10,... | collective-permute-start | bytes 98312 | tf_op jit(solution)/shard_map/ppermute | solution.py:374
  37.7 0.9 %collective-permute-start.9 = (f32[16,512]{1,0:T(8,128)S(1)}, f32[16,512]{1,0:T(8,128)S(1)}, u32[]{:S(2)}, u32[]{:S(2)}) collective-permute-start(f32[16,512]{1,0:T(8,128)S(1)} %get-tuple-element.51.refs_1_), channel_id=1, source_target_pairs={{0,1},{1,0},{2,3},{3,2},{4,5},{5,4},{6,7},{7,6},{8,9},{9,8},{10,11... | collective-permute-start | bytes 98312 | tf_op jit(solution)/shard_map/ppermute | solution.py:374
  38.7 1.5 %collective-permute-done.11.refs_4_ = f32[16,512]{1,0:T(8,128)S(1)} collective-permute-done((f32[16,512]{1,0:T(8,128)S(1)}, f32[16,512]{1,0:T(8,128)S(1)}, u32[]{:S(2)}, u32[]{:S(2)}) %collective-permute-start.11) | collective-permute-done | bytes 32800 | tf_op jit(solution)/shard_map/ppermute | solution.py:374
  40.1 1.0 %collective-permute-done.10.refs_3_ = f32[16,512]{1,0:T(8,128)S(1)} collective-permute-done((f32[16,512]{1,0:T(8,128)S(1)}, f32[16,512]{1,0:T(8,128)S(1)}, u32[]{:S(2)}, u32[]{:S(2)}) %collective-permute-start.10) | collective-permute-done | bytes 32800 | tf_op jit(solution)/shard_map/ppermute | solution.py:374
  41.1 0.0 collective-permute-done.9.refs_2_
  41.1 0.9 collective-permute-done.8.refs_0_.refs_2_
  42.0 0.0 copy-done.1
  42.0 0.0 copy-done
  42.0 1.2 %right_up.1 = (f32[64,512]{1,0:T(8,128)S(1)}, f32[64,64]{1,0:T(8,128)S(1)}, f32[4,8,1536]{2,1,0:T(8,128)S(1)}, f32[4,8,1536]{2,1,0:T(8,128)S(1)}) custom-call(f32[4,8,1536]{2,1,0:T(8,128)S(1)} %collective-permute-done.8.refs_0_.refs_2_, f32[16,512]{1,0:T(8,128)S(1)} %get-tuple-element.51.refs_1_, f32[16,512]{1,0:T(8,128)S(1)} %collective-permute-done.9.refs_2_, ...), custom_call_target="tpu_custom_call" | custom-call | flops 805306368 | bytes 3817472 | tf_op jit(solution)/shard_map/right_up/pallas_call | solution.py:365
  43.2 0.7 collective-permute-start.15
  43.9 0.0 copy-done.2
  43.9 0.0 copy-done.3
  43.9 1.2 %right_down.1 = (f32[64,1536]{1,0:T(8,128)S(1)}, f32[16,768]{1,0:T(8,128)S(1)}, f32[16,768]{1,0:T(8,128)S(1)}, f32[16,768]{1,0:T(8,128)S(1)}, f32[16,768]{1,0:T(8,128)S(1)}) custom-call(f32[64,512]{1,0:T(8,128)S(1)} %get-tuple-element.52.refs_0_, f32[4,8,1536]{2,1,0:T(8,128)S(1)} %get-tuple-element.50.refs_1_, ...), custom_call_target="tpu_custom_call" | custom-call | flops 805306368 | bytes 4128768 | tf_op jit(solution)/shard_map/right_down/pallas_call | solution.py:365
  45.1 4.2 %collective-permute-done.15.refs_2_ = f32[4,8,1536]{2,1,0:T(8,128)S(1)} collective-permute-done((f32[4,8,1536]{2,1,0:T(8,128)S(1)}, f32[4,8,1536]{2,1,0:T(8,128)S(1)}, u32[]{:S(2)}, u32[]{:S(2)}) %collective-permute-start.15) | collective-permute-done | bytes 196640 | tf_op jit(solution)/shard_map/ppermute | solution.py:374
  49.3 0.7 collective-permute-start.16
  50.0 0.0 collective-permute-start.12
  50.0 0.9 %collective-permute-start.13 = (f32[16,768]{1,0:T(8,128)S(1)}, f32[16,768]{1,0:T(8,128)S(1)}, u32[]{:S(2)}, u32[]{:S(2)}) collective-permute-start(f32[16,768]{1,0:T(8,128)S(1)} %get-tuple-element.57), channel_id=1, source_target_pairs={{0,2},{1,3},{2,0},{3,1},{4,6},{5,7},{6,4},{7,5},{8,10},{9,11},{10,... | collective-permute-start | bytes 147464 | tf_op jit(solution)/shard_map/ppermute | solution.py:374
  51.0 0.9 %collective-permute-start.14 = (f32[16,768]{1,0:T(8,128)S(1)}, f32[16,768]{1,0:T(8,128)S(1)}, u32[]{:S(2)}, u32[]{:S(2)}) collective-permute-start(f32[16,768]{1,0:T(8,128)S(1)} %get-tuple-element.58), channel_id=1, source_target_pairs={{0,3},{1,2},{2,1},{3,0},{4,7},{5,6},{6,5},{7,4},{8,11},{9,10},{10,... | collective-permute-start | bytes 147464 | tf_op jit(solution)/shard_map/ppermute | solution.py:374
  51.9 0.0 collective-permute-done.12.refs_1_
  51.9 2.5 %collective-permute-done.13.refs_2_ = f32[16,768]{1,0:T(8,128)S(1)} collective-permute-done((f32[16,768]{1,0:T(8,128)S(1)}, f32[16,768]{1,0:T(8,128)S(1)}, u32[]{:S(2)}, u32[]{:S(2)}) %collective-permute-start.13) | collective-permute-done | bytes 49184 | tf_op jit(solution)/shard_map/ppermute | solution.py:374
  54.4 0.6 collective-permute-done.14.refs_3_
  55.0 0.1 shard_sum.3
  55.1 0.0 collective-permute-done.16.refs_1_
  55.1 3.4 %collective-permute-start.17 = (f32[2,8,2048]{2,1,0:T(8,128)S(1)}, f32[2,8,2048]{2,1,0:T(8,128)S(1)}, u32[]{:S(2)}, u32[]{:S(2)}) collective-permute-start(f32[2,8,2048]{2,1,0:T(8,128)S(1)} %half_sum.3.refs_0_), channel_id=1, source_target_pairs={{0,16},{4,20},{8,24},{12,28},{16,0},{20,4},{24,8},{28,12},{1,17},{... | collective-permute-start | bytes 393224 | tf_op jit(solution)/shard_map/ppermute | solution.py:374
  58.6 6.6 %collective-permute-done.17.refs_1_ = f32[2,8,2048]{2,1,0:T(8,128)S(1)} collective-permute-done((f32[2,8,2048]{2,1,0:T(8,128)S(1)}, f32[2,8,2048]{2,1,0:T(8,128)S(1)}, u32[]{:S(2)}, u32[]{:S(2)}) %collective-permute-start.17) | collective-permute-done | bytes 131104 | tf_op jit(solution)/shard_map/ppermute | solution.py:374
  65.2 0.1 collective-permute-start.18
  65.2 5.3 %collective-permute-done.18.refs_1_ = f32[2,8,2048]{2,1,0:T(8,128)S(1)} collective-permute-done((f32[2,8,2048]{2,1,0:T(8,128)S(1)}, f32[2,8,2048]{2,1,0:T(8,128)S(1)}, u32[]{:S(2)}, u32[]{:S(2)}) %collective-permute-start.18) | collective-permute-done | bytes 131104 | tf_op jit(solution)/shard_map/ppermute | solution.py:374
  70.7 1.5 %collective-permute-start.19 = (f32[4,8,1792]{2,1,0:T(8,128)S(1)}, f32[4,8,1792]{2,1,0:T(8,128)S(1)}, u32[]{:S(2)}, u32[]{:S(2)}) collective-permute-start(f32[4,8,1792]{2,1,0:T(8,128)S(1)} %add_columns.1.refs_8_.refs_0_), channel_id=1, source_target_pairs={{0,4},{4,0},{8,12},{12,8},{16,20},{20,16},{24,28},{28,24},{1,5},{5... | collective-permute-start | bytes 688136 | tf_op jit(solution)/shard_map/ppermute | solution.py:374
  72.2 3.2 %basis.1 = (f32[64,64]{1,0:T(8,128)S(1)}, f32[64,64]{1,0:T(8,128)S(1)}, bf16[512,256]{1,0:T(8,128)(2,1)S(1)}, bf16[1536,256]{1,0:T(8,128)(2,1)S(1)}) custom-call(f32[64,512]{1,0:T(8,128)S(1)} %get-tuple-element.52.refs_0_, f32[64,1536]{1,0:T(8,128)S(1)} %get-tuple-element.53.refs_0_.refs_1_, f32[64,64]{1,0:T(8,128)S(1)} %get-tuple-element.54.refs_2_, ...), custom_call_target="tpu_custom_call" | custom-call | bytes 8159232 | tf_op jit(solution)/shard_map/basis/pallas_call | solution.py:365
  75.4 2.0 %collective-permute-done.19.refs_1_ = f32[4,8,1792]{2,1,0:T(8,128)S(1)} collective-permute-done((f32[4,8,1792]{2,1,0:T(8,128)S(1)}, f32[4,8,1792]{2,1,0:T(8,128)S(1)}, u32[]{:S(2)}, u32[]{:S(2)}) %collective-permute-start.19) | collective-permute-done | bytes 229408 | tf_op jit(solution)/shard_map/ppermute | solution.py:374
  77.3 0.7 factor_up.1
  78.0 0.1 collective-permute-start.22
  78.1 0.9 %collective-permute-start.21 = (f32[16,640]{1,0:T(8,128)S(1)}, f32[16,640]{1,0:T(8,128)S(1)}, u32[]{:S(2)}, u32[]{:S(2)}) collective-permute-start(f32[16,640]{1,0:T(8,128)S(1)} %get-tuple-element.72.refs_0_), channel_id=1, source_target_pairs={{0,2},{1,3},{2,0},{3,1},{4,6},{5,7},{6,4},{7,5},{8,10},{9,11},{10,... | collective-permute-start | bytes 122888 | tf_op jit(solution)/shard_map/ppermute | solution.py:374
  79.0 0.9 %collective-permute-start.20 = (f32[16,640]{1,0:T(8,128)S(1)}, f32[16,640]{1,0:T(8,128)S(1)}, u32[]{:S(2)}, u32[]{:S(2)}) collective-permute-start(f32[16,640]{1,0:T(8,128)S(1)} %get-tuple-element.72.refs_0_), channel_id=1, source_target_pairs={{0,1},{1,0},{2,3},{3,2},{4,5},{5,4},{6,7},{7,6},{8,9},{9,8},{10,11... | collective-permute-start | bytes 122888 | tf_op jit(solution)/shard_map/ppermute | solution.py:374
  79.9 2.3 %error_up.1 = (bf16[1,512,1536]{2,1,0:T(8,128)(2,1)}, f32[8,128]{1,0:T(8,128)S(1)}) custom-call(bf16[1,512,1536]{2,1,0:T(8,128)(2,1)S(1)} %copy-done, bf16[1,512,1536]{2,1,0:T(8,128)(2,1)S(1)} %copy-done.1, bf16[512,256]{1,0:T(8,128)(2,1)S(1)} %get-tuple-element.67.refs_2_, bf16[256,1536]{1,0:T(8,128)(2,1)S(1)} %get-tuple-element.69.refs_3_), custom_call_target="tpu_custom_call" | custom-call | flops 402653184 | bytes 5771264 | tf_op jit(solution)/shard_map/error_up/pallas_call | solution.py:365
  82.3 0.0 collective-permute-done.22.refs_3_
  82.3 0.3 collective-permute-done.21.refs_2_
  82.5 0.0 collective-permute-done.20.refs_1_
  82.5 0.4 factor_down.1
  83.0 3.0 %last.1 = (bf16[1,1536,512]{2,1,0:T(8,128)(2,1)}, bf16[512,1536]{1,0:T(8,128)(2,1)}, bf16[1536,512]{1,0:T(8,128)(2,1)}) custom-call(bf16[1,1536,512]{2,1,0:T(8,128)(2,1)S(1)} %copy-done.2, bf16[1,1536,512]{2,1,0:T(8,128)(2,1)S(1)} %copy-done.3, bf16[512,256]{1,0:T(8,128)(2,1)S(1)} %get-tuple-element.67.refs_2_, ...), custom_call_target="tpu_custom_call" | custom-call | flops 805306368 | bytes 9965568 | tf_op jit(solution)/shard_map/last/pallas_call | solution.py:365
  (16 shorter events, 0.2 us)
Async XLA Ops:
  4.7 12.6 %collective-permute-start.3 = (f32[4,8,1536]{2,1,0:T(8,128)}, f32[4,8,1536]{2,1,0:T(8,128)S(1)}, u32[]{:S(2)}, u32[]{:S(2)}) collective-permute-start(f32[4,8,1536]{2,1,0:T(8,128)} %get-tuple-element.47), channel_id=1, source_target_pairs={{0,4},{4,0},{8,12},{12,8},{16,20},{20,16},{24,28},{28,24},{1,5},{5... | collective-permute-start | bytes 589832 | tf_op jit(solution)/shard_map/ppermute | solution.py:374
  7.7 6.3 %copy-start.5 = (f32[4,8,1536]{2,1,0:T(8,128)S(1)}, f32[4,8,1536]{2,1,0:T(8,128)}, u32[]{:S(2)}) copy-start(f32[4,8,1536]{2,1,0:T(8,128)} %get-tuple-element.46.refs_1_) | copy-start | bytes 589828
  7.7 34.2 %copy-start.1 = (bf16[1,512,1536]{2,1,0:T(8,128)(2,1)S(1)}, bf16[1,512,1536]{2,1,0:T(8,128)(2,1)}, u32[]{:S(2)}) copy-start(bf16[1,512,1536]{2,1,0:T(8,128)(2,1)} %refs_1_.6) | copy-start | bytes 4718596
  12.1 29.9 %copy-start = (bf16[1,512,1536]{2,1,0:T(8,128)(2,1)S(1)}, bf16[1,512,1536]{2,1,0:T(8,128)(2,1)}, u32[]{:S(2)}) copy-start(bf16[1,512,1536]{2,1,0:T(8,128)(2,1)} %refs_0_.6) | copy-start | bytes 4718596
  12.1 2.7 %collective-permute-start = (f32[16,512]{1,0:T(8,128)}, f32[16,512]{1,0:T(8,128)S(1)}, u32[]{:S(2)}, u32[]{:S(2)}) collective-permute-start(f32[16,512]{1,0:T(8,128)} %get-tuple-element.43), channel_id=1, source_target_pairs={{0,1},{1,0},{2,3},{3,2},{4,5},{5,4},{6,7},{7,6},{8,9},{9,8},{10,11... | collective-permute-start | bytes 98312 | tf_op jit(solution)/shard_map/ppermute | solution.py:374
  12.1 4.2 %collective-permute-start.1 = (f32[16,512]{1,0:T(8,128)}, f32[16,512]{1,0:T(8,128)S(1)}, u32[]{:S(2)}, u32[]{:S(2)}) collective-permute-start(f32[16,512]{1,0:T(8,128)} %get-tuple-element.44), channel_id=1, source_target_pairs={{0,2},{1,3},{2,0},{3,1},{4,6},{5,7},{6,4},{7,5},{8,10},{9,11},{10,... | collective-permute-start | bytes 98312 | tf_op jit(solution)/shard_map/ppermute | solution.py:374
  13.7 3.6 %collective-permute-start.2 = (f32[16,512]{1,0:T(8,128)}, f32[16,512]{1,0:T(8,128)S(1)}, u32[]{:S(2)}, u32[]{:S(2)}) collective-permute-start(f32[16,512]{1,0:T(8,128)} %get-tuple-element.45), channel_id=1, source_target_pairs={{0,3},{1,2},{2,1},{3,0},{4,7},{5,6},{6,5},{7,4},{8,11},{9,10},{10,... | collective-permute-start | bytes 98312 | tf_op jit(solution)/shard_map/ppermute | solution.py:374
  14.0 0.8 copy-start.4
  17.3 5.6 %collective-permute-start.4 = (f32[2,8,1536]{2,1,0:T(8,128)S(1)}, f32[2,8,1536]{2,1,0:T(8,128)S(1)}, u32[]{:S(2)}, u32[]{:S(2)}) collective-permute-start(f32[2,8,1536]{2,1,0:T(8,128)S(1)} %get-tuple-element.49), channel_id=1, source_target_pairs={{0,8},{4,12},{8,0},{12,4},{16,24},{20,28},{24,16},{28,20},{1,9},{5... | collective-permute-start | bytes 294920 | tf_op jit(solution)/shard_map/ppermute | solution.py:374
  19.0 3.9 %collective-permute-start.5 = (f32[16,512]{1,0:T(8,128)S(1)}, f32[16,512]{1,0:T(8,128)S(1)}, u32[]{:S(2)}, u32[]{:S(2)}) collective-permute-start(f32[16,512]{1,0:T(8,128)S(1)} %shard_sum.2.refs_0_), channel_id=1, source_target_pairs={{0,4},{4,0},{8,12},{12,8},{16,20},{20,16},{24,28},{28,24},{1,5},{5... | collective-permute-start | bytes 98312 | tf_op jit(solution)/shard_map/ppermute | solution.py:374
  22.9 8.2 %collective-permute-start.6 = (f32[2,8,2048]{2,1,0:T(8,128)S(1)}, f32[2,8,2048]{2,1,0:T(8,128)S(1)}, u32[]{:S(2)}, u32[]{:S(2)}) collective-permute-start(f32[2,8,2048]{2,1,0:T(8,128)S(1)} %half_sum.2.refs_0_), channel_id=1, source_target_pairs={{0,16},{4,20},{8,24},{12,28},{16,0},{20,4},{24,8},{28,12},{1,17},{... | collective-permute-start | bytes 393224 | tf_op jit(solution)/shard_map/ppermute | solution.py:374
  31.2 5.0 %collective-permute-start.7 = (f32[2,8,2048]{2,1,0:T(8,128)S(1)}, f32[2,8,2048]{2,1,0:T(8,128)S(1)}, u32[]{:S(2)}, u32[]{:S(2)}) collective-permute-start(f32[2,8,2048]{2,1,0:T(8,128)S(1)} %mean.2.refs_0_), channel_id=1, source_target_pairs={{0,8},{4,12},{8,0},{12,4},{16,24},{20,28},{24,16},{28,20},{1,9},{5... | collective-permute-start | bytes 393224 | tf_op jit(solution)/shard_map/ppermute | solution.py:374
  36.2 5.7 %collective-permute-start.8 = (f32[4,8,1536]{2,1,0:T(8,128)S(1)}, f32[4,8,1536]{2,1,0:T(8,128)S(1)}, u32[]{:S(2)}, u32[]{:S(2)}) collective-permute-start(f32[4,8,1536]{2,1,0:T(8,128)S(1)} %get-tuple-element.50.refs_1_), channel_id=1, source_target_pairs={{0,4},{4,0},{8,12},{12,8},{16,20},{20,16},{24,28},{28,24},{1,5},{5... | collective-permute-start | bytes 589832 | tf_op jit(solution)/shard_map/ppermute | solution.py:374
  36.8 7.1 %copy-start.2 = (bf16[1,1536,512]{2,1,0:T(8,128)(2,1)S(1)}, bf16[1,1536,512]{2,1,0:T(8,128)(2,1)}, u32[]{:S(2)}) copy-start(bf16[1,1536,512]{2,1,0:T(8,128)(2,1)} %refs_0_.7) | copy-start | bytes 4718596
  36.8 7.1 %copy-start.3 = (bf16[1,1536,512]{2,1,0:T(8,128)(2,1)S(1)}, bf16[1,1536,512]{2,1,0:T(8,128)(2,1)}, u32[]{:S(2)}) copy-start(bf16[1,1536,512]{2,1,0:T(8,128)(2,1)} %refs_1_.7) | copy-start | bytes 4718596
  36.8 3.3 %collective-permute-start.11 = (f32[16,512]{1,0:T(8,128)S(1)}, f32[16,512]{1,0:T(8,128)S(1)}, u32[]{:S(2)}, u32[]{:S(2)}) collective-permute-start(f32[16,512]{1,0:T(8,128)S(1)} %get-tuple-element.51.refs_1_), channel_id=1, source_target_pairs={{0,3},{1,2},{2,1},{3,0},{4,7},{5,6},{6,5},{7,4},{8,11},{9,10},{10,... | collective-permute-start | bytes 98312 | tf_op jit(solution)/shard_map/ppermute | solution.py:374
  36.8 4.3 %collective-permute-start.10 = (f32[16,512]{1,0:T(8,128)S(1)}, f32[16,512]{1,0:T(8,128)S(1)}, u32[]{:S(2)}, u32[]{:S(2)}) collective-permute-start(f32[16,512]{1,0:T(8,128)S(1)} %get-tuple-element.51.refs_1_), channel_id=1, source_target_pairs={{0,2},{1,3},{2,0},{3,1},{4,6},{5,7},{6,4},{7,5},{8,10},{9,11},{10,... | collective-permute-start | bytes 98312 | tf_op jit(solution)/shard_map/ppermute | solution.py:374
  37.7 3.4 %collective-permute-start.9 = (f32[16,512]{1,0:T(8,128)S(1)}, f32[16,512]{1,0:T(8,128)S(1)}, u32[]{:S(2)}, u32[]{:S(2)}) collective-permute-start(f32[16,512]{1,0:T(8,128)S(1)} %get-tuple-element.51.refs_1_), channel_id=1, source_target_pairs={{0,1},{1,0},{2,3},{3,2},{4,5},{5,4},{6,7},{7,6},{8,9},{9,8},{10,11... | collective-permute-start | bytes 98312 | tf_op jit(solution)/shard_map/ppermute | solution.py:374
  43.2 6.1 %collective-permute-start.15 = (f32[4,8,1536]{2,1,0:T(8,128)S(1)}, f32[4,8,1536]{2,1,0:T(8,128)S(1)}, u32[]{:S(2)}, u32[]{:S(2)}) collective-permute-start(f32[4,8,1536]{2,1,0:T(8,128)S(1)} %get-tuple-element.61), channel_id=1, source_target_pairs={{0,4},{4,0},{8,12},{12,8},{16,20},{20,16},{24,28},{28,24},{1,5},{5... | collective-permute-start | bytes 589832 | tf_op jit(solution)/shard_map/ppermute | solution.py:374
  49.3 5.8 %collective-permute-start.16 = (f32[2,8,1536]{2,1,0:T(8,128)S(1)}, f32[2,8,1536]{2,1,0:T(8,128)S(1)}, u32[]{:S(2)}, u32[]{:S(2)}) collective-permute-start(f32[2,8,1536]{2,1,0:T(8,128)S(1)} %get-tuple-element.63), channel_id=1, source_target_pairs={{0,8},{4,12},{8,0},{12,4},{16,24},{20,28},{24,16},{28,20},{1,9},{5... | collective-permute-start | bytes 294920 | tf_op jit(solution)/shard_map/ppermute | solution.py:374
  50.0 1.9 %collective-permute-start.12 = (f32[16,768]{1,0:T(8,128)S(1)}, f32[16,768]{1,0:T(8,128)S(1)}, u32[]{:S(2)}, u32[]{:S(2)}) collective-permute-start(f32[16,768]{1,0:T(8,128)S(1)} %get-tuple-element.56), channel_id=1, source_target_pairs={{0,1},{1,0},{2,3},{3,2},{4,5},{5,4},{6,7},{7,6},{8,9},{9,8},{10,11... | collective-permute-start | bytes 147464 | tf_op jit(solution)/shard_map/ppermute | solution.py:374
  50.0 4.4 %collective-permute-start.13 = (f32[16,768]{1,0:T(8,128)S(1)}, f32[16,768]{1,0:T(8,128)S(1)}, u32[]{:S(2)}, u32[]{:S(2)}) collective-permute-start(f32[16,768]{1,0:T(8,128)S(1)} %get-tuple-element.57), channel_id=1, source_target_pairs={{0,2},{1,3},{2,0},{3,1},{4,6},{5,7},{6,4},{7,5},{8,10},{9,11},{10,... | collective-permute-start | bytes 147464 | tf_op jit(solution)/shard_map/ppermute | solution.py:374
  51.0 4.0 %collective-permute-start.14 = (f32[16,768]{1,0:T(8,128)S(1)}, f32[16,768]{1,0:T(8,128)S(1)}, u32[]{:S(2)}, u32[]{:S(2)}) collective-permute-start(f32[16,768]{1,0:T(8,128)S(1)} %get-tuple-element.58), channel_id=1, source_target_pairs={{0,3},{1,2},{2,1},{3,0},{4,7},{5,6},{6,5},{7,4},{8,11},{9,10},{10,... | collective-permute-start | bytes 147464 | tf_op jit(solution)/shard_map/ppermute | solution.py:374
  55.1 10.0 %collective-permute-start.17 = (f32[2,8,2048]{2,1,0:T(8,128)S(1)}, f32[2,8,2048]{2,1,0:T(8,128)S(1)}, u32[]{:S(2)}, u32[]{:S(2)}) collective-permute-start(f32[2,8,2048]{2,1,0:T(8,128)S(1)} %half_sum.3.refs_0_), channel_id=1, source_target_pairs={{0,16},{4,20},{8,24},{12,28},{16,0},{20,4},{24,8},{28,12},{1,17},{... | collective-permute-start | bytes 393224 | tf_op jit(solution)/shard_map/ppermute | solution.py:374
  65.2 5.4 %collective-permute-start.18 = (f32[2,8,2048]{2,1,0:T(8,128)S(1)}, f32[2,8,2048]{2,1,0:T(8,128)S(1)}, u32[]{:S(2)}, u32[]{:S(2)}) collective-permute-start(f32[2,8,2048]{2,1,0:T(8,128)S(1)} %mean.3.refs_0_), channel_id=1, source_target_pairs={{0,8},{4,12},{8,0},{12,4},{16,24},{20,28},{24,16},{28,20},{1,9},{5... | collective-permute-start | bytes 393224 | tf_op jit(solution)/shard_map/ppermute | solution.py:374
  70.7 6.7 %collective-permute-start.19 = (f32[4,8,1792]{2,1,0:T(8,128)S(1)}, f32[4,8,1792]{2,1,0:T(8,128)S(1)}, u32[]{:S(2)}, u32[]{:S(2)}) collective-permute-start(f32[4,8,1792]{2,1,0:T(8,128)S(1)} %add_columns.1.refs_8_.refs_0_), channel_id=1, source_target_pairs={{0,4},{4,0},{8,12},{12,8},{16,20},{20,16},{24,28},{28,24},{1,5},{5... | collective-permute-start | bytes 688136 | tf_op jit(solution)/shard_map/ppermute | solution.py:374
  78.0 4.3 %collective-permute-start.22 = (f32[16,640]{1,0:T(8,128)S(1)}, f32[16,640]{1,0:T(8,128)S(1)}, u32[]{:S(2)}, u32[]{:S(2)}) collective-permute-start(f32[16,640]{1,0:T(8,128)S(1)} %get-tuple-element.72.refs_0_), channel_id=1, source_target_pairs={{0,3},{1,2},{2,1},{3,0},{4,7},{5,6},{6,5},{7,4},{8,11},{9,10},{10,... | collective-permute-start | bytes 122888 | tf_op jit(solution)/shard_map/ppermute | solution.py:374
  78.1 4.4 %collective-permute-start.21 = (f32[16,640]{1,0:T(8,128)S(1)}, f32[16,640]{1,0:T(8,128)S(1)}, u32[]{:S(2)}, u32[]{:S(2)}) collective-permute-start(f32[16,640]{1,0:T(8,128)S(1)} %get-tuple-element.72.refs_0_), channel_id=1, source_target_pairs={{0,2},{1,3},{2,0},{3,1},{4,6},{5,7},{6,4},{7,5},{8,10},{9,11},{10,... | collective-permute-start | bytes 122888 | tf_op jit(solution)/shard_map/ppermute | solution.py:374
  79.0 3.5 %collective-permute-start.20 = (f32[16,640]{1,0:T(8,128)S(1)}, f32[16,640]{1,0:T(8,128)S(1)}, u32[]{:S(2)}, u32[]{:S(2)}) collective-permute-start(f32[16,640]{1,0:T(8,128)S(1)} %get-tuple-element.72.refs_0_), channel_id=1, source_target_pairs={{0,1},{1,0},{2,3},{3,2},{4,5},{5,4},{6,7},{7,6},{8,9},{9,8},{10,11... | collective-permute-start | bytes 122888 | tf_op jit(solution)/shard_map/ppermute | solution.py:374

commit v14 on v11

--- a/solution.py
+++ b/solution.py
@@ -139,6 +139,63 @@
     refs[-1][...] = tree_sum(term[...] for term in refs[:-1])
 
 
+def own_and_other(j, bit):
+    mine = lax.bitwise_and(lax.shift_right_logical(lax.axis_index("dp"), bit), 1)
+    return 2 * j + mine, 2 * j + 1 - mine
+
+
+def split_chunks(bit, chunks, keep, send):
+    for j in range(keep.shape[0]):
+        mine, other = own_and_other(j, bit)
+        keep[j] = chunks[mine]
+        send[j] = chunks[other]
+
+
+def halve_kernel(bit, keep, got, keep_out, send_out, chunks):
+    chunks[...] = keep[...] + got[...]
+    split_chunks(bit, chunks, keep_out, send_out)
+
+
+def sum_kernel(scale, mine, other, out):
+    out[...] = (mine[...] + other[...]) * scale
+
+
+def double_kernel(bit, mine, other, out):
+    for j in range(mine.shape[0]):
+        here, there = own_and_other(j, bit)
+        out[here] = mine[j]
+        out[there] = other[j]
+
+
+def half_sum_kernel(keep, got, shard, out):
+    count, per, ff = keep.shape
+    block = shard.shape[1] // count
+    for c in range(count):
+        out[c, :, :ff] = keep[c] + got[c]
+        out[c, :, ff:] = fold(shard[:, c * block : (c + 1) * block], per)
+
+
+def join_shard(chunks, ff, rows):
+    return jnp.concatenate([unfold(chunks[c, :, ff:], rows) for c in range(chunks.shape[0])], axis=1)
+
+
+def double_apart_kernel(bit, mine, other, out, shard):
+    ff = out.shape[2]
+    for j in range(mine.shape[0]):
+        here, there = own_and_other(j, bit)
+        out[here] = mine[j, :, :ff]
+        out[there] = other[j, :, :ff]
+    shard[...] = join_shard(mine, ff, shard.shape[0]) + join_shard(other, ff, shard.shape[0])
+
+
+def add_columns_kernel(chunks, shard, out):
+    count, per, ff = chunks.shape
+    block = shard.shape[1] // count
+    for c in range(count):
+        out[c, :, :ff] = chunks[c]
+        out[c, :, ff:] = fold(shard[:, c * block : (c + 1) * block], per)
+
+
 def split_z_kernel(keep, got, shard, *refs):
     *outs, stage = refs
     _, z = place("dp")
@@ -161,14 +218,6 @@
         refs[-1][lax.bitwise_xor(z, j)] = ref[...]
 
 
-def stack_apart_kernel(*refs):
-    *pieces, out, shard, stack = refs
-    stack_kernel(*pieces, stack)
-    half, _, ff = out.shape
-    out[...] = stack[:, :, :ff]
-    shard[...] = jnp.concatenate([unfold(stack[c, :, ff:], shard.shape[0]) for c in range(half)], axis=1)
-
-
 def shard_rows(mine, other, ff, rows):
     half = mine.shape[0]
     return jnp.concatenate([unfold(mine[c, :, ff:] + other[c, :, ff:], rows) for c in range(half)], axis=1)
@@ -185,7 +234,7 @@
     return t[:rank] + (t[rank : 2 * rank] + t[2 * rank :])
 
 
-def right_down_kernel(_, mine, other, g, e, left, *refs):
+def right_down_kernel(mine, other, g, e, left, *refs):
     *outs, pieces, total, stage = refs
     join_replicas(mine, other, stage, left)
     split_rows(left, pieces)
@@ -292,21 +341,21 @@
     return pl.ds(pl.multiple_of(pl.program_id(0) * block, block), block)
 
 
-def error_up_kernel(g, e, lhs, rhs, error, made):
-    made[...] = jnp.zeros_like(made)
+def error_up_kernel(g, e, lhs, rhs, error, kept):
     part = rows_of(error.shape[1])
     rebuilt = dot(lhs[part, :], rhs[...])
+    kept[part, :] = rebuilt
     error[0] = (g[0, part, :].astype(F32) + e[0, part, :].astype(F32) - rebuilt).astype(BF16)
 
 
-def last_kernel(g, e, lhs_up, rhs_up, lhs_down, rhs_down, clip, error, update_up, update_down):
+def last_kernel(g, e, rebuilt_up, lhs_down, rhs_down, clip, error, update_up, update_down):
     factor = clip[:1, :1]
     part = rows_of(update_down.shape[0])
     rebuilt = dot(lhs_down[part, :], rhs_down[...])
     update_down[...] = (factor * rebuilt).astype(BF16)
     error[0] = (g[0, part, :].astype(F32) + e[0, part, :].astype(F32) - rebuilt).astype(BF16)
     part = rows_of(update_up.shape[0])
-    update_up[...] = (factor * dot(lhs_up[part, :], rhs_up[...])).astype(BF16)
+    update_up[...] = (factor * rebuilt_up[part, :]).astype(BF16)
 
 
 def shaped(*dims, dtype=F32):
@@ -329,12 +378,15 @@
 ANY = pl.BlockSpec(memory_space=pl.ANY)
 
 
-def call(kernel, out_shape, *args, flops=0, limit=12, name=None, **more):
+def call(kernel, out_shape, *args, after=(), in_specs=None, flops=0, limit=12, name=None, **more):
     arrays = list(args) + jax.tree.leaves(out_shape)
     size = sum(a.size * a.dtype.itemsize for a in arrays)
-    cost = pl.CostEstimate(flops=flops, bytes_accessed=size, transcendentals=0)
-    params = pltpu.CompilerParams(vmem_limit_bytes=limit * MIB)
-    return pl.pallas_call(kernel, out_shape=out_shape, compiler_params=params, cost_estimate=cost, name=name, **more)(*args)
+    skip = len(after)
+    return pl.pallas_call(
+        lambda *refs: kernel(*refs[skip:]), out_shape=out_shape, in_specs=[ANY] * skip + (in_specs or [VMEM] * len(args)),
+        compiler_params=pltpu.CompilerParams(vmem_limit_bytes=limit * MIB),
+        cost_estimate=pl.CostEstimate(flops=flops, bytes_accessed=size, transcendentals=0), name=name, **more,
+    )(*after, *args)
 
 
 def swap(x, axis, distance):
@@ -344,6 +396,37 @@
 
 def from_shards(parts):
     return [parts[0]] + [swap(parts[j], "tensor", j) for j in range(1, len(parts))]
+
+
+def scatter_replicas(keep, send, got, after):
+    n_dp = lax.axis_size("dp")
+    for bit in range(n_dp.bit_length() - 2):
+        got = swap(send, "dp", 1 << bit) if bit else got
+        if bit == n_dp.bit_length() - 3:
+            return keep, got
+        count, per, ff = keep.shape
+        out = shaped(count // 2, per, ff)
+        keep, send = call(
+            functools.partial(halve_kernel, bit + 1), [out, out], keep, got, after=after if bit == 0 else (), name="halve",
+            scratch_shapes=[pltpu.VMEM(keep.shape, F32)],
+        )
+
+
+def gather_replicas(keep, got, shard):
+    n_dp = lax.axis_size("dp")
+    last = n_dp.bit_length() - 2
+    count, per, ff = keep.shape
+    columns = ff + shard.shape[0] * shard.shape[1] // (count * per)
+    both = shaped(count, per, columns)
+    total = call(half_sum_kernel, both, keep, got, shard, name="half_sum")
+    mine = call(functools.partial(sum_kernel, 1.0 / n_dp), both, total, swap(total, "dp", 1 << last), name="mean")
+    for bit in range(last - 1, 0, -1):
+        other = swap(mine, "dp", 1 << bit)
+        count *= 2
+        mine, shard = call(functools.partial(double_apart_kernel, bit), [shaped(count, per, ff), shaped(*shard.shape)], mine, other, name="double")
+        if bit > 1:
+            mine = call(add_columns_kernel, shaped(count, per, ff + (columns - ff) // (count // keep.shape[0])), mine, shard, name="add_columns")
+    return mine, shard
 
 
 def from_z(parts):
@@ -388,22 +471,19 @@
     parts = from_shards(parts)
     parts[0], keep = call(fetch_kernel, [shard_rows_here, replica_half], parts[0], keep, name="fetch", flops=product // 4)
     shard = call(first_shards_kernel, shard_rows_here, *parts, name="shard_sum")
-    pieces = mean_replicas(keep, got, shard)
-    mine, shard = call(
-        stack_apart_kernel, [replica_half, shard_rows_here], *pieces, name="stack_z",
-        scratch_shapes=[pltpu.VMEM((half, *pieces[0].shape), F32)],
-    )
+    keep, got = scatter_replicas(keep, send, got, (shard,))
     shard = call(first_shards_kernel, shard_rows_here, shard, swap(shard, "dp", 1), name="replica_sum")
+    mine, shard = gather_replicas(keep, got, shard)
     other = swap(mine, "dp", 1)
     left_rows = from_shards([shard] * n_shards)
     left_up, gram_up, keep, send = call(
         functools.partial(right_up_kernel, n_shards), [shaped(rank, rows), shaped(rank, rank), replica_half, replica_half],
-        *left_rows, gu, eu, name="right_up", flops=product,
+        *left_rows, gu, eu, after=(other,), name="right_up", flops=product,
         scratch_shapes=[pltpu.VMEM((3 * rank, rows), BF16), wide, stage],
     )
     left_down, *parts = call(
-        right_down_kernel, [shaped(rank, ff)] + [shaped(rows_here, rows + rank * n_shards)] * n_shards, left_up, mine, other, gd, ed,
-        name="right_down", flops=product, in_specs=[ANY] + [VMEM] * 4, scratch_shapes=[pltpu.VMEM((3 * rank, ff), BF16), narrow, stage],
+        right_down_kernel, [shaped(rank, ff)] + [shaped(rows_here, rows + rank * n_shards)] * n_shards, mine, other, gd, ed, after=(left_up,),
+        name="right_down", flops=product, scratch_shapes=[pltpu.VMEM((3 * rank, ff), BF16), narrow, stage],
     )
     got = swap(send, "dp", 1)
     shard, gram_down = call(
@@ -422,19 +502,19 @@
         name="factor_up", scratch_shapes=[wide, stage],
     )
     right_rows = from_shards([shard] * n_shards)
-    new_error_up, made = call(
-        error_up_kernel, [shaped(1, rows, ff, dtype=BF16), shaped(8, 128)], gu, eu, lhs_up, rhs_up, name="error_up", flops=product // 2,
-        grid=(STEPS,), in_specs=[VMEM] * 4, out_specs=[replica_blocks(rows, ff), whole((8, 128))],
+    new_error_up, rebuilt_up = call(
+        error_up_kernel, [shaped(1, rows, ff, dtype=BF16), shaped(rows, ff)], gu, eu, lhs_up, rhs_up, name="error_up", flops=product // 2,
+        grid=(STEPS,), in_specs=[VMEM] * 4, out_specs=[replica_blocks(rows, ff), VMEM],
     )
     limit = CLIP_RMS * (2.0 * rows * ff * n_shards) ** 0.5
     rhs_down, clip = call(
         functools.partial(factor_down_kernel, limit, n_shards), [shaped(4 * rank, rows, dtype=BF16), shaped(8, 128)],
-        *right_rows, inv_down, made, name="factor_down", in_specs=[VMEM] * (n_shards + 1) + [ANY], scratch_shapes=[narrow],
+        *right_rows, inv_down, rebuilt_up, name="factor_down", in_specs=[VMEM] * (n_shards + 1) + [ANY], scratch_shapes=[narrow],
     )
     new_error_down, update_up, update_down = call(
         last_kernel, [shaped(1, ff, rows, dtype=BF16), shaped(rows, ff, dtype=BF16), shaped(ff, rows, dtype=BF16)],
-        gd, ed, lhs_up, rhs_up, lhs_down, rhs_down, clip, name="last", flops=product, grid=(STEPS,),
-        in_specs=[VMEM] * 7, out_specs=[replica_blocks(ff, rows), row_blocks(rows, ff), row_blocks(ff, rows)],
+        gd, ed, rebuilt_up, lhs_down, rhs_down, clip, name="last", flops=product, grid=(STEPS,),
+        in_specs=[VMEM] * 6, out_specs=[replica_blocks(ff, rows), row_blocks(rows, ff), row_blocks(ff, rows)],
     )
     return new_error_up, update_up, new_error_down, update_down
 

time: 82.6 us -> 80.1 us (0.970)
  starting transfers between devices: 32.7 us -> 29.3 us
  waiting for transfers between devices: 28.7 us -> 29.7 us
    ppermute x29 -> x26, starting transfers between devices: 32.7 us -> 29.3 us  [swap(): return lax.ppermute(x, axis, pairs)]
    ppermute x29 -> x26, waiting for transfers between devices: 28.7 us -> 29.7 us  [swap(): return lax.ppermute(x, axis, pairs)]
    pallas_call x18 -> x19, Pallas kernels: 18.5 us -> 18.4 us  [call(): pl.pallas_call(lambda *refs: kernel(*refs[skip:]), out_shape=out_shape, i...]
  transfers between devices with their start and end apart: 29 -> 26, of which waited for: 17 -> 18; matrix products, arithmetic and copies ran while one was open for 0% -> 0% of each run, Pallas kernels for 10% -> 8%
where the time goes in v14:
time: 80.1 us; the launch traced here: 79.9 us
  waiting for transfers between devices  29.7 us (37%)
  starting transfers between devices  29.3 us (37%)
  Pallas kernels  18.4 us (23%)
  local copies, waits for them, and re-layouts  1.7 us (2%)
    ppermute x26, waiting for transfers between devices, swap(): return lax.ppermute(x, axis, pairs)  29.7 us
    ppermute x26, starting transfers between devices, swap(): return lax.ppermute(x, axis, pairs)  29.3 us
    pallas_call x19, Pallas kernels, call(): pl.pallas_call(lambda *refs: kernel(*refs[skip:]), out_shape=out_shape, i...  18.4 us
    unnamed x12, local copies, waits for them, and re-layouts  1.7 us
  transfers between devices with their start and end apart: 26, of which 18 were waited for; matrix products, arithmetic and copies ran while one was open for 0% of the time, Pallas kernels for 8%

profile of v14, /device:TPU:0, one launch (start us, length us, event | category | flops | bytes accessed | tf_op | source)
XLA Modules:
  0.0 79.9 jit_solution(2307924630896164525)
XLA Ops:
  0.6 6.2 %left.1 = (f32[16,512]{1,0:T(8,128)}, f32[16,512]{1,0:T(8,128)}, f32[16,512]{1,0:T(8,128)}, f32[16,512]{1,0:T(8,128)}, f32[4,8,1536]{2,1,0:T(8,128)}, /*index=5*/f32[4,8,1536]{2,1,0:T(8,128)}) custom-call(bf16[1,512,1536]{2,1,0:T(8,128)(2,1)} %refs_0_.4, bf16[1,512,1536]{2,1,0:T(8,128)(2,1)} %refs_1_.4, f32[64,1536]{1,0:T(8,128)} %bitcast.2, ...), custom_call_target="tpu_custom_call" | custom-call | flops 1610612736 | bytes 7340032 | tf_op jit(solution)/shard_map/left/pallas_call | solution.py:385
  6.8 0.0 copy-start.2
  6.8 3.0 %collective-permute-start.3 = (f32[4,8,1536]{2,1,0:T(8,128)}, f32[4,8,1536]{2,1,0:T(8,128)S(1)}, u32[]{:S(2)}, u32[]{:S(2)}) collective-permute-start(f32[4,8,1536]{2,1,0:T(8,128)} %get-tuple-element.51), channel_id=1, source_target_pairs={{0,4},{4,0},{8,12},{12,8},{16,20},{20,16},{24,28},{28,24},{1,5},{5... | collective-permute-start | bytes 589832 | tf_op jit(solution)/shard_map/ppermute | solution.py:394
  9.9 0.0 collective-permute-start
  9.9 1.5 %collective-permute-start.1 = (f32[16,512]{1,0:T(8,128)}, f32[16,512]{1,0:T(8,128)S(1)}, u32[]{:S(2)}, u32[]{:S(2)}) collective-permute-start(f32[16,512]{1,0:T(8,128)} %get-tuple-element.48), channel_id=1, source_target_pairs={{0,2},{1,3},{2,0},{3,1},{4,6},{5,7},{6,4},{7,5},{8,10},{9,11},{10,... | collective-permute-start | bytes 98312 | tf_op jit(solution)/shard_map/ppermute | solution.py:394
  11.4 0.4 collective-permute-start.2
  11.7 0.9 %copy-done.4 = f32[4,8,1536]{2,1,0:T(8,128)S(1)} copy-done((f32[4,8,1536]{2,1,0:T(8,128)S(1)}, f32[4,8,1536]{2,1,0:T(8,128)}, u32[]{:S(2)}) %copy-start.4) | copy-done | bytes 196632
  12.7 0.8 copy-done.5
  13.4 0.0 collective-permute-done.refs_1_
  13.5 0.6 collective-permute-done.1.refs_2_
  14.0 0.9 %collective-permute-done.2.refs_3_ = f32[16,512]{1,0:T(8,128)S(1)} collective-permute-done((f32[16,512]{1,0:T(8,128)}, f32[16,512]{1,0:T(8,128)S(1)}, u32[]{:S(2)}, u32[]{:S(2)}) %collective-permute-start.2) | collective-permute-done | bytes 32800 | tf_op jit(solution)/shard_map/ppermute | solution.py:394
  14.9 0.1 collective-permute-done.3.refs_2_
  15.0 1.9 %collective-permute-start.4 = (f32[2,8,1536]{2,1,0:T(8,128)S(1)}, f32[2,8,1536]{2,1,0:T(8,128)S(1)}, u32[]{:S(2)}, u32[]{:S(2)}) collective-permute-start(f32[2,8,1536]{2,1,0:T(8,128)S(1)} %get-tuple-element.53), channel_id=1, source_target_pairs={{0,8},{4,12},{8,0},{12,4},{16,24},{20,28},{24,16},{28,20},{1,9},{5... | collective-permute-start | bytes 294920 | tf_op jit(solution)/shard_map/ppermute | solution.py:394
  16.9 1.5 %collective-permute-start.5 = (f32[16,512]{1,0:T(8,128)S(1)}, f32[16,512]{1,0:T(8,128)S(1)}, u32[]{:S(2)}, u32[]{:S(2)}) collective-permute-start(f32[16,512]{1,0:T(8,128)S(1)} %shard_sum.2.refs_0_), channel_id=1, source_target_pairs={{0,4},{4,0},{8,12},{12,8},{16,20},{20,16},{24,28},{28,24},{1,5},{5... | collective-permute-start | bytes 98312 | tf_op jit(solution)/shard_map/ppermute | solution.py:394
  18.4 2.4 %collective-permute-done.5.refs_1_ = f32[16,512]{1,0:T(8,128)S(1)} collective-permute-done((f32[16,512]{1,0:T(8,128)S(1)}, f32[16,512]{1,0:T(8,128)S(1)}, u32[]{:S(2)}, u32[]{:S(2)}) %collective-permute-start.5) | collective-permute-done | bytes 32800 | tf_op jit(solution)/shard_map/ppermute | solution.py:394
  20.8 0.0 collective-permute-done.4.refs_1_
  20.9 2.6 %collective-permute-start.6 = (f32[2,8,2048]{2,1,0:T(8,128)S(1)}, f32[2,8,2048]{2,1,0:T(8,128)S(1)}, u32[]{:S(2)}, u32[]{:S(2)}) collective-permute-start(f32[2,8,2048]{2,1,0:T(8,128)S(1)} %half_sum.1.refs_0_), channel_id=1, source_target_pairs={{0,16},{4,20},{8,24},{12,28},{16,0},{20,4},{24,8},{28,12},{1,17},{... | collective-permute-start | bytes 393224 | tf_op jit(solution)/shard_map/ppermute | solution.py:394
  23.5 5.5 %collective-permute-done.6.refs_1_ = f32[2,8,2048]{2,1,0:T(8,128)S(1)} collective-permute-done((f32[2,8,2048]{2,1,0:T(8,128)S(1)}, f32[2,8,2048]{2,1,0:T(8,128)S(1)}, u32[]{:S(2)}, u32[]{:S(2)}) %collective-permute-start.6) | collective-permute-done | bytes 131104 | tf_op jit(solution)/shard_map/ppermute | solution.py:394
  29.1 0.5 collective-permute-start.7
  29.5 4.5 %collective-permute-done.7.refs_1_ = f32[2,8,2048]{2,1,0:T(8,128)S(1)} collective-permute-done((f32[2,8,2048]{2,1,0:T(8,128)S(1)}, f32[2,8,2048]{2,1,0:T(8,128)S(1)}, u32[]{:S(2)}, u32[]{:S(2)}) %collective-permute-start.7) | collective-permute-done | bytes 131104 | tf_op jit(solution)/shard_map/ppermute | solution.py:394
  34.1 0.8 %collective-permute-start.8 = (f32[4,8,1536]{2,1,0:T(8,128)S(1)}, f32[4,8,1536]{2,1,0:T(8,128)S(1)}, u32[]{:S(2)}, u32[]{:S(2)}) collective-permute-start(f32[4,8,1536]{2,1,0:T(8,128)S(1)} %get-tuple-element.54.refs_1_), channel_id=1, source_target_pairs={{0,4},{4,0},{8,12},{12,8},{16,20},{20,16},{24,28},{28,24},{1,5},{5... | collective-permute-start | bytes 589832 | tf_op jit(solution)/shard_map/ppermute | solution.py:394
  34.9 0.0 collective-permute-start.11
  34.9 1.6 %collective-permute-start.10 = (f32[16,512]{1,0:T(8,128)S(1)}, f32[16,512]{1,0:T(8,128)S(1)}, u32[]{:S(2)}, u32[]{:S(2)}) collective-permute-start(f32[16,512]{1,0:T(8,128)S(1)} %get-tuple-element.55.refs_1_), channel_id=1, source_target_pairs={{0,2},{1,3},{2,0},{3,1},{4,6},{5,7},{6,4},{7,5},{8,10},{9,11},{10,... | collective-permute-start | bytes 98312 | tf_op jit(solution)/shard_map/ppermute | solution.py:394
  36.5 0.3 collective-permute-start.9
  36.8 1.7 %collective-permute-done.11.refs_4_ = f32[16,512]{1,0:T(8,128)S(1)} collective-permute-done((f32[16,512]{1,0:T(8,128)S(1)}, f32[16,512]{1,0:T(8,128)S(1)}, u32[]{:S(2)}, u32[]{:S(2)}) %collective-permute-start.11) | collective-permute-done | bytes 32800 | tf_op jit(solution)/shard_map/ppermute | solution.py:394
  38.5 0.4 collective-permute-done.10.refs_3_
  39.0 0.0 collective-permute-done.9.refs_2_
  39.0 0.9 %collective-permute-done.8.refs_0_.refs_2_ = f32[4,8,1536]{2,1,0:T(8,128)S(1)} collective-permute-done((f32[4,8,1536]{2,1,0:T(8,128)S(1)}, f32[4,8,1536]{2,1,0:T(8,128)S(1)}, u32[]{:S(2)}, u32[]{:S(2)}) %collective-permute-start.8) | collective-permute-done | bytes 196640 | tf_op jit(solution)/shard_map/ppermute | solution.py:394
  39.9 1.2 %right_up.1 = (f32[64,512]{1,0:T(8,128)S(1)}, f32[64,64]{1,0:T(8,128)S(1)}, f32[4,8,1536]{2,1,0:T(8,128)S(1)}, f32[4,8,1536]{2,1,0:T(8,128)S(1)}) custom-call(f32[4,8,1536]{2,1,0:T(8,128)S(1)} %collective-permute-done.8.refs_0_.refs_2_, f32[16,512]{1,0:T(8,128)S(1)} %get-tuple-element.55.refs_1_, f32[16,512]{1,0:T(8,128)S(1)} %collective-permute-done.9.refs_2_, ...), custom_call_target="tpu_custom_call" | custom-call | flops 805306368 | bytes 3817472 | tf_op jit(solution)/shard_map/right_up/pallas_call | solution.py:385
  41.1 0.8 %collective-permute-start.15 = (f32[4,8,1536]{2,1,0:T(8,128)S(1)}, f32[4,8,1536]{2,1,0:T(8,128)S(1)}, u32[]{:S(2)}, u32[]{:S(2)}) collective-permute-start(f32[4,8,1536]{2,1,0:T(8,128)S(1)} %get-tuple-element.65), channel_id=1, source_target_pairs={{0,4},{4,0},{8,12},{12,8},{16,20},{20,16},{24,28},{28,24},{1,5},{5... | collective-permute-start | bytes 589832 | tf_op jit(solution)/shard_map/ppermute | solution.py:394
  41.9 1.2 %right_down.1 = (f32[64,1536]{1,0:T(8,128)S(1)}, f32[16,768]{1,0:T(8,128)S(1)}, f32[16,768]{1,0:T(8,128)S(1)}, f32[16,768]{1,0:T(8,128)S(1)}, f32[16,768]{1,0:T(8,128)S(1)}) custom-call(f32[64,512]{1,0:T(8,128)S(1)} %get-tuple-element.56.refs_0_, f32[4,8,1536]{2,1,0:T(8,128)S(1)} %get-tuple-element.54.refs_1_, ...), custom_call_target="tpu_custom_call" | custom-call | flops 805306368 | bytes 4128768 | tf_op jit(solution)/shard_map/right_down/pallas_call | solution.py:385
  43.1 0.0 collective-permute-start.12
  43.1 1.6 %collective-permute-start.13 = (f32[16,768]{1,0:T(8,128)S(1)}, f32[16,768]{1,0:T(8,128)S(1)}, u32[]{:S(2)}, u32[]{:S(2)}) collective-permute-start(f32[16,768]{1,0:T(8,128)S(1)} %get-tuple-element.61), channel_id=1, source_target_pairs={{0,2},{1,3},{2,0},{3,1},{4,6},{5,7},{6,4},{7,5},{8,10},{9,11},{10,... | collective-permute-start | bytes 147464 | tf_op jit(solution)/shard_map/ppermute | solution.py:394
  44.7 0.3 collective-permute-start.14
  45.0 0.0 collective-permute-done.12.refs_1_
  45.0 2.3 %collective-permute-done.13.refs_2_ = f32[16,768]{1,0:T(8,128)S(1)} collective-permute-done((f32[16,768]{1,0:T(8,128)S(1)}, f32[16,768]{1,0:T(8,128)S(1)}, u32[]{:S(2)}, u32[]{:S(2)}) %collective-permute-start.13) | collective-permute-done | bytes 49184 | tf_op jit(solution)/shard_map/ppermute | solution.py:394
  47.3 1.1 %collective-permute-done.14.refs_3_ = f32[16,768]{1,0:T(8,128)S(1)} collective-permute-done((f32[16,768]{1,0:T(8,128)S(1)}, f32[16,768]{1,0:T(8,128)S(1)}, u32[]{:S(2)}, u32[]{:S(2)}) %collective-permute-start.14) | collective-permute-done | bytes 49184 | tf_op jit(solution)/shard_map/ppermute | solution.py:394
  48.4 0.1 shard_sum.3
  48.5 0.0 collective-permute-done.15.refs_1_
  48.5 0.1 collective-permute-start.16
  48.6 3.3 %collective-permute-start.17 = (f32[8,1792]{1,0:T(8,128)S(1)}, f32[8,1792]{1,0:T(8,128)S(1)}, u32[]{:S(2)}, u32[]{:S(2)}) collective-permute-start(f32[8,1792]{1,0:T(8,128)S(1)} %get-tuple-element.69), channel_id=1, source_target_pairs={{0,16},{4,20},{8,24},{12,28},{16,0},{20,4},{24,8},{28,12},{1,17},{... | collective-permute-start | bytes 172040 | tf_op jit(solution)/shard_map/ppermute | solution.py:394
  51.9 1.0 %collective-permute-start.18 = (f32[8,1792]{1,0:T(8,128)S(1)}, f32[8,1792]{1,0:T(8,128)S(1)}, u32[]{:S(2)}, u32[]{:S(2)}) collective-permute-start(f32[8,1792]{1,0:T(8,128)S(1)} %get-tuple-element.70), channel_id=1, source_target_pairs={{0,24},{4,28},{8,16},{12,20},{16,8},{20,12},{24,0},{28,4},{1,25},{... | collective-permute-start | bytes 172040 | tf_op jit(solution)/shard_map/ppermute | solution.py:394
  53.0 0.4 collective-permute-done.16.refs_1_
  53.4 2.2 %collective-permute-done.17.refs_2_ = f32[8,1792]{1,0:T(8,128)S(1)} collective-permute-done((f32[8,1792]{1,0:T(8,128)S(1)}, f32[8,1792]{1,0:T(8,128)S(1)}, u32[]{:S(2)}, u32[]{:S(2)}) %collective-permute-start.17) | collective-permute-done | bytes 57376 | tf_op jit(solution)/shard_map/ppermute | solution.py:394
  55.6 2.3 %collective-permute-done.18.refs_3_ = f32[8,1792]{1,0:T(8,128)S(1)} collective-permute-done((f32[8,1792]{1,0:T(8,128)S(1)}, f32[8,1792]{1,0:T(8,128)S(1)}, u32[]{:S(2)}, u32[]{:S(2)}) %collective-permute-start.18) | collective-permute-done | bytes 57376 | tf_op jit(solution)/shard_map/ppermute | solution.py:394
  57.9 1.8 %collective-permute-start.21 = (f32[8,1792]{1,0:T(8,128)S(1)}, f32[8,1792]{1,0:T(8,128)S(1)}, u32[]{:S(2)}, u32[]{:S(2)}) collective-permute-start(f32[8,1792]{1,0:T(8,128)S(1)} %replica_mean.1.refs_0_), channel_id=1, source_target_pairs={{0,24},{4,28},{8,16},{12,20},{16,8},{20,12},{24,0},{28,4},{1,25},{... | collective-permute-start | bytes 172040 | tf_op jit(solution)/shard_map/ppermute | solution.py:394
  59.7 0.0 collective-permute-start.20
  59.7 2.7 %collective-permute-start.19 = (f32[8,1792]{1,0:T(8,128)S(1)}, f32[8,1792]{1,0:T(8,128)S(1)}, u32[]{:S(2)}, u32[]{:S(2)}) collective-permute-start(f32[8,1792]{1,0:T(8,128)S(1)} %replica_mean.1.refs_0_), channel_id=1, source_target_pairs={{0,8},{4,12},{8,0},{12,4},{16,24},{20,28},{24,16},{28,20},{1,9},{5... | collective-permute-start | bytes 172040 | tf_op jit(solution)/shard_map/ppermute | solution.py:394
  62.4 1.6 %collective-permute-done.21.refs_3_ = f32[8,1792]{1,0:T(8,128)S(1)} collective-permute-done((f32[8,1792]{1,0:T(8,128)S(1)}, f32[8,1792]{1,0:T(8,128)S(1)}, u32[]{:S(2)}, u32[]{:S(2)}) %collective-permute-start.21) | collective-permute-done | bytes 57376 | tf_op jit(solution)/shard_map/ppermute | solution.py:394
  64.0 1.2 %collective-permute-done.20.refs_2_ = f32[8,1792]{1,0:T(8,128)S(1)} collective-permute-done((f32[8,1792]{1,0:T(8,128)S(1)}, f32[8,1792]{1,0:T(8,128)S(1)}, u32[]{:S(2)}, u32[]{:S(2)}) %collective-permute-start.20) | collective-permute-done | bytes 57376 | tf_op jit(solution)/shard_map/ppermute | solution.py:394
  65.2 0.0 collective-permute-done.19.refs_1_
  65.2 1.7 %collective-permute-start.22 = (f32[4,8,1792]{2,1,0:T(8,128)S(1)}, f32[4,8,1792]{2,1,0:T(8,128)S(1)}, u32[]{:S(2)}, u32[]{:S(2)}) collective-permute-start(f32[4,8,1792]{2,1,0:T(8,128)S(1)} %stack_z.1.refs_8_.refs_0_), channel_id=1, source_target_pairs={{0,4},{4,0},{8,12},{12,8},{16,20},{20,16},{24,28},{28,24},{1,5},{5... | collective-permute-start | bytes 688136 | tf_op jit(solution)/shard_map/ppermute | solution.py:394
  66.9 3.2 %basis.1 = (f32[64,64]{1,0:T(8,128)S(1)}, f32[64,64]{1,0:T(8,128)S(1)}, bf16[512,256]{1,0:T(8,128)(2,1)S(1)}, bf16[1536,256]{1,0:T(8,128)(2,1)S(1)}) custom-call(f32[64,512]{1,0:T(8,128)S(1)} %get-tuple-element.56.refs_0_, f32[64,1536]{1,0:T(8,128)S(1)} %get-tuple-element.57.refs_1_, f32[64,64]{1,0:T(8,128)S(1)} %get-tuple-element.58.refs_2_, ...), custom_call_target="tpu_custom_call" | custom-call | bytes 8159232 | tf_op jit(solution)/shard_map/basis/pallas_call | solution.py:385
  70.1 1.3 %collective-permute-done.22.refs_1_ = f32[4,8,1792]{2,1,0:T(8,128)S(1)} collective-permute-done((f32[4,8,1792]{2,1,0:T(8,128)S(1)}, f32[4,8,1792]{2,1,0:T(8,128)S(1)}, u32[]{:S(2)}, u32[]{:S(2)}) %collective-permute-start.22) | collective-permute-done | bytes 229408 | tf_op jit(solution)/shard_map/ppermute | solution.py:394
  71.3 0.7 factor_up.1
  72.0 0.1 collective-permute-start.25
  72.1 1.1 %collective-permute-start.24 = (f32[16,640]{1,0:T(8,128)S(1)}, f32[16,640]{1,0:T(8,128)S(1)}, u32[]{:S(2)}, u32[]{:S(2)}) collective-permute-start(f32[16,640]{1,0:T(8,128)S(1)} %get-tuple-element.77.refs_0_), channel_id=1, source_target_pairs={{0,2},{1,3},{2,0},{3,1},{4,6},{5,7},{6,4},{7,5},{8,10},{9,11},{10,... | collective-permute-start | bytes 122888 | tf_op jit(solution)/shard_map/ppermute | solution.py:394
  73.2 0.8 collective-permute-start.23
  73.9 2.3 %error_up.1 = (bf16[1,512,1536]{2,1,0:T(8,128)(2,1)}, f32[512,1536]{1,0:T(8,128)S(1)}) custom-call(bf16[1,512,1536]{2,1,0:T(8,128)(2,1)S(1)} %copy-done.2, bf16[1,512,1536]{2,1,0:T(8,128)(2,1)S(1)} %copy-done.3, bf16[512,256]{1,0:T(8,128)(2,1)S(1)} %get-tuple-element.71.refs_2_, bf16[256,1536]{1,0:T(8,128)(2,1)S(1)} %get-tuple-element.73.refs_3_), custom_call_target="tpu_custom_call" | custom-call | flops 402653184 | bytes 8912896 | tf_op jit(solution)/shard_map/error_up/pallas_call | solution.py:385
  76.3 0.0 collective-permute-done.25.refs_3_
  76.3 0.2 collective-permute-done.24.refs_2_
  76.5 0.0 collective-permute-done.23.refs_1_
  76.5 0.4 factor_down.1
  76.9 3.0 %last.1 = (bf16[1,1536,512]{2,1,0:T(8,128)(2,1)}, bf16[512,1536]{1,0:T(8,128)(2,1)}, bf16[1536,512]{1,0:T(8,128)(2,1)}) custom-call(bf16[1,1536,512]{2,1,0:T(8,128)(2,1)S(1)} %copy-done, bf16[1,1536,512]{2,1,0:T(8,128)(2,1)S(1)} %copy-done.1, f32[512,1536]{1,0:T(8,128)S(1)} %get-tuple-element.75.refs_5_.refs_2_, ...), custom_call_target="tpu_custom_call" | custom-call | flops 805306368 | bytes 12062720 | tf_op jit(solution)/shard_map/last/pallas_call | solution.py:385
  (19 shorter events, 0.2 us)
Async XLA Ops:
  0.6 39.2 %copy-start.3 = (bf16[1,512,1536]{2,1,0:T(8,128)(2,1)S(1)}, bf16[1,512,1536]{2,1,0:T(8,128)(2,1)}, u32[]{:S(2)}) copy-start(bf16[1,512,1536]{2,1,0:T(8,128)(2,1)} %refs_1_.4) | copy-start | bytes 4718596
  6.8 33.0 %copy-start.2 = (bf16[1,512,1536]{2,1,0:T(8,128)(2,1)S(1)}, bf16[1,512,1536]{2,1,0:T(8,128)(2,1)}, u32[]{:S(2)}) copy-start(bf16[1,512,1536]{2,1,0:T(8,128)(2,1)} %refs_0_.4) | copy-start | bytes 4718596
  6.8 8.1 %collective-permute-start.3 = (f32[4,8,1536]{2,1,0:T(8,128)}, f32[4,8,1536]{2,1,0:T(8,128)S(1)}, u32[]{:S(2)}, u32[]{:S(2)}) collective-permute-start(f32[4,8,1536]{2,1,0:T(8,128)} %get-tuple-element.51), channel_id=1, source_target_pairs={{0,4},{4,0},{8,12},{12,8},{16,20},{20,16},{24,28},{28,24},{1,5},{5... | collective-permute-start | bytes 589832 | tf_op jit(solution)/shard_map/ppermute | solution.py:394
  9.9 3.6 %collective-permute-start = (f32[16,512]{1,0:T(8,128)}, f32[16,512]{1,0:T(8,128)S(1)}, u32[]{:S(2)}, u32[]{:S(2)}) collective-permute-start(f32[16,512]{1,0:T(8,128)} %get-tuple-element.47), channel_id=1, source_target_pairs={{0,1},{1,0},{2,3},{3,2},{4,5},{5,4},{6,7},{7,6},{8,9},{9,8},{10,11... | collective-permute-start | bytes 98312 | tf_op jit(solution)/shard_map/ppermute | solution.py:394
  9.9 4.1 %collective-permute-start.1 = (f32[16,512]{1,0:T(8,128)}, f32[16,512]{1,0:T(8,128)S(1)}, u32[]{:S(2)}, u32[]{:S(2)}) collective-permute-start(f32[16,512]{1,0:T(8,128)} %get-tuple-element.48), channel_id=1, source_target_pairs={{0,2},{1,3},{2,0},{3,1},{4,6},{5,7},{6,4},{7,5},{8,10},{9,11},{10,... | collective-permute-start | bytes 98312 | tf_op jit(solution)/shard_map/ppermute | solution.py:394
  11.4 3.6 %collective-permute-start.2 = (f32[16,512]{1,0:T(8,128)}, f32[16,512]{1,0:T(8,128)S(1)}, u32[]{:S(2)}, u32[]{:S(2)}) collective-permute-start(f32[16,512]{1,0:T(8,128)} %get-tuple-element.49), channel_id=1, source_target_pairs={{0,3},{1,2},{2,1},{3,0},{4,7},{5,6},{6,5},{7,4},{8,11},{9,10},{10,... | collective-permute-start | bytes 98312 | tf_op jit(solution)/shard_map/ppermute | solution.py:394
  11.7 0.9 %copy-start.4 = (f32[4,8,1536]{2,1,0:T(8,128)S(1)}, f32[4,8,1536]{2,1,0:T(8,128)}, u32[]{:S(2)}) copy-start(f32[4,8,1536]{2,1,0:T(8,128)} %get-tuple-element.45.refs_1_) | copy-start | bytes 589828
  12.7 0.8 copy-start.5
  15.0 5.8 %collective-permute-start.4 = (f32[2,8,1536]{2,1,0:T(8,128)S(1)}, f32[2,8,1536]{2,1,0:T(8,128)S(1)}, u32[]{:S(2)}, u32[]{:S(2)}) collective-permute-start(f32[2,8,1536]{2,1,0:T(8,128)S(1)} %get-tuple-element.53), channel_id=1, source_target_pairs={{0,8},{4,12},{8,0},{12,4},{16,24},{20,28},{24,16},{28,20},{1,9},{5... | collective-permute-start | bytes 294920 | tf_op jit(solution)/shard_map/ppermute | solution.py:394
  16.9 3.9 %collective-permute-start.5 = (f32[16,512]{1,0:T(8,128)S(1)}, f32[16,512]{1,0:T(8,128)S(1)}, u32[]{:S(2)}, u32[]{:S(2)}) collective-permute-start(f32[16,512]{1,0:T(8,128)S(1)} %shard_sum.2.refs_0_), channel_id=1, source_target_pairs={{0,4},{4,0},{8,12},{12,8},{16,20},{20,16},{24,28},{28,24},{1,5},{5... | collective-permute-start | bytes 98312 | tf_op jit(solution)/shard_map/ppermute | solution.py:394
  20.9 8.2 %collective-permute-start.6 = (f32[2,8,2048]{2,1,0:T(8,128)S(1)}, f32[2,8,2048]{2,1,0:T(8,128)S(1)}, u32[]{:S(2)}, u32[]{:S(2)}) collective-permute-start(f32[2,8,2048]{2,1,0:T(8,128)S(1)} %half_sum.1.refs_0_), channel_id=1, source_target_pairs={{0,16},{4,20},{8,24},{12,28},{16,0},{20,4},{24,8},{28,12},{1,17},{... | collective-permute-start | bytes 393224 | tf_op jit(solution)/shard_map/ppermute | solution.py:394
  29.1 5.0 %collective-permute-start.7 = (f32[2,8,2048]{2,1,0:T(8,128)S(1)}, f32[2,8,2048]{2,1,0:T(8,128)S(1)}, u32[]{:S(2)}, u32[]{:S(2)}) collective-permute-start(f32[2,8,2048]{2,1,0:T(8,128)S(1)} %mean.1.refs_0_), channel_id=1, source_target_pairs={{0,8},{4,12},{8,0},{12,4},{16,24},{20,28},{24,16},{28,20},{1,9},{5... | collective-permute-start | bytes 393224 | tf_op jit(solution)/shard_map/ppermute | solution.py:394
  34.1 5.7 %collective-permute-start.8 = (f32[4,8,1536]{2,1,0:T(8,128)S(1)}, f32[4,8,1536]{2,1,0:T(8,128)S(1)}, u32[]{:S(2)}, u32[]{:S(2)}) collective-permute-start(f32[4,8,1536]{2,1,0:T(8,128)S(1)} %get-tuple-element.54.refs_1_), channel_id=1, source_target_pairs={{0,4},{4,0},{8,12},{12,8},{16,20},{20,16},{24,28},{28,24},{1,5},{5... | collective-permute-start | bytes 589832 | tf_op jit(solution)/shard_map/ppermute | solution.py:394
  34.9 7.0 %copy-start = (bf16[1,1536,512]{2,1,0:T(8,128)(2,1)S(1)}, bf16[1,1536,512]{2,1,0:T(8,128)(2,1)}, u32[]{:S(2)}) copy-start(bf16[1,1536,512]{2,1,0:T(8,128)(2,1)} %refs_0_.5) | copy-start | bytes 4718596
  34.9 7.0 %copy-start.1 = (bf16[1,1536,512]{2,1,0:T(8,128)(2,1)S(1)}, bf16[1,1536,512]{2,1,0:T(8,128)(2,1)}, u32[]{:S(2)}) copy-start(bf16[1,1536,512]{2,1,0:T(8,128)(2,1)} %refs_1_.5) | copy-start | bytes 4718596
  34.9 3.6 %collective-permute-start.11 = (f32[16,512]{1,0:T(8,128)S(1)}, f32[16,512]{1,0:T(8,128)S(1)}, u32[]{:S(2)}, u32[]{:S(2)}) collective-permute-start(f32[16,512]{1,0:T(8,128)S(1)} %get-tuple-element.55.refs_1_), channel_id=1, source_target_pairs={{0,3},{1,2},{2,1},{3,0},{4,7},{5,6},{6,5},{7,4},{8,11},{9,10},{10,... | collective-permute-start | bytes 98312 | tf_op jit(solution)/shard_map/ppermute | solution.py:394
  34.9 4.0 %collective-permute-start.10 = (f32[16,512]{1,0:T(8,128)S(1)}, f32[16,512]{1,0:T(8,128)S(1)}, u32[]{:S(2)}, u32[]{:S(2)}) collective-permute-start(f32[16,512]{1,0:T(8,128)S(1)} %get-tuple-element.55.refs_1_), channel_id=1, source_target_pairs={{0,2},{1,3},{2,0},{3,1},{4,6},{5,7},{6,4},{7,5},{8,10},{9,11},{10,... | collective-permute-start | bytes 98312 | tf_op jit(solution)/shard_map/ppermute | solution.py:394
  36.5 2.5 %collective-permute-start.9 = (f32[16,512]{1,0:T(8,128)S(1)}, f32[16,512]{1,0:T(8,128)S(1)}, u32[]{:S(2)}, u32[]{:S(2)}) collective-permute-start(f32[16,512]{1,0:T(8,128)S(1)} %get-tuple-element.55.refs_1_), channel_id=1, source_target_pairs={{0,1},{1,0},{2,3},{3,2},{4,5},{5,4},{6,7},{7,6},{8,9},{9,8},{10,11... | collective-permute-start | bytes 98312 | tf_op jit(solution)/shard_map/ppermute | solution.py:394
  41.1 7.4 %collective-permute-start.15 = (f32[4,8,1536]{2,1,0:T(8,128)S(1)}, f32[4,8,1536]{2,1,0:T(8,128)S(1)}, u32[]{:S(2)}, u32[]{:S(2)}) collective-permute-start(f32[4,8,1536]{2,1,0:T(8,128)S(1)} %get-tuple-element.65), channel_id=1, source_target_pairs={{0,4},{4,0},{8,12},{12,8},{16,20},{20,16},{24,28},{28,24},{1,5},{5... | collective-permute-start | bytes 589832 | tf_op jit(solution)/shard_map/ppermute | solution.py:394
  43.1 1.9 %collective-permute-start.12 = (f32[16,768]{1,0:T(8,128)S(1)}, f32[16,768]{1,0:T(8,128)S(1)}, u32[]{:S(2)}, u32[]{:S(2)}) collective-permute-start(f32[16,768]{1,0:T(8,128)S(1)} %get-tuple-element.60), channel_id=1, source_target_pairs={{0,1},{1,0},{2,3},{3,2},{4,5},{5,4},{6,7},{7,6},{8,9},{9,8},{10,11... | collective-permute-start | bytes 147464 | tf_op jit(solution)/shard_map/ppermute | solution.py:394
  43.1 4.2 %collective-permute-start.13 = (f32[16,768]{1,0:T(8,128)S(1)}, f32[16,768]{1,0:T(8,128)S(1)}, u32[]{:S(2)}, u32[]{:S(2)}) collective-permute-start(f32[16,768]{1,0:T(8,128)S(1)} %get-tuple-element.61), channel_id=1, source_target_pairs={{0,2},{1,3},{2,0},{3,1},{4,6},{5,7},{6,4},{7,5},{8,10},{9,11},{10,... | collective-permute-start | bytes 147464 | tf_op jit(solution)/shard_map/ppermute | solution.py:394
  44.7 3.7 %collective-permute-start.14 = (f32[16,768]{1,0:T(8,128)S(1)}, f32[16,768]{1,0:T(8,128)S(1)}, u32[]{:S(2)}, u32[]{:S(2)}) collective-permute-start(f32[16,768]{1,0:T(8,128)S(1)} %get-tuple-element.62), channel_id=1, source_target_pairs={{0,3},{1,2},{2,1},{3,0},{4,7},{5,6},{6,5},{7,4},{8,11},{9,10},{10,... | collective-permute-start | bytes 147464 | tf_op jit(solution)/shard_map/ppermute | solution.py:394
  48.5 4.9 %collective-permute-start.16 = (f32[8,1792]{1,0:T(8,128)S(1)}, f32[8,1792]{1,0:T(8,128)S(1)}, u32[]{:S(2)}, u32[]{:S(2)}) collective-permute-start(f32[8,1792]{1,0:T(8,128)S(1)} %get-tuple-element.68), channel_id=1, source_target_pairs={{0,8},{4,12},{8,0},{12,4},{16,24},{20,28},{24,16},{28,20},{1,9},{5... | collective-permute-start | bytes 172040 | tf_op jit(solution)/shard_map/ppermute | solution.py:394
  48.6 7.0 %collective-permute-start.17 = (f32[8,1792]{1,0:T(8,128)S(1)}, f32[8,1792]{1,0:T(8,128)S(1)}, u32[]{:S(2)}, u32[]{:S(2)}) collective-permute-start(f32[8,1792]{1,0:T(8,128)S(1)} %get-tuple-element.69), channel_id=1, source_target_pairs={{0,16},{4,20},{8,24},{12,28},{16,0},{20,4},{24,8},{28,12},{1,17},{... | collective-permute-start | bytes 172040 | tf_op jit(solution)/shard_map/ppermute | solution.py:394
  51.9 6.0 %collective-permute-start.18 = (f32[8,1792]{1,0:T(8,128)S(1)}, f32[8,1792]{1,0:T(8,128)S(1)}, u32[]{:S(2)}, u32[]{:S(2)}) collective-permute-start(f32[8,1792]{1,0:T(8,128)S(1)} %get-tuple-element.70), channel_id=1, source_target_pairs={{0,24},{4,28},{8,16},{12,20},{16,8},{20,12},{24,0},{28,4},{1,25},{... | collective-permute-start | bytes 172040 | tf_op jit(solution)/shard_map/ppermute | solution.py:394
  57.9 6.0 %collective-permute-start.21 = (f32[8,1792]{1,0:T(8,128)S(1)}, f32[8,1792]{1,0:T(8,128)S(1)}, u32[]{:S(2)}, u32[]{:S(2)}) collective-permute-start(f32[8,1792]{1,0:T(8,128)S(1)} %replica_mean.1.refs_0_), channel_id=1, source_target_pairs={{0,24},{4,28},{8,16},{12,20},{16,8},{20,12},{24,0},{28,4},{1,25},{... | collective-permute-start | bytes 172040 | tf_op jit(solution)/shard_map/ppermute | solution.py:394
  59.7 5.5 %collective-permute-start.20 = (f32[8,1792]{1,0:T(8,128)S(1)}, f32[8,1792]{1,0:T(8,128)S(1)}, u32[]{:S(2)}, u32[]{:S(2)}) collective-permute-start(f32[8,1792]{1,0:T(8,128)S(1)} %replica_mean.1.refs_0_), channel_id=1, source_target_pairs={{0,16},{4,20},{8,24},{12,28},{16,0},{20,4},{24,8},{28,12},{1,17},{... | collective-permute-start | bytes 172040 | tf_op jit(solution)/shard_map/ppermute | solution.py:394
  59.7 5.5 %collective-permute-start.19 = (f32[8,1792]{1,0:T(8,128)S(1)}, f32[8,1792]{1,0:T(8,128)S(1)}, u32[]{:S(2)}, u32[]{:S(2)}) collective-permute-start(f32[8,1792]{1,0:T(8,128)S(1)} %replica_mean.1.refs_0_), channel_id=1, source_target_pairs={{0,8},{4,12},{8,0},{12,4},{16,24},{20,28},{24,16},{28,20},{1,9},{5... | collective-permute-start | bytes 172040 | tf_op jit(solution)/shard_map/ppermute | solution.py:394
  65.2 6.1 %collective-permute-start.22 = (f32[4,8,1792]{2,1,0:T(8,128)S(1)}, f32[4,8,1792]{2,1,0:T(8,128)S(1)}, u32[]{:S(2)}, u32[]{:S(2)}) collective-permute-start(f32[4,8,1792]{2,1,0:T(8,128)S(1)} %stack_z.1.refs_8_.refs_0_), channel_id=1, source_target_pairs={{0,4},{4,0},{8,12},{12,8},{16,20},{20,16},{24,28},{28,24},{1,5},{5... | collective-permute-start | bytes 688136 | tf_op jit(solution)/shard_map/ppermute | solution.py:394
  72.0 4.3 %collective-permute-start.25 = (f32[16,640]{1,0:T(8,128)S(1)}, f32[16,640]{1,0:T(8,128)S(1)}, u32[]{:S(2)}, u32[]{:S(2)}) collective-permute-start(f32[16,640]{1,0:T(8,128)S(1)} %get-tuple-element.77.refs_0_), channel_id=1, source_target_pairs={{0,3},{1,2},{2,1},{3,0},{4,7},{5,6},{6,5},{7,4},{8,11},{9,10},{10,... | collective-permute-start | bytes 122888 | tf_op jit(solution)/shard_map/ppermute | solution.py:394
  72.1 4.4 %collective-permute-start.24 = (f32[16,640]{1,0:T(8,128)S(1)}, f32[16,640]{1,0:T(8,128)S(1)}, u32[]{:S(2)}, u32[]{:S(2)}) collective-permute-start(f32[16,640]{1,0:T(8,128)S(1)} %get-tuple-element.77.refs_0_), channel_id=1, source_target_pairs={{0,2},{1,3},{2,0},{3,1},{4,6},{5,7},{6,4},{7,5},{8,10},{9,11},{10,... | collective-permute-start | bytes 122888 | tf_op jit(solution)/shard_map/ppermute | solution.py:394
  73.2 3.3 %collective-permute-start.23 = (f32[16,640]{1,0:T(8,128)S(1)}, f32[16,640]{1,0:T(8,128)S(1)}, u32[]{:S(2)}, u32[]{:S(2)}) collective-permute-start(f32[16,640]{1,0:T(8,128)S(1)} %get-tuple-element.77.refs_0_), channel_id=1, source_target_pairs={{0,1},{1,0},{2,3},{3,2},{4,5},{5,4},{6,7},{7,6},{8,9},{9,8},{10,11... | collective-permute-start | bytes 122888 | tf_op jit(solution)/shard_map/ppermute | solution.py:394

commit v15 on v14

--- a/solution.py
+++ b/solution.py
@@ -179,13 +179,29 @@
     return jnp.concatenate([unfold(chunks[c, :, ff:], rows) for c in range(chunks.shape[0])], axis=1)
 
 
-def double_apart_kernel(bit, mine, other, out, shard):
+def double_apart_kernel(bit, mine, other, out, rest, shard):
     ff = out.shape[2]
     for j in range(mine.shape[0]):
         here, there = own_and_other(j, bit)
         out[here] = mine[j, :, :ff]
         out[there] = other[j, :, :ff]
+        rest[j] = other[j, :, :ff]
     shard[...] = join_shard(mine, ff, shard.shape[0]) + join_shard(other, ff, shard.shape[0])
+
+
+def strip_kernel(both, out):
+    out[...] = both[:, :, : out.shape[2]]
+
+
+def stack_rest_kernel(own, *refs):
+    *pieces, out, rest = refs
+    stack_kernel(own, *pieces, out)
+    for j, piece in enumerate(pieces):
+        rest[j] = piece[...]
+
+
+def place_other_kernel(own, rest, out):
+    stack_kernel(own, *[rest.at[j] for j in range(rest.shape[0])], out)
 
 
 def add_columns_kernel(chunks, shard, out):
@@ -422,11 +438,16 @@
     mine = call(functools.partial(sum_kernel, 1.0 / n_dp), both, total, swap(total, "dp", 1 << last), name="mean")
     for bit in range(last - 1, 0, -1):
         other = swap(mine, "dp", 1 << bit)
+        half = shaped(count, per, ff)
+        early = swap(call(strip_kernel, half, mine, name="strip"), "dp", 1) if bit == 1 else None
         count *= 2
-        mine, shard = call(functools.partial(double_apart_kernel, bit), [shaped(count, per, ff), shaped(*shard.shape)], mine, other, name="double")
+        mine, rest, shard = call(
+            functools.partial(double_apart_kernel, bit), [shaped(count, per, ff), half, shaped(*shard.shape)], mine, other,
+            after=(early,) if bit == 1 else (), name="double",
+        )
         if bit > 1:
             mine = call(add_columns_kernel, shaped(count, per, ff + (columns - ff) // (count // keep.shape[0])), mine, shard, name="add_columns")
-    return mine, shard
+    return mine, early, swap(rest, "dp", 1), shard
 
 
 def from_z(parts):
@@ -473,12 +494,12 @@
     shard = call(first_shards_kernel, shard_rows_here, *parts, name="shard_sum")
     keep, got = scatter_replicas(keep, send, got, (shard,))
     shard = call(first_shards_kernel, shard_rows_here, shard, swap(shard, "dp", 1), name="replica_sum")
-    mine, shard = gather_replicas(keep, got, shard)
-    other = swap(mine, "dp", 1)
+    mine, early, late, shard = gather_replicas(keep, got, shard)
+    other = call(functools.partial(double_kernel, 1), replica_half, early, late, name="other")
     left_rows = from_shards([shard] * n_shards)
     left_up, gram_up, keep, send = call(
         functools.partial(right_up_kernel, n_shards), [shaped(rank, rows), shaped(rank, rank), replica_half, replica_half],
-        *left_rows, gu, eu, after=(other,), name="right_up", flops=product,
+        *left_rows, gu, eu, after=(late,), name="right_up", flops=product,
         scratch_shapes=[pltpu.VMEM((3 * rank, rows), BF16), wide, stage],
     )
     left_down, *parts = call(
@@ -490,8 +511,10 @@
         functools.partial(sum_shards_kernel, n_shards), [shard_rows_here, shaped(rank, rank)], *from_shards(parts), name="shard_sum"
     )
     pieces = mean_replicas(keep, got, shard)
-    mine = call(stack_kernel, shaped(half, *pieces[0].shape), *pieces, name="stack_z")
-    other = swap(mine, "dp", 1)
+    early = swap(pieces[0], "dp", 1)
+    piece = pieces[0].shape
+    mine, rest = call(stack_rest_kernel, [shaped(half, *piece), shaped(half - 1, *piece)], *pieces, after=(early,), name="stack_z")
+    other = call(place_other_kernel, shaped(half, *piece), early, swap(rest, "dp", 1), name="other")
     inv_up, inv_down, lhs_up, lhs_down = call(
         basis_kernel,
         [shaped(rank, rank)] * 2 + [shaped(rows, 4 * rank, dtype=BF16), shaped(ff, 4 * rank, dtype=BF16)],

time: 80.1 us -> 80.8 us (level)
  starting transfers between devices: 29.3 us -> 31.7 us
  waiting for transfers between devices: 29.7 us -> 27.9 us
    ppermute x26 -> x28, starting transfers between devices: 29.3 us -> 31.7 us  [swap(): return lax.ppermute(x, axis, pairs)]
    ppermute x26 -> x28, waiting for transfers between devices: 29.7 us -> 27.9 us  [swap(): return lax.ppermute(x, axis, pairs)]
    pallas_call x19 -> x22, Pallas kernels: 18.4 us -> 18.5 us  [call(): pl.pallas_call(lambda *refs: kernel(*refs[skip:]), out_shape=out_shape, i...]
  transfers between devices with their start and end apart: 26 -> 28, of which waited for: 18 -> 17; matrix products, arithmetic and copies ran while one was open for 0% -> 0% of each run, Pallas kernels for 8% -> 8%
where the time goes in v15:
time: 80.8 us; the launch traced here: 80.6 us
  starting transfers between devices  31.7 us (39%)
  waiting for transfers between devices  27.9 us (35%)
  Pallas kernels  18.5 us (23%)
  local copies, waits for them, and re-layouts  1.7 us (2%)
  between operations  0.81 us (1%)
    ppermute x28, starting transfers between devices, swap(): return lax.ppermute(x, axis, pairs)  31.7 us
    ppermute x28, waiting for transfers between devices, swap(): return lax.ppermute(x, axis, pairs)  27.9 us
    pallas_call x22, Pallas kernels, call(): pl.pallas_call(lambda *refs: kernel(*refs[skip:]), out_shape=out_shape, i...  18.5 us
    unnamed x12, local copies, waits for them, and re-layouts  1.7 us
  transfers between devices with their start and end apart: 28, of which 17 were waited for; matrix products, arithmetic and copies ran while one was open for 0% of the time, Pallas kernels for 8%

profile of v15, /device:TPU:0, one launch (start us, length us, event | category | flops | bytes accessed | tf_op | source)
XLA Modules:
  0.0 80.6 jit_solution(128554444360577372)
XLA Ops:
  0.6 6.2 %left.1 = (f32[16,512]{1,0:T(8,128)}, f32[16,512]{1,0:T(8,128)}, f32[16,512]{1,0:T(8,128)}, f32[16,512]{1,0:T(8,128)}, f32[4,8,1536]{2,1,0:T(8,128)}, /*index=5*/f32[4,8,1536]{2,1,0:T(8,128)}) custom-call(bf16[1,512,1536]{2,1,0:T(8,128)(2,1)} %refs_0_.4, bf16[1,512,1536]{2,1,0:T(8,128)(2,1)} %refs_1_.4, f32[64,1536]{1,0:T(8,128)} %bitcast.2, ...), custom_call_target="tpu_custom_call" | custom-call | flops 1610612736 | bytes 7340032 | tf_op jit(solution)/shard_map/left/pallas_call | solution.py:401
  6.8 0.0 copy-start.2
  6.8 3.0 %collective-permute-start.3 = (f32[4,8,1536]{2,1,0:T(8,128)}, f32[4,8,1536]{2,1,0:T(8,128)S(1)}, u32[]{:S(2)}, u32[]{:S(2)}) collective-permute-start(f32[4,8,1536]{2,1,0:T(8,128)} %get-tuple-element.54), channel_id=1, source_target_pairs={{0,4},{4,0},{8,12},{12,8},{16,20},{20,16},{24,28},{28,24},{1,5},{5... | collective-permute-start | bytes 589832 | tf_op jit(solution)/shard_map/ppermute | solution.py:410
  9.9 0.0 collective-permute-start
  9.9 1.5 %collective-permute-start.1 = (f32[16,512]{1,0:T(8,128)}, f32[16,512]{1,0:T(8,128)S(1)}, u32[]{:S(2)}, u32[]{:S(2)}) collective-permute-start(f32[16,512]{1,0:T(8,128)} %get-tuple-element.51), channel_id=1, source_target_pairs={{0,2},{1,3},{2,0},{3,1},{4,6},{5,7},{6,4},{7,5},{8,10},{9,11},{10,... | collective-permute-start | bytes 98312 | tf_op jit(solution)/shard_map/ppermute | solution.py:410
  11.4 0.4 collective-permute-start.2
  11.7 0.9 %copy-done.4 = f32[4,8,1536]{2,1,0:T(8,128)S(1)} copy-done((f32[4,8,1536]{2,1,0:T(8,128)S(1)}, f32[4,8,1536]{2,1,0:T(8,128)}, u32[]{:S(2)}) %copy-start.4) | copy-done | bytes 196632
  12.7 0.8 copy-done.5
  13.4 0.0 collective-permute-done.refs_1_
  13.5 0.6 collective-permute-done.1.refs_2_
  14.0 0.9 %collective-permute-done.2.refs_3_ = f32[16,512]{1,0:T(8,128)S(1)} collective-permute-done((f32[16,512]{1,0:T(8,128)}, f32[16,512]{1,0:T(8,128)S(1)}, u32[]{:S(2)}, u32[]{:S(2)}) %collective-permute-start.2) | collective-permute-done | bytes 32800 | tf_op jit(solution)/shard_map/ppermute | solution.py:410
  14.9 0.1 collective-permute-done.3.refs_2_
  15.0 1.9 %collective-permute-start.4 = (f32[2,8,1536]{2,1,0:T(8,128)S(1)}, f32[2,8,1536]{2,1,0:T(8,128)S(1)}, u32[]{:S(2)}, u32[]{:S(2)}) collective-permute-start(f32[2,8,1536]{2,1,0:T(8,128)S(1)} %get-tuple-element.56), channel_id=1, source_target_pairs={{0,8},{4,12},{8,0},{12,4},{16,24},{20,28},{24,16},{28,20},{1,9},{5... | collective-permute-start | bytes 294920 | tf_op jit(solution)/shard_map/ppermute | solution.py:410
  16.9 1.5 %collective-permute-start.5 = (f32[16,512]{1,0:T(8,128)S(1)}, f32[16,512]{1,0:T(8,128)S(1)}, u32[]{:S(2)}, u32[]{:S(2)}) collective-permute-start(f32[16,512]{1,0:T(8,128)S(1)} %shard_sum.2.refs_0_), channel_id=1, source_target_pairs={{0,4},{4,0},{8,12},{12,8},{16,20},{20,16},{24,28},{28,24},{1,5},{5... | collective-permute-start | bytes 98312 | tf_op jit(solution)/shard_map/ppermute | solution.py:410
  18.4 2.4 %collective-permute-done.5.refs_1_ = f32[16,512]{1,0:T(8,128)S(1)} collective-permute-done((f32[16,512]{1,0:T(8,128)S(1)}, f32[16,512]{1,0:T(8,128)S(1)}, u32[]{:S(2)}, u32[]{:S(2)}) %collective-permute-start.5) | collective-permute-done | bytes 32800 | tf_op jit(solution)/shard_map/ppermute | solution.py:410
  20.8 0.0 collective-permute-done.4.refs_1_
  20.9 2.6 %collective-permute-start.6 = (f32[2,8,2048]{2,1,0:T(8,128)S(1)}, f32[2,8,2048]{2,1,0:T(8,128)S(1)}, u32[]{:S(2)}, u32[]{:S(2)}) collective-permute-start(f32[2,8,2048]{2,1,0:T(8,128)S(1)} %half_sum.1.refs_0_), channel_id=1, source_target_pairs={{0,16},{4,20},{8,24},{12,28},{16,0},{20,4},{24,8},{28,12},{1,17},{... | collective-permute-start | bytes 393224 | tf_op jit(solution)/shard_map/ppermute | solution.py:410
  23.5 5.5 %collective-permute-done.6.refs_1_ = f32[2,8,2048]{2,1,0:T(8,128)S(1)} collective-permute-done((f32[2,8,2048]{2,1,0:T(8,128)S(1)}, f32[2,8,2048]{2,1,0:T(8,128)S(1)}, u32[]{:S(2)}, u32[]{:S(2)}) %collective-permute-start.6) | collective-permute-done | bytes 131104 | tf_op jit(solution)/shard_map/ppermute | solution.py:410
  29.1 0.5 collective-permute-start.8
  29.6 0.4 collective-permute-start.7
  30.0 4.3 %collective-permute-done.7.refs_0_ = f32[2,8,1536]{2,1,0:T(8,128)S(1)} collective-permute-done((f32[2,8,1536]{2,1,0:T(8,128)S(1)}, f32[2,8,1536]{2,1,0:T(8,128)S(1)}, u32[]{:S(2)}, u32[]{:S(2)}) %collective-permute-start.7) | collective-permute-done | bytes 98336 | tf_op jit(solution)/shard_map/ppermute | solution.py:410
  34.2 0.0 collective-permute-done.8.refs_2_
  34.3 0.7 collective-permute-start.9
  34.9 0.0 collective-permute-start.12
  34.9 1.6 %collective-permute-start.11 = (f32[16,512]{1,0:T(8,128)S(1)}, f32[16,512]{1,0:T(8,128)S(1)}, u32[]{:S(2)}, u32[]{:S(2)}) collective-permute-start(f32[16,512]{1,0:T(8,128)S(1)} %get-tuple-element.58.refs_1_), channel_id=1, source_target_pairs={{0,2},{1,3},{2,0},{3,1},{4,6},{5,7},{6,4},{7,5},{8,10},{9,11},{10,... | collective-permute-start | bytes 98312 | tf_op jit(solution)/shard_map/ppermute | solution.py:410
  36.6 0.2 collective-permute-start.10
  36.8 1.7 %collective-permute-done.12.refs_4_ = f32[16,512]{1,0:T(8,128)S(1)} collective-permute-done((f32[16,512]{1,0:T(8,128)S(1)}, f32[16,512]{1,0:T(8,128)S(1)}, u32[]{:S(2)}, u32[]{:S(2)}) %collective-permute-start.12) | collective-permute-done | bytes 32800 | tf_op jit(solution)/shard_map/ppermute | solution.py:410
  38.5 0.5 collective-permute-done.11.refs_3_
  39.0 0.0 collective-permute-done.10.refs_2_
  39.0 0.0 collective-permute-done.9.refs_0_.refs_1_
  39.0 1.2 %right_up.1 = (f32[64,512]{1,0:T(8,128)S(1)}, f32[64,64]{1,0:T(8,128)S(1)}, f32[4,8,1536]{2,1,0:T(8,128)S(1)}, f32[4,8,1536]{2,1,0:T(8,128)S(1)}) custom-call(f32[2,8,1536]{2,1,0:T(8,128)S(1)} %collective-permute-done.9.refs_0_.refs_1_, f32[16,512]{1,0:T(8,128)S(1)} %get-tuple-element.58.refs_1_, f32[16,512]{1,0:T(8,128)S(1)} %collective-permute-done.10.refs_2_, ...), custom_call_target="tpu_custom_call" | custom-call | flops 805306368 | bytes 3817472 | tf_op jit(solution)/shard_map/right_up/pallas_call | solution.py:401
  40.2 1.7 %collective-permute-start.16 = (f32[4,8,1536]{2,1,0:T(8,128)S(1)}, f32[4,8,1536]{2,1,0:T(8,128)S(1)}, u32[]{:S(2)}, u32[]{:S(2)}) collective-permute-start(f32[4,8,1536]{2,1,0:T(8,128)S(1)} %get-tuple-element.69), channel_id=1, source_target_pairs={{0,4},{4,0},{8,12},{12,8},{16,20},{20,16},{24,28},{28,24},{1,5},{5... | collective-permute-start | bytes 589832 | tf_op jit(solution)/shard_map/ppermute | solution.py:410
  41.9 1.2 %right_down.1 = (f32[64,1536]{1,0:T(8,128)S(1)}, f32[16,768]{1,0:T(8,128)S(1)}, f32[16,768]{1,0:T(8,128)S(1)}, f32[16,768]{1,0:T(8,128)S(1)}, f32[16,768]{1,0:T(8,128)S(1)}) custom-call(f32[64,512]{1,0:T(8,128)S(1)} %get-tuple-element.59.refs_0_, f32[4,8,1536]{2,1,0:T(8,128)S(1)} %get-tuple-element.60.refs_1_, f32[4,8,1536]{2,1,0:T(8,128)S(1)} %other.2.refs_2_, ...), custom_call_target="tpu_custom_call" | custom-call | flops 805306368 | bytes 4128768 | tf_op jit(solution)/shard_map/right_down/pallas_call | solution.py:401
  43.1 0.0 collective-permute-start.13
  43.2 0.6 collective-permute-start.14
  43.8 1.3 %collective-permute-start.15 = (f32[16,768]{1,0:T(8,128)S(1)}, f32[16,768]{1,0:T(8,128)S(1)}, u32[]{:S(2)}, u32[]{:S(2)}) collective-permute-start(f32[16,768]{1,0:T(8,128)S(1)} %get-tuple-element.66), channel_id=1, source_target_pairs={{0,3},{1,2},{2,1},{3,0},{4,7},{5,6},{6,5},{7,4},{8,11},{9,10},{10,... | collective-permute-start | bytes 147464 | tf_op jit(solution)/shard_map/ppermute | solution.py:410
  45.0 2.7 %collective-permute-done.14.refs_2_ = f32[16,768]{1,0:T(8,128)S(1)} collective-permute-done((f32[16,768]{1,0:T(8,128)S(1)}, f32[16,768]{1,0:T(8,128)S(1)}, u32[]{:S(2)}, u32[]{:S(2)}) %collective-permute-start.14) | collective-permute-done | bytes 49184 | tf_op jit(solution)/shard_map/ppermute | solution.py:410
  47.8 0.1 collective-permute-done.15.refs_3_
  47.9 0.1 shard_sum.3
  48.0 0.0 collective-permute-done.16.refs_1_
  48.1 1.9 %collective-permute-start.17 = (f32[8,1792]{1,0:T(8,128)S(1)}, f32[8,1792]{1,0:T(8,128)S(1)}, u32[]{:S(2)}, u32[]{:S(2)}) collective-permute-start(f32[8,1792]{1,0:T(8,128)S(1)} %get-tuple-element.72), channel_id=1, source_target_pairs={{0,8},{4,12},{8,0},{12,4},{16,24},{20,28},{24,16},{28,20},{1,9},{5... | collective-permute-start | bytes 172040 | tf_op jit(solution)/shard_map/ppermute | solution.py:410
  49.9 2.0 %collective-permute-start.18 = (f32[8,1792]{1,0:T(8,128)S(1)}, f32[8,1792]{1,0:T(8,128)S(1)}, u32[]{:S(2)}, u32[]{:S(2)}) collective-permute-start(f32[8,1792]{1,0:T(8,128)S(1)} %get-tuple-element.73), channel_id=1, source_target_pairs={{0,16},{4,20},{8,24},{12,28},{16,0},{20,4},{24,8},{28,12},{1,17},{... | collective-permute-start | bytes 172040 | tf_op jit(solution)/shard_map/ppermute | solution.py:410
  51.9 1.3 %collective-permute-start.19 = (f32[8,1792]{1,0:T(8,128)S(1)}, f32[8,1792]{1,0:T(8,128)S(1)}, u32[]{:S(2)}, u32[]{:S(2)}) collective-permute-start(f32[8,1792]{1,0:T(8,128)S(1)} %get-tuple-element.74), channel_id=1, source_target_pairs={{0,24},{4,28},{8,16},{12,20},{16,8},{20,12},{24,0},{28,4},{1,25},{... | collective-permute-start | bytes 172040 | tf_op jit(solution)/shard_map/ppermute | solution.py:410
  53.2 2.6 %collective-permute-done.18.refs_2_ = f32[8,1792]{1,0:T(8,128)S(1)} collective-permute-done((f32[8,1792]{1,0:T(8,128)S(1)}, f32[8,1792]{1,0:T(8,128)S(1)}, u32[]{:S(2)}, u32[]{:S(2)}) %collective-permute-start.18) | collective-permute-done | bytes 57376 | tf_op jit(solution)/shard_map/ppermute | solution.py:410
  55.8 2.2 %collective-permute-done.19.refs_3_ = f32[8,1792]{1,0:T(8,128)S(1)} collective-permute-done((f32[8,1792]{1,0:T(8,128)S(1)}, f32[8,1792]{1,0:T(8,128)S(1)}, u32[]{:S(2)}, u32[]{:S(2)}) %collective-permute-start.19) | collective-permute-done | bytes 57376 | tf_op jit(solution)/shard_map/ppermute | solution.py:410
  57.9 2.5 %collective-permute-start.23 = (f32[8,1792]{1,0:T(8,128)S(1)}, f32[8,1792]{1,0:T(8,128)S(1)}, u32[]{:S(2)}, u32[]{:S(2)}) collective-permute-start(f32[8,1792]{1,0:T(8,128)S(1)} %replica_mean.1.refs_1_), channel_id=1, source_target_pairs={{0,24},{4,28},{8,16},{12,20},{16,8},{20,12},{24,0},{28,4},{1,25},{... | collective-permute-start | bytes 172040 | tf_op jit(solution)/shard_map/ppermute | solution.py:410
  60.4 0.4 collective-permute-start.22
  60.8 1.6 %collective-permute-start.21 = (f32[8,1792]{1,0:T(8,128)S(1)}, f32[8,1792]{1,0:T(8,128)S(1)}, u32[]{:S(2)}, u32[]{:S(2)}) collective-permute-start(f32[8,1792]{1,0:T(8,128)S(1)} %replica_mean.1.refs_1_), channel_id=1, source_target_pairs={{0,8},{4,12},{8,0},{12,4},{16,24},{20,28},{24,16},{28,20},{1,9},{5... | collective-permute-start | bytes 172040 | tf_op jit(solution)/shard_map/ppermute | solution.py:410
  62.4 1.1 %collective-permute-start.20 = (f32[8,1792]{1,0:T(8,128)S(1)}, f32[8,1792]{1,0:T(8,128)S(1)}, u32[]{:S(2)}, u32[]{:S(2)}) collective-permute-start(f32[8,1792]{1,0:T(8,128)S(1)} %replica_mean.1.refs_1_), channel_id=1, source_target_pairs={{0,4},{4,0},{8,12},{12,8},{16,20},{20,16},{24,28},{28,24},{1,5},{5... | collective-permute-start | bytes 172040 | tf_op jit(solution)/shard_map/ppermute | solution.py:410
  63.5 1.0 %collective-permute-done.23.refs_4_ = f32[8,1792]{1,0:T(8,128)S(1)} collective-permute-done((f32[8,1792]{1,0:T(8,128)S(1)}, f32[8,1792]{1,0:T(8,128)S(1)}, u32[]{:S(2)}, u32[]{:S(2)}) %collective-permute-start.23) | collective-permute-done | bytes 57376 | tf_op jit(solution)/shard_map/ppermute | solution.py:410
  64.6 1.7 %collective-permute-done.22.refs_3_ = f32[8,1792]{1,0:T(8,128)S(1)} collective-permute-done((f32[8,1792]{1,0:T(8,128)S(1)}, f32[8,1792]{1,0:T(8,128)S(1)}, u32[]{:S(2)}, u32[]{:S(2)}) %collective-permute-start.22) | collective-permute-done | bytes 57376 | tf_op jit(solution)/shard_map/ppermute | solution.py:410
  66.3 0.3 collective-permute-done.20.refs_0_
  66.6 1.2 %collective-permute-start.24 = (f32[3,8,1792]{2,1,0:T(8,128)S(1)}, f32[3,8,1792]{2,1,0:T(8,128)S(1)}, u32[]{:S(2)}, u32[]{:S(2)}) collective-permute-start(f32[3,8,1792]{2,1,0:T(8,128)S(1)} %get-tuple-element.77), channel_id=1, source_target_pairs={{0,4},{4,0},{8,12},{12,8},{16,20},{20,16},{24,28},{28,24},{1,5},{5... | collective-permute-start | bytes 516104 | tf_op jit(solution)/shard_map/ppermute | solution.py:410
  67.8 3.2 %basis.1 = (f32[64,64]{1,0:T(8,128)S(1)}, f32[64,64]{1,0:T(8,128)S(1)}, bf16[512,256]{1,0:T(8,128)(2,1)S(1)}, bf16[1536,256]{1,0:T(8,128)(2,1)S(1)}) custom-call(f32[64,512]{1,0:T(8,128)S(1)} %get-tuple-element.59.refs_0_, f32[64,1536]{1,0:T(8,128)S(1)} %get-tuple-element.61.refs_1_, f32[64,64]{1,0:T(8,128)S(1)} %get-tuple-element.62.refs_2_, ...), custom_call_target="tpu_custom_call" | custom-call | bytes 8159232 | tf_op jit(solution)/shard_map/basis/pallas_call | solution.py:401
  71.0 1.1 %collective-permute-done.24.refs_1_ = f32[3,8,1792]{2,1,0:T(8,128)S(1)} collective-permute-done((f32[3,8,1792]{2,1,0:T(8,128)S(1)}, f32[3,8,1792]{2,1,0:T(8,128)S(1)}, u32[]{:S(2)}, u32[]{:S(2)}) %collective-permute-start.24) | collective-permute-done | bytes 172064 | tf_op jit(solution)/shard_map/ppermute | solution.py:410
  72.1 0.7 factor_up.1
  72.8 0.1 collective-permute-start.27
  72.9 1.6 %collective-permute-start.26 = (f32[16,640]{1,0:T(8,128)S(1)}, f32[16,640]{1,0:T(8,128)S(1)}, u32[]{:S(2)}, u32[]{:S(2)}) collective-permute-start(f32[16,640]{1,0:T(8,128)S(1)} %get-tuple-element.83.refs_0_), channel_id=1, source_target_pairs={{0,2},{1,3},{2,0},{3,1},{4,6},{5,7},{6,4},{7,5},{8,10},{9,11},{10,... | collective-permute-start | bytes 122888 | tf_op jit(solution)/shard_map/ppermute | solution.py:410
  74.5 0.3 collective-permute-start.25
  74.7 2.3 %error_up.1 = (bf16[1,512,1536]{2,1,0:T(8,128)(2,1)}, f32[512,1536]{1,0:T(8,128)S(1)}) custom-call(bf16[1,512,1536]{2,1,0:T(8,128)(2,1)S(1)} %copy-done.2, bf16[1,512,1536]{2,1,0:T(8,128)(2,1)S(1)} %copy-done.3, bf16[512,256]{1,0:T(8,128)(2,1)S(1)} %get-tuple-element.76.refs_2_, bf16[256,1536]{1,0:T(8,128)(2,1)S(1)} %get-tuple-element.79.refs_3_), custom_call_target="tpu_custom_call" | custom-call | flops 402653184 | bytes 8912896 | tf_op jit(solution)/shard_map/error_up/pallas_call | solution.py:401
  77.1 0.2 collective-permute-done.26.refs_2_
  77.2 0.0 collective-permute-done.25.refs_1_
  77.2 0.4 factor_down.1
  77.6 3.0 %last.1 = (bf16[1,1536,512]{2,1,0:T(8,128)(2,1)}, bf16[512,1536]{1,0:T(8,128)(2,1)}, bf16[1536,512]{1,0:T(8,128)(2,1)}) custom-call(bf16[1,1536,512]{2,1,0:T(8,128)(2,1)S(1)} %copy-done, bf16[1,1536,512]{2,1,0:T(8,128)(2,1)S(1)} %copy-done.1, f32[512,1536]{1,0:T(8,128)S(1)} %get-tuple-element.81.refs_5_.refs_2_, ...), custom_call_target="tpu_custom_call" | custom-call | flops 805306368 | bytes 12062720 | tf_op jit(solution)/shard_map/last/pallas_call | solution.py:401
  (26 shorter events, 0.3 us)
Async XLA Ops:
  0.6 38.3 %copy-start.3 = (bf16[1,512,1536]{2,1,0:T(8,128)(2,1)S(1)}, bf16[1,512,1536]{2,1,0:T(8,128)(2,1)}, u32[]{:S(2)}) copy-start(bf16[1,512,1536]{2,1,0:T(8,128)(2,1)} %refs_1_.4) | copy-start | bytes 4718596
  6.8 32.1 %copy-start.2 = (bf16[1,512,1536]{2,1,0:T(8,128)(2,1)S(1)}, bf16[1,512,1536]{2,1,0:T(8,128)(2,1)}, u32[]{:S(2)}) copy-start(bf16[1,512,1536]{2,1,0:T(8,128)(2,1)} %refs_0_.4) | copy-start | bytes 4718596
  6.8 8.1 %collective-permute-start.3 = (f32[4,8,1536]{2,1,0:T(8,128)}, f32[4,8,1536]{2,1,0:T(8,128)S(1)}, u32[]{:S(2)}, u32[]{:S(2)}) collective-permute-start(f32[4,8,1536]{2,1,0:T(8,128)} %get-tuple-element.54), channel_id=1, source_target_pairs={{0,4},{4,0},{8,12},{12,8},{16,20},{20,16},{24,28},{28,24},{1,5},{5... | collective-permute-start | bytes 589832 | tf_op jit(solution)/shard_map/ppermute | solution.py:410
  9.9 3.6 %collective-permute-start = (f32[16,512]{1,0:T(8,128)}, f32[16,512]{1,0:T(8,128)S(1)}, u32[]{:S(2)}, u32[]{:S(2)}) collective-permute-start(f32[16,512]{1,0:T(8,128)} %get-tuple-element.50), channel_id=1, source_target_pairs={{0,1},{1,0},{2,3},{3,2},{4,5},{5,4},{6,7},{7,6},{8,9},{9,8},{10,11... | collective-permute-start | bytes 98312 | tf_op jit(solution)/shard_map/ppermute | solution.py:410
  9.9 4.1 %collective-permute-start.1 = (f32[16,512]{1,0:T(8,128)}, f32[16,512]{1,0:T(8,128)S(1)}, u32[]{:S(2)}, u32[]{:S(2)}) collective-permute-start(f32[16,512]{1,0:T(8,128)} %get-tuple-element.51), channel_id=1, source_target_pairs={{0,2},{1,3},{2,0},{3,1},{4,6},{5,7},{6,4},{7,5},{8,10},{9,11},{10,... | collective-permute-start | bytes 98312 | tf_op jit(solution)/shard_map/ppermute | solution.py:410
  11.4 3.6 %collective-permute-start.2 = (f32[16,512]{1,0:T(8,128)}, f32[16,512]{1,0:T(8,128)S(1)}, u32[]{:S(2)}, u32[]{:S(2)}) collective-permute-start(f32[16,512]{1,0:T(8,128)} %get-tuple-element.52), channel_id=1, source_target_pairs={{0,3},{1,2},{2,1},{3,0},{4,7},{5,6},{6,5},{7,4},{8,11},{9,10},{10,... | collective-permute-start | bytes 98312 | tf_op jit(solution)/shard_map/ppermute | solution.py:410
  11.7 0.9 %copy-start.4 = (f32[4,8,1536]{2,1,0:T(8,128)S(1)}, f32[4,8,1536]{2,1,0:T(8,128)}, u32[]{:S(2)}) copy-start(f32[4,8,1536]{2,1,0:T(8,128)} %get-tuple-element.48.refs_1_) | copy-start | bytes 589828
  12.7 0.8 copy-start.5
  15.0 5.8 %collective-permute-start.4 = (f32[2,8,1536]{2,1,0:T(8,128)S(1)}, f32[2,8,1536]{2,1,0:T(8,128)S(1)}, u32[]{:S(2)}, u32[]{:S(2)}) collective-permute-start(f32[2,8,1536]{2,1,0:T(8,128)S(1)} %get-tuple-element.56), channel_id=1, source_target_pairs={{0,8},{4,12},{8,0},{12,4},{16,24},{20,28},{24,16},{28,20},{1,9},{5... | collective-permute-start | bytes 294920 | tf_op jit(solution)/shard_map/ppermute | solution.py:410
  16.9 3.9 %collective-permute-start.5 = (f32[16,512]{1,0:T(8,128)S(1)}, f32[16,512]{1,0:T(8,128)S(1)}, u32[]{:S(2)}, u32[]{:S(2)}) collective-permute-start(f32[16,512]{1,0:T(8,128)S(1)} %shard_sum.2.refs_0_), channel_id=1, source_target_pairs={{0,4},{4,0},{8,12},{12,8},{16,20},{20,16},{24,28},{28,24},{1,5},{5... | collective-permute-start | bytes 98312 | tf_op jit(solution)/shard_map/ppermute | solution.py:410
  20.9 8.2 %collective-permute-start.6 = (f32[2,8,2048]{2,1,0:T(8,128)S(1)}, f32[2,8,2048]{2,1,0:T(8,128)S(1)}, u32[]{:S(2)}, u32[]{:S(2)}) collective-permute-start(f32[2,8,2048]{2,1,0:T(8,128)S(1)} %half_sum.1.refs_0_), channel_id=1, source_target_pairs={{0,16},{4,20},{8,24},{12,28},{16,0},{20,4},{24,8},{28,12},{1,17},{... | collective-permute-start | bytes 393224 | tf_op jit(solution)/shard_map/ppermute | solution.py:410
  29.1 5.2 %collective-permute-start.8 = (f32[2,8,2048]{2,1,0:T(8,128)S(1)}, f32[2,8,2048]{2,1,0:T(8,128)S(1)}, u32[]{:S(2)}, u32[]{:S(2)}) collective-permute-start(f32[2,8,2048]{2,1,0:T(8,128)S(1)} %mean.1.refs_0_.refs_1_), channel_id=1, source_target_pairs={{0,8},{4,12},{8,0},{12,4},{16,24},{20,28},{24,16},{28,20},{1,9},{5... | collective-permute-start | bytes 393224 | tf_op jit(solution)/shard_map/ppermute | solution.py:410
  29.6 4.7 %collective-permute-start.7 = (f32[2,8,1536]{2,1,0:T(8,128)S(1)}, f32[2,8,1536]{2,1,0:T(8,128)S(1)}, u32[]{:S(2)}, u32[]{:S(2)}) collective-permute-start(f32[2,8,1536]{2,1,0:T(8,128)S(1)} %strip.1), channel_id=1, source_target_pairs={{0,4},{4,0},{8,12},{12,8},{16,20},{20,16},{24,28},{28,24},{1,5},{5... | collective-permute-start | bytes 294920 | tf_op jit(solution)/shard_map/ppermute | solution.py:410
  34.3 4.7 %collective-permute-start.9 = (f32[2,8,1536]{2,1,0:T(8,128)S(1)}, f32[2,8,1536]{2,1,0:T(8,128)S(1)}, u32[]{:S(2)}, u32[]{:S(2)}) collective-permute-start(f32[2,8,1536]{2,1,0:T(8,128)S(1)} %get-tuple-element.57), channel_id=1, source_target_pairs={{0,4},{4,0},{8,12},{12,8},{16,20},{20,16},{24,28},{28,24},{1,5},{5... | collective-permute-start | bytes 294920 | tf_op jit(solution)/shard_map/ppermute | solution.py:410
  34.9 7.0 %copy-start = (bf16[1,1536,512]{2,1,0:T(8,128)(2,1)S(1)}, bf16[1,1536,512]{2,1,0:T(8,128)(2,1)}, u32[]{:S(2)}) copy-start(bf16[1,1536,512]{2,1,0:T(8,128)(2,1)} %refs_0_.5) | copy-start | bytes 4718596
  34.9 7.0 %copy-start.1 = (bf16[1,1536,512]{2,1,0:T(8,128)(2,1)S(1)}, bf16[1,1536,512]{2,1,0:T(8,128)(2,1)}, u32[]{:S(2)}) copy-start(bf16[1,1536,512]{2,1,0:T(8,128)(2,1)} %refs_1_.5) | copy-start | bytes 4718596
  34.9 3.5 %collective-permute-start.12 = (f32[16,512]{1,0:T(8,128)S(1)}, f32[16,512]{1,0:T(8,128)S(1)}, u32[]{:S(2)}, u32[]{:S(2)}) collective-permute-start(f32[16,512]{1,0:T(8,128)S(1)} %get-tuple-element.58.refs_1_), channel_id=1, source_target_pairs={{0,3},{1,2},{2,1},{3,0},{4,7},{5,6},{6,5},{7,4},{8,11},{9,10},{10,... | collective-permute-start | bytes 98312 | tf_op jit(solution)/shard_map/ppermute | solution.py:410
  34.9 4.0 %collective-permute-start.11 = (f32[16,512]{1,0:T(8,128)S(1)}, f32[16,512]{1,0:T(8,128)S(1)}, u32[]{:S(2)}, u32[]{:S(2)}) collective-permute-start(f32[16,512]{1,0:T(8,128)S(1)} %get-tuple-element.58.refs_1_), channel_id=1, source_target_pairs={{0,2},{1,3},{2,0},{3,1},{4,6},{5,7},{6,4},{7,5},{8,10},{9,11},{10,... | collective-permute-start | bytes 98312 | tf_op jit(solution)/shard_map/ppermute | solution.py:410
  36.6 2.4 %collective-permute-start.10 = (f32[16,512]{1,0:T(8,128)S(1)}, f32[16,512]{1,0:T(8,128)S(1)}, u32[]{:S(2)}, u32[]{:S(2)}) collective-permute-start(f32[16,512]{1,0:T(8,128)S(1)} %get-tuple-element.58.refs_1_), channel_id=1, source_target_pairs={{0,1},{1,0},{2,3},{3,2},{4,5},{5,4},{6,7},{7,6},{8,9},{9,8},{10,11... | collective-permute-start | bytes 98312 | tf_op jit(solution)/shard_map/ppermute | solution.py:410
  40.2 7.8 %collective-permute-start.16 = (f32[4,8,1536]{2,1,0:T(8,128)S(1)}, f32[4,8,1536]{2,1,0:T(8,128)S(1)}, u32[]{:S(2)}, u32[]{:S(2)}) collective-permute-start(f32[4,8,1536]{2,1,0:T(8,128)S(1)} %get-tuple-element.69), channel_id=1, source_target_pairs={{0,4},{4,0},{8,12},{12,8},{16,20},{20,16},{24,28},{28,24},{1,5},{5... | collective-permute-start | bytes 589832 | tf_op jit(solution)/shard_map/ppermute | solution.py:410
  43.1 1.9 %collective-permute-start.13 = (f32[16,768]{1,0:T(8,128)S(1)}, f32[16,768]{1,0:T(8,128)S(1)}, u32[]{:S(2)}, u32[]{:S(2)}) collective-permute-start(f32[16,768]{1,0:T(8,128)S(1)} %get-tuple-element.64), channel_id=1, source_target_pairs={{0,1},{1,0},{2,3},{3,2},{4,5},{5,4},{6,7},{7,6},{8,9},{9,8},{10,11... | collective-permute-start | bytes 147464 | tf_op jit(solution)/shard_map/ppermute | solution.py:410
  43.2 4.6 %collective-permute-start.14 = (f32[16,768]{1,0:T(8,128)S(1)}, f32[16,768]{1,0:T(8,128)S(1)}, u32[]{:S(2)}, u32[]{:S(2)}) collective-permute-start(f32[16,768]{1,0:T(8,128)S(1)} %get-tuple-element.65), channel_id=1, source_target_pairs={{0,2},{1,3},{2,0},{3,1},{4,6},{5,7},{6,4},{7,5},{8,10},{9,11},{10,... | collective-permute-start | bytes 147464 | tf_op jit(solution)/shard_map/ppermute | solution.py:410
  43.8 4.1 %collective-permute-start.15 = (f32[16,768]{1,0:T(8,128)S(1)}, f32[16,768]{1,0:T(8,128)S(1)}, u32[]{:S(2)}, u32[]{:S(2)}) collective-permute-start(f32[16,768]{1,0:T(8,128)S(1)} %get-tuple-element.66), channel_id=1, source_target_pairs={{0,3},{1,2},{2,1},{3,0},{4,7},{5,6},{6,5},{7,4},{8,11},{9,10},{10,... | collective-permute-start | bytes 147464 | tf_op jit(solution)/shard_map/ppermute | solution.py:410
  48.1 5.1 %collective-permute-start.17 = (f32[8,1792]{1,0:T(8,128)S(1)}, f32[8,1792]{1,0:T(8,128)S(1)}, u32[]{:S(2)}, u32[]{:S(2)}) collective-permute-start(f32[8,1792]{1,0:T(8,128)S(1)} %get-tuple-element.72), channel_id=1, source_target_pairs={{0,8},{4,12},{8,0},{12,4},{16,24},{20,28},{24,16},{28,20},{1,9},{5... | collective-permute-start | bytes 172040 | tf_op jit(solution)/shard_map/ppermute | solution.py:410
  49.9 5.8 %collective-permute-start.18 = (f32[8,1792]{1,0:T(8,128)S(1)}, f32[8,1792]{1,0:T(8,128)S(1)}, u32[]{:S(2)}, u32[]{:S(2)}) collective-permute-start(f32[8,1792]{1,0:T(8,128)S(1)} %get-tuple-element.73), channel_id=1, source_target_pairs={{0,16},{4,20},{8,24},{12,28},{16,0},{20,4},{24,8},{28,12},{1,17},{... | collective-permute-start | bytes 172040 | tf_op jit(solution)/shard_map/ppermute | solution.py:410
  51.9 6.0 %collective-permute-start.19 = (f32[8,1792]{1,0:T(8,128)S(1)}, f32[8,1792]{1,0:T(8,128)S(1)}, u32[]{:S(2)}, u32[]{:S(2)}) collective-permute-start(f32[8,1792]{1,0:T(8,128)S(1)} %get-tuple-element.74), channel_id=1, source_target_pairs={{0,24},{4,28},{8,16},{12,20},{16,8},{20,12},{24,0},{28,4},{1,25},{... | collective-permute-start | bytes 172040 | tf_op jit(solution)/shard_map/ppermute | solution.py:410
  57.9 6.6 %collective-permute-start.23 = (f32[8,1792]{1,0:T(8,128)S(1)}, f32[8,1792]{1,0:T(8,128)S(1)}, u32[]{:S(2)}, u32[]{:S(2)}) collective-permute-start(f32[8,1792]{1,0:T(8,128)S(1)} %replica_mean.1.refs_1_), channel_id=1, source_target_pairs={{0,24},{4,28},{8,16},{12,20},{16,8},{20,12},{24,0},{28,4},{1,25},{... | collective-permute-start | bytes 172040 | tf_op jit(solution)/shard_map/ppermute | solution.py:410
  60.4 5.8 %collective-permute-start.22 = (f32[8,1792]{1,0:T(8,128)S(1)}, f32[8,1792]{1,0:T(8,128)S(1)}, u32[]{:S(2)}, u32[]{:S(2)}) collective-permute-start(f32[8,1792]{1,0:T(8,128)S(1)} %replica_mean.1.refs_1_), channel_id=1, source_target_pairs={{0,16},{4,20},{8,24},{12,28},{16,0},{20,4},{24,8},{28,12},{1,17},{... | collective-permute-start | bytes 172040 | tf_op jit(solution)/shard_map/ppermute | solution.py:410
  60.8 5.4 %collective-permute-start.21 = (f32[8,1792]{1,0:T(8,128)S(1)}, f32[8,1792]{1,0:T(8,128)S(1)}, u32[]{:S(2)}, u32[]{:S(2)}) collective-permute-start(f32[8,1792]{1,0:T(8,128)S(1)} %replica_mean.1.refs_1_), channel_id=1, source_target_pairs={{0,8},{4,12},{8,0},{12,4},{16,24},{20,28},{24,16},{28,20},{1,9},{5... | collective-permute-start | bytes 172040 | tf_op jit(solution)/shard_map/ppermute | solution.py:410
  62.4 4.2 %collective-permute-start.20 = (f32[8,1792]{1,0:T(8,128)S(1)}, f32[8,1792]{1,0:T(8,128)S(1)}, u32[]{:S(2)}, u32[]{:S(2)}) collective-permute-start(f32[8,1792]{1,0:T(8,128)S(1)} %replica_mean.1.refs_1_), channel_id=1, source_target_pairs={{0,4},{4,0},{8,12},{12,8},{16,20},{20,16},{24,28},{28,24},{1,5},{5... | collective-permute-start | bytes 172040 | tf_op jit(solution)/shard_map/ppermute | solution.py:410
  66.6 5.5 %collective-permute-start.24 = (f32[3,8,1792]{2,1,0:T(8,128)S(1)}, f32[3,8,1792]{2,1,0:T(8,128)S(1)}, u32[]{:S(2)}, u32[]{:S(2)}) collective-permute-start(f32[3,8,1792]{2,1,0:T(8,128)S(1)} %get-tuple-element.77), channel_id=1, source_target_pairs={{0,4},{4,0},{8,12},{12,8},{16,20},{20,16},{24,28},{28,24},{1,5},{5... | collective-permute-start | bytes 516104 | tf_op jit(solution)/shard_map/ppermute | solution.py:410
  72.8 4.3 %collective-permute-start.27 = (f32[16,640]{1,0:T(8,128)S(1)}, f32[16,640]{1,0:T(8,128)S(1)}, u32[]{:S(2)}, u32[]{:S(2)}) collective-permute-start(f32[16,640]{1,0:T(8,128)S(1)} %get-tuple-element.83.refs_0_), channel_id=1, source_target_pairs={{0,3},{1,2},{2,1},{3,0},{4,7},{5,6},{6,5},{7,4},{8,11},{9,10},{10,... | collective-permute-start | bytes 122888 | tf_op jit(solution)/shard_map/ppermute | solution.py:410
  72.9 4.3 %collective-permute-start.26 = (f32[16,640]{1,0:T(8,128)S(1)}, f32[16,640]{1,0:T(8,128)S(1)}, u32[]{:S(2)}, u32[]{:S(2)}) collective-permute-start(f32[16,640]{1,0:T(8,128)S(1)} %get-tuple-element.83.refs_0_), channel_id=1, source_target_pairs={{0,2},{1,3},{2,0},{3,1},{4,6},{5,7},{6,4},{7,5},{8,10},{9,11},{10,... | collective-permute-start | bytes 122888 | tf_op jit(solution)/shard_map/ppermute | solution.py:410
  74.5 2.7 %collective-permute-start.25 = (f32[16,640]{1,0:T(8,128)S(1)}, f32[16,640]{1,0:T(8,128)S(1)}, u32[]{:S(2)}, u32[]{:S(2)}) collective-permute-start(f32[16,640]{1,0:T(8,128)S(1)} %get-tuple-element.83.refs_0_), channel_id=1, source_target_pairs={{0,1},{1,0},{2,3},{3,2},{4,5},{5,4},{6,7},{7,6},{8,9},{9,8},{10,11... | collective-permute-start | bytes 122888 | tf_op jit(solution)/shard_map/ppermute | solution.py:410

commit v16 on v15

--- a/solution.py
+++ b/solution.py
@@ -93,13 +93,16 @@
     up, down = (qu_in, pieces_up, total_up), (qd_in, pieces_down, total_down)
     firsts = [pltpu.make_async_copy(src, dst, q_sems.at[i]) for i, (src, dst) in enumerate(((qd, qd_in), (qu, qu_in)))]
     stages = []
-    for g, e, g_in, e_in, part, count in ((gd, ed, gd_in, ed_in, down, 3), (gu, eu, gu_in, eu_in, up, 2)):
+    for g, e, g_in, e_in, part, count in ((gd, ed, gd_in, ed_in, down, 6), (gu, eu, gu_in, eu_in, up, 2)):
         block = g_in.shape[0] // count
-        for i in range(count):
-            rows = pl.ds(i * block, block)
+        at = 0
+        for size in (1, 1, 2, 2) if count == 6 else (1, 1):
+            rows = slice(at * block, (at + size) * block)
+            window = pl.ds(at * block, size * block)
             n = len(stages)
-            copies = [pltpu.make_async_copy(src.at[0, rows, :], dst.at[rows, :], sems.at[n, k]) for k, (src, dst) in enumerate(((g, g_in), (e, e_in)))]
-            stages.append((copies, g_in, e_in, slice(i * block, (i + 1) * block), part))
+            copies = [pltpu.make_async_copy(src.at[0, window, :], dst.at[window, :], sems.at[n, k]) for k, (src, dst) in enumerate(((g, g_in), (e, e_in)))]
+            stages.append((copies, g_in, e_in, rows, part))
+            at += size
 
     def fetch(n):
         if n < len(stages):
@@ -108,15 +111,16 @@
 
     firsts[0].start()
     fetch(0)
+    fetch(1)
     firsts[1].start()
     for n, (first, (q, pieces, _)) in enumerate(zip(firsts, (down, up))):
         first.wait()
-        fetch(n + 1)
+        fetch(n + 2)
         split_rows(q, pieces)
     for n, (copies, g, e, rows, (_, pieces, total)) in enumerate(stages):
         for copy in copies:
             copy.wait()
-        fetch(n + 3)
+        fetch(n + 4)
         total[:, rows] = add_pieces(dot(pieces[...], g[rows, :], NT) + dot(pieces[...], e[rows, :], NT))
     split_shards(total_up, None, outs[:n_shards])
     split_replicas(total_down, stage, *outs[n_shards:])
@@ -191,17 +195,6 @@
 
 def strip_kernel(both, out):
     out[...] = both[:, :, : out.shape[2]]
-
-
-def stack_rest_kernel(own, *refs):
-    *pieces, out, rest = refs
-    stack_kernel(own, *pieces, out)
-    for j, piece in enumerate(pieces):
-        rest[j] = piece[...]
-
-
-def place_other_kernel(own, rest, out):
-    stack_kernel(own, *[rest.at[j] for j in range(rest.shape[0])], out)
 
 
 def add_columns_kernel(chunks, shard, out):
@@ -486,7 +479,7 @@
     *parts, keep, send = call(
         functools.partial(left_kernel, n_shards), [shard_rows_here] * n_shards + [replica_half] * 2, gu, eu, qu, gd, ed, qd,
         name="left", flops=2 * product, limit=61, in_specs=[pl.BlockSpec(memory_space=pltpu.HBM)] * 6,
-        scratch_shapes=buffers[0] + buffers[1] + [stage, pltpu.SemaphoreType.DMA((2,)), pltpu.SemaphoreType.DMA((5, 2))],
+        scratch_shapes=buffers[0] + buffers[1] + [stage, pltpu.SemaphoreType.DMA((2,)), pltpu.SemaphoreType.DMA((6, 2))],
     )
     got = swap(send, "dp", 1)
     parts = from_shards(parts)
@@ -511,10 +504,8 @@
         functools.partial(sum_shards_kernel, n_shards), [shard_rows_here, shaped(rank, rank)], *from_shards(parts), name="shard_sum"
     )
     pieces = mean_replicas(keep, got, shard)
-    early = swap(pieces[0], "dp", 1)
-    piece = pieces[0].shape
-    mine, rest = call(stack_rest_kernel, [shaped(half, *piece), shaped(half - 1, *piece)], *pieces, after=(early,), name="stack_z")
-    other = call(place_other_kernel, shaped(half, *piece), early, swap(rest, "dp", 1), name="other")
+    mine = call(stack_kernel, shaped(half, *pieces[0].shape), *pieces, name="stack_z")
+    other = swap(mine, "dp", 1)
     inv_up, inv_down, lhs_up, lhs_down = call(
         basis_kernel,
         [shaped(rank, rank)] * 2 + [shaped(rows, 4 * rank, dtype=BF16), shaped(ff, 4 * rank, dtype=BF16)],

time: 80.8 us -> 81.9 us (1.014)
  waiting for transfers between devices: 27.9 us -> 30.1 us
  starting transfers between devices: 31.7 us -> 30.4 us
    ppermute x28 -> x27, waiting for transfers between devices: 27.9 us -> 30.1 us  [swap(): return lax.ppermute(x, axis, pairs)]
    ppermute x28 -> x27, starting transfers between devices: 31.7 us -> 30.4 us  [swap(): return lax.ppermute(x, axis, pairs)]
    pallas_call x22 -> x21, Pallas kernels: 18.5 us -> 18.6 us  [call(): pl.pallas_call(lambda *refs: kernel(*refs[skip:]), out_shape=out_shape, i...]
  transfers between devices with their start and end apart: 28 -> 27, of which waited for: 17 -> 16; matrix products, arithmetic and copies ran while one was open for 0% -> 0% of each run, Pallas kernels for 8% -> 8%
where the time goes in v16:
time: 81.9 us; the launch traced here: 81.6 us
  starting transfers between devices  30.4 us (37%)
  waiting for transfers between devices  30.1 us (37%)
  Pallas kernels  18.6 us (23%)
  local copies, waits for them, and re-layouts  1.7 us (2%)
    ppermute x27, starting transfers between devices, swap(): return lax.ppermute(x, axis, pairs)  30.4 us
    ppermute x27, waiting for transfers between devices, swap(): return lax.ppermute(x, axis, pairs)  30.1 us
    pallas_call x21, Pallas kernels, call(): pl.pallas_call(lambda *refs: kernel(*refs[skip:]), out_shape=out_shape, i...  18.6 us
    unnamed x12, local copies, waits for them, and re-layouts  1.7 us
  transfers between devices with their start and end apart: 27, of which 16 were waited for; matrix products, arithmetic and copies ran while one was open for 0% of the time, Pallas kernels for 8%

profile of v16, /device:TPU:0, one launch (start us, length us, event | category | flops | bytes accessed | tf_op | source)
XLA Modules:
  0.0 81.6 jit_solution(8574888767074254668)
XLA Ops:
  0.6 6.3 %left.1 = (f32[16,512]{1,0:T(8,128)}, f32[16,512]{1,0:T(8,128)}, f32[16,512]{1,0:T(8,128)}, f32[16,512]{1,0:T(8,128)}, f32[4,8,1536]{2,1,0:T(8,128)}, /*index=5*/f32[4,8,1536]{2,1,0:T(8,128)}) custom-call(bf16[1,512,1536]{2,1,0:T(8,128)(2,1)} %refs_0_.4, bf16[1,512,1536]{2,1,0:T(8,128)(2,1)} %refs_1_.4, f32[64,1536]{1,0:T(8,128)} %bitcast.2, ...), custom_call_target="tpu_custom_call" | custom-call | flops 1610612736 | bytes 7340032 | tf_op jit(solution)/shard_map/left/pallas_call | solution.py:394
  7.0 0.0 copy-start.2
  7.0 3.0 %collective-permute-start.3 = (f32[4,8,1536]{2,1,0:T(8,128)}, f32[4,8,1536]{2,1,0:T(8,128)S(1)}, u32[]{:S(2)}, u32[]{:S(2)}) collective-permute-start(f32[4,8,1536]{2,1,0:T(8,128)} %get-tuple-element.52), channel_id=1, source_target_pairs={{0,4},{4,0},{8,12},{12,8},{16,20},{20,16},{24,28},{28,24},{1,5},{5... | collective-permute-start | bytes 589832 | tf_op jit(solution)/shard_map/ppermute | solution.py:403
  10.0 0.0 collective-permute-start
  10.0 1.5 %collective-permute-start.1 = (f32[16,512]{1,0:T(8,128)}, f32[16,512]{1,0:T(8,128)S(1)}, u32[]{:S(2)}, u32[]{:S(2)}) collective-permute-start(f32[16,512]{1,0:T(8,128)} %get-tuple-element.49), channel_id=1, source_target_pairs={{0,2},{1,3},{2,0},{3,1},{4,6},{5,7},{6,4},{7,5},{8,10},{9,11},{10,... | collective-permute-start | bytes 98312 | tf_op jit(solution)/shard_map/ppermute | solution.py:403
  11.5 0.4 collective-permute-start.2
  11.9 0.9 %copy-done.4 = f32[4,8,1536]{2,1,0:T(8,128)S(1)} copy-done((f32[4,8,1536]{2,1,0:T(8,128)S(1)}, f32[4,8,1536]{2,1,0:T(8,128)}, u32[]{:S(2)}) %copy-start.4) | copy-done | bytes 196632
  12.8 0.8 copy-done.5
  13.6 0.0 collective-permute-done.refs_1_
  13.6 0.6 collective-permute-done.1.refs_2_
  14.1 0.9 %collective-permute-done.2.refs_3_ = f32[16,512]{1,0:T(8,128)S(1)} collective-permute-done((f32[16,512]{1,0:T(8,128)}, f32[16,512]{1,0:T(8,128)S(1)}, u32[]{:S(2)}, u32[]{:S(2)}) %collective-permute-start.2) | collective-permute-done | bytes 32800 | tf_op jit(solution)/shard_map/ppermute | solution.py:403
  15.1 0.1 collective-permute-done.3.refs_2_
  15.2 1.9 %collective-permute-start.4 = (f32[2,8,1536]{2,1,0:T(8,128)S(1)}, f32[2,8,1536]{2,1,0:T(8,128)S(1)}, u32[]{:S(2)}, u32[]{:S(2)}) collective-permute-start(f32[2,8,1536]{2,1,0:T(8,128)S(1)} %get-tuple-element.54), channel_id=1, source_target_pairs={{0,8},{4,12},{8,0},{12,4},{16,24},{20,28},{24,16},{28,20},{1,9},{5... | collective-permute-start | bytes 294920 | tf_op jit(solution)/shard_map/ppermute | solution.py:403
  17.0 1.5 %collective-permute-start.5 = (f32[16,512]{1,0:T(8,128)S(1)}, f32[16,512]{1,0:T(8,128)S(1)}, u32[]{:S(2)}, u32[]{:S(2)}) collective-permute-start(f32[16,512]{1,0:T(8,128)S(1)} %shard_sum.2.refs_0_), channel_id=1, source_target_pairs={{0,4},{4,0},{8,12},{12,8},{16,20},{20,16},{24,28},{28,24},{1,5},{5... | collective-permute-start | bytes 98312 | tf_op jit(solution)/shard_map/ppermute | solution.py:403
  18.6 2.4 %collective-permute-done.5.refs_1_ = f32[16,512]{1,0:T(8,128)S(1)} collective-permute-done((f32[16,512]{1,0:T(8,128)S(1)}, f32[16,512]{1,0:T(8,128)S(1)}, u32[]{:S(2)}, u32[]{:S(2)}) %collective-permute-start.5) | collective-permute-done | bytes 32800 | tf_op jit(solution)/shard_map/ppermute | solution.py:403
  20.9 0.0 collective-permute-done.4.refs_1_
  21.0 2.7 %collective-permute-start.6 = (f32[2,8,2048]{2,1,0:T(8,128)S(1)}, f32[2,8,2048]{2,1,0:T(8,128)S(1)}, u32[]{:S(2)}, u32[]{:S(2)}) collective-permute-start(f32[2,8,2048]{2,1,0:T(8,128)S(1)} %half_sum.1.refs_0_), channel_id=1, source_target_pairs={{0,16},{4,20},{8,24},{12,28},{16,0},{20,4},{24,8},{28,12},{1,17},{... | collective-permute-start | bytes 393224 | tf_op jit(solution)/shard_map/ppermute | solution.py:403
  23.6 5.5 %collective-permute-done.6.refs_1_ = f32[2,8,2048]{2,1,0:T(8,128)S(1)} collective-permute-done((f32[2,8,2048]{2,1,0:T(8,128)S(1)}, f32[2,8,2048]{2,1,0:T(8,128)S(1)}, u32[]{:S(2)}, u32[]{:S(2)}) %collective-permute-start.6) | collective-permute-done | bytes 131104 | tf_op jit(solution)/shard_map/ppermute | solution.py:403
  29.2 0.5 collective-permute-start.8
  29.7 0.4 collective-permute-start.7
  30.1 4.3 %collective-permute-done.7.refs_0_ = f32[2,8,1536]{2,1,0:T(8,128)S(1)} collective-permute-done((f32[2,8,1536]{2,1,0:T(8,128)S(1)}, f32[2,8,1536]{2,1,0:T(8,128)S(1)}, u32[]{:S(2)}, u32[]{:S(2)}) %collective-permute-start.7) | collective-permute-done | bytes 98336 | tf_op jit(solution)/shard_map/ppermute | solution.py:403
  34.4 0.0 collective-permute-done.8.refs_2_
  34.4 0.7 collective-permute-start.9
  35.1 1.6 %collective-permute-start.11 = (f32[16,512]{1,0:T(8,128)S(1)}, f32[16,512]{1,0:T(8,128)S(1)}, u32[]{:S(2)}, u32[]{:S(2)}) collective-permute-start(f32[16,512]{1,0:T(8,128)S(1)} %get-tuple-element.56.refs_1_), channel_id=1, source_target_pairs={{0,2},{1,3},{2,0},{3,1},{4,6},{5,7},{6,4},{7,5},{8,10},{9,11},{10,... | collective-permute-start | bytes 98312 | tf_op jit(solution)/shard_map/ppermute | solution.py:403
  36.7 0.2 collective-permute-start.10
  36.9 1.7 %collective-permute-done.12.refs_4_ = f32[16,512]{1,0:T(8,128)S(1)} collective-permute-done((f32[16,512]{1,0:T(8,128)S(1)}, f32[16,512]{1,0:T(8,128)S(1)}, u32[]{:S(2)}, u32[]{:S(2)}) %collective-permute-start.12) | collective-permute-done | bytes 32800 | tf_op jit(solution)/shard_map/ppermute | solution.py:403
  38.6 0.5 collective-permute-done.11.refs_3_
  39.1 0.0 collective-permute-done.10.refs_2_
  39.1 0.0 collective-permute-done.9.refs_0_.refs_1_
  39.1 1.2 %right_up.1 = (f32[64,512]{1,0:T(8,128)S(1)}, f32[64,64]{1,0:T(8,128)S(1)}, f32[4,8,1536]{2,1,0:T(8,128)S(1)}, f32[4,8,1536]{2,1,0:T(8,128)S(1)}) custom-call(f32[2,8,1536]{2,1,0:T(8,128)S(1)} %collective-permute-done.9.refs_0_.refs_1_, f32[16,512]{1,0:T(8,128)S(1)} %get-tuple-element.56.refs_1_, f32[16,512]{1,0:T(8,128)S(1)} %collective-permute-done.10.refs_2_, ...), custom_call_target="tpu_custom_call" | custom-call | flops 805306368 | bytes 3817472 | tf_op jit(solution)/shard_map/right_up/pallas_call | solution.py:394
  40.3 1.7 %collective-permute-start.16 = (f32[4,8,1536]{2,1,0:T(8,128)S(1)}, f32[4,8,1536]{2,1,0:T(8,128)S(1)}, u32[]{:S(2)}, u32[]{:S(2)}) collective-permute-start(f32[4,8,1536]{2,1,0:T(8,128)S(1)} %get-tuple-element.67), channel_id=1, source_target_pairs={{0,4},{4,0},{8,12},{12,8},{16,20},{20,16},{24,28},{28,24},{1,5},{5... | collective-permute-start | bytes 589832 | tf_op jit(solution)/shard_map/ppermute | solution.py:403
  42.1 1.2 %right_down.1 = (f32[64,1536]{1,0:T(8,128)S(1)}, f32[16,768]{1,0:T(8,128)S(1)}, f32[16,768]{1,0:T(8,128)S(1)}, f32[16,768]{1,0:T(8,128)S(1)}, f32[16,768]{1,0:T(8,128)S(1)}) custom-call(f32[64,512]{1,0:T(8,128)S(1)} %get-tuple-element.57.refs_0_, f32[4,8,1536]{2,1,0:T(8,128)S(1)} %get-tuple-element.58.refs_1_, f32[4,8,1536]{2,1,0:T(8,128)S(1)} %other.1.refs_2_, ...), custom_call_target="tpu_custom_call" | custom-call | flops 805306368 | bytes 4128768 | tf_op jit(solution)/shard_map/right_down/pallas_call | solution.py:394
  43.2 0.0 collective-permute-start.13
  43.3 0.6 collective-permute-start.14
  43.9 1.2 %collective-permute-start.15 = (f32[16,768]{1,0:T(8,128)S(1)}, f32[16,768]{1,0:T(8,128)S(1)}, u32[]{:S(2)}, u32[]{:S(2)}) collective-permute-start(f32[16,768]{1,0:T(8,128)S(1)} %get-tuple-element.64), channel_id=1, source_target_pairs={{0,3},{1,2},{2,1},{3,0},{4,7},{5,6},{6,5},{7,4},{8,11},{9,10},{10,... | collective-permute-start | bytes 147464 | tf_op jit(solution)/shard_map/ppermute | solution.py:403
  45.2 0.0 collective-permute-done.13.refs_1_
  45.2 2.7 %collective-permute-done.14.refs_2_ = f32[16,768]{1,0:T(8,128)S(1)} collective-permute-done((f32[16,768]{1,0:T(8,128)S(1)}, f32[16,768]{1,0:T(8,128)S(1)}, u32[]{:S(2)}, u32[]{:S(2)}) %collective-permute-start.14) | collective-permute-done | bytes 49184 | tf_op jit(solution)/shard_map/ppermute | solution.py:403
  47.9 0.1 collective-permute-done.15.refs_3_
  48.1 0.1 shard_sum.3
  48.1 0.0 collective-permute-done.16.refs_1_
  48.2 1.9 %collective-permute-start.17 = (f32[8,1792]{1,0:T(8,128)S(1)}, f32[8,1792]{1,0:T(8,128)S(1)}, u32[]{:S(2)}, u32[]{:S(2)}) collective-permute-start(f32[8,1792]{1,0:T(8,128)S(1)} %get-tuple-element.70), channel_id=1, source_target_pairs={{0,8},{4,12},{8,0},{12,4},{16,24},{20,28},{24,16},{28,20},{1,9},{5... | collective-permute-start | bytes 172040 | tf_op jit(solution)/shard_map/ppermute | solution.py:403
  50.1 2.0 %collective-permute-start.18 = (f32[8,1792]{1,0:T(8,128)S(1)}, f32[8,1792]{1,0:T(8,128)S(1)}, u32[]{:S(2)}, u32[]{:S(2)}) collective-permute-start(f32[8,1792]{1,0:T(8,128)S(1)} %get-tuple-element.71), channel_id=1, source_target_pairs={{0,16},{4,20},{8,24},{12,28},{16,0},{20,4},{24,8},{28,12},{1,17},{... | collective-permute-start | bytes 172040 | tf_op jit(solution)/shard_map/ppermute | solution.py:403
  52.0 1.3 %collective-permute-start.19 = (f32[8,1792]{1,0:T(8,128)S(1)}, f32[8,1792]{1,0:T(8,128)S(1)}, u32[]{:S(2)}, u32[]{:S(2)}) collective-permute-start(f32[8,1792]{1,0:T(8,128)S(1)} %get-tuple-element.72), channel_id=1, source_target_pairs={{0,24},{4,28},{8,16},{12,20},{16,8},{20,12},{24,0},{28,4},{1,25},{... | collective-permute-start | bytes 172040 | tf_op jit(solution)/shard_map/ppermute | solution.py:403
  53.3 2.5 %collective-permute-done.18.refs_2_ = f32[8,1792]{1,0:T(8,128)S(1)} collective-permute-done((f32[8,1792]{1,0:T(8,128)S(1)}, f32[8,1792]{1,0:T(8,128)S(1)}, u32[]{:S(2)}, u32[]{:S(2)}) %collective-permute-start.18) | collective-permute-done | bytes 57376 | tf_op jit(solution)/shard_map/ppermute | solution.py:403
  55.9 2.2 %collective-permute-done.19.refs_3_ = f32[8,1792]{1,0:T(8,128)S(1)} collective-permute-done((f32[8,1792]{1,0:T(8,128)S(1)}, f32[8,1792]{1,0:T(8,128)S(1)}, u32[]{:S(2)}, u32[]{:S(2)}) %collective-permute-start.19) | collective-permute-done | bytes 57376 | tf_op jit(solution)/shard_map/ppermute | solution.py:403
  58.1 2.5 %collective-permute-start.22 = (f32[8,1792]{1,0:T(8,128)S(1)}, f32[8,1792]{1,0:T(8,128)S(1)}, u32[]{:S(2)}, u32[]{:S(2)}) collective-permute-start(f32[8,1792]{1,0:T(8,128)S(1)} %replica_mean.1.refs_0_), channel_id=1, source_target_pairs={{0,24},{4,28},{8,16},{12,20},{16,8},{20,12},{24,0},{28,4},{1,25},{... | collective-permute-start | bytes 172040 | tf_op jit(solution)/shard_map/ppermute | solution.py:403
  60.5 0.4 collective-permute-start.21
  60.9 1.6 %collective-permute-start.20 = (f32[8,1792]{1,0:T(8,128)S(1)}, f32[8,1792]{1,0:T(8,128)S(1)}, u32[]{:S(2)}, u32[]{:S(2)}) collective-permute-start(f32[8,1792]{1,0:T(8,128)S(1)} %replica_mean.1.refs_0_), channel_id=1, source_target_pairs={{0,8},{4,12},{8,0},{12,4},{16,24},{20,28},{24,16},{28,20},{1,9},{5... | collective-permute-start | bytes 172040 | tf_op jit(solution)/shard_map/ppermute | solution.py:403
  62.5 2.2 %collective-permute-done.22.refs_3_ = f32[8,1792]{1,0:T(8,128)S(1)} collective-permute-done((f32[8,1792]{1,0:T(8,128)S(1)}, f32[8,1792]{1,0:T(8,128)S(1)}, u32[]{:S(2)}, u32[]{:S(2)}) %collective-permute-start.22) | collective-permute-done | bytes 57376 | tf_op jit(solution)/shard_map/ppermute | solution.py:403
  64.7 1.7 %collective-permute-done.21.refs_2_ = f32[8,1792]{1,0:T(8,128)S(1)} collective-permute-done((f32[8,1792]{1,0:T(8,128)S(1)}, f32[8,1792]{1,0:T(8,128)S(1)}, u32[]{:S(2)}, u32[]{:S(2)}) %collective-permute-start.21) | collective-permute-done | bytes 57376 | tf_op jit(solution)/shard_map/ppermute | solution.py:403
  66.4 0.0 collective-permute-done.20.refs_1_
  66.4 0.8 %collective-permute-start.23 = (f32[4,8,1792]{2,1,0:T(8,128)S(1)}, f32[4,8,1792]{2,1,0:T(8,128)S(1)}, u32[]{:S(2)}, u32[]{:S(2)}) collective-permute-start(f32[4,8,1792]{2,1,0:T(8,128)S(1)} %stack_z.1.refs_8_.refs_0_), channel_id=1, source_target_pairs={{0,4},{4,0},{8,12},{12,8},{16,20},{20,16},{24,28},{28,24},{1,5},{5... | collective-permute-start | bytes 688136 | tf_op jit(solution)/shard_map/ppermute | solution.py:403
  67.3 3.2 %basis.1 = (f32[64,64]{1,0:T(8,128)S(1)}, f32[64,64]{1,0:T(8,128)S(1)}, bf16[512,256]{1,0:T(8,128)(2,1)S(1)}, bf16[1536,256]{1,0:T(8,128)(2,1)S(1)}) custom-call(f32[64,512]{1,0:T(8,128)S(1)} %get-tuple-element.57.refs_0_, f32[64,1536]{1,0:T(8,128)S(1)} %get-tuple-element.59.refs_1_, f32[64,64]{1,0:T(8,128)S(1)} %get-tuple-element.60.refs_2_, ...), custom_call_target="tpu_custom_call" | custom-call | bytes 8159232 | tf_op jit(solution)/shard_map/basis/pallas_call | solution.py:394
  70.4 2.7 %collective-permute-done.23.refs_1_ = f32[4,8,1792]{2,1,0:T(8,128)S(1)} collective-permute-done((f32[4,8,1792]{2,1,0:T(8,128)S(1)}, f32[4,8,1792]{2,1,0:T(8,128)S(1)}, u32[]{:S(2)}, u32[]{:S(2)}) %collective-permute-start.23) | collective-permute-done | bytes 229408 | tf_op jit(solution)/shard_map/ppermute | solution.py:403
  73.1 0.7 factor_up.1
  73.8 0.5 collective-permute-start.26
  74.2 1.6 %collective-permute-start.25 = (f32[16,640]{1,0:T(8,128)S(1)}, f32[16,640]{1,0:T(8,128)S(1)}, u32[]{:S(2)}, u32[]{:S(2)}) collective-permute-start(f32[16,640]{1,0:T(8,128)S(1)} %get-tuple-element.79.refs_0_), channel_id=1, source_target_pairs={{0,2},{1,3},{2,0},{3,1},{4,6},{5,7},{6,4},{7,5},{8,10},{9,11},{10,... | collective-permute-start | bytes 122888 | tf_op jit(solution)/shard_map/ppermute | solution.py:403
  75.8 0.0 collective-permute-start.24
  75.8 2.3 %error_up.1 = (bf16[1,512,1536]{2,1,0:T(8,128)(2,1)}, f32[512,1536]{1,0:T(8,128)S(1)}) custom-call(bf16[1,512,1536]{2,1,0:T(8,128)(2,1)S(1)} %copy-done.2, bf16[1,512,1536]{2,1,0:T(8,128)(2,1)S(1)} %copy-done.3, bf16[512,256]{1,0:T(8,128)(2,1)S(1)} %get-tuple-element.73.refs_2_, bf16[256,1536]{1,0:T(8,128)(2,1)S(1)} %get-tuple-element.75.refs_3_), custom_call_target="tpu_custom_call" | custom-call | flops 402653184 | bytes 8912896 | tf_op jit(solution)/shard_map/error_up/pallas_call | solution.py:394
  78.2 0.0 collective-permute-done.26.refs_3_
  78.2 0.1 collective-permute-done.25.refs_2_
  78.2 0.0 collective-permute-done.24.refs_1_
  78.2 0.4 factor_down.1
  78.7 3.0 %last.1 = (bf16[1,1536,512]{2,1,0:T(8,128)(2,1)}, bf16[512,1536]{1,0:T(8,128)(2,1)}, bf16[1536,512]{1,0:T(8,128)(2,1)}) custom-call(bf16[1,1536,512]{2,1,0:T(8,128)(2,1)S(1)} %copy-done, bf16[1,1536,512]{2,1,0:T(8,128)(2,1)S(1)} %copy-done.1, f32[512,1536]{1,0:T(8,128)S(1)} %get-tuple-element.77.refs_5_.refs_2_, ...), custom_call_target="tpu_custom_call" | custom-call | flops 805306368 | bytes 12062720 | tf_op jit(solution)/shard_map/last/pallas_call | solution.py:394
  (23 shorter events, 0.3 us)
Async XLA Ops:
  0.6 38.5 %copy-start.3 = (bf16[1,512,1536]{2,1,0:T(8,128)(2,1)S(1)}, bf16[1,512,1536]{2,1,0:T(8,128)(2,1)}, u32[]{:S(2)}) copy-start(bf16[1,512,1536]{2,1,0:T(8,128)(2,1)} %refs_1_.4) | copy-start | bytes 4718596
  7.0 32.1 %copy-start.2 = (bf16[1,512,1536]{2,1,0:T(8,128)(2,1)S(1)}, bf16[1,512,1536]{2,1,0:T(8,128)(2,1)}, u32[]{:S(2)}) copy-start(bf16[1,512,1536]{2,1,0:T(8,128)(2,1)} %refs_0_.4) | copy-start | bytes 4718596
  7.0 8.1 %collective-permute-start.3 = (f32[4,8,1536]{2,1,0:T(8,128)}, f32[4,8,1536]{2,1,0:T(8,128)S(1)}, u32[]{:S(2)}, u32[]{:S(2)}) collective-permute-start(f32[4,8,1536]{2,1,0:T(8,128)} %get-tuple-element.52), channel_id=1, source_target_pairs={{0,4},{4,0},{8,12},{12,8},{16,20},{20,16},{24,28},{28,24},{1,5},{5... | collective-permute-start | bytes 589832 | tf_op jit(solution)/shard_map/ppermute | solution.py:403
  10.0 3.6 %collective-permute-start = (f32[16,512]{1,0:T(8,128)}, f32[16,512]{1,0:T(8,128)S(1)}, u32[]{:S(2)}, u32[]{:S(2)}) collective-permute-start(f32[16,512]{1,0:T(8,128)} %get-tuple-element.48), channel_id=1, source_target_pairs={{0,1},{1,0},{2,3},{3,2},{4,5},{5,4},{6,7},{7,6},{8,9},{9,8},{10,11... | collective-permute-start | bytes 98312 | tf_op jit(solution)/shard_map/ppermute | solution.py:403
  10.0 4.1 %collective-permute-start.1 = (f32[16,512]{1,0:T(8,128)}, f32[16,512]{1,0:T(8,128)S(1)}, u32[]{:S(2)}, u32[]{:S(2)}) collective-permute-start(f32[16,512]{1,0:T(8,128)} %get-tuple-element.49), channel_id=1, source_target_pairs={{0,2},{1,3},{2,0},{3,1},{4,6},{5,7},{6,4},{7,5},{8,10},{9,11},{10,... | collective-permute-start | bytes 98312 | tf_op jit(solution)/shard_map/ppermute | solution.py:403
  11.5 3.6 %collective-permute-start.2 = (f32[16,512]{1,0:T(8,128)}, f32[16,512]{1,0:T(8,128)S(1)}, u32[]{:S(2)}, u32[]{:S(2)}) collective-permute-start(f32[16,512]{1,0:T(8,128)} %get-tuple-element.50), channel_id=1, source_target_pairs={{0,3},{1,2},{2,1},{3,0},{4,7},{5,6},{6,5},{7,4},{8,11},{9,10},{10,... | collective-permute-start | bytes 98312 | tf_op jit(solution)/shard_map/ppermute | solution.py:403
  11.9 0.9 %copy-start.4 = (f32[4,8,1536]{2,1,0:T(8,128)S(1)}, f32[4,8,1536]{2,1,0:T(8,128)}, u32[]{:S(2)}) copy-start(f32[4,8,1536]{2,1,0:T(8,128)} %get-tuple-element.46.refs_1_) | copy-start | bytes 589828
  12.8 0.8 copy-start.5
  15.2 5.8 %collective-permute-start.4 = (f32[2,8,1536]{2,1,0:T(8,128)S(1)}, f32[2,8,1536]{2,1,0:T(8,128)S(1)}, u32[]{:S(2)}, u32[]{:S(2)}) collective-permute-start(f32[2,8,1536]{2,1,0:T(8,128)S(1)} %get-tuple-element.54), channel_id=1, source_target_pairs={{0,8},{4,12},{8,0},{12,4},{16,24},{20,28},{24,16},{28,20},{1,9},{5... | collective-permute-start | bytes 294920 | tf_op jit(solution)/shard_map/ppermute | solution.py:403
  17.0 3.9 %collective-permute-start.5 = (f32[16,512]{1,0:T(8,128)S(1)}, f32[16,512]{1,0:T(8,128)S(1)}, u32[]{:S(2)}, u32[]{:S(2)}) collective-permute-start(f32[16,512]{1,0:T(8,128)S(1)} %shard_sum.2.refs_0_), channel_id=1, source_target_pairs={{0,4},{4,0},{8,12},{12,8},{16,20},{20,16},{24,28},{28,24},{1,5},{5... | collective-permute-start | bytes 98312 | tf_op jit(solution)/shard_map/ppermute | solution.py:403
  21.0 8.2 %collective-permute-start.6 = (f32[2,8,2048]{2,1,0:T(8,128)S(1)}, f32[2,8,2048]{2,1,0:T(8,128)S(1)}, u32[]{:S(2)}, u32[]{:S(2)}) collective-permute-start(f32[2,8,2048]{2,1,0:T(8,128)S(1)} %half_sum.1.refs_0_), channel_id=1, source_target_pairs={{0,16},{4,20},{8,24},{12,28},{16,0},{20,4},{24,8},{28,12},{1,17},{... | collective-permute-start | bytes 393224 | tf_op jit(solution)/shard_map/ppermute | solution.py:403
  29.2 5.2 %collective-permute-start.8 = (f32[2,8,2048]{2,1,0:T(8,128)S(1)}, f32[2,8,2048]{2,1,0:T(8,128)S(1)}, u32[]{:S(2)}, u32[]{:S(2)}) collective-permute-start(f32[2,8,2048]{2,1,0:T(8,128)S(1)} %mean.1.refs_0_.refs_1_), channel_id=1, source_target_pairs={{0,8},{4,12},{8,0},{12,4},{16,24},{20,28},{24,16},{28,20},{1,9},{5... | collective-permute-start | bytes 393224 | tf_op jit(solution)/shard_map/ppermute | solution.py:403
  29.7 4.7 %collective-permute-start.7 = (f32[2,8,1536]{2,1,0:T(8,128)S(1)}, f32[2,8,1536]{2,1,0:T(8,128)S(1)}, u32[]{:S(2)}, u32[]{:S(2)}) collective-permute-start(f32[2,8,1536]{2,1,0:T(8,128)S(1)} %strip.1), channel_id=1, source_target_pairs={{0,4},{4,0},{8,12},{12,8},{16,20},{20,16},{24,28},{28,24},{1,5},{5... | collective-permute-start | bytes 294920 | tf_op jit(solution)/shard_map/ppermute | solution.py:403
  34.4 4.7 %collective-permute-start.9 = (f32[2,8,1536]{2,1,0:T(8,128)S(1)}, f32[2,8,1536]{2,1,0:T(8,128)S(1)}, u32[]{:S(2)}, u32[]{:S(2)}) collective-permute-start(f32[2,8,1536]{2,1,0:T(8,128)S(1)} %get-tuple-element.55), channel_id=1, source_target_pairs={{0,4},{4,0},{8,12},{12,8},{16,20},{20,16},{24,28},{28,24},{1,5},{5... | collective-permute-start | bytes 294920 | tf_op jit(solution)/shard_map/ppermute | solution.py:403
  35.1 7.0 %copy-start = (bf16[1,1536,512]{2,1,0:T(8,128)(2,1)S(1)}, bf16[1,1536,512]{2,1,0:T(8,128)(2,1)}, u32[]{:S(2)}) copy-start(bf16[1,1536,512]{2,1,0:T(8,128)(2,1)} %refs_0_.5) | copy-start | bytes 4718596
  35.1 7.0 %copy-start.1 = (bf16[1,1536,512]{2,1,0:T(8,128)(2,1)S(1)}, bf16[1,1536,512]{2,1,0:T(8,128)(2,1)}, u32[]{:S(2)}) copy-start(bf16[1,1536,512]{2,1,0:T(8,128)(2,1)} %refs_1_.5) | copy-start | bytes 4718596
  35.1 3.5 %collective-permute-start.12 = (f32[16,512]{1,0:T(8,128)S(1)}, f32[16,512]{1,0:T(8,128)S(1)}, u32[]{:S(2)}, u32[]{:S(2)}) collective-permute-start(f32[16,512]{1,0:T(8,128)S(1)} %get-tuple-element.56.refs_1_), channel_id=1, source_target_pairs={{0,3},{1,2},{2,1},{3,0},{4,7},{5,6},{6,5},{7,4},{8,11},{9,10},{10,... | collective-permute-start | bytes 98312 | tf_op jit(solution)/shard_map/ppermute | solution.py:403
  35.1 4.0 %collective-permute-start.11 = (f32[16,512]{1,0:T(8,128)S(1)}, f32[16,512]{1,0:T(8,128)S(1)}, u32[]{:S(2)}, u32[]{:S(2)}) collective-permute-start(f32[16,512]{1,0:T(8,128)S(1)} %get-tuple-element.56.refs_1_), channel_id=1, source_target_pairs={{0,2},{1,3},{2,0},{3,1},{4,6},{5,7},{6,4},{7,5},{8,10},{9,11},{10,... | collective-permute-start | bytes 98312 | tf_op jit(solution)/shard_map/ppermute | solution.py:403
  36.7 2.4 %collective-permute-start.10 = (f32[16,512]{1,0:T(8,128)S(1)}, f32[16,512]{1,0:T(8,128)S(1)}, u32[]{:S(2)}, u32[]{:S(2)}) collective-permute-start(f32[16,512]{1,0:T(8,128)S(1)} %get-tuple-element.56.refs_1_), channel_id=1, source_target_pairs={{0,1},{1,0},{2,3},{3,2},{4,5},{5,4},{6,7},{7,6},{8,9},{9,8},{10,11... | collective-permute-start | bytes 98312 | tf_op jit(solution)/shard_map/ppermute | solution.py:403
  40.3 7.8 %collective-permute-start.16 = (f32[4,8,1536]{2,1,0:T(8,128)S(1)}, f32[4,8,1536]{2,1,0:T(8,128)S(1)}, u32[]{:S(2)}, u32[]{:S(2)}) collective-permute-start(f32[4,8,1536]{2,1,0:T(8,128)S(1)} %get-tuple-element.67), channel_id=1, source_target_pairs={{0,4},{4,0},{8,12},{12,8},{16,20},{20,16},{24,28},{28,24},{1,5},{5... | collective-permute-start | bytes 589832 | tf_op jit(solution)/shard_map/ppermute | solution.py:403
  43.2 1.9 %collective-permute-start.13 = (f32[16,768]{1,0:T(8,128)S(1)}, f32[16,768]{1,0:T(8,128)S(1)}, u32[]{:S(2)}, u32[]{:S(2)}) collective-permute-start(f32[16,768]{1,0:T(8,128)S(1)} %get-tuple-element.62), channel_id=1, source_target_pairs={{0,1},{1,0},{2,3},{3,2},{4,5},{5,4},{6,7},{7,6},{8,9},{9,8},{10,11... | collective-permute-start | bytes 147464 | tf_op jit(solution)/shard_map/ppermute | solution.py:403
  43.3 4.6 %collective-permute-start.14 = (f32[16,768]{1,0:T(8,128)S(1)}, f32[16,768]{1,0:T(8,128)S(1)}, u32[]{:S(2)}, u32[]{:S(2)}) collective-permute-start(f32[16,768]{1,0:T(8,128)S(1)} %get-tuple-element.63), channel_id=1, source_target_pairs={{0,2},{1,3},{2,0},{3,1},{4,6},{5,7},{6,4},{7,5},{8,10},{9,11},{10,... | collective-permute-start | bytes 147464 | tf_op jit(solution)/shard_map/ppermute | solution.py:403
  43.9 4.1 %collective-permute-start.15 = (f32[16,768]{1,0:T(8,128)S(1)}, f32[16,768]{1,0:T(8,128)S(1)}, u32[]{:S(2)}, u32[]{:S(2)}) collective-permute-start(f32[16,768]{1,0:T(8,128)S(1)} %get-tuple-element.64), channel_id=1, source_target_pairs={{0,3},{1,2},{2,1},{3,0},{4,7},{5,6},{6,5},{7,4},{8,11},{9,10},{10,... | collective-permute-start | bytes 147464 | tf_op jit(solution)/shard_map/ppermute | solution.py:403
  48.2 5.1 %collective-permute-start.17 = (f32[8,1792]{1,0:T(8,128)S(1)}, f32[8,1792]{1,0:T(8,128)S(1)}, u32[]{:S(2)}, u32[]{:S(2)}) collective-permute-start(f32[8,1792]{1,0:T(8,128)S(1)} %get-tuple-element.70), channel_id=1, source_target_pairs={{0,8},{4,12},{8,0},{12,4},{16,24},{20,28},{24,16},{28,20},{1,9},{5... | collective-permute-start | bytes 172040 | tf_op jit(solution)/shard_map/ppermute | solution.py:403
  50.1 5.8 %collective-permute-start.18 = (f32[8,1792]{1,0:T(8,128)S(1)}, f32[8,1792]{1,0:T(8,128)S(1)}, u32[]{:S(2)}, u32[]{:S(2)}) collective-permute-start(f32[8,1792]{1,0:T(8,128)S(1)} %get-tuple-element.71), channel_id=1, source_target_pairs={{0,16},{4,20},{8,24},{12,28},{16,0},{20,4},{24,8},{28,12},{1,17},{... | collective-permute-start | bytes 172040 | tf_op jit(solution)/shard_map/ppermute | solution.py:403
  52.0 6.0 %collective-permute-start.19 = (f32[8,1792]{1,0:T(8,128)S(1)}, f32[8,1792]{1,0:T(8,128)S(1)}, u32[]{:S(2)}, u32[]{:S(2)}) collective-permute-start(f32[8,1792]{1,0:T(8,128)S(1)} %get-tuple-element.72), channel_id=1, source_target_pairs={{0,24},{4,28},{8,16},{12,20},{16,8},{20,12},{24,0},{28,4},{1,25},{... | collective-permute-start | bytes 172040 | tf_op jit(solution)/shard_map/ppermute | solution.py:403
  58.1 6.6 %collective-permute-start.22 = (f32[8,1792]{1,0:T(8,128)S(1)}, f32[8,1792]{1,0:T(8,128)S(1)}, u32[]{:S(2)}, u32[]{:S(2)}) collective-permute-start(f32[8,1792]{1,0:T(8,128)S(1)} %replica_mean.1.refs_0_), channel_id=1, source_target_pairs={{0,24},{4,28},{8,16},{12,20},{16,8},{20,12},{24,0},{28,4},{1,25},{... | collective-permute-start | bytes 172040 | tf_op jit(solution)/shard_map/ppermute | solution.py:403
  60.5 5.8 %collective-permute-start.21 = (f32[8,1792]{1,0:T(8,128)S(1)}, f32[8,1792]{1,0:T(8,128)S(1)}, u32[]{:S(2)}, u32[]{:S(2)}) collective-permute-start(f32[8,1792]{1,0:T(8,128)S(1)} %replica_mean.1.refs_0_), channel_id=1, source_target_pairs={{0,16},{4,20},{8,24},{12,28},{16,0},{20,4},{24,8},{28,12},{1,17},{... | collective-permute-start | bytes 172040 | tf_op jit(solution)/shard_map/ppermute | solution.py:403
  60.9 5.5 %collective-permute-start.20 = (f32[8,1792]{1,0:T(8,128)S(1)}, f32[8,1792]{1,0:T(8,128)S(1)}, u32[]{:S(2)}, u32[]{:S(2)}) collective-permute-start(f32[8,1792]{1,0:T(8,128)S(1)} %replica_mean.1.refs_0_), channel_id=1, source_target_pairs={{0,8},{4,12},{8,0},{12,4},{16,24},{20,28},{24,16},{28,20},{1,9},{5... | collective-permute-start | bytes 172040 | tf_op jit(solution)/shard_map/ppermute | solution.py:403
  66.4 6.7 %collective-permute-start.23 = (f32[4,8,1792]{2,1,0:T(8,128)S(1)}, f32[4,8,1792]{2,1,0:T(8,128)S(1)}, u32[]{:S(2)}, u32[]{:S(2)}) collective-permute-start(f32[4,8,1792]{2,1,0:T(8,128)S(1)} %stack_z.1.refs_8_.refs_0_), channel_id=1, source_target_pairs={{0,4},{4,0},{8,12},{12,8},{16,20},{20,16},{24,28},{28,24},{1,5},{5... | collective-permute-start | bytes 688136 | tf_op jit(solution)/shard_map/ppermute | solution.py:403
  73.8 4.4 %collective-permute-start.26 = (f32[16,640]{1,0:T(8,128)S(1)}, f32[16,640]{1,0:T(8,128)S(1)}, u32[]{:S(2)}, u32[]{:S(2)}) collective-permute-start(f32[16,640]{1,0:T(8,128)S(1)} %get-tuple-element.79.refs_0_), channel_id=1, source_target_pairs={{0,3},{1,2},{2,1},{3,0},{4,7},{5,6},{6,5},{7,4},{8,11},{9,10},{10,... | collective-permute-start | bytes 122888 | tf_op jit(solution)/shard_map/ppermute | solution.py:403
  74.2 4.0 %collective-permute-start.25 = (f32[16,640]{1,0:T(8,128)S(1)}, f32[16,640]{1,0:T(8,128)S(1)}, u32[]{:S(2)}, u32[]{:S(2)}) collective-permute-start(f32[16,640]{1,0:T(8,128)S(1)} %get-tuple-element.79.refs_0_), channel_id=1, source_target_pairs={{0,2},{1,3},{2,0},{3,1},{4,6},{5,7},{6,4},{7,5},{8,10},{9,11},{10,... | collective-permute-start | bytes 122888 | tf_op jit(solution)/shard_map/ppermute | solution.py:403
  75.8 2.5 %collective-permute-start.24 = (f32[16,640]{1,0:T(8,128)S(1)}, f32[16,640]{1,0:T(8,128)S(1)}, u32[]{:S(2)}, u32[]{:S(2)}) collective-permute-start(f32[16,640]{1,0:T(8,128)S(1)} %get-tuple-element.79.refs_0_), channel_id=1, source_target_pairs={{0,1},{1,0},{2,3},{3,2},{4,5},{5,4},{6,7},{7,6},{8,9},{9,8},{10,11... | collective-permute-start | bytes 122888 | tf_op jit(solution)/shard_map/ppermute | solution.py:403

commit v17 on v14

--- a/solution.py
+++ b/solution.py
@@ -89,7 +89,8 @@
 
 
 def left_kernel(n_shards, gu, eu, qu, gd, ed, qd, *refs):
-    *outs, gu_in, eu_in, qu_in, pieces_up, total_up, gd_in, ed_in, qd_in, pieces_down, total_down, stage, q_sems, sems = refs
+    *outs, gu_in, eu_in, qu_in, pieces_up, total_up, gd_in, ed_in, qd_in, pieces_down, total_down, stage, kept, sent, q_sems, sems, out_sems = refs
+    halves = [pltpu.make_async_copy(src, dst, out_sems.at[i]) for i, (src, dst) in enumerate(((sent, outs[-1]), (kept, outs[-2])))]
     up, down = (qu_in, pieces_up, total_up), (qd_in, pieces_down, total_down)
     firsts = [pltpu.make_async_copy(src, dst, q_sems.at[i]) for i, (src, dst) in enumerate(((qd, qd_in), (qu, qu_in)))]
     stages = []
@@ -118,8 +119,13 @@
             copy.wait()
         fetch(n + 3)
         total[:, rows] = add_pieces(dot(pieces[...], g[rows, :], NT) + dot(pieces[...], e[rows, :], NT))
+        if n == 2:
+            split_replicas(total_down, stage, kept, sent)
+            for half in halves:
+                half.start()
     split_shards(total_up, None, outs[:n_shards])
-    split_replicas(total_down, stage, *outs[n_shards:])
+    for half in halves:
+        half.wait()
 
 
 def fetch_kernel(*refs):
@@ -376,6 +382,7 @@
 
 VMEM = pl.BlockSpec(memory_space=pltpu.VMEM)
 ANY = pl.BlockSpec(memory_space=pl.ANY)
+HBM = pl.BlockSpec(memory_space=pltpu.HBM)
 
 
 def call(kernel, out_shape, *args, after=(), in_specs=None, flops=0, limit=12, name=None, **more):
@@ -384,7 +391,7 @@
     skip = len(after)
     return pl.pallas_call(
         lambda *refs: kernel(*refs[skip:]), out_shape=out_shape, in_specs=[ANY] * skip + (in_specs or [VMEM] * len(args)),
-        compiler_params=pltpu.CompilerParams(vmem_limit_bytes=limit * MIB),
+        compiler_params=pltpu.CompilerParams(vmem_limit_bytes=int(limit * MIB)),
         cost_estimate=pl.CostEstimate(flops=flops, bytes_accessed=size, transcendentals=0), name=name, **more,
     )(*after, *args)
 
@@ -464,8 +471,9 @@
     ]
     *parts, keep, send = call(
         functools.partial(left_kernel, n_shards), [shard_rows_here] * n_shards + [replica_half] * 2, gu, eu, qu, gd, ed, qd,
-        name="left", flops=2 * product, limit=61, in_specs=[pl.BlockSpec(memory_space=pltpu.HBM)] * 6,
-        scratch_shapes=buffers[0] + buffers[1] + [stage, pltpu.SemaphoreType.DMA((2,)), pltpu.SemaphoreType.DMA((5, 2))],
+        name="left", flops=2 * product, limit=53.75, in_specs=[HBM] * 6, out_specs=[VMEM] * n_shards + [HBM] * 2,
+        scratch_shapes=buffers[0] + buffers[1] + [stage] + [pltpu.VMEM(replica_half.shape, F32)] * 2
+        + [pltpu.SemaphoreType.DMA((2,)), pltpu.SemaphoreType.DMA((5, 2)), pltpu.SemaphoreType.DMA((2,))],
     )
     got = swap(send, "dp", 1)
     parts = from_shards(parts)

time: 80.1 us -> 79.2 us (0.989)
  waiting for transfers between devices: 29.7 us -> 30.6 us
    ppermute x26, waiting for transfers between devices: 29.7 us -> 30.6 us  [swap(): return lax.ppermute(x, axis, pairs)]
    unnamed x12 -> x10, local copies, waits for them, and re-layouts: 1.7 us -> 0.94 us
  transfers between devices with their start and end apart: 26 -> 26, of which waited for: 18 -> 18; matrix products, arithmetic and copies ran while one was open for 0% -> 0% of each run, Pallas kernels for 8% -> 9%
where the time goes in v17:
time: 79.2 us; the launch traced here: 79 us
  waiting for transfers between devices  30.6 us (39%)
  starting transfers between devices  29 us (37%)
  Pallas kernels  17.7 us (22%)
  local copies, waits for them, and re-layouts  0.94 us (1%)
    ppermute x26, waiting for transfers between devices, swap(): return lax.ppermute(x, axis, pairs)  30.6 us
    ppermute x26, starting transfers between devices, swap(): return lax.ppermute(x, axis, pairs)  29 us
    pallas_call x19, Pallas kernels, call(): pl.pallas_call(lambda *refs: kernel(*refs[skip:]), out_shape=out_shape, i...  17.7 us
  transfers between devices with their start and end apart: 26, of which 18 were waited for; matrix products, arithmetic and copies ran while one was open for 0% of the time, Pallas kernels for 9%

profile of v17, /device:TPU:0, one launch (start us, length us, event | category | flops | bytes accessed | tf_op | source)
XLA Modules:
  0.0 79.0 jit_solution(13517062399406561577)
XLA Ops:
  0.6 0.0 copy-start.3
  0.6 5.5 %left.1 = (f32[16,512]{1,0:T(8,128)S(1)}, f32[16,512]{1,0:T(8,128)S(1)}, f32[16,512]{1,0:T(8,128)S(1)}, f32[16,512]{1,0:T(8,128)S(1)}, f32[4,8,1536]{2,1,0:T(8,128)}, /*index=5*/f32[4,8,1536]{2,1,0:T(8,128)}) custom-call(bf16[1,512,1536]{2,1,0:T(8,128)(2,1)} %refs_0_.4, bf16[1,512,1536]{2,1,0:T(8,128)(2,1)} %refs_1_.4, f32[64,1536]{1,0:T(8,128)} %bitcast.2, ...), custom_call_target="tpu_custom_call" | custom-call | flops 1610612736 | bytes 7340032 | tf_op jit(solution)/shard_map/left/pallas_call | solution.py:392
  6.2 0.0 copy-start.2
  6.2 3.0 %collective-permute-start.3 = (f32[4,8,1536]{2,1,0:T(8,128)}, f32[4,8,1536]{2,1,0:T(8,128)S(1)}, u32[]{:S(2)}, u32[]{:S(2)}) collective-permute-start(f32[4,8,1536]{2,1,0:T(8,128)} %get-tuple-element.51), channel_id=1, source_target_pairs={{0,4},{4,0},{8,12},{12,8},{16,20},{20,16},{24,28},{28,24},{1,5},{5... | collective-permute-start | bytes 589832 | tf_op jit(solution)/shard_map/ppermute | solution.py:401
  9.2 0.0 collective-permute-start
  9.2 1.5 %collective-permute-start.1 = (f32[16,512]{1,0:T(8,128)S(1)}, f32[16,512]{1,0:T(8,128)S(1)}, u32[]{:S(2)}, u32[]{:S(2)}) collective-permute-start(f32[16,512]{1,0:T(8,128)S(1)} %get-tuple-element.48), channel_id=1, source_target_pairs={{0,2},{1,3},{2,0},{3,1},{4,6},{5,7},{6,4},{7,5},{8,10},{9,11},{10,... | collective-permute-start | bytes 98312 | tf_op jit(solution)/shard_map/ppermute | solution.py:401
  10.7 0.4 collective-permute-start.2
  11.1 0.9 %copy-done.4 = f32[4,8,1536]{2,1,0:T(8,128)S(1)} copy-done((f32[4,8,1536]{2,1,0:T(8,128)S(1)}, f32[4,8,1536]{2,1,0:T(8,128)}, u32[]{:S(2)}) %copy-start.4) | copy-done | bytes 196632
  12.0 0.0 collective-permute-done.refs_1_
  12.0 1.1 %collective-permute-done.1.refs_2_ = f32[16,512]{1,0:T(8,128)S(1)} collective-permute-done((f32[16,512]{1,0:T(8,128)S(1)}, f32[16,512]{1,0:T(8,128)S(1)}, u32[]{:S(2)}, u32[]{:S(2)}) %collective-permute-start.1) | collective-permute-done | bytes 32800 | tf_op jit(solution)/shard_map/ppermute | solution.py:401
  13.1 0.9 %collective-permute-done.2.refs_3_ = f32[16,512]{1,0:T(8,128)S(1)} collective-permute-done((f32[16,512]{1,0:T(8,128)S(1)}, f32[16,512]{1,0:T(8,128)S(1)}, u32[]{:S(2)}, u32[]{:S(2)}) %collective-permute-start.2) | collective-permute-done | bytes 32800 | tf_op jit(solution)/shard_map/ppermute | solution.py:401
  14.0 0.3 collective-permute-done.3.refs_2_
  14.4 1.9 %collective-permute-start.4 = (f32[2,8,1536]{2,1,0:T(8,128)S(1)}, f32[2,8,1536]{2,1,0:T(8,128)S(1)}, u32[]{:S(2)}, u32[]{:S(2)}) collective-permute-start(f32[2,8,1536]{2,1,0:T(8,128)S(1)} %get-tuple-element.53), channel_id=1, source_target_pairs={{0,8},{4,12},{8,0},{12,4},{16,24},{20,28},{24,16},{28,20},{1,9},{5... | collective-permute-start | bytes 294920 | tf_op jit(solution)/shard_map/ppermute | solution.py:401
  16.2 1.5 %collective-permute-start.5 = (f32[16,512]{1,0:T(8,128)S(1)}, f32[16,512]{1,0:T(8,128)S(1)}, u32[]{:S(2)}, u32[]{:S(2)}) collective-permute-start(f32[16,512]{1,0:T(8,128)S(1)} %shard_sum.2.refs_0_), channel_id=1, source_target_pairs={{0,4},{4,0},{8,12},{12,8},{16,20},{20,16},{24,28},{28,24},{1,5},{5... | collective-permute-start | bytes 98312 | tf_op jit(solution)/shard_map/ppermute | solution.py:401
  17.7 2.4 %collective-permute-done.5.refs_1_ = f32[16,512]{1,0:T(8,128)S(1)} collective-permute-done((f32[16,512]{1,0:T(8,128)S(1)}, f32[16,512]{1,0:T(8,128)S(1)}, u32[]{:S(2)}, u32[]{:S(2)}) %collective-permute-start.5) | collective-permute-done | bytes 32800 | tf_op jit(solution)/shard_map/ppermute | solution.py:401
  20.1 0.0 collective-permute-done.4.refs_1_
  20.2 2.7 %collective-permute-start.6 = (f32[2,8,2048]{2,1,0:T(8,128)S(1)}, f32[2,8,2048]{2,1,0:T(8,128)S(1)}, u32[]{:S(2)}, u32[]{:S(2)}) collective-permute-start(f32[2,8,2048]{2,1,0:T(8,128)S(1)} %half_sum.1.refs_0_), channel_id=1, source_target_pairs={{0,16},{4,20},{8,24},{12,28},{16,0},{20,4},{24,8},{28,12},{1,17},{... | collective-permute-start | bytes 393224 | tf_op jit(solution)/shard_map/ppermute | solution.py:401
  22.8 5.4 %collective-permute-done.6.refs_1_ = f32[2,8,2048]{2,1,0:T(8,128)S(1)} collective-permute-done((f32[2,8,2048]{2,1,0:T(8,128)S(1)}, f32[2,8,2048]{2,1,0:T(8,128)S(1)}, u32[]{:S(2)}, u32[]{:S(2)}) %collective-permute-start.6) | collective-permute-done | bytes 131104 | tf_op jit(solution)/shard_map/ppermute | solution.py:401
  28.3 0.4 collective-permute-start.7
  28.7 4.6 %collective-permute-done.7.refs_1_ = f32[2,8,2048]{2,1,0:T(8,128)S(1)} collective-permute-done((f32[2,8,2048]{2,1,0:T(8,128)S(1)}, f32[2,8,2048]{2,1,0:T(8,128)S(1)}, u32[]{:S(2)}, u32[]{:S(2)}) %collective-permute-start.7) | collective-permute-done | bytes 131104 | tf_op jit(solution)/shard_map/ppermute | solution.py:401
  33.3 0.9 %collective-permute-start.8 = (f32[4,8,1536]{2,1,0:T(8,128)S(1)}, f32[4,8,1536]{2,1,0:T(8,128)S(1)}, u32[]{:S(2)}, u32[]{:S(2)}) collective-permute-start(f32[4,8,1536]{2,1,0:T(8,128)S(1)} %get-tuple-element.54.refs_1_), channel_id=1, source_target_pairs={{0,4},{4,0},{8,12},{12,8},{16,20},{20,16},{24,28},{28,24},{1,5},{5... | collective-permute-start | bytes 589832 | tf_op jit(solution)/shard_map/ppermute | solution.py:401
  34.3 0.0 collective-permute-start.11
  34.3 1.5 %collective-permute-start.10 = (f32[16,512]{1,0:T(8,128)S(1)}, f32[16,512]{1,0:T(8,128)S(1)}, u32[]{:S(2)}, u32[]{:S(2)}) collective-permute-start(f32[16,512]{1,0:T(8,128)S(1)} %get-tuple-element.55.refs_1_), channel_id=1, source_target_pairs={{0,2},{1,3},{2,0},{3,1},{4,6},{5,7},{6,4},{7,5},{8,10},{9,11},{10,... | collective-permute-start | bytes 98312 | tf_op jit(solution)/shard_map/ppermute | solution.py:401
  35.8 0.3 collective-permute-start.9
  36.1 1.8 %collective-permute-done.11.refs_4_ = f32[16,512]{1,0:T(8,128)S(1)} collective-permute-done((f32[16,512]{1,0:T(8,128)S(1)}, f32[16,512]{1,0:T(8,128)S(1)}, u32[]{:S(2)}, u32[]{:S(2)}) %collective-permute-start.11) | collective-permute-done | bytes 32800 | tf_op jit(solution)/shard_map/ppermute | solution.py:401
  37.9 0.4 collective-permute-done.10.refs_3_
  38.3 0.0 collective-permute-done.9.refs_2_
  38.3 0.8 collective-permute-done.8.refs_0_.refs_2_
  39.1 1.2 %right_up.1 = (f32[64,512]{1,0:T(8,128)S(1)}, f32[64,64]{1,0:T(8,128)S(1)}, f32[4,8,1536]{2,1,0:T(8,128)S(1)}, f32[4,8,1536]{2,1,0:T(8,128)S(1)}) custom-call(f32[4,8,1536]{2,1,0:T(8,128)S(1)} %collective-permute-done.8.refs_0_.refs_2_, f32[16,512]{1,0:T(8,128)S(1)} %get-tuple-element.55.refs_1_, f32[16,512]{1,0:T(8,128)S(1)} %collective-permute-done.9.refs_2_, ...), custom_call_target="tpu_custom_call" | custom-call | flops 805306368 | bytes 3817472 | tf_op jit(solution)/shard_map/right_up/pallas_call | solution.py:392
  40.3 0.9 %collective-permute-start.15 = (f32[4,8,1536]{2,1,0:T(8,128)S(1)}, f32[4,8,1536]{2,1,0:T(8,128)S(1)}, u32[]{:S(2)}, u32[]{:S(2)}) collective-permute-start(f32[4,8,1536]{2,1,0:T(8,128)S(1)} %get-tuple-element.65), channel_id=1, source_target_pairs={{0,4},{4,0},{8,12},{12,8},{16,20},{20,16},{24,28},{28,24},{1,5},{5... | collective-permute-start | bytes 589832 | tf_op jit(solution)/shard_map/ppermute | solution.py:401
  41.2 1.2 %right_down.1 = (f32[64,1536]{1,0:T(8,128)S(1)}, f32[16,768]{1,0:T(8,128)S(1)}, f32[16,768]{1,0:T(8,128)S(1)}, f32[16,768]{1,0:T(8,128)S(1)}, f32[16,768]{1,0:T(8,128)S(1)}) custom-call(f32[64,512]{1,0:T(8,128)S(1)} %get-tuple-element.56.refs_0_, f32[4,8,1536]{2,1,0:T(8,128)S(1)} %get-tuple-element.54.refs_1_, ...), custom_call_target="tpu_custom_call" | custom-call | flops 805306368 | bytes 4128768 | tf_op jit(solution)/shard_map/right_down/pallas_call | solution.py:392
  42.4 0.0 collective-permute-start.12
  42.4 1.6 %collective-permute-start.13 = (f32[16,768]{1,0:T(8,128)S(1)}, f32[16,768]{1,0:T(8,128)S(1)}, u32[]{:S(2)}, u32[]{:S(2)}) collective-permute-start(f32[16,768]{1,0:T(8,128)S(1)} %get-tuple-element.61), channel_id=1, source_target_pairs={{0,2},{1,3},{2,0},{3,1},{4,6},{5,7},{6,4},{7,5},{8,10},{9,11},{10,... | collective-permute-start | bytes 147464 | tf_op jit(solution)/shard_map/ppermute | solution.py:401
  44.0 0.3 collective-permute-start.14
  44.3 0.0 collective-permute-done.12.refs_1_
  44.3 2.3 %collective-permute-done.13.refs_2_ = f32[16,768]{1,0:T(8,128)S(1)} collective-permute-done((f32[16,768]{1,0:T(8,128)S(1)}, f32[16,768]{1,0:T(8,128)S(1)}, u32[]{:S(2)}, u32[]{:S(2)}) %collective-permute-start.13) | collective-permute-done | bytes 49184 | tf_op jit(solution)/shard_map/ppermute | solution.py:401
  46.6 1.1 %collective-permute-done.14.refs_3_ = f32[16,768]{1,0:T(8,128)S(1)} collective-permute-done((f32[16,768]{1,0:T(8,128)S(1)}, f32[16,768]{1,0:T(8,128)S(1)}, u32[]{:S(2)}, u32[]{:S(2)}) %collective-permute-start.14) | collective-permute-done | bytes 49184 | tf_op jit(solution)/shard_map/ppermute | solution.py:401
  47.7 0.1 shard_sum.3
  47.8 0.0 collective-permute-done.15.refs_1_
  47.8 0.1 collective-permute-start.16
  47.9 3.0 %collective-permute-start.17 = (f32[8,1792]{1,0:T(8,128)S(1)}, f32[8,1792]{1,0:T(8,128)S(1)}, u32[]{:S(2)}, u32[]{:S(2)}) collective-permute-start(f32[8,1792]{1,0:T(8,128)S(1)} %get-tuple-element.69), channel_id=1, source_target_pairs={{0,16},{4,20},{8,24},{12,28},{16,0},{20,4},{24,8},{28,12},{1,17},{... | collective-permute-start | bytes 172040 | tf_op jit(solution)/shard_map/ppermute | solution.py:401
  50.9 1.4 %collective-permute-start.18 = (f32[8,1792]{1,0:T(8,128)S(1)}, f32[8,1792]{1,0:T(8,128)S(1)}, u32[]{:S(2)}, u32[]{:S(2)}) collective-permute-start(f32[8,1792]{1,0:T(8,128)S(1)} %get-tuple-element.70), channel_id=1, source_target_pairs={{0,24},{4,28},{8,16},{12,20},{16,8},{20,12},{24,0},{28,4},{1,25},{... | collective-permute-start | bytes 172040 | tf_op jit(solution)/shard_map/ppermute | solution.py:401
  52.3 0.9 %collective-permute-done.16.refs_1_ = f32[8,1792]{1,0:T(8,128)S(1)} collective-permute-done((f32[8,1792]{1,0:T(8,128)S(1)}, f32[8,1792]{1,0:T(8,128)S(1)}, u32[]{:S(2)}, u32[]{:S(2)}) %collective-permute-start.16) | collective-permute-done | bytes 57376 | tf_op jit(solution)/shard_map/ppermute | solution.py:401
  53.2 0.2 collective-permute-done.17.refs_2_
  53.4 3.4 %collective-permute-done.18.refs_3_ = f32[8,1792]{1,0:T(8,128)S(1)} collective-permute-done((f32[8,1792]{1,0:T(8,128)S(1)}, f32[8,1792]{1,0:T(8,128)S(1)}, u32[]{:S(2)}, u32[]{:S(2)}) %collective-permute-start.18) | collective-permute-done | bytes 57376 | tf_op jit(solution)/shard_map/ppermute | solution.py:401
  56.9 2.1 %collective-permute-start.21 = (f32[8,1792]{1,0:T(8,128)S(1)}, f32[8,1792]{1,0:T(8,128)S(1)}, u32[]{:S(2)}, u32[]{:S(2)}) collective-permute-start(f32[8,1792]{1,0:T(8,128)S(1)} %replica_mean.1.refs_0_), channel_id=1, source_target_pairs={{0,24},{4,28},{8,16},{12,20},{16,8},{20,12},{24,0},{28,4},{1,25},{... | collective-permute-start | bytes 172040 | tf_op jit(solution)/shard_map/ppermute | solution.py:401
  59.0 0.0 collective-permute-start.20
  59.0 2.3 %collective-permute-start.19 = (f32[8,1792]{1,0:T(8,128)S(1)}, f32[8,1792]{1,0:T(8,128)S(1)}, u32[]{:S(2)}, u32[]{:S(2)}) collective-permute-start(f32[8,1792]{1,0:T(8,128)S(1)} %replica_mean.1.refs_0_), channel_id=1, source_target_pairs={{0,8},{4,12},{8,0},{12,4},{16,24},{20,28},{24,16},{28,20},{1,9},{5... | collective-permute-start | bytes 172040 | tf_op jit(solution)/shard_map/ppermute | solution.py:401
  61.3 1.7 %collective-permute-done.21.refs_3_ = f32[8,1792]{1,0:T(8,128)S(1)} collective-permute-done((f32[8,1792]{1,0:T(8,128)S(1)}, f32[8,1792]{1,0:T(8,128)S(1)}, u32[]{:S(2)}, u32[]{:S(2)}) %collective-permute-start.21) | collective-permute-done | bytes 57376 | tf_op jit(solution)/shard_map/ppermute | solution.py:401
  63.0 1.4 %collective-permute-done.20.refs_2_ = f32[8,1792]{1,0:T(8,128)S(1)} collective-permute-done((f32[8,1792]{1,0:T(8,128)S(1)}, f32[8,1792]{1,0:T(8,128)S(1)}, u32[]{:S(2)}, u32[]{:S(2)}) %collective-permute-start.20) | collective-permute-done | bytes 57376 | tf_op jit(solution)/shard_map/ppermute | solution.py:401
  64.4 0.0 collective-permute-done.19.refs_1_
  64.5 1.3 %collective-permute-start.22 = (f32[4,8,1792]{2,1,0:T(8,128)S(1)}, f32[4,8,1792]{2,1,0:T(8,128)S(1)}, u32[]{:S(2)}, u32[]{:S(2)}) collective-permute-start(f32[4,8,1792]{2,1,0:T(8,128)S(1)} %stack_z.1.refs_8_.refs_0_), channel_id=1, source_target_pairs={{0,4},{4,0},{8,12},{12,8},{16,20},{20,16},{24,28},{28,24},{1,5},{5... | collective-permute-start | bytes 688136 | tf_op jit(solution)/shard_map/ppermute | solution.py:401
  65.8 3.2 %basis.1 = (f32[64,64]{1,0:T(8,128)S(1)}, f32[64,64]{1,0:T(8,128)S(1)}, bf16[512,256]{1,0:T(8,128)(2,1)S(1)}, bf16[1536,256]{1,0:T(8,128)(2,1)S(1)}) custom-call(f32[64,512]{1,0:T(8,128)S(1)} %get-tuple-element.56.refs_0_, f32[64,1536]{1,0:T(8,128)S(1)} %get-tuple-element.57.refs_1_, f32[64,64]{1,0:T(8,128)S(1)} %get-tuple-element.58.refs_2_, ...), custom_call_target="tpu_custom_call" | custom-call | bytes 8159232 | tf_op jit(solution)/shard_map/basis/pallas_call | solution.py:392
  68.9 1.6 %collective-permute-done.22.refs_1_ = f32[4,8,1792]{2,1,0:T(8,128)S(1)} collective-permute-done((f32[4,8,1792]{2,1,0:T(8,128)S(1)}, f32[4,8,1792]{2,1,0:T(8,128)S(1)}, u32[]{:S(2)}, u32[]{:S(2)}) %collective-permute-start.22) | collective-permute-done | bytes 229408 | tf_op jit(solution)/shard_map/ppermute | solution.py:401
  70.6 0.7 factor_up.1
  71.2 0.1 collective-permute-start.25
  71.3 1.2 %collective-permute-start.24 = (f32[16,640]{1,0:T(8,128)S(1)}, f32[16,640]{1,0:T(8,128)S(1)}, u32[]{:S(2)}, u32[]{:S(2)}) collective-permute-start(f32[16,640]{1,0:T(8,128)S(1)} %get-tuple-element.77.refs_0_), channel_id=1, source_target_pairs={{0,2},{1,3},{2,0},{3,1},{4,6},{5,7},{6,4},{7,5},{8,10},{9,11},{10,... | collective-permute-start | bytes 122888 | tf_op jit(solution)/shard_map/ppermute | solution.py:401
  72.5 0.7 collective-permute-start.23
  73.2 2.3 %error_up.1 = (bf16[1,512,1536]{2,1,0:T(8,128)(2,1)}, f32[512,1536]{1,0:T(8,128)S(1)}) custom-call(bf16[1,512,1536]{2,1,0:T(8,128)(2,1)S(1)} %copy-done.2, bf16[1,512,1536]{2,1,0:T(8,128)(2,1)S(1)} %copy-done.3, bf16[512,256]{1,0:T(8,128)(2,1)S(1)} %get-tuple-element.71.refs_2_, bf16[256,1536]{1,0:T(8,128)(2,1)S(1)} %get-tuple-element.73.refs_3_), custom_call_target="tpu_custom_call" | custom-call | flops 402653184 | bytes 8912896 | tf_op jit(solution)/shard_map/error_up/pallas_call | solution.py:392
  75.5 0.0 collective-permute-done.25.refs_3_
  75.5 0.2 collective-permute-done.24.refs_2_
  75.7 0.0 collective-permute-done.23.refs_1_
  75.7 0.4 factor_down.1
  76.1 3.0 %last.1 = (bf16[1,1536,512]{2,1,0:T(8,128)(2,1)}, bf16[512,1536]{1,0:T(8,128)(2,1)}, bf16[1536,512]{1,0:T(8,128)(2,1)}) custom-call(bf16[1,1536,512]{2,1,0:T(8,128)(2,1)S(1)} %copy-done, bf16[1,1536,512]{2,1,0:T(8,128)(2,1)S(1)} %copy-done.1, f32[512,1536]{1,0:T(8,128)S(1)} %get-tuple-element.75.refs_5_.refs_2_, ...), custom_call_target="tpu_custom_call" | custom-call | flops 805306368 | bytes 12062720 | tf_op jit(solution)/shard_map/last/pallas_call | solution.py:392
  (17 shorter events, 0.2 us)
Async XLA Ops:
  0.6 38.5 %copy-start.3 = (bf16[1,512,1536]{2,1,0:T(8,128)(2,1)S(1)}, bf16[1,512,1536]{2,1,0:T(8,128)(2,1)}, u32[]{:S(2)}) copy-start(bf16[1,512,1536]{2,1,0:T(8,128)(2,1)} %refs_1_.4) | copy-start | bytes 4718596
  6.2 32.9 %copy-start.2 = (bf16[1,512,1536]{2,1,0:T(8,128)(2,1)S(1)}, bf16[1,512,1536]{2,1,0:T(8,128)(2,1)}, u32[]{:S(2)}) copy-start(bf16[1,512,1536]{2,1,0:T(8,128)(2,1)} %refs_0_.4) | copy-start | bytes 4718596
  6.2 8.1 %collective-permute-start.3 = (f32[4,8,1536]{2,1,0:T(8,128)}, f32[4,8,1536]{2,1,0:T(8,128)S(1)}, u32[]{:S(2)}, u32[]{:S(2)}) collective-permute-start(f32[4,8,1536]{2,1,0:T(8,128)} %get-tuple-element.51), channel_id=1, source_target_pairs={{0,4},{4,0},{8,12},{12,8},{16,20},{20,16},{24,28},{28,24},{1,5},{5... | collective-permute-start | bytes 589832 | tf_op jit(solution)/shard_map/ppermute | solution.py:401
  9.2 2.8 %collective-permute-start = (f32[16,512]{1,0:T(8,128)S(1)}, f32[16,512]{1,0:T(8,128)S(1)}, u32[]{:S(2)}, u32[]{:S(2)}) collective-permute-start(f32[16,512]{1,0:T(8,128)S(1)} %get-tuple-element.47), channel_id=1, source_target_pairs={{0,1},{1,0},{2,3},{3,2},{4,5},{5,4},{6,7},{7,6},{8,9},{9,8},{10,11... | collective-permute-start | bytes 98312 | tf_op jit(solution)/shard_map/ppermute | solution.py:401
  9.2 3.9 %collective-permute-start.1 = (f32[16,512]{1,0:T(8,128)S(1)}, f32[16,512]{1,0:T(8,128)S(1)}, u32[]{:S(2)}, u32[]{:S(2)}) collective-permute-start(f32[16,512]{1,0:T(8,128)S(1)} %get-tuple-element.48), channel_id=1, source_target_pairs={{0,2},{1,3},{2,0},{3,1},{4,6},{5,7},{6,4},{7,5},{8,10},{9,11},{10,... | collective-permute-start | bytes 98312 | tf_op jit(solution)/shard_map/ppermute | solution.py:401
  10.7 3.3 %collective-permute-start.2 = (f32[16,512]{1,0:T(8,128)S(1)}, f32[16,512]{1,0:T(8,128)S(1)}, u32[]{:S(2)}, u32[]{:S(2)}) collective-permute-start(f32[16,512]{1,0:T(8,128)S(1)} %get-tuple-element.49), channel_id=1, source_target_pairs={{0,3},{1,2},{2,1},{3,0},{4,7},{5,6},{6,5},{7,4},{8,11},{9,10},{10,... | collective-permute-start | bytes 98312 | tf_op jit(solution)/shard_map/ppermute | solution.py:401
  11.1 0.9 %copy-start.4 = (f32[4,8,1536]{2,1,0:T(8,128)S(1)}, f32[4,8,1536]{2,1,0:T(8,128)}, u32[]{:S(2)}) copy-start(f32[4,8,1536]{2,1,0:T(8,128)} %get-tuple-element.45.refs_1_) | copy-start | bytes 589828
  14.4 5.8 %collective-permute-start.4 = (f32[2,8,1536]{2,1,0:T(8,128)S(1)}, f32[2,8,1536]{2,1,0:T(8,128)S(1)}, u32[]{:S(2)}, u32[]{:S(2)}) collective-permute-start(f32[2,8,1536]{2,1,0:T(8,128)S(1)} %get-tuple-element.53), channel_id=1, source_target_pairs={{0,8},{4,12},{8,0},{12,4},{16,24},{20,28},{24,16},{28,20},{1,9},{5... | collective-permute-start | bytes 294920 | tf_op jit(solution)/shard_map/ppermute | solution.py:401
  16.2 3.9 %collective-permute-start.5 = (f32[16,512]{1,0:T(8,128)S(1)}, f32[16,512]{1,0:T(8,128)S(1)}, u32[]{:S(2)}, u32[]{:S(2)}) collective-permute-start(f32[16,512]{1,0:T(8,128)S(1)} %shard_sum.2.refs_0_), channel_id=1, source_target_pairs={{0,4},{4,0},{8,12},{12,8},{16,20},{20,16},{24,28},{28,24},{1,5},{5... | collective-permute-start | bytes 98312 | tf_op jit(solution)/shard_map/ppermute | solution.py:401
  20.2 8.1 %collective-permute-start.6 = (f32[2,8,2048]{2,1,0:T(8,128)S(1)}, f32[2,8,2048]{2,1,0:T(8,128)S(1)}, u32[]{:S(2)}, u32[]{:S(2)}) collective-permute-start(f32[2,8,2048]{2,1,0:T(8,128)S(1)} %half_sum.1.refs_0_), channel_id=1, source_target_pairs={{0,16},{4,20},{8,24},{12,28},{16,0},{20,4},{24,8},{28,12},{1,17},{... | collective-permute-start | bytes 393224 | tf_op jit(solution)/shard_map/ppermute | solution.py:401
  28.3 5.0 %collective-permute-start.7 = (f32[2,8,2048]{2,1,0:T(8,128)S(1)}, f32[2,8,2048]{2,1,0:T(8,128)S(1)}, u32[]{:S(2)}, u32[]{:S(2)}) collective-permute-start(f32[2,8,2048]{2,1,0:T(8,128)S(1)} %mean.1.refs_0_), channel_id=1, source_target_pairs={{0,8},{4,12},{8,0},{12,4},{16,24},{20,28},{24,16},{28,20},{1,9},{5... | collective-permute-start | bytes 393224 | tf_op jit(solution)/shard_map/ppermute | solution.py:401
  33.3 5.7 %collective-permute-start.8 = (f32[4,8,1536]{2,1,0:T(8,128)S(1)}, f32[4,8,1536]{2,1,0:T(8,128)S(1)}, u32[]{:S(2)}, u32[]{:S(2)}) collective-permute-start(f32[4,8,1536]{2,1,0:T(8,128)S(1)} %get-tuple-element.54.refs_1_), channel_id=1, source_target_pairs={{0,4},{4,0},{8,12},{12,8},{16,20},{20,16},{24,28},{28,24},{1,5},{5... | collective-permute-start | bytes 589832 | tf_op jit(solution)/shard_map/ppermute | solution.py:401
  34.3 7.0 %copy-start = (bf16[1,1536,512]{2,1,0:T(8,128)(2,1)S(1)}, bf16[1,1536,512]{2,1,0:T(8,128)(2,1)}, u32[]{:S(2)}) copy-start(bf16[1,1536,512]{2,1,0:T(8,128)(2,1)} %refs_0_.5) | copy-start | bytes 4718596
  34.3 7.0 %copy-start.1 = (bf16[1,1536,512]{2,1,0:T(8,128)(2,1)S(1)}, bf16[1,1536,512]{2,1,0:T(8,128)(2,1)}, u32[]{:S(2)}) copy-start(bf16[1,1536,512]{2,1,0:T(8,128)(2,1)} %refs_1_.5) | copy-start | bytes 4718596
  34.3 3.6 %collective-permute-start.11 = (f32[16,512]{1,0:T(8,128)S(1)}, f32[16,512]{1,0:T(8,128)S(1)}, u32[]{:S(2)}, u32[]{:S(2)}) collective-permute-start(f32[16,512]{1,0:T(8,128)S(1)} %get-tuple-element.55.refs_1_), channel_id=1, source_target_pairs={{0,3},{1,2},{2,1},{3,0},{4,7},{5,6},{6,5},{7,4},{8,11},{9,10},{10,... | collective-permute-start | bytes 98312 | tf_op jit(solution)/shard_map/ppermute | solution.py:401
  34.3 4.0 %collective-permute-start.10 = (f32[16,512]{1,0:T(8,128)S(1)}, f32[16,512]{1,0:T(8,128)S(1)}, u32[]{:S(2)}, u32[]{:S(2)}) collective-permute-start(f32[16,512]{1,0:T(8,128)S(1)} %get-tuple-element.55.refs_1_), channel_id=1, source_target_pairs={{0,2},{1,3},{2,0},{3,1},{4,6},{5,7},{6,4},{7,5},{8,10},{9,11},{10,... | collective-permute-start | bytes 98312 | tf_op jit(solution)/shard_map/ppermute | solution.py:401
  35.8 2.5 %collective-permute-start.9 = (f32[16,512]{1,0:T(8,128)S(1)}, f32[16,512]{1,0:T(8,128)S(1)}, u32[]{:S(2)}, u32[]{:S(2)}) collective-permute-start(f32[16,512]{1,0:T(8,128)S(1)} %get-tuple-element.55.refs_1_), channel_id=1, source_target_pairs={{0,1},{1,0},{2,3},{3,2},{4,5},{5,4},{6,7},{7,6},{8,9},{9,8},{10,11... | collective-permute-start | bytes 98312 | tf_op jit(solution)/shard_map/ppermute | solution.py:401
  40.3 7.5 %collective-permute-start.15 = (f32[4,8,1536]{2,1,0:T(8,128)S(1)}, f32[4,8,1536]{2,1,0:T(8,128)S(1)}, u32[]{:S(2)}, u32[]{:S(2)}) collective-permute-start(f32[4,8,1536]{2,1,0:T(8,128)S(1)} %get-tuple-element.65), channel_id=1, source_target_pairs={{0,4},{4,0},{8,12},{12,8},{16,20},{20,16},{24,28},{28,24},{1,5},{5... | collective-permute-start | bytes 589832 | tf_op jit(solution)/shard_map/ppermute | solution.py:401
  42.4 1.9 %collective-permute-start.12 = (f32[16,768]{1,0:T(8,128)S(1)}, f32[16,768]{1,0:T(8,128)S(1)}, u32[]{:S(2)}, u32[]{:S(2)}) collective-permute-start(f32[16,768]{1,0:T(8,128)S(1)} %get-tuple-element.60), channel_id=1, source_target_pairs={{0,1},{1,0},{2,3},{3,2},{4,5},{5,4},{6,7},{7,6},{8,9},{9,8},{10,11... | collective-permute-start | bytes 147464 | tf_op jit(solution)/shard_map/ppermute | solution.py:401
  42.4 4.2 %collective-permute-start.13 = (f32[16,768]{1,0:T(8,128)S(1)}, f32[16,768]{1,0:T(8,128)S(1)}, u32[]{:S(2)}, u32[]{:S(2)}) collective-permute-start(f32[16,768]{1,0:T(8,128)S(1)} %get-tuple-element.61), channel_id=1, source_target_pairs={{0,2},{1,3},{2,0},{3,1},{4,6},{5,7},{6,4},{7,5},{8,10},{9,11},{10,... | collective-permute-start | bytes 147464 | tf_op jit(solution)/shard_map/ppermute | solution.py:401
  44.0 3.7 %collective-permute-start.14 = (f32[16,768]{1,0:T(8,128)S(1)}, f32[16,768]{1,0:T(8,128)S(1)}, u32[]{:S(2)}, u32[]{:S(2)}) collective-permute-start(f32[16,768]{1,0:T(8,128)S(1)} %get-tuple-element.62), channel_id=1, source_target_pairs={{0,3},{1,2},{2,1},{3,0},{4,7},{5,6},{6,5},{7,4},{8,11},{9,10},{10,... | collective-permute-start | bytes 147464 | tf_op jit(solution)/shard_map/ppermute | solution.py:401
  47.8 5.4 %collective-permute-start.16 = (f32[8,1792]{1,0:T(8,128)S(1)}, f32[8,1792]{1,0:T(8,128)S(1)}, u32[]{:S(2)}, u32[]{:S(2)}) collective-permute-start(f32[8,1792]{1,0:T(8,128)S(1)} %get-tuple-element.68), channel_id=1, source_target_pairs={{0,8},{4,12},{8,0},{12,4},{16,24},{20,28},{24,16},{28,20},{1,9},{5... | collective-permute-start | bytes 172040 | tf_op jit(solution)/shard_map/ppermute | solution.py:401
  47.9 5.5 %collective-permute-start.17 = (f32[8,1792]{1,0:T(8,128)S(1)}, f32[8,1792]{1,0:T(8,128)S(1)}, u32[]{:S(2)}, u32[]{:S(2)}) collective-permute-start(f32[8,1792]{1,0:T(8,128)S(1)} %get-tuple-element.69), channel_id=1, source_target_pairs={{0,16},{4,20},{8,24},{12,28},{16,0},{20,4},{24,8},{28,12},{1,17},{... | collective-permute-start | bytes 172040 | tf_op jit(solution)/shard_map/ppermute | solution.py:401
  50.9 6.0 %collective-permute-start.18 = (f32[8,1792]{1,0:T(8,128)S(1)}, f32[8,1792]{1,0:T(8,128)S(1)}, u32[]{:S(2)}, u32[]{:S(2)}) collective-permute-start(f32[8,1792]{1,0:T(8,128)S(1)} %get-tuple-element.70), channel_id=1, source_target_pairs={{0,24},{4,28},{8,16},{12,20},{16,8},{20,12},{24,0},{28,4},{1,25},{... | collective-permute-start | bytes 172040 | tf_op jit(solution)/shard_map/ppermute | solution.py:401
  56.9 6.1 %collective-permute-start.21 = (f32[8,1792]{1,0:T(8,128)S(1)}, f32[8,1792]{1,0:T(8,128)S(1)}, u32[]{:S(2)}, u32[]{:S(2)}) collective-permute-start(f32[8,1792]{1,0:T(8,128)S(1)} %replica_mean.1.refs_0_), channel_id=1, source_target_pairs={{0,24},{4,28},{8,16},{12,20},{16,8},{20,12},{24,0},{28,4},{1,25},{... | collective-permute-start | bytes 172040 | tf_op jit(solution)/shard_map/ppermute | solution.py:401
  59.0 5.4 %collective-permute-start.20 = (f32[8,1792]{1,0:T(8,128)S(1)}, f32[8,1792]{1,0:T(8,128)S(1)}, u32[]{:S(2)}, u32[]{:S(2)}) collective-permute-start(f32[8,1792]{1,0:T(8,128)S(1)} %replica_mean.1.refs_0_), channel_id=1, source_target_pairs={{0,16},{4,20},{8,24},{12,28},{16,0},{20,4},{24,8},{28,12},{1,17},{... | collective-permute-start | bytes 172040 | tf_op jit(solution)/shard_map/ppermute | solution.py:401
  59.0 5.4 %collective-permute-start.19 = (f32[8,1792]{1,0:T(8,128)S(1)}, f32[8,1792]{1,0:T(8,128)S(1)}, u32[]{:S(2)}, u32[]{:S(2)}) collective-permute-start(f32[8,1792]{1,0:T(8,128)S(1)} %replica_mean.1.refs_0_), channel_id=1, source_target_pairs={{0,8},{4,12},{8,0},{12,4},{16,24},{20,28},{24,16},{28,20},{1,9},{5... | collective-permute-start | bytes 172040 | tf_op jit(solution)/shard_map/ppermute | solution.py:401
  64.5 6.1 %collective-permute-start.22 = (f32[4,8,1792]{2,1,0:T(8,128)S(1)}, f32[4,8,1792]{2,1,0:T(8,128)S(1)}, u32[]{:S(2)}, u32[]{:S(2)}) collective-permute-start(f32[4,8,1792]{2,1,0:T(8,128)S(1)} %stack_z.1.refs_8_.refs_0_), channel_id=1, source_target_pairs={{0,4},{4,0},{8,12},{12,8},{16,20},{20,16},{24,28},{28,24},{1,5},{5... | collective-permute-start | bytes 688136 | tf_op jit(solution)/shard_map/ppermute | solution.py:401
  71.2 4.3 %collective-permute-start.25 = (f32[16,640]{1,0:T(8,128)S(1)}, f32[16,640]{1,0:T(8,128)S(1)}, u32[]{:S(2)}, u32[]{:S(2)}) collective-permute-start(f32[16,640]{1,0:T(8,128)S(1)} %get-tuple-element.77.refs_0_), channel_id=1, source_target_pairs={{0,3},{1,2},{2,1},{3,0},{4,7},{5,6},{6,5},{7,4},{8,11},{9,10},{10,... | collective-permute-start | bytes 122888 | tf_op jit(solution)/shard_map/ppermute | solution.py:401
  71.3 4.3 %collective-permute-start.24 = (f32[16,640]{1,0:T(8,128)S(1)}, f32[16,640]{1,0:T(8,128)S(1)}, u32[]{:S(2)}, u32[]{:S(2)}) collective-permute-start(f32[16,640]{1,0:T(8,128)S(1)} %get-tuple-element.77.refs_0_), channel_id=1, source_target_pairs={{0,2},{1,3},{2,0},{3,1},{4,6},{5,7},{6,4},{7,5},{8,10},{9,11},{10,... | collective-permute-start | bytes 122888 | tf_op jit(solution)/shard_map/ppermute | solution.py:401
  72.5 3.2 %collective-permute-start.23 = (f32[16,640]{1,0:T(8,128)S(1)}, f32[16,640]{1,0:T(8,128)S(1)}, u32[]{:S(2)}, u32[]{:S(2)}) collective-permute-start(f32[16,640]{1,0:T(8,128)S(1)} %get-tuple-element.77.refs_0_), channel_id=1, source_target_pairs={{0,1},{1,0},{2,3},{3,2},{4,5},{5,4},{6,7},{7,6},{8,9},{9,8},{10,11... | collective-permute-start | bytes 122888 | tf_op jit(solution)/shard_map/ppermute | solution.py:401

commit v18 on v17

--- a/solution.py
+++ b/solution.py
@@ -333,35 +333,45 @@
     shard[:, width:] = jnp.full((rows, 128), square, F32)
 
 
-def factor_down_kernel(limit, n_shards, *refs):
+def blocks_of(rows):
+    block = rows // STEPS
+    return [slice(i * block, (i + 1) * block) for i in range(STEPS)]
+
+
+def error_up_kernel(g, e, lhs, rhs, error, kept):
+    for part in blocks_of(error.shape[1]):
+        rebuilt = dot(lhs[part, :], rhs[...])
+        kept[part, :] = rebuilt
+        error[0, part, :] = (g[0, part, :].astype(F32) + e[0, part, :].astype(F32) - rebuilt).astype(BF16)
+
+
+def last_kernel(limit, n_shards, error_up, *refs):
     shards, refs = refs[:n_shards], refs[n_shards:]
-    inv, _, rhs, clip, total = refs
+    inv, g, e, rebuilt_up, lhs, out_error_up, out_error, out_up, out_down, total, rhs, error, up, down, sems = refs
+    copies = []
+
+    def write(src, dst):
+        copies.append(pltpu.make_async_copy(src, dst, sems.at[len(copies)]))
+        copies[-1].start()
+
+    write(error_up, out_error_up)
     join_shards(shards, total)
     square = right_factor(inv, total, rhs)
     width = total.shape[1]
     norm_sq = square + tree_sum(shard[:8, width:] for shard in shards)
-    clip[...] = jnp.minimum(jnp.float32(1.0), limit / jnp.sqrt(norm_sq))
-
-
-def rows_of(block):
-    return pl.ds(pl.multiple_of(pl.program_id(0) * block, block), block)
-
-
-def error_up_kernel(g, e, lhs, rhs, error, kept):
-    part = rows_of(error.shape[1])
-    rebuilt = dot(lhs[part, :], rhs[...])
-    kept[part, :] = rebuilt
-    error[0] = (g[0, part, :].astype(F32) + e[0, part, :].astype(F32) - rebuilt).astype(BF16)
-
-
-def last_kernel(g, e, rebuilt_up, lhs_down, rhs_down, clip, error, update_up, update_down):
-    factor = clip[:1, :1]
-    part = rows_of(update_down.shape[0])
-    rebuilt = dot(lhs_down[part, :], rhs_down[...])
-    update_down[...] = (factor * rebuilt).astype(BF16)
-    error[0] = (g[0, part, :].astype(F32) + e[0, part, :].astype(F32) - rebuilt).astype(BF16)
-    part = rows_of(update_up.shape[0])
-    update_up[...] = (factor * rebuilt_up[part, :]).astype(BF16)
+    factor = jnp.minimum(jnp.float32(1.0), limit / jnp.sqrt(norm_sq))[:1, :1]
+    for part, part_up in zip(blocks_of(down.shape[0]), blocks_of(up.shape[0])):
+        rebuilt = dot(lhs[part, :], rhs[...])
+        down[part, :] = (factor * rebuilt).astype(BF16)
+        error[part, :] = (g[0, part, :].astype(F32) + e[0, part, :].astype(F32) - rebuilt).astype(BF16)
+        up[part_up, :] = (factor * rebuilt_up[part_up, :]).astype(BF16)
+        window = pl.ds(part.start, part.stop - part.start)
+        write(down.at[window, :], out_down.at[window, :])
+        write(error.at[window, :], out_error.at[0, window, :])
+        window = pl.ds(part_up.start, part_up.stop - part_up.start)
+        write(up.at[window, :], out_up.at[window, :])
+    for copy in copies:
+        copy.wait()
 
 
 def shaped(*dims, dtype=F32):
@@ -510,19 +520,16 @@
         name="factor_up", scratch_shapes=[wide, stage],
     )
     right_rows = from_shards([shard] * n_shards)
-    new_error_up, rebuilt_up = call(
+    error_up, rebuilt_up = call(
         error_up_kernel, [shaped(1, rows, ff, dtype=BF16), shaped(rows, ff)], gu, eu, lhs_up, rhs_up, name="error_up", flops=product // 2,
-        grid=(STEPS,), in_specs=[VMEM] * 4, out_specs=[replica_blocks(rows, ff), VMEM],
     )
     limit = CLIP_RMS * (2.0 * rows * ff * n_shards) ** 0.5
-    rhs_down, clip = call(
-        functools.partial(factor_down_kernel, limit, n_shards), [shaped(4 * rank, rows, dtype=BF16), shaped(8, 128)],
-        *right_rows, inv_down, rebuilt_up, name="factor_down", in_specs=[VMEM] * (n_shards + 1) + [ANY], scratch_shapes=[narrow],
-    )
-    new_error_down, update_up, update_down = call(
-        last_kernel, [shaped(1, ff, rows, dtype=BF16), shaped(rows, ff, dtype=BF16), shaped(ff, rows, dtype=BF16)],
-        gd, ed, rebuilt_up, lhs_down, rhs_down, clip, name="last", flops=product, grid=(STEPS,),
-        in_specs=[VMEM] * 6, out_specs=[replica_blocks(ff, rows), row_blocks(rows, ff), row_blocks(ff, rows)],
+    outs = [shaped(1, rows, ff, dtype=BF16), shaped(1, ff, rows, dtype=BF16), shaped(rows, ff, dtype=BF16), shaped(ff, rows, dtype=BF16)]
+    new_error_up, new_error_down, update_up, update_down = call(
+        functools.partial(last_kernel, limit, n_shards), outs, error_up, *right_rows, inv_down, gd, ed, rebuilt_up, lhs_down, name="last",
+        flops=product, limit=16, out_specs=[HBM] * 4,
+        scratch_shapes=[narrow, pltpu.VMEM((4 * rank, rows), BF16)] + [pltpu.VMEM(shape, BF16) for shape in ((ff, rows), (rows, ff), (ff, rows))]
+        + [pltpu.SemaphoreType.DMA((3 * STEPS + 1,))],
     )
     return new_error_up, update_up, new_error_down, update_down
 

time: 79.2 us -> 78.6 us (level)
  Pallas kernels: 17.7 us -> 15.5 us
  waiting for transfers between devices: 30.6 us -> 32.3 us
    pallas_call x19 -> x18, Pallas kernels: 17.7 us -> 15.5 us  [call(): pl.pallas_call(lambda *refs: kernel(*refs[skip:]), out_shape=out_shape, i...]
    ppermute x26, waiting for transfers between devices: 30.6 us -> 32.3 us  [swap(): return lax.ppermute(x, axis, pairs)]
  transfers between devices with their start and end apart: 26 -> 26, of which waited for: 18 -> 19; matrix products, arithmetic and copies ran while one was open for 0% -> 0% of each run, Pallas kernels for 9% -> 6%
where the time goes in v18:
time: 78.6 us; the launch traced here: 78.5 us
  waiting for transfers between devices  32.3 us (41%)
  starting transfers between devices  29 us (37%)
  Pallas kernels  15.5 us (20%)
  local copies, waits for them, and re-layouts  0.94 us (1%)
    ppermute x26, waiting for transfers between devices, swap(): return lax.ppermute(x, axis, pairs)  32.3 us
    ppermute x26, starting transfers between devices, swap(): return lax.ppermute(x, axis, pairs)  29 us
    pallas_call x18, Pallas kernels, call(): pl.pallas_call(lambda *refs: kernel(*refs[skip:]), out_shape=out_shape, i...  15.5 us
  transfers between devices with their start and end apart: 26, of which 19 were waited for; matrix products, arithmetic and copies ran while one was open for 0% of the time, Pallas kernels for 6%

profile of v18, /device:TPU:0, one launch (start us, length us, event | category | flops | bytes accessed | tf_op | source)
XLA Modules:
  0.0 78.5 jit_solution(4715317278479541749)
XLA Ops:
  0.6 0.0 copy-start.1
  0.6 5.5 %left.1 = (f32[16,512]{1,0:T(8,128)S(1)}, f32[16,512]{1,0:T(8,128)S(1)}, f32[16,512]{1,0:T(8,128)S(1)}, f32[16,512]{1,0:T(8,128)S(1)}, f32[4,8,1536]{2,1,0:T(8,128)}, /*index=5*/f32[4,8,1536]{2,1,0:T(8,128)}) custom-call(bf16[1,512,1536]{2,1,0:T(8,128)(2,1)} %refs_0_.3, bf16[1,512,1536]{2,1,0:T(8,128)(2,1)} %refs_1_.3, f32[64,1536]{1,0:T(8,128)} %bitcast.2, ...), custom_call_target="tpu_custom_call" | custom-call | flops 1610612736 | bytes 7340032 | tf_op jit(solution)/shard_map/left/pallas_call | solution.py:402
  6.2 0.0 copy-start
  6.2 3.0 %collective-permute-start.3 = (f32[4,8,1536]{2,1,0:T(8,128)}, f32[4,8,1536]{2,1,0:T(8,128)S(1)}, u32[]{:S(2)}, u32[]{:S(2)}) collective-permute-start(f32[4,8,1536]{2,1,0:T(8,128)} %get-tuple-element.50), channel_id=1, source_target_pairs={{0,4},{4,0},{8,12},{12,8},{16,20},{20,16},{24,28},{28,24},{1,5},{5... | collective-permute-start | bytes 589832 | tf_op jit(solution)/shard_map/ppermute | solution.py:411
  9.2 0.0 collective-permute-start
  9.2 1.5 %collective-permute-start.1 = (f32[16,512]{1,0:T(8,128)S(1)}, f32[16,512]{1,0:T(8,128)S(1)}, u32[]{:S(2)}, u32[]{:S(2)}) collective-permute-start(f32[16,512]{1,0:T(8,128)S(1)} %get-tuple-element.47), channel_id=1, source_target_pairs={{0,2},{1,3},{2,0},{3,1},{4,6},{5,7},{6,4},{7,5},{8,10},{9,11},{10,... | collective-permute-start | bytes 98312 | tf_op jit(solution)/shard_map/ppermute | solution.py:411
  10.7 0.4 collective-permute-start.2
  11.1 0.9 %copy-done.4 = f32[4,8,1536]{2,1,0:T(8,128)S(1)} copy-done((f32[4,8,1536]{2,1,0:T(8,128)S(1)}, f32[4,8,1536]{2,1,0:T(8,128)}, u32[]{:S(2)}) %copy-start.4) | copy-done | bytes 196632
  12.0 0.0 collective-permute-done.refs_1_
  12.0 1.1 %collective-permute-done.1.refs_2_ = f32[16,512]{1,0:T(8,128)S(1)} collective-permute-done((f32[16,512]{1,0:T(8,128)S(1)}, f32[16,512]{1,0:T(8,128)S(1)}, u32[]{:S(2)}, u32[]{:S(2)}) %collective-permute-start.1) | collective-permute-done | bytes 32800 | tf_op jit(solution)/shard_map/ppermute | solution.py:411
  13.1 0.9 %collective-permute-done.2.refs_3_ = f32[16,512]{1,0:T(8,128)S(1)} collective-permute-done((f32[16,512]{1,0:T(8,128)S(1)}, f32[16,512]{1,0:T(8,128)S(1)}, u32[]{:S(2)}, u32[]{:S(2)}) %collective-permute-start.2) | collective-permute-done | bytes 32800 | tf_op jit(solution)/shard_map/ppermute | solution.py:411
  14.0 0.3 collective-permute-done.3.refs_2_
  14.4 1.9 %collective-permute-start.4 = (f32[2,8,1536]{2,1,0:T(8,128)S(1)}, f32[2,8,1536]{2,1,0:T(8,128)S(1)}, u32[]{:S(2)}, u32[]{:S(2)}) collective-permute-start(f32[2,8,1536]{2,1,0:T(8,128)S(1)} %get-tuple-element.52), channel_id=1, source_target_pairs={{0,8},{4,12},{8,0},{12,4},{16,24},{20,28},{24,16},{28,20},{1,9},{5... | collective-permute-start | bytes 294920 | tf_op jit(solution)/shard_map/ppermute | solution.py:411
  16.2 1.5 %collective-permute-start.5 = (f32[16,512]{1,0:T(8,128)S(1)}, f32[16,512]{1,0:T(8,128)S(1)}, u32[]{:S(2)}, u32[]{:S(2)}) collective-permute-start(f32[16,512]{1,0:T(8,128)S(1)} %shard_sum.2.refs_0_), channel_id=1, source_target_pairs={{0,4},{4,0},{8,12},{12,8},{16,20},{20,16},{24,28},{28,24},{1,5},{5... | collective-permute-start | bytes 98312 | tf_op jit(solution)/shard_map/ppermute | solution.py:411
  17.7 2.4 %collective-permute-done.5.refs_1_ = f32[16,512]{1,0:T(8,128)S(1)} collective-permute-done((f32[16,512]{1,0:T(8,128)S(1)}, f32[16,512]{1,0:T(8,128)S(1)}, u32[]{:S(2)}, u32[]{:S(2)}) %collective-permute-start.5) | collective-permute-done | bytes 32800 | tf_op jit(solution)/shard_map/ppermute | solution.py:411
  20.1 0.0 collective-permute-done.4.refs_1_
  20.2 2.7 %collective-permute-start.6 = (f32[2,8,2048]{2,1,0:T(8,128)S(1)}, f32[2,8,2048]{2,1,0:T(8,128)S(1)}, u32[]{:S(2)}, u32[]{:S(2)}) collective-permute-start(f32[2,8,2048]{2,1,0:T(8,128)S(1)} %half_sum.1.refs_0_), channel_id=1, source_target_pairs={{0,16},{4,20},{8,24},{12,28},{16,0},{20,4},{24,8},{28,12},{1,17},{... | collective-permute-start | bytes 393224 | tf_op jit(solution)/shard_map/ppermute | solution.py:411
  22.8 5.4 %collective-permute-done.6.refs_1_ = f32[2,8,2048]{2,1,0:T(8,128)S(1)} collective-permute-done((f32[2,8,2048]{2,1,0:T(8,128)S(1)}, f32[2,8,2048]{2,1,0:T(8,128)S(1)}, u32[]{:S(2)}, u32[]{:S(2)}) %collective-permute-start.6) | collective-permute-done | bytes 131104 | tf_op jit(solution)/shard_map/ppermute | solution.py:411
  28.3 0.4 collective-permute-start.7
  28.7 4.6 %collective-permute-done.7.refs_1_ = f32[2,8,2048]{2,1,0:T(8,128)S(1)} collective-permute-done((f32[2,8,2048]{2,1,0:T(8,128)S(1)}, f32[2,8,2048]{2,1,0:T(8,128)S(1)}, u32[]{:S(2)}, u32[]{:S(2)}) %collective-permute-start.7) | collective-permute-done | bytes 131104 | tf_op jit(solution)/shard_map/ppermute | solution.py:411
  33.3 0.9 %collective-permute-start.8 = (f32[4,8,1536]{2,1,0:T(8,128)S(1)}, f32[4,8,1536]{2,1,0:T(8,128)S(1)}, u32[]{:S(2)}, u32[]{:S(2)}) collective-permute-start(f32[4,8,1536]{2,1,0:T(8,128)S(1)} %get-tuple-element.53.refs_1_), channel_id=1, source_target_pairs={{0,4},{4,0},{8,12},{12,8},{16,20},{20,16},{24,28},{28,24},{1,5},{5... | collective-permute-start | bytes 589832 | tf_op jit(solution)/shard_map/ppermute | solution.py:411
  34.3 0.0 collective-permute-start.11
  34.3 1.5 %collective-permute-start.10 = (f32[16,512]{1,0:T(8,128)S(1)}, f32[16,512]{1,0:T(8,128)S(1)}, u32[]{:S(2)}, u32[]{:S(2)}) collective-permute-start(f32[16,512]{1,0:T(8,128)S(1)} %get-tuple-element.54.refs_1_), channel_id=1, source_target_pairs={{0,2},{1,3},{2,0},{3,1},{4,6},{5,7},{6,4},{7,5},{8,10},{9,11},{10,... | collective-permute-start | bytes 98312 | tf_op jit(solution)/shard_map/ppermute | solution.py:411
  35.8 0.3 collective-permute-start.9
  36.1 1.8 %collective-permute-done.11.refs_4_ = f32[16,512]{1,0:T(8,128)S(1)} collective-permute-done((f32[16,512]{1,0:T(8,128)S(1)}, f32[16,512]{1,0:T(8,128)S(1)}, u32[]{:S(2)}, u32[]{:S(2)}) %collective-permute-start.11) | collective-permute-done | bytes 32800 | tf_op jit(solution)/shard_map/ppermute | solution.py:411
  37.9 0.4 collective-permute-done.10.refs_3_
  38.3 0.0 collective-permute-done.9.refs_2_
  38.3 0.8 collective-permute-done.8.refs_0_.refs_2_
  39.1 1.2 %right_up.1 = (f32[64,512]{1,0:T(8,128)S(1)}, f32[64,64]{1,0:T(8,128)S(1)}, f32[4,8,1536]{2,1,0:T(8,128)S(1)}, f32[4,8,1536]{2,1,0:T(8,128)S(1)}) custom-call(f32[4,8,1536]{2,1,0:T(8,128)S(1)} %collective-permute-done.8.refs_0_.refs_2_, f32[16,512]{1,0:T(8,128)S(1)} %get-tuple-element.54.refs_1_, f32[16,512]{1,0:T(8,128)S(1)} %collective-permute-done.9.refs_2_, ...), custom_call_target="tpu_custom_call" | custom-call | flops 805306368 | bytes 3817472 | tf_op jit(solution)/shard_map/right_up/pallas_call | solution.py:402
  40.3 0.9 %collective-permute-start.15 = (f32[4,8,1536]{2,1,0:T(8,128)S(1)}, f32[4,8,1536]{2,1,0:T(8,128)S(1)}, u32[]{:S(2)}, u32[]{:S(2)}) collective-permute-start(f32[4,8,1536]{2,1,0:T(8,128)S(1)} %get-tuple-element.64), channel_id=1, source_target_pairs={{0,4},{4,0},{8,12},{12,8},{16,20},{20,16},{24,28},{28,24},{1,5},{5... | collective-permute-start | bytes 589832 | tf_op jit(solution)/shard_map/ppermute | solution.py:411
  41.2 0.0 copy-done.3
  41.2 1.2 %right_down.1 = (f32[64,1536]{1,0:T(8,128)S(1)}, f32[16,768]{1,0:T(8,128)S(1)}, f32[16,768]{1,0:T(8,128)S(1)}, f32[16,768]{1,0:T(8,128)S(1)}, f32[16,768]{1,0:T(8,128)S(1)}) custom-call(f32[64,512]{1,0:T(8,128)S(1)} %get-tuple-element.55.refs_0_, f32[4,8,1536]{2,1,0:T(8,128)S(1)} %get-tuple-element.53.refs_1_, ...), custom_call_target="tpu_custom_call" | custom-call | flops 805306368 | bytes 4128768 | tf_op jit(solution)/shard_map/right_down/pallas_call | solution.py:402
  42.4 0.0 collective-permute-start.12
  42.4 1.6 %collective-permute-start.13 = (f32[16,768]{1,0:T(8,128)S(1)}, f32[16,768]{1,0:T(8,128)S(1)}, u32[]{:S(2)}, u32[]{:S(2)}) collective-permute-start(f32[16,768]{1,0:T(8,128)S(1)} %get-tuple-element.60), channel_id=1, source_target_pairs={{0,2},{1,3},{2,0},{3,1},{4,6},{5,7},{6,4},{7,5},{8,10},{9,11},{10,... | collective-permute-start | bytes 147464 | tf_op jit(solution)/shard_map/ppermute | solution.py:411
  44.0 0.3 collective-permute-start.14
  44.3 0.0 collective-permute-done.12.refs_1_
  44.3 2.3 %collective-permute-done.13.refs_2_ = f32[16,768]{1,0:T(8,128)S(1)} collective-permute-done((f32[16,768]{1,0:T(8,128)S(1)}, f32[16,768]{1,0:T(8,128)S(1)}, u32[]{:S(2)}, u32[]{:S(2)}) %collective-permute-start.13) | collective-permute-done | bytes 49184 | tf_op jit(solution)/shard_map/ppermute | solution.py:411
  46.6 1.1 %collective-permute-done.14.refs_3_ = f32[16,768]{1,0:T(8,128)S(1)} collective-permute-done((f32[16,768]{1,0:T(8,128)S(1)}, f32[16,768]{1,0:T(8,128)S(1)}, u32[]{:S(2)}, u32[]{:S(2)}) %collective-permute-start.14) | collective-permute-done | bytes 49184 | tf_op jit(solution)/shard_map/ppermute | solution.py:411
  47.7 0.1 shard_sum.3
  47.8 0.0 collective-permute-done.15.refs_1_
  47.8 0.1 collective-permute-start.16
  47.9 3.0 %collective-permute-start.17 = (f32[8,1792]{1,0:T(8,128)S(1)}, f32[8,1792]{1,0:T(8,128)S(1)}, u32[]{:S(2)}, u32[]{:S(2)}) collective-permute-start(f32[8,1792]{1,0:T(8,128)S(1)} %get-tuple-element.68), channel_id=1, source_target_pairs={{0,16},{4,20},{8,24},{12,28},{16,0},{20,4},{24,8},{28,12},{1,17},{... | collective-permute-start | bytes 172040 | tf_op jit(solution)/shard_map/ppermute | solution.py:411
  50.9 1.4 %collective-permute-start.18 = (f32[8,1792]{1,0:T(8,128)S(1)}, f32[8,1792]{1,0:T(8,128)S(1)}, u32[]{:S(2)}, u32[]{:S(2)}) collective-permute-start(f32[8,1792]{1,0:T(8,128)S(1)} %get-tuple-element.69), channel_id=1, source_target_pairs={{0,24},{4,28},{8,16},{12,20},{16,8},{20,12},{24,0},{28,4},{1,25},{... | collective-permute-start | bytes 172040 | tf_op jit(solution)/shard_map/ppermute | solution.py:411
  52.3 0.9 %collective-permute-done.16.refs_1_ = f32[8,1792]{1,0:T(8,128)S(1)} collective-permute-done((f32[8,1792]{1,0:T(8,128)S(1)}, f32[8,1792]{1,0:T(8,128)S(1)}, u32[]{:S(2)}, u32[]{:S(2)}) %collective-permute-start.16) | collective-permute-done | bytes 57376 | tf_op jit(solution)/shard_map/ppermute | solution.py:411
  53.2 0.2 collective-permute-done.17.refs_2_
  53.4 3.4 %collective-permute-done.18.refs_3_ = f32[8,1792]{1,0:T(8,128)S(1)} collective-permute-done((f32[8,1792]{1,0:T(8,128)S(1)}, f32[8,1792]{1,0:T(8,128)S(1)}, u32[]{:S(2)}, u32[]{:S(2)}) %collective-permute-start.18) | collective-permute-done | bytes 57376 | tf_op jit(solution)/shard_map/ppermute | solution.py:411
  56.9 2.1 %collective-permute-start.21 = (f32[8,1792]{1,0:T(8,128)S(1)}, f32[8,1792]{1,0:T(8,128)S(1)}, u32[]{:S(2)}, u32[]{:S(2)}) collective-permute-start(f32[8,1792]{1,0:T(8,128)S(1)} %replica_mean.1.refs_0_), channel_id=1, source_target_pairs={{0,24},{4,28},{8,16},{12,20},{16,8},{20,12},{24,0},{28,4},{1,25},{... | collective-permute-start | bytes 172040 | tf_op jit(solution)/shard_map/ppermute | solution.py:411
  59.0 0.0 collective-permute-start.20
  59.0 2.3 %collective-permute-start.19 = (f32[8,1792]{1,0:T(8,128)S(1)}, f32[8,1792]{1,0:T(8,128)S(1)}, u32[]{:S(2)}, u32[]{:S(2)}) collective-permute-start(f32[8,1792]{1,0:T(8,128)S(1)} %replica_mean.1.refs_0_), channel_id=1, source_target_pairs={{0,8},{4,12},{8,0},{12,4},{16,24},{20,28},{24,16},{28,20},{1,9},{5... | collective-permute-start | bytes 172040 | tf_op jit(solution)/shard_map/ppermute | solution.py:411
  61.3 1.7 %collective-permute-done.21.refs_3_ = f32[8,1792]{1,0:T(8,128)S(1)} collective-permute-done((f32[8,1792]{1,0:T(8,128)S(1)}, f32[8,1792]{1,0:T(8,128)S(1)}, u32[]{:S(2)}, u32[]{:S(2)}) %collective-permute-start.21) | collective-permute-done | bytes 57376 | tf_op jit(solution)/shard_map/ppermute | solution.py:411
  63.0 1.4 %collective-permute-done.20.refs_2_ = f32[8,1792]{1,0:T(8,128)S(1)} collective-permute-done((f32[8,1792]{1,0:T(8,128)S(1)}, f32[8,1792]{1,0:T(8,128)S(1)}, u32[]{:S(2)}, u32[]{:S(2)}) %collective-permute-start.20) | collective-permute-done | bytes 57376 | tf_op jit(solution)/shard_map/ppermute | solution.py:411
  64.4 0.0 collective-permute-done.19.refs_1_
  64.5 1.3 %collective-permute-start.22 = (f32[4,8,1792]{2,1,0:T(8,128)S(1)}, f32[4,8,1792]{2,1,0:T(8,128)S(1)}, u32[]{:S(2)}, u32[]{:S(2)}) collective-permute-start(f32[4,8,1792]{2,1,0:T(8,128)S(1)} %stack_z.1.refs_8_.refs_0_), channel_id=1, source_target_pairs={{0,4},{4,0},{8,12},{12,8},{16,20},{20,16},{24,28},{28,24},{1,5},{5... | collective-permute-start | bytes 688136 | tf_op jit(solution)/shard_map/ppermute | solution.py:411
  65.8 3.2 %basis.1 = (f32[64,64]{1,0:T(8,128)S(1)}, f32[64,64]{1,0:T(8,128)S(1)}, bf16[512,256]{1,0:T(8,128)(2,1)S(1)}, bf16[1536,256]{1,0:T(8,128)(2,1)S(1)}) custom-call(f32[64,512]{1,0:T(8,128)S(1)} %get-tuple-element.55.refs_0_, f32[64,1536]{1,0:T(8,128)S(1)} %get-tuple-element.56.refs_1_, f32[64,64]{1,0:T(8,128)S(1)} %get-tuple-element.57.refs_2_, ...), custom_call_target="tpu_custom_call" | custom-call | bytes 8159232 | tf_op jit(solution)/shard_map/basis/pallas_call | solution.py:402
  68.9 1.6 %collective-permute-done.22.refs_1_ = f32[4,8,1792]{2,1,0:T(8,128)S(1)} collective-permute-done((f32[4,8,1792]{2,1,0:T(8,128)S(1)}, f32[4,8,1792]{2,1,0:T(8,128)S(1)}, u32[]{:S(2)}, u32[]{:S(2)}) %collective-permute-start.22) | collective-permute-done | bytes 229408 | tf_op jit(solution)/shard_map/ppermute | solution.py:411
  70.6 0.7 factor_up.1
  71.2 0.1 collective-permute-start.25
  71.3 1.2 %collective-permute-start.24 = (f32[16,640]{1,0:T(8,128)S(1)}, f32[16,640]{1,0:T(8,128)S(1)}, u32[]{:S(2)}, u32[]{:S(2)}) collective-permute-start(f32[16,640]{1,0:T(8,128)S(1)} %get-tuple-element.74.refs_1_), channel_id=1, source_target_pairs={{0,2},{1,3},{2,0},{3,1},{4,6},{5,7},{6,4},{7,5},{8,10},{9,11},{10,... | collective-permute-start | bytes 122888 | tf_op jit(solution)/shard_map/ppermute | solution.py:411
  72.5 0.7 collective-permute-start.23
  73.2 0.6 error_up.1
  73.8 1.0 %collective-permute-done.25.refs_4_ = f32[16,640]{1,0:T(8,128)S(1)} collective-permute-done((f32[16,640]{1,0:T(8,128)S(1)}, f32[16,640]{1,0:T(8,128)S(1)}, u32[]{:S(2)}, u32[]{:S(2)}) %collective-permute-start.25) | collective-permute-done | bytes 40992 | tf_op jit(solution)/shard_map/ppermute | solution.py:411
  74.8 0.8 %collective-permute-done.24.refs_3_ = f32[16,640]{1,0:T(8,128)S(1)} collective-permute-done((f32[16,640]{1,0:T(8,128)S(1)}, f32[16,640]{1,0:T(8,128)S(1)}, u32[]{:S(2)}, u32[]{:S(2)}) %collective-permute-start.24) | collective-permute-done | bytes 40992 | tf_op jit(solution)/shard_map/ppermute | solution.py:411
  75.7 0.0 collective-permute-done.23.refs_2_
  75.7 2.8 %last.1 = (bf16[1,512,1536]{2,1,0:T(8,128)(2,1)}, bf16[1,1536,512]{2,1,0:T(8,128)(2,1)}, bf16[512,1536]{1,0:T(8,128)(2,1)}, bf16[1536,512]{1,0:T(8,128)(2,1)}) custom-call(bf16[1,512,1536]{2,1,0:T(8,128)(2,1)S(1)} %get-tuple-element.73.refs_0_, f32[16,640]{1,0:T(8,128)S(1)} %get-tuple-element.74.refs_1_, f32[16,640]{1,0:T(8,128)S(1)} %collective-permute-done.23.refs_2_, ...), custom_call_target="tpu_custom_call" | custom-call | flops 805306368 | bytes 15122432 | tf_op jit(solution)/shard_map/last/pallas_call | solution.py:402
  (16 shorter events, 0.2 us)
Async XLA Ops:
  0.6 38.5 %copy-start.1 = (bf16[1,512,1536]{2,1,0:T(8,128)(2,1)S(1)}, bf16[1,512,1536]{2,1,0:T(8,128)(2,1)}, u32[]{:S(2)}) copy-start(bf16[1,512,1536]{2,1,0:T(8,128)(2,1)} %refs_1_.3) | copy-start | bytes 4718596
  6.2 32.9 %copy-start = (bf16[1,512,1536]{2,1,0:T(8,128)(2,1)S(1)}, bf16[1,512,1536]{2,1,0:T(8,128)(2,1)}, u32[]{:S(2)}) copy-start(bf16[1,512,1536]{2,1,0:T(8,128)(2,1)} %refs_0_.3) | copy-start | bytes 4718596
  6.2 8.1 %collective-permute-start.3 = (f32[4,8,1536]{2,1,0:T(8,128)}, f32[4,8,1536]{2,1,0:T(8,128)S(1)}, u32[]{:S(2)}, u32[]{:S(2)}) collective-permute-start(f32[4,8,1536]{2,1,0:T(8,128)} %get-tuple-element.50), channel_id=1, source_target_pairs={{0,4},{4,0},{8,12},{12,8},{16,20},{20,16},{24,28},{28,24},{1,5},{5... | collective-permute-start | bytes 589832 | tf_op jit(solution)/shard_map/ppermute | solution.py:411
  9.2 2.8 %collective-permute-start = (f32[16,512]{1,0:T(8,128)S(1)}, f32[16,512]{1,0:T(8,128)S(1)}, u32[]{:S(2)}, u32[]{:S(2)}) collective-permute-start(f32[16,512]{1,0:T(8,128)S(1)} %get-tuple-element.46), channel_id=1, source_target_pairs={{0,1},{1,0},{2,3},{3,2},{4,5},{5,4},{6,7},{7,6},{8,9},{9,8},{10,11... | collective-permute-start | bytes 98312 | tf_op jit(solution)/shard_map/ppermute | solution.py:411
  9.2 3.9 %collective-permute-start.1 = (f32[16,512]{1,0:T(8,128)S(1)}, f32[16,512]{1,0:T(8,128)S(1)}, u32[]{:S(2)}, u32[]{:S(2)}) collective-permute-start(f32[16,512]{1,0:T(8,128)S(1)} %get-tuple-element.47), channel_id=1, source_target_pairs={{0,2},{1,3},{2,0},{3,1},{4,6},{5,7},{6,4},{7,5},{8,10},{9,11},{10,... | collective-permute-start | bytes 98312 | tf_op jit(solution)/shard_map/ppermute | solution.py:411
  10.7 3.3 %collective-permute-start.2 = (f32[16,512]{1,0:T(8,128)S(1)}, f32[16,512]{1,0:T(8,128)S(1)}, u32[]{:S(2)}, u32[]{:S(2)}) collective-permute-start(f32[16,512]{1,0:T(8,128)S(1)} %get-tuple-element.48), channel_id=1, source_target_pairs={{0,3},{1,2},{2,1},{3,0},{4,7},{5,6},{6,5},{7,4},{8,11},{9,10},{10,... | collective-permute-start | bytes 98312 | tf_op jit(solution)/shard_map/ppermute | solution.py:411
  11.1 0.9 %copy-start.4 = (f32[4,8,1536]{2,1,0:T(8,128)S(1)}, f32[4,8,1536]{2,1,0:T(8,128)}, u32[]{:S(2)}) copy-start(f32[4,8,1536]{2,1,0:T(8,128)} %get-tuple-element.44.refs_1_) | copy-start | bytes 589828
  14.4 5.8 %collective-permute-start.4 = (f32[2,8,1536]{2,1,0:T(8,128)S(1)}, f32[2,8,1536]{2,1,0:T(8,128)S(1)}, u32[]{:S(2)}, u32[]{:S(2)}) collective-permute-start(f32[2,8,1536]{2,1,0:T(8,128)S(1)} %get-tuple-element.52), channel_id=1, source_target_pairs={{0,8},{4,12},{8,0},{12,4},{16,24},{20,28},{24,16},{28,20},{1,9},{5... | collective-permute-start | bytes 294920 | tf_op jit(solution)/shard_map/ppermute | solution.py:411
  16.2 3.9 %collective-permute-start.5 = (f32[16,512]{1,0:T(8,128)S(1)}, f32[16,512]{1,0:T(8,128)S(1)}, u32[]{:S(2)}, u32[]{:S(2)}) collective-permute-start(f32[16,512]{1,0:T(8,128)S(1)} %shard_sum.2.refs_0_), channel_id=1, source_target_pairs={{0,4},{4,0},{8,12},{12,8},{16,20},{20,16},{24,28},{28,24},{1,5},{5... | collective-permute-start | bytes 98312 | tf_op jit(solution)/shard_map/ppermute | solution.py:411
  20.2 8.1 %collective-permute-start.6 = (f32[2,8,2048]{2,1,0:T(8,128)S(1)}, f32[2,8,2048]{2,1,0:T(8,128)S(1)}, u32[]{:S(2)}, u32[]{:S(2)}) collective-permute-start(f32[2,8,2048]{2,1,0:T(8,128)S(1)} %half_sum.1.refs_0_), channel_id=1, source_target_pairs={{0,16},{4,20},{8,24},{12,28},{16,0},{20,4},{24,8},{28,12},{1,17},{... | collective-permute-start | bytes 393224 | tf_op jit(solution)/shard_map/ppermute | solution.py:411
  28.3 5.0 %collective-permute-start.7 = (f32[2,8,2048]{2,1,0:T(8,128)S(1)}, f32[2,8,2048]{2,1,0:T(8,128)S(1)}, u32[]{:S(2)}, u32[]{:S(2)}) collective-permute-start(f32[2,8,2048]{2,1,0:T(8,128)S(1)} %mean.1.refs_0_), channel_id=1, source_target_pairs={{0,8},{4,12},{8,0},{12,4},{16,24},{20,28},{24,16},{28,20},{1,9},{5... | collective-permute-start | bytes 393224 | tf_op jit(solution)/shard_map/ppermute | solution.py:411
  33.3 5.7 %collective-permute-start.8 = (f32[4,8,1536]{2,1,0:T(8,128)S(1)}, f32[4,8,1536]{2,1,0:T(8,128)S(1)}, u32[]{:S(2)}, u32[]{:S(2)}) collective-permute-start(f32[4,8,1536]{2,1,0:T(8,128)S(1)} %get-tuple-element.53.refs_1_), channel_id=1, source_target_pairs={{0,4},{4,0},{8,12},{12,8},{16,20},{20,16},{24,28},{28,24},{1,5},{5... | collective-permute-start | bytes 589832 | tf_op jit(solution)/shard_map/ppermute | solution.py:411
  34.3 7.0 %copy-start.2 = (bf16[1,1536,512]{2,1,0:T(8,128)(2,1)S(1)}, bf16[1,1536,512]{2,1,0:T(8,128)(2,1)}, u32[]{:S(2)}) copy-start(bf16[1,1536,512]{2,1,0:T(8,128)(2,1)} %refs_6_.5) | copy-start | bytes 4718596
  34.3 7.0 %copy-start.3 = (bf16[1,1536,512]{2,1,0:T(8,128)(2,1)S(1)}, bf16[1,1536,512]{2,1,0:T(8,128)(2,1)}, u32[]{:S(2)}) copy-start(bf16[1,1536,512]{2,1,0:T(8,128)(2,1)} %refs_7_.3) | copy-start | bytes 4718596
  34.3 3.6 %collective-permute-start.11 = (f32[16,512]{1,0:T(8,128)S(1)}, f32[16,512]{1,0:T(8,128)S(1)}, u32[]{:S(2)}, u32[]{:S(2)}) collective-permute-start(f32[16,512]{1,0:T(8,128)S(1)} %get-tuple-element.54.refs_1_), channel_id=1, source_target_pairs={{0,3},{1,2},{2,1},{3,0},{4,7},{5,6},{6,5},{7,4},{8,11},{9,10},{10,... | collective-permute-start | bytes 98312 | tf_op jit(solution)/shard_map/ppermute | solution.py:411
  34.3 4.0 %collective-permute-start.10 = (f32[16,512]{1,0:T(8,128)S(1)}, f32[16,512]{1,0:T(8,128)S(1)}, u32[]{:S(2)}, u32[]{:S(2)}) collective-permute-start(f32[16,512]{1,0:T(8,128)S(1)} %get-tuple-element.54.refs_1_), channel_id=1, source_target_pairs={{0,2},{1,3},{2,0},{3,1},{4,6},{5,7},{6,4},{7,5},{8,10},{9,11},{10,... | collective-permute-start | bytes 98312 | tf_op jit(solution)/shard_map/ppermute | solution.py:411
  35.8 2.5 %collective-permute-start.9 = (f32[16,512]{1,0:T(8,128)S(1)}, f32[16,512]{1,0:T(8,128)S(1)}, u32[]{:S(2)}, u32[]{:S(2)}) collective-permute-start(f32[16,512]{1,0:T(8,128)S(1)} %get-tuple-element.54.refs_1_), channel_id=1, source_target_pairs={{0,1},{1,0},{2,3},{3,2},{4,5},{5,4},{6,7},{7,6},{8,9},{9,8},{10,11... | collective-permute-start | bytes 98312 | tf_op jit(solution)/shard_map/ppermute | solution.py:411
  40.3 7.5 %collective-permute-start.15 = (f32[4,8,1536]{2,1,0:T(8,128)S(1)}, f32[4,8,1536]{2,1,0:T(8,128)S(1)}, u32[]{:S(2)}, u32[]{:S(2)}) collective-permute-start(f32[4,8,1536]{2,1,0:T(8,128)S(1)} %get-tuple-element.64), channel_id=1, source_target_pairs={{0,4},{4,0},{8,12},{12,8},{16,20},{20,16},{24,28},{28,24},{1,5},{5... | collective-permute-start | bytes 589832 | tf_op jit(solution)/shard_map/ppermute | solution.py:411
  42.4 1.9 %collective-permute-start.12 = (f32[16,768]{1,0:T(8,128)S(1)}, f32[16,768]{1,0:T(8,128)S(1)}, u32[]{:S(2)}, u32[]{:S(2)}) collective-permute-start(f32[16,768]{1,0:T(8,128)S(1)} %get-tuple-element.59), channel_id=1, source_target_pairs={{0,1},{1,0},{2,3},{3,2},{4,5},{5,4},{6,7},{7,6},{8,9},{9,8},{10,11... | collective-permute-start | bytes 147464 | tf_op jit(solution)/shard_map/ppermute | solution.py:411
  42.4 4.2 %collective-permute-start.13 = (f32[16,768]{1,0:T(8,128)S(1)}, f32[16,768]{1,0:T(8,128)S(1)}, u32[]{:S(2)}, u32[]{:S(2)}) collective-permute-start(f32[16,768]{1,0:T(8,128)S(1)} %get-tuple-element.60), channel_id=1, source_target_pairs={{0,2},{1,3},{2,0},{3,1},{4,6},{5,7},{6,4},{7,5},{8,10},{9,11},{10,... | collective-permute-start | bytes 147464 | tf_op jit(solution)/shard_map/ppermute | solution.py:411
  44.0 3.7 %collective-permute-start.14 = (f32[16,768]{1,0:T(8,128)S(1)}, f32[16,768]{1,0:T(8,128)S(1)}, u32[]{:S(2)}, u32[]{:S(2)}) collective-permute-start(f32[16,768]{1,0:T(8,128)S(1)} %get-tuple-element.61), channel_id=1, source_target_pairs={{0,3},{1,2},{2,1},{3,0},{4,7},{5,6},{6,5},{7,4},{8,11},{9,10},{10,... | collective-permute-start | bytes 147464 | tf_op jit(solution)/shard_map/ppermute | solution.py:411
  47.8 5.4 %collective-permute-start.16 = (f32[8,1792]{1,0:T(8,128)S(1)}, f32[8,1792]{1,0:T(8,128)S(1)}, u32[]{:S(2)}, u32[]{:S(2)}) collective-permute-start(f32[8,1792]{1,0:T(8,128)S(1)} %get-tuple-element.67), channel_id=1, source_target_pairs={{0,8},{4,12},{8,0},{12,4},{16,24},{20,28},{24,16},{28,20},{1,9},{5... | collective-permute-start | bytes 172040 | tf_op jit(solution)/shard_map/ppermute | solution.py:411
  47.9 5.5 %collective-permute-start.17 = (f32[8,1792]{1,0:T(8,128)S(1)}, f32[8,1792]{1,0:T(8,128)S(1)}, u32[]{:S(2)}, u32[]{:S(2)}) collective-permute-start(f32[8,1792]{1,0:T(8,128)S(1)} %get-tuple-element.68), channel_id=1, source_target_pairs={{0,16},{4,20},{8,24},{12,28},{16,0},{20,4},{24,8},{28,12},{1,17},{... | collective-permute-start | bytes 172040 | tf_op jit(solution)/shard_map/ppermute | solution.py:411
  50.9 6.0 %collective-permute-start.18 = (f32[8,1792]{1,0:T(8,128)S(1)}, f32[8,1792]{1,0:T(8,128)S(1)}, u32[]{:S(2)}, u32[]{:S(2)}) collective-permute-start(f32[8,1792]{1,0:T(8,128)S(1)} %get-tuple-element.69), channel_id=1, source_target_pairs={{0,24},{4,28},{8,16},{12,20},{16,8},{20,12},{24,0},{28,4},{1,25},{... | collective-permute-start | bytes 172040 | tf_op jit(solution)/shard_map/ppermute | solution.py:411
  56.9 6.1 %collective-permute-start.21 = (f32[8,1792]{1,0:T(8,128)S(1)}, f32[8,1792]{1,0:T(8,128)S(1)}, u32[]{:S(2)}, u32[]{:S(2)}) collective-permute-start(f32[8,1792]{1,0:T(8,128)S(1)} %replica_mean.1.refs_0_), channel_id=1, source_target_pairs={{0,24},{4,28},{8,16},{12,20},{16,8},{20,12},{24,0},{28,4},{1,25},{... | collective-permute-start | bytes 172040 | tf_op jit(solution)/shard_map/ppermute | solution.py:411
  59.0 5.4 %collective-permute-start.20 = (f32[8,1792]{1,0:T(8,128)S(1)}, f32[8,1792]{1,0:T(8,128)S(1)}, u32[]{:S(2)}, u32[]{:S(2)}) collective-permute-start(f32[8,1792]{1,0:T(8,128)S(1)} %replica_mean.1.refs_0_), channel_id=1, source_target_pairs={{0,16},{4,20},{8,24},{12,28},{16,0},{20,4},{24,8},{28,12},{1,17},{... | collective-permute-start | bytes 172040 | tf_op jit(solution)/shard_map/ppermute | solution.py:411
  59.0 5.4 %collective-permute-start.19 = (f32[8,1792]{1,0:T(8,128)S(1)}, f32[8,1792]{1,0:T(8,128)S(1)}, u32[]{:S(2)}, u32[]{:S(2)}) collective-permute-start(f32[8,1792]{1,0:T(8,128)S(1)} %replica_mean.1.refs_0_), channel_id=1, source_target_pairs={{0,8},{4,12},{8,0},{12,4},{16,24},{20,28},{24,16},{28,20},{1,9},{5... | collective-permute-start | bytes 172040 | tf_op jit(solution)/shard_map/ppermute | solution.py:411
  64.5 6.1 %collective-permute-start.22 = (f32[4,8,1792]{2,1,0:T(8,128)S(1)}, f32[4,8,1792]{2,1,0:T(8,128)S(1)}, u32[]{:S(2)}, u32[]{:S(2)}) collective-permute-start(f32[4,8,1792]{2,1,0:T(8,128)S(1)} %stack_z.1.refs_8_.refs_0_), channel_id=1, source_target_pairs={{0,4},{4,0},{8,12},{12,8},{16,20},{20,16},{24,28},{28,24},{1,5},{5... | collective-permute-start | bytes 688136 | tf_op jit(solution)/shard_map/ppermute | solution.py:411
  71.2 3.6 %collective-permute-start.25 = (f32[16,640]{1,0:T(8,128)S(1)}, f32[16,640]{1,0:T(8,128)S(1)}, u32[]{:S(2)}, u32[]{:S(2)}) collective-permute-start(f32[16,640]{1,0:T(8,128)S(1)} %get-tuple-element.74.refs_1_), channel_id=1, source_target_pairs={{0,3},{1,2},{2,1},{3,0},{4,7},{5,6},{6,5},{7,4},{8,11},{9,10},{10,... | collective-permute-start | bytes 122888 | tf_op jit(solution)/shard_map/ppermute | solution.py:411
  71.3 4.3 %collective-permute-start.24 = (f32[16,640]{1,0:T(8,128)S(1)}, f32[16,640]{1,0:T(8,128)S(1)}, u32[]{:S(2)}, u32[]{:S(2)}) collective-permute-start(f32[16,640]{1,0:T(8,128)S(1)} %get-tuple-element.74.refs_1_), channel_id=1, source_target_pairs={{0,2},{1,3},{2,0},{3,1},{4,6},{5,7},{6,4},{7,5},{8,10},{9,11},{10,... | collective-permute-start | bytes 122888 | tf_op jit(solution)/shard_map/ppermute | solution.py:411
  72.5 3.2 %collective-permute-start.23 = (f32[16,640]{1,0:T(8,128)S(1)}, f32[16,640]{1,0:T(8,128)S(1)}, u32[]{:S(2)}, u32[]{:S(2)}) collective-permute-start(f32[16,640]{1,0:T(8,128)S(1)} %get-tuple-element.74.refs_1_), channel_id=1, source_target_pairs={{0,1},{1,0},{2,3},{3,2},{4,5},{5,4},{6,7},{7,6},{8,9},{9,8},{10,11... | collective-permute-start | bytes 122888 | tf_op jit(solution)/shard_map/ppermute | solution.py:411

commit v19 on v18

--- a/solution.py
+++ b/solution.py
@@ -338,23 +338,28 @@
     return [slice(i * block, (i + 1) * block) for i in range(STEPS)]
 
 
-def error_up_kernel(g, e, lhs, rhs, error, kept):
-    for part in blocks_of(error.shape[1]):
+def error_up_kernel(g, e, lhs, rhs, out, kept, error, sems):
+    copies = []
+    for i, part in enumerate(blocks_of(error.shape[0])):
         rebuilt = dot(lhs[part, :], rhs[...])
         kept[part, :] = rebuilt
-        error[0, part, :] = (g[0, part, :].astype(F32) + e[0, part, :].astype(F32) - rebuilt).astype(BF16)
-
-
-def last_kernel(limit, n_shards, error_up, *refs):
+        error[part, :] = (g[0, part, :].astype(F32) + e[0, part, :].astype(F32) - rebuilt).astype(BF16)
+        window = pl.ds(part.start, part.stop - part.start)
+        copies.append(pltpu.make_async_copy(error.at[window, :], out.at[0, window, :], sems.at[i]))
+        copies[i].start()
+    for copy in copies:
+        copy.wait()
+
+
+def last_kernel(limit, n_shards, *refs):
     shards, refs = refs[:n_shards], refs[n_shards:]
-    inv, g, e, rebuilt_up, lhs, out_error_up, out_error, out_up, out_down, total, rhs, error, up, down, sems = refs
+    inv, g, e, rebuilt_up, lhs, out_error, out_up, out_down, total, rhs, error, up, down, sems = refs
     copies = []
 
     def write(src, dst):
         copies.append(pltpu.make_async_copy(src, dst, sems.at[len(copies)]))
         copies[-1].start()
 
-    write(error_up, out_error_up)
     join_shards(shards, total)
     square = right_factor(inv, total, rhs)
     width = total.shape[1]
@@ -520,16 +525,17 @@
         name="factor_up", scratch_shapes=[wide, stage],
     )
     right_rows = from_shards([shard] * n_shards)
-    error_up, rebuilt_up = call(
+    new_error_up, rebuilt_up = call(
         error_up_kernel, [shaped(1, rows, ff, dtype=BF16), shaped(rows, ff)], gu, eu, lhs_up, rhs_up, name="error_up", flops=product // 2,
+        out_specs=[HBM, VMEM], scratch_shapes=[pltpu.VMEM((rows, ff), BF16), pltpu.SemaphoreType.DMA((STEPS,))],
     )
     limit = CLIP_RMS * (2.0 * rows * ff * n_shards) ** 0.5
-    outs = [shaped(1, rows, ff, dtype=BF16), shaped(1, ff, rows, dtype=BF16), shaped(rows, ff, dtype=BF16), shaped(ff, rows, dtype=BF16)]
-    new_error_up, new_error_down, update_up, update_down = call(
-        functools.partial(last_kernel, limit, n_shards), outs, error_up, *right_rows, inv_down, gd, ed, rebuilt_up, lhs_down, name="last",
-        flops=product, limit=16, out_specs=[HBM] * 4,
+    outs = [shaped(1, ff, rows, dtype=BF16), shaped(rows, ff, dtype=BF16), shaped(ff, rows, dtype=BF16)]
+    new_error_down, update_up, update_down = call(
+        functools.partial(last_kernel, limit, n_shards), outs, *right_rows, inv_down, gd, ed, rebuilt_up, lhs_down, name="last",
+        flops=product, limit=16, out_specs=[HBM] * 3,
         scratch_shapes=[narrow, pltpu.VMEM((4 * rank, rows), BF16)] + [pltpu.VMEM(shape, BF16) for shape in ((ff, rows), (rows, ff), (ff, rows))]
-        + [pltpu.SemaphoreType.DMA((3 * STEPS + 1,))],
+        + [pltpu.SemaphoreType.DMA((3 * STEPS,))],
     )
     return new_error_up, update_up, new_error_down, update_down
 

time: 78.6 us -> 78.7 us (level)
  waiting for transfers between devices: 32.3 us -> 31.4 us
  Pallas kernels: 15.5 us -> 16.3 us
    pallas_call x18, Pallas kernels: 15.5 us -> 16.3 us  [call(): pl.pallas_call(lambda *refs: kernel(*refs[skip:]), out_shape=out_shape, i...]
    ppermute x26, waiting for transfers between devices: 32.3 us -> 31.4 us  [swap(): return lax.ppermute(x, axis, pairs)]
  transfers between devices with their start and end apart: 26 -> 26, of which waited for: 19 -> 19; matrix products, arithmetic and copies ran while one was open for 0% -> 0% of each run, Pallas kernels for 6% -> 8%
where the time goes in v19:
time: 78.7 us; the launch traced here: 78.5 us
  waiting for transfers between devices  31.4 us (40%)
  starting transfers between devices  29 us (37%)
  Pallas kernels  16.3 us (21%)
  local copies, waits for them, and re-layouts  0.94 us (1%)
    ppermute x26, waiting for transfers between devices, swap(): return lax.ppermute(x, axis, pairs)  31.4 us
    ppermute x26, starting transfers between devices, swap(): return lax.ppermute(x, axis, pairs)  29 us
    pallas_call x18, Pallas kernels, call(): pl.pallas_call(lambda *refs: kernel(*refs[skip:]), out_shape=out_shape, i...  16.3 us
  transfers between devices with their start and end apart: 26, of which 19 were waited for; matrix products, arithmetic and copies ran while one was open for 0% of the time, Pallas kernels for 8%

profile of v19, /device:TPU:0, one launch (start us, length us, event | category | flops | bytes accessed | tf_op | source)
XLA Modules:
  0.0 78.5 jit_solution(658382651487796741)
XLA Ops:
  0.6 0.0 copy-start.3
  0.6 5.5 %left.1 = (f32[16,512]{1,0:T(8,128)S(1)}, f32[16,512]{1,0:T(8,128)S(1)}, f32[16,512]{1,0:T(8,128)S(1)}, f32[16,512]{1,0:T(8,128)S(1)}, f32[4,8,1536]{2,1,0:T(8,128)}, /*index=5*/f32[4,8,1536]{2,1,0:T(8,128)}) custom-call(bf16[1,512,1536]{2,1,0:T(8,128)(2,1)} %refs_0_.3, bf16[1,512,1536]{2,1,0:T(8,128)(2,1)} %refs_1_.3, f32[64,1536]{1,0:T(8,128)} %bitcast.2, ...), custom_call_target="tpu_custom_call" | custom-call | flops 1610612736 | bytes 7340032 | tf_op jit(solution)/shard_map/left/pallas_call | solution.py:407
  6.2 0.0 copy-start.2
  6.2 3.0 %collective-permute-start.3 = (f32[4,8,1536]{2,1,0:T(8,128)}, f32[4,8,1536]{2,1,0:T(8,128)S(1)}, u32[]{:S(2)}, u32[]{:S(2)}) collective-permute-start(f32[4,8,1536]{2,1,0:T(8,128)} %get-tuple-element.49), channel_id=1, source_target_pairs={{0,4},{4,0},{8,12},{12,8},{16,20},{20,16},{24,28},{28,24},{1,5},{5... | collective-permute-start | bytes 589832 | tf_op jit(solution)/shard_map/ppermute | solution.py:416
  9.2 0.0 collective-permute-start
  9.2 1.5 %collective-permute-start.1 = (f32[16,512]{1,0:T(8,128)S(1)}, f32[16,512]{1,0:T(8,128)S(1)}, u32[]{:S(2)}, u32[]{:S(2)}) collective-permute-start(f32[16,512]{1,0:T(8,128)S(1)} %get-tuple-element.46), channel_id=1, source_target_pairs={{0,2},{1,3},{2,0},{3,1},{4,6},{5,7},{6,4},{7,5},{8,10},{9,11},{10,... | collective-permute-start | bytes 98312 | tf_op jit(solution)/shard_map/ppermute | solution.py:416
  10.7 0.4 collective-permute-start.2
  11.1 0.9 %copy-done.4 = f32[4,8,1536]{2,1,0:T(8,128)S(1)} copy-done((f32[4,8,1536]{2,1,0:T(8,128)S(1)}, f32[4,8,1536]{2,1,0:T(8,128)}, u32[]{:S(2)}) %copy-start.4) | copy-done | bytes 196632
  12.0 0.0 collective-permute-done.refs_1_
  12.0 1.1 %collective-permute-done.1.refs_2_ = f32[16,512]{1,0:T(8,128)S(1)} collective-permute-done((f32[16,512]{1,0:T(8,128)S(1)}, f32[16,512]{1,0:T(8,128)S(1)}, u32[]{:S(2)}, u32[]{:S(2)}) %collective-permute-start.1) | collective-permute-done | bytes 32800 | tf_op jit(solution)/shard_map/ppermute | solution.py:416
  13.1 0.9 %collective-permute-done.2.refs_3_ = f32[16,512]{1,0:T(8,128)S(1)} collective-permute-done((f32[16,512]{1,0:T(8,128)S(1)}, f32[16,512]{1,0:T(8,128)S(1)}, u32[]{:S(2)}, u32[]{:S(2)}) %collective-permute-start.2) | collective-permute-done | bytes 32800 | tf_op jit(solution)/shard_map/ppermute | solution.py:416
  14.0 0.3 collective-permute-done.3.refs_2_
  14.4 1.9 %collective-permute-start.4 = (f32[2,8,1536]{2,1,0:T(8,128)S(1)}, f32[2,8,1536]{2,1,0:T(8,128)S(1)}, u32[]{:S(2)}, u32[]{:S(2)}) collective-permute-start(f32[2,8,1536]{2,1,0:T(8,128)S(1)} %get-tuple-element.51), channel_id=1, source_target_pairs={{0,8},{4,12},{8,0},{12,4},{16,24},{20,28},{24,16},{28,20},{1,9},{5... | collective-permute-start | bytes 294920 | tf_op jit(solution)/shard_map/ppermute | solution.py:416
  16.2 1.5 %collective-permute-start.5 = (f32[16,512]{1,0:T(8,128)S(1)}, f32[16,512]{1,0:T(8,128)S(1)}, u32[]{:S(2)}, u32[]{:S(2)}) collective-permute-start(f32[16,512]{1,0:T(8,128)S(1)} %shard_sum.2.refs_0_), channel_id=1, source_target_pairs={{0,4},{4,0},{8,12},{12,8},{16,20},{20,16},{24,28},{28,24},{1,5},{5... | collective-permute-start | bytes 98312 | tf_op jit(solution)/shard_map/ppermute | solution.py:416
  17.7 2.4 %collective-permute-done.5.refs_1_ = f32[16,512]{1,0:T(8,128)S(1)} collective-permute-done((f32[16,512]{1,0:T(8,128)S(1)}, f32[16,512]{1,0:T(8,128)S(1)}, u32[]{:S(2)}, u32[]{:S(2)}) %collective-permute-start.5) | collective-permute-done | bytes 32800 | tf_op jit(solution)/shard_map/ppermute | solution.py:416
  20.1 0.0 collective-permute-done.4.refs_1_
  20.2 2.7 %collective-permute-start.6 = (f32[2,8,2048]{2,1,0:T(8,128)S(1)}, f32[2,8,2048]{2,1,0:T(8,128)S(1)}, u32[]{:S(2)}, u32[]{:S(2)}) collective-permute-start(f32[2,8,2048]{2,1,0:T(8,128)S(1)} %half_sum.1.refs_0_), channel_id=1, source_target_pairs={{0,16},{4,20},{8,24},{12,28},{16,0},{20,4},{24,8},{28,12},{1,17},{... | collective-permute-start | bytes 393224 | tf_op jit(solution)/shard_map/ppermute | solution.py:416
  22.8 5.4 %collective-permute-done.6.refs_1_ = f32[2,8,2048]{2,1,0:T(8,128)S(1)} collective-permute-done((f32[2,8,2048]{2,1,0:T(8,128)S(1)}, f32[2,8,2048]{2,1,0:T(8,128)S(1)}, u32[]{:S(2)}, u32[]{:S(2)}) %collective-permute-start.6) | collective-permute-done | bytes 131104 | tf_op jit(solution)/shard_map/ppermute | solution.py:416
  28.3 0.4 collective-permute-start.7
  28.7 4.6 %collective-permute-done.7.refs_1_ = f32[2,8,2048]{2,1,0:T(8,128)S(1)} collective-permute-done((f32[2,8,2048]{2,1,0:T(8,128)S(1)}, f32[2,8,2048]{2,1,0:T(8,128)S(1)}, u32[]{:S(2)}, u32[]{:S(2)}) %collective-permute-start.7) | collective-permute-done | bytes 131104 | tf_op jit(solution)/shard_map/ppermute | solution.py:416
  33.3 0.9 %collective-permute-start.8 = (f32[4,8,1536]{2,1,0:T(8,128)S(1)}, f32[4,8,1536]{2,1,0:T(8,128)S(1)}, u32[]{:S(2)}, u32[]{:S(2)}) collective-permute-start(f32[4,8,1536]{2,1,0:T(8,128)S(1)} %get-tuple-element.52.refs_1_), channel_id=1, source_target_pairs={{0,4},{4,0},{8,12},{12,8},{16,20},{20,16},{24,28},{28,24},{1,5},{5... | collective-permute-start | bytes 589832 | tf_op jit(solution)/shard_map/ppermute | solution.py:416
  34.3 0.0 collective-permute-start.11
  34.3 1.5 %collective-permute-start.10 = (f32[16,512]{1,0:T(8,128)S(1)}, f32[16,512]{1,0:T(8,128)S(1)}, u32[]{:S(2)}, u32[]{:S(2)}) collective-permute-start(f32[16,512]{1,0:T(8,128)S(1)} %get-tuple-element.53.refs_1_), channel_id=1, source_target_pairs={{0,2},{1,3},{2,0},{3,1},{4,6},{5,7},{6,4},{7,5},{8,10},{9,11},{10,... | collective-permute-start | bytes 98312 | tf_op jit(solution)/shard_map/ppermute | solution.py:416
  35.8 0.3 collective-permute-start.9
  36.1 1.8 %collective-permute-done.11.refs_4_ = f32[16,512]{1,0:T(8,128)S(1)} collective-permute-done((f32[16,512]{1,0:T(8,128)S(1)}, f32[16,512]{1,0:T(8,128)S(1)}, u32[]{:S(2)}, u32[]{:S(2)}) %collective-permute-start.11) | collective-permute-done | bytes 32800 | tf_op jit(solution)/shard_map/ppermute | solution.py:416
  37.9 0.4 collective-permute-done.10.refs_3_
  38.3 0.0 collective-permute-done.9.refs_2_
  38.3 0.8 collective-permute-done.8.refs_0_.refs_2_
  39.1 1.2 %right_up.1 = (f32[64,512]{1,0:T(8,128)S(1)}, f32[64,64]{1,0:T(8,128)S(1)}, f32[4,8,1536]{2,1,0:T(8,128)S(1)}, f32[4,8,1536]{2,1,0:T(8,128)S(1)}) custom-call(f32[4,8,1536]{2,1,0:T(8,128)S(1)} %collective-permute-done.8.refs_0_.refs_2_, f32[16,512]{1,0:T(8,128)S(1)} %get-tuple-element.53.refs_1_, f32[16,512]{1,0:T(8,128)S(1)} %collective-permute-done.9.refs_2_, ...), custom_call_target="tpu_custom_call" | custom-call | flops 805306368 | bytes 3817472 | tf_op jit(solution)/shard_map/right_up/pallas_call | solution.py:407
  40.3 0.9 %collective-permute-start.15 = (f32[4,8,1536]{2,1,0:T(8,128)S(1)}, f32[4,8,1536]{2,1,0:T(8,128)S(1)}, u32[]{:S(2)}, u32[]{:S(2)}) collective-permute-start(f32[4,8,1536]{2,1,0:T(8,128)S(1)} %get-tuple-element.63), channel_id=1, source_target_pairs={{0,4},{4,0},{8,12},{12,8},{16,20},{20,16},{24,28},{28,24},{1,5},{5... | collective-permute-start | bytes 589832 | tf_op jit(solution)/shard_map/ppermute | solution.py:416
  41.2 0.0 copy-done.1
  41.2 1.2 %right_down.1 = (f32[64,1536]{1,0:T(8,128)S(1)}, f32[16,768]{1,0:T(8,128)S(1)}, f32[16,768]{1,0:T(8,128)S(1)}, f32[16,768]{1,0:T(8,128)S(1)}, f32[16,768]{1,0:T(8,128)S(1)}) custom-call(f32[64,512]{1,0:T(8,128)S(1)} %get-tuple-element.54.refs_0_, f32[4,8,1536]{2,1,0:T(8,128)S(1)} %get-tuple-element.52.refs_1_, ...), custom_call_target="tpu_custom_call" | custom-call | flops 805306368 | bytes 4128768 | tf_op jit(solution)/shard_map/right_down/pallas_call | solution.py:407
  42.4 0.0 collective-permute-start.12
  42.4 1.6 %collective-permute-start.13 = (f32[16,768]{1,0:T(8,128)S(1)}, f32[16,768]{1,0:T(8,128)S(1)}, u32[]{:S(2)}, u32[]{:S(2)}) collective-permute-start(f32[16,768]{1,0:T(8,128)S(1)} %get-tuple-element.59), channel_id=1, source_target_pairs={{0,2},{1,3},{2,0},{3,1},{4,6},{5,7},{6,4},{7,5},{8,10},{9,11},{10,... | collective-permute-start | bytes 147464 | tf_op jit(solution)/shard_map/ppermute | solution.py:416
  44.0 0.3 collective-permute-start.14
  44.3 0.0 collective-permute-done.12.refs_1_
  44.3 2.3 %collective-permute-done.13.refs_2_ = f32[16,768]{1,0:T(8,128)S(1)} collective-permute-done((f32[16,768]{1,0:T(8,128)S(1)}, f32[16,768]{1,0:T(8,128)S(1)}, u32[]{:S(2)}, u32[]{:S(2)}) %collective-permute-start.13) | collective-permute-done | bytes 49184 | tf_op jit(solution)/shard_map/ppermute | solution.py:416
  46.6 1.1 %collective-permute-done.14.refs_3_ = f32[16,768]{1,0:T(8,128)S(1)} collective-permute-done((f32[16,768]{1,0:T(8,128)S(1)}, f32[16,768]{1,0:T(8,128)S(1)}, u32[]{:S(2)}, u32[]{:S(2)}) %collective-permute-start.14) | collective-permute-done | bytes 49184 | tf_op jit(solution)/shard_map/ppermute | solution.py:416
  47.7 0.1 shard_sum.3
  47.8 0.0 collective-permute-done.15.refs_1_
  47.8 0.1 collective-permute-start.16
  47.9 3.0 %collective-permute-start.17 = (f32[8,1792]{1,0:T(8,128)S(1)}, f32[8,1792]{1,0:T(8,128)S(1)}, u32[]{:S(2)}, u32[]{:S(2)}) collective-permute-start(f32[8,1792]{1,0:T(8,128)S(1)} %get-tuple-element.67), channel_id=1, source_target_pairs={{0,16},{4,20},{8,24},{12,28},{16,0},{20,4},{24,8},{28,12},{1,17},{... | collective-permute-start | bytes 172040 | tf_op jit(solution)/shard_map/ppermute | solution.py:416
  50.9 1.4 %collective-permute-start.18 = (f32[8,1792]{1,0:T(8,128)S(1)}, f32[8,1792]{1,0:T(8,128)S(1)}, u32[]{:S(2)}, u32[]{:S(2)}) collective-permute-start(f32[8,1792]{1,0:T(8,128)S(1)} %get-tuple-element.68), channel_id=1, source_target_pairs={{0,24},{4,28},{8,16},{12,20},{16,8},{20,12},{24,0},{28,4},{1,25},{... | collective-permute-start | bytes 172040 | tf_op jit(solution)/shard_map/ppermute | solution.py:416
  52.3 0.9 %collective-permute-done.16.refs_1_ = f32[8,1792]{1,0:T(8,128)S(1)} collective-permute-done((f32[8,1792]{1,0:T(8,128)S(1)}, f32[8,1792]{1,0:T(8,128)S(1)}, u32[]{:S(2)}, u32[]{:S(2)}) %collective-permute-start.16) | collective-permute-done | bytes 57376 | tf_op jit(solution)/shard_map/ppermute | solution.py:416
  53.2 0.2 collective-permute-done.17.refs_2_
  53.4 3.4 %collective-permute-done.18.refs_3_ = f32[8,1792]{1,0:T(8,128)S(1)} collective-permute-done((f32[8,1792]{1,0:T(8,128)S(1)}, f32[8,1792]{1,0:T(8,128)S(1)}, u32[]{:S(2)}, u32[]{:S(2)}) %collective-permute-start.18) | collective-permute-done | bytes 57376 | tf_op jit(solution)/shard_map/ppermute | solution.py:416
  56.9 2.1 %collective-permute-start.21 = (f32[8,1792]{1,0:T(8,128)S(1)}, f32[8,1792]{1,0:T(8,128)S(1)}, u32[]{:S(2)}, u32[]{:S(2)}) collective-permute-start(f32[8,1792]{1,0:T(8,128)S(1)} %replica_mean.1.refs_0_), channel_id=1, source_target_pairs={{0,24},{4,28},{8,16},{12,20},{16,8},{20,12},{24,0},{28,4},{1,25},{... | collective-permute-start | bytes 172040 | tf_op jit(solution)/shard_map/ppermute | solution.py:416
  59.0 0.0 collective-permute-start.20
  59.0 2.3 %collective-permute-start.19 = (f32[8,1792]{1,0:T(8,128)S(1)}, f32[8,1792]{1,0:T(8,128)S(1)}, u32[]{:S(2)}, u32[]{:S(2)}) collective-permute-start(f32[8,1792]{1,0:T(8,128)S(1)} %replica_mean.1.refs_0_), channel_id=1, source_target_pairs={{0,8},{4,12},{8,0},{12,4},{16,24},{20,28},{24,16},{28,20},{1,9},{5... | collective-permute-start | bytes 172040 | tf_op jit(solution)/shard_map/ppermute | solution.py:416
  61.3 1.7 %collective-permute-done.21.refs_3_ = f32[8,1792]{1,0:T(8,128)S(1)} collective-permute-done((f32[8,1792]{1,0:T(8,128)S(1)}, f32[8,1792]{1,0:T(8,128)S(1)}, u32[]{:S(2)}, u32[]{:S(2)}) %collective-permute-start.21) | collective-permute-done | bytes 57376 | tf_op jit(solution)/shard_map/ppermute | solution.py:416
  63.0 1.4 %collective-permute-done.20.refs_2_ = f32[8,1792]{1,0:T(8,128)S(1)} collective-permute-done((f32[8,1792]{1,0:T(8,128)S(1)}, f32[8,1792]{1,0:T(8,128)S(1)}, u32[]{:S(2)}, u32[]{:S(2)}) %collective-permute-start.20) | collective-permute-done | bytes 57376 | tf_op jit(solution)/shard_map/ppermute | solution.py:416
  64.4 0.0 collective-permute-done.19.refs_1_
  64.5 1.3 %collective-permute-start.22 = (f32[4,8,1792]{2,1,0:T(8,128)S(1)}, f32[4,8,1792]{2,1,0:T(8,128)S(1)}, u32[]{:S(2)}, u32[]{:S(2)}) collective-permute-start(f32[4,8,1792]{2,1,0:T(8,128)S(1)} %stack_z.1.refs_8_.refs_0_), channel_id=1, source_target_pairs={{0,4},{4,0},{8,12},{12,8},{16,20},{20,16},{24,28},{28,24},{1,5},{5... | collective-permute-start | bytes 688136 | tf_op jit(solution)/shard_map/ppermute | solution.py:416
  65.8 3.2 %basis.1 = (f32[64,64]{1,0:T(8,128)S(1)}, f32[64,64]{1,0:T(8,128)S(1)}, bf16[512,256]{1,0:T(8,128)(2,1)S(1)}, bf16[1536,256]{1,0:T(8,128)(2,1)S(1)}) custom-call(f32[64,512]{1,0:T(8,128)S(1)} %get-tuple-element.54.refs_0_, f32[64,1536]{1,0:T(8,128)S(1)} %get-tuple-element.55.refs_1_, f32[64,64]{1,0:T(8,128)S(1)} %get-tuple-element.56.refs_2_, ...), custom_call_target="tpu_custom_call" | custom-call | bytes 8159232 | tf_op jit(solution)/shard_map/basis/pallas_call | solution.py:407
  68.9 1.6 %collective-permute-done.22.refs_1_ = f32[4,8,1792]{2,1,0:T(8,128)S(1)} collective-permute-done((f32[4,8,1792]{2,1,0:T(8,128)S(1)}, f32[4,8,1792]{2,1,0:T(8,128)S(1)}, u32[]{:S(2)}, u32[]{:S(2)}) %collective-permute-start.22) | collective-permute-done | bytes 229408 | tf_op jit(solution)/shard_map/ppermute | solution.py:416
  70.6 0.7 factor_up.1
  71.2 0.1 collective-permute-start.25
  71.3 1.2 %collective-permute-start.24 = (f32[16,640]{1,0:T(8,128)S(1)}, f32[16,640]{1,0:T(8,128)S(1)}, u32[]{:S(2)}, u32[]{:S(2)}) collective-permute-start(f32[16,640]{1,0:T(8,128)S(1)} %get-tuple-element.73.refs_0_), channel_id=1, source_target_pairs={{0,2},{1,3},{2,0},{3,1},{4,6},{5,7},{6,4},{7,5},{8,10},{9,11},{10,... | collective-permute-start | bytes 122888 | tf_op jit(solution)/shard_map/ppermute | solution.py:416
  72.5 0.7 collective-permute-start.23
  73.2 1.5 %error_up.1 = (bf16[1,512,1536]{2,1,0:T(8,128)(2,1)}, f32[512,1536]{1,0:T(8,128)S(1)}) custom-call(bf16[1,512,1536]{2,1,0:T(8,128)(2,1)S(1)} %copy-done.2, bf16[1,512,1536]{2,1,0:T(8,128)(2,1)S(1)} %copy-done.3, bf16[512,256]{1,0:T(8,128)(2,1)S(1)} %get-tuple-element.69.refs_2_, bf16[256,1536]{1,0:T(8,128)(2,1)S(1)} %get-tuple-element.71.refs_3_), custom_call_target="tpu_custom_call" | custom-call | flops 402653184 | bytes 8912896 | tf_op jit(solution)/shard_map/error_up/pallas_call | solution.py:407
  74.6 0.2 collective-permute-done.25.refs_3_
  74.8 0.8 %collective-permute-done.24.refs_2_ = f32[16,640]{1,0:T(8,128)S(1)} collective-permute-done((f32[16,640]{1,0:T(8,128)S(1)}, f32[16,640]{1,0:T(8,128)S(1)}, u32[]{:S(2)}, u32[]{:S(2)}) %collective-permute-start.24) | collective-permute-done | bytes 40992 | tf_op jit(solution)/shard_map/ppermute | solution.py:416
  75.7 0.0 collective-permute-done.23.refs_1_
  75.7 2.8 %last.1 = (bf16[1,1536,512]{2,1,0:T(8,128)(2,1)}, bf16[512,1536]{1,0:T(8,128)(2,1)}, bf16[1536,512]{1,0:T(8,128)(2,1)}) custom-call(f32[16,640]{1,0:T(8,128)S(1)} %get-tuple-element.73.refs_0_, f32[16,640]{1,0:T(8,128)S(1)} %collective-permute-done.23.refs_1_, f32[16,640]{1,0:T(8,128)S(1)} %collective-permute-done.24.refs_2_, ...), custom_call_target="tpu_custom_call" | custom-call | flops 805306368 | bytes 11976704 | tf_op jit(solution)/shard_map/last/pallas_call | solution.py:407
  (16 shorter events, 0.2 us)
Async XLA Ops:
  0.6 38.5 %copy-start.3 = (bf16[1,512,1536]{2,1,0:T(8,128)(2,1)S(1)}, bf16[1,512,1536]{2,1,0:T(8,128)(2,1)}, u32[]{:S(2)}) copy-start(bf16[1,512,1536]{2,1,0:T(8,128)(2,1)} %refs_1_.3) | copy-start | bytes 4718596
  6.2 32.9 %copy-start.2 = (bf16[1,512,1536]{2,1,0:T(8,128)(2,1)S(1)}, bf16[1,512,1536]{2,1,0:T(8,128)(2,1)}, u32[]{:S(2)}) copy-start(bf16[1,512,1536]{2,1,0:T(8,128)(2,1)} %refs_0_.3) | copy-start | bytes 4718596
  6.2 8.1 %collective-permute-start.3 = (f32[4,8,1536]{2,1,0:T(8,128)}, f32[4,8,1536]{2,1,0:T(8,128)S(1)}, u32[]{:S(2)}, u32[]{:S(2)}) collective-permute-start(f32[4,8,1536]{2,1,0:T(8,128)} %get-tuple-element.49), channel_id=1, source_target_pairs={{0,4},{4,0},{8,12},{12,8},{16,20},{20,16},{24,28},{28,24},{1,5},{5... | collective-permute-start | bytes 589832 | tf_op jit(solution)/shard_map/ppermute | solution.py:416
  9.2 2.8 %collective-permute-start = (f32[16,512]{1,0:T(8,128)S(1)}, f32[16,512]{1,0:T(8,128)S(1)}, u32[]{:S(2)}, u32[]{:S(2)}) collective-permute-start(f32[16,512]{1,0:T(8,128)S(1)} %get-tuple-element.45), channel_id=1, source_target_pairs={{0,1},{1,0},{2,3},{3,2},{4,5},{5,4},{6,7},{7,6},{8,9},{9,8},{10,11... | collective-permute-start | bytes 98312 | tf_op jit(solution)/shard_map/ppermute | solution.py:416
  9.2 3.9 %collective-permute-start.1 = (f32[16,512]{1,0:T(8,128)S(1)}, f32[16,512]{1,0:T(8,128)S(1)}, u32[]{:S(2)}, u32[]{:S(2)}) collective-permute-start(f32[16,512]{1,0:T(8,128)S(1)} %get-tuple-element.46), channel_id=1, source_target_pairs={{0,2},{1,3},{2,0},{3,1},{4,6},{5,7},{6,4},{7,5},{8,10},{9,11},{10,... | collective-permute-start | bytes 98312 | tf_op jit(solution)/shard_map/ppermute | solution.py:416
  10.7 3.3 %collective-permute-start.2 = (f32[16,512]{1,0:T(8,128)S(1)}, f32[16,512]{1,0:T(8,128)S(1)}, u32[]{:S(2)}, u32[]{:S(2)}) collective-permute-start(f32[16,512]{1,0:T(8,128)S(1)} %get-tuple-element.47), channel_id=1, source_target_pairs={{0,3},{1,2},{2,1},{3,0},{4,7},{5,6},{6,5},{7,4},{8,11},{9,10},{10,... | collective-permute-start | bytes 98312 | tf_op jit(solution)/shard_map/ppermute | solution.py:416
  11.1 0.9 %copy-start.4 = (f32[4,8,1536]{2,1,0:T(8,128)S(1)}, f32[4,8,1536]{2,1,0:T(8,128)}, u32[]{:S(2)}) copy-start(f32[4,8,1536]{2,1,0:T(8,128)} %get-tuple-element.43.refs_1_) | copy-start | bytes 589828
  14.4 5.8 %collective-permute-start.4 = (f32[2,8,1536]{2,1,0:T(8,128)S(1)}, f32[2,8,1536]{2,1,0:T(8,128)S(1)}, u32[]{:S(2)}, u32[]{:S(2)}) collective-permute-start(f32[2,8,1536]{2,1,0:T(8,128)S(1)} %get-tuple-element.51), channel_id=1, source_target_pairs={{0,8},{4,12},{8,0},{12,4},{16,24},{20,28},{24,16},{28,20},{1,9},{5... | collective-permute-start | bytes 294920 | tf_op jit(solution)/shard_map/ppermute | solution.py:416
  16.2 3.9 %collective-permute-start.5 = (f32[16,512]{1,0:T(8,128)S(1)}, f32[16,512]{1,0:T(8,128)S(1)}, u32[]{:S(2)}, u32[]{:S(2)}) collective-permute-start(f32[16,512]{1,0:T(8,128)S(1)} %shard_sum.2.refs_0_), channel_id=1, source_target_pairs={{0,4},{4,0},{8,12},{12,8},{16,20},{20,16},{24,28},{28,24},{1,5},{5... | collective-permute-start | bytes 98312 | tf_op jit(solution)/shard_map/ppermute | solution.py:416
  20.2 8.1 %collective-permute-start.6 = (f32[2,8,2048]{2,1,0:T(8,128)S(1)}, f32[2,8,2048]{2,1,0:T(8,128)S(1)}, u32[]{:S(2)}, u32[]{:S(2)}) collective-permute-start(f32[2,8,2048]{2,1,0:T(8,128)S(1)} %half_sum.1.refs_0_), channel_id=1, source_target_pairs={{0,16},{4,20},{8,24},{12,28},{16,0},{20,4},{24,8},{28,12},{1,17},{... | collective-permute-start | bytes 393224 | tf_op jit(solution)/shard_map/ppermute | solution.py:416
  28.3 5.0 %collective-permute-start.7 = (f32[2,8,2048]{2,1,0:T(8,128)S(1)}, f32[2,8,2048]{2,1,0:T(8,128)S(1)}, u32[]{:S(2)}, u32[]{:S(2)}) collective-permute-start(f32[2,8,2048]{2,1,0:T(8,128)S(1)} %mean.1.refs_0_), channel_id=1, source_target_pairs={{0,8},{4,12},{8,0},{12,4},{16,24},{20,28},{24,16},{28,20},{1,9},{5... | collective-permute-start | bytes 393224 | tf_op jit(solution)/shard_map/ppermute | solution.py:416
  33.3 5.7 %collective-permute-start.8 = (f32[4,8,1536]{2,1,0:T(8,128)S(1)}, f32[4,8,1536]{2,1,0:T(8,128)S(1)}, u32[]{:S(2)}, u32[]{:S(2)}) collective-permute-start(f32[4,8,1536]{2,1,0:T(8,128)S(1)} %get-tuple-element.52.refs_1_), channel_id=1, source_target_pairs={{0,4},{4,0},{8,12},{12,8},{16,20},{20,16},{24,28},{28,24},{1,5},{5... | collective-permute-start | bytes 589832 | tf_op jit(solution)/shard_map/ppermute | solution.py:416
  34.3 7.0 %copy-start = (bf16[1,1536,512]{2,1,0:T(8,128)(2,1)S(1)}, bf16[1,1536,512]{2,1,0:T(8,128)(2,1)}, u32[]{:S(2)}) copy-start(bf16[1,1536,512]{2,1,0:T(8,128)(2,1)} %refs_5_.5) | copy-start | bytes 4718596
  34.3 7.0 %copy-start.1 = (bf16[1,1536,512]{2,1,0:T(8,128)(2,1)S(1)}, bf16[1,1536,512]{2,1,0:T(8,128)(2,1)}, u32[]{:S(2)}) copy-start(bf16[1,1536,512]{2,1,0:T(8,128)(2,1)} %refs_6_.5) | copy-start | bytes 4718596
  34.3 3.6 %collective-permute-start.11 = (f32[16,512]{1,0:T(8,128)S(1)}, f32[16,512]{1,0:T(8,128)S(1)}, u32[]{:S(2)}, u32[]{:S(2)}) collective-permute-start(f32[16,512]{1,0:T(8,128)S(1)} %get-tuple-element.53.refs_1_), channel_id=1, source_target_pairs={{0,3},{1,2},{2,1},{3,0},{4,7},{5,6},{6,5},{7,4},{8,11},{9,10},{10,... | collective-permute-start | bytes 98312 | tf_op jit(solution)/shard_map/ppermute | solution.py:416
  34.3 4.0 %collective-permute-start.10 = (f32[16,512]{1,0:T(8,128)S(1)}, f32[16,512]{1,0:T(8,128)S(1)}, u32[]{:S(2)}, u32[]{:S(2)}) collective-permute-start(f32[16,512]{1,0:T(8,128)S(1)} %get-tuple-element.53.refs_1_), channel_id=1, source_target_pairs={{0,2},{1,3},{2,0},{3,1},{4,6},{5,7},{6,4},{7,5},{8,10},{9,11},{10,... | collective-permute-start | bytes 98312 | tf_op jit(solution)/shard_map/ppermute | solution.py:416
  35.8 2.5 %collective-permute-start.9 = (f32[16,512]{1,0:T(8,128)S(1)}, f32[16,512]{1,0:T(8,128)S(1)}, u32[]{:S(2)}, u32[]{:S(2)}) collective-permute-start(f32[16,512]{1,0:T(8,128)S(1)} %get-tuple-element.53.refs_1_), channel_id=1, source_target_pairs={{0,1},{1,0},{2,3},{3,2},{4,5},{5,4},{6,7},{7,6},{8,9},{9,8},{10,11... | collective-permute-start | bytes 98312 | tf_op jit(solution)/shard_map/ppermute | solution.py:416
  40.3 7.5 %collective-permute-start.15 = (f32[4,8,1536]{2,1,0:T(8,128)S(1)}, f32[4,8,1536]{2,1,0:T(8,128)S(1)}, u32[]{:S(2)}, u32[]{:S(2)}) collective-permute-start(f32[4,8,1536]{2,1,0:T(8,128)S(1)} %get-tuple-element.63), channel_id=1, source_target_pairs={{0,4},{4,0},{8,12},{12,8},{16,20},{20,16},{24,28},{28,24},{1,5},{5... | collective-permute-start | bytes 589832 | tf_op jit(solution)/shard_map/ppermute | solution.py:416
  42.4 1.9 %collective-permute-start.12 = (f32[16,768]{1,0:T(8,128)S(1)}, f32[16,768]{1,0:T(8,128)S(1)}, u32[]{:S(2)}, u32[]{:S(2)}) collective-permute-start(f32[16,768]{1,0:T(8,128)S(1)} %get-tuple-element.58), channel_id=1, source_target_pairs={{0,1},{1,0},{2,3},{3,2},{4,5},{5,4},{6,7},{7,6},{8,9},{9,8},{10,11... | collective-permute-start | bytes 147464 | tf_op jit(solution)/shard_map/ppermute | solution.py:416
  42.4 4.2 %collective-permute-start.13 = (f32[16,768]{1,0:T(8,128)S(1)}, f32[16,768]{1,0:T(8,128)S(1)}, u32[]{:S(2)}, u32[]{:S(2)}) collective-permute-start(f32[16,768]{1,0:T(8,128)S(1)} %get-tuple-element.59), channel_id=1, source_target_pairs={{0,2},{1,3},{2,0},{3,1},{4,6},{5,7},{6,4},{7,5},{8,10},{9,11},{10,... | collective-permute-start | bytes 147464 | tf_op jit(solution)/shard_map/ppermute | solution.py:416
  44.0 3.7 %collective-permute-start.14 = (f32[16,768]{1,0:T(8,128)S(1)}, f32[16,768]{1,0:T(8,128)S(1)}, u32[]{:S(2)}, u32[]{:S(2)}) collective-permute-start(f32[16,768]{1,0:T(8,128)S(1)} %get-tuple-element.60), channel_id=1, source_target_pairs={{0,3},{1,2},{2,1},{3,0},{4,7},{5,6},{6,5},{7,4},{8,11},{9,10},{10,... | collective-permute-start | bytes 147464 | tf_op jit(solution)/shard_map/ppermute | solution.py:416
  47.8 5.4 %collective-permute-start.16 = (f32[8,1792]{1,0:T(8,128)S(1)}, f32[8,1792]{1,0:T(8,128)S(1)}, u32[]{:S(2)}, u32[]{:S(2)}) collective-permute-start(f32[8,1792]{1,0:T(8,128)S(1)} %get-tuple-element.66), channel_id=1, source_target_pairs={{0,8},{4,12},{8,0},{12,4},{16,24},{20,28},{24,16},{28,20},{1,9},{5... | collective-permute-start | bytes 172040 | tf_op jit(solution)/shard_map/ppermute | solution.py:416
  47.9 5.5 %collective-permute-start.17 = (f32[8,1792]{1,0:T(8,128)S(1)}, f32[8,1792]{1,0:T(8,128)S(1)}, u32[]{:S(2)}, u32[]{:S(2)}) collective-permute-start(f32[8,1792]{1,0:T(8,128)S(1)} %get-tuple-element.67), channel_id=1, source_target_pairs={{0,16},{4,20},{8,24},{12,28},{16,0},{20,4},{24,8},{28,12},{1,17},{... | collective-permute-start | bytes 172040 | tf_op jit(solution)/shard_map/ppermute | solution.py:416
  50.9 6.0 %collective-permute-start.18 = (f32[8,1792]{1,0:T(8,128)S(1)}, f32[8,1792]{1,0:T(8,128)S(1)}, u32[]{:S(2)}, u32[]{:S(2)}) collective-permute-start(f32[8,1792]{1,0:T(8,128)S(1)} %get-tuple-element.68), channel_id=1, source_target_pairs={{0,24},{4,28},{8,16},{12,20},{16,8},{20,12},{24,0},{28,4},{1,25},{... | collective-permute-start | bytes 172040 | tf_op jit(solution)/shard_map/ppermute | solution.py:416
  56.9 6.1 %collective-permute-start.21 = (f32[8,1792]{1,0:T(8,128)S(1)}, f32[8,1792]{1,0:T(8,128)S(1)}, u32[]{:S(2)}, u32[]{:S(2)}) collective-permute-start(f32[8,1792]{1,0:T(8,128)S(1)} %replica_mean.1.refs_0_), channel_id=1, source_target_pairs={{0,24},{4,28},{8,16},{12,20},{16,8},{20,12},{24,0},{28,4},{1,25},{... | collective-permute-start | bytes 172040 | tf_op jit(solution)/shard_map/ppermute | solution.py:416
  59.0 5.4 %collective-permute-start.20 = (f32[8,1792]{1,0:T(8,128)S(1)}, f32[8,1792]{1,0:T(8,128)S(1)}, u32[]{:S(2)}, u32[]{:S(2)}) collective-permute-start(f32[8,1792]{1,0:T(8,128)S(1)} %replica_mean.1.refs_0_), channel_id=1, source_target_pairs={{0,16},{4,20},{8,24},{12,28},{16,0},{20,4},{24,8},{28,12},{1,17},{... | collective-permute-start | bytes 172040 | tf_op jit(solution)/shard_map/ppermute | solution.py:416
  59.0 5.4 %collective-permute-start.19 = (f32[8,1792]{1,0:T(8,128)S(1)}, f32[8,1792]{1,0:T(8,128)S(1)}, u32[]{:S(2)}, u32[]{:S(2)}) collective-permute-start(f32[8,1792]{1,0:T(8,128)S(1)} %replica_mean.1.refs_0_), channel_id=1, source_target_pairs={{0,8},{4,12},{8,0},{12,4},{16,24},{20,28},{24,16},{28,20},{1,9},{5... | collective-permute-start | bytes 172040 | tf_op jit(solution)/shard_map/ppermute | solution.py:416
  64.5 6.1 %collective-permute-start.22 = (f32[4,8,1792]{2,1,0:T(8,128)S(1)}, f32[4,8,1792]{2,1,0:T(8,128)S(1)}, u32[]{:S(2)}, u32[]{:S(2)}) collective-permute-start(f32[4,8,1792]{2,1,0:T(8,128)S(1)} %stack_z.1.refs_8_.refs_0_), channel_id=1, source_target_pairs={{0,4},{4,0},{8,12},{12,8},{16,20},{20,16},{24,28},{28,24},{1,5},{5... | collective-permute-start | bytes 688136 | tf_op jit(solution)/shard_map/ppermute | solution.py:416
  71.2 3.6 %collective-permute-start.25 = (f32[16,640]{1,0:T(8,128)S(1)}, f32[16,640]{1,0:T(8,128)S(1)}, u32[]{:S(2)}, u32[]{:S(2)}) collective-permute-start(f32[16,640]{1,0:T(8,128)S(1)} %get-tuple-element.73.refs_0_), channel_id=1, source_target_pairs={{0,3},{1,2},{2,1},{3,0},{4,7},{5,6},{6,5},{7,4},{8,11},{9,10},{10,... | collective-permute-start | bytes 122888 | tf_op jit(solution)/shard_map/ppermute | solution.py:416
  71.3 4.3 %collective-permute-start.24 = (f32[16,640]{1,0:T(8,128)S(1)}, f32[16,640]{1,0:T(8,128)S(1)}, u32[]{:S(2)}, u32[]{:S(2)}) collective-permute-start(f32[16,640]{1,0:T(8,128)S(1)} %get-tuple-element.73.refs_0_), channel_id=1, source_target_pairs={{0,2},{1,3},{2,0},{3,1},{4,6},{5,7},{6,4},{7,5},{8,10},{9,11},{10,... | collective-permute-start | bytes 122888 | tf_op jit(solution)/shard_map/ppermute | solution.py:416
  72.5 3.2 %collective-permute-start.23 = (f32[16,640]{1,0:T(8,128)S(1)}, f32[16,640]{1,0:T(8,128)S(1)}, u32[]{:S(2)}, u32[]{:S(2)}) collective-permute-start(f32[16,640]{1,0:T(8,128)S(1)} %get-tuple-element.73.refs_0_), channel_id=1, source_target_pairs={{0,1},{1,0},{2,3},{3,2},{4,5},{5,4},{6,7},{7,6},{8,9},{9,8},{10,11... | collective-permute-start | bytes 122888 | tf_op jit(solution)/shard_map/ppermute | solution.py:416

commit v20 on v19

--- a/solution.py
+++ b/solution.py
@@ -338,7 +338,7 @@
     return [slice(i * block, (i + 1) * block) for i in range(STEPS)]
 
 
-def error_up_kernel(g, e, lhs, rhs, out, kept, error, sems):
+def error_up_kernel(g, e, lhs, rhs, g_down, e_down, out, kept, merged, error, sems):
     copies = []
     for i, part in enumerate(blocks_of(error.shape[0])):
         rebuilt = dot(lhs[part, :], rhs[...])
@@ -347,13 +347,15 @@
         window = pl.ds(part.start, part.stop - part.start)
         copies.append(pltpu.make_async_copy(error.at[window, :], out.at[0, window, :], sems.at[i]))
         copies[i].start()
+    for part in blocks_of(merged.shape[0]):
+        merged[part, :] = g_down[0, part, :].astype(F32) + e_down[0, part, :].astype(F32)
     for copy in copies:
         copy.wait()
 
 
 def last_kernel(limit, n_shards, *refs):
     shards, refs = refs[:n_shards], refs[n_shards:]
-    inv, g, e, rebuilt_up, lhs, out_error, out_up, out_down, total, rhs, error, up, down, sems = refs
+    inv, merged, rebuilt_up, lhs, out_error, out_up, out_down, total, rhs, error, up, down, sems = refs
     copies = []
 
     def write(src, dst):
@@ -365,16 +367,17 @@
     width = total.shape[1]
     norm_sq = square + tree_sum(shard[:8, width:] for shard in shards)
     factor = jnp.minimum(jnp.float32(1.0), limit / jnp.sqrt(norm_sq))[:1, :1]
-    for part, part_up in zip(blocks_of(down.shape[0]), blocks_of(up.shape[0])):
+    for part in blocks_of(up.shape[0]):
+        up[part, :] = (factor * rebuilt_up[part, :]).astype(BF16)
+        window = pl.ds(part.start, part.stop - part.start)
+        write(up.at[window, :], out_up.at[window, :])
+    for part in blocks_of(down.shape[0]):
         rebuilt = dot(lhs[part, :], rhs[...])
         down[part, :] = (factor * rebuilt).astype(BF16)
-        error[part, :] = (g[0, part, :].astype(F32) + e[0, part, :].astype(F32) - rebuilt).astype(BF16)
-        up[part_up, :] = (factor * rebuilt_up[part_up, :]).astype(BF16)
+        error[part, :] = (merged[part, :] - rebuilt).astype(BF16)
         window = pl.ds(part.start, part.stop - part.start)
         write(down.at[window, :], out_down.at[window, :])
         write(error.at[window, :], out_error.at[0, window, :])
-        window = pl.ds(part_up.start, part_up.stop - part_up.start)
-        write(up.at[window, :], out_up.at[window, :])
     for copy in copies:
         copy.wait()
 
@@ -525,14 +528,14 @@
         name="factor_up", scratch_shapes=[wide, stage],
     )
     right_rows = from_shards([shard] * n_shards)
-    new_error_up, rebuilt_up = call(
-        error_up_kernel, [shaped(1, rows, ff, dtype=BF16), shaped(rows, ff)], gu, eu, lhs_up, rhs_up, name="error_up", flops=product // 2,
-        out_specs=[HBM, VMEM], scratch_shapes=[pltpu.VMEM((rows, ff), BF16), pltpu.SemaphoreType.DMA((STEPS,))],
+    new_error_up, rebuilt_up, merged_down = call(
+        error_up_kernel, [shaped(1, rows, ff, dtype=BF16), shaped(rows, ff), shaped(ff, rows)], gu, eu, lhs_up, rhs_up, gd, ed, name="error_up", flops=product // 2,
+        out_specs=[HBM, VMEM, VMEM], limit=16, scratch_shapes=[pltpu.VMEM((rows, ff), BF16), pltpu.SemaphoreType.DMA((STEPS,))],
     )
     limit = CLIP_RMS * (2.0 * rows * ff * n_shards) ** 0.5
     outs = [shaped(1, ff, rows, dtype=BF16), shaped(rows, ff, dtype=BF16), shaped(ff, rows, dtype=BF16)]
     new_error_down, update_up, update_down = call(
-        functools.partial(last_kernel, limit, n_shards), outs, *right_rows, inv_down, gd, ed, rebuilt_up, lhs_down, name="last",
+        functools.partial(last_kernel, limit, n_shards), outs, *right_rows, inv_down, merged_down, rebuilt_up, lhs_down, name="last",
         flops=product, limit=16, out_specs=[HBM] * 3,
         scratch_shapes=[narrow, pltpu.VMEM((4 * rank, rows), BF16)] + [pltpu.VMEM(shape, BF16) for shape in ((ff, rows), (rows, ff), (ff, rows))]
         + [pltpu.SemaphoreType.DMA((3 * STEPS,))],

time: 78.7 us -> 78.7 us (level)
  no operation moved by 1% of the time
where the time goes in v20:
time: 78.7 us; the launch traced here: 78.5 us
  waiting for transfers between devices  31.4 us (40%)
  starting transfers between devices  29 us (37%)
  Pallas kernels  16.3 us (21%)
  local copies, waits for them, and re-layouts  0.94 us (1%)
    ppermute x26, waiting for transfers between devices, swap(): return lax.ppermute(x, axis, pairs)  31.4 us
    ppermute x26, starting transfers between devices, swap(): return lax.ppermute(x, axis, pairs)  29 us
    pallas_call x18, Pallas kernels, call(): pl.pallas_call(lambda *refs: kernel(*refs[skip:]), out_shape=out_shape, i...  16.3 us
  transfers between devices with their start and end apart: 26, of which 19 were waited for; matrix products, arithmetic and copies ran while one was open for 0% of the time, Pallas kernels for 8%

profile of v20, /device:TPU:0, one launch (start us, length us, event | category | flops | bytes accessed | tf_op | source)
XLA Modules:
  0.0 78.5 jit_solution(12599189798830033694)
XLA Ops:
  0.6 0.0 copy-start.1
  0.6 5.5 %left.1 = (f32[16,512]{1,0:T(8,128)S(1)}, f32[16,512]{1,0:T(8,128)S(1)}, f32[16,512]{1,0:T(8,128)S(1)}, f32[16,512]{1,0:T(8,128)S(1)}, f32[4,8,1536]{2,1,0:T(8,128)}, /*index=5*/f32[4,8,1536]{2,1,0:T(8,128)}) custom-call(bf16[1,512,1536]{2,1,0:T(8,128)(2,1)} %refs_0_.3, bf16[1,512,1536]{2,1,0:T(8,128)(2,1)} %refs_1_.3, f32[64,1536]{1,0:T(8,128)} %bitcast.2, ...), custom_call_target="tpu_custom_call" | custom-call | flops 1610612736 | bytes 7340032 | tf_op jit(solution)/shard_map/left/pallas_call | solution.py:410
  6.2 0.0 copy-start
  6.2 3.0 %collective-permute-start.3 = (f32[4,8,1536]{2,1,0:T(8,128)}, f32[4,8,1536]{2,1,0:T(8,128)S(1)}, u32[]{:S(2)}, u32[]{:S(2)}) collective-permute-start(f32[4,8,1536]{2,1,0:T(8,128)} %get-tuple-element.50), channel_id=1, source_target_pairs={{0,4},{4,0},{8,12},{12,8},{16,20},{20,16},{24,28},{28,24},{1,5},{5... | collective-permute-start | bytes 589832 | tf_op jit(solution)/shard_map/ppermute | solution.py:419
  9.2 0.0 collective-permute-start
  9.2 1.5 %collective-permute-start.1 = (f32[16,512]{1,0:T(8,128)S(1)}, f32[16,512]{1,0:T(8,128)S(1)}, u32[]{:S(2)}, u32[]{:S(2)}) collective-permute-start(f32[16,512]{1,0:T(8,128)S(1)} %get-tuple-element.47), channel_id=1, source_target_pairs={{0,2},{1,3},{2,0},{3,1},{4,6},{5,7},{6,4},{7,5},{8,10},{9,11},{10,... | collective-permute-start | bytes 98312 | tf_op jit(solution)/shard_map/ppermute | solution.py:419
  10.7 0.4 collective-permute-start.2
  11.1 0.9 %copy-done.4 = f32[4,8,1536]{2,1,0:T(8,128)S(1)} copy-done((f32[4,8,1536]{2,1,0:T(8,128)S(1)}, f32[4,8,1536]{2,1,0:T(8,128)}, u32[]{:S(2)}) %copy-start.4) | copy-done | bytes 196632
  12.0 0.0 collective-permute-done.refs_1_
  12.0 1.1 %collective-permute-done.1.refs_2_ = f32[16,512]{1,0:T(8,128)S(1)} collective-permute-done((f32[16,512]{1,0:T(8,128)S(1)}, f32[16,512]{1,0:T(8,128)S(1)}, u32[]{:S(2)}, u32[]{:S(2)}) %collective-permute-start.1) | collective-permute-done | bytes 32800 | tf_op jit(solution)/shard_map/ppermute | solution.py:419
  13.1 0.9 %collective-permute-done.2.refs_3_ = f32[16,512]{1,0:T(8,128)S(1)} collective-permute-done((f32[16,512]{1,0:T(8,128)S(1)}, f32[16,512]{1,0:T(8,128)S(1)}, u32[]{:S(2)}, u32[]{:S(2)}) %collective-permute-start.2) | collective-permute-done | bytes 32800 | tf_op jit(solution)/shard_map/ppermute | solution.py:419
  14.0 0.3 collective-permute-done.3.refs_2_
  14.4 1.9 %collective-permute-start.4 = (f32[2,8,1536]{2,1,0:T(8,128)S(1)}, f32[2,8,1536]{2,1,0:T(8,128)S(1)}, u32[]{:S(2)}, u32[]{:S(2)}) collective-permute-start(f32[2,8,1536]{2,1,0:T(8,128)S(1)} %get-tuple-element.52), channel_id=1, source_target_pairs={{0,8},{4,12},{8,0},{12,4},{16,24},{20,28},{24,16},{28,20},{1,9},{5... | collective-permute-start | bytes 294920 | tf_op jit(solution)/shard_map/ppermute | solution.py:419
  16.2 1.5 %collective-permute-start.5 = (f32[16,512]{1,0:T(8,128)S(1)}, f32[16,512]{1,0:T(8,128)S(1)}, u32[]{:S(2)}, u32[]{:S(2)}) collective-permute-start(f32[16,512]{1,0:T(8,128)S(1)} %shard_sum.2.refs_0_), channel_id=1, source_target_pairs={{0,4},{4,0},{8,12},{12,8},{16,20},{20,16},{24,28},{28,24},{1,5},{5... | collective-permute-start | bytes 98312 | tf_op jit(solution)/shard_map/ppermute | solution.py:419
  17.7 2.4 %collective-permute-done.5.refs_1_ = f32[16,512]{1,0:T(8,128)S(1)} collective-permute-done((f32[16,512]{1,0:T(8,128)S(1)}, f32[16,512]{1,0:T(8,128)S(1)}, u32[]{:S(2)}, u32[]{:S(2)}) %collective-permute-start.5) | collective-permute-done | bytes 32800 | tf_op jit(solution)/shard_map/ppermute | solution.py:419
  20.1 0.0 collective-permute-done.4.refs_1_
  20.2 2.7 %collective-permute-start.6 = (f32[2,8,2048]{2,1,0:T(8,128)S(1)}, f32[2,8,2048]{2,1,0:T(8,128)S(1)}, u32[]{:S(2)}, u32[]{:S(2)}) collective-permute-start(f32[2,8,2048]{2,1,0:T(8,128)S(1)} %half_sum.1.refs_0_), channel_id=1, source_target_pairs={{0,16},{4,20},{8,24},{12,28},{16,0},{20,4},{24,8},{28,12},{1,17},{... | collective-permute-start | bytes 393224 | tf_op jit(solution)/shard_map/ppermute | solution.py:419
  22.8 5.4 %collective-permute-done.6.refs_1_ = f32[2,8,2048]{2,1,0:T(8,128)S(1)} collective-permute-done((f32[2,8,2048]{2,1,0:T(8,128)S(1)}, f32[2,8,2048]{2,1,0:T(8,128)S(1)}, u32[]{:S(2)}, u32[]{:S(2)}) %collective-permute-start.6) | collective-permute-done | bytes 131104 | tf_op jit(solution)/shard_map/ppermute | solution.py:419
  28.3 0.4 collective-permute-start.7
  28.7 4.6 %collective-permute-done.7.refs_1_ = f32[2,8,2048]{2,1,0:T(8,128)S(1)} collective-permute-done((f32[2,8,2048]{2,1,0:T(8,128)S(1)}, f32[2,8,2048]{2,1,0:T(8,128)S(1)}, u32[]{:S(2)}, u32[]{:S(2)}) %collective-permute-start.7) | collective-permute-done | bytes 131104 | tf_op jit(solution)/shard_map/ppermute | solution.py:419
  33.3 0.9 %collective-permute-start.8 = (f32[4,8,1536]{2,1,0:T(8,128)S(1)}, f32[4,8,1536]{2,1,0:T(8,128)S(1)}, u32[]{:S(2)}, u32[]{:S(2)}) collective-permute-start(f32[4,8,1536]{2,1,0:T(8,128)S(1)} %get-tuple-element.53.refs_1_), channel_id=1, source_target_pairs={{0,4},{4,0},{8,12},{12,8},{16,20},{20,16},{24,28},{28,24},{1,5},{5... | collective-permute-start | bytes 589832 | tf_op jit(solution)/shard_map/ppermute | solution.py:419
  34.3 0.0 collective-permute-start.11
  34.3 1.5 %collective-permute-start.10 = (f32[16,512]{1,0:T(8,128)S(1)}, f32[16,512]{1,0:T(8,128)S(1)}, u32[]{:S(2)}, u32[]{:S(2)}) collective-permute-start(f32[16,512]{1,0:T(8,128)S(1)} %get-tuple-element.54.refs_1_), channel_id=1, source_target_pairs={{0,2},{1,3},{2,0},{3,1},{4,6},{5,7},{6,4},{7,5},{8,10},{9,11},{10,... | collective-permute-start | bytes 98312 | tf_op jit(solution)/shard_map/ppermute | solution.py:419
  35.8 0.3 collective-permute-start.9
  36.1 1.8 %collective-permute-done.11.refs_4_ = f32[16,512]{1,0:T(8,128)S(1)} collective-permute-done((f32[16,512]{1,0:T(8,128)S(1)}, f32[16,512]{1,0:T(8,128)S(1)}, u32[]{:S(2)}, u32[]{:S(2)}) %collective-permute-start.11) | collective-permute-done | bytes 32800 | tf_op jit(solution)/shard_map/ppermute | solution.py:419
  37.9 0.4 collective-permute-done.10.refs_3_
  38.3 0.0 collective-permute-done.9.refs_2_
  38.3 0.8 collective-permute-done.8.refs_0_.refs_2_
  39.1 0.0 copy-done.1
  39.1 1.2 %right_up.1 = (f32[64,512]{1,0:T(8,128)S(1)}, f32[64,64]{1,0:T(8,128)S(1)}, f32[4,8,1536]{2,1,0:T(8,128)S(1)}, f32[4,8,1536]{2,1,0:T(8,128)S(1)}) custom-call(f32[4,8,1536]{2,1,0:T(8,128)S(1)} %collective-permute-done.8.refs_0_.refs_2_, f32[16,512]{1,0:T(8,128)S(1)} %get-tuple-element.54.refs_1_, f32[16,512]{1,0:T(8,128)S(1)} %collective-permute-done.9.refs_2_, ...), custom_call_target="tpu_custom_call" | custom-call | flops 805306368 | bytes 3817472 | tf_op jit(solution)/shard_map/right_up/pallas_call | solution.py:410
  40.3 0.9 %collective-permute-start.15 = (f32[4,8,1536]{2,1,0:T(8,128)S(1)}, f32[4,8,1536]{2,1,0:T(8,128)S(1)}, u32[]{:S(2)}, u32[]{:S(2)}) collective-permute-start(f32[4,8,1536]{2,1,0:T(8,128)S(1)} %get-tuple-element.64), channel_id=1, source_target_pairs={{0,4},{4,0},{8,12},{12,8},{16,20},{20,16},{24,28},{28,24},{1,5},{5... | collective-permute-start | bytes 589832 | tf_op jit(solution)/shard_map/ppermute | solution.py:419
  41.2 1.2 %right_down.1 = (f32[64,1536]{1,0:T(8,128)S(1)}, f32[16,768]{1,0:T(8,128)S(1)}, f32[16,768]{1,0:T(8,128)S(1)}, f32[16,768]{1,0:T(8,128)S(1)}, f32[16,768]{1,0:T(8,128)S(1)}) custom-call(f32[64,512]{1,0:T(8,128)S(1)} %get-tuple-element.55.refs_0_, f32[4,8,1536]{2,1,0:T(8,128)S(1)} %get-tuple-element.53.refs_1_, ...), custom_call_target="tpu_custom_call" | custom-call | flops 805306368 | bytes 4128768 | tf_op jit(solution)/shard_map/right_down/pallas_call | solution.py:410
  42.4 0.0 collective-permute-start.12
  42.4 1.6 %collective-permute-start.13 = (f32[16,768]{1,0:T(8,128)S(1)}, f32[16,768]{1,0:T(8,128)S(1)}, u32[]{:S(2)}, u32[]{:S(2)}) collective-permute-start(f32[16,768]{1,0:T(8,128)S(1)} %get-tuple-element.60), channel_id=1, source_target_pairs={{0,2},{1,3},{2,0},{3,1},{4,6},{5,7},{6,4},{7,5},{8,10},{9,11},{10,... | collective-permute-start | bytes 147464 | tf_op jit(solution)/shard_map/ppermute | solution.py:419
  44.0 0.3 collective-permute-start.14
  44.3 0.0 collective-permute-done.12.refs_1_
  44.3 2.3 %collective-permute-done.13.refs_2_ = f32[16,768]{1,0:T(8,128)S(1)} collective-permute-done((f32[16,768]{1,0:T(8,128)S(1)}, f32[16,768]{1,0:T(8,128)S(1)}, u32[]{:S(2)}, u32[]{:S(2)}) %collective-permute-start.13) | collective-permute-done | bytes 49184 | tf_op jit(solution)/shard_map/ppermute | solution.py:419
  46.6 1.1 %collective-permute-done.14.refs_3_ = f32[16,768]{1,0:T(8,128)S(1)} collective-permute-done((f32[16,768]{1,0:T(8,128)S(1)}, f32[16,768]{1,0:T(8,128)S(1)}, u32[]{:S(2)}, u32[]{:S(2)}) %collective-permute-start.14) | collective-permute-done | bytes 49184 | tf_op jit(solution)/shard_map/ppermute | solution.py:419
  47.7 0.1 shard_sum.3
  47.8 0.0 collective-permute-done.15.refs_1_
  47.8 0.1 collective-permute-start.16
  47.9 3.0 %collective-permute-start.17 = (f32[8,1792]{1,0:T(8,128)S(1)}, f32[8,1792]{1,0:T(8,128)S(1)}, u32[]{:S(2)}, u32[]{:S(2)}) collective-permute-start(f32[8,1792]{1,0:T(8,128)S(1)} %get-tuple-element.68), channel_id=1, source_target_pairs={{0,16},{4,20},{8,24},{12,28},{16,0},{20,4},{24,8},{28,12},{1,17},{... | collective-permute-start | bytes 172040 | tf_op jit(solution)/shard_map/ppermute | solution.py:419
  50.9 1.4 %collective-permute-start.18 = (f32[8,1792]{1,0:T(8,128)S(1)}, f32[8,1792]{1,0:T(8,128)S(1)}, u32[]{:S(2)}, u32[]{:S(2)}) collective-permute-start(f32[8,1792]{1,0:T(8,128)S(1)} %get-tuple-element.69), channel_id=1, source_target_pairs={{0,24},{4,28},{8,16},{12,20},{16,8},{20,12},{24,0},{28,4},{1,25},{... | collective-permute-start | bytes 172040 | tf_op jit(solution)/shard_map/ppermute | solution.py:419
  52.3 0.9 %collective-permute-done.16.refs_1_ = f32[8,1792]{1,0:T(8,128)S(1)} collective-permute-done((f32[8,1792]{1,0:T(8,128)S(1)}, f32[8,1792]{1,0:T(8,128)S(1)}, u32[]{:S(2)}, u32[]{:S(2)}) %collective-permute-start.16) | collective-permute-done | bytes 57376 | tf_op jit(solution)/shard_map/ppermute | solution.py:419
  53.2 0.2 collective-permute-done.17.refs_2_
  53.4 3.4 %collective-permute-done.18.refs_3_ = f32[8,1792]{1,0:T(8,128)S(1)} collective-permute-done((f32[8,1792]{1,0:T(8,128)S(1)}, f32[8,1792]{1,0:T(8,128)S(1)}, u32[]{:S(2)}, u32[]{:S(2)}) %collective-permute-start.18) | collective-permute-done | bytes 57376 | tf_op jit(solution)/shard_map/ppermute | solution.py:419
  56.9 2.1 %collective-permute-start.21 = (f32[8,1792]{1,0:T(8,128)S(1)}, f32[8,1792]{1,0:T(8,128)S(1)}, u32[]{:S(2)}, u32[]{:S(2)}) collective-permute-start(f32[8,1792]{1,0:T(8,128)S(1)} %replica_mean.1.refs_0_), channel_id=1, source_target_pairs={{0,24},{4,28},{8,16},{12,20},{16,8},{20,12},{24,0},{28,4},{1,25},{... | collective-permute-start | bytes 172040 | tf_op jit(solution)/shard_map/ppermute | solution.py:419
  59.0 0.0 collective-permute-start.20
  59.0 2.3 %collective-permute-start.19 = (f32[8,1792]{1,0:T(8,128)S(1)}, f32[8,1792]{1,0:T(8,128)S(1)}, u32[]{:S(2)}, u32[]{:S(2)}) collective-permute-start(f32[8,1792]{1,0:T(8,128)S(1)} %replica_mean.1.refs_0_), channel_id=1, source_target_pairs={{0,8},{4,12},{8,0},{12,4},{16,24},{20,28},{24,16},{28,20},{1,9},{5... | collective-permute-start | bytes 172040 | tf_op jit(solution)/shard_map/ppermute | solution.py:419
  61.3 1.7 %collective-permute-done.21.refs_3_ = f32[8,1792]{1,0:T(8,128)S(1)} collective-permute-done((f32[8,1792]{1,0:T(8,128)S(1)}, f32[8,1792]{1,0:T(8,128)S(1)}, u32[]{:S(2)}, u32[]{:S(2)}) %collective-permute-start.21) | collective-permute-done | bytes 57376 | tf_op jit(solution)/shard_map/ppermute | solution.py:419
  63.0 1.4 %collective-permute-done.20.refs_2_ = f32[8,1792]{1,0:T(8,128)S(1)} collective-permute-done((f32[8,1792]{1,0:T(8,128)S(1)}, f32[8,1792]{1,0:T(8,128)S(1)}, u32[]{:S(2)}, u32[]{:S(2)}) %collective-permute-start.20) | collective-permute-done | bytes 57376 | tf_op jit(solution)/shard_map/ppermute | solution.py:419
  64.4 0.0 collective-permute-done.19.refs_1_
  64.5 1.3 %collective-permute-start.22 = (f32[4,8,1792]{2,1,0:T(8,128)S(1)}, f32[4,8,1792]{2,1,0:T(8,128)S(1)}, u32[]{:S(2)}, u32[]{:S(2)}) collective-permute-start(f32[4,8,1792]{2,1,0:T(8,128)S(1)} %stack_z.1.refs_8_.refs_0_), channel_id=1, source_target_pairs={{0,4},{4,0},{8,12},{12,8},{16,20},{20,16},{24,28},{28,24},{1,5},{5... | collective-permute-start | bytes 688136 | tf_op jit(solution)/shard_map/ppermute | solution.py:419
  65.8 3.2 %basis.1 = (f32[64,64]{1,0:T(8,128)S(1)}, f32[64,64]{1,0:T(8,128)S(1)}, bf16[512,256]{1,0:T(8,128)(2,1)S(1)}, bf16[1536,256]{1,0:T(8,128)(2,1)S(1)}) custom-call(f32[64,512]{1,0:T(8,128)S(1)} %get-tuple-element.55.refs_0_, f32[64,1536]{1,0:T(8,128)S(1)} %get-tuple-element.56.refs_1_, f32[64,64]{1,0:T(8,128)S(1)} %get-tuple-element.57.refs_2_, ...), custom_call_target="tpu_custom_call" | custom-call | bytes 8159232 | tf_op jit(solution)/shard_map/basis/pallas_call | solution.py:410
  68.9 1.6 %collective-permute-done.22.refs_1_ = f32[4,8,1792]{2,1,0:T(8,128)S(1)} collective-permute-done((f32[4,8,1792]{2,1,0:T(8,128)S(1)}, f32[4,8,1792]{2,1,0:T(8,128)S(1)}, u32[]{:S(2)}, u32[]{:S(2)}) %collective-permute-start.22) | collective-permute-done | bytes 229408 | tf_op jit(solution)/shard_map/ppermute | solution.py:419
  70.6 0.7 factor_up.1
  71.2 0.1 collective-permute-start.25
  71.3 1.2 %collective-permute-start.24 = (f32[16,640]{1,0:T(8,128)S(1)}, f32[16,640]{1,0:T(8,128)S(1)}, u32[]{:S(2)}, u32[]{:S(2)}) collective-permute-start(f32[16,640]{1,0:T(8,128)S(1)} %get-tuple-element.74.refs_0_), channel_id=1, source_target_pairs={{0,2},{1,3},{2,0},{3,1},{4,6},{5,7},{6,4},{7,5},{8,10},{9,11},{10,... | collective-permute-start | bytes 122888 | tf_op jit(solution)/shard_map/ppermute | solution.py:419
  72.5 0.7 collective-permute-start.23
  73.2 1.5 %error_up.1 = (bf16[1,512,1536]{2,1,0:T(8,128)(2,1)}, f32[512,1536]{1,0:T(8,128)S(1)}, f32[1536,512]{1,0:T(8,128)S(1)}) custom-call(bf16[1,512,1536]{2,1,0:T(8,128)(2,1)S(1)} %copy-done, bf16[1,512,1536]{2,1,0:T(8,128)(2,1)S(1)} %copy-done.1, bf16[512,256]{1,0:T(8,128)(2,1)S(1)} %get-tuple-element.70.refs_2_, ...), custom_call_target="tpu_custom_call" | custom-call | flops 402653184 | bytes 15204352 | tf_op jit(solution)/shard_map/error_up/pallas_call | solution.py:410
  74.6 0.2 collective-permute-done.25.refs_3_
  74.8 0.8 %collective-permute-done.24.refs_2_ = f32[16,640]{1,0:T(8,128)S(1)} collective-permute-done((f32[16,640]{1,0:T(8,128)S(1)}, f32[16,640]{1,0:T(8,128)S(1)}, u32[]{:S(2)}, u32[]{:S(2)}) %collective-permute-start.24) | collective-permute-done | bytes 40992 | tf_op jit(solution)/shard_map/ppermute | solution.py:419
  75.7 0.0 collective-permute-done.23.refs_1_
  75.7 2.8 %last.1 = (bf16[1,1536,512]{2,1,0:T(8,128)(2,1)}, bf16[512,1536]{1,0:T(8,128)(2,1)}, bf16[1536,512]{1,0:T(8,128)(2,1)}) custom-call(f32[16,640]{1,0:T(8,128)S(1)} %get-tuple-element.74.refs_0_, f32[16,640]{1,0:T(8,128)S(1)} %collective-permute-done.23.refs_1_, f32[16,640]{1,0:T(8,128)S(1)} %collective-permute-done.24.refs_2_, ...), custom_call_target="tpu_custom_call" | custom-call | flops 805306368 | bytes 11976704 | tf_op jit(solution)/shard_map/last/pallas_call | solution.py:410
  (16 shorter events, 0.2 us)
Async XLA Ops:
  0.6 38.5 %copy-start.1 = (bf16[1,512,1536]{2,1,0:T(8,128)(2,1)S(1)}, bf16[1,512,1536]{2,1,0:T(8,128)(2,1)}, u32[]{:S(2)}) copy-start(bf16[1,512,1536]{2,1,0:T(8,128)(2,1)} %refs_1_.3) | copy-start | bytes 4718596
  6.2 32.9 %copy-start = (bf16[1,512,1536]{2,1,0:T(8,128)(2,1)S(1)}, bf16[1,512,1536]{2,1,0:T(8,128)(2,1)}, u32[]{:S(2)}) copy-start(bf16[1,512,1536]{2,1,0:T(8,128)(2,1)} %refs_0_.3) | copy-start | bytes 4718596
  6.2 8.1 %collective-permute-start.3 = (f32[4,8,1536]{2,1,0:T(8,128)}, f32[4,8,1536]{2,1,0:T(8,128)S(1)}, u32[]{:S(2)}, u32[]{:S(2)}) collective-permute-start(f32[4,8,1536]{2,1,0:T(8,128)} %get-tuple-element.50), channel_id=1, source_target_pairs={{0,4},{4,0},{8,12},{12,8},{16,20},{20,16},{24,28},{28,24},{1,5},{5... | collective-permute-start | bytes 589832 | tf_op jit(solution)/shard_map/ppermute | solution.py:419
  9.2 2.8 %collective-permute-start = (f32[16,512]{1,0:T(8,128)S(1)}, f32[16,512]{1,0:T(8,128)S(1)}, u32[]{:S(2)}, u32[]{:S(2)}) collective-permute-start(f32[16,512]{1,0:T(8,128)S(1)} %get-tuple-element.46), channel_id=1, source_target_pairs={{0,1},{1,0},{2,3},{3,2},{4,5},{5,4},{6,7},{7,6},{8,9},{9,8},{10,11... | collective-permute-start | bytes 98312 | tf_op jit(solution)/shard_map/ppermute | solution.py:419
  9.2 3.9 %collective-permute-start.1 = (f32[16,512]{1,0:T(8,128)S(1)}, f32[16,512]{1,0:T(8,128)S(1)}, u32[]{:S(2)}, u32[]{:S(2)}) collective-permute-start(f32[16,512]{1,0:T(8,128)S(1)} %get-tuple-element.47), channel_id=1, source_target_pairs={{0,2},{1,3},{2,0},{3,1},{4,6},{5,7},{6,4},{7,5},{8,10},{9,11},{10,... | collective-permute-start | bytes 98312 | tf_op jit(solution)/shard_map/ppermute | solution.py:419
  10.7 3.3 %collective-permute-start.2 = (f32[16,512]{1,0:T(8,128)S(1)}, f32[16,512]{1,0:T(8,128)S(1)}, u32[]{:S(2)}, u32[]{:S(2)}) collective-permute-start(f32[16,512]{1,0:T(8,128)S(1)} %get-tuple-element.48), channel_id=1, source_target_pairs={{0,3},{1,2},{2,1},{3,0},{4,7},{5,6},{6,5},{7,4},{8,11},{9,10},{10,... | collective-permute-start | bytes 98312 | tf_op jit(solution)/shard_map/ppermute | solution.py:419
  11.1 0.9 %copy-start.4 = (f32[4,8,1536]{2,1,0:T(8,128)S(1)}, f32[4,8,1536]{2,1,0:T(8,128)}, u32[]{:S(2)}) copy-start(f32[4,8,1536]{2,1,0:T(8,128)} %get-tuple-element.44.refs_1_) | copy-start | bytes 589828
  14.4 5.8 %collective-permute-start.4 = (f32[2,8,1536]{2,1,0:T(8,128)S(1)}, f32[2,8,1536]{2,1,0:T(8,128)S(1)}, u32[]{:S(2)}, u32[]{:S(2)}) collective-permute-start(f32[2,8,1536]{2,1,0:T(8,128)S(1)} %get-tuple-element.52), channel_id=1, source_target_pairs={{0,8},{4,12},{8,0},{12,4},{16,24},{20,28},{24,16},{28,20},{1,9},{5... | collective-permute-start | bytes 294920 | tf_op jit(solution)/shard_map/ppermute | solution.py:419
  16.2 3.9 %collective-permute-start.5 = (f32[16,512]{1,0:T(8,128)S(1)}, f32[16,512]{1,0:T(8,128)S(1)}, u32[]{:S(2)}, u32[]{:S(2)}) collective-permute-start(f32[16,512]{1,0:T(8,128)S(1)} %shard_sum.2.refs_0_), channel_id=1, source_target_pairs={{0,4},{4,0},{8,12},{12,8},{16,20},{20,16},{24,28},{28,24},{1,5},{5... | collective-permute-start | bytes 98312 | tf_op jit(solution)/shard_map/ppermute | solution.py:419
  20.2 8.1 %collective-permute-start.6 = (f32[2,8,2048]{2,1,0:T(8,128)S(1)}, f32[2,8,2048]{2,1,0:T(8,128)S(1)}, u32[]{:S(2)}, u32[]{:S(2)}) collective-permute-start(f32[2,8,2048]{2,1,0:T(8,128)S(1)} %half_sum.1.refs_0_), channel_id=1, source_target_pairs={{0,16},{4,20},{8,24},{12,28},{16,0},{20,4},{24,8},{28,12},{1,17},{... | collective-permute-start | bytes 393224 | tf_op jit(solution)/shard_map/ppermute | solution.py:419
  28.3 5.0 %collective-permute-start.7 = (f32[2,8,2048]{2,1,0:T(8,128)S(1)}, f32[2,8,2048]{2,1,0:T(8,128)S(1)}, u32[]{:S(2)}, u32[]{:S(2)}) collective-permute-start(f32[2,8,2048]{2,1,0:T(8,128)S(1)} %mean.1.refs_0_), channel_id=1, source_target_pairs={{0,8},{4,12},{8,0},{12,4},{16,24},{20,28},{24,16},{28,20},{1,9},{5... | collective-permute-start | bytes 393224 | tf_op jit(solution)/shard_map/ppermute | solution.py:419
  33.3 5.7 %collective-permute-start.8 = (f32[4,8,1536]{2,1,0:T(8,128)S(1)}, f32[4,8,1536]{2,1,0:T(8,128)S(1)}, u32[]{:S(2)}, u32[]{:S(2)}) collective-permute-start(f32[4,8,1536]{2,1,0:T(8,128)S(1)} %get-tuple-element.53.refs_1_), channel_id=1, source_target_pairs={{0,4},{4,0},{8,12},{12,8},{16,20},{20,16},{24,28},{28,24},{1,5},{5... | collective-permute-start | bytes 589832 | tf_op jit(solution)/shard_map/ppermute | solution.py:419
  34.3 7.0 %copy-start.2 = (bf16[1,1536,512]{2,1,0:T(8,128)(2,1)S(1)}, bf16[1,1536,512]{2,1,0:T(8,128)(2,1)}, u32[]{:S(2)}) copy-start(bf16[1,1536,512]{2,1,0:T(8,128)(2,1)} %refs_4_.7) | copy-start | bytes 4718596
  34.3 7.0 %copy-start.3 = (bf16[1,1536,512]{2,1,0:T(8,128)(2,1)S(1)}, bf16[1,1536,512]{2,1,0:T(8,128)(2,1)}, u32[]{:S(2)}) copy-start(bf16[1,1536,512]{2,1,0:T(8,128)(2,1)} %refs_5_.5) | copy-start | bytes 4718596
  34.3 3.6 %collective-permute-start.11 = (f32[16,512]{1,0:T(8,128)S(1)}, f32[16,512]{1,0:T(8,128)S(1)}, u32[]{:S(2)}, u32[]{:S(2)}) collective-permute-start(f32[16,512]{1,0:T(8,128)S(1)} %get-tuple-element.54.refs_1_), channel_id=1, source_target_pairs={{0,3},{1,2},{2,1},{3,0},{4,7},{5,6},{6,5},{7,4},{8,11},{9,10},{10,... | collective-permute-start | bytes 98312 | tf_op jit(solution)/shard_map/ppermute | solution.py:419
  34.3 4.0 %collective-permute-start.10 = (f32[16,512]{1,0:T(8,128)S(1)}, f32[16,512]{1,0:T(8,128)S(1)}, u32[]{:S(2)}, u32[]{:S(2)}) collective-permute-start(f32[16,512]{1,0:T(8,128)S(1)} %get-tuple-element.54.refs_1_), channel_id=1, source_target_pairs={{0,2},{1,3},{2,0},{3,1},{4,6},{5,7},{6,4},{7,5},{8,10},{9,11},{10,... | collective-permute-start | bytes 98312 | tf_op jit(solution)/shard_map/ppermute | solution.py:419
  35.8 2.5 %collective-permute-start.9 = (f32[16,512]{1,0:T(8,128)S(1)}, f32[16,512]{1,0:T(8,128)S(1)}, u32[]{:S(2)}, u32[]{:S(2)}) collective-permute-start(f32[16,512]{1,0:T(8,128)S(1)} %get-tuple-element.54.refs_1_), channel_id=1, source_target_pairs={{0,1},{1,0},{2,3},{3,2},{4,5},{5,4},{6,7},{7,6},{8,9},{9,8},{10,11... | collective-permute-start | bytes 98312 | tf_op jit(solution)/shard_map/ppermute | solution.py:419
  40.3 7.5 %collective-permute-start.15 = (f32[4,8,1536]{2,1,0:T(8,128)S(1)}, f32[4,8,1536]{2,1,0:T(8,128)S(1)}, u32[]{:S(2)}, u32[]{:S(2)}) collective-permute-start(f32[4,8,1536]{2,1,0:T(8,128)S(1)} %get-tuple-element.64), channel_id=1, source_target_pairs={{0,4},{4,0},{8,12},{12,8},{16,20},{20,16},{24,28},{28,24},{1,5},{5... | collective-permute-start | bytes 589832 | tf_op jit(solution)/shard_map/ppermute | solution.py:419
  42.4 1.9 %collective-permute-start.12 = (f32[16,768]{1,0:T(8,128)S(1)}, f32[16,768]{1,0:T(8,128)S(1)}, u32[]{:S(2)}, u32[]{:S(2)}) collective-permute-start(f32[16,768]{1,0:T(8,128)S(1)} %get-tuple-element.59), channel_id=1, source_target_pairs={{0,1},{1,0},{2,3},{3,2},{4,5},{5,4},{6,7},{7,6},{8,9},{9,8},{10,11... | collective-permute-start | bytes 147464 | tf_op jit(solution)/shard_map/ppermute | solution.py:419
  42.4 4.2 %collective-permute-start.13 = (f32[16,768]{1,0:T(8,128)S(1)}, f32[16,768]{1,0:T(8,128)S(1)}, u32[]{:S(2)}, u32[]{:S(2)}) collective-permute-start(f32[16,768]{1,0:T(8,128)S(1)} %get-tuple-element.60), channel_id=1, source_target_pairs={{0,2},{1,3},{2,0},{3,1},{4,6},{5,7},{6,4},{7,5},{8,10},{9,11},{10,... | collective-permute-start | bytes 147464 | tf_op jit(solution)/shard_map/ppermute | solution.py:419
  44.0 3.7 %collective-permute-start.14 = (f32[16,768]{1,0:T(8,128)S(1)}, f32[16,768]{1,0:T(8,128)S(1)}, u32[]{:S(2)}, u32[]{:S(2)}) collective-permute-start(f32[16,768]{1,0:T(8,128)S(1)} %get-tuple-element.61), channel_id=1, source_target_pairs={{0,3},{1,2},{2,1},{3,0},{4,7},{5,6},{6,5},{7,4},{8,11},{9,10},{10,... | collective-permute-start | bytes 147464 | tf_op jit(solution)/shard_map/ppermute | solution.py:419
  47.8 5.4 %collective-permute-start.16 = (f32[8,1792]{1,0:T(8,128)S(1)}, f32[8,1792]{1,0:T(8,128)S(1)}, u32[]{:S(2)}, u32[]{:S(2)}) collective-permute-start(f32[8,1792]{1,0:T(8,128)S(1)} %get-tuple-element.67), channel_id=1, source_target_pairs={{0,8},{4,12},{8,0},{12,4},{16,24},{20,28},{24,16},{28,20},{1,9},{5... | collective-permute-start | bytes 172040 | tf_op jit(solution)/shard_map/ppermute | solution.py:419
  47.9 5.5 %collective-permute-start.17 = (f32[8,1792]{1,0:T(8,128)S(1)}, f32[8,1792]{1,0:T(8,128)S(1)}, u32[]{:S(2)}, u32[]{:S(2)}) collective-permute-start(f32[8,1792]{1,0:T(8,128)S(1)} %get-tuple-element.68), channel_id=1, source_target_pairs={{0,16},{4,20},{8,24},{12,28},{16,0},{20,4},{24,8},{28,12},{1,17},{... | collective-permute-start | bytes 172040 | tf_op jit(solution)/shard_map/ppermute | solution.py:419
  50.9 6.0 %collective-permute-start.18 = (f32[8,1792]{1,0:T(8,128)S(1)}, f32[8,1792]{1,0:T(8,128)S(1)}, u32[]{:S(2)}, u32[]{:S(2)}) collective-permute-start(f32[8,1792]{1,0:T(8,128)S(1)} %get-tuple-element.69), channel_id=1, source_target_pairs={{0,24},{4,28},{8,16},{12,20},{16,8},{20,12},{24,0},{28,4},{1,25},{... | collective-permute-start | bytes 172040 | tf_op jit(solution)/shard_map/ppermute | solution.py:419
  56.9 6.1 %collective-permute-start.21 = (f32[8,1792]{1,0:T(8,128)S(1)}, f32[8,1792]{1,0:T(8,128)S(1)}, u32[]{:S(2)}, u32[]{:S(2)}) collective-permute-start(f32[8,1792]{1,0:T(8,128)S(1)} %replica_mean.1.refs_0_), channel_id=1, source_target_pairs={{0,24},{4,28},{8,16},{12,20},{16,8},{20,12},{24,0},{28,4},{1,25},{... | collective-permute-start | bytes 172040 | tf_op jit(solution)/shard_map/ppermute | solution.py:419
  59.0 5.4 %collective-permute-start.20 = (f32[8,1792]{1,0:T(8,128)S(1)}, f32[8,1792]{1,0:T(8,128)S(1)}, u32[]{:S(2)}, u32[]{:S(2)}) collective-permute-start(f32[8,1792]{1,0:T(8,128)S(1)} %replica_mean.1.refs_0_), channel_id=1, source_target_pairs={{0,16},{4,20},{8,24},{12,28},{16,0},{20,4},{24,8},{28,12},{1,17},{... | collective-permute-start | bytes 172040 | tf_op jit(solution)/shard_map/ppermute | solution.py:419
  59.0 5.4 %collective-permute-start.19 = (f32[8,1792]{1,0:T(8,128)S(1)}, f32[8,1792]{1,0:T(8,128)S(1)}, u32[]{:S(2)}, u32[]{:S(2)}) collective-permute-start(f32[8,1792]{1,0:T(8,128)S(1)} %replica_mean.1.refs_0_), channel_id=1, source_target_pairs={{0,8},{4,12},{8,0},{12,4},{16,24},{20,28},{24,16},{28,20},{1,9},{5... | collective-permute-start | bytes 172040 | tf_op jit(solution)/shard_map/ppermute | solution.py:419
  64.5 6.1 %collective-permute-start.22 = (f32[4,8,1792]{2,1,0:T(8,128)S(1)}, f32[4,8,1792]{2,1,0:T(8,128)S(1)}, u32[]{:S(2)}, u32[]{:S(2)}) collective-permute-start(f32[4,8,1792]{2,1,0:T(8,128)S(1)} %stack_z.1.refs_8_.refs_0_), channel_id=1, source_target_pairs={{0,4},{4,0},{8,12},{12,8},{16,20},{20,16},{24,28},{28,24},{1,5},{5... | collective-permute-start | bytes 688136 | tf_op jit(solution)/shard_map/ppermute | solution.py:419
  71.2 3.6 %collective-permute-start.25 = (f32[16,640]{1,0:T(8,128)S(1)}, f32[16,640]{1,0:T(8,128)S(1)}, u32[]{:S(2)}, u32[]{:S(2)}) collective-permute-start(f32[16,640]{1,0:T(8,128)S(1)} %get-tuple-element.74.refs_0_), channel_id=1, source_target_pairs={{0,3},{1,2},{2,1},{3,0},{4,7},{5,6},{6,5},{7,4},{8,11},{9,10},{10,... | collective-permute-start | bytes 122888 | tf_op jit(solution)/shard_map/ppermute | solution.py:419
  71.3 4.3 %collective-permute-start.24 = (f32[16,640]{1,0:T(8,128)S(1)}, f32[16,640]{1,0:T(8,128)S(1)}, u32[]{:S(2)}, u32[]{:S(2)}) collective-permute-start(f32[16,640]{1,0:T(8,128)S(1)} %get-tuple-element.74.refs_0_), channel_id=1, source_target_pairs={{0,2},{1,3},{2,0},{3,1},{4,6},{5,7},{6,4},{7,5},{8,10},{9,11},{10,... | collective-permute-start | bytes 122888 | tf_op jit(solution)/shard_map/ppermute | solution.py:419
  72.5 3.2 %collective-permute-start.23 = (f32[16,640]{1,0:T(8,128)S(1)}, f32[16,640]{1,0:T(8,128)S(1)}, u32[]{:S(2)}, u32[]{:S(2)}) collective-permute-start(f32[16,640]{1,0:T(8,128)S(1)} %get-tuple-element.74.refs_0_), channel_id=1, source_target_pairs={{0,1},{1,0},{2,3},{3,2},{4,5},{5,4},{6,7},{7,6},{8,9},{9,8},{10,11... | collective-permute-start | bytes 122888 | tf_op jit(solution)/shard_map/ppermute | solution.py:419

commit v21 on v20

--- a/solution.py
+++ b/solution.py
@@ -466,7 +466,8 @@
     stage = pltpu.VMEM((half, *piece.shape), F32)
     parts = call(split_z_kernel, [piece] * half, keep, got, shard, name="split_z", scratch_shapes=[stage])
     parts = [parts[0], *parts[:0:-1]]
-    mean = call(functools.partial(mean_kernel, n_dp), piece, *from_z(parts), name="replica_mean")
+    parts = from_z(parts)
+    mean = call(functools.partial(mean_kernel, n_dp), piece, parts[0], *parts[:0:-1], name="replica_mean")
     return from_z([mean] * half)
 
 

time: 78.7 us -> 80.2 us (1.019)
  waiting for transfers between devices: 31.4 us -> 32.8 us
    ppermute x26, waiting for transfers between devices: 31.4 us -> 32.8 us  [swap(): return lax.ppermute(x, axis, pairs)]
  transfers between devices with their start and end apart: 26 -> 26, of which waited for: 19 -> 18; matrix products, arithmetic and copies ran while one was open for 0% -> 0% of each run, Pallas kernels for 8% -> 7%
where the time goes in v21:
time: 80.2 us; the launch traced here: 80 us
  waiting for transfers between devices  32.8 us (41%)
  starting transfers between devices  29.1 us (36%)
  Pallas kernels  16.3 us (20%)
  local copies, waits for them, and re-layouts  0.94 us (1%)
    ppermute x26, waiting for transfers between devices, swap(): return lax.ppermute(x, axis, pairs)  32.8 us
    ppermute x26, starting transfers between devices, swap(): return lax.ppermute(x, axis, pairs)  29.1 us
    pallas_call x18, Pallas kernels, call(): pl.pallas_call(lambda *refs: kernel(*refs[skip:]), out_shape=out_shape, i...  16.3 us
  transfers between devices with their start and end apart: 26, of which 18 were waited for; matrix products, arithmetic and copies ran while one was open for 0% of the time, Pallas kernels for 7%

profile of v21, /device:TPU:0, one launch (start us, length us, event | category | flops | bytes accessed | tf_op | source)
XLA Modules:
  0.0 80.0 jit_solution(3237440644039385431)
XLA Ops:
  0.6 0.0 copy-start.1
  0.6 5.5 %left.1 = (f32[16,512]{1,0:T(8,128)S(1)}, f32[16,512]{1,0:T(8,128)S(1)}, f32[16,512]{1,0:T(8,128)S(1)}, f32[16,512]{1,0:T(8,128)S(1)}, f32[4,8,1536]{2,1,0:T(8,128)}, /*index=5*/f32[4,8,1536]{2,1,0:T(8,128)}) custom-call(bf16[1,512,1536]{2,1,0:T(8,128)(2,1)} %refs_0_.3, bf16[1,512,1536]{2,1,0:T(8,128)(2,1)} %refs_1_.3, f32[64,1536]{1,0:T(8,128)} %bitcast.2, ...), custom_call_target="tpu_custom_call" | custom-call | flops 1610612736 | bytes 7340032 | tf_op jit(solution)/shard_map/left/pallas_call | solution.py:410
  6.2 0.0 copy-start
  6.2 3.0 %collective-permute-start.3 = (f32[4,8,1536]{2,1,0:T(8,128)}, f32[4,8,1536]{2,1,0:T(8,128)S(1)}, u32[]{:S(2)}, u32[]{:S(2)}) collective-permute-start(f32[4,8,1536]{2,1,0:T(8,128)} %get-tuple-element.50), channel_id=1, source_target_pairs={{0,4},{4,0},{8,12},{12,8},{16,20},{20,16},{24,28},{28,24},{1,5},{5... | collective-permute-start | bytes 589832 | tf_op jit(solution)/shard_map/ppermute | solution.py:419
  9.2 0.0 collective-permute-start
  9.2 1.5 %collective-permute-start.1 = (f32[16,512]{1,0:T(8,128)S(1)}, f32[16,512]{1,0:T(8,128)S(1)}, u32[]{:S(2)}, u32[]{:S(2)}) collective-permute-start(f32[16,512]{1,0:T(8,128)S(1)} %get-tuple-element.47), channel_id=1, source_target_pairs={{0,2},{1,3},{2,0},{3,1},{4,6},{5,7},{6,4},{7,5},{8,10},{9,11},{10,... | collective-permute-start | bytes 98312 | tf_op jit(solution)/shard_map/ppermute | solution.py:419
  10.7 0.4 collective-permute-start.2
  11.1 0.9 %copy-done.4 = f32[4,8,1536]{2,1,0:T(8,128)S(1)} copy-done((f32[4,8,1536]{2,1,0:T(8,128)S(1)}, f32[4,8,1536]{2,1,0:T(8,128)}, u32[]{:S(2)}) %copy-start.4) | copy-done | bytes 196632
  12.0 0.0 collective-permute-done.refs_1_
  12.0 1.1 %collective-permute-done.1.refs_2_ = f32[16,512]{1,0:T(8,128)S(1)} collective-permute-done((f32[16,512]{1,0:T(8,128)S(1)}, f32[16,512]{1,0:T(8,128)S(1)}, u32[]{:S(2)}, u32[]{:S(2)}) %collective-permute-start.1) | collective-permute-done | bytes 32800 | tf_op jit(solution)/shard_map/ppermute | solution.py:419
  13.1 0.9 %collective-permute-done.2.refs_3_ = f32[16,512]{1,0:T(8,128)S(1)} collective-permute-done((f32[16,512]{1,0:T(8,128)S(1)}, f32[16,512]{1,0:T(8,128)S(1)}, u32[]{:S(2)}, u32[]{:S(2)}) %collective-permute-start.2) | collective-permute-done | bytes 32800 | tf_op jit(solution)/shard_map/ppermute | solution.py:419
  14.0 0.3 collective-permute-done.3.refs_2_
  14.4 1.9 %collective-permute-start.4 = (f32[2,8,1536]{2,1,0:T(8,128)S(1)}, f32[2,8,1536]{2,1,0:T(8,128)S(1)}, u32[]{:S(2)}, u32[]{:S(2)}) collective-permute-start(f32[2,8,1536]{2,1,0:T(8,128)S(1)} %get-tuple-element.52), channel_id=1, source_target_pairs={{0,8},{4,12},{8,0},{12,4},{16,24},{20,28},{24,16},{28,20},{1,9},{5... | collective-permute-start | bytes 294920 | tf_op jit(solution)/shard_map/ppermute | solution.py:419
  16.2 1.5 %collective-permute-start.5 = (f32[16,512]{1,0:T(8,128)S(1)}, f32[16,512]{1,0:T(8,128)S(1)}, u32[]{:S(2)}, u32[]{:S(2)}) collective-permute-start(f32[16,512]{1,0:T(8,128)S(1)} %shard_sum.2.refs_0_), channel_id=1, source_target_pairs={{0,4},{4,0},{8,12},{12,8},{16,20},{20,16},{24,28},{28,24},{1,5},{5... | collective-permute-start | bytes 98312 | tf_op jit(solution)/shard_map/ppermute | solution.py:419
  17.7 2.4 %collective-permute-done.5.refs_1_ = f32[16,512]{1,0:T(8,128)S(1)} collective-permute-done((f32[16,512]{1,0:T(8,128)S(1)}, f32[16,512]{1,0:T(8,128)S(1)}, u32[]{:S(2)}, u32[]{:S(2)}) %collective-permute-start.5) | collective-permute-done | bytes 32800 | tf_op jit(solution)/shard_map/ppermute | solution.py:419
  20.1 0.0 collective-permute-done.4.refs_1_
  20.2 2.7 %collective-permute-start.6 = (f32[2,8,2048]{2,1,0:T(8,128)S(1)}, f32[2,8,2048]{2,1,0:T(8,128)S(1)}, u32[]{:S(2)}, u32[]{:S(2)}) collective-permute-start(f32[2,8,2048]{2,1,0:T(8,128)S(1)} %half_sum.1.refs_0_), channel_id=1, source_target_pairs={{0,16},{4,20},{8,24},{12,28},{16,0},{20,4},{24,8},{28,12},{1,17},{... | collective-permute-start | bytes 393224 | tf_op jit(solution)/shard_map/ppermute | solution.py:419
  22.8 5.4 %collective-permute-done.6.refs_1_ = f32[2,8,2048]{2,1,0:T(8,128)S(1)} collective-permute-done((f32[2,8,2048]{2,1,0:T(8,128)S(1)}, f32[2,8,2048]{2,1,0:T(8,128)S(1)}, u32[]{:S(2)}, u32[]{:S(2)}) %collective-permute-start.6) | collective-permute-done | bytes 131104 | tf_op jit(solution)/shard_map/ppermute | solution.py:419
  28.3 0.4 collective-permute-start.7
  28.7 4.6 %collective-permute-done.7.refs_1_ = f32[2,8,2048]{2,1,0:T(8,128)S(1)} collective-permute-done((f32[2,8,2048]{2,1,0:T(8,128)S(1)}, f32[2,8,2048]{2,1,0:T(8,128)S(1)}, u32[]{:S(2)}, u32[]{:S(2)}) %collective-permute-start.7) | collective-permute-done | bytes 131104 | tf_op jit(solution)/shard_map/ppermute | solution.py:419
  33.3 0.9 %collective-permute-start.8 = (f32[4,8,1536]{2,1,0:T(8,128)S(1)}, f32[4,8,1536]{2,1,0:T(8,128)S(1)}, u32[]{:S(2)}, u32[]{:S(2)}) collective-permute-start(f32[4,8,1536]{2,1,0:T(8,128)S(1)} %get-tuple-element.53.refs_1_), channel_id=1, source_target_pairs={{0,4},{4,0},{8,12},{12,8},{16,20},{20,16},{24,28},{28,24},{1,5},{5... | collective-permute-start | bytes 589832 | tf_op jit(solution)/shard_map/ppermute | solution.py:419
  34.3 0.0 collective-permute-start.11
  34.3 1.5 %collective-permute-start.10 = (f32[16,512]{1,0:T(8,128)S(1)}, f32[16,512]{1,0:T(8,128)S(1)}, u32[]{:S(2)}, u32[]{:S(2)}) collective-permute-start(f32[16,512]{1,0:T(8,128)S(1)} %get-tuple-element.54.refs_1_), channel_id=1, source_target_pairs={{0,2},{1,3},{2,0},{3,1},{4,6},{5,7},{6,4},{7,5},{8,10},{9,11},{10,... | collective-permute-start | bytes 98312 | tf_op jit(solution)/shard_map/ppermute | solution.py:419
  35.8 0.3 collective-permute-start.9
  36.1 1.8 %collective-permute-done.11.refs_4_ = f32[16,512]{1,0:T(8,128)S(1)} collective-permute-done((f32[16,512]{1,0:T(8,128)S(1)}, f32[16,512]{1,0:T(8,128)S(1)}, u32[]{:S(2)}, u32[]{:S(2)}) %collective-permute-start.11) | collective-permute-done | bytes 32800 | tf_op jit(solution)/shard_map/ppermute | solution.py:419
  37.9 0.4 collective-permute-done.10.refs_3_
  38.3 0.0 collective-permute-done.9.refs_2_
  38.3 0.8 collective-permute-done.8.refs_0_.refs_2_
  39.1 0.0 copy-done.1
  39.1 1.2 %right_up.1 = (f32[64,512]{1,0:T(8,128)S(1)}, f32[64,64]{1,0:T(8,128)S(1)}, f32[4,8,1536]{2,1,0:T(8,128)S(1)}, f32[4,8,1536]{2,1,0:T(8,128)S(1)}) custom-call(f32[4,8,1536]{2,1,0:T(8,128)S(1)} %collective-permute-done.8.refs_0_.refs_2_, f32[16,512]{1,0:T(8,128)S(1)} %get-tuple-element.54.refs_1_, f32[16,512]{1,0:T(8,128)S(1)} %collective-permute-done.9.refs_2_, ...), custom_call_target="tpu_custom_call" | custom-call | flops 805306368 | bytes 3817472 | tf_op jit(solution)/shard_map/right_up/pallas_call | solution.py:410
  40.3 0.9 %collective-permute-start.15 = (f32[4,8,1536]{2,1,0:T(8,128)S(1)}, f32[4,8,1536]{2,1,0:T(8,128)S(1)}, u32[]{:S(2)}, u32[]{:S(2)}) collective-permute-start(f32[4,8,1536]{2,1,0:T(8,128)S(1)} %get-tuple-element.64), channel_id=1, source_target_pairs={{0,4},{4,0},{8,12},{12,8},{16,20},{20,16},{24,28},{28,24},{1,5},{5... | collective-permute-start | bytes 589832 | tf_op jit(solution)/shard_map/ppermute | solution.py:419
  41.2 1.2 %right_down.1 = (f32[64,1536]{1,0:T(8,128)S(1)}, f32[16,768]{1,0:T(8,128)S(1)}, f32[16,768]{1,0:T(8,128)S(1)}, f32[16,768]{1,0:T(8,128)S(1)}, f32[16,768]{1,0:T(8,128)S(1)}) custom-call(f32[64,512]{1,0:T(8,128)S(1)} %get-tuple-element.55.refs_0_, f32[4,8,1536]{2,1,0:T(8,128)S(1)} %get-tuple-element.53.refs_1_, ...), custom_call_target="tpu_custom_call" | custom-call | flops 805306368 | bytes 4128768 | tf_op jit(solution)/shard_map/right_down/pallas_call | solution.py:410
  42.4 0.0 collective-permute-start.12
  42.4 1.6 %collective-permute-start.13 = (f32[16,768]{1,0:T(8,128)S(1)}, f32[16,768]{1,0:T(8,128)S(1)}, u32[]{:S(2)}, u32[]{:S(2)}) collective-permute-start(f32[16,768]{1,0:T(8,128)S(1)} %get-tuple-element.60), channel_id=1, source_target_pairs={{0,2},{1,3},{2,0},{3,1},{4,6},{5,7},{6,4},{7,5},{8,10},{9,11},{10,... | collective-permute-start | bytes 147464 | tf_op jit(solution)/shard_map/ppermute | solution.py:419
  44.0 0.3 collective-permute-start.14
  44.3 0.0 collective-permute-done.12.refs_1_
  44.3 2.3 %collective-permute-done.13.refs_2_ = f32[16,768]{1,0:T(8,128)S(1)} collective-permute-done((f32[16,768]{1,0:T(8,128)S(1)}, f32[16,768]{1,0:T(8,128)S(1)}, u32[]{:S(2)}, u32[]{:S(2)}) %collective-permute-start.13) | collective-permute-done | bytes 49184 | tf_op jit(solution)/shard_map/ppermute | solution.py:419
  46.6 1.1 %collective-permute-done.14.refs_3_ = f32[16,768]{1,0:T(8,128)S(1)} collective-permute-done((f32[16,768]{1,0:T(8,128)S(1)}, f32[16,768]{1,0:T(8,128)S(1)}, u32[]{:S(2)}, u32[]{:S(2)}) %collective-permute-start.14) | collective-permute-done | bytes 49184 | tf_op jit(solution)/shard_map/ppermute | solution.py:419
  47.7 0.1 shard_sum.3
  47.8 0.0 collective-permute-done.15.refs_1_
  47.8 2.5 %collective-permute-start.16 = (f32[8,1792]{1,0:T(8,128)S(1)}, f32[8,1792]{1,0:T(8,128)S(1)}, u32[]{:S(2)}, u32[]{:S(2)}) collective-permute-start(f32[8,1792]{1,0:T(8,128)S(1)} %get-tuple-element.67), channel_id=1, source_target_pairs={{0,24},{4,28},{8,16},{12,20},{16,8},{20,12},{24,0},{28,4},{1,25},{... | collective-permute-start | bytes 172040 | tf_op jit(solution)/shard_map/ppermute | solution.py:419
  50.3 0.0 collective-permute-start.17
  50.3 2.0 %collective-permute-start.18 = (f32[8,1792]{1,0:T(8,128)S(1)}, f32[8,1792]{1,0:T(8,128)S(1)}, u32[]{:S(2)}, u32[]{:S(2)}) collective-permute-start(f32[8,1792]{1,0:T(8,128)S(1)} %get-tuple-element.69), channel_id=1, source_target_pairs={{0,8},{4,12},{8,0},{12,4},{16,24},{20,28},{24,16},{28,20},{1,9},{5... | collective-permute-start | bytes 172040 | tf_op jit(solution)/shard_map/ppermute | solution.py:419
  52.3 2.2 %collective-permute-done.16.refs_1_ = f32[8,1792]{1,0:T(8,128)S(1)} collective-permute-done((f32[8,1792]{1,0:T(8,128)S(1)}, f32[8,1792]{1,0:T(8,128)S(1)}, u32[]{:S(2)}, u32[]{:S(2)}) %collective-permute-start.16) | collective-permute-done | bytes 57376 | tf_op jit(solution)/shard_map/ppermute | solution.py:419
  54.5 1.8 %collective-permute-done.17.refs_2_ = f32[8,1792]{1,0:T(8,128)S(1)} collective-permute-done((f32[8,1792]{1,0:T(8,128)S(1)}, f32[8,1792]{1,0:T(8,128)S(1)}, u32[]{:S(2)}, u32[]{:S(2)}) %collective-permute-start.17) | collective-permute-done | bytes 57376 | tf_op jit(solution)/shard_map/ppermute | solution.py:419
  56.3 0.0 collective-permute-done.18.refs_3_
  56.3 2.4 %collective-permute-start.21 = (f32[8,1792]{1,0:T(8,128)S(1)}, f32[8,1792]{1,0:T(8,128)S(1)}, u32[]{:S(2)}, u32[]{:S(2)}) collective-permute-start(f32[8,1792]{1,0:T(8,128)S(1)} %replica_mean.1.refs_0_), channel_id=1, source_target_pairs={{0,24},{4,28},{8,16},{12,20},{16,8},{20,12},{24,0},{28,4},{1,25},{... | collective-permute-start | bytes 172040 | tf_op jit(solution)/shard_map/ppermute | solution.py:419
  58.7 0.0 collective-permute-start.20
  58.7 2.1 %collective-permute-start.19 = (f32[8,1792]{1,0:T(8,128)S(1)}, f32[8,1792]{1,0:T(8,128)S(1)}, u32[]{:S(2)}, u32[]{:S(2)}) collective-permute-start(f32[8,1792]{1,0:T(8,128)S(1)} %replica_mean.1.refs_0_), channel_id=1, source_target_pairs={{0,8},{4,12},{8,0},{12,4},{16,24},{20,28},{24,16},{28,20},{1,9},{5... | collective-permute-start | bytes 172040 | tf_op jit(solution)/shard_map/ppermute | solution.py:419
  60.7 2.0 %collective-permute-done.21.refs_3_ = f32[8,1792]{1,0:T(8,128)S(1)} collective-permute-done((f32[8,1792]{1,0:T(8,128)S(1)}, f32[8,1792]{1,0:T(8,128)S(1)}, u32[]{:S(2)}, u32[]{:S(2)}) %collective-permute-start.21) | collective-permute-done | bytes 57376 | tf_op jit(solution)/shard_map/ppermute | solution.py:419
  62.7 1.7 %collective-permute-done.20.refs_2_ = f32[8,1792]{1,0:T(8,128)S(1)} collective-permute-done((f32[8,1792]{1,0:T(8,128)S(1)}, f32[8,1792]{1,0:T(8,128)S(1)}, u32[]{:S(2)}, u32[]{:S(2)}) %collective-permute-start.20) | collective-permute-done | bytes 57376 | tf_op jit(solution)/shard_map/ppermute | solution.py:419
  64.4 0.0 collective-permute-done.19.refs_1_
  64.5 1.4 %collective-permute-start.22 = (f32[4,8,1792]{2,1,0:T(8,128)S(1)}, f32[4,8,1792]{2,1,0:T(8,128)S(1)}, u32[]{:S(2)}, u32[]{:S(2)}) collective-permute-start(f32[4,8,1792]{2,1,0:T(8,128)S(1)} %stack_z.1.refs_8_.refs_0_), channel_id=1, source_target_pairs={{0,4},{4,0},{8,12},{12,8},{16,20},{20,16},{24,28},{28,24},{1,5},{5... | collective-permute-start | bytes 688136 | tf_op jit(solution)/shard_map/ppermute | solution.py:419
  65.9 3.2 %basis.1 = (f32[64,64]{1,0:T(8,128)S(1)}, f32[64,64]{1,0:T(8,128)S(1)}, bf16[512,256]{1,0:T(8,128)(2,1)S(1)}, bf16[1536,256]{1,0:T(8,128)(2,1)S(1)}) custom-call(f32[64,512]{1,0:T(8,128)S(1)} %get-tuple-element.55.refs_0_, f32[64,1536]{1,0:T(8,128)S(1)} %get-tuple-element.56.refs_1_, f32[64,64]{1,0:T(8,128)S(1)} %get-tuple-element.57.refs_2_, ...), custom_call_target="tpu_custom_call" | custom-call | bytes 8159232 | tf_op jit(solution)/shard_map/basis/pallas_call | solution.py:410
  69.0 3.0 %collective-permute-done.22.refs_1_ = f32[4,8,1792]{2,1,0:T(8,128)S(1)} collective-permute-done((f32[4,8,1792]{2,1,0:T(8,128)S(1)}, f32[4,8,1792]{2,1,0:T(8,128)S(1)}, u32[]{:S(2)}, u32[]{:S(2)}) %collective-permute-start.22) | collective-permute-done | bytes 229408 | tf_op jit(solution)/shard_map/ppermute | solution.py:419
  72.1 0.7 factor_up.1
  72.7 0.1 collective-permute-start.25
  72.8 1.2 %collective-permute-start.24 = (f32[16,640]{1,0:T(8,128)S(1)}, f32[16,640]{1,0:T(8,128)S(1)}, u32[]{:S(2)}, u32[]{:S(2)}) collective-permute-start(f32[16,640]{1,0:T(8,128)S(1)} %get-tuple-element.74.refs_0_), channel_id=1, source_target_pairs={{0,2},{1,3},{2,0},{3,1},{4,6},{5,7},{6,4},{7,5},{8,10},{9,11},{10,... | collective-permute-start | bytes 122888 | tf_op jit(solution)/shard_map/ppermute | solution.py:419
  74.0 0.7 collective-permute-start.23
  74.7 1.5 %error_up.1 = (bf16[1,512,1536]{2,1,0:T(8,128)(2,1)}, f32[512,1536]{1,0:T(8,128)S(1)}, f32[1536,512]{1,0:T(8,128)S(1)}) custom-call(bf16[1,512,1536]{2,1,0:T(8,128)(2,1)S(1)} %copy-done, bf16[1,512,1536]{2,1,0:T(8,128)(2,1)S(1)} %copy-done.1, bf16[512,256]{1,0:T(8,128)(2,1)S(1)} %get-tuple-element.70.refs_2_, ...), custom_call_target="tpu_custom_call" | custom-call | flops 402653184 | bytes 15204352 | tf_op jit(solution)/shard_map/error_up/pallas_call | solution.py:410
  76.2 0.2 collective-permute-done.25.refs_3_
  76.3 0.9 %collective-permute-done.24.refs_2_ = f32[16,640]{1,0:T(8,128)S(1)} collective-permute-done((f32[16,640]{1,0:T(8,128)S(1)}, f32[16,640]{1,0:T(8,128)S(1)}, u32[]{:S(2)}, u32[]{:S(2)}) %collective-permute-start.24) | collective-permute-done | bytes 40992 | tf_op jit(solution)/shard_map/ppermute | solution.py:419
  77.2 0.0 collective-permute-done.23.refs_1_
  77.2 2.8 %last.1 = (bf16[1,1536,512]{2,1,0:T(8,128)(2,1)}, bf16[512,1536]{1,0:T(8,128)(2,1)}, bf16[1536,512]{1,0:T(8,128)(2,1)}) custom-call(f32[16,640]{1,0:T(8,128)S(1)} %get-tuple-element.74.refs_0_, f32[16,640]{1,0:T(8,128)S(1)} %collective-permute-done.23.refs_1_, f32[16,640]{1,0:T(8,128)S(1)} %collective-permute-done.24.refs_2_, ...), custom_call_target="tpu_custom_call" | custom-call | flops 805306368 | bytes 11976704 | tf_op jit(solution)/shard_map/last/pallas_call | solution.py:410
  (16 shorter events, 0.2 us)
Async XLA Ops:
  0.6 38.5 %copy-start.1 = (bf16[1,512,1536]{2,1,0:T(8,128)(2,1)S(1)}, bf16[1,512,1536]{2,1,0:T(8,128)(2,1)}, u32[]{:S(2)}) copy-start(bf16[1,512,1536]{2,1,0:T(8,128)(2,1)} %refs_1_.3) | copy-start | bytes 4718596
  6.2 32.9 %copy-start = (bf16[1,512,1536]{2,1,0:T(8,128)(2,1)S(1)}, bf16[1,512,1536]{2,1,0:T(8,128)(2,1)}, u32[]{:S(2)}) copy-start(bf16[1,512,1536]{2,1,0:T(8,128)(2,1)} %refs_0_.3) | copy-start | bytes 4718596
  6.2 8.1 %collective-permute-start.3 = (f32[4,8,1536]{2,1,0:T(8,128)}, f32[4,8,1536]{2,1,0:T(8,128)S(1)}, u32[]{:S(2)}, u32[]{:S(2)}) collective-permute-start(f32[4,8,1536]{2,1,0:T(8,128)} %get-tuple-element.50), channel_id=1, source_target_pairs={{0,4},{4,0},{8,12},{12,8},{16,20},{20,16},{24,28},{28,24},{1,5},{5... | collective-permute-start | bytes 589832 | tf_op jit(solution)/shard_map/ppermute | solution.py:419
  9.2 2.8 %collective-permute-start = (f32[16,512]{1,0:T(8,128)S(1)}, f32[16,512]{1,0:T(8,128)S(1)}, u32[]{:S(2)}, u32[]{:S(2)}) collective-permute-start(f32[16,512]{1,0:T(8,128)S(1)} %get-tuple-element.46), channel_id=1, source_target_pairs={{0,1},{1,0},{2,3},{3,2},{4,5},{5,4},{6,7},{7,6},{8,9},{9,8},{10,11... | collective-permute-start | bytes 98312 | tf_op jit(solution)/shard_map/ppermute | solution.py:419
  9.2 3.9 %collective-permute-start.1 = (f32[16,512]{1,0:T(8,128)S(1)}, f32[16,512]{1,0:T(8,128)S(1)}, u32[]{:S(2)}, u32[]{:S(2)}) collective-permute-start(f32[16,512]{1,0:T(8,128)S(1)} %get-tuple-element.47), channel_id=1, source_target_pairs={{0,2},{1,3},{2,0},{3,1},{4,6},{5,7},{6,4},{7,5},{8,10},{9,11},{10,... | collective-permute-start | bytes 98312 | tf_op jit(solution)/shard_map/ppermute | solution.py:419
  10.7 3.3 %collective-permute-start.2 = (f32[16,512]{1,0:T(8,128)S(1)}, f32[16,512]{1,0:T(8,128)S(1)}, u32[]{:S(2)}, u32[]{:S(2)}) collective-permute-start(f32[16,512]{1,0:T(8,128)S(1)} %get-tuple-element.48), channel_id=1, source_target_pairs={{0,3},{1,2},{2,1},{3,0},{4,7},{5,6},{6,5},{7,4},{8,11},{9,10},{10,... | collective-permute-start | bytes 98312 | tf_op jit(solution)/shard_map/ppermute | solution.py:419
  11.1 0.9 %copy-start.4 = (f32[4,8,1536]{2,1,0:T(8,128)S(1)}, f32[4,8,1536]{2,1,0:T(8,128)}, u32[]{:S(2)}) copy-start(f32[4,8,1536]{2,1,0:T(8,128)} %get-tuple-element.44.refs_1_) | copy-start | bytes 589828
  14.4 5.8 %collective-permute-start.4 = (f32[2,8,1536]{2,1,0:T(8,128)S(1)}, f32[2,8,1536]{2,1,0:T(8,128)S(1)}, u32[]{:S(2)}, u32[]{:S(2)}) collective-permute-start(f32[2,8,1536]{2,1,0:T(8,128)S(1)} %get-tuple-element.52), channel_id=1, source_target_pairs={{0,8},{4,12},{8,0},{12,4},{16,24},{20,28},{24,16},{28,20},{1,9},{5... | collective-permute-start | bytes 294920 | tf_op jit(solution)/shard_map/ppermute | solution.py:419
  16.2 3.9 %collective-permute-start.5 = (f32[16,512]{1,0:T(8,128)S(1)}, f32[16,512]{1,0:T(8,128)S(1)}, u32[]{:S(2)}, u32[]{:S(2)}) collective-permute-start(f32[16,512]{1,0:T(8,128)S(1)} %shard_sum.2.refs_0_), channel_id=1, source_target_pairs={{0,4},{4,0},{8,12},{12,8},{16,20},{20,16},{24,28},{28,24},{1,5},{5... | collective-permute-start | bytes 98312 | tf_op jit(solution)/shard_map/ppermute | solution.py:419
  20.2 8.1 %collective-permute-start.6 = (f32[2,8,2048]{2,1,0:T(8,128)S(1)}, f32[2,8,2048]{2,1,0:T(8,128)S(1)}, u32[]{:S(2)}, u32[]{:S(2)}) collective-permute-start(f32[2,8,2048]{2,1,0:T(8,128)S(1)} %half_sum.1.refs_0_), channel_id=1, source_target_pairs={{0,16},{4,20},{8,24},{12,28},{16,0},{20,4},{24,8},{28,12},{1,17},{... | collective-permute-start | bytes 393224 | tf_op jit(solution)/shard_map/ppermute | solution.py:419
  28.3 5.0 %collective-permute-start.7 = (f32[2,8,2048]{2,1,0:T(8,128)S(1)}, f32[2,8,2048]{2,1,0:T(8,128)S(1)}, u32[]{:S(2)}, u32[]{:S(2)}) collective-permute-start(f32[2,8,2048]{2,1,0:T(8,128)S(1)} %mean.1.refs_0_), channel_id=1, source_target_pairs={{0,8},{4,12},{8,0},{12,4},{16,24},{20,28},{24,16},{28,20},{1,9},{5... | collective-permute-start | bytes 393224 | tf_op jit(solution)/shard_map/ppermute | solution.py:419
  33.3 5.7 %collective-permute-start.8 = (f32[4,8,1536]{2,1,0:T(8,128)S(1)}, f32[4,8,1536]{2,1,0:T(8,128)S(1)}, u32[]{:S(2)}, u32[]{:S(2)}) collective-permute-start(f32[4,8,1536]{2,1,0:T(8,128)S(1)} %get-tuple-element.53.refs_1_), channel_id=1, source_target_pairs={{0,4},{4,0},{8,12},{12,8},{16,20},{20,16},{24,28},{28,24},{1,5},{5... | collective-permute-start | bytes 589832 | tf_op jit(solution)/shard_map/ppermute | solution.py:419
  34.3 7.0 %copy-start.2 = (bf16[1,1536,512]{2,1,0:T(8,128)(2,1)S(1)}, bf16[1,1536,512]{2,1,0:T(8,128)(2,1)}, u32[]{:S(2)}) copy-start(bf16[1,1536,512]{2,1,0:T(8,128)(2,1)} %refs_4_.7) | copy-start | bytes 4718596
  34.3 7.0 %copy-start.3 = (bf16[1,1536,512]{2,1,0:T(8,128)(2,1)S(1)}, bf16[1,1536,512]{2,1,0:T(8,128)(2,1)}, u32[]{:S(2)}) copy-start(bf16[1,1536,512]{2,1,0:T(8,128)(2,1)} %refs_5_.5) | copy-start | bytes 4718596
  34.3 3.6 %collective-permute-start.11 = (f32[16,512]{1,0:T(8,128)S(1)}, f32[16,512]{1,0:T(8,128)S(1)}, u32[]{:S(2)}, u32[]{:S(2)}) collective-permute-start(f32[16,512]{1,0:T(8,128)S(1)} %get-tuple-element.54.refs_1_), channel_id=1, source_target_pairs={{0,3},{1,2},{2,1},{3,0},{4,7},{5,6},{6,5},{7,4},{8,11},{9,10},{10,... | collective-permute-start | bytes 98312 | tf_op jit(solution)/shard_map/ppermute | solution.py:419
  34.3 4.0 %collective-permute-start.10 = (f32[16,512]{1,0:T(8,128)S(1)}, f32[16,512]{1,0:T(8,128)S(1)}, u32[]{:S(2)}, u32[]{:S(2)}) collective-permute-start(f32[16,512]{1,0:T(8,128)S(1)} %get-tuple-element.54.refs_1_), channel_id=1, source_target_pairs={{0,2},{1,3},{2,0},{3,1},{4,6},{5,7},{6,4},{7,5},{8,10},{9,11},{10,... | collective-permute-start | bytes 98312 | tf_op jit(solution)/shard_map/ppermute | solution.py:419
  35.8 2.5 %collective-permute-start.9 = (f32[16,512]{1,0:T(8,128)S(1)}, f32[16,512]{1,0:T(8,128)S(1)}, u32[]{:S(2)}, u32[]{:S(2)}) collective-permute-start(f32[16,512]{1,0:T(8,128)S(1)} %get-tuple-element.54.refs_1_), channel_id=1, source_target_pairs={{0,1},{1,0},{2,3},{3,2},{4,5},{5,4},{6,7},{7,6},{8,9},{9,8},{10,11... | collective-permute-start | bytes 98312 | tf_op jit(solution)/shard_map/ppermute | solution.py:419
  40.3 7.5 %collective-permute-start.15 = (f32[4,8,1536]{2,1,0:T(8,128)S(1)}, f32[4,8,1536]{2,1,0:T(8,128)S(1)}, u32[]{:S(2)}, u32[]{:S(2)}) collective-permute-start(f32[4,8,1536]{2,1,0:T(8,128)S(1)} %get-tuple-element.64), channel_id=1, source_target_pairs={{0,4},{4,0},{8,12},{12,8},{16,20},{20,16},{24,28},{28,24},{1,5},{5... | collective-permute-start | bytes 589832 | tf_op jit(solution)/shard_map/ppermute | solution.py:419
  42.4 1.9 %collective-permute-start.12 = (f32[16,768]{1,0:T(8,128)S(1)}, f32[16,768]{1,0:T(8,128)S(1)}, u32[]{:S(2)}, u32[]{:S(2)}) collective-permute-start(f32[16,768]{1,0:T(8,128)S(1)} %get-tuple-element.59), channel_id=1, source_target_pairs={{0,1},{1,0},{2,3},{3,2},{4,5},{5,4},{6,7},{7,6},{8,9},{9,8},{10,11... | collective-permute-start | bytes 147464 | tf_op jit(solution)/shard_map/ppermute | solution.py:419
  42.4 4.2 %collective-permute-start.13 = (f32[16,768]{1,0:T(8,128)S(1)}, f32[16,768]{1,0:T(8,128)S(1)}, u32[]{:S(2)}, u32[]{:S(2)}) collective-permute-start(f32[16,768]{1,0:T(8,128)S(1)} %get-tuple-element.60), channel_id=1, source_target_pairs={{0,2},{1,3},{2,0},{3,1},{4,6},{5,7},{6,4},{7,5},{8,10},{9,11},{10,... | collective-permute-start | bytes 147464 | tf_op jit(solution)/shard_map/ppermute | solution.py:419
  44.0 3.7 %collective-permute-start.14 = (f32[16,768]{1,0:T(8,128)S(1)}, f32[16,768]{1,0:T(8,128)S(1)}, u32[]{:S(2)}, u32[]{:S(2)}) collective-permute-start(f32[16,768]{1,0:T(8,128)S(1)} %get-tuple-element.61), channel_id=1, source_target_pairs={{0,3},{1,2},{2,1},{3,0},{4,7},{5,6},{6,5},{7,4},{8,11},{9,10},{10,... | collective-permute-start | bytes 147464 | tf_op jit(solution)/shard_map/ppermute | solution.py:419
  47.8 6.6 %collective-permute-start.16 = (f32[8,1792]{1,0:T(8,128)S(1)}, f32[8,1792]{1,0:T(8,128)S(1)}, u32[]{:S(2)}, u32[]{:S(2)}) collective-permute-start(f32[8,1792]{1,0:T(8,128)S(1)} %get-tuple-element.67), channel_id=1, source_target_pairs={{0,24},{4,28},{8,16},{12,20},{16,8},{20,12},{24,0},{28,4},{1,25},{... | collective-permute-start | bytes 172040 | tf_op jit(solution)/shard_map/ppermute | solution.py:419
  50.3 5.9 %collective-permute-start.17 = (f32[8,1792]{1,0:T(8,128)S(1)}, f32[8,1792]{1,0:T(8,128)S(1)}, u32[]{:S(2)}, u32[]{:S(2)}) collective-permute-start(f32[8,1792]{1,0:T(8,128)S(1)} %get-tuple-element.68), channel_id=1, source_target_pairs={{0,16},{4,20},{8,24},{12,28},{16,0},{20,4},{24,8},{28,12},{1,17},{... | collective-permute-start | bytes 172040 | tf_op jit(solution)/shard_map/ppermute | solution.py:419
  50.3 5.9 %collective-permute-start.18 = (f32[8,1792]{1,0:T(8,128)S(1)}, f32[8,1792]{1,0:T(8,128)S(1)}, u32[]{:S(2)}, u32[]{:S(2)}) collective-permute-start(f32[8,1792]{1,0:T(8,128)S(1)} %get-tuple-element.69), channel_id=1, source_target_pairs={{0,8},{4,12},{8,0},{12,4},{16,24},{20,28},{24,16},{28,20},{1,9},{5... | collective-permute-start | bytes 172040 | tf_op jit(solution)/shard_map/ppermute | solution.py:419
  56.3 6.4 %collective-permute-start.21 = (f32[8,1792]{1,0:T(8,128)S(1)}, f32[8,1792]{1,0:T(8,128)S(1)}, u32[]{:S(2)}, u32[]{:S(2)}) collective-permute-start(f32[8,1792]{1,0:T(8,128)S(1)} %replica_mean.1.refs_0_), channel_id=1, source_target_pairs={{0,24},{4,28},{8,16},{12,20},{16,8},{20,12},{24,0},{28,4},{1,25},{... | collective-permute-start | bytes 172040 | tf_op jit(solution)/shard_map/ppermute | solution.py:419
  58.7 5.8 %collective-permute-start.20 = (f32[8,1792]{1,0:T(8,128)S(1)}, f32[8,1792]{1,0:T(8,128)S(1)}, u32[]{:S(2)}, u32[]{:S(2)}) collective-permute-start(f32[8,1792]{1,0:T(8,128)S(1)} %replica_mean.1.refs_0_), channel_id=1, source_target_pairs={{0,16},{4,20},{8,24},{12,28},{16,0},{20,4},{24,8},{28,12},{1,17},{... | collective-permute-start | bytes 172040 | tf_op jit(solution)/shard_map/ppermute | solution.py:419
  58.7 5.8 %collective-permute-start.19 = (f32[8,1792]{1,0:T(8,128)S(1)}, f32[8,1792]{1,0:T(8,128)S(1)}, u32[]{:S(2)}, u32[]{:S(2)}) collective-permute-start(f32[8,1792]{1,0:T(8,128)S(1)} %replica_mean.1.refs_0_), channel_id=1, source_target_pairs={{0,8},{4,12},{8,0},{12,4},{16,24},{20,28},{24,16},{28,20},{1,9},{5... | collective-permute-start | bytes 172040 | tf_op jit(solution)/shard_map/ppermute | solution.py:419
  64.5 7.6 %collective-permute-start.22 = (f32[4,8,1792]{2,1,0:T(8,128)S(1)}, f32[4,8,1792]{2,1,0:T(8,128)S(1)}, u32[]{:S(2)}, u32[]{:S(2)}) collective-permute-start(f32[4,8,1792]{2,1,0:T(8,128)S(1)} %stack_z.1.refs_8_.refs_0_), channel_id=1, source_target_pairs={{0,4},{4,0},{8,12},{12,8},{16,20},{20,16},{24,28},{28,24},{1,5},{5... | collective-permute-start | bytes 688136 | tf_op jit(solution)/shard_map/ppermute | solution.py:419
  72.7 3.6 %collective-permute-start.25 = (f32[16,640]{1,0:T(8,128)S(1)}, f32[16,640]{1,0:T(8,128)S(1)}, u32[]{:S(2)}, u32[]{:S(2)}) collective-permute-start(f32[16,640]{1,0:T(8,128)S(1)} %get-tuple-element.74.refs_0_), channel_id=1, source_target_pairs={{0,3},{1,2},{2,1},{3,0},{4,7},{5,6},{6,5},{7,4},{8,11},{9,10},{10,... | collective-permute-start | bytes 122888 | tf_op jit(solution)/shard_map/ppermute | solution.py:419
  72.8 4.3 %collective-permute-start.24 = (f32[16,640]{1,0:T(8,128)S(1)}, f32[16,640]{1,0:T(8,128)S(1)}, u32[]{:S(2)}, u32[]{:S(2)}) collective-permute-start(f32[16,640]{1,0:T(8,128)S(1)} %get-tuple-element.74.refs_0_), channel_id=1, source_target_pairs={{0,2},{1,3},{2,0},{3,1},{4,6},{5,7},{6,4},{7,5},{8,10},{9,11},{10,... | collective-permute-start | bytes 122888 | tf_op jit(solution)/shard_map/ppermute | solution.py:419
  74.0 3.2 %collective-permute-start.23 = (f32[16,640]{1,0:T(8,128)S(1)}, f32[16,640]{1,0:T(8,128)S(1)}, u32[]{:S(2)}, u32[]{:S(2)}) collective-permute-start(f32[16,640]{1,0:T(8,128)S(1)} %get-tuple-element.74.refs_0_), channel_id=1, source_target_pairs={{0,1},{1,0},{2,3},{3,2},{4,5},{5,4},{6,7},{7,6},{8,9},{9,8},{10,11... | collective-permute-start | bytes 122888 | tf_op jit(solution)/shard_map/ppermute | solution.py:419
